TPU v7x, 32 devices: a whole 2x2x4 slice. The times are simulated.
32 devices in a mesh: groups: 2 (over y), ctx: 4 (over z), head: 4 (over x, core).
Axes of the slice: x: 2, y: 2, z: 4, core: 2. Of those that a mesh axis runs over, the one named last changes fastest.
Arguments:
- queries: bfloat16 [1024, 12288], P(('groups', 'ctx'), 'head'), parts along dimension 0, may hold values from -12 to 12
- kv_rows: bfloat16 [2048, 576], P(('groups', 'ctx')), parts along dimension 0, may hold values from -4.5 to 4.5
- w_kv_up: bfloat16 [512, 16384], P(None, 'head'), may hold values from -0.25 to 0.25
- w_out: bfloat16 [8192, 7168], P('head', 'ctx'), may hold values from -1 to 1
- stretch_order: int32 [8], P('groups'), parts along dimension 0, may hold values from 0 to 3, each once
- prefix_len: int32 [2], P('groups'), parts along dimension 0, may hold values from 128 to 512
Outputs:
- mixed: bfloat16 [1024, 7168], P(('groups', 'ctx', 'head')), parts along dimension 0
There are 2 independent parts, one for each index of `groups`. A program takes and returns all parts, laid end to end along the dimension named above; an argument that names none is the same for every part. Nothing has to cross between parts.
All inputs are finite; a program needn't handle non-finite values.
Results may differ from a plain program's by a relative error of at most 0.012.
Values may be sent and summed in bfloat16 or wider, within the bound.
No kernel may reach another device: no remote copies, remote signals or barrier semaphores. Data moves between devices by JAX's collectives and lax.ppermute only.
A program may use at most 128 MiB of HBM per device.

v0:
```python
import math

import jax
import jax.numpy as jnp
from jax import lax
from jax.sharding import PartitionSpec as P

LAT = 512
NOPE = 128
ROPE = 64
VD = 128


def lookup(table, indices):
    positions = jnp.arange(table.shape[0], dtype=jnp.int32)
    return jnp.sum(jnp.where(indices[..., None] == positions, table, 0), axis=-1)


def shards(queries, kv_rows, w_kv_up, w_out, stretch_order, prefix_len):
    query_rows = queries.shape[0]
    row_span = kv_rows.shape[0]
    cache_rows = row_span - query_rows
    head_count = w_kv_up.shape[1] // (NOPE + VD)
    score_scale = 1.0 / math.sqrt(NOPE + ROPE)
    own_block = lookup(stretch_order, lax.axis_index("ctx"))
    query_pos = own_block * query_rows + jnp.arange(query_rows, dtype=jnp.int32)
    query_heads = queries.reshape(query_rows, head_count, NOPE + ROPE)
    query_nope = query_heads[:, :, :NOPE]
    query_rope = query_heads[:, :, NOPE:]
    prefix_end = prefix_len[0]

    def fold_block(folded, key_rows, first_row):
        running_max, running_sum, weighted = folded
        amount = key_rows.shape[0]
        row_ids = first_row + jnp.arange(amount, dtype=jnp.int32)
        shard_ids = row_ids // row_span
        within = row_ids % row_span
        is_cache = within < cache_rows
        slot_ids = shard_ids * cache_rows + within
        key_pos = lookup(stretch_order, shard_ids) * query_rows + within - cache_rows
        visible = jnp.where(
            is_cache[None, :],
            (slot_ids < prefix_end)[None, :],
            key_pos[None, :] <= query_pos[:, None],
        )
        projected = jnp.dot(key_rows[:, :LAT], w_kv_up, preferred_element_type=jnp.float32).astype(
            jnp.bfloat16
        )
        projected = projected.reshape(amount, head_count, NOPE + VD)
        scores = jnp.einsum(
            "qhd,khd->hqk", query_nope, projected[:, :, :NOPE], preferred_element_type=jnp.float32
        )
        scores = scores + jnp.einsum(
            "qhd,kd->hqk", query_rope, key_rows[:, LAT:], preferred_element_type=jnp.float32
        )
        scores = jnp.where(visible[None], scores * score_scale, -jnp.inf)
        new_max = jnp.maximum(running_max, jnp.max(scores, axis=2))
        factor = jnp.exp(running_max - new_max)
        weights = jnp.exp(scores - new_max[:, :, None])
        running_sum = running_sum * factor + jnp.sum(weights, axis=2)
        weighted = weighted * factor[:, :, None] + jnp.einsum(
            "hqk,khd->hqd",
            weights.astype(jnp.bfloat16),
            projected[:, :, NOPE:],
            preferred_element_type=jnp.float32,
        )
        return (new_max, running_sum, weighted)

    initial = (
        jnp.full((head_count, query_rows), -1e30, jnp.float32),
        jnp.zeros((head_count, query_rows), jnp.float32),
        jnp.zeros((head_count, query_rows, VD), jnp.float32),
    )
    folded = initial
    key_rows = lax.all_gather(kv_rows, "ctx", axis=0, tiled=True)
    amount = key_rows.shape[0]
    blocks = key_rows.reshape(amount // 512, 512, key_rows.shape[1])
    offsets = 512 * jnp.arange(amount // 512, dtype=jnp.int32)

    def advance(state_now, inputs):
        return (fold_block(state_now, inputs[0], inputs[1]), None)

    folded, unused = lax.scan(advance, folded, (blocks, offsets))
    running_max, running_sum, weighted = folded
    attended = (weighted / running_sum[:, :, None]).astype(jnp.bfloat16)
    weight_piece = lax.all_gather(w_out, "ctx", axis=1, tiled=True)
    partial_sums = jnp.einsum(
        "hqd,hde->qe",
        attended,
        weight_piece.reshape(head_count, VD, weight_piece.shape[1]),
        preferred_element_type=jnp.float32,
    )
    mixed = lax.psum_scatter(
        partial_sums.astype(jnp.bfloat16), "head", scatter_dimension=0, tiled=True
    )
    return mixed


def solution(mesh):
    placed = (
        P(("groups", "ctx"), "head"),
        P(("groups", "ctx"), None),
        P(None, "head"),
        P("head", "ctx"),
        P("groups"),
        P("groups"),
    )
    return jax.shard_map(
        shards,
        mesh=mesh,
        in_specs=placed,
        out_specs=P(("groups", "ctx", "head"), None),
        check_vma=False,
    )
```

profile of v0, /device:TPU:0, one launch (start us, length us, event | category | flops | bytes accessed | tf_op | source)
XLA Modules:
  0.0 584.2 jit_solution(9466703823029653641)
XLA Ops:
  6.5 0.0 copy-start.2
  6.5 0.0 all-gather.3.cloned.1.call-start
  6.5 0.7 all-gather.3.cloned.1.call-update
  7.3 0.0 copy-start.3
  7.3 0.0 all-gather.5.cloned.1.call-start
  7.3 0.7 all-gather.5.cloned.1.call-update
  8.0 0.0 reduce-scatter.2.cloned.1.call-start
  8.1 0.0 copy-done.2
  8.1 0.4 copy.21
  8.6 1.1 copy.23
  9.6 0.0 copy-done.3
  9.6 0.7 fusion.24
  10.9 32.5 %all-gather.3.cloned.1.call-done = bf16[1024,576]{0,1:T(8,128)(2,1)} async-done(((bf16[256,576]{0,1:T(8,128)(2,1)}), bf16[1024,576]{0,1:T(8,128)(2,1)}) %all-gather.3.cloned.1.call-update) | async-done | bytes 1179664 | tf_op jit(solution)/shard_map/all_gather | solution.py:75
  43.4 2.4 copy.36
  45.8 43.8 %while.17 = (s32[]{:T(128)}, f32[16,128]{1,0:T(8,128)S(1)}, f32[16,128]{1,0:T(8,128)S(1)}, f32[16,128,128]{2,1,0:T(8,128)S(1)}, s32[2]{0:T(128)S(1)}, /*index=5*...) while((s32[]{:T(128)}, f32[16,128]{1,0:T(8,128)S(1)}, ...), condition=%wide.region_5.6_spmd.clone, body=%wide.region_1.5_spmd.clone.sunk | while | flops 2830019584 | bytes 74136824 | solution.py:83
  45.8 0.6 dynamic_slice.20
  46.4 0.6 add_select_fusion.3
  47.0 0.1 select_reduce_fusion.2
  47.1 0.6 add_add_fusion.2
  47.8 1.3 add_compare_fusion.2
  49.1 0.3 compare_select_fusion.3
  49.4 1.2 dynamic-slice_bitcast_fusion.2
  50.6 5.7 convolution_convert_fusion.2
  56.3 1.4 copy.42
  57.7 0.0 copy-start.1
  57.7 0.7 fusion.51
  58.4 0.4 copy-done.1
  58.8 0.7 fusion.52
  59.5 2.8 fusion.53
  62.4 0.0 copy-start
  62.4 3.3 fusion.54
  65.7 0.9 copy-done
  66.7 2.1 fusion.56
  68.8 0.6 dynamic_slice.20
  69.3 0.6 add_select_fusion.3
  70.0 0.1 select_reduce_fusion.2
  70.1 0.6 add_add_fusion.2
  70.7 1.3 add_compare_fusion.2
  72.0 0.3 compare_select_fusion.3
  72.3 1.1 dynamic-slice_bitcast_fusion.2
  73.4 4.6 convolution_convert_fusion.2
  78.0 1.4 copy.42
  79.4 0.0 copy-start.1
  79.4 0.7 fusion.51
  80.1 0.3 copy-done.1
  80.4 0.7 fusion.52
  81.2 2.9 fusion.53
  84.0 0.0 copy-start
  84.0 3.0 fusion.54
  87.0 0.5 copy-done
  87.5 2.1 fusion.56
  89.6 446.9 %all-gather.5.cloned.1.call-done = bf16[2048,7168]{1,0:T(8,128)(2,1)} async-done(((bf16[2048,1792]{1,0:T(8,128)(2,1)}), bf16[2048,7168]{1,0:T(8,128)(2,1)}) %all-gather.5.cloned.1.call-update) | async-done | bytes 29360144 | tf_op jit(solution)/shard_map/all_gather | solution.py:86
  536.5 13.0 %fusion.22 = bf16[128,7168]{1,0:T(8,128)(2,1)} fusion(bf16[16,128,7168]{2,1,0:T(8,128)(2,1)} %bitcast.51, f32[16,128,128]{2,1,0:T(8,128)S(1)} %get-tuple-element.159, f32[16,128]{1,0:T(8,128)S(1)} %get-tuple-element.160), kind=kOutput, calls=%fused_computation.40 | convolution fusion | flops 3759538176 | bytes 32251904 | tf_op jit(solution)/shard_map/hqd,hde->qe/dot_general | solution.py:87
  549.5 0.0 reduce-scatter.2.cloned.1.call-update
  549.5 28.2 %reduce-scatter.2.cloned.1.call-done = bf16[32,7168]{1,0:T(8,128)(2,1)} async-done(((bf16[128,7168]{1,0:T(8,128)(2,1)}), bf16[32,7168]{1,0:T(8,128)(2,1)}) %reduce-scatter.2.cloned.1.call-update) | async-done | bytes 458768 | tf_op jit(solution)/shard_map/reduce_scatter | solution.py:93
  (14 shorter events, 0.1 us)
Async XLA Ops:
  6.5 1.5 copy-start.2
  6.5 36.9 %all-gather.3.cloned.1.call-start = ((), (), s32[]{:S(2)}) async-start(), calls=%async_computation.1 | async-start | bytes 1474560 | tf_op jit(solution)/shard_map/all_gather | solution.py:75
  7.3 2.3 copy-start.3
  7.3 529.2 %all-gather.5.cloned.1.call-start = ((), (), s32[]{:S(2)}) async-start(), calls=%async_computation.2 | async-start | bytes 36700160 | tf_op jit(solution)/shard_map/all_gather | solution.py:86
  8.0 569.7 %reduce-scatter.2.cloned.1.call-start = ((), (), s32[]{:S(2)}) async-start(), calls=%async_computation.3 | async-start | bytes 2293760 | tf_op jit(solution)/shard_map/reduce_scatter | solution.py:93
  57.7 1.1 copy-start.1
  62.4 4.3 copy-start
  79.4 1.0 copy-start.1
  84.0 3.5 copy-start
Sparse Core Ops, SparseCore 0:
  8.9 34.4 all-gather.2
  45.0 491.4 all-gather.4
  549.6 28.0 reduce-scatter.1
where the time goes:
time: 585 us; the launch traced here: 584 us
  waiting for transfers between devices  509 us (87%)
  matrix products  34.5 us (6%)
  local copies, waits for them, and re-layouts  13.8 us (2%)
  between operations  13.8 us (2%)
  other arithmetic  12.8 us (2%)
    all_gather x1, waiting for transfers between devices, shards(): weight_piece = lax.all_gather(w_out, 'ctx', axis=1, tiled=True)  447 us
    all_gather x1, waiting for transfers between devices, shards(): key_rows = lax.all_gather(kv_rows, 'ctx', axis=0, tiled=True)  32.5 us
    reduce_scatter x1, waiting for transfers between devices, shards(): lax.psum_scatter(partial_sums.astype(jnp.bfloat16), 'head', scatter_dimen...  28.2 us
    dot_general x1, matrix products, shards(): jnp.einsum('hqd,hde->qe', attended, weight_piece.reshape(head_count, VD,...  13 us
  transfers between devices with their start and end apart: 3, of which 3 were waited for; matrix products, arithmetic and copies ran while one was open for 8% of the time, Pallas kernels for 0%

commit v1 on v0

v1 whole, which is shorter than its diff:
```python
import functools
import math

import jax
import jax.numpy as jnp
from jax import lax
from jax.experimental import pallas as pl
from jax.experimental.pallas import tpu as pltpu
from jax.sharding import PartitionSpec as P

LAT = 512
NOPE = 128
ROPE = 64
VD = 128
CHUNKS = 2
HEAD_BLOCK = 8
MASKED = -1e30
LOG2E = 1.4426950408889634


def lookup(table, indices):
    positions = jnp.arange(table.shape[0], dtype=jnp.int32)
    return jnp.sum(jnp.where(indices[..., None] == positions, table, 0), axis=-1)


def shift(array, axis, size, by):
    return lax.ppermute(array, axis, [(i, (i + by) % size) for i in range(size)])


def swap_cores(array, size):
    return lax.ppermute(array, "head", [(i, i ^ 1) for i in range(size)])


def attention_kernel(heads, rows, q_ref, keys_ref, bias_ref, weight_ref, out_ref):
    for head in range(heads):
        scores = jnp.dot(q_ref[head], keys_ref[...], preferred_element_type=jnp.float32)
        scores = scores + bias_ref[...]
        top = jnp.max(scores, axis=1, keepdims=True)
        weights = jnp.exp2(scores - top)
        total = jnp.sum(weights, axis=1, keepdims=True)
        mixed = lax.dot_general(
            weights.astype(jnp.bfloat16),
            keys_ref[:LAT, :],
            (((1,), (1,)), ((), ())),
            preferred_element_type=jnp.float32,
        )
        mixed = (mixed / total).astype(jnp.bfloat16)
        w_value = weight_ref[:, head * (NOPE + VD) + NOPE : (head + 1) * (NOPE + VD)]
        result = jnp.dot(mixed, w_value, preferred_element_type=jnp.float32)
        out_ref[:, head * VD : (head + 1) * VD] = result.astype(jnp.bfloat16)


def attention(q_ext, keys, bias, w_kv_up):
    head_count, rows, depth = q_ext.shape
    amount = keys.shape[1]
    block = math.gcd(HEAD_BLOCK, head_count)
    macs = head_count * rows * (amount * (depth + LAT) + LAT * VD)
    return pl.pallas_call(
        functools.partial(attention_kernel, block, rows),
        grid=(head_count // block,),
        out_shape=jax.ShapeDtypeStruct((rows, head_count * VD), jnp.bfloat16),
        in_specs=[
            pl.BlockSpec((block, rows, depth), lambda i: (i, 0, 0)),
            pl.BlockSpec((depth, amount), lambda i: (0, 0)),
            pl.BlockSpec((rows, amount), lambda i: (0, 0)),
            pl.BlockSpec((LAT, block * (NOPE + VD)), lambda i: (0, i)),
        ],
        out_specs=pl.BlockSpec((rows, block * VD), lambda i: (0, i)),
        compiler_params=pltpu.CompilerParams(vmem_limit_bytes=40 * 1024 * 1024),
        cost_estimate=pl.CostEstimate(
            flops=2 * macs,
            bytes_accessed=2 * (q_ext.size + keys.size) + 4 * bias.size + 2 * w_kv_up.size,
            transcendentals=head_count * rows * amount,
        ),
    )(q_ext, keys, bias, w_kv_up)


def shards(n_ctx, n_head, queries, kv_rows, w_kv_up, w_out, stretch_order, prefix_len):
    query_rows = queries.shape[0]
    row_span = kv_rows.shape[0]
    cache_rows = row_span - query_rows
    half = row_span // 2
    head_count = w_kv_up.shape[1] // (NOPE + VD)
    columns = w_out.shape[1]
    n_x = n_head // 2
    owned = query_rows // n_head
    piece = owned // CHUNKS
    ctx = lax.axis_index("ctx")
    head = lax.axis_index("head")
    core = head % 2
    x = head // 2

    with jax.named_scope("keys_over_ctx"):
        kv_t = kv_rows.T
        own_half = lax.dynamic_slice(kv_t, (0, core * half), (LAT + ROPE, half))
        halves = [own_half] + [shift(own_half, "ctx", n_ctx, d) for d in range(1, n_ctx)]
        others = [swap_cores(array, n_head) for array in halves[1:]]
        other_half = lax.dynamic_slice(kv_t, (0, (1 - core) * half), (LAT + ROPE, half))
        keys = jnp.concatenate(halves + [other_half] + others, axis=1)

    with jax.named_scope("visible"):
        scale = LOG2E / math.sqrt(NOPE + ROPE)
        query_ids = jnp.arange(query_rows, dtype=jnp.int32)
        query_pos = lookup(stretch_order, ctx) * query_rows + query_ids
        sources = (ctx - jnp.arange(n_ctx, dtype=jnp.int32)) % n_ctx
        offsets = jnp.arange(half, dtype=jnp.int32)
        within = jnp.stack([core * half + offsets, (1 - core) * half + offsets])
        within = jnp.broadcast_to(within[:, None, :], (2, n_ctx, half))
        sources = jnp.broadcast_to(sources[None, :, None], (2, n_ctx, half))
        is_cache = within < cache_rows
        slot_ids = sources * cache_rows + within
        key_pos = lookup(stretch_order, sources) * query_rows + within - cache_rows
        cache_pos = jnp.where(slot_ids < prefix_len[0], -1, n_ctx * query_rows)
        first_seen = jnp.where(is_cache, cache_pos, key_pos).reshape(-1)
        query_pos = query_pos.reshape(n_head, CHUNKS, piece).transpose(1, 0, 2)
        query_pos = query_pos.reshape(CHUNKS, query_rows // CHUNKS)
        bias = jnp.where(first_seen[None, None, :] <= query_pos[:, :, None], 0.0, MASKED)
        bias = bias.astype(jnp.float32)

    with jax.named_scope("queries_to_latent"):
        query_heads = queries.reshape(n_head, CHUNKS, piece, head_count, NOPE + ROPE)
        query_heads = query_heads.transpose(1, 3, 0, 2, 4)
        query_heads = query_heads.reshape(CHUNKS, head_count, query_rows // CHUNKS, NOPE + ROPE)
        w_keys = w_kv_up.reshape(LAT, head_count, NOPE + VD)[:, :, :NOPE]
        absorbed = jnp.einsum(
            "chqd,lhd->chql", query_heads[..., :NOPE], w_keys, preferred_element_type=jnp.float32
        )
        rope = query_heads[..., NOPE:].astype(jnp.float32)
        q_ext = (jnp.concatenate([absorbed, rope], axis=3) * scale).astype(jnp.bfloat16)

    results = []
    for chunk in range(CHUNKS):
        with jax.named_scope("attention"):
            attended = attention(q_ext[chunk], keys, bias[chunk], w_kv_up)
        with jax.named_scope("attended_over_ctx"):
            gathered = [attended] + [shift(attended, "ctx", n_ctx, d) for d in range(1, n_ctx)]
            gathered = jnp.concatenate(gathered, axis=0)
        with jax.named_scope("out_product"):
            partial = jnp.dot(gathered, w_out, preferred_element_type=jnp.float32)
            partial = partial.reshape(n_ctx, n_x, 2, piece, columns)
        with jax.named_scope("sum_over_cores"):
            sent = lax.dynamic_index_in_dim(partial, 1 - core, 2, keepdims=False)
            kept = lax.dynamic_index_in_dim(partial, core, 2, keepdims=False)
            summed = kept + swap_cores(sent.astype(jnp.bfloat16), n_head).astype(jnp.float32)
        with jax.named_scope("sum_over_x"):
            total = lax.dynamic_index_in_dim(summed, x, 1, keepdims=False)
            for d in range(1, n_x):
                sent = lax.dynamic_index_in_dim(summed, (x + d) % n_x, 1, keepdims=False)
                sent = shift(sent.astype(jnp.bfloat16), "head", n_head, 2 * d)
                total = total + sent.astype(jnp.float32)
        with jax.named_scope("columns_over_ctx"):
            total = total.astype(jnp.bfloat16)
            blocks = [total[0]] + [shift(total[d], "ctx", n_ctx, -d) for d in range(1, n_ctx)]
        results.append(blocks)
    with jax.named_scope("output"):
        stacked = [jnp.concatenate([r[d] for r in results], axis=0) for d in range(n_ctx)]
        doubled = jnp.concatenate(stacked + stacked, axis=1)
        start = ((n_ctx - ctx) % n_ctx) * columns
        return lax.dynamic_slice(doubled, (0, start), (owned, n_ctx * columns))


def solution(mesh):
    placed = (
        P(("groups", "ctx"), "head"),
        P(("groups", "ctx"), None),
        P(None, "head"),
        P("head", "ctx"),
        P("groups"),
        P("groups"),
    )
    return jax.shard_map(
        functools.partial(shards, mesh.shape["ctx"], mesh.shape["head"]),
        mesh=mesh,
        in_specs=placed,
        out_specs=P(("groups", "ctx", "head"), None),
        check_vma=False,
    )
```

time: 585 us -> 127 us (0.22)
  waiting for transfers between devices: 509 us -> 34.1 us
  Pallas kernels: 0 us -> 26.8 us
  matrix products: 34.5 us -> 9.47 us
  starting transfers between devices: 0.08 us -> 25.1 us
  local copies, waits for them, and re-layouts: 13.8 us -> 26.9 us
  between operations: 13.8 us -> 1.57 us
  other arithmetic: 12.8 us -> 2.21 us
    all_gather x2 -> x0, waiting for transfers between devices: 479 us -> none  [the longest x1 447 us: shards(): weight_piece = lax.all_gather(w_out, 'ctx', axis=1, tiled=True)]
    ppermute x0 -> x22, waiting for transfers between devices: none -> 34.1 us  [the longest x17 34 us: shift(): lax.ppermute(array, axis, [(i, (i + by) % size) for i in range(size)])]
    reduce_scatter x1 -> x0, waiting for transfers between devices: 28.2 us -> none  [shards(): lax.psum_scatter(partial_sums.astype(jnp.bfloat16), 'head', scatter_dimen...]
    pallas_call x0 -> x2, Pallas kernels: none -> 26.8 us  [attention(): pl.pallas_call(functools.partial(attention_kernel, block, rows), grid=(he...]
    ppermute x0 -> x22, starting transfers between devices: none -> 25.1 us  [the longest x17 24.4 us: shift(): lax.ppermute(array, axis, [(i, (i + by) % size) for i in range(size)])]
    dot_general x9 -> x3, matrix products: 34.5 us -> 9.47 us  [the longest x2 7.19 us: shards(): partial = jnp.dot(gathered, w_out, preferred_element_type=jnp.float32)]
    unnamed x6 -> x22, local copies, waits for them, and re-layouts: 1.43 us -> 22.2 us
    reduce_sum x2 -> x0, other arithmetic: 6.31 us -> none  [fold_block(): running_sum = running_sum * factor + jnp.sum(weights, axis=2)]
  transfers between devices with their start and end apart: 3 -> 22, of which waited for: 3 -> 7; matrix products, arithmetic and copies ran while one was open for 8% -> 22% of each run, Pallas kernels for 0% -> 11%
where the time goes in v1:
time: 127 us; the launch traced here: 126 us
  waiting for transfers between devices  34.1 us (27%)
  local copies, waits for them, and re-layouts  26.9 us (21%)
  Pallas kernels  26.8 us (21%)
  starting transfers between devices  25.1 us (20%)
  matrix products  9.47 us (7%)
  other arithmetic  2.21 us (2%)
  between operations  1.57 us (1%)
    ppermute x17, waiting for transfers between devices, shift(): lax.ppermute(array, axis, [(i, (i + by) % size) for i in range(size)])  34 us
    pallas_call x2, Pallas kernels, attention(): pl.pallas_call(functools.partial(attention_kernel, block, rows), grid=(he...  26.8 us
    ppermute x17, starting transfers between devices, shift(): lax.ppermute(array, axis, [(i, (i + by) % size) for i in range(size)])  24.4 us
    unnamed x22, local copies, waits for them, and re-layouts  22.2 us
    dot_general x2, matrix products, shards(): partial = jnp.dot(gathered, w_out, preferred_element_type=jnp.float32)  7.19 us
    reshape x2, local copies, waits for them, and re-layouts, shards(): queries.reshape(n_head, CHUNKS, piece, head_count, NOPE + ROPE)  2.59 us
  transfers between devices with their start and end apart: 22, of which 7 were waited for; matrix products, arithmetic and copies ran while one was open for 22% of the time, Pallas kernels for 11%

profile of v1, /device:TPU:0, one launch (start us, length us, event | category | flops | bytes accessed | tf_op | source)
XLA Modules:
  0.0 126.3 jit_solution(11700528979654612151)
XLA Ops:
  0.0 1.7 %constant_dynamic-update-slice_fusion.6 = (bf16[576,1024]{1,0:T(8,128)(2,1)}, bf16[576,128]{1,0:T(8,128)(2,1)}) fusion(bf16[256,576]{0,1:T(8,128)(2,1)} %param.7, s32[]{:T(128)S(6)} %select_n.90), kind=kLoop, calls=%fused_computation.69 | loop fusion | bytes 442372
  1.7 3.0 %collective-permute-start = (bf16[576,128]{1,0:T(8,128)(2,1)}, bf16[576,128]{1,0:T(8,128)(2,1)}, u32[]{:S(2)}, u32[]{:S(2)}) collective-permute-start(bf16[576,128]{1,0:T(8,128)(2,1)} %get-tuple-element.6), channel_id=1, source_target_pairs={{0,4},{4,8},{8,12},{12,0},{1,5},{5,9},{9,13},{13,1},{2,6},{6,10},{... | collective-permute-start | bytes 442376 | tf_op jit(solution)/shard_map/keys_over_ctx/ppermute | solution.py:27
  4.7 2.6 %collective-permute-start.1 = (bf16[576,128]{1,0:T(8,128)(2,1)}, bf16[576,128]{1,0:T(8,128)(2,1)}, u32[]{:S(2)}, u32[]{:S(2)}) collective-permute-start(bf16[576,128]{1,0:T(8,128)(2,1)} %get-tuple-element.6), channel_id=1, source_target_pairs={{0,8},{4,12},{8,0},{12,4},{1,9},{5,13},{9,1},{13,5},{2,10},{6,14},... | collective-permute-start | bytes 442376 | tf_op jit(solution)/shard_map/keys_over_ctx/ppermute | solution.py:27
  7.3 1.3 %collective-permute-start.2 = (bf16[576,128]{1,0:T(8,128)(2,1)}, bf16[576,128]{1,0:T(8,128)(2,1)S(1)}, u32[]{:S(2)}, u32[]{:S(2)}) collective-permute-start(bf16[576,128]{1,0:T(8,128)(2,1)} %get-tuple-element.6), channel_id=1, source_target_pairs={{0,12},{4,0},{8,4},{12,8},{1,13},{5,1},{9,5},{13,9},{2,14},{6,2},{... | collective-permute-start | bytes 442376 | tf_op jit(solution)/shard_map/keys_over_ctx/ppermute | solution.py:27
  8.7 2.2 %reshape.107 = bf16[4,2,16,16,192]{4,3,2,1,0:T(8,128)(2,1)S(1)} reshape(bf16[128,3072]{1,0:T(8,128)(2,1)} %param.6) | data formatting | bytes 1572864 | tf_op jit(solution)/shard_map/queries_to_latent/reshape | solution.py:121
  10.9 0.3 copy.25
  11.3 0.1 slice_convert_fusion
  11.4 6.5 %copy.23 = bf16[512,4096]{0,1:T(8,128)(2,1)} copy(bf16[512,4096]{1,0:T(8,128)(2,1)} %weight_ref.3) | data formatting | bytes 8388608 | tf_op args[2]
  17.9 2.3 %convolution_bitcast_fusion = f32[2,16,64,512]{3,2,1,0:T(8,128)S(1)} fusion(bf16[512,16,256]{0,2,1:T(8,128)(2,1)} %bitcast.66, bf16[2,16,64,192]{3,2,1,0:T(8,128)(2,1)S(1)} %bitcast.68), kind=kOutput, calls=%fused_computation.2 | convolution fusion | flops 268435456 | bytes 6815744 | tf_op jit(solution)/shard_map/queries_to_latent/chqd,lhd->chql/dot_general | solution.py:125
  20.2 0.8 fusion
  21.0 0.0 copy-start.4
  21.0 0.2 slice_bitcast_fusion.3
  21.2 0.1 iota.72
  21.3 0.1 iota.63
  21.4 0.2 copy-done.4
  21.7 0.6 and_select_fusion
  22.9 0.1 select_reduce_fusion
  23.6 0.1 add_select_fusion
  23.7 0.1 compare_select_fusion
  23.9 0.1 collective-permute-start.3
  23.9 1.6 %constant_dynamic-update-slice_fusion.5 = bf16[576,1024]{1,0:T(8,128)(2,1)} fusion(bf16[576,1024]{1,0:T(8,128)(2,1)} %get-tuple-element.5, bf16[576,128]{1,0:T(8,128)(2,1)} %collective-permute-done), kind=kLoop, calls=%fused_computation.68 | loop fusion | bytes 294912
  25.5 0.0 collective-permute-done.1
  25.5 0.5 collective-permute-start.4
  26.0 1.6 %constant_dynamic-update-slice_fusion.4 = bf16[576,1024]{1,0:T(8,128)(2,1)} fusion(bf16[576,1024]{1,0:T(8,128)(2,1)} %constant_dynamic-update-slice_fusion.5, bf16[576,128]{1,0:T(8,128)(2,1)} %collective-permute-done.1), kind=kLoop, calls=%fused_computation.67 | loop fusion | bytes 294912
  27.6 0.7 constant_dynamic-update-slice_fusion.3
  28.3 1.6 %bitcast_dynamic-update-slice_fusion = bf16[576,1024]{1,0:T(8,128)(2,1)} fusion(bf16[576,1024]{1,0:T(8,128)(2,1)} %constant_dynamic-update-slice_fusion.3, bf16[256,576]{0,1:T(8,128)(2,1)} %param.7, s32[]{:T(128)S(6)} %select_n.91), kind=kLoop, calls=%fused_computation.41 | loop fusion | bytes 294916
  29.9 0.0 collective-permute-start.5
  29.9 0.7 constant_dynamic-update-slice_fusion.2
  30.6 0.7 constant_dynamic-update-slice_fusion.1
  31.3 0.7 constant_dynamic-update-slice_fusion.keys_ref
  32.0 2.2 %copy-done = bf16[512,4096]{1,0:T(8,128)(2,1)S(1)} copy-done((bf16[512,4096]{1,0:T(8,128)(2,1)S(1)}, bf16[512,4096]{1,0:T(8,128)(2,1)}, u32[]{:S(2)}) %copy-start) | copy-done | bytes 4194328
  34.2 1.3 %copy-done.2 = bf16[576,1024]{1,0:T(8,128)(2,1)S(1)} copy-done((bf16[576,1024]{1,0:T(8,128)(2,1)S(1)}, bf16[576,1024]{1,0:T(8,128)(2,1)}, u32[]{:S(2)}) %copy-start.2) | copy-done | bytes 1179672
  35.5 13.4 %attention.3 = bf16[64,2048]{1,0:T(8,128)(2,1)S(1)} custom-call(bf16[16,64,576]{2,1,0:T(8,128)(2,1)S(1)} %get-tuple-element.8.q_ref, bf16[576,1024]{1,0:T(8,128)(2,1)S(1)} %copy-done.2, f32[64,1024]{1,0:T(8,128)S(1)} %get-tuple-element.10.bias_ref, bf16[512,4096]{1,0:T(8,128)(2,1)S(1)} %copy-done), custom_call_target="tpu_custom_call" | custom-call | flops 2415919104 | bytes 6815744 | tf_op jit(solution)/shard_map/attention/pallas_call | solution.py:58
  48.9 0.5 collective-permute-start.13
  49.4 1.7 %collective-permute-start.12 = (bf16[64,2048]{1,0:T(8,128)(2,1)S(1)}, bf16[64,2048]{1,0:T(8,128)(2,1)S(1)}, u32[]{:S(2)}, u32[]{:S(2)}) collective-permute-start(bf16[64,2048]{1,0:T(8,128)(2,1)S(1)} %attention.3), channel_id=1, source_target_pairs={{0,8},{4,12},{8,0},{12,4},{1,9},{5,13},{9,1},{13,5},{2,10},{6,14},... | collective-permute-start | bytes 786440 | tf_op jit(solution)/shard_map/attended_over_ctx/ppermute | solution.py:27
  51.1 2.2 %copy-done.1 = bf16[512,4096]{1,0:T(8,128)(2,1)S(1)} copy-done((bf16[512,4096]{1,0:T(8,128)(2,1)S(1)}, bf16[512,4096]{1,0:T(8,128)(2,1)}, u32[]{:S(2)}) %copy-start.1) | copy-done | bytes 4194328
  53.3 1.3 %copy-done.3 = bf16[576,1024]{1,0:T(8,128)(2,1)S(1)} copy-done((bf16[576,1024]{1,0:T(8,128)(2,1)S(1)}, bf16[576,1024]{1,0:T(8,128)(2,1)}, u32[]{:S(2)}) %copy-start.3) | copy-done | bytes 1179672
  54.6 13.4 %attention.2 = bf16[64,2048]{1,0:T(8,128)(2,1)S(1)} custom-call(bf16[16,64,576]{2,1,0:T(8,128)(2,1)S(1)} %get-tuple-element.7.q_ref, bf16[576,1024]{1,0:T(8,128)(2,1)S(1)} %copy-done.3, f32[64,1024]{1,0:T(8,128)S(1)} %get-tuple-element.9.bias_ref, bf16[512,4096]{1,0:T(8,128)(2,1)S(1)} %copy-done.1), custom_call_target="tpu_custom_call" | custom-call | flops 2415919104 | bytes 6815744 | tf_op jit(solution)/shard_map/attention/pallas_call | solution.py:58
  68.0 0.0 slice-start.1
  68.0 4.1 %collective-permute-start.8 = (bf16[64,2048]{1,0:T(8,128)(2,1)S(1)}, bf16[64,2048]{1,0:T(8,128)(2,1)S(1)}, u32[]{:S(2)}, u32[]{:S(2)}) collective-permute-start(bf16[64,2048]{1,0:T(8,128)(2,1)S(1)} %attention.2), channel_id=1, source_target_pairs={{0,12},{4,0},{8,4},{12,8},{1,13},{5,1},{9,5},{13,9},{2,14},{6,2},{... | collective-permute-start | bytes 786440 | tf_op jit(solution)/shard_map/attended_over_ctx/ppermute | solution.py:27
  72.0 1.0 collective-permute-start.6
  73.0 2.0 %collective-permute-done.12 = bf16[64,2048]{1,0:T(8,128)(2,1)S(1)} collective-permute-done((bf16[64,2048]{1,0:T(8,128)(2,1)S(1)}, bf16[64,2048]{1,0:T(8,128)(2,1)S(1)}, u32[]{:S(2)}, u32[]{:S(2)}) %collective-permute-start.12) | collective-permute-done | bytes 262176 | tf_op jit(solution)/shard_map/attended_over_ctx/ppermute | solution.py:27
  75.1 5.1 %fusion.9 = f32[256,1792]{1,0:T(8,128)S(1)} fusion(bf16[2048,1792]{1,0:T(8,128)(2,1)} %param.9, bf16[64,2048]{1,0:T(8,128)(2,1)S(1)} %collective-permute-done.13, bf16[64,2048]{1,0:T(8,128)(2,1)S(1)} %collective-permute-done.12, bf16[64,2048]{1,0:T(8,128)(2,1)S(1)} %collective-permute-done.11, bf16[64,2048]{1,0:T(8,128)(2,1)S(1)} %attention.3), kind=kOutput, calls=%fused_computation.14 | convolution fusion | flops 1883242496 | bytes 10223616 | tf_op jit(solution)/shard_map/out_product/dot_general | solution.py:139
  80.2 0.1 fusion.19
  80.3 0.1 collective-permute-start.14
  80.4 16.8 %collective-permute-done.7 = bf16[64,2048]{1,0:T(8,128)(2,1)S(1)} collective-permute-done((bf16[64,2048]{1,0:T(8,128)(2,1)S(1)}, bf16[64,2048]{1,0:T(8,128)(2,1)S(1)}, u32[]{:S(2)}, u32[]{:S(2)}) %collective-permute-start.7) | collective-permute-done | bytes 262176 | tf_op jit(solution)/shard_map/attended_over_ctx/ppermute | solution.py:27
  97.2 2.1 %fusion.1 = f32[256,1792]{1,0:T(8,128)S(1)} fusion(bf16[2048,1792]{1,0:T(8,128)(2,1)S(1)} %bitcast.75, bf16[64,2048]{1,0:T(8,128)(2,1)S(1)} %collective-permute-done.8, bf16[64,2048]{1,0:T(8,128)(2,1)S(1)} %collective-permute-done.7, bf16[64,2048]{1,0:T(8,128)(2,1)S(1)} %collective-permute-done.6, bf16[64,2048]{1,0:T(8,128)(2,1)S(1)} %attention.2), kind=kOutput, calls=%fused_computation.6 | convolution fusion | flops 1883242496 | bytes 10223616 | tf_op jit(solution)/shard_map/out_product/dot_general | solution.py:139
  99.2 0.1 fusion.18
  99.3 0.1 collective-permute-start.9
  99.4 0.1 bitcast_add_fusion
  99.5 1.6 %collective-permute-start.15 = (bf16[4,16,1792]{2,1,0:T(8,128)(2,1)S(1)}, bf16[4,16,1792]{2,1,0:T(8,128)(2,1)S(1)}, u32[]{:S(2)}, u32[]{:S(2)}) collective-permute-start(bf16[4,16,1792]{2,1,0:T(8,128)(2,1)S(1)} %fusion.23), channel_id=1, source_target_pairs={{0,2},{1,3},{2,0},{3,1},{4,6},{5,7},{6,4},{7,5},{8,10},{9,11},{10,... | collective-permute-start | bytes 688136 | tf_op jit(solution)/shard_map/sum_over_x/ppermute | solution.py:27
  101.1 0.1 collective-permute-done.9
  101.2 0.1 bitcast_add_fusion.1
  101.3 1.6 %collective-permute-start.10 = (bf16[4,16,1792]{2,1,0:T(8,128)(2,1)S(1)}, bf16[4,16,1792]{2,1,0:T(8,128)(2,1)S(1)}, u32[]{:S(2)}, u32[]{:S(2)}) collective-permute-start(bf16[4,16,1792]{2,1,0:T(8,128)(2,1)S(1)} %fusion.22), channel_id=1, source_target_pairs={{0,2},{1,3},{2,0},{3,1},{4,6},{5,7},{6,4},{7,5},{8,10},{9,11},{10,... | collective-permute-start | bytes 688136 | tf_op jit(solution)/shard_map/sum_over_x/ppermute | solution.py:27
  102.9 5.1 %collective-permute-done.15 = bf16[4,16,1792]{2,1,0:T(8,128)(2,1)S(1)} collective-permute-done((bf16[4,16,1792]{2,1,0:T(8,128)(2,1)S(1)}, bf16[4,16,1792]{2,1,0:T(8,128)(2,1)S(1)}, u32[]{:S(2)}, u32[]{:S(2)}) %collective-permute-start.15) | collective-permute-done | bytes 229408 | tf_op jit(solution)/shard_map/sum_over_x/ppermute | solution.py:27
  108.0 4.4 %collective-permute-done.10 = bf16[4,16,1792]{2,1,0:T(8,128)(2,1)S(1)} collective-permute-done((bf16[4,16,1792]{2,1,0:T(8,128)(2,1)S(1)}, bf16[4,16,1792]{2,1,0:T(8,128)(2,1)S(1)}, u32[]{:S(2)}, u32[]{:S(2)}) %collective-permute-start.10) | collective-permute-done | bytes 229408 | tf_op jit(solution)/shard_map/sum_over_x/ppermute | solution.py:27
  112.6 0.1 collective-permute-start.17
  112.6 2.7 %collective-permute-start.16 = (bf16[16,1792]{1,0:T(8,128)(2,1)S(1)}, bf16[16,1792]{1,0:T(8,128)(2,1)S(1)}, u32[]{:S(2)}, u32[]{:S(2)}) collective-permute-start(bf16[16,1792]{1,0:T(8,128)(2,1)S(1)} %get-tuple-element.13), channel_id=1, source_target_pairs={{0,12},{4,0},{8,4},{12,8},{1,13},{5,1},{9,5},{13,9},{2,14},{6,2},{... | collective-permute-start | bytes 172040 | tf_op jit(solution)/shard_map/columns_over_ctx/ppermute | solution.py:27
  115.3 0.8 collective-permute-start.19
  116.1 2.1 %collective-permute-start.18 = (bf16[16,1792]{1,0:T(8,128)(2,1)S(1)}, bf16[16,1792]{1,0:T(8,128)(2,1)S(1)}, u32[]{:S(2)}, u32[]{:S(2)}) collective-permute-start(bf16[16,1792]{1,0:T(8,128)(2,1)S(1)} %get-tuple-element.12), channel_id=1, source_target_pairs={{0,8},{4,12},{8,0},{12,4},{1,9},{5,13},{9,1},{13,5},{2,10},{6,14},... | collective-permute-start | bytes 172040 | tf_op jit(solution)/shard_map/columns_over_ctx/ppermute | solution.py:27
  118.2 1.4 %collective-permute-start.20 = (bf16[16,1792]{1,0:T(8,128)(2,1)S(1)}, bf16[16,1792]{1,0:T(8,128)(2,1)S(1)}, u32[]{:S(2)}, u32[]{:S(2)}) collective-permute-start(bf16[16,1792]{1,0:T(8,128)(2,1)S(1)} %get-tuple-element.11), channel_id=1, source_target_pairs={{0,4},{4,8},{8,12},{12,0},{1,5},{5,9},{9,13},{13,1},{2,6},{6,10},{... | collective-permute-start | bytes 172040 | tf_op jit(solution)/shard_map/columns_over_ctx/ppermute | solution.py:27
  119.7 3.7 %collective-permute-done.19 = bf16[16,1792]{1,0:T(8,128)(2,1)S(1)} collective-permute-done((bf16[16,1792]{1,0:T(8,128)(2,1)S(1)}, bf16[16,1792]{1,0:T(8,128)(2,1)S(1)}, u32[]{:S(2)}, u32[]{:S(2)}) %collective-permute-start.19) | collective-permute-done | bytes 57376 | tf_op jit(solution)/shard_map/columns_over_ctx/ppermute | solution.py:27
  123.4 2.0 %collective-permute-done.18 = bf16[16,1792]{1,0:T(8,128)(2,1)S(1)} collective-permute-done((bf16[16,1792]{1,0:T(8,128)(2,1)S(1)}, bf16[16,1792]{1,0:T(8,128)(2,1)S(1)}, u32[]{:S(2)}, u32[]{:S(2)}) %collective-permute-start.18) | collective-permute-done | bytes 57376 | tf_op jit(solution)/shard_map/columns_over_ctx/ppermute | solution.py:27
  125.5 0.8 constant_dynamic-slice_fusion
  (47 shorter events, 0.4 us)
Async XLA Ops:
  1.7 22.2 %collective-permute-start = (bf16[576,128]{1,0:T(8,128)(2,1)}, bf16[576,128]{1,0:T(8,128)(2,1)}, u32[]{:S(2)}, u32[]{:S(2)}) collective-permute-start(bf16[576,128]{1,0:T(8,128)(2,1)} %get-tuple-element.6), channel_id=1, source_target_pairs={{0,4},{4,8},{8,12},{12,0},{1,5},{5,9},{9,13},{13,1},{2,6},{6,10},{... | collective-permute-start | bytes 442376 | tf_op jit(solution)/shard_map/keys_over_ctx/ppermute | solution.py:27
  4.7 20.8 %collective-permute-start.1 = (bf16[576,128]{1,0:T(8,128)(2,1)}, bf16[576,128]{1,0:T(8,128)(2,1)}, u32[]{:S(2)}, u32[]{:S(2)}) collective-permute-start(bf16[576,128]{1,0:T(8,128)(2,1)} %get-tuple-element.6), channel_id=1, source_target_pairs={{0,8},{4,12},{8,0},{12,4},{1,9},{5,13},{9,1},{13,5},{2,10},{6,14},... | collective-permute-start | bytes 442376 | tf_op jit(solution)/shard_map/keys_over_ctx/ppermute | solution.py:27
  7.3 20.3 %collective-permute-start.2 = (bf16[576,128]{1,0:T(8,128)(2,1)}, bf16[576,128]{1,0:T(8,128)(2,1)S(1)}, u32[]{:S(2)}, u32[]{:S(2)}) collective-permute-start(bf16[576,128]{1,0:T(8,128)(2,1)} %get-tuple-element.6), channel_id=1, source_target_pairs={{0,12},{4,0},{8,4},{12,8},{1,13},{5,1},{9,5},{13,9},{2,14},{6,2},{... | collective-permute-start | bytes 442376 | tf_op jit(solution)/shard_map/keys_over_ctx/ppermute | solution.py:27
  21.0 0.7 copy-start.4
  23.9 6.1 %collective-permute-start.3 = (bf16[576,128]{1,0:T(8,128)(2,1)}, bf16[576,128]{1,0:T(8,128)(2,1)S(1)}, u32[]{:S(2)}, u32[]{:S(2)}) collective-permute-start(bf16[576,128]{1,0:T(8,128)(2,1)} %collective-permute-done), channel_id=1, source_target_pairs={{0,1},{1,0},{2,3},{3,2},{4,5},{5,4},{6,7},{7,6},{8,9},{9,8},{10,11... | collective-permute-start | bytes 442376 | tf_op jit(solution)/shard_map/keys_over_ctx/ppermute | solution.py:31
  25.5 5.1 %collective-permute-start.4 = (bf16[576,128]{1,0:T(8,128)(2,1)}, bf16[576,128]{1,0:T(8,128)(2,1)S(1)}, u32[]{:S(2)}, u32[]{:S(2)}) collective-permute-start(bf16[576,128]{1,0:T(8,128)(2,1)} %collective-permute-done.1), channel_id=1, source_target_pairs={{0,1},{1,0},{2,3},{3,2},{4,5},{5,4},{6,7},{7,6},{8,9},{9,8},{10,11... | collective-permute-start | bytes 442376 | tf_op jit(solution)/shard_map/keys_over_ctx/ppermute | solution.py:31
  29.9 1.4 %collective-permute-start.5 = (bf16[576,128]{1,0:T(8,128)(2,1)S(1)}, bf16[576,128]{1,0:T(8,128)(2,1)S(1)}, u32[]{:S(2)}, u32[]{:S(2)}) collective-permute-start(bf16[576,128]{1,0:T(8,128)(2,1)S(1)} %collective-permute-done.2), channel_id=1, source_target_pairs={{0,1},{1,0},{2,3},{3,2},{4,5},{5,4},{6,7},{7,6},{8,9},{9,8},{10,11... | collective-permute-start | bytes 442376 | tf_op jit(solution)/shard_map/keys_over_ctx/ppermute | solution.py:31
  32.0 2.2 %copy-start = (bf16[512,4096]{1,0:T(8,128)(2,1)S(1)}, bf16[512,4096]{1,0:T(8,128)(2,1)}, u32[]{:S(2)}) copy-start(bf16[512,4096]{1,0:T(8,128)(2,1)} %weight_ref.3) | copy-start | bytes 12582916
  34.2 1.3 %copy-start.2 = (bf16[576,1024]{1,0:T(8,128)(2,1)S(1)}, bf16[576,1024]{1,0:T(8,128)(2,1)}, u32[]{:S(2)}) copy-start(bf16[576,1024]{1,0:T(8,128)(2,1)} %constant_dynamic-update-slice_fusion.keys_ref) | copy-start | bytes 3538948
  48.9 23.1 %collective-permute-start.13 = (bf16[64,2048]{1,0:T(8,128)(2,1)S(1)}, bf16[64,2048]{1,0:T(8,128)(2,1)S(1)}, u32[]{:S(2)}, u32[]{:S(2)}) collective-permute-start(bf16[64,2048]{1,0:T(8,128)(2,1)S(1)} %attention.3), channel_id=1, source_target_pairs={{0,12},{4,0},{8,4},{12,8},{1,13},{5,1},{9,5},{13,9},{2,14},{6,2},{... | collective-permute-start | bytes 786440 | tf_op jit(solution)/shard_map/attended_over_ctx/ppermute | solution.py:27
  49.4 25.7 %collective-permute-start.12 = (bf16[64,2048]{1,0:T(8,128)(2,1)S(1)}, bf16[64,2048]{1,0:T(8,128)(2,1)S(1)}, u32[]{:S(2)}, u32[]{:S(2)}) collective-permute-start(bf16[64,2048]{1,0:T(8,128)(2,1)S(1)} %attention.3), channel_id=1, source_target_pairs={{0,8},{4,12},{8,0},{12,4},{1,9},{5,13},{9,1},{13,5},{2,10},{6,14},... | collective-permute-start | bytes 786440 | tf_op jit(solution)/shard_map/attended_over_ctx/ppermute | solution.py:27
  51.1 24.0 %collective-permute-start.11 = (bf16[64,2048]{1,0:T(8,128)(2,1)S(1)}, bf16[64,2048]{1,0:T(8,128)(2,1)S(1)}, u32[]{:S(2)}, u32[]{:S(2)}) collective-permute-start(bf16[64,2048]{1,0:T(8,128)(2,1)S(1)} %attention.3), channel_id=1, source_target_pairs={{0,4},{4,8},{8,12},{12,0},{1,5},{5,9},{9,13},{13,1},{2,6},{6,10},{... | collective-permute-start | bytes 786440 | tf_op jit(solution)/shard_map/attended_over_ctx/ppermute | solution.py:27
  51.1 2.2 %copy-start.1 = (bf16[512,4096]{1,0:T(8,128)(2,1)S(1)}, bf16[512,4096]{1,0:T(8,128)(2,1)}, u32[]{:S(2)}) copy-start(bf16[512,4096]{1,0:T(8,128)(2,1)} %weight_ref.3) | copy-start | bytes 12582916
  53.3 1.3 %copy-start.3 = (bf16[576,1024]{1,0:T(8,128)(2,1)S(1)}, bf16[576,1024]{1,0:T(8,128)(2,1)}, u32[]{:S(2)}) copy-start(bf16[576,1024]{1,0:T(8,128)(2,1)} %constant_dynamic-update-slice_fusion.keys_ref) | copy-start | bytes 3538948
  54.5 42.6 %slice-start = ((s8[7340032]{0:T(1024)(128)(4,1)}), s8[3145728]{0:T(1024)(128)(4,1)S(1)}, s32[]{:S(2)}) async-start(s8[7340032]{0:T(1024)(128)(4,1)} %bitcast.74), calls=%async_computation | async-start | bytes 6291456
  68.0 29.2 %slice-start.1 = ((s8[7340032]{0:T(1024)(128)(4,1)}), s8[4194304]{0:T(1024)(128)(4,1)S(1)}, s32[]{:S(2)}) async-start(s8[7340032]{0:T(1024)(128)(4,1)} %bitcast.74), calls=%async_computation.1 | async-start | bytes 8388608
  68.0 12.4 %collective-permute-start.8 = (bf16[64,2048]{1,0:T(8,128)(2,1)S(1)}, bf16[64,2048]{1,0:T(8,128)(2,1)S(1)}, u32[]{:S(2)}, u32[]{:S(2)}) collective-permute-start(bf16[64,2048]{1,0:T(8,128)(2,1)S(1)} %attention.2), channel_id=1, source_target_pairs={{0,12},{4,0},{8,4},{12,8},{1,13},{5,1},{9,5},{13,9},{2,14},{6,2},{... | collective-permute-start | bytes 786440 | tf_op jit(solution)/shard_map/attended_over_ctx/ppermute | solution.py:27
  72.0 25.1 %collective-permute-start.7 = (bf16[64,2048]{1,0:T(8,128)(2,1)S(1)}, bf16[64,2048]{1,0:T(8,128)(2,1)S(1)}, u32[]{:S(2)}, u32[]{:S(2)}) collective-permute-start(bf16[64,2048]{1,0:T(8,128)(2,1)S(1)} %attention.2), channel_id=1, source_target_pairs={{0,8},{4,12},{8,0},{12,4},{1,9},{5,13},{9,1},{13,5},{2,10},{6,14},... | collective-permute-start | bytes 786440 | tf_op jit(solution)/shard_map/attended_over_ctx/ppermute | solution.py:27
  72.0 25.1 %collective-permute-start.6 = (bf16[64,2048]{1,0:T(8,128)(2,1)S(1)}, bf16[64,2048]{1,0:T(8,128)(2,1)S(1)}, u32[]{:S(2)}, u32[]{:S(2)}) collective-permute-start(bf16[64,2048]{1,0:T(8,128)(2,1)S(1)} %attention.2), channel_id=1, source_target_pairs={{0,4},{4,8},{8,12},{12,0},{1,5},{5,9},{9,13},{13,1},{2,6},{6,10},{... | collective-permute-start | bytes 786440 | tf_op jit(solution)/shard_map/attended_over_ctx/ppermute | solution.py:27
  80.3 19.1 %collective-permute-start.14 = (bf16[4,2,16,1792]{3,2,0,1:T(8,128)(2,1)S(1)}, bf16[4,2,16,1792]{3,2,0,1:T(8,128)(2,1)S(1)}, u32[]{:S(2)}, u32[]{:S(2)}) collective-permute-start(bf16[4,2,16,1792]{3,2,0,1:T(8,128)(2,1)S(1)} %fusion.19), channel_id=1, source_target_pairs={{0,1},{1,0},{2,3},{3,2},{4,5},{5,4},{6,7},{7,6},{8,9},{9,8},{10,11... | collective-permute-start | bytes 1376264 | tf_op jit(solution)/shard_map/sum_over_cores/ppermute | solution.py:31
  99.3 1.9 %collective-permute-start.9 = (bf16[4,2,16,1792]{3,2,0,1:T(8,128)(2,1)S(1)}, bf16[4,2,16,1792]{3,2,0,1:T(8,128)(2,1)S(1)}, u32[]{:S(2)}, u32[]{:S(2)}) collective-permute-start(bf16[4,2,16,1792]{3,2,0,1:T(8,128)(2,1)S(1)} %fusion.18), channel_id=1, source_target_pairs={{0,1},{1,0},{2,3},{3,2},{4,5},{5,4},{6,7},{7,6},{8,9},{9,8},{10,11... | collective-permute-start | bytes 1376264 | tf_op jit(solution)/shard_map/sum_over_cores/ppermute | solution.py:31
  99.5 8.5 %collective-permute-start.15 = (bf16[4,16,1792]{2,1,0:T(8,128)(2,1)S(1)}, bf16[4,16,1792]{2,1,0:T(8,128)(2,1)S(1)}, u32[]{:S(2)}, u32[]{:S(2)}) collective-permute-start(bf16[4,16,1792]{2,1,0:T(8,128)(2,1)S(1)} %fusion.23), channel_id=1, source_target_pairs={{0,2},{1,3},{2,0},{3,1},{4,6},{5,7},{6,4},{7,5},{8,10},{9,11},{10,... | collective-permute-start | bytes 688136 | tf_op jit(solution)/shard_map/sum_over_x/ppermute | solution.py:27
  101.3 11.2 %collective-permute-start.10 = (bf16[4,16,1792]{2,1,0:T(8,128)(2,1)S(1)}, bf16[4,16,1792]{2,1,0:T(8,128)(2,1)S(1)}, u32[]{:S(2)}, u32[]{:S(2)}) collective-permute-start(bf16[4,16,1792]{2,1,0:T(8,128)(2,1)S(1)} %fusion.22), channel_id=1, source_target_pairs={{0,2},{1,3},{2,0},{3,1},{4,6},{5,7},{6,4},{7,5},{8,10},{9,11},{10,... | collective-permute-start | bytes 688136 | tf_op jit(solution)/shard_map/sum_over_x/ppermute | solution.py:27
  112.6 5.7 %collective-permute-start.17 = (bf16[16,1792]{1,0:T(8,128)(2,1)S(1)}, bf16[16,1792]{1,0:T(8,128)(2,1)S(1)}, u32[]{:S(2)}, u32[]{:S(2)}) collective-permute-start(bf16[16,1792]{1,0:T(8,128)(2,1)S(1)} %get-tuple-element.17), channel_id=1, source_target_pairs={{0,12},{4,0},{8,4},{12,8},{1,13},{5,1},{9,5},{13,9},{2,14},{6,2},{... | collective-permute-start | bytes 172040 | tf_op jit(solution)/shard_map/columns_over_ctx/ppermute | solution.py:27
  112.6 7.0 %collective-permute-start.16 = (bf16[16,1792]{1,0:T(8,128)(2,1)S(1)}, bf16[16,1792]{1,0:T(8,128)(2,1)S(1)}, u32[]{:S(2)}, u32[]{:S(2)}) collective-permute-start(bf16[16,1792]{1,0:T(8,128)(2,1)S(1)} %get-tuple-element.13), channel_id=1, source_target_pairs={{0,12},{4,0},{8,4},{12,8},{1,13},{5,1},{9,5},{13,9},{2,14},{6,2},{... | collective-permute-start | bytes 172040 | tf_op jit(solution)/shard_map/columns_over_ctx/ppermute | solution.py:27
  115.3 8.1 %collective-permute-start.19 = (bf16[16,1792]{1,0:T(8,128)(2,1)S(1)}, bf16[16,1792]{1,0:T(8,128)(2,1)S(1)}, u32[]{:S(2)}, u32[]{:S(2)}) collective-permute-start(bf16[16,1792]{1,0:T(8,128)(2,1)S(1)} %get-tuple-element.16), channel_id=1, source_target_pairs={{0,8},{4,12},{8,0},{12,4},{1,9},{5,13},{9,1},{13,5},{2,10},{6,14},... | collective-permute-start | bytes 172040 | tf_op jit(solution)/shard_map/columns_over_ctx/ppermute | solution.py:27
  116.1 9.2 %collective-permute-start.18 = (bf16[16,1792]{1,0:T(8,128)(2,1)S(1)}, bf16[16,1792]{1,0:T(8,128)(2,1)S(1)}, u32[]{:S(2)}, u32[]{:S(2)}) collective-permute-start(bf16[16,1792]{1,0:T(8,128)(2,1)S(1)} %get-tuple-element.12), channel_id=1, source_target_pairs={{0,8},{4,12},{8,0},{12,4},{1,9},{5,13},{9,1},{13,5},{2,10},{6,14},... | collective-permute-start | bytes 172040 | tf_op jit(solution)/shard_map/columns_over_ctx/ppermute | solution.py:27
  118.2 7.1 %collective-permute-start.21 = (bf16[16,1792]{1,0:T(8,128)(2,1)S(1)}, bf16[16,1792]{1,0:T(8,128)(2,1)S(1)}, u32[]{:S(2)}, u32[]{:S(2)}) collective-permute-start(bf16[16,1792]{1,0:T(8,128)(2,1)S(1)} %get-tuple-element.15), channel_id=1, source_target_pairs={{0,4},{4,8},{8,12},{12,0},{1,5},{5,9},{9,13},{13,1},{2,6},{6,10},{... | collective-permute-start | bytes 172040 | tf_op jit(solution)/shard_map/columns_over_ctx/ppermute | solution.py:27
  118.2 7.1 %collective-permute-start.20 = (bf16[16,1792]{1,0:T(8,128)(2,1)S(1)}, bf16[16,1792]{1,0:T(8,128)(2,1)S(1)}, u32[]{:S(2)}, u32[]{:S(2)}) collective-permute-start(bf16[16,1792]{1,0:T(8,128)(2,1)S(1)} %get-tuple-element.11), channel_id=1, source_target_pairs={{0,4},{4,8},{8,12},{12,0},{1,5},{5,9},{9,13},{13,1},{2,6},{6,10},{... | collective-permute-start | bytes 172040 | tf_op jit(solution)/shard_map/columns_over_ctx/ppermute | solution.py:27

commit v2 on v1

v2 whole, which is shorter than its diff:
```python
import functools
import math

import jax
import jax.numpy as jnp
from jax import lax
from jax.experimental import pallas as pl
from jax.experimental.pallas import tpu as pltpu
from jax.sharding import PartitionSpec as P

LAT = 512
NOPE = 128
ROPE = 64
VD = 128
HEAD = NOPE + ROPE
PROJ = NOPE + VD
CHUNKS = 2
SUB_ROWS = 256
MASKED = -1e30
VMEM_LIMIT = 20 * 1024 * 1024
LOG2E = 1.4426950408889634
SCALE = LOG2E / math.sqrt(HEAD)
SHORT = pl.CostEstimate(flops=1024, bytes_accessed=1024, transcendentals=0)


def lookup(table, indices):
    positions = jnp.arange(table.shape[0], dtype=jnp.int32)
    return jnp.sum(jnp.where(indices[..., None] == positions, table, 0), axis=-1)


def exchange(array, axis, size, bit):
    return lax.ppermute(array, axis, [(i, i ^ bit) for i in range(size)])


def tie_kernel(*refs):
    pass


def tie(array, after):
    if not after:
        return array
    anywhere = pl.BlockSpec(memory_space=pl.ANY)
    return pl.pallas_call(
        tie_kernel,
        out_shape=jax.ShapeDtypeStruct(array.shape, array.dtype),
        in_specs=[anywhere] * (1 + len(after)),
        out_specs=anywhere,
        input_output_aliases={0: 0},
        cost_estimate=SHORT,
    )(array, *after)


def gather_pieces(own, size, after=()):
    pieces = {0: own}
    bit = size // 2
    while bit:
        for offset in sorted(pieces, reverse=True):
            pieces[offset ^ bit] = exchange(pieces[offset], "ctx", size, bit)
        if bit == size // 2:
            pieces[bit] = tie(pieces[bit], after)
        bit //= 2
    return [pieces[offset] for offset in range(size)]


def absorb_kernel(owners, piece, q_ref, weight_ref, *out_refs):
    rows = q_ref.shape[0]
    chunks = len(out_refs)
    queries = q_ref[...].astype(jnp.float32)
    for head in range(out_refs[0].shape[0]):
        nope = queries[:, head * HEAD : head * HEAD + NOPE].astype(jnp.bfloat16)
        rope = queries[:, head * HEAD + NOPE : (head + 1) * HEAD] * SCALE
        absorbed = lax.dot_general(
            nope,
            weight_ref[:, head * PROJ : head * PROJ + NOPE],
            (((1,), (1,)), ((), ())),
            preferred_element_type=jnp.float32,
        )
        absorbed = (absorbed * SCALE).reshape(owners, chunks, piece, LAT)
        rope = rope.reshape(owners, chunks, piece, ROPE)
        for chunk, out_ref in enumerate(out_refs):
            part = absorbed[:, chunk].reshape(rows // chunks, LAT)
            out_ref[head, :, :LAT] = part.astype(jnp.bfloat16)
            part = rope[:, chunk].reshape(rows // chunks, ROPE)
            out_ref[head, :, LAT:] = part.astype(jnp.bfloat16)


def absorb(queries, w_kv_up, owners, piece):
    rows = queries.shape[0]
    head_count = w_kv_up.shape[1] // PROJ
    pair = 2
    return pl.pallas_call(
        functools.partial(absorb_kernel, owners, piece),
        grid=(head_count // pair,),
        out_shape=[
            jax.ShapeDtypeStruct((head_count, rows // CHUNKS, LAT + ROPE), jnp.bfloat16)
            for chunk in range(CHUNKS)
        ],
        in_specs=[
            pl.BlockSpec((rows, pair * HEAD), lambda i: (0, i)),
            pl.BlockSpec((LAT, pair * PROJ), lambda i: (0, i)),
        ],
        out_specs=[
            pl.BlockSpec((pair, rows // CHUNKS, LAT + ROPE), lambda i: (i, 0, 0))
            for chunk in range(CHUNKS)
        ],
        cost_estimate=SHORT,
    )(queries, w_kv_up)


def attention_kernel(count, q_ref, bias_ref, weight_ref, *refs):
    piece_refs = refs[:count]
    out_ref, keys_ref = refs[count:]

    @pl.when(pl.program_id(0) == 0)
    def _():
        start = 0
        for piece_ref in piece_refs:
            width = piece_ref.shape[1]
            keys_ref[:, start : start + width] = piece_ref[...]
            start += width

    heads, rows, depth = q_ref.shape
    amount = keys_ref.shape[1]
    group = max(1, min(heads, SUB_ROWS // rows))
    for first in range(0, heads, group):
        size = group * rows
        queries = q_ref[first : first + group].reshape(size, depth)
        scores = jnp.dot(queries, keys_ref[...], preferred_element_type=jnp.float32)
        scores = scores.reshape(group, rows, amount) + bias_ref[...][None]
        top = jnp.max(scores, axis=2, keepdims=True)
        weights = jnp.exp2(scores - top)
        total = jnp.sum(weights, axis=2, keepdims=True).reshape(size, 1)
        mixed = lax.dot_general(
            weights.reshape(size, amount).astype(jnp.bfloat16),
            keys_ref[:LAT, :],
            (((1,), (1,)), ((), ())),
            preferred_element_type=jnp.float32,
        )
        mixed = (mixed / total).astype(jnp.bfloat16)
        for head in range(first, first + group):
            result = jnp.dot(
                mixed[(head - first) * rows : (head - first + 1) * rows],
                weight_ref[:, head * PROJ + NOPE : (head + 1) * PROJ],
                preferred_element_type=jnp.float32,
            )
            out_ref[:, head * VD : (head + 1) * VD] = result.astype(jnp.bfloat16)


def attention(q_ext, bias, w_kv_up, key_pieces):
    head_count, rows, depth = q_ext.shape
    amount = sum(piece.shape[1] for piece in key_pieces)
    block = head_count // 2
    macs = head_count * rows * (amount * (depth + LAT) + LAT * VD)
    return pl.pallas_call(
        functools.partial(attention_kernel, len(key_pieces)),
        grid=(head_count // block,),
        out_shape=jax.ShapeDtypeStruct((rows, head_count * VD), jnp.bfloat16),
        in_specs=[
            pl.BlockSpec((block, rows, depth), lambda i: (i, 0, 0)),
            pl.BlockSpec((rows, amount), lambda i: (0, 0)),
            pl.BlockSpec((LAT, block * PROJ), lambda i: (0, i)),
        ]
        + [pl.BlockSpec(piece.shape, lambda i: (0, 0)) for piece in key_pieces],
        out_specs=pl.BlockSpec((rows, block * VD), lambda i: (0, i)),
        scratch_shapes=[pltpu.VMEM((depth, amount), jnp.bfloat16)],
        compiler_params=pltpu.CompilerParams(vmem_limit_bytes=VMEM_LIMIT),
        cost_estimate=SHORT,
    )(q_ext, bias, w_kv_up, *key_pieces)


def product_kernel(count, n_x, core_ref, weight_ref, *refs):
    piece_refs = refs[:count]
    sent_ref, kept_ref, rows_ref = refs[-3:]
    rows = piece_refs[0].shape[0]

    @pl.when(pl.program_id(0) == 0)
    def _():
        for index, piece_ref in enumerate(piece_refs):
            rows_ref[index * rows : (index + 1) * rows, :] = piece_ref[...]

    width = weight_ref.shape[1]
    result = jnp.dot(rows_ref[...], weight_ref[...], preferred_element_type=jnp.float32)
    result = result.reshape(count, n_x, 2, rows // (2 * n_x), width)
    is_first = core_ref[0] == 0
    for x in range(n_x):
        first, second = result[:, x, 0], result[:, x, 1]
        sent_ref[x] = jnp.where(is_first, second, first).astype(jnp.bfloat16)
        kept_ref[x] = jnp.where(is_first, first, second)


def product(pieces, w_out, core, n_x, after):
    rows, depth = pieces[0].shape
    count = len(pieces)
    columns = w_out.shape[1]
    tile = 256 if columns % 256 == 0 else columns
    shape = (n_x, count, rows // (2 * n_x), columns)
    block = pl.BlockSpec(shape[:3] + (tile,), lambda i: (0, 0, 0, i))
    return pl.pallas_call(
        functools.partial(product_kernel, count, n_x),
        grid=(columns // tile,),
        out_shape=[jax.ShapeDtypeStruct(shape, jnp.bfloat16), jax.ShapeDtypeStruct(shape, jnp.float32)],
        in_specs=[
            pl.BlockSpec(memory_space=pltpu.SMEM),
            pl.BlockSpec((depth, tile), lambda i: (0, i)),
        ]
        + [pl.BlockSpec((rows, depth), lambda i: (0, 0)) for piece in pieces]
        + [pl.BlockSpec(memory_space=pl.ANY) for array in after],
        out_specs=[block, block],
        scratch_shapes=[pltpu.VMEM((count * rows, depth), jnp.bfloat16)],
        compiler_params=pltpu.CompilerParams(vmem_limit_bytes=VMEM_LIMIT),
        cost_estimate=SHORT,
    )(core, w_out, *pieces, *after)


def output_kernel(n_ctx, ctx_ref, *refs):
    blocks, out_ref, sems = refs[:-2], refs[-2], refs[-1]
    rows, width = blocks[0].shape
    copies = []
    for index, block in enumerate(blocks):
        chunk, offset = index // n_ctx, index % n_ctx
        column = pl.multiple_of((ctx_ref[0] ^ offset) * width, 64)
        target = out_ref.at[pl.ds(chunk * rows, rows), pl.ds(column, width)]
        copies.append(pltpu.make_async_copy(block, target, sems.at[index]))
    for copy in copies:
        copy.start()
    for copy in copies:
        copy.wait()


def place_columns(results, ctx, n_ctx):
    rows, width = results[0][0].shape
    blocks = [block for result in results for block in result]
    return pl.pallas_call(
        functools.partial(output_kernel, n_ctx),
        out_shape=jax.ShapeDtypeStruct((rows * len(results), n_ctx * width), jnp.bfloat16),
        in_specs=[pl.BlockSpec(memory_space=pltpu.SMEM)]
        + [pl.BlockSpec(memory_space=pl.ANY) for block in blocks],
        out_specs=pl.BlockSpec(memory_space=pl.ANY),
        scratch_shapes=[pltpu.SemaphoreType.DMA((len(blocks),))],
    )(ctx, *blocks)


def place_columns_plain(results, ctx, n_ctx):
    rows, width = results[0][0].shape
    out = jnp.zeros((rows * len(results), n_ctx * width), jnp.bfloat16)
    for chunk, result in enumerate(results):
        for offset, block in enumerate(result):
            out = lax.dynamic_update_slice(out, block, (chunk * rows, (ctx ^ offset) * width))
    return out


def shards(n_ctx, n_head, queries, kv_rows, w_kv_up, w_out, stretch_order, prefix_len):
    query_rows = queries.shape[0]
    row_span = kv_rows.shape[0]
    cache_rows = row_span - query_rows
    half = row_span // 2
    columns = w_out.shape[1]
    n_x = n_head // 2
    owned = query_rows // n_head
    piece = owned // CHUNKS
    ctx = lax.axis_index("ctx")
    head = lax.axis_index("head")
    core = head % 2
    x = head // 2

    with jax.named_scope("keys_over_ctx"):
        kv_t = kv_rows.T
        own_half = jnp.where(core == 0, kv_t[:, :half], kv_t[:, half:])
        halves = gather_pieces(own_half, n_ctx)[1:]
        others = [exchange(array, "head", n_head, 1) for array in halves]
        key_pieces = [kv_t] + halves + others

    with jax.named_scope("visible"):
        query_pos = lookup(stretch_order, ctx) * query_rows + jnp.arange(query_rows, dtype=jnp.int32)
        offsets = jnp.arange(half, dtype=jnp.int32)
        remote = ctx ^ jnp.arange(1, n_ctx, dtype=jnp.int32)
        sources = jnp.concatenate([jnp.full((2,), ctx, jnp.int32), remote, remote])
        starts = jnp.concatenate(
            [
                jnp.array([0, half], jnp.int32),
                jnp.full((n_ctx - 1,), core * half, jnp.int32),
                jnp.full((n_ctx - 1,), (1 - core) * half, jnp.int32),
            ]
        )
        within = starts[:, None] + offsets[None, :]
        slot_ids = sources[:, None] * cache_rows + within
        key_pos = lookup(stretch_order, sources)[:, None] * query_rows + within - cache_rows
        cache_pos = jnp.where(slot_ids < prefix_len[0], -1, n_ctx * query_rows)
        first_seen = jnp.where(within < cache_rows, cache_pos, key_pos).reshape(-1)
        query_pos = query_pos.reshape(n_head, CHUNKS, piece).transpose(1, 0, 2)
        query_pos = query_pos.reshape(CHUNKS, query_rows // CHUNKS)
        bias = [
            jnp.where(first_seen[None, :] <= query_pos[chunk][:, None], 0.0, MASKED).astype(jnp.float32)
            for chunk in range(CHUNKS)
        ]

    with jax.named_scope("queries_to_latent"):
        q_ext = absorb(queries, w_kv_up, n_head, piece)

    results = []
    core_array = jnp.full((1,), core, jnp.int32)
    with jax.named_scope("attention"):
        attended = [attention(q, mask, w_kv_up, key_pieces) for q, mask in zip(q_ext, bias)]
    with jax.named_scope("attended_over_ctx"):
        gathered = [gather_pieces(own, n_ctx, attended[i + 1 :]) for i, own in enumerate(attended)]
    total = None
    for chunk in range(CHUNKS):
        after = attended[chunk + 1 :] if total is None else [total]
        with jax.named_scope("out_product"):
            sent, kept = product(gathered[chunk], w_out, core_array, n_x, after)
        with jax.named_scope("sum_over_cores"):
            summed = kept + exchange(sent, "head", n_head, 1).astype(jnp.float32)
        with jax.named_scope("sum_over_x"):
            total = lax.dynamic_index_in_dim(summed, x, 0, keepdims=False)
            for offset in range(1, n_x):
                sent = lax.dynamic_index_in_dim(summed, x ^ offset, 0, keepdims=False)
                sent = exchange(sent.astype(jnp.bfloat16), "head", n_head, 2 * offset)
                total = total + sent.astype(jnp.float32)
        with jax.named_scope("columns_over_ctx"):
            total = total.astype(jnp.bfloat16)
            blocks = [total[0]] + [exchange(total[d], "ctx", n_ctx, d) for d in range(1, n_ctx)]
        results.append(blocks)
    with jax.named_scope("output"):
        place = place_columns if columns % 128 == 0 and piece % 16 == 0 else place_columns_plain
        return place(results, jnp.full((1,), ctx, jnp.int32) if place is place_columns else ctx, n_ctx)


def solution(mesh):
    placed = (
        P(("groups", "ctx"), "head"),
        P(("groups", "ctx"), None),
        P(None, "head"),
        P("head", "ctx"),
        P("groups"),
        P("groups"),
    )
    return jax.shard_map(
        functools.partial(shards, mesh.shape["ctx"], mesh.shape["head"]),
        mesh=mesh,
        in_specs=placed,
        out_specs=P(("groups", "ctx", "head"), None),
        check_vma=False,
    )
```

time: 127 us -> 130 us (1.024)
  waiting for transfers between devices: 34.1 us -> 48.6 us
  Pallas kernels: 26.8 us -> 40.7 us
  local copies, waits for them, and re-layouts: 26.9 us -> 15.1 us
  matrix products: 9.47 us -> 0 us
  starting transfers between devices: 25.1 us -> 19.8 us
  other arithmetic: 2.21 us -> 3.62 us
    ppermute x22, waiting for transfers between devices: 34.1 us -> 48.6 us  [exchange(): return lax.ppermute(array, axis, [(i, i ^ bit) for i in range(size)])]
    pallas_call x2 -> x7, Pallas kernels: 26.8 us -> 40.7 us  [the longest x1 15.1 us: place_columns(): pl.pallas_call(functools.partial(output_kernel, n_ctx), out_shape=jax.Sha...]
    dot_general x3 -> x0, matrix products: 9.47 us -> none  [the longest x2 7.19 us: shards(): partial = jnp.dot(gathered, w_out, preferred_element_type=jnp.float32)]
    unnamed x22 -> x34, local copies, waits for them, and re-layouts: 22.2 us -> 13.6 us
    ppermute x22, starting transfers between devices: 25.1 us -> 19.8 us  [exchange(): return lax.ppermute(array, axis, [(i, i ^ bit) for i in range(size)])]
    reshape x2 -> x0, local copies, waits for them, and re-layouts: 2.59 us -> none  [shards(): queries.reshape(n_head, CHUNKS, piece, head_count, NOPE + ROPE)]
    reduce_sum x1 -> x2, other arithmetic: 0.09 us -> 2.06 us  [lookup(): jnp.sum(jnp.where(indices[..., None] == positions, table, 0), axis=-1)]
  transfers between devices with their start and end apart: 22 -> 22, of which waited for: 7 -> 12; matrix products, arithmetic and copies ran while one was open for 22% -> 3% of each run, Pallas kernels for 11% -> 10%
where the time goes in v2:
time: 130 us
  waiting for transfers between devices  48.6 us (37%)
  Pallas kernels  40.7 us (31%)
  starting transfers between devices  19.8 us (15%)
  local copies, waits for them, and re-layouts  15.1 us (12%)
  other arithmetic  3.62 us (3%)
  between operations  1.58 us (1%)
    ppermute x22, waiting for transfers between devices, exchange(): return lax.ppermute(array, axis, [(i, i ^ bit) for i in range(size)])  48.6 us
    ppermute x22, starting transfers between devices, exchange(): return lax.ppermute(array, axis, [(i, i ^ bit) for i in range(size)])  19.8 us
    pallas_call x1, Pallas kernels, place_columns(): pl.pallas_call(functools.partial(output_kernel, n_ctx), out_shape=jax.Sha...  15.1 us
    unnamed x34, local copies, waits for them, and re-layouts  13.6 us
    pallas_call x2, Pallas kernels, attention(): pl.pallas_call(functools.partial(attention_kernel, len(key_pieces)), grid...  10.6 us
    pallas_call x2, Pallas kernels, product(): pl.pallas_call(functools.partial(product_kernel, count, n_x), grid=(colum...  7.77 us
    pallas_call x1, Pallas kernels, absorb(): pl.pallas_call(functools.partial(absorb_kernel, owners, piece), grid=(hea...  7.23 us
  transfers between devices with their start and end apart: 22, of which 12 were waited for; matrix products, arithmetic and copies ran while one was open for 3% of the time, Pallas kernels for 10%

profile of v2, /device:TPU:0, one launch (start us, length us, event | category | flops | bytes accessed | tf_op | source)
XLA Modules:
  0.0 129.5 jit_solution(12274251321224074089)
XLA Ops:
  0.0 1.0 slice_select_fusion
  1.1 4.1 %collective-permute-start.1 = (bf16[576,128]{1,0:T(8,128)(2,1)S(1)}, bf16[576,128]{1,0:T(8,128)(2,1)S(1)}, u32[]{:S(2)}, u32[]{:S(2)}) collective-permute-start(bf16[576,128]{1,0:T(8,128)(2,1)S(1)} %slice_select_fusion), channel_id=1, source_target_pairs={{0,8},{4,12},{8,0},{12,4},{1,9},{5,13},{9,1},{13,5},{2,10},{6,14},... | collective-permute-start | bytes 442376 | tf_op jit(solution)/shard_map/keys_over_ctx/ppermute | solution.py:32
  5.2 1.6 %collective-permute-start = (bf16[576,128]{1,0:T(8,128)(2,1)S(1)}, bf16[576,128]{1,0:T(8,128)(2,1)S(1)}, u32[]{:S(2)}, u32[]{:S(2)}) collective-permute-start(bf16[576,128]{1,0:T(8,128)(2,1)S(1)} %slice_select_fusion), channel_id=1, source_target_pairs={{0,4},{4,0},{8,12},{12,8},{1,5},{5,1},{9,13},{13,9},{2,6},{6,2},{1... | collective-permute-start | bytes 442376 | tf_op jit(solution)/shard_map/keys_over_ctx/ppermute | solution.py:32
  7.4 1.3 %fusion.5 = s32[]{:T(128)} fusion(s32[4]{0:T(128)} %param.11, s32[]{:T(128)} %axis_index.23), kind=kLoop, calls=%fused_computation.29 | loop fusion | flops 11 | bytes 24 | tf_op jit(solution)/shard_map/visible/reduce_sum | solution.py:28
  9.4 0.1 broadcast_multiply_fusion.1
  9.5 0.7 select_reduce_fusion
  10.2 0.1 le.32
  10.3 0.1 le.29
  10.4 7.2 %queries_to_latent.1 = (bf16[16,64,576]{2,1,0:T(8,128)(2,1)}, bf16[16,64,576]{2,1,0:T(8,128)(2,1)}) custom-call(bf16[128,3072]{1,0:T(8,128)(2,1)} %q_ref.1, bf16[512,4096]{1,0:T(8,128)(2,1)} %weight_ref.7), custom_call_target="tpu_custom_call" | custom-call | flops 1024 | bytes 1024 | tf_op jit(solution)/shard_map/queries_to_latent/pallas_call | solution.py:91
  17.6 0.0 collective-permute-done.1.refs_2_
  17.6 0.5 collective-permute-start.2
  18.2 0.1 select_bitcast_fusion
  18.2 0.0 collective-permute-start.4
  18.2 0.0 collective-permute-done.refs_1_
  18.3 0.5 collective-permute-start.3
  18.7 4.1 %collective-permute-done.2.refs_3_ = bf16[576,128]{1,0:T(8,128)(2,1)S(1)} collective-permute-done((bf16[576,128]{1,0:T(8,128)(2,1)S(1)}, bf16[576,128]{1,0:T(8,128)(2,1)S(1)}, u32[]{:S(2)}, u32[]{:S(2)}) %collective-permute-start.2) | collective-permute-done | bytes 147488 | tf_op jit(solution)/shard_map/keys_over_ctx/ppermute | solution.py:32
  22.9 0.1 compare_select_fusion
  23.0 0.0 collective-permute-done.4.refs_5_
  23.0 1.2 collective-permute-done.5.refs_6_
  24.2 2.2 %copy-done = bf16[512,4096]{1,0:T(8,128)(2,1)S(1)} copy-done((bf16[512,4096]{1,0:T(8,128)(2,1)S(1)}, bf16[512,4096]{1,0:T(8,128)(2,1)}, u32[]{:S(2)}) %copy-start) | copy-done | bytes 4194328
  26.4 1.3 %copy-done.8 = bf16[16,64,576]{2,1,0:T(8,128)(2,1)S(1)} copy-done((bf16[16,64,576]{2,1,0:T(8,128)(2,1)S(1)}, bf16[16,64,576]{2,1,0:T(8,128)(2,1)}, u32[]{:S(2)}) %copy-start.8) | copy-done | bytes 1179672
  27.7 5.3 %attention.2.refs_0_ = bf16[64,2048]{1,0:T(8,128)(2,1)S(1)} custom-call(bf16[16,64,576]{2,1,0:T(8,128)(2,1)S(1)} %copy-done.8, f32[64,1024]{1,0:T(8,128)S(1)} %get-tuple-element.28.bias_ref, bf16[512,4096]{1,0:T(8,128)(2,1)S(1)} %copy-done, bf16[576,256]{1,0:T(8,128)(2,1)S(1)} %bitcast.36, bf16[576,128]{1,0:T(8,128)(2,1)S(1)} %collective-permute-done.refs_1_, ...), custom_call_target="tpu_custom_call" | custom-call | flops 1024 | bytes 1024 | tf_op jit(solution)/shard_map/attention/pallas_call | solution.py:154
  33.1 0.4 collective-permute-start.7
  33.5 0.4 collective-permute-start.6
  33.8 5.3 %attention.3.refs_1_.refs_4_.refs_0_ = bf16[64,2048]{1,0:T(8,128)(2,1)S(1)} custom-call(bf16[16,64,576]{2,1,0:T(8,128)(2,1)S(1)} %copy-done.7, f32[64,1024]{1,0:T(8,128)S(1)} %get-tuple-element.27.bias_ref, bf16[512,4096]{1,0:T(8,128)(2,1)S(1)} %copy-done, bf16[576,256]{1,0:T(8,128)(2,1)S(1)} %bitcast.37, bf16[576,128]{1,0:T(8,128)(2,1)S(1)} %collective-permute-done.refs_1_, ...), custom_call_target="tpu_custom_call" | custom-call | flops 1024 | bytes 1024 | tf_op jit(solution)/shard_map/attention/pallas_call | solution.py:154
  39.2 0.7 copy-done.3
  39.9 8.0 %collective-permute-done.7.refs_0_ = bf16[64,2048]{1,0:T(8,128)(2,1)S(1)} collective-permute-done((bf16[64,2048]{1,0:T(8,128)(2,1)S(1)}, bf16[64,2048]{1,0:T(8,128)(2,1)S(1)}, u32[]{:S(2)}, u32[]{:S(2)}) %collective-permute-start.7) | collective-permute-done | bytes 262176 | tf_op jit(solution)/shard_map/attended_over_ctx/ppermute | solution.py:32
  47.9 0.7 copy-done.9
  48.6 8.5 %collective-permute-done.8.refs_3_ = bf16[64,2048]{1,0:T(8,128)(2,1)S(1)} collective-permute-done((bf16[64,2048]{1,0:T(8,128)(2,1)}, bf16[64,2048]{1,0:T(8,128)(2,1)S(1)}, u32[]{:S(2)}, u32[]{:S(2)}) %collective-permute-start.8) | collective-permute-done | bytes 262176 | tf_op jit(solution)/shard_map/attended_over_ctx/ppermute | solution.py:32
  57.1 3.1 %copy-done.1 = bf16[2048,1792]{1,0:T(8,128)(2,1)S(1)} copy-done((bf16[2048,1792]{1,0:T(8,128)(2,1)S(1)}, bf16[2048,1792]{1,0:T(8,128)(2,1)}, u32[]{:S(2)}) %copy-start.1) | copy-done | bytes 7340056
  60.1 0.9 copy-done.4
  61.1 0.9 copy-done.10
  62.0 3.9 %out_product.2 = (bf16[2,4,16,1792]{3,2,1,0:T(8,128)(2,1)S(1)}, f32[2,4,16,1792]{3,2,1,0:T(8,128)S(1)}) custom-call(s32[1]{0:T(128)} %bitcast.1.core_ref, bf16[2048,1792]{1,0:T(8,128)(2,1)S(1)} %copy-done.1, bf16[64,2048]{1,0:T(8,128)(2,1)S(1)} %attention.2.refs_0_, bf16[64,2048]{1,0:T(8,128)(2,1)S(1)} %collective-permute-done.6.refs_1_, ...), custom_call_target="tpu_custom_call" | custom-call | flops 1024 | bytes 1024 | tf_op jit(solution)/shard_map/out_product/pallas_call | solution.py:198
  65.9 0.1 collective-permute-start.9
  66.0 0.1 collective-permute-start.15
  66.1 1.7 %collective-permute-done.9 = bf16[2,4,16,1792]{3,2,1,0:T(8,128)(2,1)S(1)} collective-permute-done((bf16[2,4,16,1792]{3,2,1,0:T(8,128)(2,1)S(1)}, bf16[2,4,16,1792]{3,2,1,0:T(8,128)(2,1)S(1)}, u32[]{:S(2)}, u32[]{:S(2)}) %collective-permute-start.9) | collective-permute-done | bytes 458784 | tf_op jit(solution)/shard_map/sum_over_cores/ppermute | solution.py:32
  67.8 0.1 convert_add_fusion.1
  67.9 1.6 %collective-permute-start.10 = (bf16[4,16,1792]{2,1,0:T(8,128)(2,1)S(1)}, bf16[4,16,1792]{2,1,0:T(8,128)(2,1)S(1)}, u32[]{:S(2)}, u32[]{:S(2)}) collective-permute-start(bf16[4,16,1792]{2,1,0:T(8,128)(2,1)S(1)} %fusion.2), channel_id=1, source_target_pairs={{0,2},{1,3},{2,0},{3,1},{4,6},{5,7},{6,4},{7,5},{8,10},{9,11},{10,... | collective-permute-start | bytes 688136 | tf_op jit(solution)/shard_map/sum_over_x/ppermute | solution.py:32
  69.5 0.3 collective-permute-start.14
  69.8 11.3 %collective-permute-done.15.refs_2_ = bf16[64,2048]{1,0:T(8,128)(2,1)S(1)} collective-permute-done((bf16[64,2048]{1,0:T(8,128)(2,1)S(1)}, bf16[64,2048]{1,0:T(8,128)(2,1)S(1)}, u32[]{:S(2)}, u32[]{:S(2)}) %collective-permute-start.15) | collective-permute-done | bytes 262176 | tf_op jit(solution)/shard_map/attended_over_ctx/ppermute | solution.py:32
  81.1 0.0 collective-permute-start.16
  81.1 0.0 collective-permute-done.10
  81.2 1.9 %collective-permute-done.14.refs_1_ = bf16[64,2048]{1,0:T(8,128)(2,1)S(1)} collective-permute-done((bf16[64,2048]{1,0:T(8,128)(2,1)S(1)}, bf16[64,2048]{1,0:T(8,128)(2,1)S(1)}, u32[]{:S(2)}, u32[]{:S(2)}) %collective-permute-start.14) | collective-permute-done | bytes 262176 | tf_op jit(solution)/shard_map/attended_over_ctx/ppermute | solution.py:32
  83.1 6.2 %collective-permute-done.16.refs_3_ = bf16[64,2048]{1,0:T(8,128)(2,1)S(1)} collective-permute-done((bf16[64,2048]{1,0:T(8,128)(2,1)S(1)}, bf16[64,2048]{1,0:T(8,128)(2,1)S(1)}, u32[]{:S(2)}, u32[]{:S(2)}) %collective-permute-start.16) | collective-permute-done | bytes 262176 | tf_op jit(solution)/shard_map/attended_over_ctx/ppermute | solution.py:32
  89.3 3.1 %copy-done.2 = bf16[2048,1792]{1,0:T(8,128)(2,1)S(1)} copy-done((bf16[2048,1792]{1,0:T(8,128)(2,1)S(1)}, bf16[2048,1792]{1,0:T(8,128)(2,1)}, u32[]{:S(2)}) %copy-start.2) | copy-done | bytes 7340056
  92.4 3.9 %out_product.3 = (bf16[2,4,16,1792]{3,2,1,0:T(8,128)(2,1)S(1)}, f32[2,4,16,1792]{3,2,1,0:T(8,128)S(1)}) custom-call(s32[1]{0:T(128)} %bitcast.1.core_ref, bf16[2048,1792]{1,0:T(8,128)(2,1)S(1)} %copy-done.2, bf16[64,2048]{1,0:T(8,128)(2,1)S(1)} %copy-done.5, bf16[64,2048]{1,0:T(8,128)(2,1)S(1)} %collective-permute-done.14.refs_1_, ...), custom_call_target="tpu_custom_call" | custom-call | flops 1024 | bytes 1024 | tf_op jit(solution)/shard_map/out_product/pallas_call | solution.py:198
  96.3 0.1 collective-permute-start.17
  96.4 1.8 %collective-permute-done.17 = bf16[2,4,16,1792]{3,2,1,0:T(8,128)(2,1)S(1)} collective-permute-done((bf16[2,4,16,1792]{3,2,1,0:T(8,128)(2,1)S(1)}, bf16[2,4,16,1792]{3,2,1,0:T(8,128)(2,1)S(1)}, u32[]{:S(2)}, u32[]{:S(2)}) %collective-permute-start.17) | collective-permute-done | bytes 458784 | tf_op jit(solution)/shard_map/sum_over_cores/ppermute | solution.py:32
  98.2 0.1 convert_add_fusion
  98.3 1.6 %collective-permute-start.18 = (bf16[4,16,1792]{2,1,0:T(8,128)(2,1)S(1)}, bf16[4,16,1792]{2,1,0:T(8,128)(2,1)S(1)}, u32[]{:S(2)}, u32[]{:S(2)}) collective-permute-start(bf16[4,16,1792]{2,1,0:T(8,128)(2,1)S(1)} %fusion.3), channel_id=1, source_target_pairs={{0,2},{1,3},{2,0},{3,1},{4,6},{5,7},{6,4},{7,5},{8,10},{9,11},{10,... | collective-permute-start | bytes 688136 | tf_op jit(solution)/shard_map/sum_over_x/ppermute | solution.py:32
  99.9 0.6 slice_bitcast_fusion.4
  100.5 0.0 collective-permute-start.13
  100.5 1.7 %collective-permute-start.12 = (bf16[16,1792]{1,0:T(8,128)(2,1)S(1)}, bf16[16,1792]{1,0:T(8,128)(2,1)S(1)}, u32[]{:S(2)}, u32[]{:S(2)}) collective-permute-start(bf16[16,1792]{1,0:T(8,128)(2,1)S(1)} %get-tuple-element.24), channel_id=1, source_target_pairs={{0,8},{4,12},{8,0},{12,4},{1,9},{5,13},{9,1},{13,5},{2,10},{6,14},... | collective-permute-start | bytes 172040 | tf_op jit(solution)/shard_map/columns_over_ctx/ppermute | solution.py:32
  102.2 2.6 %collective-permute-start.11 = (bf16[16,1792]{1,0:T(8,128)(2,1)S(1)}, bf16[16,1792]{1,0:T(8,128)(2,1)S(1)}, u32[]{:S(2)}, u32[]{:S(2)}) collective-permute-start(bf16[16,1792]{1,0:T(8,128)(2,1)S(1)} %get-tuple-element.25), channel_id=1, source_target_pairs={{0,4},{4,0},{8,12},{12,8},{1,5},{5,1},{9,13},{13,9},{2,6},{6,2},{1... | collective-permute-start | bytes 172040 | tf_op jit(solution)/shard_map/columns_over_ctx/ppermute | solution.py:32
  104.9 1.1 collective-permute-done.18
  106.1 0.6 slice_bitcast_fusion
  106.7 0.0 collective-permute-start.21
  106.7 1.7 %collective-permute-start.20 = (bf16[16,1792]{1,0:T(8,128)(2,1)S(1)}, bf16[16,1792]{1,0:T(8,128)(2,1)S(1)}, u32[]{:S(2)}, u32[]{:S(2)}) collective-permute-start(bf16[16,1792]{1,0:T(8,128)(2,1)S(1)} %get-tuple-element.20), channel_id=1, source_target_pairs={{0,8},{4,12},{8,0},{12,4},{1,9},{5,13},{9,1},{13,5},{2,10},{6,14},... | collective-permute-start | bytes 172040 | tf_op jit(solution)/shard_map/columns_over_ctx/ppermute | solution.py:32
  108.4 2.6 %collective-permute-start.19 = (bf16[16,1792]{1,0:T(8,128)(2,1)S(1)}, bf16[16,1792]{1,0:T(8,128)(2,1)S(1)}, u32[]{:S(2)}, u32[]{:S(2)}) collective-permute-start(bf16[16,1792]{1,0:T(8,128)(2,1)S(1)} %get-tuple-element.21), channel_id=1, source_target_pairs={{0,4},{4,0},{8,12},{12,8},{1,5},{5,1},{9,13},{13,9},{2,6},{6,2},{1... | collective-permute-start | bytes 172040 | tf_op jit(solution)/shard_map/columns_over_ctx/ppermute | solution.py:32
  111.1 1.8 %collective-permute-done.21.refs_7_ = bf16[16,1792]{1,0:T(8,128)(2,1)S(1)} collective-permute-done((bf16[16,1792]{1,0:T(8,128)(2,1)S(1)}, bf16[16,1792]{1,0:T(8,128)(2,1)S(1)}, u32[]{:S(2)}, u32[]{:S(2)}) %collective-permute-start.21) | collective-permute-done | bytes 57376 | tf_op jit(solution)/shard_map/columns_over_ctx/ppermute | solution.py:32
  112.9 0.9 collective-permute-done.20.refs_6_
  113.8 0.6 copy-done.15
  114.4 0.0 copy-done.16
  114.5 15.1 %output.1 = bf16[32,7168]{1,0:T(8,128)(2,1)} custom-call(s32[1]{0:T(128)} %bitcast.ctx_ref, bf16[16,1792]{1,0:T(8,128)(2,1)} %get-tuple-element.26.refs_0_, bf16[16,1792]{1,0:T(8,128)(2,1)} %copy-done.13, bf16[16,1792]{1,0:T(8,128)(2,1)} %copy-done.12, bf16[16,1792]{1,0:T(8,128)(2,1)} %copy-done.11, bf16[16,1792]{1,0:T(8,128)(2,1)} %get-tuple-element.22.refs_4_, ...), custom_call_target="tpu_custom_call" | custom-call | tf_op jit(solution)/shard_map/output/pallas_call | solution.py:233
  (45 shorter events, 0.3 us)
Async XLA Ops:
  0.0 24.2 %copy-start.6 = (bf16[256,576]{0,1:T(8,128)(2,1)S(1)}, bf16[256,576]{0,1:T(8,128)(2,1)}, u32[]{:S(2)}) copy-start(bf16[256,576]{0,1:T(8,128)(2,1)} %param.8) | copy-start | bytes 884740
  1.1 16.6 %collective-permute-start.1 = (bf16[576,128]{1,0:T(8,128)(2,1)S(1)}, bf16[576,128]{1,0:T(8,128)(2,1)S(1)}, u32[]{:S(2)}, u32[]{:S(2)}) collective-permute-start(bf16[576,128]{1,0:T(8,128)(2,1)S(1)} %slice_select_fusion), channel_id=1, source_target_pairs={{0,8},{4,12},{8,0},{12,4},{1,9},{5,13},{9,1},{13,5},{2,10},{6,14},... | collective-permute-start | bytes 442376 | tf_op jit(solution)/shard_map/keys_over_ctx/ppermute | solution.py:32
  5.2 13.1 %collective-permute-start = (bf16[576,128]{1,0:T(8,128)(2,1)S(1)}, bf16[576,128]{1,0:T(8,128)(2,1)S(1)}, u32[]{:S(2)}, u32[]{:S(2)}) collective-permute-start(bf16[576,128]{1,0:T(8,128)(2,1)S(1)} %slice_select_fusion), channel_id=1, source_target_pairs={{0,4},{4,0},{8,12},{12,8},{1,5},{5,1},{9,13},{13,9},{2,6},{6,2},{1... | collective-permute-start | bytes 442376 | tf_op jit(solution)/shard_map/keys_over_ctx/ppermute | solution.py:32
  17.6 5.2 %collective-permute-start.2 = (bf16[576,128]{1,0:T(8,128)(2,1)S(1)}, bf16[576,128]{1,0:T(8,128)(2,1)S(1)}, u32[]{:S(2)}, u32[]{:S(2)}) collective-permute-start(bf16[576,128]{1,0:T(8,128)(2,1)S(1)} %collective-permute-done.1.refs_2_), channel_id=1, source_target_pairs={{0,4},{4,0},{8,12},{12,8},{1,5},{5,1},{9,13},{13,9},{2,6},{6,2},{1... | collective-permute-start | bytes 442376 | tf_op jit(solution)/shard_map/keys_over_ctx/ppermute | solution.py:32
  18.2 4.7 %collective-permute-start.4 = (bf16[576,128]{1,0:T(8,128)(2,1)S(1)}, bf16[576,128]{1,0:T(8,128)(2,1)S(1)}, u32[]{:S(2)}, u32[]{:S(2)}) collective-permute-start(bf16[576,128]{1,0:T(8,128)(2,1)S(1)} %collective-permute-done.1.refs_2_), channel_id=1, source_target_pairs={{0,1},{1,0},{2,3},{3,2},{4,5},{5,4},{6,7},{7,6},{8,9},{9,8},{10,11... | collective-permute-start | bytes 442376 | tf_op jit(solution)/shard_map/keys_over_ctx/ppermute | solution.py:32
  18.3 4.7 %collective-permute-start.3 = (bf16[576,128]{1,0:T(8,128)(2,1)S(1)}, bf16[576,128]{1,0:T(8,128)(2,1)S(1)}, u32[]{:S(2)}, u32[]{:S(2)}) collective-permute-start(bf16[576,128]{1,0:T(8,128)(2,1)S(1)} %collective-permute-done.refs_1_), channel_id=1, source_target_pairs={{0,1},{1,0},{2,3},{3,2},{4,5},{5,4},{6,7},{7,6},{8,9},{9,8},{10,11... | collective-permute-start | bytes 442376 | tf_op jit(solution)/shard_map/keys_over_ctx/ppermute | solution.py:32
  22.8 1.4 %collective-permute-start.5 = (bf16[576,128]{1,0:T(8,128)(2,1)S(1)}, bf16[576,128]{1,0:T(8,128)(2,1)S(1)}, u32[]{:S(2)}, u32[]{:S(2)}) collective-permute-start(bf16[576,128]{1,0:T(8,128)(2,1)S(1)} %collective-permute-done.2.refs_3_), channel_id=1, source_target_pairs={{0,1},{1,0},{2,3},{3,2},{4,5},{5,4},{6,7},{7,6},{8,9},{9,8},{10,11... | collective-permute-start | bytes 442376 | tf_op jit(solution)/shard_map/keys_over_ctx/ppermute | solution.py:32
  24.2 2.2 %copy-start = (bf16[512,4096]{1,0:T(8,128)(2,1)S(1)}, bf16[512,4096]{1,0:T(8,128)(2,1)}, u32[]{:S(2)}) copy-start(bf16[512,4096]{1,0:T(8,128)(2,1)} %weight_ref.7) | copy-start | bytes 12582916
  26.4 1.3 %copy-start.8 = (bf16[16,64,576]{2,1,0:T(8,128)(2,1)S(1)}, bf16[16,64,576]{2,1,0:T(8,128)(2,1)}, u32[]{:S(2)}) copy-start(bf16[16,64,576]{2,1,0:T(8,128)(2,1)} %get-tuple-element.11.q_ref) | copy-start | bytes 3538948
  27.7 6.1 %copy-start.7 = (bf16[16,64,576]{2,1,0:T(8,128)(2,1)S(1)}, bf16[16,64,576]{2,1,0:T(8,128)(2,1)}, u32[]{:S(2)}) copy-start(bf16[16,64,576]{2,1,0:T(8,128)(2,1)} %get-tuple-element.12.q_ref) | copy-start | bytes 3538948
  33.1 14.8 %collective-permute-start.7 = (bf16[64,2048]{1,0:T(8,128)(2,1)S(1)}, bf16[64,2048]{1,0:T(8,128)(2,1)S(1)}, u32[]{:S(2)}, u32[]{:S(2)}) collective-permute-start(bf16[64,2048]{1,0:T(8,128)(2,1)S(1)} %attention.2.refs_0_), channel_id=1, source_target_pairs={{0,8},{4,12},{8,0},{12,4},{1,9},{5,13},{9,1},{13,5},{2,10},{6,14},... | collective-permute-start | bytes 786440 | tf_op jit(solution)/shard_map/attended_over_ctx/ppermute | solution.py:32
  33.5 15.1 %collective-permute-start.6 = (bf16[64,2048]{1,0:T(8,128)(2,1)S(1)}, bf16[64,2048]{1,0:T(8,128)(2,1)S(1)}, u32[]{:S(2)}, u32[]{:S(2)}) collective-permute-start(bf16[64,2048]{1,0:T(8,128)(2,1)S(1)} %attention.2.refs_0_), channel_id=1, source_target_pairs={{0,4},{4,0},{8,12},{12,8},{1,5},{5,1},{9,13},{13,9},{2,6},{6,2},{1... | collective-permute-start | bytes 786440 | tf_op jit(solution)/shard_map/attended_over_ctx/ppermute | solution.py:32
  39.2 0.7 copy-start.3
  47.9 0.7 copy-start.9
  48.6 8.5 %collective-permute-start.8 = (bf16[64,2048]{1,0:T(8,128)(2,1)}, bf16[64,2048]{1,0:T(8,128)(2,1)S(1)}, u32[]{:S(2)}, u32[]{:S(2)}) collective-permute-start(bf16[64,2048]{1,0:T(8,128)(2,1)} %attended_over_ctx.1.refs_2_), channel_id=1, source_target_pairs={{0,4},{4,0},{8,12},{12,8},{1,5},{5,1},{9,13},{13,9},{2,6},{6,2},{1... | collective-permute-start | bytes 786440 | tf_op jit(solution)/shard_map/attended_over_ctx/ppermute | solution.py:32
  57.1 3.1 %copy-start.1 = (bf16[2048,1792]{1,0:T(8,128)(2,1)S(1)}, bf16[2048,1792]{1,0:T(8,128)(2,1)}, u32[]{:S(2)}) copy-start(bf16[2048,1792]{1,0:T(8,128)(2,1)} %weight_ref.9) | copy-start | bytes 22020100
  60.1 0.9 copy-start.4
  61.1 0.9 copy-start.10
  62.0 4.0 %copy-start.5 = (bf16[64,2048]{1,0:T(8,128)(2,1)S(1)}, bf16[64,2048]{1,0:T(8,128)(2,1)}, u32[]{:S(2)}) copy-start(bf16[64,2048]{1,0:T(8,128)(2,1)} %copy-done.3) | copy-start | bytes 786436
  65.9 1.9 %collective-permute-start.9 = (bf16[2,4,16,1792]{3,2,1,0:T(8,128)(2,1)S(1)}, bf16[2,4,16,1792]{3,2,1,0:T(8,128)(2,1)S(1)}, u32[]{:S(2)}, u32[]{:S(2)}) collective-permute-start(bf16[2,4,16,1792]{3,2,1,0:T(8,128)(2,1)S(1)} %get-tuple-element.14), channel_id=1, source_target_pairs={{0,1},{1,0},{2,3},{3,2},{4,5},{5,4},{6,7},{7,6},{8,9},{9,8},{10,11... | collective-permute-start | bytes 1376264 | tf_op jit(solution)/shard_map/sum_over_cores/ppermute | solution.py:32
  66.0 15.0 %collective-permute-start.15 = (bf16[64,2048]{1,0:T(8,128)(2,1)S(1)}, bf16[64,2048]{1,0:T(8,128)(2,1)S(1)}, u32[]{:S(2)}, u32[]{:S(2)}) collective-permute-start(bf16[64,2048]{1,0:T(8,128)(2,1)S(1)} %copy-done.5), channel_id=1, source_target_pairs={{0,8},{4,12},{8,0},{12,4},{1,9},{5,13},{9,1},{13,5},{2,10},{6,14},... | collective-permute-start | bytes 786440 | tf_op jit(solution)/shard_map/attended_over_ctx/ppermute | solution.py:32
  67.9 13.2 %collective-permute-start.10 = (bf16[4,16,1792]{2,1,0:T(8,128)(2,1)S(1)}, bf16[4,16,1792]{2,1,0:T(8,128)(2,1)S(1)}, u32[]{:S(2)}, u32[]{:S(2)}) collective-permute-start(bf16[4,16,1792]{2,1,0:T(8,128)(2,1)S(1)} %fusion.2), channel_id=1, source_target_pairs={{0,2},{1,3},{2,0},{3,1},{4,6},{5,7},{6,4},{7,5},{8,10},{9,11},{10,... | collective-permute-start | bytes 688136 | tf_op jit(solution)/shard_map/sum_over_x/ppermute | solution.py:32
  69.5 13.6 %collective-permute-start.14 = (bf16[64,2048]{1,0:T(8,128)(2,1)S(1)}, bf16[64,2048]{1,0:T(8,128)(2,1)S(1)}, u32[]{:S(2)}, u32[]{:S(2)}) collective-permute-start(bf16[64,2048]{1,0:T(8,128)(2,1)S(1)} %copy-done.5), channel_id=1, source_target_pairs={{0,4},{4,0},{8,12},{12,8},{1,5},{5,1},{9,13},{13,9},{2,6},{6,2},{1... | collective-permute-start | bytes 786440 | tf_op jit(solution)/shard_map/attended_over_ctx/ppermute | solution.py:32
  81.1 8.2 %collective-permute-start.16 = (bf16[64,2048]{1,0:T(8,128)(2,1)S(1)}, bf16[64,2048]{1,0:T(8,128)(2,1)S(1)}, u32[]{:S(2)}, u32[]{:S(2)}) collective-permute-start(bf16[64,2048]{1,0:T(8,128)(2,1)S(1)} %collective-permute-done.15.refs_2_), channel_id=1, source_target_pairs={{0,4},{4,0},{8,12},{12,8},{1,5},{5,1},{9,13},{13,9},{2,6},{6,2},{1... | collective-permute-start | bytes 786440 | tf_op jit(solution)/shard_map/attended_over_ctx/ppermute | solution.py:32
  89.3 3.1 %copy-start.2 = (bf16[2048,1792]{1,0:T(8,128)(2,1)S(1)}, bf16[2048,1792]{1,0:T(8,128)(2,1)}, u32[]{:S(2)}) copy-start(bf16[2048,1792]{1,0:T(8,128)(2,1)} %weight_ref.9) | copy-start | bytes 22020100
  96.3 1.9 %collective-permute-start.17 = (bf16[2,4,16,1792]{3,2,1,0:T(8,128)(2,1)S(1)}, bf16[2,4,16,1792]{3,2,1,0:T(8,128)(2,1)S(1)}, u32[]{:S(2)}, u32[]{:S(2)}) collective-permute-start(bf16[2,4,16,1792]{3,2,1,0:T(8,128)(2,1)S(1)} %get-tuple-element.16), channel_id=1, source_target_pairs={{0,1},{1,0},{2,3},{3,2},{4,5},{5,4},{6,7},{7,6},{8,9},{9,8},{10,11... | collective-permute-start | bytes 1376264 | tf_op jit(solution)/shard_map/sum_over_cores/ppermute | solution.py:32
  98.3 7.7 %collective-permute-start.18 = (bf16[4,16,1792]{2,1,0:T(8,128)(2,1)S(1)}, bf16[4,16,1792]{2,1,0:T(8,128)(2,1)S(1)}, u32[]{:S(2)}, u32[]{:S(2)}) collective-permute-start(bf16[4,16,1792]{2,1,0:T(8,128)(2,1)S(1)} %fusion.3), channel_id=1, source_target_pairs={{0,2},{1,3},{2,0},{3,1},{4,6},{5,7},{6,4},{7,5},{8,10},{9,11},{10,... | collective-permute-start | bytes 688136 | tf_op jit(solution)/shard_map/sum_over_x/ppermute | solution.py:32
  100.5 7.9 %collective-permute-start.13 = (bf16[16,1792]{1,0:T(8,128)(2,1)S(1)}, bf16[16,1792]{1,0:T(8,128)(2,1)S(1)}, u32[]{:S(2)}, u32[]{:S(2)}) collective-permute-start(bf16[16,1792]{1,0:T(8,128)(2,1)S(1)} %get-tuple-element.23), channel_id=1, source_target_pairs={{0,12},{4,8},{8,4},{12,0},{1,13},{5,9},{9,5},{13,1},{2,14},{6,10},... | collective-permute-start | bytes 172040 | tf_op jit(solution)/shard_map/columns_over_ctx/ppermute | solution.py:32
  100.5 10.6 %collective-permute-start.12 = (bf16[16,1792]{1,0:T(8,128)(2,1)S(1)}, bf16[16,1792]{1,0:T(8,128)(2,1)S(1)}, u32[]{:S(2)}, u32[]{:S(2)}) collective-permute-start(bf16[16,1792]{1,0:T(8,128)(2,1)S(1)} %get-tuple-element.24), channel_id=1, source_target_pairs={{0,8},{4,12},{8,0},{12,4},{1,9},{5,13},{9,1},{13,5},{2,10},{6,14},... | collective-permute-start | bytes 172040 | tf_op jit(solution)/shard_map/columns_over_ctx/ppermute | solution.py:32
  102.2 8.8 %collective-permute-start.11 = (bf16[16,1792]{1,0:T(8,128)(2,1)S(1)}, bf16[16,1792]{1,0:T(8,128)(2,1)S(1)}, u32[]{:S(2)}, u32[]{:S(2)}) collective-permute-start(bf16[16,1792]{1,0:T(8,128)(2,1)S(1)} %get-tuple-element.25), channel_id=1, source_target_pairs={{0,4},{4,0},{8,12},{12,8},{1,5},{5,1},{9,13},{13,9},{2,6},{6,2},{1... | collective-permute-start | bytes 172040 | tf_op jit(solution)/shard_map/columns_over_ctx/ppermute | solution.py:32
  106.7 6.2 %collective-permute-start.21 = (bf16[16,1792]{1,0:T(8,128)(2,1)S(1)}, bf16[16,1792]{1,0:T(8,128)(2,1)S(1)}, u32[]{:S(2)}, u32[]{:S(2)}) collective-permute-start(bf16[16,1792]{1,0:T(8,128)(2,1)S(1)} %get-tuple-element.19), channel_id=1, source_target_pairs={{0,12},{4,8},{8,4},{12,0},{1,13},{5,9},{9,5},{13,1},{2,14},{6,10},... | collective-permute-start | bytes 172040 | tf_op jit(solution)/shard_map/columns_over_ctx/ppermute | solution.py:32
  106.7 7.1 %collective-permute-start.20 = (bf16[16,1792]{1,0:T(8,128)(2,1)S(1)}, bf16[16,1792]{1,0:T(8,128)(2,1)S(1)}, u32[]{:S(2)}, u32[]{:S(2)}) collective-permute-start(bf16[16,1792]{1,0:T(8,128)(2,1)S(1)} %get-tuple-element.20), channel_id=1, source_target_pairs={{0,8},{4,12},{8,0},{12,4},{1,9},{5,13},{9,1},{13,5},{2,10},{6,14},... | collective-permute-start | bytes 172040 | tf_op jit(solution)/shard_map/columns_over_ctx/ppermute | solution.py:32
  108.4 5.4 %copy-start.11 = (bf16[16,1792]{1,0:T(8,128)(2,1)}, bf16[16,1792]{1,0:T(8,128)(2,1)S(1)}, u32[]{:S(2)}) copy-start(bf16[16,1792]{1,0:T(8,128)(2,1)S(1)} %collective-permute-done.13.refs_3_) | copy-start | bytes 172036
  108.4 5.4 %collective-permute-start.19 = (bf16[16,1792]{1,0:T(8,128)(2,1)S(1)}, bf16[16,1792]{1,0:T(8,128)(2,1)S(1)}, u32[]{:S(2)}, u32[]{:S(2)}) collective-permute-start(bf16[16,1792]{1,0:T(8,128)(2,1)S(1)} %get-tuple-element.21), channel_id=1, source_target_pairs={{0,4},{4,0},{8,12},{12,8},{1,5},{5,1},{9,13},{13,9},{2,6},{6,2},{1... | collective-permute-start | bytes 172040 | tf_op jit(solution)/shard_map/columns_over_ctx/ppermute | solution.py:32
  111.1 2.7 %copy-start.12 = (bf16[16,1792]{1,0:T(8,128)(2,1)}, bf16[16,1792]{1,0:T(8,128)(2,1)S(1)}, u32[]{:S(2)}) copy-start(bf16[16,1792]{1,0:T(8,128)(2,1)S(1)} %collective-permute-done.12.refs_2_) | copy-start | bytes 172036
  111.1 2.7 %copy-start.13 = (bf16[16,1792]{1,0:T(8,128)(2,1)}, bf16[16,1792]{1,0:T(8,128)(2,1)S(1)}, u32[]{:S(2)}) copy-start(bf16[16,1792]{1,0:T(8,128)(2,1)S(1)} %collective-permute-done.11.refs_1_) | copy-start | bytes 172036
  112.9 0.9 copy-start.14
  113.8 0.6 copy-start.15
  113.8 0.6 copy-start.16

commit v3 on v2

v3 whole, which is shorter than its diff:
```python
import functools
import math

import jax
import jax.numpy as jnp
from jax import lax
from jax.experimental import pallas as pl
from jax.experimental.pallas import tpu as pltpu
from jax.sharding import PartitionSpec as P

LAT = 512
NOPE = 128
ROPE = 64
VD = 128
HEAD = NOPE + ROPE
PROJ = NOPE + VD
CHUNKS = 2
SUB_ROWS = 256
MASKED = -1e30
LOG2E = 1.4426950408889634
SCALE = LOG2E / math.sqrt(HEAD)
SHORT = pl.CostEstimate(flops=1024, bytes_accessed=1024, transcendentals=0)
IN_VMEM = pl.BlockSpec(memory_space=pltpu.VMEM)
IN_SMEM = pl.BlockSpec(memory_space=pltpu.SMEM)
IN_HBM = pl.BlockSpec(memory_space=pltpu.HBM)
ANYWHERE = pl.BlockSpec(memory_space=pl.ANY)


def params(mebibytes):
    return pltpu.CompilerParams(vmem_limit_bytes=mebibytes * 1024 * 1024)


def exchange(array, axis, size, bit):
    return lax.ppermute(array, axis, [(i, i ^ bit) for i in range(size)])


def tie_kernel(*refs):
    pass


def tie(array, after):
    if not after:
        return array
    return pl.pallas_call(
        tie_kernel,
        out_shape=jax.ShapeDtypeStruct(array.shape, array.dtype),
        in_specs=[ANYWHERE] * (1 + len(after)),
        out_specs=ANYWHERE,
        input_output_aliases={0: 0},
        cost_estimate=SHORT,
    )(array, *after)


def gather_pieces(own, size, after=()):
    pieces = {0: own}
    bit = size // 2
    while bit:
        for offset in sorted(pieces, reverse=True):
            pieces[offset ^ bit] = exchange(pieces[offset], "ctx", size, bit)
        if bit == size // 2:
            pieces[bit] = tie(pieces[bit], after)
        bit //= 2
    return [pieces[offset] for offset in range(size)]


def absorb_kernel(owners, piece, q_hbm, weight_hbm, *refs):
    out_refs = refs[:CHUNKS]
    q_ref, weight_ref, q_sem, weight_sems = refs[CHUNKS:]
    rows = q_ref.shape[0]
    head_count = weight_ref.shape[0]
    q_copy = pltpu.make_async_copy(q_hbm, q_ref, q_sem)
    q_copy.start()
    copies = []
    for head in range(head_count):
        source = weight_hbm.at[:, pl.ds(head * PROJ, NOPE)]
        copies.append(pltpu.make_async_copy(source, weight_ref.at[head], weight_sems.at[head]))
        copies[-1].start()
    q_copy.wait()
    for head in range(head_count):
        nope = q_ref[:, head * HEAD : head * HEAD + NOPE]
        rope = q_ref[:, head * HEAD + NOPE : (head + 1) * HEAD].astype(jnp.float32) * SCALE
        copies[head].wait()
        absorbed = lax.dot_general(
            nope, weight_ref[head], (((1,), (1,)), ((), ())), preferred_element_type=jnp.float32
        )
        absorbed = (absorbed * SCALE).reshape(owners, CHUNKS, piece, LAT)
        rope = rope.reshape(owners, CHUNKS, piece, ROPE)
        for chunk, out_ref in enumerate(out_refs):
            part = absorbed[:, chunk].reshape(rows // CHUNKS, LAT)
            out_ref[head, :, :LAT] = part.astype(jnp.bfloat16)
            part = rope[:, chunk].reshape(rows // CHUNKS, ROPE)
            out_ref[head, :, LAT:] = part.astype(jnp.bfloat16)


def absorb(queries, w_kv_up, owners, piece):
    rows = queries.shape[0]
    head_count = w_kv_up.shape[1] // PROJ
    shape = jax.ShapeDtypeStruct((head_count, rows // CHUNKS, LAT + ROPE), jnp.bfloat16)
    return pl.pallas_call(
        functools.partial(absorb_kernel, owners, piece),
        out_shape=[shape] * CHUNKS,
        in_specs=[IN_HBM, IN_HBM],
        out_specs=[IN_VMEM] * CHUNKS,
        scratch_shapes=[
            pltpu.VMEM(queries.shape, jnp.bfloat16),
            pltpu.VMEM((head_count, LAT, NOPE), jnp.bfloat16),
            pltpu.SemaphoreType.DMA,
            pltpu.SemaphoreType.DMA((head_count,)),
        ],
        compiler_params=params(50),
        cost_estimate=SHORT,
    )(queries, w_kv_up)


def visible_bias(order_ref, prefix_ref, own, piece, chunk, blocks, half, cache_rows, rows):
    n_ctx = order_ref.shape[0]
    query_rows = rows * CHUNKS
    row = lax.broadcasted_iota(jnp.int32, (rows, half), 0)
    column = lax.broadcasted_iota(jnp.int32, (rows, half), 1)
    owner = row // piece
    query_pos = order_ref[own] * query_rows + owner * (piece * CHUNKS) + chunk * piece + row % piece
    parts = []
    for offset, second in blocks:
        source = own ^ offset
        within = second * half + column
        cache_pos = jnp.where(
            source * cache_rows + within < prefix_ref[0], -1, n_ctx * query_rows
        )
        key_pos = order_ref[source] * query_rows + within - cache_rows
        first_seen = jnp.where(within < cache_rows, cache_pos, key_pos)
        parts.append(jnp.where(first_seen <= query_pos, 0.0, MASKED).astype(jnp.float32))
    return jnp.concatenate(parts, axis=1)


def attention_kernel(chunk, piece, cache_rows, order_ref, prefix_ref, q_ref, weight_hbm, *refs):
    heads, rows, depth = q_ref.shape
    n_ctx = order_ref.shape[0]
    if chunk == 0:
        own_hbm = refs[0]
        remote_refs = refs[1 : 2 * n_ctx - 1]
        out_ref, keys_ref, latent_ref, weight_ref, weight_sems, own_sem = refs[2 * n_ctx - 1 :]
        own_width = own_hbm.shape[1]
        own_copy = pltpu.make_async_copy(own_hbm, keys_ref.at[:, pl.ds(0, own_width)], own_sem)
        own_copy.start()
    else:
        keys_ref, latent_ref, out_ref, weight_ref, weight_sems = refs
    copies = []
    for head in range(heads):
        source = weight_hbm.at[:, pl.ds(head * PROJ + NOPE, VD)]
        copies.append(pltpu.make_async_copy(source, weight_ref.at[head], weight_sems.at[head]))
        copies[-1].start()
    amount = keys_ref.shape[1]
    half = amount // (2 * n_ctx)
    if chunk == 0:
        start = own_width
        for remote_ref in remote_refs:
            keys_ref[:, start : start + half] = remote_ref[...]
            start += half
        own_copy.wait()
        latent_ref[...] = keys_ref[:LAT, :].T
    own = lax.axis_index("ctx")
    core = lax.axis_index("head") % 2
    blocks = [(0, 0), (0, 1)]
    blocks += [(offset, core) for offset in range(1, n_ctx)]
    blocks += [(offset, 1 - core) for offset in range(1, n_ctx)]
    bias = visible_bias(
        order_ref, prefix_ref, own, piece, chunk, blocks, half, cache_rows, rows
    )
    for copy in copies:
        copy.wait()
    group = max(1, min(heads, SUB_ROWS // rows))
    for first in range(0, heads, group):
        size = group * rows
        queries = q_ref[first : first + group].reshape(size, depth)
        scores = jnp.dot(queries, keys_ref[...], preferred_element_type=jnp.float32)
        scores = scores.reshape(group, rows, amount) + bias[None]
        top = jnp.max(scores, axis=2, keepdims=True)
        weights = jnp.exp2(scores - top)
        total = jnp.sum(weights, axis=2, keepdims=True).reshape(size, 1)
        mixed = jnp.dot(
            weights.reshape(size, amount).astype(jnp.bfloat16),
            latent_ref[...],
            preferred_element_type=jnp.float32,
        )
        mixed = (mixed / total).astype(jnp.bfloat16)
        for head in range(first, first + group):
            result = jnp.dot(
                mixed[(head - first) * rows : (head - first + 1) * rows],
                weight_ref[head],
                preferred_element_type=jnp.float32,
            )
            out_ref[:, head * VD : (head + 1) * VD] = result.astype(jnp.bfloat16)


def attention(chunk, piece, cache_rows, q_ext, w_kv_up, stretch_order, prefix_len, keys):
    head_count, rows, depth = q_ext.shape
    n_ctx = stretch_order.shape[0]
    first = chunk == 0
    amount = n_ctx * keys[0].shape[1] if first else keys[0].shape[1]
    out_shape = [jax.ShapeDtypeStruct((rows, head_count * VD), jnp.bfloat16)]
    key_specs = [IN_VMEM] * len(keys)
    scratch = [
        pltpu.VMEM((head_count, LAT, VD), jnp.bfloat16),
        pltpu.SemaphoreType.DMA((head_count,)),
    ]
    if first:
        key_specs[0] = IN_HBM
        scratch.append(pltpu.SemaphoreType.DMA)
        out_shape.append(jax.ShapeDtypeStruct((depth, amount), jnp.bfloat16))
        out_shape.append(jax.ShapeDtypeStruct((amount, LAT), jnp.bfloat16))
    return pl.pallas_call(
        functools.partial(attention_kernel, chunk, piece, cache_rows),
        out_shape=out_shape,
        in_specs=[IN_SMEM, IN_SMEM, IN_VMEM, IN_HBM] + key_specs,
        out_specs=[IN_VMEM] * len(out_shape),
        scratch_shapes=scratch,
        compiler_params=params(50),
        cost_estimate=SHORT,
    )(stretch_order, prefix_len, q_ext, w_kv_up, *keys)


def product_kernel(count, n_x, after, weight_hbm, *refs):
    piece_refs = refs[:count]
    sent_ref, kept_ref, rows_ref, weight_ref, sems = refs[count + after :]
    rows = piece_refs[0].shape[0]
    tiles = weight_ref.shape[0]
    width = weight_ref.shape[2]
    copies = []
    for tile in range(tiles):
        source = weight_hbm.at[:, pl.ds(tile * width, width)]
        copies.append(pltpu.make_async_copy(source, weight_ref.at[tile], sems.at[tile]))
        copies[-1].start()
    for index, piece_ref in enumerate(piece_refs):
        rows_ref[index * rows : (index + 1) * rows, :] = piece_ref[...]
    is_first = lax.axis_index("head") % 2 == 0
    for tile in range(tiles):
        copies[tile].wait()
        result = jnp.dot(rows_ref[...], weight_ref[tile], preferred_element_type=jnp.float32)
        result = result.reshape(count, n_x, 2, rows // (2 * n_x), width)
        span = slice(tile * width, (tile + 1) * width)
        for x in range(n_x):
            first, second = result[:, x, 0], result[:, x, 1]
            sent_ref[x, :, :, span] = jnp.where(is_first, second, first).astype(jnp.bfloat16)
            kept_ref[x, :, :, span] = jnp.where(is_first, first, second)


def product(pieces, w_out, n_x, after):
    rows, depth = pieces[0].shape
    count = len(pieces)
    columns = w_out.shape[1]
    width = 256 if columns % 256 == 0 else columns
    tiles = columns // width
    shape = (n_x, count, rows // (2 * n_x), columns)
    return pl.pallas_call(
        functools.partial(product_kernel, count, n_x, len(after)),
        out_shape=[jax.ShapeDtypeStruct(shape, jnp.bfloat16), jax.ShapeDtypeStruct(shape, jnp.float32)],
        in_specs=[IN_HBM] + [IN_VMEM] * count + [ANYWHERE] * len(after),
        out_specs=[IN_VMEM, IN_VMEM],
        scratch_shapes=[
            pltpu.VMEM((count * rows, depth), jnp.bfloat16),
            pltpu.VMEM((tiles, depth, width), jnp.bfloat16),
            pltpu.SemaphoreType.DMA((tiles,)),
        ],
        compiler_params=params(50),
        cost_estimate=SHORT,
    )(w_out, *pieces, *after)


def place_kernel(n_ctx, ctx_ref, *refs):
    blocks, out_ref = refs[:-1], refs[-1]
    rows = blocks[0].shape[0]
    for offset in range(n_ctx):

        @pl.when(pl.program_id(0) == offset)
        def _():
            for chunk in range(CHUNKS):
                block = blocks[chunk * n_ctx + offset][...]
                out_ref[chunk * rows : (chunk + 1) * rows, :] = block


def place_columns(results, ctx, n_ctx):
    rows, width = results[0][0].shape
    total = rows * len(results)
    if width % 128 or rows % 16:
        out = jnp.zeros((total, n_ctx * width), jnp.bfloat16)
        for offset in range(n_ctx):
            block = jnp.concatenate([result[offset] for result in results], axis=0)
            out = lax.dynamic_update_slice(out, block, (0, (ctx ^ offset) * width))
        return out
    blocks = [block for result in results for block in result]
    return pl.pallas_call(
        functools.partial(place_kernel, n_ctx),
        out_shape=jax.ShapeDtypeStruct((total, n_ctx * width), jnp.bfloat16),
        grid_spec=pltpu.PrefetchScalarGridSpec(
            num_scalar_prefetch=1,
            grid=(n_ctx,),
            in_specs=[IN_VMEM] * len(blocks),
            out_specs=pl.BlockSpec((total, width), lambda i, ctx_ref: (0, ctx_ref[0] ^ i)),
        ),
        cost_estimate=SHORT,
    )(jnp.full((1,), ctx, jnp.int32), *blocks)


def shards(n_ctx, n_head, queries, kv_rows, w_kv_up, w_out, stretch_order, prefix_len):
    query_rows = queries.shape[0]
    row_span = kv_rows.shape[0]
    cache_rows = row_span - query_rows
    half = row_span // 2
    n_x = n_head // 2
    piece = query_rows // n_head // CHUNKS
    ctx = lax.axis_index("ctx")
    head = lax.axis_index("head")
    x = head // 2

    with jax.named_scope("keys_over_ctx"):
        kv_t = kv_rows.T
        own_half = jnp.where(head % 2 == 0, kv_t[:, :half], kv_t[:, half:])
        halves = [exchange(own_half, "ctx", n_ctx, offset) for offset in range(1, n_ctx)]
    with jax.named_scope("queries_to_latent"):
        q_ext = absorb(queries, w_kv_up, n_head, piece)
    with jax.named_scope("keys_over_cores"):
        halves = [tie(array, q_ext[:1]) for array in halves]
        others = [exchange(array, "head", n_head, 1) for array in halves]
    keys = [kv_t] + halves + others
    attended = []
    for chunk in range(CHUNKS):
        with jax.named_scope("attention"):
            result = attention(
                chunk, piece, cache_rows, q_ext[chunk], w_kv_up, stretch_order, prefix_len, keys
            )
        attended.append(result[0])
        if chunk == 0:
            keys = list(result[1:])
    with jax.named_scope("attended_over_ctx"):
        gathered = [
            gather_pieces(own, n_ctx, attended[chunk + 1 :]) for chunk, own in enumerate(attended)
        ]
    results = []
    after = attended[1:]
    for chunk in range(CHUNKS):
        with jax.named_scope("out_product"):
            sent, kept = product(gathered[chunk], w_out, n_x, after)
        with jax.named_scope("sum_over_cores"):
            if chunk + 1 < CHUNKS:
                later = gathered[chunk + 1]
                sent = tie(sent, [later[n_ctx // 2], later[1]])
            summed = kept + exchange(sent, "head", n_head, 1).astype(jnp.float32)
        with jax.named_scope("sum_over_x"):
            total = lax.dynamic_index_in_dim(summed, x, 0, keepdims=False)
            for offset in range(1, n_x):
                sent = lax.dynamic_index_in_dim(summed, x ^ offset, 0, keepdims=False)
                sent = exchange(sent.astype(jnp.bfloat16), "head", n_head, 2 * offset)
                total = total + sent.astype(jnp.float32)
        with jax.named_scope("columns_over_ctx"):
            total = total.astype(jnp.bfloat16)
            after = [total]
            blocks = [total[0]] + [exchange(total[d], "ctx", n_ctx, d) for d in range(1, n_ctx)]
        results.append(blocks)
    with jax.named_scope("output"):
        return place_columns(results, ctx, n_ctx)


def solution(mesh):
    placed = (
        P(("groups", "ctx"), "head"),
        P(("groups", "ctx"), None),
        P(None, "head"),
        P("head", "ctx"),
        P("groups"),
        P("groups"),
    )
    return jax.shard_map(
        functools.partial(shards, mesh.shape["ctx"], mesh.shape["head"]),
        mesh=mesh,
        in_specs=placed,
        out_specs=P(("groups", "ctx", "head"), None),
        check_vma=False,
    )
```

time: 130 us -> 109 us (0.84)
  waiting for transfers between devices: 48.6 us -> 38.1 us
  Pallas kernels: 40.7 us -> 33.3 us
  starting transfers between devices: 19.8 us -> 23.4 us
  local copies, waits for them, and re-layouts: 15.1 us -> 11.9 us
  other arithmetic: 3.62 us -> 1.24 us
    ppermute x22, waiting for transfers between devices: 48.6 us -> 38.1 us  [exchange(): return lax.ppermute(array, axis, [(i, i ^ bit) for i in range(size)])]
    pallas_call x6, Pallas kernels: 40.7 us -> 33.3 us  [the longest x2 14.5 us: attention(): pl.pallas_call(functools.partial(attention_kernel, chunk, piece, cache_ro...]
    ppermute x22, starting transfers between devices: 19.8 us -> 23.4 us  [exchange(): return lax.ppermute(array, axis, [(i, i ^ bit) for i in range(size)])]
    unnamed x34 -> x52, local copies, waits for them, and re-layouts: 13.6 us -> 10.6 us
    reduce_sum x2 -> x0, other arithmetic: 2.06 us -> none  [lookup(): jnp.sum(jnp.where(indices[..., None] == positions, table, 0), axis=-1)]
  transfers between devices with their start and end apart: 22 -> 22, of which waited for: 12 -> 11; matrix products, arithmetic and copies ran while one was open for 3% -> 1% of each run, Pallas kernels for 10% -> 16%
where the time goes in v3:
time: 109 us
  waiting for transfers between devices  38.1 us (35%)
  Pallas kernels  33.3 us (31%)
  starting transfers between devices  23.4 us (21%)
  local copies, waits for them, and re-layouts  11.9 us (11%)
  other arithmetic  1.24 us (1%)
    ppermute x22, waiting for transfers between devices, exchange(): return lax.ppermute(array, axis, [(i, i ^ bit) for i in range(size)])  38.1 us
    ppermute x22, starting transfers between devices, exchange(): return lax.ppermute(array, axis, [(i, i ^ bit) for i in range(size)])  23.4 us
    pallas_call x2, Pallas kernels, attention(): pl.pallas_call(functools.partial(attention_kernel, chunk, piece, cache_ro...  14.5 us
    pallas_call x2, Pallas kernels, product(): pl.pallas_call(functools.partial(product_kernel, count, n_x, len(after)),...  11.7 us
    unnamed x52, local copies, waits for them, and re-layouts  10.6 us
    pallas_call x1, Pallas kernels, absorb(): pl.pallas_call(functools.partial(absorb_kernel, owners, piece), out_shape...  4.65 us
    pallas_call x1, Pallas kernels, place_columns(): pl.pallas_call(functools.partial(place_kernel, n_ctx), out_shape=jax.Shap...  2.39 us
  transfers between devices with their start and end apart: 22, of which 11 were waited for; matrix products, arithmetic and copies ran while one was open for 1% of the time, Pallas kernels for 16%

profile of v3, /device:TPU:0, one launch (start us, length us, event | category | flops | bytes accessed | tf_op | source)
XLA Modules:
  0.0 108.9 jit_solution(7752770473120151037)
XLA Ops:
  0.0 1.0 slice_select_fusion
  1.0 3.1 %collective-permute-start = (bf16[576,128]{1,0:T(8,128)(2,1)S(1)}, bf16[576,128]{1,0:T(8,128)(2,1)S(1)}, u32[]{:S(2)}, u32[]{:S(2)}) collective-permute-start(bf16[576,128]{1,0:T(8,128)(2,1)S(1)} %slice_select_fusion), channel_id=1, source_target_pairs={{0,4},{4,0},{8,12},{12,8},{1,5},{5,1},{9,13},{13,9},{2,6},{6,2},{1... | collective-permute-start | bytes 442376 | tf_op jit(solution)/shard_map/keys_over_ctx/ppermute | solution.py:34
  4.1 2.6 %collective-permute-start.1 = (bf16[576,128]{1,0:T(8,128)(2,1)S(1)}, bf16[576,128]{1,0:T(8,128)(2,1)S(1)}, u32[]{:S(2)}, u32[]{:S(2)}) collective-permute-start(bf16[576,128]{1,0:T(8,128)(2,1)S(1)} %slice_select_fusion), channel_id=1, source_target_pairs={{0,8},{4,12},{8,0},{12,4},{1,9},{5,13},{9,1},{13,5},{2,10},{6,14},... | collective-permute-start | bytes 442376 | tf_op jit(solution)/shard_map/keys_over_ctx/ppermute | solution.py:34
  6.7 0.0 collective-permute-start.2
  6.7 1.1 %copy-done.11 = bf16[128,3072]{1,0:T(8,128)(2,1)S(1)} copy-done((bf16[128,3072]{1,0:T(8,128)(2,1)S(1)}, bf16[128,3072]{1,0:T(8,128)(2,1)}, u32[]{:S(2)}) %copy-start.11) | copy-done | bytes 786456
  7.8 4.6 %queries_to_latent.1 = (bf16[16,64,576]{2,1,0:T(8,128)(2,1)S(1)}, bf16[16,64,576]{2,1,0:T(8,128)(2,1)S(1)}) custom-call(bf16[128,3072]{1,0:T(8,128)(2,1)S(1)} %copy-done.11, bf16[512,4096]{1,0:T(8,128)(2,1)} %weight_hbm.7), custom_call_target="tpu_custom_call" | custom-call | flops 1024 | bytes 1024 | tf_op jit(solution)/shard_map/queries_to_latent/pallas_call | solution.py:99
  12.5 1.1 %copy-done = bf16[16,64,576]{2,1,0:T(8,128)(2,1)} copy-done((bf16[16,64,576]{2,1,0:T(8,128)(2,1)}, bf16[16,64,576]{2,1,0:T(8,128)(2,1)S(1)}, u32[]{:S(2)}) %copy-start) | copy-done | bytes 1179672
  13.6 0.0 collective-permute-done.refs_0_
  13.6 0.7 copy-done.16
  14.3 3.8 %collective-permute-done.1.refs_0_ = bf16[576,128]{1,0:T(8,128)(2,1)S(1)} collective-permute-done((bf16[576,128]{1,0:T(8,128)(2,1)S(1)}, bf16[576,128]{1,0:T(8,128)(2,1)S(1)}, u32[]{:S(2)}, u32[]{:S(2)}) %collective-permute-start.1) | collective-permute-done | bytes 147488 | tf_op jit(solution)/shard_map/keys_over_ctx/ppermute | solution.py:34
  18.1 0.7 copy-done.14
  18.8 0.0 collective-permute-done.2.refs_0_
  18.8 0.6 copy-done.12
  19.4 0.5 collective-permute-start.5
  20.6 0.0 collective-permute-done.3.refs_4_
  20.6 0.0 collective-permute-done.4.refs_5_
  20.6 0.5 collective-permute-done.5.refs_6_
  21.2 0.9 copy-done.13
  22.1 7.7 %attention.2 = (bf16[64,2048]{1,0:T(8,128)(2,1)S(1)}, bf16[576,1024]{1,0:T(8,128)(2,1)S(1)}, bf16[1024,512]{1,0:T(8,128)(2,1)S(1)}) custom-call(s32[4]{0:T(128)S(1)} %copy-done.19, s32[1]{0:T(128)S(6)} %copy.17.prefix_ref, bf16[16,64,576]{2,1,0:T(8,128)(2,1)} %copy-done, bf16[512,4096]{1,0:T(8,128)(2,1)} %weight_hbm.7, bf16[576,256]{1,0:T(8,128)(2,1)S(1)} %bitcast.31, ...), custom_call_target="tpu_custom_call" | custom-call | flops 1024 | bytes 1024 | tf_op jit(solution)/shard_map/attention/pallas_call | solution.py:211
  29.7 2.6 %collective-permute-start.7 = (bf16[64,2048]{1,0:T(8,128)(2,1)S(1)}, bf16[64,2048]{1,0:T(8,128)(2,1)S(1)}, u32[]{:S(2)}, u32[]{:S(2)}) collective-permute-start(bf16[64,2048]{1,0:T(8,128)(2,1)S(1)} %get-tuple-element.15.refs_0_), channel_id=1, source_target_pairs={{0,8},{4,12},{8,0},{12,4},{1,9},{5,13},{9,1},{13,5},{2,10},{6,14},... | collective-permute-start | bytes 786440 | tf_op jit(solution)/shard_map/attended_over_ctx/ppermute | solution.py:34
  32.3 0.3 collective-permute-start.6
  32.6 6.8 %attention.3.refs_1_.refs_4_.refs_0_ = bf16[64,2048]{1,0:T(8,128)(2,1)S(1)} custom-call(s32[4]{0:T(128)S(1)} %copy-done.19, s32[1]{0:T(128)S(6)} %copy.17.prefix_ref, bf16[16,64,576]{2,1,0:T(8,128)(2,1)S(1)} %get-tuple-element.16.q_ref, bf16[512,4096]{1,0:T(8,128)(2,1)} %weight_hbm.7, bf16[576,1024]{1,0:T(8,128)(2,1)S(1)} %get-tuple-element.17.refs_0_, ...), custom_call_target="tpu_custom_call" | custom-call | flops 1024 | bytes 1024 | tf_op jit(solution)/shard_map/attention/pallas_call | solution.py:211
  39.5 0.7 copy-done.1
  40.2 4.8 %collective-permute-done.7.refs_0_ = bf16[64,2048]{1,0:T(8,128)(2,1)S(1)} collective-permute-done((bf16[64,2048]{1,0:T(8,128)(2,1)S(1)}, bf16[64,2048]{1,0:T(8,128)(2,1)S(1)}, u32[]{:S(2)}, u32[]{:S(2)}) %collective-permute-start.7) | collective-permute-done | bytes 262176 | tf_op jit(solution)/shard_map/attended_over_ctx/ppermute | solution.py:34
  45.0 0.7 copy-done.5
  45.7 0.0 collective-permute-start.8
  45.7 2.0 %collective-permute-start.10 = (bf16[64,2048]{1,0:T(8,128)(2,1)}, bf16[64,2048]{1,0:T(8,128)(2,1)S(1)}, u32[]{:S(2)}, u32[]{:S(2)}) collective-permute-start(bf16[64,2048]{1,0:T(8,128)(2,1)} %copy-done.1), channel_id=1, source_target_pairs={{0,4},{4,0},{8,12},{12,8},{1,5},{5,1},{9,13},{13,9},{2,6},{6,2},{1... | collective-permute-start | bytes 786440 | tf_op jit(solution)/shard_map/attended_over_ctx/ppermute | solution.py:34
  47.7 0.7 collective-permute-start.9
  48.5 0.0 collective-permute-done.6.refs_1_
  48.5 12.3 %collective-permute-done.8.refs_3_ = bf16[64,2048]{1,0:T(8,128)(2,1)S(1)} collective-permute-done((bf16[64,2048]{1,0:T(8,128)(2,1)}, bf16[64,2048]{1,0:T(8,128)(2,1)S(1)}, u32[]{:S(2)}, u32[]{:S(2)}) %collective-permute-start.8) | collective-permute-done | bytes 262176 | tf_op jit(solution)/shard_map/attended_over_ctx/ppermute | solution.py:34
  60.8 0.9 copy-done.2
  61.7 0.9 copy-done.6
  62.7 5.9 %out_product.2 = (bf16[2,4,16,1792]{3,2,1,0:T(8,128)(2,1)S(1)}, f32[2,4,16,1792]{3,2,1,0:T(8,128)S(1)}) custom-call(bf16[2048,1792]{1,0:T(8,128)(2,1)} %weight_hbm.9, bf16[64,2048]{1,0:T(8,128)(2,1)S(1)} %get-tuple-element.15.refs_0_, bf16[64,2048]{1,0:T(8,128)(2,1)S(1)} %collective-permute-done.6.refs_1_, bf16[64,2048]{1,0:T(8,128)(2,1)S(1)} %copy-done.6, ...), custom_call_target="tpu_custom_call" | custom-call | flops 1024 | bytes 1024 | tf_op jit(solution)/shard_map/out_product/pallas_call | solution.py:254
  68.6 0.0 copy-start.18
  68.6 0.8 copy-done.18
  69.3 0.0 collective-permute-done.10.refs_2_.refs_1_
  69.3 0.0 collective-permute-done.9.refs_1_.refs_2_
  69.3 0.7 copy-done.7
  70.0 0.1 copy-done.9
  70.1 0.0 collective-permute-start.11
  70.1 2.0 %collective-permute-done.11 = bf16[2,4,16,1792]{3,2,1,0:T(8,128)(2,1)S(1)} collective-permute-done((bf16[2,4,16,1792]{3,2,1,0:T(8,128)(2,1)}, bf16[2,4,16,1792]{3,2,1,0:T(8,128)(2,1)S(1)}, u32[]{:S(2)}, u32[]{:S(2)}) %collective-permute-start.11) | collective-permute-done | bytes 458784 | tf_op jit(solution)/shard_map/sum_over_cores/ppermute | solution.py:34
  72.2 0.1 convert_add_fusion.1
  72.3 1.6 %collective-permute-start.12 = (bf16[4,16,1792]{2,1,0:T(8,128)(2,1)S(1)}, bf16[4,16,1792]{2,1,0:T(8,128)(2,1)S(1)}, u32[]{:S(2)}, u32[]{:S(2)}) collective-permute-start(bf16[4,16,1792]{2,1,0:T(8,128)(2,1)S(1)} %fusion.2), channel_id=1, source_target_pairs={{0,2},{1,3},{2,0},{3,1},{4,6},{5,7},{6,4},{7,5},{8,10},{9,11},{10,... | collective-permute-start | bytes 688136 | tf_op jit(solution)/shard_map/sum_over_x/ppermute | solution.py:34
  73.9 6.2 %collective-permute-done.12 = bf16[4,16,1792]{2,1,0:T(8,128)(2,1)S(1)} collective-permute-done((bf16[4,16,1792]{2,1,0:T(8,128)(2,1)S(1)}, bf16[4,16,1792]{2,1,0:T(8,128)(2,1)S(1)}, u32[]{:S(2)}, u32[]{:S(2)}) %collective-permute-start.12) | collective-permute-done | bytes 229408 | tf_op jit(solution)/shard_map/sum_over_x/ppermute | solution.py:34
  80.0 1.9 %collective-permute-done.16.refs_3_ = bf16[64,2048]{1,0:T(8,128)(2,1)S(1)} collective-permute-done((bf16[64,2048]{1,0:T(8,128)(2,1)S(1)}, bf16[64,2048]{1,0:T(8,128)(2,1)S(1)}, u32[]{:S(2)}, u32[]{:S(2)}) %collective-permute-start.16) | collective-permute-done | bytes 262176 | tf_op jit(solution)/shard_map/attended_over_ctx/ppermute | solution.py:34
  81.9 5.9 %out_product.3 = (bf16[2,4,16,1792]{3,2,1,0:T(8,128)(2,1)S(1)}, f32[2,4,16,1792]{3,2,1,0:T(8,128)S(1)}) custom-call(bf16[2048,1792]{1,0:T(8,128)(2,1)} %weight_hbm.9, bf16[64,2048]{1,0:T(8,128)(2,1)S(1)} %copy-done.3, bf16[64,2048]{1,0:T(8,128)(2,1)S(1)} %copy-done.8, bf16[64,2048]{1,0:T(8,128)(2,1)S(1)} %copy-done.10, ...), custom_call_target="tpu_custom_call" | custom-call | flops 1024 | bytes 1024 | tf_op jit(solution)/shard_map/out_product/pallas_call | solution.py:254
  87.8 0.1 collective-permute-start.17
  87.9 1.8 %collective-permute-done.17 = bf16[2,4,16,1792]{3,2,1,0:T(8,128)(2,1)S(1)} collective-permute-done((bf16[2,4,16,1792]{3,2,1,0:T(8,128)(2,1)S(1)}, bf16[2,4,16,1792]{3,2,1,0:T(8,128)(2,1)S(1)}, u32[]{:S(2)}, u32[]{:S(2)}) %collective-permute-start.17) | collective-permute-done | bytes 458784 | tf_op jit(solution)/shard_map/sum_over_cores/ppermute | solution.py:34
  89.7 0.1 convert_add_fusion
  89.8 1.1 %collective-permute-start.18 = (bf16[4,16,1792]{2,1,0:T(8,128)(2,1)S(1)}, bf16[4,16,1792]{2,1,0:T(8,128)(2,1)S(1)}, u32[]{:S(2)}, u32[]{:S(2)}) collective-permute-start(bf16[4,16,1792]{2,1,0:T(8,128)(2,1)S(1)} %fusion.3), channel_id=1, source_target_pairs={{0,2},{1,3},{2,0},{3,1},{4,6},{5,7},{6,4},{7,5},{8,10},{9,11},{10,... | collective-permute-start | bytes 688136 | tf_op jit(solution)/shard_map/sum_over_x/ppermute | solution.py:34
  90.9 0.6 slice_bitcast_fusion.4
  91.5 2.2 %collective-permute-start.15 = (bf16[16,1792]{1,0:T(8,128)(2,1)S(1)}, bf16[16,1792]{1,0:T(8,128)(2,1)S(1)}, u32[]{:S(2)}, u32[]{:S(2)}) collective-permute-start(bf16[16,1792]{1,0:T(8,128)(2,1)S(1)} %get-tuple-element.27), channel_id=1, source_target_pairs={{0,12},{4,8},{8,4},{12,0},{1,13},{5,9},{9,5},{13,1},{2,14},{6,10},... | collective-permute-start | bytes 172040 | tf_op jit(solution)/shard_map/columns_over_ctx/ppermute | solution.py:34
  93.7 0.0 collective-permute-start.14
  93.7 2.2 %collective-permute-start.13 = (bf16[16,1792]{1,0:T(8,128)(2,1)S(1)}, bf16[16,1792]{1,0:T(8,128)(2,1)S(1)}, u32[]{:S(2)}, u32[]{:S(2)}) collective-permute-start(bf16[16,1792]{1,0:T(8,128)(2,1)S(1)} %get-tuple-element.29), channel_id=1, source_target_pairs={{0,4},{4,0},{8,12},{12,8},{1,5},{5,1},{9,13},{13,9},{2,6},{6,2},{1... | collective-permute-start | bytes 172040 | tf_op jit(solution)/shard_map/columns_over_ctx/ppermute | solution.py:34
  95.9 1.6 %collective-permute-done.18 = bf16[4,16,1792]{2,1,0:T(8,128)(2,1)S(1)} collective-permute-done((bf16[4,16,1792]{2,1,0:T(8,128)(2,1)S(1)}, bf16[4,16,1792]{2,1,0:T(8,128)(2,1)S(1)}, u32[]{:S(2)}, u32[]{:S(2)}) %collective-permute-start.18) | collective-permute-done | bytes 229408 | tf_op jit(solution)/shard_map/sum_over_x/ppermute | solution.py:34
  97.6 0.6 slice_bitcast_fusion
  98.2 2.2 %collective-permute-start.21 = (bf16[16,1792]{1,0:T(8,128)(2,1)S(1)}, bf16[16,1792]{1,0:T(8,128)(2,1)S(1)}, u32[]{:S(2)}, u32[]{:S(2)}) collective-permute-start(bf16[16,1792]{1,0:T(8,128)(2,1)S(1)} %get-tuple-element.23), channel_id=1, source_target_pairs={{0,12},{4,8},{8,4},{12,0},{1,13},{5,9},{9,5},{13,1},{2,14},{6,10},... | collective-permute-start | bytes 172040 | tf_op jit(solution)/shard_map/columns_over_ctx/ppermute | solution.py:34
  100.4 0.0 collective-permute-start.20
  100.4 2.2 %collective-permute-start.19 = (bf16[16,1792]{1,0:T(8,128)(2,1)S(1)}, bf16[16,1792]{1,0:T(8,128)(2,1)S(1)}, u32[]{:S(2)}, u32[]{:S(2)}) collective-permute-start(bf16[16,1792]{1,0:T(8,128)(2,1)S(1)} %get-tuple-element.25), channel_id=1, source_target_pairs={{0,4},{4,0},{8,12},{12,8},{1,5},{5,1},{9,13},{13,9},{2,6},{6,2},{1... | collective-permute-start | bytes 172040 | tf_op jit(solution)/shard_map/columns_over_ctx/ppermute | solution.py:34
  102.6 1.8 %collective-permute-done.21.refs_7_ = bf16[16,1792]{1,0:T(8,128)(2,1)S(1)} collective-permute-done((bf16[16,1792]{1,0:T(8,128)(2,1)S(1)}, bf16[16,1792]{1,0:T(8,128)(2,1)S(1)}, u32[]{:S(2)}, u32[]{:S(2)}) %collective-permute-start.21) | collective-permute-done | bytes 57376 | tf_op jit(solution)/shard_map/columns_over_ctx/ppermute | solution.py:34
  104.4 1.4 %collective-permute-done.20.refs_6_ = bf16[16,1792]{1,0:T(8,128)(2,1)S(1)} collective-permute-done((bf16[16,1792]{1,0:T(8,128)(2,1)S(1)}, bf16[16,1792]{1,0:T(8,128)(2,1)S(1)}, u32[]{:S(2)}, u32[]{:S(2)}) %collective-permute-start.20) | collective-permute-done | bytes 57376 | tf_op jit(solution)/shard_map/columns_over_ctx/ppermute | solution.py:34
  105.9 0.6 copy-done.24
  106.5 0.0 copy-done.25
  106.5 2.4 %output.1 = bf16[32,7168]{1,0:T(8,128)(2,1)} custom-call(s32[1]{0:T(128)} %bitcast.ctx_ref, bf16[16,1792]{1,0:T(8,128)(2,1)} %get-tuple-element.30.refs_0_, bf16[16,1792]{1,0:T(8,128)(2,1)} %copy-done.22, bf16[16,1792]{1,0:T(8,128)(2,1)} %copy-done.21, bf16[16,1792]{1,0:T(8,128)(2,1)} %copy-done.20, bf16[16,1792]{1,0:T(8,128)(2,1)} %get-tuple-element.26.refs_4_, ...), custom_call_target="tpu_custom_call" | custom-call | flops 1024 | bytes 1024 | tf_op jit(solution)/shard_map/output/pallas_call | solution.py:291
  (52 shorter events, 0.2 us)
Async XLA Ops:
  1.0 12.6 %collective-permute-start = (bf16[576,128]{1,0:T(8,128)(2,1)S(1)}, bf16[576,128]{1,0:T(8,128)(2,1)S(1)}, u32[]{:S(2)}, u32[]{:S(2)}) collective-permute-start(bf16[576,128]{1,0:T(8,128)(2,1)S(1)} %slice_select_fusion), channel_id=1, source_target_pairs={{0,4},{4,0},{8,12},{12,8},{1,5},{5,1},{9,13},{13,9},{2,6},{6,2},{1... | collective-permute-start | bytes 442376 | tf_op jit(solution)/shard_map/keys_over_ctx/ppermute | solution.py:34
  4.1 14.0 %collective-permute-start.1 = (bf16[576,128]{1,0:T(8,128)(2,1)S(1)}, bf16[576,128]{1,0:T(8,128)(2,1)S(1)}, u32[]{:S(2)}, u32[]{:S(2)}) collective-permute-start(bf16[576,128]{1,0:T(8,128)(2,1)S(1)} %slice_select_fusion), channel_id=1, source_target_pairs={{0,8},{4,12},{8,0},{12,4},{1,9},{5,13},{9,1},{13,5},{2,10},{6,14},... | collective-permute-start | bytes 442376 | tf_op jit(solution)/shard_map/keys_over_ctx/ppermute | solution.py:34
  6.7 12.1 %collective-permute-start.2 = (bf16[576,128]{1,0:T(8,128)(2,1)S(1)}, bf16[576,128]{1,0:T(8,128)(2,1)S(1)}, u32[]{:S(2)}, u32[]{:S(2)}) collective-permute-start(bf16[576,128]{1,0:T(8,128)(2,1)S(1)} %slice_select_fusion), channel_id=1, source_target_pairs={{0,12},{4,8},{8,4},{12,0},{1,13},{5,9},{9,5},{13,1},{2,14},{6,10},... | collective-permute-start | bytes 442376 | tf_op jit(solution)/shard_map/keys_over_ctx/ppermute | solution.py:34
  6.7 1.1 %copy-start.11 = (bf16[128,3072]{1,0:T(8,128)(2,1)S(1)}, bf16[128,3072]{1,0:T(8,128)(2,1)}, u32[]{:S(2)}) copy-start(bf16[128,3072]{1,0:T(8,128)(2,1)} %q_hbm.1) | copy-start | bytes 2359300
  12.5 1.1 %copy-start = (bf16[16,64,576]{2,1,0:T(8,128)(2,1)}, bf16[16,64,576]{2,1,0:T(8,128)(2,1)S(1)}, u32[]{:S(2)}) copy-start(bf16[16,64,576]{2,1,0:T(8,128)(2,1)S(1)} %get-tuple-element.14.refs_1_.q_ref) | copy-start | bytes 3538948
  13.6 0.7 copy-start.16
  14.2 6.9 %copy-start.4 = (bf16[256,576]{0,1:T(8,128)(2,1)S(1)}, bf16[256,576]{0,1:T(8,128)(2,1)}, u32[]{:S(2)}) copy-start(bf16[256,576]{0,1:T(8,128)(2,1)} %param.7) | copy-start | bytes 884740
  14.3 6.9 %copy-start.17 = (bf16[576,128]{1,0:T(8,128)(2,1)S(1)}, bf16[576,128]{1,0:T(8,128)(2,1)}, u32[]{:S(2)}) copy-start(bf16[576,128]{1,0:T(8,128)(2,1)} %keys_over_cores.3.refs_1_) | copy-start | bytes 442372
  14.3 6.9 %copy-start.19 = (s32[4]{0:T(128)S(1)}, s32[4]{0:T(128)}, u32[]{:S(2)}) copy-start(s32[4]{0:T(128)} %order_ref.3) | copy-start | bytes 52
  14.3 6.3 %collective-permute-start.3 = (bf16[576,128]{1,0:T(8,128)(2,1)}, bf16[576,128]{1,0:T(8,128)(2,1)S(1)}, u32[]{:S(2)}, u32[]{:S(2)}) collective-permute-start(bf16[576,128]{1,0:T(8,128)(2,1)} %keys_over_cores.3.refs_1_), channel_id=1, source_target_pairs={{0,1},{1,0},{2,3},{3,2},{4,5},{5,4},{6,7},{7,6},{8,9},{9,8},{10,11... | collective-permute-start | bytes 442376 | tf_op jit(solution)/shard_map/keys_over_cores/ppermute | solution.py:34
  18.1 0.7 copy-start.14
  18.7 2.4 %copy-start.15 = (bf16[576,128]{1,0:T(8,128)(2,1)S(1)}, bf16[576,128]{1,0:T(8,128)(2,1)}, u32[]{:S(2)}) copy-start(bf16[576,128]{1,0:T(8,128)(2,1)} %keys_over_cores.4.refs_2_) | copy-start | bytes 442372
  18.7 1.8 %collective-permute-start.4 = (bf16[576,128]{1,0:T(8,128)(2,1)}, bf16[576,128]{1,0:T(8,128)(2,1)S(1)}, u32[]{:S(2)}, u32[]{:S(2)}) collective-permute-start(bf16[576,128]{1,0:T(8,128)(2,1)} %keys_over_cores.4.refs_2_), channel_id=1, source_target_pairs={{0,1},{1,0},{2,3},{3,2},{4,5},{5,4},{6,7},{7,6},{8,9},{9,8},{10,11... | collective-permute-start | bytes 442376 | tf_op jit(solution)/shard_map/keys_over_cores/ppermute | solution.py:34
  18.8 0.7 copy-start.12
  19.4 1.7 %collective-permute-start.5 = (bf16[576,128]{1,0:T(8,128)(2,1)}, bf16[576,128]{1,0:T(8,128)(2,1)S(1)}, u32[]{:S(2)}, u32[]{:S(2)}) collective-permute-start(bf16[576,128]{1,0:T(8,128)(2,1)} %keys_over_cores.5.refs_3_), channel_id=1, source_target_pairs={{0,1},{1,0},{2,3},{3,2},{4,5},{5,4},{6,7},{7,6},{8,9},{9,8},{10,11... | collective-permute-start | bytes 442376 | tf_op jit(solution)/shard_map/keys_over_cores/ppermute | solution.py:34
  21.1 0.9 copy-start.13
  29.7 15.3 %collective-permute-start.7 = (bf16[64,2048]{1,0:T(8,128)(2,1)S(1)}, bf16[64,2048]{1,0:T(8,128)(2,1)S(1)}, u32[]{:S(2)}, u32[]{:S(2)}) collective-permute-start(bf16[64,2048]{1,0:T(8,128)(2,1)S(1)} %get-tuple-element.15.refs_0_), channel_id=1, source_target_pairs={{0,8},{4,12},{8,0},{12,4},{1,9},{5,13},{9,1},{13,5},{2,10},{6,14},... | collective-permute-start | bytes 786440 | tf_op jit(solution)/shard_map/attended_over_ctx/ppermute | solution.py:34
  32.3 16.2 %collective-permute-start.6 = (bf16[64,2048]{1,0:T(8,128)(2,1)S(1)}, bf16[64,2048]{1,0:T(8,128)(2,1)S(1)}, u32[]{:S(2)}, u32[]{:S(2)}) collective-permute-start(bf16[64,2048]{1,0:T(8,128)(2,1)S(1)} %get-tuple-element.15.refs_0_), channel_id=1, source_target_pairs={{0,4},{4,0},{8,12},{12,8},{1,5},{5,1},{9,13},{13,9},{2,6},{6,2},{1... | collective-permute-start | bytes 786440 | tf_op jit(solution)/shard_map/attended_over_ctx/ppermute | solution.py:34
  39.5 0.7 copy-start.1
  45.0 0.7 copy-start.5
  45.7 15.1 %collective-permute-start.8 = (bf16[64,2048]{1,0:T(8,128)(2,1)}, bf16[64,2048]{1,0:T(8,128)(2,1)S(1)}, u32[]{:S(2)}, u32[]{:S(2)}) collective-permute-start(bf16[64,2048]{1,0:T(8,128)(2,1)} %attended_over_ctx.1.refs_2_), channel_id=1, source_target_pairs={{0,4},{4,0},{8,12},{12,8},{1,5},{5,1},{9,13},{13,9},{2,6},{6,2},{1... | collective-permute-start | bytes 786440 | tf_op jit(solution)/shard_map/attended_over_ctx/ppermute | solution.py:34
  45.7 23.6 %collective-permute-start.10 = (bf16[64,2048]{1,0:T(8,128)(2,1)}, bf16[64,2048]{1,0:T(8,128)(2,1)S(1)}, u32[]{:S(2)}, u32[]{:S(2)}) collective-permute-start(bf16[64,2048]{1,0:T(8,128)(2,1)} %copy-done.1), channel_id=1, source_target_pairs={{0,4},{4,0},{8,12},{12,8},{1,5},{5,1},{9,13},{13,9},{2,6},{6,2},{1... | collective-permute-start | bytes 786440 | tf_op jit(solution)/shard_map/attended_over_ctx/ppermute | solution.py:34
  47.7 21.6 %collective-permute-start.9 = (bf16[64,2048]{1,0:T(8,128)(2,1)}, bf16[64,2048]{1,0:T(8,128)(2,1)S(1)}, u32[]{:S(2)}, u32[]{:S(2)}) collective-permute-start(bf16[64,2048]{1,0:T(8,128)(2,1)} %copy-done.1), channel_id=1, source_target_pairs={{0,8},{4,12},{8,0},{12,4},{1,9},{5,13},{9,1},{13,5},{2,10},{6,14},... | collective-permute-start | bytes 786440 | tf_op jit(solution)/shard_map/attended_over_ctx/ppermute | solution.py:34
  60.8 1.0 copy-start.2
  61.7 0.9 copy-start.6
  68.6 0.8 copy-start.18
  69.3 0.7 copy-start.7
  69.3 0.8 copy-start.9
  70.1 2.0 %collective-permute-start.11 = (bf16[2,4,16,1792]{3,2,1,0:T(8,128)(2,1)}, bf16[2,4,16,1792]{3,2,1,0:T(8,128)(2,1)S(1)}, u32[]{:S(2)}, u32[]{:S(2)}) collective-permute-start(bf16[2,4,16,1792]{3,2,1,0:T(8,128)(2,1)} %sum_over_cores.1), channel_id=1, source_target_pairs={{0,1},{1,0},{2,3},{3,2},{4,5},{5,4},{6,7},{7,6},{8,9},{9,8},{10,11... | collective-permute-start | bytes 1376264 | tf_op jit(solution)/shard_map/sum_over_cores/ppermute | solution.py:34
  72.2 1.7 %copy-start.10 = (bf16[64,2048]{1,0:T(8,128)(2,1)S(1)}, bf16[64,2048]{1,0:T(8,128)(2,1)}, u32[]{:S(2)}) copy-start(bf16[64,2048]{1,0:T(8,128)(2,1)} %copy-done.9) | copy-start | bytes 786436
  72.2 9.8 %copy-start.3 = (bf16[64,2048]{1,0:T(8,128)(2,1)S(1)}, bf16[64,2048]{1,0:T(8,128)(2,1)}, u32[]{:S(2)}) copy-start(bf16[64,2048]{1,0:T(8,128)(2,1)} %copy-done.1) | copy-start | bytes 786436
  72.2 9.8 %copy-start.8 = (bf16[64,2048]{1,0:T(8,128)(2,1)S(1)}, bf16[64,2048]{1,0:T(8,128)(2,1)}, u32[]{:S(2)}) copy-start(bf16[64,2048]{1,0:T(8,128)(2,1)} %copy-done.7) | copy-start | bytes 786436
  72.3 7.7 %collective-permute-start.12 = (bf16[4,16,1792]{2,1,0:T(8,128)(2,1)S(1)}, bf16[4,16,1792]{2,1,0:T(8,128)(2,1)S(1)}, u32[]{:S(2)}, u32[]{:S(2)}) collective-permute-start(bf16[4,16,1792]{2,1,0:T(8,128)(2,1)S(1)} %fusion.2), channel_id=1, source_target_pairs={{0,2},{1,3},{2,0},{3,1},{4,6},{5,7},{6,4},{7,5},{8,10},{9,11},{10,... | collective-permute-start | bytes 688136 | tf_op jit(solution)/shard_map/sum_over_x/ppermute | solution.py:34
  73.8 8.1 %collective-permute-start.16 = (bf16[64,2048]{1,0:T(8,128)(2,1)S(1)}, bf16[64,2048]{1,0:T(8,128)(2,1)S(1)}, u32[]{:S(2)}, u32[]{:S(2)}) collective-permute-start(bf16[64,2048]{1,0:T(8,128)(2,1)S(1)} %copy-done.10), channel_id=1, source_target_pairs={{0,4},{4,0},{8,12},{12,8},{1,5},{5,1},{9,13},{13,9},{2,6},{6,2},{1... | collective-permute-start | bytes 786440 | tf_op jit(solution)/shard_map/attended_over_ctx/ppermute | solution.py:34
  87.8 1.9 %collective-permute-start.17 = (bf16[2,4,16,1792]{3,2,1,0:T(8,128)(2,1)S(1)}, bf16[2,4,16,1792]{3,2,1,0:T(8,128)(2,1)S(1)}, u32[]{:S(2)}, u32[]{:S(2)}) collective-permute-start(bf16[2,4,16,1792]{3,2,1,0:T(8,128)(2,1)S(1)} %get-tuple-element.22), channel_id=1, source_target_pairs={{0,1},{1,0},{2,3},{3,2},{4,5},{5,4},{6,7},{7,6},{8,9},{9,8},{10,11... | collective-permute-start | bytes 1376264 | tf_op jit(solution)/shard_map/sum_over_cores/ppermute | solution.py:34
  89.8 7.7 %collective-permute-start.18 = (bf16[4,16,1792]{2,1,0:T(8,128)(2,1)S(1)}, bf16[4,16,1792]{2,1,0:T(8,128)(2,1)S(1)}, u32[]{:S(2)}, u32[]{:S(2)}) collective-permute-start(bf16[4,16,1792]{2,1,0:T(8,128)(2,1)S(1)} %fusion.3), channel_id=1, source_target_pairs={{0,2},{1,3},{2,0},{3,1},{4,6},{5,7},{6,4},{7,5},{8,10},{9,11},{10,... | collective-permute-start | bytes 688136 | tf_op jit(solution)/shard_map/sum_over_x/ppermute | solution.py:34
  91.5 8.8 %collective-permute-start.15 = (bf16[16,1792]{1,0:T(8,128)(2,1)S(1)}, bf16[16,1792]{1,0:T(8,128)(2,1)S(1)}, u32[]{:S(2)}, u32[]{:S(2)}) collective-permute-start(bf16[16,1792]{1,0:T(8,128)(2,1)S(1)} %get-tuple-element.27), channel_id=1, source_target_pairs={{0,12},{4,8},{8,4},{12,0},{1,13},{5,9},{9,5},{13,1},{2,14},{6,10},... | collective-permute-start | bytes 172040 | tf_op jit(solution)/shard_map/columns_over_ctx/ppermute | solution.py:34
  93.7 8.9 %collective-permute-start.14 = (bf16[16,1792]{1,0:T(8,128)(2,1)S(1)}, bf16[16,1792]{1,0:T(8,128)(2,1)S(1)}, u32[]{:S(2)}, u32[]{:S(2)}) collective-permute-start(bf16[16,1792]{1,0:T(8,128)(2,1)S(1)} %get-tuple-element.28), channel_id=1, source_target_pairs={{0,8},{4,12},{8,0},{12,4},{1,9},{5,13},{9,1},{13,5},{2,10},{6,14},... | collective-permute-start | bytes 172040 | tf_op jit(solution)/shard_map/columns_over_ctx/ppermute | solution.py:34
  93.7 8.9 %collective-permute-start.13 = (bf16[16,1792]{1,0:T(8,128)(2,1)S(1)}, bf16[16,1792]{1,0:T(8,128)(2,1)S(1)}, u32[]{:S(2)}, u32[]{:S(2)}) collective-permute-start(bf16[16,1792]{1,0:T(8,128)(2,1)S(1)} %get-tuple-element.29), channel_id=1, source_target_pairs={{0,4},{4,0},{8,12},{12,8},{1,5},{5,1},{9,13},{13,9},{2,6},{6,2},{1... | collective-permute-start | bytes 172040 | tf_op jit(solution)/shard_map/columns_over_ctx/ppermute | solution.py:34
  98.2 6.2 %collective-permute-start.21 = (bf16[16,1792]{1,0:T(8,128)(2,1)S(1)}, bf16[16,1792]{1,0:T(8,128)(2,1)S(1)}, u32[]{:S(2)}, u32[]{:S(2)}) collective-permute-start(bf16[16,1792]{1,0:T(8,128)(2,1)S(1)} %get-tuple-element.23), channel_id=1, source_target_pairs={{0,12},{4,8},{8,4},{12,0},{1,13},{5,9},{9,5},{13,1},{2,14},{6,10},... | collective-permute-start | bytes 172040 | tf_op jit(solution)/shard_map/columns_over_ctx/ppermute | solution.py:34
  100.4 5.5 %collective-permute-start.20 = (bf16[16,1792]{1,0:T(8,128)(2,1)S(1)}, bf16[16,1792]{1,0:T(8,128)(2,1)S(1)}, u32[]{:S(2)}, u32[]{:S(2)}) collective-permute-start(bf16[16,1792]{1,0:T(8,128)(2,1)S(1)} %get-tuple-element.24), channel_id=1, source_target_pairs={{0,8},{4,12},{8,0},{12,4},{1,9},{5,13},{9,1},{13,5},{2,10},{6,14},... | collective-permute-start | bytes 172040 | tf_op jit(solution)/shard_map/columns_over_ctx/ppermute | solution.py:34
  100.4 5.5 %copy-start.20 = (bf16[16,1792]{1,0:T(8,128)(2,1)}, bf16[16,1792]{1,0:T(8,128)(2,1)S(1)}, u32[]{:S(2)}) copy-start(bf16[16,1792]{1,0:T(8,128)(2,1)S(1)} %collective-permute-done.15.refs_3_) | copy-start | bytes 172036
  100.4 5.4 %collective-permute-start.19 = (bf16[16,1792]{1,0:T(8,128)(2,1)S(1)}, bf16[16,1792]{1,0:T(8,128)(2,1)S(1)}, u32[]{:S(2)}, u32[]{:S(2)}) collective-permute-start(bf16[16,1792]{1,0:T(8,128)(2,1)S(1)} %get-tuple-element.25), channel_id=1, source_target_pairs={{0,4},{4,0},{8,12},{12,8},{1,5},{5,1},{9,13},{13,9},{2,6},{6,2},{1... | collective-permute-start | bytes 172040 | tf_op jit(solution)/shard_map/columns_over_ctx/ppermute | solution.py:34
  102.6 3.2 %copy-start.21 = (bf16[16,1792]{1,0:T(8,128)(2,1)}, bf16[16,1792]{1,0:T(8,128)(2,1)S(1)}, u32[]{:S(2)}) copy-start(bf16[16,1792]{1,0:T(8,128)(2,1)S(1)} %collective-permute-done.14.refs_2_) | copy-start | bytes 172036
  102.6 3.2 %copy-start.22 = (bf16[16,1792]{1,0:T(8,128)(2,1)}, bf16[16,1792]{1,0:T(8,128)(2,1)S(1)}, u32[]{:S(2)}) copy-start(bf16[16,1792]{1,0:T(8,128)(2,1)S(1)} %collective-permute-done.13.refs_1_) | copy-start | bytes 172036
  104.4 1.5 %copy-start.23 = (bf16[16,1792]{1,0:T(8,128)(2,1)}, bf16[16,1792]{1,0:T(8,128)(2,1)S(1)}, u32[]{:S(2)}) copy-start(bf16[16,1792]{1,0:T(8,128)(2,1)S(1)} %collective-permute-done.21.refs_7_) | copy-start | bytes 172036
  105.8 0.6 copy-start.24
  105.8 0.7 copy-start.25

commit v4 on v3

v4 whole, which is shorter than its diff:
```python
import functools
import math

import jax
import jax.numpy as jnp
from jax import lax
from jax.experimental import pallas as pl
from jax.experimental.pallas import tpu as pltpu
from jax.sharding import PartitionSpec as P

LAT = 512
NOPE = 128
ROPE = 64
VD = 128
HEAD = NOPE + ROPE
PROJ = NOPE + VD
CHUNKS = 2
SUB_ROWS = 256
LOAD_LIMIT = 44
MASKED = -1e30
LOG2E = 1.4426950408889634
SCALE = LOG2E / math.sqrt(HEAD)
SHORT = pl.CostEstimate(flops=1024, bytes_accessed=1024, transcendentals=0)
IN_VMEM = pl.BlockSpec(memory_space=pltpu.VMEM)
IN_SMEM = pl.BlockSpec(memory_space=pltpu.SMEM)
IN_HBM = pl.BlockSpec(memory_space=pltpu.HBM)
ANYWHERE = pl.BlockSpec(memory_space=pl.ANY)


def params(mebibytes):
    return pltpu.CompilerParams(vmem_limit_bytes=mebibytes * 1024 * 1024)


def exchange(array, axis, size, bit):
    return lax.ppermute(array, axis, [(i, i ^ bit) for i in range(size)])


def tie_kernel(*refs):
    pass


def tie(array, after):
    if not after:
        return array
    return pl.pallas_call(
        tie_kernel,
        out_shape=jax.ShapeDtypeStruct(array.shape, array.dtype),
        in_specs=[ANYWHERE] * (1 + len(after)),
        out_specs=ANYWHERE,
        input_output_aliases={0: 0},
        compiler_params=params(1),
        cost_estimate=SHORT,
    )(array, *after)


def gather_pieces(own, size, after=()):
    pieces = {0: own}
    bit = size // 2
    while bit:
        for offset in sorted(pieces, reverse=True):
            pieces[offset ^ bit] = exchange(pieces[offset], "ctx", size, bit)
        if bit == size // 2:
            pieces[bit] = tie(pieces[bit], after)
        bit //= 2
    return [pieces[offset] for offset in range(size)]


def load_kernel(owners, piece, cache_rows, order_ref, prefix_ref, q_hbm, up_hbm, own_hbm, *refs):
    q_exts, refs = refs[:CHUNKS], refs[CHUNKS:]
    biases, refs = refs[:CHUNKS], refs[CHUNKS:]
    value_ref, own_ref, q_ref, key_ref, sems, key_sems, value_sems = refs
    rows = q_ref.shape[0]
    head_count = key_ref.shape[0]
    q_copy = pltpu.make_async_copy(q_hbm, q_ref, sems.at[0])
    own_copy = pltpu.make_async_copy(own_hbm, own_ref, sems.at[1])
    q_copy.start()
    key_copies, value_copies = [], []
    for head in range(head_count):
        source = up_hbm.at[:, pl.ds(head * PROJ, NOPE)]
        key_copies.append(pltpu.make_async_copy(source, key_ref.at[head], key_sems.at[head]))
        source = up_hbm.at[:, pl.ds(head * PROJ + NOPE, VD)]
        value_copies.append(pltpu.make_async_copy(source, value_ref.at[head], value_sems.at[head]))
    for copy in key_copies + [own_copy] + value_copies:
        copy.start()
    for chunk, bias_ref in enumerate(biases):
        visible_bias(order_ref, prefix_ref, bias_ref, piece, chunk, own_hbm.shape[1], cache_rows)
    q_copy.wait()
    for head in range(head_count):
        nope = q_ref[:, head * HEAD : head * HEAD + NOPE]
        rope = q_ref[:, head * HEAD + NOPE : (head + 1) * HEAD].astype(jnp.float32) * SCALE
        key_copies[head].wait()
        absorbed = lax.dot_general(
            nope, key_ref[head], (((1,), (1,)), ((), ())), preferred_element_type=jnp.float32
        )
        absorbed = (absorbed * SCALE).reshape(owners, CHUNKS, piece, LAT)
        rope = rope.reshape(owners, CHUNKS, piece, ROPE)
        for chunk, q_ext in enumerate(q_exts):
            part = absorbed[:, chunk].reshape(rows // CHUNKS, LAT)
            q_ext[head, :, :LAT] = part.astype(jnp.bfloat16)
            part = rope[:, chunk].reshape(rows // CHUNKS, ROPE)
            q_ext[head, :, LAT:] = part.astype(jnp.bfloat16)
    for copy in [own_copy] + value_copies:
        copy.wait()


def load(queries, w_kv_up, own_keys, stretch_order, prefix_len, owners, cache_rows):
    rows = queries.shape[0]
    part = rows // CHUNKS
    head_count = w_kv_up.shape[1] // PROJ
    n_ctx = stretch_order.shape[0]
    out_shape = [jax.ShapeDtypeStruct((head_count, part, LAT + ROPE), jnp.bfloat16)] * CHUNKS
    out_shape += [jax.ShapeDtypeStruct((part, n_ctx * own_keys.shape[1]), jnp.float32)] * CHUNKS
    out_shape += [
        jax.ShapeDtypeStruct((head_count, LAT, VD), jnp.bfloat16),
        jax.ShapeDtypeStruct(own_keys.shape, jnp.bfloat16),
    ]
    out = pl.pallas_call(
        functools.partial(load_kernel, owners, part // owners, cache_rows),
        out_shape=out_shape,
        in_specs=[IN_SMEM, IN_SMEM] + [IN_HBM] * 3,
        out_specs=[IN_VMEM] * len(out_shape),
        scratch_shapes=[
            pltpu.VMEM(queries.shape, jnp.bfloat16),
            pltpu.VMEM((head_count, LAT, NOPE), jnp.bfloat16),
            pltpu.SemaphoreType.DMA((2,)),
            pltpu.SemaphoreType.DMA((head_count,)),
            pltpu.SemaphoreType.DMA((head_count,)),
        ],
        compiler_params=params(LOAD_LIMIT),
        cost_estimate=SHORT,
    )(stretch_order, prefix_len, queries, w_kv_up, own_keys)
    return out[:CHUNKS], out[CHUNKS : 2 * CHUNKS], *out[2 * CHUNKS :]


def visible_bias(order_ref, prefix_ref, bias_ref, piece, chunk, row_span, cache_rows):
    n_ctx = order_ref.shape[0]
    half = row_span // 2
    rows = bias_ref.shape[0]
    query_rows = rows * CHUNKS
    own = lax.axis_index("ctx")
    core = lax.axis_index("head") % 2
    blocks = [(0, 0), (0, 1)]
    blocks += [(offset, core) for offset in range(1, n_ctx)]
    blocks += [(offset, 1 - core) for offset in range(1, n_ctx)]
    row = lax.broadcasted_iota(jnp.int32, (rows, half), 0)
    column = lax.broadcasted_iota(jnp.int32, (rows, half), 1)
    owner = row // piece
    query_pos = order_ref[own] * query_rows + owner * (piece * CHUNKS) + chunk * piece + row % piece
    for index, (offset, second) in enumerate(blocks):
        source = own ^ offset
        within = second * half + column
        cache_pos = jnp.where(
            source * cache_rows + within < prefix_ref[0], -1, n_ctx * query_rows
        )
        key_pos = order_ref[source] * query_rows + within - cache_rows
        first_seen = jnp.where(within < cache_rows, cache_pos, key_pos)
        bias = jnp.where(first_seen <= query_pos, 0.0, MASKED).astype(jnp.float32)
        bias_ref[:, index * half : (index + 1) * half] = bias


def attention_kernel(count, q_ref, bias_ref, value_ref, *refs):
    heads, rows, depth = q_ref.shape
    if count:
        piece_refs, (out_ref, keys_ref, latent_ref) = refs[:count], refs[count:]
        start = 0
        for piece_ref in piece_refs:
            width = piece_ref.shape[1]
            keys_ref[:, start : start + width] = piece_ref[...]
            latent_ref[start : start + width, :] = piece_ref[:LAT, :].T
            start += width
    else:
        keys_ref, latent_ref, out_ref = refs
    amount = keys_ref.shape[1]
    group = max(1, min(heads, SUB_ROWS // rows))
    size = group * rows

    def score(first):
        queries = q_ref[first : first + group].reshape(size, depth)
        return jnp.dot(queries, keys_ref[...], preferred_element_type=jnp.float32)

    scores = score(0)
    for first in range(0, heads, group):
        later = score(first + group) if first + group < heads else None
        scores = scores.reshape(group, rows, amount) + bias_ref[...][None]
        top = jnp.max(scores, axis=2, keepdims=True)
        weights = jnp.exp2(scores - top)
        total = jnp.sum(weights, axis=2, keepdims=True).reshape(size, 1)
        mixed = jnp.dot(
            weights.reshape(size, amount).astype(jnp.bfloat16),
            latent_ref[...],
            preferred_element_type=jnp.float32,
        )
        mixed = (mixed / total).astype(jnp.bfloat16)
        for head in range(first, first + group):
            result = jnp.dot(
                mixed[(head - first) * rows : (head - first + 1) * rows],
                value_ref[head],
                preferred_element_type=jnp.float32,
            )
            out_ref[:, head * VD : (head + 1) * VD] = result.astype(jnp.bfloat16)
        scores = later


def attention(q_ext, bias, w_values, keys, gathered):
    head_count, rows, depth = q_ext.shape
    amount = bias.shape[1]
    out_shape = [jax.ShapeDtypeStruct((rows, head_count * VD), jnp.bfloat16)]
    if not gathered:
        out_shape.append(jax.ShapeDtypeStruct((depth, amount), jnp.bfloat16))
        out_shape.append(jax.ShapeDtypeStruct((amount, LAT), jnp.bfloat16))
    return pl.pallas_call(
        functools.partial(attention_kernel, 0 if gathered else len(keys)),
        out_shape=out_shape,
        in_specs=[IN_VMEM] * (3 + len(keys)),
        out_specs=[IN_VMEM] * len(out_shape),
        compiler_params=params(16 if amount <= 1024 else 40),
        cost_estimate=SHORT,
    )(q_ext, bias, w_values, *keys)


def product_kernel(count, n_x, after, weight_ref, *refs):
    piece_refs = refs[:count]
    sent_ref, kept_ref, rows_ref = refs[count + after :]
    rows = piece_refs[0].shape[0]
    columns = weight_ref.shape[1]
    for index, piece_ref in enumerate(piece_refs):
        rows_ref[index * rows : (index + 1) * rows, :] = piece_ref[...]
    is_first = lax.axis_index("head") % 2 == 0
    width = 256 if columns % 256 == 0 else columns
    for start in range(0, columns, width):
        span = slice(start, start + width)
        result = jnp.dot(rows_ref[...], weight_ref[:, span], preferred_element_type=jnp.float32)
        result = result.reshape(count, n_x, 2, rows // (2 * n_x), width)
        for x in range(n_x):
            first, second = result[:, x, 0], result[:, x, 1]
            sent_ref[x, :, :, span] = jnp.where(is_first, second, first).astype(jnp.bfloat16)
            kept_ref[x, :, :, span] = jnp.where(is_first, first, second)


def product(pieces, w_out, n_x, after):
    rows, depth = pieces[0].shape
    count = len(pieces)
    shape = (n_x, count, rows // (2 * n_x), w_out.shape[1])
    return pl.pallas_call(
        functools.partial(product_kernel, count, n_x, len(after)),
        out_shape=[jax.ShapeDtypeStruct(shape, jnp.bfloat16), jax.ShapeDtypeStruct(shape, jnp.float32)],
        in_specs=[IN_VMEM] * (1 + count) + [ANYWHERE] * len(after),
        out_specs=[IN_VMEM, IN_VMEM],
        scratch_shapes=[pltpu.VMEM((count * rows, depth), jnp.bfloat16)],
        compiler_params=params(16),
        cost_estimate=SHORT,
    )(w_out, *pieces, *after)


def place_kernel(n_ctx, ctx_ref, *refs):
    blocks, out_ref = refs[:-1], refs[-1]
    rows = blocks[0].shape[0]
    for offset in range(n_ctx):

        @pl.when(pl.program_id(0) == offset)
        def _():
            for chunk in range(CHUNKS):
                block = blocks[chunk * n_ctx + offset][...]
                out_ref[chunk * rows : (chunk + 1) * rows, :] = block


def place_columns(results, ctx, n_ctx):
    rows, width = results[0][0].shape
    total = rows * len(results)
    if width % 128 or rows % 16:
        out = jnp.zeros((total, n_ctx * width), jnp.bfloat16)
        for offset in range(n_ctx):
            block = jnp.concatenate([result[offset] for result in results], axis=0)
            out = lax.dynamic_update_slice(out, block, (0, (ctx ^ offset) * width))
        return out
    blocks = [block for result in results for block in result]
    return pl.pallas_call(
        functools.partial(place_kernel, n_ctx),
        out_shape=jax.ShapeDtypeStruct((total, n_ctx * width), jnp.bfloat16),
        grid_spec=pltpu.PrefetchScalarGridSpec(
            num_scalar_prefetch=1,
            grid=(n_ctx,),
            in_specs=[IN_VMEM] * len(blocks),
            out_specs=pl.BlockSpec((total, width), lambda i, ctx_ref: (0, ctx_ref[0] ^ i)),
        ),
        compiler_params=params(4),
        cost_estimate=SHORT,
    )(jnp.full((1,), ctx, jnp.int32), *blocks)


def shards(n_ctx, n_head, queries, kv_rows, w_kv_up, w_out, stretch_order, prefix_len):
    query_rows = queries.shape[0]
    row_span = kv_rows.shape[0]
    cache_rows = row_span - query_rows
    half = row_span // 2
    n_x = n_head // 2
    ctx = lax.axis_index("ctx")
    head = lax.axis_index("head")
    x = head // 2

    with jax.named_scope("keys_over_ctx"):
        kv_t = kv_rows.T
        own_half = jnp.where(head % 2 == 0, kv_t[:, :half], kv_t[:, half:])
        halves = [exchange(own_half, "ctx", n_ctx, offset) for offset in range(1, n_ctx)]
    with jax.named_scope("load"):
        q_ext, bias, w_values, own_keys = load(
            queries, w_kv_up, kv_t, stretch_order, prefix_len, n_head, cache_rows
        )
    with jax.named_scope("keys_over_cores"):
        halves = [tie(array, [own_keys]) for array in halves]
        others = [exchange(array, "head", n_head, 1) for array in halves]
    keys = [own_keys] + halves + others
    attended = []
    for chunk in range(CHUNKS):
        with jax.named_scope("attention"):
            result = attention(q_ext[chunk], bias[chunk], w_values, keys, chunk > 0)
        attended.append(result[0])
        if chunk == 0:
            keys = list(result[1:])
    with jax.named_scope("attended_over_ctx"):
        gathered = [gather_pieces(attended[0], n_ctx, attended[1:])]
        for own in attended[1:]:
            gathered.append([own] + [exchange(own, "ctx", n_ctx, d) for d in range(1, n_ctx)])
    results = []
    after = attended[1:]
    for chunk in range(CHUNKS):
        with jax.named_scope("out_product"):
            sent, kept = product(gathered[chunk], w_out, n_x, after)
            after = [sent]
        with jax.named_scope("sum_over_cores"):
            if chunk + 1 < CHUNKS:
                later = gathered[chunk + 1]
                sent = tie(sent, later[1:])
            summed = kept + exchange(sent, "head", n_head, 1).astype(jnp.float32)
        with jax.named_scope("sum_over_x"):
            total = lax.dynamic_index_in_dim(summed, x, 0, keepdims=False)
            for offset in range(1, n_x):
                sent = lax.dynamic_index_in_dim(summed, x ^ offset, 0, keepdims=False)
                sent = exchange(sent.astype(jnp.bfloat16), "head", n_head, 2 * offset)
                total = total + sent.astype(jnp.float32)
        with jax.named_scope("columns_over_ctx"):
            total = total.astype(jnp.bfloat16)
            blocks = [total[0]] + [exchange(total[d], "ctx", n_ctx, d) for d in range(1, n_ctx)]
        results.append(blocks)
    with jax.named_scope("output"):
        return place_columns(results, ctx, n_ctx)


def solution(mesh):
    placed = (
        P(("groups", "ctx"), "head"),
        P(("groups", "ctx"), None),
        P(None, "head"),
        P("head", "ctx"),
        P("groups"),
        P("groups"),
    )
    return jax.shard_map(
        functools.partial(shards, mesh.shape["ctx"], mesh.shape["head"]),
        mesh=mesh,
        in_specs=placed,
        out_specs=P(("groups", "ctx", "head"), None),
        check_vma=False,
    )
```

time: 109 us -> 92.5 us (0.85)
  Pallas kernels: 33.3 us -> 18.9 us
  local copies, waits for them, and re-layouts: 11.9 us -> 2.85 us
  waiting for transfers between devices: 38.1 us -> 41.9 us
  starting transfers between devices: 23.4 us -> 25.4 us
    unnamed x52 -> x10, local copies, waits for them, and re-layouts: 10.6 us -> 2.75 us
    pallas_call x2, Pallas kernels: 11.7 us -> 4.21 us  [product(): pl.pallas_call(functools.partial(product_kernel, count, n_x, len(after)),...]
    pallas_call x3, Pallas kernels: 19.1 us -> 13.4 us  [the longest x2 7.69 us: attention(): pl.pallas_call(functools.partial(attention_kernel, 0 if gathered else len...]
    ppermute x22, waiting for transfers between devices: 38.1 us -> 41.9 us  [exchange(): return lax.ppermute(array, axis, [(i, i ^ bit) for i in range(size)])]
    ppermute x22, starting transfers between devices: 23.4 us -> 25.4 us  [exchange(): return lax.ppermute(array, axis, [(i, i ^ bit) for i in range(size)])]
    squeeze x2, local copies, waits for them, and re-layouts: 1.27 us -> 0.04 us  [shards(): total[d]]
  transfers between devices with their start and end apart: 22 -> 22, of which waited for: 11 -> 10; matrix products, arithmetic and copies ran while one was open for 1% -> 1% of each run, Pallas kernels for 16% -> 13%
where the time goes in v4:
time: 92.5 us; the launch traced here: 92.3 us
  waiting for transfers between devices  41.9 us (45%)
  starting transfers between devices  25.4 us (27%)
  Pallas kernels  18.9 us (20%)
  local copies, waits for them, and re-layouts  2.85 us (3%)
  other arithmetic  2.26 us (2%)
    ppermute x22, waiting for transfers between devices, exchange(): return lax.ppermute(array, axis, [(i, i ^ bit) for i in range(size)])  41.9 us
    ppermute x22, starting transfers between devices, exchange(): return lax.ppermute(array, axis, [(i, i ^ bit) for i in range(size)])  25.4 us
    pallas_call x2, Pallas kernels, attention(): pl.pallas_call(functools.partial(attention_kernel, 0 if gathered else len...  7.69 us
    pallas_call x1, Pallas kernels, load(): pl.pallas_call(functools.partial(load_kernel, owners, part // owners, cac...  5.66 us
    pallas_call x2, Pallas kernels, product(): pl.pallas_call(functools.partial(product_kernel, count, n_x, len(after)),...  4.21 us
    unnamed x10, local copies, waits for them, and re-layouts  2.75 us
  transfers between devices with their start and end apart: 22, of which 10 were waited for; matrix products, arithmetic and copies ran while one was open for 1% of the time, Pallas kernels for 13%

profile of v4, /device:TPU:0, one launch (start us, length us, event | category | flops | bytes accessed | tf_op | source)
XLA Modules:
  0.0 92.3 jit_solution(3047943416486263946)
XLA Ops:
  0.0 1.0 %slice_select_fusion = bf16[576,128]{1,0:T(8,128)(2,1)S(1)} fusion(bf16[576,256]{1,0:T(8,128)(2,1)} %bitcast.32, pred[]{:T(512)S(6)} %eq.5), kind=kLoop, calls=%fused_computation.10 | loop fusion | flops 73728 | bytes 442369 | tf_op jit(solution)/shard_map/keys_over_ctx/jit(_where)/select_n | solution.py:303
  1.0 3.1 %collective-permute-start = (bf16[576,128]{1,0:T(8,128)(2,1)S(1)}, bf16[576,128]{1,0:T(8,128)(2,1)S(1)}, u32[]{:S(2)}, u32[]{:S(2)}) collective-permute-start(bf16[576,128]{1,0:T(8,128)(2,1)S(1)} %slice_select_fusion), channel_id=1, source_target_pairs={{0,4},{4,0},{8,12},{12,8},{1,5},{5,1},{9,13},{13,9},{2,6},{6,2},{1... | collective-permute-start | bytes 442376 | tf_op jit(solution)/shard_map/keys_over_ctx/ppermute | solution.py:35
  4.1 2.6 %collective-permute-start.1 = (bf16[576,128]{1,0:T(8,128)(2,1)S(1)}, bf16[576,128]{1,0:T(8,128)(2,1)S(1)}, u32[]{:S(2)}, u32[]{:S(2)}) collective-permute-start(bf16[576,128]{1,0:T(8,128)(2,1)S(1)} %slice_select_fusion), channel_id=1, source_target_pairs={{0,8},{4,12},{8,0},{12,4},{1,9},{5,13},{9,1},{13,5},{2,10},{6,14},... | collective-permute-start | bytes 442376 | tf_op jit(solution)/shard_map/keys_over_ctx/ppermute | solution.py:35
  6.7 0.0 collective-permute-start.2
  7.3 0.0 copy-start
  7.3 1.0 %copy-done = bf16[256,576]{0,1:T(8,128)(2,1)S(1)} copy-done((bf16[256,576]{0,1:T(8,128)(2,1)S(1)}, bf16[256,576]{0,1:T(8,128)(2,1)}, u32[]{:S(2)}) %copy-start) | copy-done | bytes 294936
  8.3 0.0 copy-start.1
  8.3 1.1 %copy-done.1 = bf16[128,3072]{1,0:T(8,128)(2,1)S(1)} copy-done((bf16[128,3072]{1,0:T(8,128)(2,1)S(1)}, bf16[128,3072]{1,0:T(8,128)(2,1)}, u32[]{:S(2)}) %copy-start.1) | copy-done | bytes 786456
  9.4 0.0 copy-start.2
  9.4 0.7 copy-done.2
  10.1 0.0 slice-start
  10.1 5.7 %load.1 = (bf16[16,64,576]{2,1,0:T(8,128)(2,1)S(1)}, bf16[16,64,576]{2,1,0:T(8,128)(2,1)S(1)}, f32[64,1024]{1,0:T(8,128)S(1)}, f32[64,1024]{1,0:T(8,128)S(1)}, b...) custom-call(s32[4]{0:T(128)S(1)} %copy-done.2, s32[1]{0:T(128)S(6)} %copy.17.prefix_ref, ...), custom_call_target="tpu_custom_call" | custom-call | flops 1024 | bytes 1024 | tf_op jit(solution)/shard_map/load/pallas_call | solution.py:117
  15.8 0.0 collective-permute-done.refs_0_
  15.8 0.1 collective-permute-start.3
  15.9 2.2 %collective-permute-done.1.refs_0_ = bf16[576,128]{1,0:T(8,128)(2,1)S(1)} collective-permute-done((bf16[576,128]{1,0:T(8,128)(2,1)S(1)}, bf16[576,128]{1,0:T(8,128)(2,1)S(1)}, u32[]{:S(2)}, u32[]{:S(2)}) %collective-permute-start.1) | collective-permute-done | bytes 147488 | tf_op jit(solution)/shard_map/keys_over_ctx/ppermute | solution.py:35
  18.1 0.0 collective-permute-start.4
  18.1 0.0 collective-permute-done.2.refs_0_
  18.1 0.5 collective-permute-start.5
  18.6 0.0 collective-permute-done.3.refs_4_
  18.6 0.9 collective-permute-done.4.refs_5_
  19.5 0.2 collective-permute-done.5.refs_6_
  19.7 0.0 slice-start.1
  19.7 3.9 %attention.2 = (bf16[64,2048]{1,0:T(8,128)(2,1)S(1)}, bf16[576,1024]{1,0:T(8,128)(2,1)S(1)}, bf16[1024,512]{1,0:T(8,128)(2,1)S(1)}) custom-call(bf16[16,64,576]{2,1,0:T(8,128)(2,1)S(1)} %get-tuple-element.18.q_ref, f32[64,1024]{1,0:T(8,128)S(1)} %get-tuple-element.19.bias_ref, bf16[16,512,128]{2,1,0:T(8,128)(2,1)S(1)} %get-tuple-element.20.value_ref, ...), custom_call_target="tpu_custom_call" | custom-call | flops 1024 | bytes 1024 | tf_op jit(solution)/shard_map/attention/pallas_call | solution.py:211
  23.6 3.2 %collective-permute-start.7 = (bf16[64,2048]{1,0:T(8,128)(2,1)S(1)}, bf16[64,2048]{1,0:T(8,128)(2,1)S(1)}, u32[]{:S(2)}, u32[]{:S(2)}) collective-permute-start(bf16[64,2048]{1,0:T(8,128)(2,1)S(1)} %get-tuple-element.22.refs_0_), channel_id=1, source_target_pairs={{0,8},{4,12},{8,0},{12,4},{1,9},{5,13},{9,1},{13,5},{2,10},{6,14},... | collective-permute-start | bytes 786440 | tf_op jit(solution)/shard_map/attended_over_ctx/ppermute | solution.py:35
  26.7 0.0 collective-permute-start.6
  26.7 3.8 %attention.3.refs_1_.refs_4_.refs_0_ = bf16[64,2048]{1,0:T(8,128)(2,1)S(1)} custom-call(bf16[16,64,576]{2,1,0:T(8,128)(2,1)S(1)} %get-tuple-element.23.q_ref, f32[64,1024]{1,0:T(8,128)S(1)} %get-tuple-element.24.bias_ref, bf16[16,512,128]{2,1,0:T(8,128)(2,1)S(1)} %get-tuple-element.20.value_ref, bf16[576,1024]{1,0:T(8,128)(2,1)S(1)} %get-tuple-element.25.refs_0_, ...), custom_call_target="tpu_custom_call" | custom-call | flops 1024 | bytes 1024 | tf_op jit(solution)/shard_map/attention/pallas_call | solution.py:211
  30.5 8.5 %collective-permute-done.7.refs_0_ = bf16[64,2048]{1,0:T(8,128)(2,1)S(1)} collective-permute-done((bf16[64,2048]{1,0:T(8,128)(2,1)S(1)}, bf16[64,2048]{1,0:T(8,128)(2,1)S(1)}, u32[]{:S(2)}, u32[]{:S(2)}) %collective-permute-start.7) | collective-permute-done | bytes 262176 | tf_op jit(solution)/shard_map/attended_over_ctx/ppermute | solution.py:35
  39.1 0.0 collective-permute-start.8
  39.1 1.9 %collective-permute-start.11 = (bf16[64,2048]{1,0:T(8,128)(2,1)S(1)}, bf16[64,2048]{1,0:T(8,128)(2,1)S(1)}, u32[]{:S(2)}, u32[]{:S(2)}) collective-permute-start(bf16[64,2048]{1,0:T(8,128)(2,1)S(1)} %attention.3.refs_1_.refs_4_.refs_0_), channel_id=1, source_target_pairs={{0,12},{4,8},{8,4},{12,0},{1,13},{5,9},{9,5},{13,1},{2,14},{6,10},... | collective-permute-start | bytes 786440 | tf_op jit(solution)/shard_map/attended_over_ctx/ppermute | solution.py:35
  40.9 1.6 %collective-permute-start.10 = (bf16[64,2048]{1,0:T(8,128)(2,1)S(1)}, bf16[64,2048]{1,0:T(8,128)(2,1)S(1)}, u32[]{:S(2)}, u32[]{:S(2)}) collective-permute-start(bf16[64,2048]{1,0:T(8,128)(2,1)S(1)} %attention.3.refs_1_.refs_4_.refs_0_), channel_id=1, source_target_pairs={{0,8},{4,12},{8,0},{12,4},{1,9},{5,13},{9,1},{13,5},{2,10},{6,14},... | collective-permute-start | bytes 786440 | tf_op jit(solution)/shard_map/attended_over_ctx/ppermute | solution.py:35
  42.6 0.9 collective-permute-start.9
  43.5 0.0 collective-permute-done.6.refs_1_
  43.5 10.8 %collective-permute-done.8.refs_3_ = bf16[64,2048]{1,0:T(8,128)(2,1)S(1)} collective-permute-done((bf16[64,2048]{1,0:T(8,128)(2,1)S(1)}, bf16[64,2048]{1,0:T(8,128)(2,1)S(1)}, u32[]{:S(2)}, u32[]{:S(2)}) %collective-permute-start.8) | collective-permute-done | bytes 262176 | tf_op jit(solution)/shard_map/attended_over_ctx/ppermute | solution.py:35
  54.3 0.0 slice-done
  54.3 0.0 slice-done.1
  54.3 2.1 %out_product.2 = (bf16[2,4,16,1792]{3,2,1,0:T(8,128)(2,1)S(1)}, f32[2,4,16,1792]{3,2,1,0:T(8,128)S(1)}) custom-call(bf16[2048,1792]{1,0:T(8,128)(2,1)S(1)} %bitcast.31, bf16[64,2048]{1,0:T(8,128)(2,1)S(1)} %get-tuple-element.22.refs_0_, bf16[64,2048]{1,0:T(8,128)(2,1)S(1)} %collective-permute-done.6.refs_1_, bf16[64,2048]{1,0:T(8,128)(2,1)S(1)} %attended_over_ctx.1.refs_2_, ...), custom_call_target="tpu_custom_call" | custom-call | flops 1024 | bytes 1024 | tf_op jit(solution)/shard_map/out_product/pallas_call | solution.py:244
  56.4 0.0 collective-permute-done.11.refs_3_
  56.4 8.5 %collective-permute-done.10.refs_2_ = bf16[64,2048]{1,0:T(8,128)(2,1)S(1)} collective-permute-done((bf16[64,2048]{1,0:T(8,128)(2,1)S(1)}, bf16[64,2048]{1,0:T(8,128)(2,1)S(1)}, u32[]{:S(2)}, u32[]{:S(2)}) %collective-permute-start.10) | collective-permute-done | bytes 262176 | tf_op jit(solution)/shard_map/attended_over_ctx/ppermute | solution.py:35
  64.9 0.0 collective-permute-done.9.refs_1_
  64.9 2.1 %out_product.3 = (bf16[2,4,16,1792]{3,2,1,0:T(8,128)(2,1)S(1)}, f32[2,4,16,1792]{3,2,1,0:T(8,128)S(1)}) custom-call(bf16[2048,1792]{1,0:T(8,128)(2,1)S(1)} %bitcast.31, bf16[64,2048]{1,0:T(8,128)(2,1)S(1)} %attention.3.refs_1_.refs_4_.refs_0_, bf16[64,2048]{1,0:T(8,128)(2,1)S(1)} %collective-permute-done.9.refs_1_, ...), custom_call_target="tpu_custom_call" | custom-call | flops 1024 | bytes 1024 | tf_op jit(solution)/shard_map/out_product/pallas_call | solution.py:244
  67.0 0.1 collective-permute-start.17
  67.1 0.5 collective-permute-start.12
  67.6 1.4 %collective-permute-done.17 = bf16[2,4,16,1792]{3,2,1,0:T(8,128)(2,1)} collective-permute-done((bf16[2,4,16,1792]{3,2,1,0:T(8,128)(2,1)S(1)}, bf16[2,4,16,1792]{3,2,1,0:T(8,128)(2,1)}, u32[]{:S(2)}, u32[]{:S(2)}) %collective-permute-start.17) | collective-permute-done | bytes 458784 | tf_op jit(solution)/shard_map/sum_over_cores/ppermute | solution.py:35
  69.0 1.1 %convert_add_fusion = f32[2,4,16,1792]{3,2,1,0:T(8,128)S(1)} fusion(f32[2,4,16,1792]{3,2,1,0:T(8,128)S(1)} %get-tuple-element.29, bf16[2,4,16,1792]{3,2,1,0:T(8,128)(2,1)} %collective-permute-done.17), kind=kLoop, calls=%fused_computation | loop fusion | flops 458752 | bytes 2293760 | tf_op jit(solution)/shard_map/sum_over_cores/add | solution.py:334
  70.2 1.5 %collective-permute-start.18 = (bf16[4,16,1792]{2,1,0:T(8,128)(2,1)S(1)}, bf16[4,16,1792]{2,1,0:T(8,128)(2,1)S(1)}, u32[]{:S(2)}, u32[]{:S(2)}) collective-permute-start(bf16[4,16,1792]{2,1,0:T(8,128)(2,1)S(1)} %fusion.3), channel_id=1, source_target_pairs={{0,2},{1,3},{2,0},{3,1},{4,6},{5,7},{6,4},{7,5},{8,10},{9,11},{10,... | collective-permute-start | bytes 688136 | tf_op jit(solution)/shard_map/sum_over_x/ppermute | solution.py:35
  71.7 0.0 collective-permute-done.12
  71.7 0.1 convert_add_fusion.1
  71.8 0.6 collective-permute-start.13
  72.5 6.2 %collective-permute-done.18 = bf16[4,16,1792]{2,1,0:T(8,128)(2,1)S(1)} collective-permute-done((bf16[4,16,1792]{2,1,0:T(8,128)(2,1)S(1)}, bf16[4,16,1792]{2,1,0:T(8,128)(2,1)S(1)}, u32[]{:S(2)}, u32[]{:S(2)}) %collective-permute-start.18) | collective-permute-done | bytes 229408 | tf_op jit(solution)/shard_map/sum_over_x/ppermute | solution.py:35
  78.8 1.8 %collective-permute-start.21 = (bf16[16,1792]{1,0:T(8,128)(2,1)S(1)}, bf16[16,1792]{1,0:T(8,128)(2,1)S(1)}, u32[]{:S(2)}, u32[]{:S(2)}) collective-permute-start(bf16[16,1792]{1,0:T(8,128)(2,1)S(1)} %get-tuple-element.31), channel_id=1, source_target_pairs={{0,12},{4,8},{8,4},{12,0},{1,13},{5,9},{9,5},{13,1},{2,14},{6,10},... | collective-permute-start | bytes 172040 | tf_op jit(solution)/shard_map/columns_over_ctx/ppermute | solution.py:35
  80.6 0.0 collective-permute-start.20
  80.6 2.6 %collective-permute-start.19 = (bf16[16,1792]{1,0:T(8,128)(2,1)S(1)}, bf16[16,1792]{1,0:T(8,128)(2,1)S(1)}, u32[]{:S(2)}, u32[]{:S(2)}) collective-permute-start(bf16[16,1792]{1,0:T(8,128)(2,1)S(1)} %get-tuple-element.33), channel_id=1, source_target_pairs={{0,4},{4,0},{8,12},{12,8},{1,5},{5,1},{9,13},{13,9},{2,6},{6,2},{1... | collective-permute-start | bytes 172040 | tf_op jit(solution)/shard_map/columns_over_ctx/ppermute | solution.py:35
  83.2 0.0 collective-permute-done.13
  83.3 1.8 %collective-permute-start.16 = (bf16[16,1792]{1,0:T(8,128)(2,1)S(1)}, bf16[16,1792]{1,0:T(8,128)(2,1)S(1)}, u32[]{:S(2)}, u32[]{:S(2)}) collective-permute-start(bf16[16,1792]{1,0:T(8,128)(2,1)S(1)} %get-tuple-element.35), channel_id=1, source_target_pairs={{0,12},{4,8},{8,4},{12,0},{1,13},{5,9},{9,5},{13,1},{2,14},{6,10},... | collective-permute-start | bytes 172040 | tf_op jit(solution)/shard_map/columns_over_ctx/ppermute | solution.py:35
  85.1 0.0 collective-permute-start.15
  85.1 0.0 collective-permute-done.21.refs_7_
  85.1 2.6 %collective-permute-start.14 = (bf16[16,1792]{1,0:T(8,128)(2,1)S(1)}, bf16[16,1792]{1,0:T(8,128)(2,1)S(1)}, u32[]{:S(2)}, u32[]{:S(2)}) collective-permute-start(bf16[16,1792]{1,0:T(8,128)(2,1)S(1)} %get-tuple-element.37), channel_id=1, source_target_pairs={{0,4},{4,0},{8,12},{12,8},{1,5},{5,1},{9,13},{13,9},{2,6},{6,2},{1... | collective-permute-start | bytes 172040 | tf_op jit(solution)/shard_map/columns_over_ctx/ppermute | solution.py:35
  87.7 0.0 collective-permute-done.20.refs_6_
  87.7 0.0 collective-permute-done.19.refs_5_
  87.8 2.0 %collective-permute-done.16.refs_3_ = bf16[16,1792]{1,0:T(8,128)(2,1)S(1)} collective-permute-done((bf16[16,1792]{1,0:T(8,128)(2,1)S(1)}, bf16[16,1792]{1,0:T(8,128)(2,1)S(1)}, u32[]{:S(2)}, u32[]{:S(2)}) %collective-permute-start.16) | collective-permute-done | bytes 57376 | tf_op jit(solution)/shard_map/columns_over_ctx/ppermute | solution.py:35
  89.8 1.1 %collective-permute-done.15.refs_2_ = bf16[16,1792]{1,0:T(8,128)(2,1)S(1)} collective-permute-done((bf16[16,1792]{1,0:T(8,128)(2,1)S(1)}, bf16[16,1792]{1,0:T(8,128)(2,1)S(1)}, u32[]{:S(2)}, u32[]{:S(2)}) %collective-permute-start.15) | collective-permute-done | bytes 57376 | tf_op jit(solution)/shard_map/columns_over_ctx/ppermute | solution.py:35
  90.9 0.0 collective-permute-done.14.refs_1_
  90.9 1.4 %output.1 = bf16[32,7168]{1,0:T(8,128)(2,1)} custom-call(s32[1]{0:T(128)} %bitcast.ctx_ref, bf16[16,1792]{1,0:T(8,128)(2,1)S(1)} %get-tuple-element.38.refs_0_, bf16[16,1792]{1,0:T(8,128)(2,1)S(1)} %collective-permute-done.14.refs_1_, bf16[16,1792]{1,0:T(8,128)(2,1)S(1)} %collective-permute-done.15.refs_2_, ...), custom_call_target="tpu_custom_call" | custom-call | flops 1024 | bytes 1024 | tf_op jit(solution)/shard_map/output/pallas_call | solution.py:277
  (12 shorter events, 0.2 us)
Async XLA Ops:
  1.0 14.8 %collective-permute-start = (bf16[576,128]{1,0:T(8,128)(2,1)S(1)}, bf16[576,128]{1,0:T(8,128)(2,1)S(1)}, u32[]{:S(2)}, u32[]{:S(2)}) collective-permute-start(bf16[576,128]{1,0:T(8,128)(2,1)S(1)} %slice_select_fusion), channel_id=1, source_target_pairs={{0,4},{4,0},{8,12},{12,8},{1,5},{5,1},{9,13},{13,9},{2,6},{6,2},{1... | collective-permute-start | bytes 442376 | tf_op jit(solution)/shard_map/keys_over_ctx/ppermute | solution.py:35
  4.1 14.0 %collective-permute-start.1 = (bf16[576,128]{1,0:T(8,128)(2,1)S(1)}, bf16[576,128]{1,0:T(8,128)(2,1)S(1)}, u32[]{:S(2)}, u32[]{:S(2)}) collective-permute-start(bf16[576,128]{1,0:T(8,128)(2,1)S(1)} %slice_select_fusion), channel_id=1, source_target_pairs={{0,8},{4,12},{8,0},{12,4},{1,9},{5,13},{9,1},{13,5},{2,10},{6,14},... | collective-permute-start | bytes 442376 | tf_op jit(solution)/shard_map/keys_over_ctx/ppermute | solution.py:35
  6.7 11.4 %collective-permute-start.2 = (bf16[576,128]{1,0:T(8,128)(2,1)S(1)}, bf16[576,128]{1,0:T(8,128)(2,1)S(1)}, u32[]{:S(2)}, u32[]{:S(2)}) collective-permute-start(bf16[576,128]{1,0:T(8,128)(2,1)S(1)} %slice_select_fusion), channel_id=1, source_target_pairs={{0,12},{4,8},{8,4},{12,0},{1,13},{5,9},{9,5},{13,1},{2,14},{6,10},... | collective-permute-start | bytes 442376 | tf_op jit(solution)/shard_map/keys_over_ctx/ppermute | solution.py:35
  7.3 1.0 %copy-start = (bf16[256,576]{0,1:T(8,128)(2,1)S(1)}, bf16[256,576]{0,1:T(8,128)(2,1)}, u32[]{:S(2)}) copy-start(bf16[256,576]{0,1:T(8,128)(2,1)} %param.7) | copy-start | bytes 884740
  8.3 1.1 %copy-start.1 = (bf16[128,3072]{1,0:T(8,128)(2,1)S(1)}, bf16[128,3072]{1,0:T(8,128)(2,1)}, u32[]{:S(2)}) copy-start(bf16[128,3072]{1,0:T(8,128)(2,1)} %q_hbm.1) | copy-start | bytes 2359300
  9.4 0.7 copy-start.2
  10.1 44.2 %slice-start = ((s8[7340032]{0:T(1024)(128)(4,1)}), s8[3145728]{0:T(1024)(128)(4,1)S(1)}, s32[]{:S(2)}) async-start(s8[7340032]{0:T(1024)(128)(4,1)} %bitcast.30), calls=%async_computation | async-start | bytes 6291456
  15.8 2.8 %collective-permute-start.3 = (bf16[576,128]{1,0:T(8,128)(2,1)S(1)}, bf16[576,128]{1,0:T(8,128)(2,1)S(1)}, u32[]{:S(2)}, u32[]{:S(2)}) collective-permute-start(bf16[576,128]{1,0:T(8,128)(2,1)S(1)} %keys_over_cores.3.refs_1_), channel_id=1, source_target_pairs={{0,1},{1,0},{2,3},{3,2},{4,5},{5,4},{6,7},{7,6},{8,9},{9,8},{10,11... | collective-permute-start | bytes 442376 | tf_op jit(solution)/shard_map/keys_over_cores/ppermute | solution.py:35
  18.1 1.4 %collective-permute-start.4 = (bf16[576,128]{1,0:T(8,128)(2,1)S(1)}, bf16[576,128]{1,0:T(8,128)(2,1)S(1)}, u32[]{:S(2)}, u32[]{:S(2)}) collective-permute-start(bf16[576,128]{1,0:T(8,128)(2,1)S(1)} %keys_over_cores.4.refs_2_), channel_id=1, source_target_pairs={{0,1},{1,0},{2,3},{3,2},{4,5},{5,4},{6,7},{7,6},{8,9},{9,8},{10,11... | collective-permute-start | bytes 442376 | tf_op jit(solution)/shard_map/keys_over_cores/ppermute | solution.py:35
  18.1 1.6 %collective-permute-start.5 = (bf16[576,128]{1,0:T(8,128)(2,1)S(1)}, bf16[576,128]{1,0:T(8,128)(2,1)S(1)}, u32[]{:S(2)}, u32[]{:S(2)}) collective-permute-start(bf16[576,128]{1,0:T(8,128)(2,1)S(1)} %keys_over_cores.5.refs_3_), channel_id=1, source_target_pairs={{0,1},{1,0},{2,3},{3,2},{4,5},{5,4},{6,7},{7,6},{8,9},{9,8},{10,11... | collective-permute-start | bytes 442376 | tf_op jit(solution)/shard_map/keys_over_cores/ppermute | solution.py:35
  19.7 34.6 %slice-start.1 = ((s8[7340032]{0:T(1024)(128)(4,1)}), s8[4194304]{0:T(1024)(128)(4,1)S(1)}, s32[]{:S(2)}) async-start(s8[7340032]{0:T(1024)(128)(4,1)} %bitcast.30), calls=%async_computation.1 | async-start | bytes 8388608
  23.6 15.5 %collective-permute-start.7 = (bf16[64,2048]{1,0:T(8,128)(2,1)S(1)}, bf16[64,2048]{1,0:T(8,128)(2,1)S(1)}, u32[]{:S(2)}, u32[]{:S(2)}) collective-permute-start(bf16[64,2048]{1,0:T(8,128)(2,1)S(1)} %get-tuple-element.22.refs_0_), channel_id=1, source_target_pairs={{0,8},{4,12},{8,0},{12,4},{1,9},{5,13},{9,1},{13,5},{2,10},{6,14},... | collective-permute-start | bytes 786440 | tf_op jit(solution)/shard_map/attended_over_ctx/ppermute | solution.py:35
  26.7 16.7 %collective-permute-start.6 = (bf16[64,2048]{1,0:T(8,128)(2,1)S(1)}, bf16[64,2048]{1,0:T(8,128)(2,1)S(1)}, u32[]{:S(2)}, u32[]{:S(2)}) collective-permute-start(bf16[64,2048]{1,0:T(8,128)(2,1)S(1)} %get-tuple-element.22.refs_0_), channel_id=1, source_target_pairs={{0,4},{4,0},{8,12},{12,8},{1,5},{5,1},{9,13},{13,9},{2,6},{6,2},{1... | collective-permute-start | bytes 786440 | tf_op jit(solution)/shard_map/attended_over_ctx/ppermute | solution.py:35
  39.1 15.2 %collective-permute-start.8 = (bf16[64,2048]{1,0:T(8,128)(2,1)S(1)}, bf16[64,2048]{1,0:T(8,128)(2,1)S(1)}, u32[]{:S(2)}, u32[]{:S(2)}) collective-permute-start(bf16[64,2048]{1,0:T(8,128)(2,1)S(1)} %attended_over_ctx.1.refs_2_), channel_id=1, source_target_pairs={{0,4},{4,0},{8,12},{12,8},{1,5},{5,1},{9,13},{13,9},{2,6},{6,2},{1... | collective-permute-start | bytes 786440 | tf_op jit(solution)/shard_map/attended_over_ctx/ppermute | solution.py:35
  39.1 17.3 %collective-permute-start.11 = (bf16[64,2048]{1,0:T(8,128)(2,1)S(1)}, bf16[64,2048]{1,0:T(8,128)(2,1)S(1)}, u32[]{:S(2)}, u32[]{:S(2)}) collective-permute-start(bf16[64,2048]{1,0:T(8,128)(2,1)S(1)} %attention.3.refs_1_.refs_4_.refs_0_), channel_id=1, source_target_pairs={{0,12},{4,8},{8,4},{12,0},{1,13},{5,9},{9,5},{13,1},{2,14},{6,10},... | collective-permute-start | bytes 786440 | tf_op jit(solution)/shard_map/attended_over_ctx/ppermute | solution.py:35
  40.9 24.0 %collective-permute-start.10 = (bf16[64,2048]{1,0:T(8,128)(2,1)S(1)}, bf16[64,2048]{1,0:T(8,128)(2,1)S(1)}, u32[]{:S(2)}, u32[]{:S(2)}) collective-permute-start(bf16[64,2048]{1,0:T(8,128)(2,1)S(1)} %attention.3.refs_1_.refs_4_.refs_0_), channel_id=1, source_target_pairs={{0,8},{4,12},{8,0},{12,4},{1,9},{5,13},{9,1},{13,5},{2,10},{6,14},... | collective-permute-start | bytes 786440 | tf_op jit(solution)/shard_map/attended_over_ctx/ppermute | solution.py:35
  42.6 22.3 %collective-permute-start.9 = (bf16[64,2048]{1,0:T(8,128)(2,1)S(1)}, bf16[64,2048]{1,0:T(8,128)(2,1)S(1)}, u32[]{:S(2)}, u32[]{:S(2)}) collective-permute-start(bf16[64,2048]{1,0:T(8,128)(2,1)S(1)} %attention.3.refs_1_.refs_4_.refs_0_), channel_id=1, source_target_pairs={{0,4},{4,0},{8,12},{12,8},{1,5},{5,1},{9,13},{13,9},{2,6},{6,2},{1... | collective-permute-start | bytes 786440 | tf_op jit(solution)/shard_map/attended_over_ctx/ppermute | solution.py:35
  67.0 2.0 %collective-permute-start.17 = (bf16[2,4,16,1792]{3,2,1,0:T(8,128)(2,1)S(1)}, bf16[2,4,16,1792]{3,2,1,0:T(8,128)(2,1)}, u32[]{:S(2)}, u32[]{:S(2)}) collective-permute-start(bf16[2,4,16,1792]{3,2,1,0:T(8,128)(2,1)S(1)} %get-tuple-element.30), channel_id=1, source_target_pairs={{0,1},{1,0},{2,3},{3,2},{4,5},{5,4},{6,7},{7,6},{8,9},{9,8},{10,11... | collective-permute-start | bytes 1376264 | tf_op jit(solution)/shard_map/sum_over_cores/ppermute | solution.py:35
  67.1 4.6 %collective-permute-start.12 = (bf16[2,4,16,1792]{3,2,1,0:T(8,128)(2,1)S(1)}, bf16[2,4,16,1792]{3,2,1,0:T(8,128)(2,1)S(1)}, u32[]{:S(2)}, u32[]{:S(2)}) collective-permute-start(bf16[2,4,16,1792]{3,2,1,0:T(8,128)(2,1)S(1)} %sum_over_cores.1), channel_id=1, source_target_pairs={{0,1},{1,0},{2,3},{3,2},{4,5},{5,4},{6,7},{7,6},{8,9},{9,8},{10,11... | collective-permute-start | bytes 1376264 | tf_op jit(solution)/shard_map/sum_over_cores/ppermute | solution.py:35
  70.2 8.5 %collective-permute-start.18 = (bf16[4,16,1792]{2,1,0:T(8,128)(2,1)S(1)}, bf16[4,16,1792]{2,1,0:T(8,128)(2,1)S(1)}, u32[]{:S(2)}, u32[]{:S(2)}) collective-permute-start(bf16[4,16,1792]{2,1,0:T(8,128)(2,1)S(1)} %fusion.3), channel_id=1, source_target_pairs={{0,2},{1,3},{2,0},{3,1},{4,6},{5,7},{6,4},{7,5},{8,10},{9,11},{10,... | collective-permute-start | bytes 688136 | tf_op jit(solution)/shard_map/sum_over_x/ppermute | solution.py:35
  71.8 11.4 %collective-permute-start.13 = (bf16[4,16,1792]{2,1,0:T(8,128)(2,1)S(1)}, bf16[4,16,1792]{2,1,0:T(8,128)(2,1)S(1)}, u32[]{:S(2)}, u32[]{:S(2)}) collective-permute-start(bf16[4,16,1792]{2,1,0:T(8,128)(2,1)S(1)} %fusion.2), channel_id=1, source_target_pairs={{0,2},{1,3},{2,0},{3,1},{4,6},{5,7},{6,4},{7,5},{8,10},{9,11},{10,... | collective-permute-start | bytes 688136 | tf_op jit(solution)/shard_map/sum_over_x/ppermute | solution.py:35
  78.8 6.4 %collective-permute-start.21 = (bf16[16,1792]{1,0:T(8,128)(2,1)S(1)}, bf16[16,1792]{1,0:T(8,128)(2,1)S(1)}, u32[]{:S(2)}, u32[]{:S(2)}) collective-permute-start(bf16[16,1792]{1,0:T(8,128)(2,1)S(1)} %get-tuple-element.31), channel_id=1, source_target_pairs={{0,12},{4,8},{8,4},{12,0},{1,13},{5,9},{9,5},{13,1},{2,14},{6,10},... | collective-permute-start | bytes 172040 | tf_op jit(solution)/shard_map/columns_over_ctx/ppermute | solution.py:35
  80.6 7.1 %collective-permute-start.20 = (bf16[16,1792]{1,0:T(8,128)(2,1)S(1)}, bf16[16,1792]{1,0:T(8,128)(2,1)S(1)}, u32[]{:S(2)}, u32[]{:S(2)}) collective-permute-start(bf16[16,1792]{1,0:T(8,128)(2,1)S(1)} %get-tuple-element.32), channel_id=1, source_target_pairs={{0,8},{4,12},{8,0},{12,4},{1,9},{5,13},{9,1},{13,5},{2,10},{6,14},... | collective-permute-start | bytes 172040 | tf_op jit(solution)/shard_map/columns_over_ctx/ppermute | solution.py:35
  80.6 7.1 %collective-permute-start.19 = (bf16[16,1792]{1,0:T(8,128)(2,1)S(1)}, bf16[16,1792]{1,0:T(8,128)(2,1)S(1)}, u32[]{:S(2)}, u32[]{:S(2)}) collective-permute-start(bf16[16,1792]{1,0:T(8,128)(2,1)S(1)} %get-tuple-element.33), channel_id=1, source_target_pairs={{0,4},{4,0},{8,12},{12,8},{1,5},{5,1},{9,13},{13,9},{2,6},{6,2},{1... | collective-permute-start | bytes 172040 | tf_op jit(solution)/shard_map/columns_over_ctx/ppermute | solution.py:35
  83.3 6.5 %collective-permute-start.16 = (bf16[16,1792]{1,0:T(8,128)(2,1)S(1)}, bf16[16,1792]{1,0:T(8,128)(2,1)S(1)}, u32[]{:S(2)}, u32[]{:S(2)}) collective-permute-start(bf16[16,1792]{1,0:T(8,128)(2,1)S(1)} %get-tuple-element.35), channel_id=1, source_target_pairs={{0,12},{4,8},{8,4},{12,0},{1,13},{5,9},{9,5},{13,1},{2,14},{6,10},... | collective-permute-start | bytes 172040 | tf_op jit(solution)/shard_map/columns_over_ctx/ppermute | solution.py:35
  85.1 5.8 %collective-permute-start.15 = (bf16[16,1792]{1,0:T(8,128)(2,1)S(1)}, bf16[16,1792]{1,0:T(8,128)(2,1)S(1)}, u32[]{:S(2)}, u32[]{:S(2)}) collective-permute-start(bf16[16,1792]{1,0:T(8,128)(2,1)S(1)} %get-tuple-element.36), channel_id=1, source_target_pairs={{0,8},{4,12},{8,0},{12,4},{1,9},{5,13},{9,1},{13,5},{2,10},{6,14},... | collective-permute-start | bytes 172040 | tf_op jit(solution)/shard_map/columns_over_ctx/ppermute | solution.py:35
  85.1 5.7 %collective-permute-start.14 = (bf16[16,1792]{1,0:T(8,128)(2,1)S(1)}, bf16[16,1792]{1,0:T(8,128)(2,1)S(1)}, u32[]{:S(2)}, u32[]{:S(2)}) collective-permute-start(bf16[16,1792]{1,0:T(8,128)(2,1)S(1)} %get-tuple-element.37), channel_id=1, source_target_pairs={{0,4},{4,0},{8,12},{12,8},{1,5},{5,1},{9,13},{13,9},{2,6},{6,2},{1... | collective-permute-start | bytes 172040 | tf_op jit(solution)/shard_map/columns_over_ctx/ppermute | solution.py:35

commit v5 on v4

--- a/solution.py
+++ b/solution.py
@@ -57,11 +57,15 @@
     pieces = {0: own}
     bit = size // 2
     while bit:
-        for offset in sorted(pieces, reverse=True):
-            pieces[offset ^ bit] = exchange(pieces[offset], "ctx", size, bit)
-        if bit == size // 2:
-            pieces[bit] = tie(pieces[bit], after)
+        pieces[bit] = exchange(own, "ctx", size, bit)
         bit //= 2
+    bit = 1
+    while bit < size:
+        for offset in range(bit + 1, 2 * bit):
+            if offset == bit + 1:
+                pieces[bit] = tie(pieces[bit], after)
+            pieces[offset] = exchange(pieces[bit], "ctx", size, offset ^ bit)
+        bit *= 2
     return [pieces[offset] for offset in range(size)]
 
 
@@ -318,25 +322,27 @@
         if chunk == 0:
             keys = list(result[1:])
     with jax.named_scope("attended_over_ctx"):
-        gathered = [gather_pieces(attended[0], n_ctx, attended[1:])]
-        for own in attended[1:]:
-            gathered.append([own] + [exchange(own, "ctx", n_ctx, d) for d in range(1, n_ctx)])
+        gathered = [
+            gather_pieces(own, n_ctx, attended[chunk + 1 :]) for chunk, own in enumerate(attended)
+        ]
     results = []
     after = attended[1:]
     for chunk in range(CHUNKS):
         with jax.named_scope("out_product"):
             sent, kept = product(gathered[chunk], w_out, n_x, after)
-            after = [sent]
         with jax.named_scope("sum_over_cores"):
             if chunk + 1 < CHUNKS:
-                later = gathered[chunk + 1]
-                sent = tie(sent, later[1:])
+                received = [gathered[chunk + 1][1], gathered[chunk + 1][n_ctx // 2]]
+            sent = tie(sent, received)
             summed = kept + exchange(sent, "head", n_head, 1).astype(jnp.float32)
+            after = [summed]
         with jax.named_scope("sum_over_x"):
             total = lax.dynamic_index_in_dim(summed, x, 0, keepdims=False)
+            received = []
             for offset in range(1, n_x):
                 sent = lax.dynamic_index_in_dim(summed, x ^ offset, 0, keepdims=False)
                 sent = exchange(sent.astype(jnp.bfloat16), "head", n_head, 2 * offset)
+                received.append(sent)
                 total = total + sent.astype(jnp.float32)
         with jax.named_scope("columns_over_ctx"):
             total = total.astype(jnp.bfloat16)

time: 92.5 us -> 91.1 us (0.985)
  local copies, waits for them, and re-layouts: 2.85 us -> 5.94 us
  waiting for transfers between devices: 41.9 us -> 39.7 us
  starting transfers between devices: 25.4 us -> 24.2 us
  other arithmetic: 2.26 us -> 1.24 us
    unnamed x10 -> x12, local copies, waits for them, and re-layouts: 2.75 us -> 5.83 us
    ppermute x22, waiting for transfers between devices: 41.9 us -> 39.7 us  [exchange(): return lax.ppermute(array, axis, [(i, i ^ bit) for i in range(size)])]
    ppermute x22, starting transfers between devices: 25.4 us -> 24.2 us  [exchange(): return lax.ppermute(array, axis, [(i, i ^ bit) for i in range(size)])]
    add x2, other arithmetic: 1.17 us -> 0.15 us  [shards(): summed = kept + exchange(sent, 'head', n_head, 1).astype(jnp.float32)]
  transfers between devices with their start and end apart: 22 -> 22, of which waited for: 10 -> 12; matrix products, arithmetic and copies ran while one was open for 1% -> 0% of each run, Pallas kernels for 13% -> 15%
where the time goes in v5:
time: 91.1 us; the launch traced here: 90.9 us
  waiting for transfers between devices  39.7 us (44%)
  starting transfers between devices  24.2 us (27%)
  Pallas kernels  18.9 us (21%)
  local copies, waits for them, and re-layouts  5.94 us (7%)
  other arithmetic  1.24 us (1%)
    ppermute x22, waiting for transfers between devices, exchange(): return lax.ppermute(array, axis, [(i, i ^ bit) for i in range(size)])  39.7 us
    ppermute x22, starting transfers between devices, exchange(): return lax.ppermute(array, axis, [(i, i ^ bit) for i in range(size)])  24.2 us
    pallas_call x2, Pallas kernels, attention(): pl.pallas_call(functools.partial(attention_kernel, 0 if gathered else len...  7.69 us
    unnamed x12, local copies, waits for them, and re-layouts  5.83 us
    pallas_call x1, Pallas kernels, load(): pl.pallas_call(functools.partial(load_kernel, owners, part // owners, cac...  5.66 us
    pallas_call x2, Pallas kernels, product(): pl.pallas_call(functools.partial(product_kernel, count, n_x, len(after)),...  4.16 us
  transfers between devices with their start and end apart: 22, of which 12 were waited for; matrix products, arithmetic and copies ran while one was open for 0% of the time, Pallas kernels for 15%

profile of v5, /device:TPU:0, one launch (start us, length us, event | category | flops | bytes accessed | tf_op | source)
XLA Modules:
  0.0 90.9 jit_solution(16413700492862197511)
XLA Ops:
  0.0 1.0 %slice_select_fusion = bf16[576,128]{1,0:T(8,128)(2,1)S(1)} fusion(bf16[576,256]{1,0:T(8,128)(2,1)} %bitcast.32, pred[]{:T(512)S(6)} %eq.5), kind=kLoop, calls=%fused_computation.10 | loop fusion | flops 73728 | bytes 442369 | tf_op jit(solution)/shard_map/keys_over_ctx/jit(_where)/select_n | solution.py:307
  1.0 3.1 %collective-permute-start = (bf16[576,128]{1,0:T(8,128)(2,1)S(1)}, bf16[576,128]{1,0:T(8,128)(2,1)S(1)}, u32[]{:S(2)}, u32[]{:S(2)}) collective-permute-start(bf16[576,128]{1,0:T(8,128)(2,1)S(1)} %slice_select_fusion), channel_id=1, source_target_pairs={{0,4},{4,0},{8,12},{12,8},{1,5},{5,1},{9,13},{13,9},{2,6},{6,2},{1... | collective-permute-start | bytes 442376 | tf_op jit(solution)/shard_map/keys_over_ctx/ppermute | solution.py:35
  4.1 2.6 %collective-permute-start.1 = (bf16[576,128]{1,0:T(8,128)(2,1)S(1)}, bf16[576,128]{1,0:T(8,128)(2,1)S(1)}, u32[]{:S(2)}, u32[]{:S(2)}) collective-permute-start(bf16[576,128]{1,0:T(8,128)(2,1)S(1)} %slice_select_fusion), channel_id=1, source_target_pairs={{0,8},{4,12},{8,0},{12,4},{1,9},{5,13},{9,1},{13,5},{2,10},{6,14},... | collective-permute-start | bytes 442376 | tf_op jit(solution)/shard_map/keys_over_ctx/ppermute | solution.py:35
  6.7 0.0 collective-permute-start.2
  7.3 0.0 copy-start.1
  7.3 1.0 %copy-done.1 = bf16[256,576]{0,1:T(8,128)(2,1)S(1)} copy-done((bf16[256,576]{0,1:T(8,128)(2,1)S(1)}, bf16[256,576]{0,1:T(8,128)(2,1)}, u32[]{:S(2)}) %copy-start.1) | copy-done | bytes 294936
  8.3 0.0 copy-start.2
  8.3 1.1 %copy-done.2 = bf16[128,3072]{1,0:T(8,128)(2,1)S(1)} copy-done((bf16[128,3072]{1,0:T(8,128)(2,1)S(1)}, bf16[128,3072]{1,0:T(8,128)(2,1)}, u32[]{:S(2)}) %copy-start.2) | copy-done | bytes 786456
  9.4 0.0 copy-start.3
  9.4 0.7 copy-done.3
  10.1 0.0 slice-start
  10.1 5.7 %load.1 = (bf16[16,64,576]{2,1,0:T(8,128)(2,1)S(1)}, bf16[16,64,576]{2,1,0:T(8,128)(2,1)S(1)}, f32[64,1024]{1,0:T(8,128)S(1)}, f32[64,1024]{1,0:T(8,128)S(1)}, b...) custom-call(s32[4]{0:T(128)S(1)} %copy-done.3, s32[1]{0:T(128)S(6)} %copy.19.prefix_ref, ...), custom_call_target="tpu_custom_call" | custom-call | flops 1024 | bytes 1024 | tf_op jit(solution)/shard_map/load/pallas_call | solution.py:121
  15.8 0.0 collective-permute-done.refs_0_
  15.8 0.1 collective-permute-start.3
  15.9 2.2 %collective-permute-done.1.refs_0_ = bf16[576,128]{1,0:T(8,128)(2,1)S(1)} collective-permute-done((bf16[576,128]{1,0:T(8,128)(2,1)S(1)}, bf16[576,128]{1,0:T(8,128)(2,1)S(1)}, u32[]{:S(2)}, u32[]{:S(2)}) %collective-permute-start.1) | collective-permute-done | bytes 147488 | tf_op jit(solution)/shard_map/keys_over_ctx/ppermute | solution.py:35
  18.1 0.0 collective-permute-start.4
  18.1 0.0 collective-permute-done.2.refs_0_
  18.1 0.5 collective-permute-start.5
  18.6 0.0 collective-permute-done.3.refs_4_
  18.6 0.9 collective-permute-done.4.refs_5_
  19.5 0.2 collective-permute-done.5.refs_6_
  19.7 3.9 %attention.2 = (bf16[64,2048]{1,0:T(8,128)(2,1)S(1)}, bf16[576,1024]{1,0:T(8,128)(2,1)S(1)}, bf16[1024,512]{1,0:T(8,128)(2,1)S(1)}) custom-call(bf16[16,64,576]{2,1,0:T(8,128)(2,1)S(1)} %get-tuple-element.18.q_ref, f32[64,1024]{1,0:T(8,128)S(1)} %get-tuple-element.19.bias_ref, bf16[16,512,128]{2,1,0:T(8,128)(2,1)S(1)} %get-tuple-element.20.value_ref, ...), custom_call_target="tpu_custom_call" | custom-call | flops 1024 | bytes 1024 | tf_op jit(solution)/shard_map/attention/pallas_call | solution.py:215
  23.6 3.2 %collective-permute-start.7 = (bf16[64,2048]{1,0:T(8,128)(2,1)S(1)}, bf16[64,2048]{1,0:T(8,128)(2,1)S(1)}, u32[]{:S(2)}, u32[]{:S(2)}) collective-permute-start(bf16[64,2048]{1,0:T(8,128)(2,1)S(1)} %get-tuple-element.22.refs_0_), channel_id=1, source_target_pairs={{0,8},{4,12},{8,0},{12,4},{1,9},{5,13},{9,1},{13,5},{2,10},{6,14},... | collective-permute-start | bytes 786440 | tf_op jit(solution)/shard_map/attended_over_ctx/ppermute | solution.py:35
  26.7 0.0 collective-permute-start.6
  26.7 3.8 %attention.3.refs_1_.refs_4_.refs_0_ = bf16[64,2048]{1,0:T(8,128)(2,1)S(1)} custom-call(bf16[16,64,576]{2,1,0:T(8,128)(2,1)S(1)} %get-tuple-element.23.q_ref, f32[64,1024]{1,0:T(8,128)S(1)} %get-tuple-element.24.bias_ref, bf16[16,512,128]{2,1,0:T(8,128)(2,1)S(1)} %get-tuple-element.20.value_ref, bf16[576,1024]{1,0:T(8,128)(2,1)S(1)} %get-tuple-element.25.refs_0_, ...), custom_call_target="tpu_custom_call" | custom-call | flops 1024 | bytes 1024 | tf_op jit(solution)/shard_map/attention/pallas_call | solution.py:215
  30.5 8.5 %collective-permute-done.7.refs_0_ = bf16[64,2048]{1,0:T(8,128)(2,1)S(1)} collective-permute-done((bf16[64,2048]{1,0:T(8,128)(2,1)S(1)}, bf16[64,2048]{1,0:T(8,128)(2,1)S(1)}, u32[]{:S(2)}, u32[]{:S(2)}) %collective-permute-start.7) | collective-permute-done | bytes 262176 | tf_op jit(solution)/shard_map/attended_over_ctx/ppermute | solution.py:35
  39.1 0.0 collective-permute-start.8
  39.1 2.4 %collective-permute-start.10 = (bf16[64,2048]{1,0:T(8,128)(2,1)S(1)}, bf16[64,2048]{1,0:T(8,128)(2,1)S(1)}, u32[]{:S(2)}, u32[]{:S(2)}) collective-permute-start(bf16[64,2048]{1,0:T(8,128)(2,1)S(1)} %attention.3.refs_1_.refs_4_.refs_0_), channel_id=1, source_target_pairs={{0,8},{4,12},{8,0},{12,4},{1,9},{5,13},{9,1},{13,5},{2,10},{6,14},... | collective-permute-start | bytes 786440 | tf_op jit(solution)/shard_map/attended_over_ctx/ppermute | solution.py:35
  41.5 0.0 collective-permute-start.9
  41.5 0.0 collective-permute-done.6.refs_1_
  41.5 12.0 %collective-permute-done.8.refs_3_ = bf16[64,2048]{1,0:T(8,128)(2,1)S(1)} collective-permute-done((bf16[64,2048]{1,0:T(8,128)(2,1)S(1)}, bf16[64,2048]{1,0:T(8,128)(2,1)S(1)}, u32[]{:S(2)}, u32[]{:S(2)}) %collective-permute-start.8) | collective-permute-done | bytes 262176 | tf_op jit(solution)/shard_map/attended_over_ctx/ppermute | solution.py:35
  53.5 0.0 slice-done
  53.5 0.0 slice-done.1
  53.5 2.1 %out_product.2 = (bf16[2,4,16,1792]{3,2,1,0:T(8,128)(2,1)S(1)}, f32[2,4,16,1792]{3,2,1,0:T(8,128)S(1)}) custom-call(bf16[2048,1792]{1,0:T(8,128)(2,1)S(1)} %bitcast.31, bf16[64,2048]{1,0:T(8,128)(2,1)S(1)} %get-tuple-element.22.refs_0_, bf16[64,2048]{1,0:T(8,128)(2,1)S(1)} %collective-permute-done.6.refs_1_, bf16[64,2048]{1,0:T(8,128)(2,1)S(1)} %attended_over_ctx.1.refs_2_, ...), custom_call_target="tpu_custom_call" | custom-call | flops 1024 | bytes 1024 | tf_op jit(solution)/shard_map/out_product/pallas_call | solution.py:248
  55.6 0.0 collective-permute-done.10.refs_2_
  55.7 2.4 %collective-permute-done.9.refs_1_ = bf16[64,2048]{1,0:T(8,128)(2,1)S(1)} collective-permute-done((bf16[64,2048]{1,0:T(8,128)(2,1)S(1)}, bf16[64,2048]{1,0:T(8,128)(2,1)S(1)}, u32[]{:S(2)}, u32[]{:S(2)}) %collective-permute-start.9) | collective-permute-done | bytes 262176 | tf_op jit(solution)/shard_map/attended_over_ctx/ppermute | solution.py:35
  58.1 0.0 collective-permute-start.11
  58.1 0.3 collective-permute-start.16
  58.4 1.5 %collective-permute-done.11 = bf16[2,4,16,1792]{3,2,1,0:T(8,128)(2,1)S(1)} collective-permute-done((bf16[2,4,16,1792]{3,2,1,0:T(8,128)(2,1)S(1)}, bf16[2,4,16,1792]{3,2,1,0:T(8,128)(2,1)S(1)}, u32[]{:S(2)}, u32[]{:S(2)}) %collective-permute-start.11) | collective-permute-done | bytes 458784 | tf_op jit(solution)/shard_map/sum_over_cores/ppermute | solution.py:35
  59.9 0.1 convert_add_fusion.1.refs_4_
  60.0 1.5 %collective-permute-start.12 = (bf16[4,16,1792]{2,1,0:T(8,128)(2,1)S(1)}, bf16[4,16,1792]{2,1,0:T(8,128)(2,1)S(1)}, u32[]{:S(2)}, u32[]{:S(2)}) collective-permute-start(bf16[4,16,1792]{2,1,0:T(8,128)(2,1)S(1)} %fusion.2), channel_id=1, source_target_pairs={{0,2},{1,3},{2,0},{3,1},{4,6},{5,7},{6,4},{7,5},{8,10},{9,11},{10,... | collective-permute-start | bytes 688136 | tf_op jit(solution)/shard_map/sum_over_x/ppermute | solution.py:35
  61.6 5.3 %collective-permute-done.16.refs_3_ = bf16[64,2048]{1,0:T(8,128)(2,1)S(1)} collective-permute-done((bf16[64,2048]{1,0:T(8,128)(2,1)S(1)}, bf16[64,2048]{1,0:T(8,128)(2,1)S(1)}, u32[]{:S(2)}, u32[]{:S(2)}) %collective-permute-start.16) | collective-permute-done | bytes 262176 | tf_op jit(solution)/shard_map/attended_over_ctx/ppermute | solution.py:35
  66.8 0.0 copy-start
  66.8 3.1 %copy-done = bf16[2048,1792]{1,0:T(8,128)(2,1)S(1)} copy-done((bf16[2048,1792]{1,0:T(8,128)(2,1)S(1)}, bf16[2048,1792]{1,0:T(8,128)(2,1)}, u32[]{:S(2)}) %copy-start) | copy-done | bytes 7340056
  69.9 2.1 %out_product.3 = (bf16[2,4,16,1792]{3,2,1,0:T(8,128)(2,1)S(1)}, f32[2,4,16,1792]{3,2,1,0:T(8,128)S(1)}) custom-call(bf16[2048,1792]{1,0:T(8,128)(2,1)S(1)} %copy-done, bf16[64,2048]{1,0:T(8,128)(2,1)S(1)} %attention.3.refs_1_.refs_4_.refs_0_, bf16[64,2048]{1,0:T(8,128)(2,1)S(1)} %collective-permute-done.9.refs_1_, ...), custom_call_target="tpu_custom_call" | custom-call | flops 1024 | bytes 1024 | tf_op jit(solution)/shard_map/out_product/pallas_call | solution.py:248
  72.0 0.0 collective-permute-done.12.refs_1_
  72.0 0.1 collective-permute-start.17
  72.1 1.7 %collective-permute-done.17 = bf16[2,4,16,1792]{3,2,1,0:T(8,128)(2,1)S(1)} collective-permute-done((bf16[2,4,16,1792]{3,2,1,0:T(8,128)(2,1)S(1)}, bf16[2,4,16,1792]{3,2,1,0:T(8,128)(2,1)S(1)}, u32[]{:S(2)}, u32[]{:S(2)}) %collective-permute-start.17) | collective-permute-done | bytes 458784 | tf_op jit(solution)/shard_map/sum_over_cores/ppermute | solution.py:35
  73.9 0.1 convert_add_fusion
  74.0 1.5 %collective-permute-start.18 = (bf16[4,16,1792]{2,1,0:T(8,128)(2,1)S(1)}, bf16[4,16,1792]{2,1,0:T(8,128)(2,1)S(1)}, u32[]{:S(2)}, u32[]{:S(2)}) collective-permute-start(bf16[4,16,1792]{2,1,0:T(8,128)(2,1)S(1)} %fusion.3), channel_id=1, source_target_pairs={{0,2},{1,3},{2,0},{3,1},{4,6},{5,7},{6,4},{7,5},{8,10},{9,11},{10,... | collective-permute-start | bytes 688136 | tf_op jit(solution)/shard_map/sum_over_x/ppermute | solution.py:35
  75.5 1.9 %collective-permute-start.15 = (bf16[16,1792]{1,0:T(8,128)(2,1)S(1)}, bf16[16,1792]{1,0:T(8,128)(2,1)S(1)}, u32[]{:S(2)}, u32[]{:S(2)}) collective-permute-start(bf16[16,1792]{1,0:T(8,128)(2,1)S(1)} %get-tuple-element.35), channel_id=1, source_target_pairs={{0,12},{4,8},{8,4},{12,0},{1,13},{5,9},{9,5},{13,1},{2,14},{6,10},... | collective-permute-start | bytes 172040 | tf_op jit(solution)/shard_map/columns_over_ctx/ppermute | solution.py:35
  77.4 0.0 collective-permute-start.14
  77.4 2.6 %collective-permute-start.13 = (bf16[16,1792]{1,0:T(8,128)(2,1)S(1)}, bf16[16,1792]{1,0:T(8,128)(2,1)S(1)}, u32[]{:S(2)}, u32[]{:S(2)}) collective-permute-start(bf16[16,1792]{1,0:T(8,128)(2,1)S(1)} %get-tuple-element.37), channel_id=1, source_target_pairs={{0,4},{4,0},{8,12},{12,8},{1,5},{5,1},{9,13},{13,9},{2,6},{6,2},{1... | collective-permute-start | bytes 172040 | tf_op jit(solution)/shard_map/columns_over_ctx/ppermute | solution.py:35
  80.0 1.7 %collective-permute-done.18 = bf16[4,16,1792]{2,1,0:T(8,128)(2,1)S(1)} collective-permute-done((bf16[4,16,1792]{2,1,0:T(8,128)(2,1)S(1)}, bf16[4,16,1792]{2,1,0:T(8,128)(2,1)S(1)}, u32[]{:S(2)}, u32[]{:S(2)}) %collective-permute-start.18) | collective-permute-done | bytes 229408 | tf_op jit(solution)/shard_map/sum_over_x/ppermute | solution.py:35
  81.8 1.8 %collective-permute-start.21 = (bf16[16,1792]{1,0:T(8,128)(2,1)S(1)}, bf16[16,1792]{1,0:T(8,128)(2,1)S(1)}, u32[]{:S(2)}, u32[]{:S(2)}) collective-permute-start(bf16[16,1792]{1,0:T(8,128)(2,1)S(1)} %get-tuple-element.31), channel_id=1, source_target_pairs={{0,12},{4,8},{8,4},{12,0},{1,13},{5,9},{9,5},{13,1},{2,14},{6,10},... | collective-permute-start | bytes 172040 | tf_op jit(solution)/shard_map/columns_over_ctx/ppermute | solution.py:35
  83.6 0.0 collective-permute-start.20
  83.6 0.0 collective-permute-done.15.refs_3_
  83.6 2.6 %collective-permute-start.19 = (bf16[16,1792]{1,0:T(8,128)(2,1)S(1)}, bf16[16,1792]{1,0:T(8,128)(2,1)S(1)}, u32[]{:S(2)}, u32[]{:S(2)}) collective-permute-start(bf16[16,1792]{1,0:T(8,128)(2,1)S(1)} %get-tuple-element.33), channel_id=1, source_target_pairs={{0,4},{4,0},{8,12},{12,8},{1,5},{5,1},{9,13},{13,9},{2,6},{6,2},{1... | collective-permute-start | bytes 172040 | tf_op jit(solution)/shard_map/columns_over_ctx/ppermute | solution.py:35
  86.2 0.0 collective-permute-done.14.refs_2_
  86.2 0.0 collective-permute-done.13.refs_1_
  86.3 2.1 %collective-permute-done.21.refs_7_ = bf16[16,1792]{1,0:T(8,128)(2,1)S(1)} collective-permute-done((bf16[16,1792]{1,0:T(8,128)(2,1)S(1)}, bf16[16,1792]{1,0:T(8,128)(2,1)S(1)}, u32[]{:S(2)}, u32[]{:S(2)}) %collective-permute-start.21) | collective-permute-done | bytes 57376 | tf_op jit(solution)/shard_map/columns_over_ctx/ppermute | solution.py:35
  88.4 1.1 %collective-permute-done.20.refs_6_ = bf16[16,1792]{1,0:T(8,128)(2,1)S(1)} collective-permute-done((bf16[16,1792]{1,0:T(8,128)(2,1)S(1)}, bf16[16,1792]{1,0:T(8,128)(2,1)S(1)}, u32[]{:S(2)}, u32[]{:S(2)}) %collective-permute-start.20) | collective-permute-done | bytes 57376 | tf_op jit(solution)/shard_map/columns_over_ctx/ppermute | solution.py:35
  89.5 0.0 collective-permute-done.19.refs_5_
  89.5 1.4 %output.1 = bf16[32,7168]{1,0:T(8,128)(2,1)} custom-call(s32[1]{0:T(128)} %bitcast.ctx_ref, bf16[16,1792]{1,0:T(8,128)(2,1)S(1)} %get-tuple-element.38.refs_0_, bf16[16,1792]{1,0:T(8,128)(2,1)S(1)} %collective-permute-done.13.refs_1_, bf16[16,1792]{1,0:T(8,128)(2,1)S(1)} %collective-permute-done.14.refs_2_, ...), custom_call_target="tpu_custom_call" | custom-call | flops 1024 | bytes 1024 | tf_op jit(solution)/shard_map/output/pallas_call | solution.py:281
  (14 shorter events, 0.2 us)
Async XLA Ops:
  1.0 14.8 %collective-permute-start = (bf16[576,128]{1,0:T(8,128)(2,1)S(1)}, bf16[576,128]{1,0:T(8,128)(2,1)S(1)}, u32[]{:S(2)}, u32[]{:S(2)}) collective-permute-start(bf16[576,128]{1,0:T(8,128)(2,1)S(1)} %slice_select_fusion), channel_id=1, source_target_pairs={{0,4},{4,0},{8,12},{12,8},{1,5},{5,1},{9,13},{13,9},{2,6},{6,2},{1... | collective-permute-start | bytes 442376 | tf_op jit(solution)/shard_map/keys_over_ctx/ppermute | solution.py:35
  4.1 14.0 %collective-permute-start.1 = (bf16[576,128]{1,0:T(8,128)(2,1)S(1)}, bf16[576,128]{1,0:T(8,128)(2,1)S(1)}, u32[]{:S(2)}, u32[]{:S(2)}) collective-permute-start(bf16[576,128]{1,0:T(8,128)(2,1)S(1)} %slice_select_fusion), channel_id=1, source_target_pairs={{0,8},{4,12},{8,0},{12,4},{1,9},{5,13},{9,1},{13,5},{2,10},{6,14},... | collective-permute-start | bytes 442376 | tf_op jit(solution)/shard_map/keys_over_ctx/ppermute | solution.py:35
  6.7 11.4 %collective-permute-start.2 = (bf16[576,128]{1,0:T(8,128)(2,1)S(1)}, bf16[576,128]{1,0:T(8,128)(2,1)S(1)}, u32[]{:S(2)}, u32[]{:S(2)}) collective-permute-start(bf16[576,128]{1,0:T(8,128)(2,1)S(1)} %slice_select_fusion), channel_id=1, source_target_pairs={{0,12},{4,8},{8,4},{12,0},{1,13},{5,9},{9,5},{13,1},{2,14},{6,10},... | collective-permute-start | bytes 442376 | tf_op jit(solution)/shard_map/keys_over_ctx/ppermute | solution.py:35
  7.3 1.0 %copy-start.1 = (bf16[256,576]{0,1:T(8,128)(2,1)S(1)}, bf16[256,576]{0,1:T(8,128)(2,1)}, u32[]{:S(2)}) copy-start(bf16[256,576]{0,1:T(8,128)(2,1)} %param.7) | copy-start | bytes 884740
  8.3 1.1 %copy-start.2 = (bf16[128,3072]{1,0:T(8,128)(2,1)S(1)}, bf16[128,3072]{1,0:T(8,128)(2,1)}, u32[]{:S(2)}) copy-start(bf16[128,3072]{1,0:T(8,128)(2,1)} %q_hbm.1) | copy-start | bytes 2359300
  9.4 0.7 copy-start.3
  10.1 43.4 %slice-start = ((s8[7340032]{0:T(1024)(128)(4,1)}), s8[3145728]{0:T(1024)(128)(4,1)S(1)}, s32[]{:S(2)}) async-start(s8[7340032]{0:T(1024)(128)(4,1)} %bitcast.30), calls=%async_computation | async-start | bytes 6291456
  15.8 2.8 %collective-permute-start.3 = (bf16[576,128]{1,0:T(8,128)(2,1)S(1)}, bf16[576,128]{1,0:T(8,128)(2,1)S(1)}, u32[]{:S(2)}, u32[]{:S(2)}) collective-permute-start(bf16[576,128]{1,0:T(8,128)(2,1)S(1)} %keys_over_cores.3.refs_1_), channel_id=1, source_target_pairs={{0,1},{1,0},{2,3},{3,2},{4,5},{5,4},{6,7},{7,6},{8,9},{9,8},{10,11... | collective-permute-start | bytes 442376 | tf_op jit(solution)/shard_map/keys_over_cores/ppermute | solution.py:35
  18.1 1.4 %collective-permute-start.4 = (bf16[576,128]{1,0:T(8,128)(2,1)S(1)}, bf16[576,128]{1,0:T(8,128)(2,1)S(1)}, u32[]{:S(2)}, u32[]{:S(2)}) collective-permute-start(bf16[576,128]{1,0:T(8,128)(2,1)S(1)} %keys_over_cores.4.refs_2_), channel_id=1, source_target_pairs={{0,1},{1,0},{2,3},{3,2},{4,5},{5,4},{6,7},{7,6},{8,9},{9,8},{10,11... | collective-permute-start | bytes 442376 | tf_op jit(solution)/shard_map/keys_over_cores/ppermute | solution.py:35
  18.1 1.6 %collective-permute-start.5 = (bf16[576,128]{1,0:T(8,128)(2,1)S(1)}, bf16[576,128]{1,0:T(8,128)(2,1)S(1)}, u32[]{:S(2)}, u32[]{:S(2)}) collective-permute-start(bf16[576,128]{1,0:T(8,128)(2,1)S(1)} %keys_over_cores.5.refs_3_), channel_id=1, source_target_pairs={{0,1},{1,0},{2,3},{3,2},{4,5},{5,4},{6,7},{7,6},{8,9},{9,8},{10,11... | collective-permute-start | bytes 442376 | tf_op jit(solution)/shard_map/keys_over_cores/ppermute | solution.py:35
  19.7 33.9 %slice-start.1 = ((s8[7340032]{0:T(1024)(128)(4,1)}), s8[4194304]{0:T(1024)(128)(4,1)S(1)}, s32[]{:S(2)}) async-start(s8[7340032]{0:T(1024)(128)(4,1)} %bitcast.30), calls=%async_computation.1 | async-start | bytes 8388608
  23.6 15.5 %collective-permute-start.7 = (bf16[64,2048]{1,0:T(8,128)(2,1)S(1)}, bf16[64,2048]{1,0:T(8,128)(2,1)S(1)}, u32[]{:S(2)}, u32[]{:S(2)}) collective-permute-start(bf16[64,2048]{1,0:T(8,128)(2,1)S(1)} %get-tuple-element.22.refs_0_), channel_id=1, source_target_pairs={{0,8},{4,12},{8,0},{12,4},{1,9},{5,13},{9,1},{13,5},{2,10},{6,14},... | collective-permute-start | bytes 786440 | tf_op jit(solution)/shard_map/attended_over_ctx/ppermute | solution.py:35
  26.7 14.8 %collective-permute-start.6 = (bf16[64,2048]{1,0:T(8,128)(2,1)S(1)}, bf16[64,2048]{1,0:T(8,128)(2,1)S(1)}, u32[]{:S(2)}, u32[]{:S(2)}) collective-permute-start(bf16[64,2048]{1,0:T(8,128)(2,1)S(1)} %get-tuple-element.22.refs_0_), channel_id=1, source_target_pairs={{0,4},{4,0},{8,12},{12,8},{1,5},{5,1},{9,13},{13,9},{2,6},{6,2},{1... | collective-permute-start | bytes 786440 | tf_op jit(solution)/shard_map/attended_over_ctx/ppermute | solution.py:35
  39.1 14.5 %collective-permute-start.8 = (bf16[64,2048]{1,0:T(8,128)(2,1)S(1)}, bf16[64,2048]{1,0:T(8,128)(2,1)S(1)}, u32[]{:S(2)}, u32[]{:S(2)}) collective-permute-start(bf16[64,2048]{1,0:T(8,128)(2,1)S(1)} %attended_over_ctx.1.refs_2_), channel_id=1, source_target_pairs={{0,4},{4,0},{8,12},{12,8},{1,5},{5,1},{9,13},{13,9},{2,6},{6,2},{1... | collective-permute-start | bytes 786440 | tf_op jit(solution)/shard_map/attended_over_ctx/ppermute | solution.py:35
  39.1 16.6 %collective-permute-start.10 = (bf16[64,2048]{1,0:T(8,128)(2,1)S(1)}, bf16[64,2048]{1,0:T(8,128)(2,1)S(1)}, u32[]{:S(2)}, u32[]{:S(2)}) collective-permute-start(bf16[64,2048]{1,0:T(8,128)(2,1)S(1)} %attention.3.refs_1_.refs_4_.refs_0_), channel_id=1, source_target_pairs={{0,8},{4,12},{8,0},{12,4},{1,9},{5,13},{9,1},{13,5},{2,10},{6,14},... | collective-permute-start | bytes 786440 | tf_op jit(solution)/shard_map/attended_over_ctx/ppermute | solution.py:35
  41.5 16.6 %collective-permute-start.9 = (bf16[64,2048]{1,0:T(8,128)(2,1)S(1)}, bf16[64,2048]{1,0:T(8,128)(2,1)S(1)}, u32[]{:S(2)}, u32[]{:S(2)}) collective-permute-start(bf16[64,2048]{1,0:T(8,128)(2,1)S(1)} %attention.3.refs_1_.refs_4_.refs_0_), channel_id=1, source_target_pairs={{0,4},{4,0},{8,12},{12,8},{1,5},{5,1},{9,13},{13,9},{2,6},{6,2},{1... | collective-permute-start | bytes 786440 | tf_op jit(solution)/shard_map/attended_over_ctx/ppermute | solution.py:35
  58.1 1.8 %collective-permute-start.11 = (bf16[2,4,16,1792]{3,2,1,0:T(8,128)(2,1)S(1)}, bf16[2,4,16,1792]{3,2,1,0:T(8,128)(2,1)S(1)}, u32[]{:S(2)}, u32[]{:S(2)}) collective-permute-start(bf16[2,4,16,1792]{3,2,1,0:T(8,128)(2,1)S(1)} %sum_over_cores.2), channel_id=1, source_target_pairs={{0,1},{1,0},{2,3},{3,2},{4,5},{5,4},{6,7},{7,6},{8,9},{9,8},{10,11... | collective-permute-start | bytes 1376264 | tf_op jit(solution)/shard_map/sum_over_cores/ppermute | solution.py:35
  58.1 8.7 %collective-permute-start.16 = (bf16[64,2048]{1,0:T(8,128)(2,1)S(1)}, bf16[64,2048]{1,0:T(8,128)(2,1)S(1)}, u32[]{:S(2)}, u32[]{:S(2)}) collective-permute-start(bf16[64,2048]{1,0:T(8,128)(2,1)S(1)} %collective-permute-done.10.refs_2_), channel_id=1, source_target_pairs={{0,4},{4,0},{8,12},{12,8},{1,5},{5,1},{9,13},{13,9},{2,6},{6,2},{1... | collective-permute-start | bytes 786440 | tf_op jit(solution)/shard_map/attended_over_ctx/ppermute | solution.py:35
  60.0 11.9 %collective-permute-start.12 = (bf16[4,16,1792]{2,1,0:T(8,128)(2,1)S(1)}, bf16[4,16,1792]{2,1,0:T(8,128)(2,1)S(1)}, u32[]{:S(2)}, u32[]{:S(2)}) collective-permute-start(bf16[4,16,1792]{2,1,0:T(8,128)(2,1)S(1)} %fusion.2), channel_id=1, source_target_pairs={{0,2},{1,3},{2,0},{3,1},{4,6},{5,7},{6,4},{7,5},{8,10},{9,11},{10,... | collective-permute-start | bytes 688136 | tf_op jit(solution)/shard_map/sum_over_x/ppermute | solution.py:35
  66.8 3.1 %copy-start = (bf16[2048,1792]{1,0:T(8,128)(2,1)S(1)}, bf16[2048,1792]{1,0:T(8,128)(2,1)}, u32[]{:S(2)}) copy-start(bf16[2048,1792]{1,0:T(8,128)(2,1)} %weight_ref.3) | copy-start | bytes 22020100
  72.0 1.9 %collective-permute-start.17 = (bf16[2,4,16,1792]{3,2,1,0:T(8,128)(2,1)S(1)}, bf16[2,4,16,1792]{3,2,1,0:T(8,128)(2,1)S(1)}, u32[]{:S(2)}, u32[]{:S(2)}) collective-permute-start(bf16[2,4,16,1792]{3,2,1,0:T(8,128)(2,1)S(1)} %sum_over_cores.3), channel_id=1, source_target_pairs={{0,1},{1,0},{2,3},{3,2},{4,5},{5,4},{6,7},{7,6},{8,9},{9,8},{10,11... | collective-permute-start | bytes 1376264 | tf_op jit(solution)/shard_map/sum_over_cores/ppermute | solution.py:35
  74.0 7.7 %collective-permute-start.18 = (bf16[4,16,1792]{2,1,0:T(8,128)(2,1)S(1)}, bf16[4,16,1792]{2,1,0:T(8,128)(2,1)S(1)}, u32[]{:S(2)}, u32[]{:S(2)}) collective-permute-start(bf16[4,16,1792]{2,1,0:T(8,128)(2,1)S(1)} %fusion.3), channel_id=1, source_target_pairs={{0,2},{1,3},{2,0},{3,1},{4,6},{5,7},{6,4},{7,5},{8,10},{9,11},{10,... | collective-permute-start | bytes 688136 | tf_op jit(solution)/shard_map/sum_over_x/ppermute | solution.py:35
  75.5 8.1 %collective-permute-start.15 = (bf16[16,1792]{1,0:T(8,128)(2,1)S(1)}, bf16[16,1792]{1,0:T(8,128)(2,1)S(1)}, u32[]{:S(2)}, u32[]{:S(2)}) collective-permute-start(bf16[16,1792]{1,0:T(8,128)(2,1)S(1)} %get-tuple-element.35), channel_id=1, source_target_pairs={{0,12},{4,8},{8,4},{12,0},{1,13},{5,9},{9,5},{13,1},{2,14},{6,10},... | collective-permute-start | bytes 172040 | tf_op jit(solution)/shard_map/columns_over_ctx/ppermute | solution.py:35
  77.4 8.8 %collective-permute-start.14 = (bf16[16,1792]{1,0:T(8,128)(2,1)S(1)}, bf16[16,1792]{1,0:T(8,128)(2,1)S(1)}, u32[]{:S(2)}, u32[]{:S(2)}) collective-permute-start(bf16[16,1792]{1,0:T(8,128)(2,1)S(1)} %get-tuple-element.36), channel_id=1, source_target_pairs={{0,8},{4,12},{8,0},{12,4},{1,9},{5,13},{9,1},{13,5},{2,10},{6,14},... | collective-permute-start | bytes 172040 | tf_op jit(solution)/shard_map/columns_over_ctx/ppermute | solution.py:35
  77.4 8.8 %collective-permute-start.13 = (bf16[16,1792]{1,0:T(8,128)(2,1)S(1)}, bf16[16,1792]{1,0:T(8,128)(2,1)S(1)}, u32[]{:S(2)}, u32[]{:S(2)}) collective-permute-start(bf16[16,1792]{1,0:T(8,128)(2,1)S(1)} %get-tuple-element.37), channel_id=1, source_target_pairs={{0,4},{4,0},{8,12},{12,8},{1,5},{5,1},{9,13},{13,9},{2,6},{6,2},{1... | collective-permute-start | bytes 172040 | tf_op jit(solution)/shard_map/columns_over_ctx/ppermute | solution.py:35
  81.8 6.6 %collective-permute-start.21 = (bf16[16,1792]{1,0:T(8,128)(2,1)S(1)}, bf16[16,1792]{1,0:T(8,128)(2,1)S(1)}, u32[]{:S(2)}, u32[]{:S(2)}) collective-permute-start(bf16[16,1792]{1,0:T(8,128)(2,1)S(1)} %get-tuple-element.31), channel_id=1, source_target_pairs={{0,12},{4,8},{8,4},{12,0},{1,13},{5,9},{9,5},{13,1},{2,14},{6,10},... | collective-permute-start | bytes 172040 | tf_op jit(solution)/shard_map/columns_over_ctx/ppermute | solution.py:35
  83.6 5.8 %collective-permute-start.20 = (bf16[16,1792]{1,0:T(8,128)(2,1)S(1)}, bf16[16,1792]{1,0:T(8,128)(2,1)S(1)}, u32[]{:S(2)}, u32[]{:S(2)}) collective-permute-start(bf16[16,1792]{1,0:T(8,128)(2,1)S(1)} %get-tuple-element.32), channel_id=1, source_target_pairs={{0,8},{4,12},{8,0},{12,4},{1,9},{5,13},{9,1},{13,5},{2,10},{6,14},... | collective-permute-start | bytes 172040 | tf_op jit(solution)/shard_map/columns_over_ctx/ppermute | solution.py:35
  83.6 5.8 %collective-permute-start.19 = (bf16[16,1792]{1,0:T(8,128)(2,1)S(1)}, bf16[16,1792]{1,0:T(8,128)(2,1)S(1)}, u32[]{:S(2)}, u32[]{:S(2)}) collective-permute-start(bf16[16,1792]{1,0:T(8,128)(2,1)S(1)} %get-tuple-element.33), channel_id=1, source_target_pairs={{0,4},{4,0},{8,12},{12,8},{1,5},{5,1},{9,13},{13,9},{2,6},{6,2},{1... | collective-permute-start | bytes 172040 | tf_op jit(solution)/shard_map/columns_over_ctx/ppermute | solution.py:35

commit v6 on v5

--- a/solution.py
+++ b/solution.py
@@ -14,7 +14,6 @@
 VD = 128
 HEAD = NOPE + ROPE
 PROJ = NOPE + VD
-CHUNKS = 2
 SUB_ROWS = 256
 LOAD_LIMIT = 44
 MASKED = -1e30
@@ -25,6 +24,12 @@
 IN_SMEM = pl.BlockSpec(memory_space=pltpu.SMEM)
 IN_HBM = pl.BlockSpec(memory_space=pltpu.HBM)
 ANYWHERE = pl.BlockSpec(memory_space=pl.ANY)
+
+
+def chunk_rows(owned):
+    if owned % 32 == 0:
+        return (owned // 2, owned // 4, owned // 4)
+    return (owned // 2, owned // 2)
 
 
 def params(mebibytes):
@@ -69,9 +74,9 @@
     return [pieces[offset] for offset in range(size)]
 
 
-def load_kernel(owners, piece, cache_rows, order_ref, prefix_ref, q_hbm, up_hbm, own_hbm, *refs):
-    q_exts, refs = refs[:CHUNKS], refs[CHUNKS:]
-    biases, refs = refs[:CHUNKS], refs[CHUNKS:]
+def load_kernel(owners, pieces, cache_rows, order_ref, prefix_ref, q_hbm, up_hbm, own_hbm, *refs):
+    count = len(pieces)
+    q_exts, biases, refs = refs[:count], refs[count : 2 * count], refs[2 * count :]
     value_ref, own_ref, q_ref, key_ref, sems, key_sems, value_sems = refs
     rows = q_ref.shape[0]
     head_count = key_ref.shape[0]
@@ -86,8 +91,12 @@
         value_copies.append(pltpu.make_async_copy(source, value_ref.at[head], value_sems.at[head]))
     for copy in key_copies + [own_copy] + value_copies:
         copy.start()
-    for chunk, bias_ref in enumerate(biases):
-        visible_bias(order_ref, prefix_ref, bias_ref, piece, chunk, own_hbm.shape[1], cache_rows)
+    start = 0
+    for piece, bias_ref in zip(pieces, biases):
+        visible_bias(
+            order_ref, prefix_ref, bias_ref, rows, owners, start, own_hbm.shape[1], cache_rows
+        )
+        start += piece
     q_copy.wait()
     for head in range(head_count):
         nope = q_ref[:, head * HEAD : head * HEAD + NOPE]
@@ -96,30 +105,33 @@
         absorbed = lax.dot_general(
             nope, key_ref[head], (((1,), (1,)), ((), ())), preferred_element_type=jnp.float32
         )
-        absorbed = (absorbed * SCALE).reshape(owners, CHUNKS, piece, LAT)
-        rope = rope.reshape(owners, CHUNKS, piece, ROPE)
-        for chunk, q_ext in enumerate(q_exts):
-            part = absorbed[:, chunk].reshape(rows // CHUNKS, LAT)
+        absorbed = (absorbed * SCALE).reshape(owners, rows // owners, LAT)
+        rope = rope.reshape(owners, rows // owners, ROPE)
+        start = 0
+        for piece, q_ext in zip(pieces, q_exts):
+            part = absorbed[:, start : start + piece].reshape(owners * piece, LAT)
             q_ext[head, :, :LAT] = part.astype(jnp.bfloat16)
-            part = rope[:, chunk].reshape(rows // CHUNKS, ROPE)
+            part = rope[:, start : start + piece].reshape(owners * piece, ROPE)
             q_ext[head, :, LAT:] = part.astype(jnp.bfloat16)
+            start += piece
     for copy in [own_copy] + value_copies:
         copy.wait()
 
 
-def load(queries, w_kv_up, own_keys, stretch_order, prefix_len, owners, cache_rows):
-    rows = queries.shape[0]
-    part = rows // CHUNKS
+def load(queries, w_kv_up, own_keys, stretch_order, prefix_len, owners, pieces, cache_rows):
     head_count = w_kv_up.shape[1] // PROJ
-    n_ctx = stretch_order.shape[0]
-    out_shape = [jax.ShapeDtypeStruct((head_count, part, LAT + ROPE), jnp.bfloat16)] * CHUNKS
-    out_shape += [jax.ShapeDtypeStruct((part, n_ctx * own_keys.shape[1]), jnp.float32)] * CHUNKS
+    amount = stretch_order.shape[0] * own_keys.shape[1]
+    out_shape = [
+        jax.ShapeDtypeStruct((head_count, owners * piece, LAT + ROPE), jnp.bfloat16)
+        for piece in pieces
+    ]
+    out_shape += [jax.ShapeDtypeStruct((owners * piece, amount), jnp.float32) for piece in pieces]
     out_shape += [
         jax.ShapeDtypeStruct((head_count, LAT, VD), jnp.bfloat16),
         jax.ShapeDtypeStruct(own_keys.shape, jnp.bfloat16),
     ]
     out = pl.pallas_call(
-        functools.partial(load_kernel, owners, part // owners, cache_rows),
+        functools.partial(load_kernel, owners, pieces, cache_rows),
         out_shape=out_shape,
         in_specs=[IN_SMEM, IN_SMEM] + [IN_HBM] * 3,
         out_specs=[IN_VMEM] * len(out_shape),
@@ -133,14 +145,15 @@
         compiler_params=params(LOAD_LIMIT),
         cost_estimate=SHORT,
     )(stretch_order, prefix_len, queries, w_kv_up, own_keys)
-    return out[:CHUNKS], out[CHUNKS : 2 * CHUNKS], *out[2 * CHUNKS :]
-
-
-def visible_bias(order_ref, prefix_ref, bias_ref, piece, chunk, row_span, cache_rows):
+    count = len(pieces)
+    return out[:count], out[count : 2 * count], *out[2 * count :]
+
+
+def visible_bias(order_ref, prefix_ref, bias_ref, query_rows, owners, start, row_span, cache_rows):
     n_ctx = order_ref.shape[0]
     half = row_span // 2
     rows = bias_ref.shape[0]
-    query_rows = rows * CHUNKS
+    piece = rows // owners
     own = lax.axis_index("ctx")
     core = lax.axis_index("head") % 2
     blocks = [(0, 0), (0, 1)]
@@ -148,8 +161,8 @@
     blocks += [(offset, 1 - core) for offset in range(1, n_ctx)]
     row = lax.broadcasted_iota(jnp.int32, (rows, half), 0)
     column = lax.broadcasted_iota(jnp.int32, (rows, half), 1)
-    owner = row // piece
-    query_pos = order_ref[own] * query_rows + owner * (piece * CHUNKS) + chunk * piece + row % piece
+    within_own = row // piece * (query_rows // owners) + start + row % piece
+    query_pos = order_ref[own] * query_rows + within_own
     for index, (offset, second) in enumerate(blocks):
         source = own ^ offset
         within = second * half + column
@@ -162,7 +175,7 @@
         bias_ref[:, index * half : (index + 1) * half] = bias
 
 
-def attention_kernel(count, q_ref, bias_ref, value_ref, *refs):
+def attention_kernel(count, hold, q_ref, bias_ref, value_ref, *refs):
     heads, rows, depth = q_ref.shape
     if count:
         piece_refs, (out_ref, keys_ref, latent_ref) = refs[:count], refs[count:]
@@ -173,7 +186,13 @@
             latent_ref[start : start + width, :] = piece_ref[:LAT, :].T
             start += width
     else:
-        keys_ref, latent_ref, out_ref = refs
+        keys_ref, latent_ref, *refs = refs
+        if hold:
+            mix_hbm, out_ref, mix_ref, mix_sem = refs
+            mix_copy = pltpu.make_async_copy(mix_hbm, mix_ref, mix_sem)
+            mix_copy.start()
+        else:
+            (out_ref,) = refs
     amount = keys_ref.shape[1]
     group = max(1, min(heads, SUB_ROWS // rows))
     size = group * rows
@@ -203,23 +222,27 @@
             )
             out_ref[:, head * VD : (head + 1) * VD] = result.astype(jnp.bfloat16)
         scores = later
-
-
-def attention(q_ext, bias, w_values, keys, gathered):
+    if hold:
+        mix_copy.wait()
+
+
+def attention(q_ext, bias, w_values, keys, gathered, held=()):
     head_count, rows, depth = q_ext.shape
     amount = bias.shape[1]
     out_shape = [jax.ShapeDtypeStruct((rows, head_count * VD), jnp.bfloat16)]
     if not gathered:
         out_shape.append(jax.ShapeDtypeStruct((depth, amount), jnp.bfloat16))
         out_shape.append(jax.ShapeDtypeStruct((amount, LAT), jnp.bfloat16))
+    out_shape += [jax.ShapeDtypeStruct(array.shape, array.dtype) for array in held]
     return pl.pallas_call(
-        functools.partial(attention_kernel, 0 if gathered else len(keys)),
+        functools.partial(attention_kernel, 0 if gathered else len(keys), len(held) > 0),
         out_shape=out_shape,
-        in_specs=[IN_VMEM] * (3 + len(keys)),
+        in_specs=[IN_VMEM] * (3 + len(keys)) + [IN_HBM] * len(held),
         out_specs=[IN_VMEM] * len(out_shape),
+        scratch_shapes=[pltpu.SemaphoreType.DMA] * len(held),
         compiler_params=params(16 if amount <= 1024 else 40),
         cost_estimate=SHORT,
-    )(q_ext, bias, w_values, *keys)
+    )(q_ext, bias, w_values, *keys, *held)
 
 
 def product_kernel(count, n_x, after, weight_ref, *refs):
@@ -236,15 +259,16 @@
         result = jnp.dot(rows_ref[...], weight_ref[:, span], preferred_element_type=jnp.float32)
         result = result.reshape(count, n_x, 2, rows // (2 * n_x), width)
         for x in range(n_x):
-            first, second = result[:, x, 0], result[:, x, 1]
-            sent_ref[x, :, :, span] = jnp.where(is_first, second, first).astype(jnp.bfloat16)
-            kept_ref[x, :, :, span] = jnp.where(is_first, first, second)
+            first = result[:, x, 0].reshape(rows * count // (2 * n_x), width)
+            second = result[:, x, 1].reshape(rows * count // (2 * n_x), width)
+            sent_ref[x, :, span] = jnp.where(is_first, second, first).astype(jnp.bfloat16)
+            kept_ref[x, :, span] = jnp.where(is_first, first, second)
 
 
 def product(pieces, w_out, n_x, after):
     rows, depth = pieces[0].shape
     count = len(pieces)
-    shape = (n_x, count, rows // (2 * n_x), w_out.shape[1])
+    shape = (n_x, count * rows // (2 * n_x), w_out.shape[1])
     return pl.pallas_call(
         functools.partial(product_kernel, count, n_x, len(after)),
         out_shape=[jax.ShapeDtypeStruct(shape, jnp.bfloat16), jax.ShapeDtypeStruct(shape, jnp.float32)],
@@ -258,20 +282,18 @@
 
 def place_kernel(n_ctx, ctx_ref, *refs):
     blocks, out_ref = refs[:-1], refs[-1]
-    rows = blocks[0].shape[0]
     for offset in range(n_ctx):
 
         @pl.when(pl.program_id(0) == offset)
         def _():
-            for chunk in range(CHUNKS):
-                block = blocks[chunk * n_ctx + offset][...]
-                out_ref[chunk * rows : (chunk + 1) * rows, :] = block
+            parts = [block[...].astype(jnp.float32) for block in blocks[offset::n_ctx]]
+            out_ref[...] = jnp.concatenate(parts, axis=0).astype(jnp.bfloat16)
 
 
 def place_columns(results, ctx, n_ctx):
-    rows, width = results[0][0].shape
-    total = rows * len(results)
-    if width % 128 or rows % 16:
+    width = results[0][0].shape[1]
+    total = sum(result[0].shape[0] for result in results)
+    if width % 128:
         out = jnp.zeros((total, n_ctx * width), jnp.bfloat16)
         for offset in range(n_ctx):
             block = jnp.concatenate([result[offset] for result in results], axis=0)
@@ -297,7 +319,9 @@
     row_span = kv_rows.shape[0]
     cache_rows = row_span - query_rows
     half = row_span // 2
+    columns = w_out.shape[1]
     n_x = n_head // 2
+    pieces = chunk_rows(query_rows // n_head)
     ctx = lax.axis_index("ctx")
     head = lax.axis_index("head")
     x = head // 2
@@ -308,44 +332,45 @@
         halves = [exchange(own_half, "ctx", n_ctx, offset) for offset in range(1, n_ctx)]
     with jax.named_scope("load"):
         q_ext, bias, w_values, own_keys = load(
-            queries, w_kv_up, kv_t, stretch_order, prefix_len, n_head, cache_rows
+            queries, w_kv_up, kv_t, stretch_order, prefix_len, n_head, pieces, cache_rows
         )
     with jax.named_scope("keys_over_cores"):
         halves = [tie(array, [own_keys]) for array in halves]
         others = [exchange(array, "head", n_head, 1) for array in halves]
-    keys = [own_keys] + halves + others
-    attended = []
-    for chunk in range(CHUNKS):
-        with jax.named_scope("attention"):
-            result = attention(q_ext[chunk], bias[chunk], w_values, keys, chunk > 0)
-        attended.append(result[0])
-        if chunk == 0:
-            keys = list(result[1:])
+    with jax.named_scope("attention"):
+        first, *keys = attention(q_ext[0], bias[0], w_values, [own_keys] + halves + others, False)
+        second, held = attention(q_ext[1], bias[1], w_values, keys, True, [w_out])
+        attended = [first, second]
+        for chunk in range(2, len(pieces)):
+            attended += attention(q_ext[chunk], bias[chunk], w_values, keys, True)
     with jax.named_scope("attended_over_ctx"):
         gathered = [
-            gather_pieces(own, n_ctx, attended[chunk + 1 :]) for chunk, own in enumerate(attended)
+            gather_pieces(own, n_ctx, attended[chunk + 1 : chunk + 2])
+            for chunk, own in enumerate(attended)
         ]
     results = []
     after = attended[1:]
-    for chunk in range(CHUNKS):
+    crossed = []
+    for chunk, piece in enumerate(pieces):
         with jax.named_scope("out_product"):
-            sent, kept = product(gathered[chunk], w_out, n_x, after)
+            sent, kept = product(gathered[chunk], held, n_x, after)
         with jax.named_scope("sum_over_cores"):
-            if chunk + 1 < CHUNKS:
-                received = [gathered[chunk + 1][1], gathered[chunk + 1][n_ctx // 2]]
-            sent = tie(sent, received)
+            ahead = list(crossed)
+            if chunk + 1 < len(pieces):
+                ahead += [gathered[chunk + 1][1], gathered[chunk + 1][n_ctx // 2]]
+            sent = tie(sent, ahead)
             summed = kept + exchange(sent, "head", n_head, 1).astype(jnp.float32)
             after = [summed]
         with jax.named_scope("sum_over_x"):
             total = lax.dynamic_index_in_dim(summed, x, 0, keepdims=False)
-            received = []
+            crossed = []
             for offset in range(1, n_x):
                 sent = lax.dynamic_index_in_dim(summed, x ^ offset, 0, keepdims=False)
                 sent = exchange(sent.astype(jnp.bfloat16), "head", n_head, 2 * offset)
-                received.append(sent)
+                crossed.append(sent)
                 total = total + sent.astype(jnp.float32)
         with jax.named_scope("columns_over_ctx"):
-            total = total.astype(jnp.bfloat16)
+            total = total.astype(jnp.bfloat16).reshape(n_ctx, piece, columns)
             blocks = [total[0]] + [exchange(total[d], "ctx", n_ctx, d) for d in range(1, n_ctx)]
         results.append(blocks)
     with jax.named_scope("output"):

time: 91.1 us -> 97.6 us (1.071)
  starting transfers between devices: 24.2 us -> 30.8 us
  waiting for transfers between devices: 39.7 us -> 38.5 us
  Pallas kernels: 18.9 us -> 19.9 us
    ppermute x22 -> x30, starting transfers between devices: 24.2 us -> 30.8 us  [exchange(): return lax.ppermute(array, axis, [(i, i ^ bit) for i in range(size)])]
    ppermute x22 -> x30, waiting for transfers between devices: 39.7 us -> 38.5 us  [exchange(): return lax.ppermute(array, axis, [(i, i ^ bit) for i in range(size)])]
    pallas_call x2 -> x3, Pallas kernels: 7.69 us -> 8.61 us  [attention(): pl.pallas_call(functools.partial(attention_kernel, 0 if gathered else len...]
    pallas_call x2 -> x3, Pallas kernels: 4.16 us -> 4.31 us  [product(): pl.pallas_call(functools.partial(product_kernel, count, n_x, len(after)),...]
    unnamed x12 -> x14, local copies, waits for them, and re-layouts: 5.83 us -> 5.84 us
  transfers between devices with their start and end apart: 22 -> 30, of which waited for: 12 -> 16; matrix products, arithmetic and copies ran while one was open for 0% -> 0% of each run, Pallas kernels for 15% -> 15%
where the time goes in v6:
time: 97.6 us; the launch traced here: 97.4 us
  waiting for transfers between devices  38.5 us (39%)
  starting transfers between devices  30.8 us (32%)
  Pallas kernels  19.9 us (20%)
  local copies, waits for them, and re-layouts  5.95 us (6%)
  other arithmetic  1.25 us (1%)
    ppermute x30, waiting for transfers between devices, exchange(): return lax.ppermute(array, axis, [(i, i ^ bit) for i in range(size)])  38.5 us
    ppermute x30, starting transfers between devices, exchange(): return lax.ppermute(array, axis, [(i, i ^ bit) for i in range(size)])  30.8 us
    pallas_call x3, Pallas kernels, attention(): pl.pallas_call(functools.partial(attention_kernel, 0 if gathered else len...  8.61 us
    unnamed x14, local copies, waits for them, and re-layouts  5.84 us
    pallas_call x1, Pallas kernels, load(): pl.pallas_call(functools.partial(load_kernel, owners, pieces, cache_rows)...  5.62 us
    pallas_call x3, Pallas kernels, product(): pl.pallas_call(functools.partial(product_kernel, count, n_x, len(after)),...  4.31 us
  transfers between devices with their start and end apart: 30, of which 16 were waited for; matrix products, arithmetic and copies ran while one was open for 0% of the time, Pallas kernels for 15%

profile of v6, /device:TPU:0, one launch (start us, length us, event | category | flops | bytes accessed | tf_op | source)
XLA Modules:
  0.0 97.4 jit_solution(12857554454399520259)
XLA Ops:
  0.0 1.0 %slice_select_fusion = bf16[576,128]{1,0:T(8,128)(2,1)S(1)} fusion(bf16[576,256]{1,0:T(8,128)(2,1)} %bitcast.20, pred[]{:T(512)S(6)} %eq.5), kind=kLoop, calls=%fused_computation.13 | loop fusion | flops 73728 | bytes 442369 | tf_op jit(solution)/shard_map/keys_over_ctx/jit(_where)/select_n | solution.py:331
  1.0 4.1 %collective-permute-start.1 = (bf16[576,128]{1,0:T(8,128)(2,1)S(1)}, bf16[576,128]{1,0:T(8,128)(2,1)S(1)}, u32[]{:S(2)}, u32[]{:S(2)}) collective-permute-start(bf16[576,128]{1,0:T(8,128)(2,1)S(1)} %slice_select_fusion), channel_id=1, source_target_pairs={{0,8},{4,12},{8,0},{12,4},{1,9},{5,13},{9,1},{13,5},{2,10},{6,14},... | collective-permute-start | bytes 442376 | tf_op jit(solution)/shard_map/keys_over_ctx/ppermute | solution.py:40
  5.1 1.3 %collective-permute-start.2 = (bf16[576,128]{1,0:T(8,128)(2,1)S(1)}, bf16[576,128]{1,0:T(8,128)(2,1)S(1)}, u32[]{:S(2)}, u32[]{:S(2)}) collective-permute-start(bf16[576,128]{1,0:T(8,128)(2,1)S(1)} %slice_select_fusion), channel_id=1, source_target_pairs={{0,12},{4,8},{8,4},{12,0},{1,13},{5,9},{9,5},{13,1},{2,14},{6,10},... | collective-permute-start | bytes 442376 | tf_op jit(solution)/shard_map/keys_over_ctx/ppermute | solution.py:40
  6.5 0.2 collective-permute-start
  7.3 0.0 copy-start.4
  7.3 1.0 copy-done.4
  8.3 1.1 %copy-done.5 = bf16[128,3072]{1,0:T(8,128)(2,1)S(1)} copy-done((bf16[128,3072]{1,0:T(8,128)(2,1)S(1)}, bf16[128,3072]{1,0:T(8,128)(2,1)}, u32[]{:S(2)}) %copy-start.5) | copy-done | bytes 786456
  9.4 0.7 copy-done.6
  10.1 5.6 %load.1 = (bf16[16,64,576]{2,1,0:T(8,128)(2,1)S(1)}, bf16[16,32,576]{2,1,0:T(8,128)(2,1)S(1)}, bf16[16,32,576]{2,1,0:T(8,128)(2,1)S(1)}, f32[64,1024]{1,0:T(8,12...) custom-call(s32[4]{0:T(128)S(1)} %copy-done.6, ...), custom_call_target="tpu_custom_call" | custom-call | flops 1024 | bytes 1024 | tf_op jit(solution)/shard_map/load/pallas_call | solution.py:133
  15.7 0.4 collective-permute-done.1.refs_0_
  16.1 0.0 collective-permute-start.4
  16.2 0.0 collective-permute-done.2.refs_0_
  16.2 0.5 collective-permute-start.5
  16.7 0.1 collective-permute-start.3
  16.7 0.8 collective-permute-done.4.refs_5_
  17.5 0.2 collective-permute-done.5.refs_6_
  17.7 0.3 collective-permute-done.3.refs_4_
  18.0 3.9 %attention.3 = (bf16[64,2048]{1,0:T(8,128)(2,1)S(1)}, bf16[576,1024]{1,0:T(8,128)(2,1)S(1)}, bf16[1024,512]{1,0:T(8,128)(2,1)S(1)}) custom-call(bf16[16,64,576]{2,1,0:T(8,128)(2,1)S(1)} %get-tuple-element.27.q_ref, f32[64,1024]{1,0:T(8,128)S(1)} %get-tuple-element.28.bias_ref, bf16[16,512,128]{2,1,0:T(8,128)(2,1)S(1)} %get-tuple-element.26.value_ref, ...), custom_call_target="tpu_custom_call" | custom-call | flops 1024 | bytes 1024 | tf_op jit(solution)/shard_map/attention/pallas_call | solution.py:237
  21.9 4.7 %collective-permute-start.7 = (bf16[64,2048]{1,0:T(8,128)(2,1)S(1)}, bf16[64,2048]{1,0:T(8,128)(2,1)S(1)}, u32[]{:S(2)}, u32[]{:S(2)}) collective-permute-start(bf16[64,2048]{1,0:T(8,128)(2,1)S(1)} %get-tuple-element.33.refs_0_), channel_id=1, source_target_pairs={{0,8},{4,12},{8,0},{12,4},{1,9},{5,13},{9,1},{13,5},{2,10},{6,14},... | collective-permute-start | bytes 786440 | tf_op jit(solution)/shard_map/attended_over_ctx/ppermute | solution.py:40
  26.6 0.0 collective-permute-start.6
  26.7 2.7 %attention.4 = (bf16[32,2048]{1,0:T(8,128)(2,1)S(1)}, bf16[2048,1792]{1,0:T(8,128)(2,1)S(1)}) custom-call(bf16[16,32,576]{2,1,0:T(8,128)(2,1)S(1)} %get-tuple-element.24.q_ref, f32[32,1024]{1,0:T(8,128)S(1)} %get-tuple-element.25.bias_ref, bf16[16,512,128]{2,1,0:T(8,128)(2,1)S(1)} %get-tuple-element.26.value_ref, ...), custom_call_target="tpu_custom_call" | custom-call | flops 1024 | bytes 1024 | tf_op jit(solution)/shard_map/attention/pallas_call | solution.py:237
  29.4 9.8 %collective-permute-done.7.refs_0_ = bf16[64,2048]{1,0:T(8,128)(2,1)S(1)} collective-permute-done((bf16[64,2048]{1,0:T(8,128)(2,1)S(1)}, bf16[64,2048]{1,0:T(8,128)(2,1)S(1)}, u32[]{:S(2)}, u32[]{:S(2)}) %collective-permute-start.7) | collective-permute-done | bytes 262176 | tf_op jit(solution)/shard_map/attended_over_ctx/ppermute | solution.py:40
  39.1 0.0 collective-permute-start.8
  39.1 1.8 %collective-permute-start.10 = (bf16[32,2048]{1,0:T(8,128)(2,1)S(1)}, bf16[32,2048]{1,0:T(8,128)(2,1)S(1)}, u32[]{:S(2)}, u32[]{:S(2)}) collective-permute-start(bf16[32,2048]{1,0:T(8,128)(2,1)S(1)} %get-tuple-element.34.refs_1_.refs_4_.refs_0_), channel_id=1, source_target_pairs={{0,8},{4,12},{8,0},{12,4},{1,9},{5,13},{9,1},{13,5},{2,10},{6,14},... | collective-permute-start | bytes 393224 | tf_op jit(solution)/shard_map/attended_over_ctx/ppermute | solution.py:40
  41.0 0.2 collective-permute-start.9
  41.2 2.0 %attention.5.refs_5_.refs_1_.refs_0_ = bf16[32,2048]{1,0:T(8,128)(2,1)S(1)} custom-call(bf16[16,32,576]{2,1,0:T(8,128)(2,1)S(1)} %get-tuple-element.35.q_ref, f32[32,1024]{1,0:T(8,128)S(1)} %get-tuple-element.36.bias_ref, bf16[16,512,128]{2,1,0:T(8,128)(2,1)S(1)} %get-tuple-element.26.value_ref, bf16[576,1024]{1,0:T(8,128)(2,1)S(1)} %get-tuple-element.30.refs_0_, ...), custom_call_target="tpu_custom_call" | custom-call | flops 1024 | bytes 1024 | tf_op jit(solution)/shard_map/attention/pallas_call | solution.py:237
  43.2 5.4 %collective-permute-done.10.refs_0_ = bf16[32,2048]{1,0:T(8,128)(2,1)S(1)} collective-permute-done((bf16[32,2048]{1,0:T(8,128)(2,1)S(1)}, bf16[32,2048]{1,0:T(8,128)(2,1)S(1)}, u32[]{:S(2)}, u32[]{:S(2)}) %collective-permute-start.10) | collective-permute-done | bytes 131104 | tf_op jit(solution)/shard_map/attended_over_ctx/ppermute | solution.py:40
  48.6 2.3 %collective-permute-done.8.refs_3_ = bf16[64,2048]{1,0:T(8,128)(2,1)S(1)} collective-permute-done((bf16[64,2048]{1,0:T(8,128)(2,1)S(1)}, bf16[64,2048]{1,0:T(8,128)(2,1)S(1)}, u32[]{:S(2)}, u32[]{:S(2)}) %collective-permute-start.8) | collective-permute-done | bytes 262176 | tf_op jit(solution)/shard_map/attended_over_ctx/ppermute | solution.py:40
  51.0 2.1 %out_product.3 = (bf16[2,64,1792]{2,1,0:T(8,128)(2,1)S(1)}, f32[2,64,1792]{2,1,0:T(8,128)S(1)}) custom-call(bf16[2048,1792]{1,0:T(8,128)(2,1)S(1)} %get-tuple-element.32.weight_ref, bf16[64,2048]{1,0:T(8,128)(2,1)S(1)} %get-tuple-element.33.refs_0_, bf16[64,2048]{1,0:T(8,128)(2,1)S(1)} %collective-permute-done.6.refs_1_, ...), custom_call_target="tpu_custom_call" | custom-call | flops 1024 | bytes 1024 | tf_op jit(solution)/shard_map/out_product/pallas_call | solution.py:272
  53.1 0.0 collective-permute-done.9.refs_1_
  53.1 0.1 collective-permute-start.11
  53.2 1.8 %collective-permute-done.11 = bf16[2,64,1792]{2,1,0:T(8,128)(2,1)S(1)} collective-permute-done((bf16[2,64,1792]{2,1,0:T(8,128)(2,1)S(1)}, bf16[2,64,1792]{2,1,0:T(8,128)(2,1)S(1)}, u32[]{:S(2)}, u32[]{:S(2)}) %collective-permute-start.11) | collective-permute-done | bytes 458784 | tf_op jit(solution)/shard_map/sum_over_cores/ppermute | solution.py:40
  55.0 0.1 convert_add_fusion.refs_4_
  55.1 1.6 %collective-permute-start.12 = (bf16[64,1792]{1,0:T(8,128)(2,1)S(1)}, bf16[64,1792]{1,0:T(8,128)(2,1)S(1)}, u32[]{:S(2)}, u32[]{:S(2)}) collective-permute-start(bf16[64,1792]{1,0:T(8,128)(2,1)S(1)} %fusion.1), channel_id=1, source_target_pairs={{0,2},{1,3},{2,0},{3,1},{4,6},{5,7},{6,4},{7,5},{8,10},{9,11},{10,... | collective-permute-start | bytes 688136 | tf_op jit(solution)/shard_map/sum_over_x/ppermute | solution.py:40
  56.6 1.0 %collective-permute-start.18 = (bf16[32,2048]{1,0:T(8,128)(2,1)S(1)}, bf16[32,2048]{1,0:T(8,128)(2,1)S(1)}, u32[]{:S(2)}, u32[]{:S(2)}) collective-permute-start(bf16[32,2048]{1,0:T(8,128)(2,1)S(1)} %attention.5.refs_5_.refs_1_.refs_0_), channel_id=1, source_target_pairs={{0,8},{4,12},{8,0},{12,4},{1,9},{5,13},{9,1},{13,5},{2,10},{6,14},... | collective-permute-start | bytes 393224 | tf_op jit(solution)/shard_map/attended_over_ctx/ppermute | solution.py:40
  57.7 0.7 collective-permute-start.16
  58.4 1.3 %collective-permute-start.17 = (bf16[32,2048]{1,0:T(8,128)(2,1)S(1)}, bf16[32,2048]{1,0:T(8,128)(2,1)S(1)}, u32[]{:S(2)}, u32[]{:S(2)}) collective-permute-start(bf16[32,2048]{1,0:T(8,128)(2,1)S(1)} %attention.5.refs_5_.refs_1_.refs_0_), channel_id=1, source_target_pairs={{0,4},{4,0},{8,12},{12,8},{1,5},{5,1},{9,13},{13,9},{2,6},{6,2},{1... | collective-permute-start | bytes 393224 | tf_op jit(solution)/shard_map/attended_over_ctx/ppermute | solution.py:40
  59.7 5.4 %collective-permute-done.18.refs_3_.refs_2_ = bf16[32,2048]{1,0:T(8,128)(2,1)S(1)} collective-permute-done((bf16[32,2048]{1,0:T(8,128)(2,1)S(1)}, bf16[32,2048]{1,0:T(8,128)(2,1)S(1)}, u32[]{:S(2)}, u32[]{:S(2)}) %collective-permute-start.18) | collective-permute-done | bytes 131104 | tf_op jit(solution)/shard_map/attended_over_ctx/ppermute | solution.py:40
  65.2 0.0 collective-permute-start.24
  65.2 1.7 %collective-permute-done.16.refs_3_ = bf16[32,2048]{1,0:T(8,128)(2,1)S(1)} collective-permute-done((bf16[32,2048]{1,0:T(8,128)(2,1)S(1)}, bf16[32,2048]{1,0:T(8,128)(2,1)S(1)}, u32[]{:S(2)}, u32[]{:S(2)}) %collective-permute-start.16) | collective-permute-done | bytes 131104 | tf_op jit(solution)/shard_map/attended_over_ctx/ppermute | solution.py:40
  66.8 3.1 %copy-done.1 = bf16[2048,1792]{1,0:T(8,128)(2,1)S(1)} copy-done((bf16[2048,1792]{1,0:T(8,128)(2,1)S(1)}, bf16[2048,1792]{1,0:T(8,128)(2,1)}, u32[]{:S(2)}) %copy-start.1) | copy-done | bytes 7340056
  69.9 1.1 %out_product.4 = (bf16[2,32,1792]{2,1,0:T(8,128)(2,1)S(1)}, f32[2,32,1792]{2,1,0:T(8,128)S(1)}) custom-call(bf16[2048,1792]{1,0:T(8,128)(2,1)S(1)} %copy-done.1, bf16[32,2048]{1,0:T(8,128)(2,1)S(1)} %get-tuple-element.34.refs_1_.refs_4_.refs_0_, bf16[32,2048]{1,0:T(8,128)(2,1)S(1)} %collective-permute-done.9.refs_1_, ...), custom_call_target="tpu_custom_call" | custom-call | flops 1024 | bytes 1024 | tf_op jit(solution)/shard_map/out_product/pallas_call | solution.py:272
  71.0 0.0 collective-permute-done.17.refs_2_.refs_1_
  71.1 0.1 collective-permute-start.19
  71.2 1.4 %collective-permute-done.19 = bf16[2,32,1792]{2,1,0:T(8,128)(2,1)S(1)} collective-permute-done((bf16[2,32,1792]{2,1,0:T(8,128)(2,1)S(1)}, bf16[2,32,1792]{2,1,0:T(8,128)(2,1)S(1)}, u32[]{:S(2)}, u32[]{:S(2)}) %collective-permute-start.19) | collective-permute-done | bytes 229408 | tf_op jit(solution)/shard_map/sum_over_cores/ppermute | solution.py:40
  72.7 0.6 collective-permute-start.20
  73.3 0.4 collective-permute-start.13
  73.7 0.7 collective-permute-start.14
  74.4 3.4 %collective-permute-start.15 = (bf16[16,1792]{1,0:T(8,128)(2,1)S(1)}, bf16[16,1792]{1,0:T(8,128)(2,1)S(1)}, u32[]{:S(2)}, u32[]{:S(2)}) collective-permute-start(bf16[16,1792]{1,0:T(8,128)(2,1)S(1)} %get-tuple-element.43), channel_id=1, source_target_pairs={{0,12},{4,8},{8,4},{12,0},{1,13},{5,9},{9,5},{13,1},{2,14},{6,10},... | collective-permute-start | bytes 172040 | tf_op jit(solution)/shard_map/columns_over_ctx/ppermute | solution.py:40
  77.8 1.1 %out_product.5 = (bf16[2,32,1792]{2,1,0:T(8,128)(2,1)S(1)}, f32[2,32,1792]{2,1,0:T(8,128)S(1)}) custom-call(bf16[2048,1792]{1,0:T(8,128)(2,1)S(1)} %copy-done.2, bf16[32,2048]{1,0:T(8,128)(2,1)S(1)} %attention.5.refs_5_.refs_1_.refs_0_, bf16[32,2048]{1,0:T(8,128)(2,1)S(1)} %collective-permute-done.17.refs_2_.refs_1_, ...), custom_call_target="tpu_custom_call" | custom-call | flops 1024 | bytes 1024 | tf_op jit(solution)/shard_map/out_product/pallas_call | solution.py:272
  78.9 0.1 collective-permute-start.25
  79.0 1.4 %collective-permute-done.25 = bf16[2,32,1792]{2,1,0:T(8,128)(2,1)S(1)} collective-permute-done((bf16[2,32,1792]{2,1,0:T(8,128)(2,1)S(1)}, bf16[2,32,1792]{2,1,0:T(8,128)(2,1)S(1)}, u32[]{:S(2)}, u32[]{:S(2)}) %collective-permute-start.25) | collective-permute-done | bytes 229408 | tf_op jit(solution)/shard_map/sum_over_cores/ppermute | solution.py:40
  80.6 1.6 %collective-permute-start.26 = (bf16[32,1792]{1,0:T(8,128)(2,1)S(1)}, bf16[32,1792]{1,0:T(8,128)(2,1)S(1)}, u32[]{:S(2)}, u32[]{:S(2)}) collective-permute-start(bf16[32,1792]{1,0:T(8,128)(2,1)S(1)} %fusion.5), channel_id=1, source_target_pairs={{0,2},{1,3},{2,0},{3,1},{4,6},{5,7},{6,4},{7,5},{8,10},{9,11},{10,... | collective-permute-start | bytes 344072 | tf_op jit(solution)/shard_map/sum_over_x/ppermute | solution.py:40
  82.1 0.1 collective-permute-start.21
  82.2 3.6 %collective-permute-done.26 = bf16[32,1792]{1,0:T(8,128)(2,1)S(1)} collective-permute-done((bf16[32,1792]{1,0:T(8,128)(2,1)S(1)}, bf16[32,1792]{1,0:T(8,128)(2,1)S(1)}, u32[]{:S(2)}, u32[]{:S(2)}) %collective-permute-start.26) | collective-permute-done | bytes 114720 | tf_op jit(solution)/shard_map/sum_over_x/ppermute | solution.py:40
  85.9 1.9 %collective-permute-start.23 = (bf16[8,1792]{1,0:T(8,128)(2,1)S(1)}, bf16[8,1792]{1,0:T(8,128)(2,1)S(1)}, u32[]{:S(2)}, u32[]{:S(2)}) collective-permute-start(bf16[8,1792]{1,0:T(8,128)(2,1)S(1)} %get-tuple-element.51), channel_id=1, source_target_pairs={{0,12},{4,8},{8,4},{12,0},{1,13},{5,9},{9,5},{13,1},{2,14},{6,10},... | collective-permute-start | bytes 86024 | tf_op jit(solution)/shard_map/columns_over_ctx/ppermute | solution.py:40
  87.7 1.7 %collective-permute-start.27 = (bf16[8,1792]{1,0:T(8,128)(2,1)S(1)}, bf16[8,1792]{1,0:T(8,128)(2,1)S(1)}, u32[]{:S(2)}, u32[]{:S(2)}) collective-permute-start(bf16[8,1792]{1,0:T(8,128)(2,1)S(1)} %get-tuple-element.49), channel_id=1, source_target_pairs={{0,4},{4,0},{8,12},{12,8},{1,5},{5,1},{9,13},{13,9},{2,6},{6,2},{1... | collective-permute-start | bytes 86024 | tf_op jit(solution)/shard_map/columns_over_ctx/ppermute | solution.py:40
  89.4 0.0 collective-permute-done.15.refs_3_
  89.4 0.9 collective-permute-start.28
  90.3 1.8 %collective-permute-start.29 = (bf16[8,1792]{1,0:T(8,128)(2,1)S(1)}, bf16[8,1792]{1,0:T(8,128)(2,1)S(1)}, u32[]{:S(2)}, u32[]{:S(2)}) collective-permute-start(bf16[8,1792]{1,0:T(8,128)(2,1)S(1)} %get-tuple-element.47), channel_id=1, source_target_pairs={{0,12},{4,8},{8,4},{12,0},{1,13},{5,9},{9,5},{13,1},{2,14},{6,10},... | collective-permute-start | bytes 86024 | tf_op jit(solution)/shard_map/columns_over_ctx/ppermute | solution.py:40
  92.1 0.1 collective-permute-done.27.refs_9_
  92.2 2.1 %collective-permute-done.28.refs_10_ = bf16[8,1792]{1,0:T(8,128)(2,1)S(1)} collective-permute-done((bf16[8,1792]{1,0:T(8,128)(2,1)S(1)}, bf16[8,1792]{1,0:T(8,128)(2,1)S(1)}, u32[]{:S(2)}, u32[]{:S(2)}) %collective-permute-start.28) | collective-permute-done | bytes 28704 | tf_op jit(solution)/shard_map/columns_over_ctx/ppermute | solution.py:40
  94.3 1.7 %collective-permute-done.29.refs_11_ = bf16[8,1792]{1,0:T(8,128)(2,1)S(1)} collective-permute-done((bf16[8,1792]{1,0:T(8,128)(2,1)S(1)}, bf16[8,1792]{1,0:T(8,128)(2,1)S(1)}, u32[]{:S(2)}, u32[]{:S(2)}) %collective-permute-start.29) | collective-permute-done | bytes 28704 | tf_op jit(solution)/shard_map/columns_over_ctx/ppermute | solution.py:40
  96.0 1.4 %output.1 = bf16[32,7168]{1,0:T(8,128)(2,1)} custom-call(s32[1]{0:T(128)} %bitcast.ctx_ref, bf16[16,1792]{1,0:T(8,128)(2,1)S(1)} %get-tuple-element.46.refs_0_, bf16[16,1792]{1,0:T(8,128)(2,1)S(1)} %collective-permute-done.13.refs_1_, bf16[16,1792]{1,0:T(8,128)(2,1)S(1)} %collective-permute-done.14.refs_2_, ...), custom_call_target="tpu_custom_call" | custom-call | flops 1024 | bytes 1024 | tf_op jit(solution)/shard_map/output/pallas_call | solution.py:303
  (39 shorter events, 0.3 us)
Async XLA Ops:
  1.0 15.1 %collective-permute-start.1 = (bf16[576,128]{1,0:T(8,128)(2,1)S(1)}, bf16[576,128]{1,0:T(8,128)(2,1)S(1)}, u32[]{:S(2)}, u32[]{:S(2)}) collective-permute-start(bf16[576,128]{1,0:T(8,128)(2,1)S(1)} %slice_select_fusion), channel_id=1, source_target_pairs={{0,8},{4,12},{8,0},{12,4},{1,9},{5,13},{9,1},{13,5},{2,10},{6,14},... | collective-permute-start | bytes 442376 | tf_op jit(solution)/shard_map/keys_over_ctx/ppermute | solution.py:40
  5.1 11.0 %collective-permute-start.2 = (bf16[576,128]{1,0:T(8,128)(2,1)S(1)}, bf16[576,128]{1,0:T(8,128)(2,1)S(1)}, u32[]{:S(2)}, u32[]{:S(2)}) collective-permute-start(bf16[576,128]{1,0:T(8,128)(2,1)S(1)} %slice_select_fusion), channel_id=1, source_target_pairs={{0,12},{4,8},{8,4},{12,0},{1,13},{5,9},{9,5},{13,1},{2,14},{6,10},... | collective-permute-start | bytes 442376 | tf_op jit(solution)/shard_map/keys_over_ctx/ppermute | solution.py:40
  6.5 10.2 %collective-permute-start = (bf16[576,128]{1,0:T(8,128)(2,1)S(1)}, bf16[576,128]{1,0:T(8,128)(2,1)S(1)}, u32[]{:S(2)}, u32[]{:S(2)}) collective-permute-start(bf16[576,128]{1,0:T(8,128)(2,1)S(1)} %slice_select_fusion), channel_id=1, source_target_pairs={{0,4},{4,0},{8,12},{12,8},{1,5},{5,1},{9,13},{13,9},{2,6},{6,2},{1... | collective-permute-start | bytes 442376 | tf_op jit(solution)/shard_map/keys_over_ctx/ppermute | solution.py:40
  7.3 1.0 copy-start.4
  8.3 1.1 %copy-start.5 = (bf16[128,3072]{1,0:T(8,128)(2,1)S(1)}, bf16[128,3072]{1,0:T(8,128)(2,1)}, u32[]{:S(2)}) copy-start(bf16[128,3072]{1,0:T(8,128)(2,1)} %q_hbm.1) | copy-start | bytes 2359300
  9.4 0.7 copy-start.6
  10.1 16.6 %copy-start.3 = (bf16[2048,1792]{1,0:T(8,128)(2,1)S(1)}, bf16[2048,1792]{1,0:T(8,128)(2,1)}, u32[]{:S(2)}) copy-start(bf16[2048,1792]{1,0:T(8,128)(2,1)} %refs_2_.1) | copy-start | bytes 22020100
  16.1 1.4 %collective-permute-start.4 = (bf16[576,128]{1,0:T(8,128)(2,1)S(1)}, bf16[576,128]{1,0:T(8,128)(2,1)S(1)}, u32[]{:S(2)}, u32[]{:S(2)}) collective-permute-start(bf16[576,128]{1,0:T(8,128)(2,1)S(1)} %keys_over_cores.4.refs_2_), channel_id=1, source_target_pairs={{0,1},{1,0},{2,3},{3,2},{4,5},{5,4},{6,7},{7,6},{8,9},{9,8},{10,11... | collective-permute-start | bytes 442376 | tf_op jit(solution)/shard_map/keys_over_cores/ppermute | solution.py:40
  16.2 1.6 %collective-permute-start.5 = (bf16[576,128]{1,0:T(8,128)(2,1)S(1)}, bf16[576,128]{1,0:T(8,128)(2,1)S(1)}, u32[]{:S(2)}, u32[]{:S(2)}) collective-permute-start(bf16[576,128]{1,0:T(8,128)(2,1)S(1)} %keys_over_cores.5.refs_3_), channel_id=1, source_target_pairs={{0,1},{1,0},{2,3},{3,2},{4,5},{5,4},{6,7},{7,6},{8,9},{9,8},{10,11... | collective-permute-start | bytes 442376 | tf_op jit(solution)/shard_map/keys_over_cores/ppermute | solution.py:40
  16.7 1.4 %collective-permute-start.3 = (bf16[576,128]{1,0:T(8,128)(2,1)S(1)}, bf16[576,128]{1,0:T(8,128)(2,1)S(1)}, u32[]{:S(2)}, u32[]{:S(2)}) collective-permute-start(bf16[576,128]{1,0:T(8,128)(2,1)S(1)} %keys_over_cores.3.refs_1_), channel_id=1, source_target_pairs={{0,1},{1,0},{2,3},{3,2},{4,5},{5,4},{6,7},{7,6},{8,9},{9,8},{10,11... | collective-permute-start | bytes 442376 | tf_op jit(solution)/shard_map/keys_over_cores/ppermute | solution.py:40
  21.9 17.2 %collective-permute-start.7 = (bf16[64,2048]{1,0:T(8,128)(2,1)S(1)}, bf16[64,2048]{1,0:T(8,128)(2,1)S(1)}, u32[]{:S(2)}, u32[]{:S(2)}) collective-permute-start(bf16[64,2048]{1,0:T(8,128)(2,1)S(1)} %get-tuple-element.33.refs_0_), channel_id=1, source_target_pairs={{0,8},{4,12},{8,0},{12,4},{1,9},{5,13},{9,1},{13,5},{2,10},{6,14},... | collective-permute-start | bytes 786440 | tf_op jit(solution)/shard_map/attended_over_ctx/ppermute | solution.py:40
  26.6 22.0 %collective-permute-start.6 = (bf16[64,2048]{1,0:T(8,128)(2,1)S(1)}, bf16[64,2048]{1,0:T(8,128)(2,1)S(1)}, u32[]{:S(2)}, u32[]{:S(2)}) collective-permute-start(bf16[64,2048]{1,0:T(8,128)(2,1)S(1)} %get-tuple-element.33.refs_0_), channel_id=1, source_target_pairs={{0,4},{4,0},{8,12},{12,8},{1,5},{5,1},{9,13},{13,9},{2,6},{6,2},{1... | collective-permute-start | bytes 786440 | tf_op jit(solution)/shard_map/attended_over_ctx/ppermute | solution.py:40
  29.4 23.7 %copy-start = (bf16[2048,1792]{1,0:T(8,128)(2,1)}, bf16[2048,1792]{1,0:T(8,128)(2,1)S(1)}, u32[]{:S(2)}) copy-start(bf16[2048,1792]{1,0:T(8,128)(2,1)S(1)} %get-tuple-element.32.weight_ref) | copy-start | bytes 22020100
  39.1 11.8 %collective-permute-start.8 = (bf16[64,2048]{1,0:T(8,128)(2,1)S(1)}, bf16[64,2048]{1,0:T(8,128)(2,1)S(1)}, u32[]{:S(2)}, u32[]{:S(2)}) collective-permute-start(bf16[64,2048]{1,0:T(8,128)(2,1)S(1)} %attended_over_ctx.2.refs_2_), channel_id=1, source_target_pairs={{0,4},{4,0},{8,12},{12,8},{1,5},{5,1},{9,13},{13,9},{2,6},{6,2},{1... | collective-permute-start | bytes 786440 | tf_op jit(solution)/shard_map/attended_over_ctx/ppermute | solution.py:40
  39.1 9.5 %collective-permute-start.10 = (bf16[32,2048]{1,0:T(8,128)(2,1)S(1)}, bf16[32,2048]{1,0:T(8,128)(2,1)S(1)}, u32[]{:S(2)}, u32[]{:S(2)}) collective-permute-start(bf16[32,2048]{1,0:T(8,128)(2,1)S(1)} %get-tuple-element.34.refs_1_.refs_4_.refs_0_), channel_id=1, source_target_pairs={{0,8},{4,12},{8,0},{12,4},{1,9},{5,13},{9,1},{13,5},{2,10},{6,14},... | collective-permute-start | bytes 393224 | tf_op jit(solution)/shard_map/attended_over_ctx/ppermute | solution.py:40
  41.0 12.1 %collective-permute-start.9 = (bf16[32,2048]{1,0:T(8,128)(2,1)S(1)}, bf16[32,2048]{1,0:T(8,128)(2,1)S(1)}, u32[]{:S(2)}, u32[]{:S(2)}) collective-permute-start(bf16[32,2048]{1,0:T(8,128)(2,1)S(1)} %get-tuple-element.34.refs_1_.refs_4_.refs_0_), channel_id=1, source_target_pairs={{0,4},{4,0},{8,12},{12,8},{1,5},{5,1},{9,13},{13,9},{2,6},{6,2},{1... | collective-permute-start | bytes 393224 | tf_op jit(solution)/shard_map/attended_over_ctx/ppermute | solution.py:40
  53.1 1.9 %collective-permute-start.11 = (bf16[2,64,1792]{2,1,0:T(8,128)(2,1)S(1)}, bf16[2,64,1792]{2,1,0:T(8,128)(2,1)S(1)}, u32[]{:S(2)}, u32[]{:S(2)}) collective-permute-start(bf16[2,64,1792]{2,1,0:T(8,128)(2,1)S(1)} %sum_over_cores.3), channel_id=1, source_target_pairs={{0,1},{1,0},{2,3},{3,2},{4,5},{5,4},{6,7},{7,6},{8,9},{9,8},{10,11... | collective-permute-start | bytes 1376264 | tf_op jit(solution)/shard_map/sum_over_cores/ppermute | solution.py:40
  55.1 16.0 %collective-permute-start.12 = (bf16[64,1792]{1,0:T(8,128)(2,1)S(1)}, bf16[64,1792]{1,0:T(8,128)(2,1)S(1)}, u32[]{:S(2)}, u32[]{:S(2)}) collective-permute-start(bf16[64,1792]{1,0:T(8,128)(2,1)S(1)} %fusion.1), channel_id=1, source_target_pairs={{0,2},{1,3},{2,0},{3,1},{4,6},{5,7},{6,4},{7,5},{8,10},{9,11},{10,... | collective-permute-start | bytes 688136 | tf_op jit(solution)/shard_map/sum_over_x/ppermute | solution.py:40
  56.6 8.5 %collective-permute-start.18 = (bf16[32,2048]{1,0:T(8,128)(2,1)S(1)}, bf16[32,2048]{1,0:T(8,128)(2,1)S(1)}, u32[]{:S(2)}, u32[]{:S(2)}) collective-permute-start(bf16[32,2048]{1,0:T(8,128)(2,1)S(1)} %attention.5.refs_5_.refs_1_.refs_0_), channel_id=1, source_target_pairs={{0,8},{4,12},{8,0},{12,4},{1,9},{5,13},{9,1},{13,5},{2,10},{6,14},... | collective-permute-start | bytes 393224 | tf_op jit(solution)/shard_map/attended_over_ctx/ppermute | solution.py:40
  57.7 9.1 %collective-permute-start.16 = (bf16[32,2048]{1,0:T(8,128)(2,1)S(1)}, bf16[32,2048]{1,0:T(8,128)(2,1)S(1)}, u32[]{:S(2)}, u32[]{:S(2)}) collective-permute-start(bf16[32,2048]{1,0:T(8,128)(2,1)S(1)} %attended_over_ctx.3.refs_2_), channel_id=1, source_target_pairs={{0,4},{4,0},{8,12},{12,8},{1,5},{5,1},{9,13},{13,9},{2,6},{6,2},{1... | collective-permute-start | bytes 393224 | tf_op jit(solution)/shard_map/attended_over_ctx/ppermute | solution.py:40
  58.4 12.7 %collective-permute-start.17 = (bf16[32,2048]{1,0:T(8,128)(2,1)S(1)}, bf16[32,2048]{1,0:T(8,128)(2,1)S(1)}, u32[]{:S(2)}, u32[]{:S(2)}) collective-permute-start(bf16[32,2048]{1,0:T(8,128)(2,1)S(1)} %attention.5.refs_5_.refs_1_.refs_0_), channel_id=1, source_target_pairs={{0,4},{4,0},{8,12},{12,8},{1,5},{5,1},{9,13},{13,9},{2,6},{6,2},{1... | collective-permute-start | bytes 393224 | tf_op jit(solution)/shard_map/attended_over_ctx/ppermute | solution.py:40
  65.2 12.6 %collective-permute-start.24 = (bf16[32,2048]{1,0:T(8,128)(2,1)S(1)}, bf16[32,2048]{1,0:T(8,128)(2,1)S(1)}, u32[]{:S(2)}, u32[]{:S(2)}) collective-permute-start(bf16[32,2048]{1,0:T(8,128)(2,1)S(1)} %collective-permute-done.18.refs_3_.refs_2_), channel_id=1, source_target_pairs={{0,4},{4,0},{8,12},{12,8},{1,5},{5,1},{9,13},{13,9},{2,6},{6,2},{1... | collective-permute-start | bytes 393224 | tf_op jit(solution)/shard_map/attended_over_ctx/ppermute | solution.py:40
  66.8 3.1 %copy-start.1 = (bf16[2048,1792]{1,0:T(8,128)(2,1)S(1)}, bf16[2048,1792]{1,0:T(8,128)(2,1)}, u32[]{:S(2)}) copy-start(bf16[2048,1792]{1,0:T(8,128)(2,1)} %copy-done) | copy-start | bytes 22020100
  69.9 7.9 %copy-start.2 = (bf16[2048,1792]{1,0:T(8,128)(2,1)S(1)}, bf16[2048,1792]{1,0:T(8,128)(2,1)}, u32[]{:S(2)}) copy-start(bf16[2048,1792]{1,0:T(8,128)(2,1)} %copy-done) | copy-start | bytes 22020100
  71.1 1.6 %collective-permute-start.19 = (bf16[2,32,1792]{2,1,0:T(8,128)(2,1)S(1)}, bf16[2,32,1792]{2,1,0:T(8,128)(2,1)S(1)}, u32[]{:S(2)}, u32[]{:S(2)}) collective-permute-start(bf16[2,32,1792]{2,1,0:T(8,128)(2,1)S(1)} %sum_over_cores.4), channel_id=1, source_target_pairs={{0,1},{1,0},{2,3},{3,2},{4,5},{5,4},{6,7},{7,6},{8,9},{9,8},{10,11... | collective-permute-start | bytes 688136 | tf_op jit(solution)/shard_map/sum_over_cores/ppermute | solution.py:40
  72.7 6.2 %collective-permute-start.20 = (bf16[32,1792]{1,0:T(8,128)(2,1)S(1)}, bf16[32,1792]{1,0:T(8,128)(2,1)S(1)}, u32[]{:S(2)}, u32[]{:S(2)}) collective-permute-start(bf16[32,1792]{1,0:T(8,128)(2,1)S(1)} %fusion.4), channel_id=1, source_target_pairs={{0,2},{1,3},{2,0},{3,1},{4,6},{5,7},{6,4},{7,5},{8,10},{9,11},{10,... | collective-permute-start | bytes 344072 | tf_op jit(solution)/shard_map/sum_over_x/ppermute | solution.py:40
  73.3 12.5 %collective-permute-start.13 = (bf16[16,1792]{1,0:T(8,128)(2,1)S(1)}, bf16[16,1792]{1,0:T(8,128)(2,1)S(1)}, u32[]{:S(2)}, u32[]{:S(2)}) collective-permute-start(bf16[16,1792]{1,0:T(8,128)(2,1)S(1)} %get-tuple-element.45), channel_id=1, source_target_pairs={{0,4},{4,0},{8,12},{12,8},{1,5},{5,1},{9,13},{13,9},{2,6},{6,2},{1... | collective-permute-start | bytes 172040 | tf_op jit(solution)/shard_map/columns_over_ctx/ppermute | solution.py:40
  73.7 14.0 %collective-permute-start.14 = (bf16[16,1792]{1,0:T(8,128)(2,1)S(1)}, bf16[16,1792]{1,0:T(8,128)(2,1)S(1)}, u32[]{:S(2)}, u32[]{:S(2)}) collective-permute-start(bf16[16,1792]{1,0:T(8,128)(2,1)S(1)} %get-tuple-element.44), channel_id=1, source_target_pairs={{0,8},{4,12},{8,0},{12,4},{1,9},{5,13},{9,1},{13,5},{2,10},{6,14},... | collective-permute-start | bytes 172040 | tf_op jit(solution)/shard_map/columns_over_ctx/ppermute | solution.py:40
  74.4 15.0 %collective-permute-start.15 = (bf16[16,1792]{1,0:T(8,128)(2,1)S(1)}, bf16[16,1792]{1,0:T(8,128)(2,1)S(1)}, u32[]{:S(2)}, u32[]{:S(2)}) collective-permute-start(bf16[16,1792]{1,0:T(8,128)(2,1)S(1)} %get-tuple-element.43), channel_id=1, source_target_pairs={{0,12},{4,8},{8,4},{12,0},{1,13},{5,9},{9,5},{13,1},{2,14},{6,10},... | collective-permute-start | bytes 172040 | tf_op jit(solution)/shard_map/columns_over_ctx/ppermute | solution.py:40
  78.9 1.6 %collective-permute-start.25 = (bf16[2,32,1792]{2,1,0:T(8,128)(2,1)S(1)}, bf16[2,32,1792]{2,1,0:T(8,128)(2,1)S(1)}, u32[]{:S(2)}, u32[]{:S(2)}) collective-permute-start(bf16[2,32,1792]{2,1,0:T(8,128)(2,1)S(1)} %sum_over_cores.5), channel_id=1, source_target_pairs={{0,1},{1,0},{2,3},{3,2},{4,5},{5,4},{6,7},{7,6},{8,9},{9,8},{10,11... | collective-permute-start | bytes 688136 | tf_op jit(solution)/shard_map/sum_over_cores/ppermute | solution.py:40
  80.6 5.3 %collective-permute-start.26 = (bf16[32,1792]{1,0:T(8,128)(2,1)S(1)}, bf16[32,1792]{1,0:T(8,128)(2,1)S(1)}, u32[]{:S(2)}, u32[]{:S(2)}) collective-permute-start(bf16[32,1792]{1,0:T(8,128)(2,1)S(1)} %fusion.5), channel_id=1, source_target_pairs={{0,2},{1,3},{2,0},{3,1},{4,6},{5,7},{6,4},{7,5},{8,10},{9,11},{10,... | collective-permute-start | bytes 344072 | tf_op jit(solution)/shard_map/sum_over_x/ppermute | solution.py:40
  82.1 8.2 %collective-permute-start.21 = (bf16[8,1792]{1,0:T(8,128)(2,1)S(1)}, bf16[8,1792]{1,0:T(8,128)(2,1)S(1)}, u32[]{:S(2)}, u32[]{:S(2)}) collective-permute-start(bf16[8,1792]{1,0:T(8,128)(2,1)S(1)} %get-tuple-element.53), channel_id=1, source_target_pairs={{0,4},{4,0},{8,12},{12,8},{1,5},{5,1},{9,13},{13,9},{2,6},{6,2},{1... | collective-permute-start | bytes 86024 | tf_op jit(solution)/shard_map/columns_over_ctx/ppermute | solution.py:40
  85.8 6.3 %collective-permute-start.22 = (bf16[8,1792]{1,0:T(8,128)(2,1)S(1)}, bf16[8,1792]{1,0:T(8,128)(2,1)S(1)}, u32[]{:S(2)}, u32[]{:S(2)}) collective-permute-start(bf16[8,1792]{1,0:T(8,128)(2,1)S(1)} %get-tuple-element.52), channel_id=1, source_target_pairs={{0,8},{4,12},{8,0},{12,4},{1,9},{5,13},{9,1},{13,5},{2,10},{6,14},... | collective-permute-start | bytes 86024 | tf_op jit(solution)/shard_map/columns_over_ctx/ppermute | solution.py:40
  85.9 6.3 %collective-permute-start.23 = (bf16[8,1792]{1,0:T(8,128)(2,1)S(1)}, bf16[8,1792]{1,0:T(8,128)(2,1)S(1)}, u32[]{:S(2)}, u32[]{:S(2)}) collective-permute-start(bf16[8,1792]{1,0:T(8,128)(2,1)S(1)} %get-tuple-element.51), channel_id=1, source_target_pairs={{0,12},{4,8},{8,4},{12,0},{1,13},{5,9},{9,5},{13,1},{2,14},{6,10},... | collective-permute-start | bytes 86024 | tf_op jit(solution)/shard_map/columns_over_ctx/ppermute | solution.py:40
  87.7 4.5 %collective-permute-start.27 = (bf16[8,1792]{1,0:T(8,128)(2,1)S(1)}, bf16[8,1792]{1,0:T(8,128)(2,1)S(1)}, u32[]{:S(2)}, u32[]{:S(2)}) collective-permute-start(bf16[8,1792]{1,0:T(8,128)(2,1)S(1)} %get-tuple-element.49), channel_id=1, source_target_pairs={{0,4},{4,0},{8,12},{12,8},{1,5},{5,1},{9,13},{13,9},{2,6},{6,2},{1... | collective-permute-start | bytes 86024 | tf_op jit(solution)/shard_map/columns_over_ctx/ppermute | solution.py:40
  89.4 4.8 %collective-permute-start.28 = (bf16[8,1792]{1,0:T(8,128)(2,1)S(1)}, bf16[8,1792]{1,0:T(8,128)(2,1)S(1)}, u32[]{:S(2)}, u32[]{:S(2)}) collective-permute-start(bf16[8,1792]{1,0:T(8,128)(2,1)S(1)} %get-tuple-element.48), channel_id=1, source_target_pairs={{0,8},{4,12},{8,0},{12,4},{1,9},{5,13},{9,1},{13,5},{2,10},{6,14},... | collective-permute-start | bytes 86024 | tf_op jit(solution)/shard_map/columns_over_ctx/ppermute | solution.py:40
  90.3 5.7 %collective-permute-start.29 = (bf16[8,1792]{1,0:T(8,128)(2,1)S(1)}, bf16[8,1792]{1,0:T(8,128)(2,1)S(1)}, u32[]{:S(2)}, u32[]{:S(2)}) collective-permute-start(bf16[8,1792]{1,0:T(8,128)(2,1)S(1)} %get-tuple-element.47), channel_id=1, source_target_pairs={{0,12},{4,8},{8,4},{12,0},{1,13},{5,9},{9,5},{13,1},{2,14},{6,10},... | collective-permute-start | bytes 86024 | tf_op jit(solution)/shard_map/columns_over_ctx/ppermute | solution.py:40

commit v7 on v6

--- a/solution.py
+++ b/solution.py
@@ -27,8 +27,6 @@
 
 
 def chunk_rows(owned):
-    if owned % 32 == 0:
-        return (owned // 2, owned // 4, owned // 4)
     return (owned // 2, owned // 2)
 
 
@@ -175,7 +173,7 @@
         bias_ref[:, index * half : (index + 1) * half] = bias
 
 
-def attention_kernel(count, hold, q_ref, bias_ref, value_ref, *refs):
+def attention_kernel(count, q_ref, bias_ref, value_ref, *refs):
     heads, rows, depth = q_ref.shape
     if count:
         piece_refs, (out_ref, keys_ref, latent_ref) = refs[:count], refs[count:]
@@ -186,13 +184,7 @@
             latent_ref[start : start + width, :] = piece_ref[:LAT, :].T
             start += width
     else:
-        keys_ref, latent_ref, *refs = refs
-        if hold:
-            mix_hbm, out_ref, mix_ref, mix_sem = refs
-            mix_copy = pltpu.make_async_copy(mix_hbm, mix_ref, mix_sem)
-            mix_copy.start()
-        else:
-            (out_ref,) = refs
+        keys_ref, latent_ref, out_ref = refs
     amount = keys_ref.shape[1]
     group = max(1, min(heads, SUB_ROWS // rows))
     size = group * rows
@@ -222,27 +214,23 @@
             )
             out_ref[:, head * VD : (head + 1) * VD] = result.astype(jnp.bfloat16)
         scores = later
-    if hold:
-        mix_copy.wait()
-
-
-def attention(q_ext, bias, w_values, keys, gathered, held=()):
+
+
+def attention(q_ext, bias, w_values, keys, gathered):
     head_count, rows, depth = q_ext.shape
     amount = bias.shape[1]
     out_shape = [jax.ShapeDtypeStruct((rows, head_count * VD), jnp.bfloat16)]
     if not gathered:
         out_shape.append(jax.ShapeDtypeStruct((depth, amount), jnp.bfloat16))
         out_shape.append(jax.ShapeDtypeStruct((amount, LAT), jnp.bfloat16))
-    out_shape += [jax.ShapeDtypeStruct(array.shape, array.dtype) for array in held]
     return pl.pallas_call(
-        functools.partial(attention_kernel, 0 if gathered else len(keys), len(held) > 0),
+        functools.partial(attention_kernel, 0 if gathered else len(keys)),
         out_shape=out_shape,
-        in_specs=[IN_VMEM] * (3 + len(keys)) + [IN_HBM] * len(held),
+        in_specs=[IN_VMEM] * (3 + len(keys)),
         out_specs=[IN_VMEM] * len(out_shape),
-        scratch_shapes=[pltpu.SemaphoreType.DMA] * len(held),
         compiler_params=params(16 if amount <= 1024 else 40),
         cost_estimate=SHORT,
-    )(q_ext, bias, w_values, *keys, *held)
+    )(q_ext, bias, w_values, *keys)
 
 
 def product_kernel(count, n_x, after, weight_ref, *refs):
@@ -280,20 +268,69 @@
     )(w_out, *pieces, *after)
 
 
-def place_kernel(n_ctx, ctx_ref, *refs):
+def core_sum_kernel(n_x, kept_ref, received_ref, total_ref, *sent_refs):
+    x = lax.axis_index("head") // 2
+    for offset in range(n_x):
+        summed = kept_ref[x ^ offset] + received_ref[x ^ offset].astype(jnp.float32)
+        if offset:
+            sent_refs[offset - 1][...] = summed.astype(jnp.bfloat16)
+        else:
+            total_ref[...] = summed
+
+
+def core_sum(kept, received):
+    n_x, rows, columns = kept.shape
+    own = jax.ShapeDtypeStruct((rows, columns), jnp.float32)
+    sent = jax.ShapeDtypeStruct((rows, columns), jnp.bfloat16)
+    out = pl.pallas_call(
+        functools.partial(core_sum_kernel, n_x),
+        out_shape=[own] + [sent] * (n_x - 1),
+        in_specs=[IN_VMEM, IN_VMEM],
+        out_specs=[IN_VMEM] * n_x,
+        compiler_params=params(4),
+        cost_estimate=SHORT,
+    )(kept, received)
+    return out[0], out[1:]
+
+
+def x_sum_kernel(count, total_ref, *refs):
+    received, block_refs = refs[:count], refs[count:]
+    total = total_ref[...]
+    for ref in received:
+        total = total + ref[...].astype(jnp.float32)
+    rows = block_refs[0].shape[0]
+    for index, block_ref in enumerate(block_refs):
+        block_ref[...] = total[index * rows : (index + 1) * rows].astype(jnp.bfloat16)
+
+
+def x_sum(total, received, n_ctx):
+    rows, columns = total.shape
+    block = jax.ShapeDtypeStruct((rows // n_ctx, columns), jnp.bfloat16)
+    return pl.pallas_call(
+        functools.partial(x_sum_kernel, len(received)),
+        out_shape=[block] * n_ctx,
+        in_specs=[IN_VMEM] * (1 + len(received)),
+        out_specs=[IN_VMEM] * n_ctx,
+        compiler_params=params(4),
+        cost_estimate=SHORT,
+    )(total, *received)
+
+
+def place_kernel(n_ctx, *refs):
     blocks, out_ref = refs[:-1], refs[-1]
+    ctx = lax.axis_index("ctx")
+    width = blocks[0].shape[1]
     for offset in range(n_ctx):
-
-        @pl.when(pl.program_id(0) == offset)
-        def _():
-            parts = [block[...].astype(jnp.float32) for block in blocks[offset::n_ctx]]
-            out_ref[...] = jnp.concatenate(parts, axis=0).astype(jnp.bfloat16)
-
-
-def place_columns(results, ctx, n_ctx):
+        parts = [block[...].astype(jnp.float32) for block in blocks[offset::n_ctx]]
+        column = pl.multiple_of((ctx ^ offset) * width, 128)
+        out_ref[:, pl.ds(column, width)] = jnp.concatenate(parts, axis=0).astype(jnp.bfloat16)
+
+
+def place_columns(results, n_ctx):
     width = results[0][0].shape[1]
     total = sum(result[0].shape[0] for result in results)
     if width % 128:
+        ctx = lax.axis_index("ctx")
         out = jnp.zeros((total, n_ctx * width), jnp.bfloat16)
         for offset in range(n_ctx):
             block = jnp.concatenate([result[offset] for result in results], axis=0)
@@ -302,16 +339,13 @@
     blocks = [block for result in results for block in result]
     return pl.pallas_call(
         functools.partial(place_kernel, n_ctx),
+        grid=(1,),
         out_shape=jax.ShapeDtypeStruct((total, n_ctx * width), jnp.bfloat16),
-        grid_spec=pltpu.PrefetchScalarGridSpec(
-            num_scalar_prefetch=1,
-            grid=(n_ctx,),
-            in_specs=[IN_VMEM] * len(blocks),
-            out_specs=pl.BlockSpec((total, width), lambda i, ctx_ref: (0, ctx_ref[0] ^ i)),
-        ),
+        in_specs=[IN_VMEM] * len(blocks),
+        out_specs=pl.BlockSpec((total, n_ctx * width), lambda i: (0, 0)),
         compiler_params=params(4),
         cost_estimate=SHORT,
-    )(jnp.full((1,), ctx, jnp.int32), *blocks)
+    )(*blocks)
 
 
 def shards(n_ctx, n_head, queries, kv_rows, w_kv_up, w_out, stretch_order, prefix_len):
@@ -319,16 +353,13 @@
     row_span = kv_rows.shape[0]
     cache_rows = row_span - query_rows
     half = row_span // 2
-    columns = w_out.shape[1]
     n_x = n_head // 2
     pieces = chunk_rows(query_rows // n_head)
-    ctx = lax.axis_index("ctx")
-    head = lax.axis_index("head")
-    x = head // 2
+    core = lax.axis_index("head") % 2
 
     with jax.named_scope("keys_over_ctx"):
         kv_t = kv_rows.T
-        own_half = jnp.where(head % 2 == 0, kv_t[:, :half], kv_t[:, half:])
+        own_half = jnp.where(core == 0, kv_t[:, :half], kv_t[:, half:])
         halves = [exchange(own_half, "ctx", n_ctx, offset) for offset in range(1, n_ctx)]
     with jax.named_scope("load"):
         q_ext, bias, w_values, own_keys = load(
@@ -339,9 +370,8 @@
         others = [exchange(array, "head", n_head, 1) for array in halves]
     with jax.named_scope("attention"):
         first, *keys = attention(q_ext[0], bias[0], w_values, [own_keys] + halves + others, False)
-        second, held = attention(q_ext[1], bias[1], w_values, keys, True, [w_out])
-        attended = [first, second]
-        for chunk in range(2, len(pieces)):
+        attended = [first]
+        for chunk in range(1, len(pieces)):
             attended += attention(q_ext[chunk], bias[chunk], w_values, keys, True)
     with jax.named_scope("attended_over_ctx"):
         gathered = [
@@ -351,30 +381,26 @@
     results = []
     after = attended[1:]
     crossed = []
-    for chunk, piece in enumerate(pieces):
+    for chunk in range(len(pieces)):
         with jax.named_scope("out_product"):
-            sent, kept = product(gathered[chunk], held, n_x, after)
+            sent, kept = product(gathered[chunk], w_out, n_x, after)
         with jax.named_scope("sum_over_cores"):
             ahead = list(crossed)
             if chunk + 1 < len(pieces):
                 ahead += [gathered[chunk + 1][1], gathered[chunk + 1][n_ctx // 2]]
             sent = tie(sent, ahead)
-            summed = kept + exchange(sent, "head", n_head, 1).astype(jnp.float32)
-            after = [summed]
+            total, sent = core_sum(kept, exchange(sent, "head", n_head, 1))
+            after = [total]
         with jax.named_scope("sum_over_x"):
-            total = lax.dynamic_index_in_dim(summed, x, 0, keepdims=False)
-            crossed = []
-            for offset in range(1, n_x):
-                sent = lax.dynamic_index_in_dim(summed, x ^ offset, 0, keepdims=False)
-                sent = exchange(sent.astype(jnp.bfloat16), "head", n_head, 2 * offset)
-                crossed.append(sent)
-                total = total + sent.astype(jnp.float32)
+            crossed = [
+                exchange(array, "head", n_head, 2 * offset) for offset, array in enumerate(sent, 1)
+            ]
+            total = x_sum(total, crossed, n_ctx)
         with jax.named_scope("columns_over_ctx"):
-            total = total.astype(jnp.bfloat16).reshape(n_ctx, piece, columns)
             blocks = [total[0]] + [exchange(total[d], "ctx", n_ctx, d) for d in range(1, n_ctx)]
         results.append(blocks)
     with jax.named_scope("output"):
-        return place_columns(results, ctx, n_ctx)
+        return place_columns(results, n_ctx)
 
 
 def solution(mesh):

time: 97.6 us -> 88.1 us (0.903)
  starting transfers between devices: 30.8 us -> 24.2 us
  local copies, waits for them, and re-layouts: 5.95 us -> 2.75 us
  waiting for transfers between devices: 38.5 us -> 40.5 us
  Pallas kernels: 19.9 us -> 18.6 us
    ppermute x30 -> x22, starting transfers between devices: 30.8 us -> 24.2 us  [exchange(): return lax.ppermute(array, axis, [(i, i ^ bit) for i in range(size)])]
    unnamed x14 -> x10, local copies, waits for them, and re-layouts: 5.84 us -> 2.75 us
    ppermute x30 -> x22, waiting for transfers between devices: 38.5 us -> 40.5 us  [exchange(): return lax.ppermute(array, axis, [(i, i ^ bit) for i in range(size)])]
    pallas_call x3 -> x2, Pallas kernels: 8.61 us -> 7.69 us  [attention(): pl.pallas_call(functools.partial(attention_kernel, 0 if gathered else len...]
    pallas_call x3 -> x2, Pallas kernels: 4.31 us -> 4.2 us  [product(): pl.pallas_call(functools.partial(product_kernel, count, n_x, len(after)),...]
  transfers between devices with their start and end apart: 30 -> 22, of which waited for: 16 -> 12; matrix products, arithmetic and copies ran while one was open for 0% -> 0% of each run, Pallas kernels for 15% -> 16%
where the time goes in v7:
time: 88.1 us; the launch traced here: 87.9 us
  waiting for transfers between devices  40.5 us (46%)
  starting transfers between devices  24.2 us (27%)
  Pallas kernels  18.6 us (21%)
  local copies, waits for them, and re-layouts  2.75 us (3%)
  other arithmetic  1 us (1%)
    ppermute x22, waiting for transfers between devices, exchange(): return lax.ppermute(array, axis, [(i, i ^ bit) for i in range(size)])  40.5 us
    ppermute x22, starting transfers between devices, exchange(): return lax.ppermute(array, axis, [(i, i ^ bit) for i in range(size)])  24.2 us
    pallas_call x2, Pallas kernels, attention(): pl.pallas_call(functools.partial(attention_kernel, 0 if gathered else len...  7.69 us
    pallas_call x1, Pallas kernels, load(): pl.pallas_call(functools.partial(load_kernel, owners, pieces, cache_rows)...  5.66 us
    pallas_call x2, Pallas kernels, product(): pl.pallas_call(functools.partial(product_kernel, count, n_x, len(after)),...  4.2 us
    unnamed x10, local copies, waits for them, and re-layouts  2.75 us
  transfers between devices with their start and end apart: 22, of which 12 were waited for; matrix products, arithmetic and copies ran while one was open for 0% of the time, Pallas kernels for 16%

profile of v7, /device:TPU:0, one launch (start us, length us, event | category | flops | bytes accessed | tf_op | source)
XLA Modules:
  0.0 87.9 jit_solution(1578624860753685577)
XLA Ops:
  0.0 1.0 %slice_select_fusion = bf16[576,128]{1,0:T(8,128)(2,1)S(1)} fusion(bf16[576,256]{1,0:T(8,128)(2,1)} %bitcast.3, pred[]{:T(512)S(6)} %eq.5), kind=kLoop, calls=%fused_computation | loop fusion | flops 73728 | bytes 442369 | tf_op jit(solution)/shard_map/keys_over_ctx/jit(_where)/select_n | solution.py:362
  1.0 3.1 %collective-permute-start = (bf16[576,128]{1,0:T(8,128)(2,1)S(1)}, bf16[576,128]{1,0:T(8,128)(2,1)S(1)}, u32[]{:S(2)}, u32[]{:S(2)}) collective-permute-start(bf16[576,128]{1,0:T(8,128)(2,1)S(1)} %slice_select_fusion), channel_id=1, source_target_pairs={{0,4},{4,0},{8,12},{12,8},{1,5},{5,1},{9,13},{13,9},{2,6},{6,2},{1... | collective-permute-start | bytes 442376 | tf_op jit(solution)/shard_map/keys_over_ctx/ppermute | solution.py:38
  4.1 2.6 %collective-permute-start.1 = (bf16[576,128]{1,0:T(8,128)(2,1)S(1)}, bf16[576,128]{1,0:T(8,128)(2,1)S(1)}, u32[]{:S(2)}, u32[]{:S(2)}) collective-permute-start(bf16[576,128]{1,0:T(8,128)(2,1)S(1)} %slice_select_fusion), channel_id=1, source_target_pairs={{0,8},{4,12},{8,0},{12,4},{1,9},{5,13},{9,1},{13,5},{2,10},{6,14},... | collective-permute-start | bytes 442376 | tf_op jit(solution)/shard_map/keys_over_ctx/ppermute | solution.py:38
  6.7 0.0 collective-permute-start.2
  7.3 0.0 copy-start
  7.3 1.0 %copy-done = bf16[256,576]{0,1:T(8,128)(2,1)S(1)} copy-done((bf16[256,576]{0,1:T(8,128)(2,1)S(1)}, bf16[256,576]{0,1:T(8,128)(2,1)}, u32[]{:S(2)}) %copy-start) | copy-done | bytes 294936
  8.3 0.0 copy-start.1
  8.3 1.1 %copy-done.1 = bf16[128,3072]{1,0:T(8,128)(2,1)S(1)} copy-done((bf16[128,3072]{1,0:T(8,128)(2,1)S(1)}, bf16[128,3072]{1,0:T(8,128)(2,1)}, u32[]{:S(2)}) %copy-start.1) | copy-done | bytes 786456
  9.4 0.0 copy-start.2
  9.4 0.7 copy-done.2
  10.1 0.0 slice-start
  10.1 5.7 %load.1 = (bf16[16,64,576]{2,1,0:T(8,128)(2,1)S(1)}, bf16[16,64,576]{2,1,0:T(8,128)(2,1)S(1)}, f32[64,1024]{1,0:T(8,128)S(1)}, f32[64,1024]{1,0:T(8,128)S(1)}, b...) custom-call(s32[4]{0:T(128)S(1)} %copy-done.2, s32[1]{0:T(128)S(6)} %copy.19.prefix_ref, ...), custom_call_target="tpu_custom_call" | custom-call | flops 1024 | bytes 1024 | tf_op jit(solution)/shard_map/load/pallas_call | solution.py:131
  15.8 0.0 collective-permute-done.refs_0_
  15.8 0.1 collective-permute-start.3
  15.9 2.2 %collective-permute-done.1.refs_0_ = bf16[576,128]{1,0:T(8,128)(2,1)S(1)} collective-permute-done((bf16[576,128]{1,0:T(8,128)(2,1)S(1)}, bf16[576,128]{1,0:T(8,128)(2,1)S(1)}, u32[]{:S(2)}, u32[]{:S(2)}) %collective-permute-start.1) | collective-permute-done | bytes 147488 | tf_op jit(solution)/shard_map/keys_over_ctx/ppermute | solution.py:38
  18.1 0.0 collective-permute-start.4
  18.1 0.0 collective-permute-done.2.refs_0_
  18.1 0.5 collective-permute-start.5
  18.6 0.0 collective-permute-done.3.refs_4_
  18.6 0.9 collective-permute-done.4.refs_5_
  19.5 0.2 collective-permute-done.5.refs_6_
  19.7 0.0 slice-start.1
  19.7 3.9 %attention.2 = (bf16[64,2048]{1,0:T(8,128)(2,1)S(1)}, bf16[576,1024]{1,0:T(8,128)(2,1)S(1)}, bf16[1024,512]{1,0:T(8,128)(2,1)S(1)}) custom-call(bf16[16,64,576]{2,1,0:T(8,128)(2,1)S(1)} %get-tuple-element.30.q_ref, f32[64,1024]{1,0:T(8,128)S(1)} %get-tuple-element.31.bias_ref, bf16[16,512,128]{2,1,0:T(8,128)(2,1)S(1)} %get-tuple-element.32.value_ref, ...), custom_call_target="tpu_custom_call" | custom-call | flops 1024 | bytes 1024 | tf_op jit(solution)/shard_map/attention/pallas_call | solution.py:226
  23.6 3.2 %collective-permute-start.7 = (bf16[64,2048]{1,0:T(8,128)(2,1)S(1)}, bf16[64,2048]{1,0:T(8,128)(2,1)S(1)}, u32[]{:S(2)}, u32[]{:S(2)}) collective-permute-start(bf16[64,2048]{1,0:T(8,128)(2,1)S(1)} %get-tuple-element.34.refs_0_), channel_id=1, source_target_pairs={{0,8},{4,12},{8,0},{12,4},{1,9},{5,13},{9,1},{13,5},{2,10},{6,14},... | collective-permute-start | bytes 786440 | tf_op jit(solution)/shard_map/attended_over_ctx/ppermute | solution.py:38
  26.7 0.0 collective-permute-start.6
  26.7 3.8 %attention.3.refs_1_.refs_4_.refs_0_ = bf16[64,2048]{1,0:T(8,128)(2,1)S(1)} custom-call(bf16[16,64,576]{2,1,0:T(8,128)(2,1)S(1)} %get-tuple-element.35.q_ref, f32[64,1024]{1,0:T(8,128)S(1)} %get-tuple-element.36.bias_ref, bf16[16,512,128]{2,1,0:T(8,128)(2,1)S(1)} %get-tuple-element.32.value_ref, bf16[576,1024]{1,0:T(8,128)(2,1)S(1)} %get-tuple-element.37.refs_0_, ...), custom_call_target="tpu_custom_call" | custom-call | flops 1024 | bytes 1024 | tf_op jit(solution)/shard_map/attention/pallas_call | solution.py:226
  30.5 8.5 %collective-permute-done.7.refs_0_ = bf16[64,2048]{1,0:T(8,128)(2,1)S(1)} collective-permute-done((bf16[64,2048]{1,0:T(8,128)(2,1)S(1)}, bf16[64,2048]{1,0:T(8,128)(2,1)S(1)}, u32[]{:S(2)}, u32[]{:S(2)}) %collective-permute-start.7) | collective-permute-done | bytes 262176 | tf_op jit(solution)/shard_map/attended_over_ctx/ppermute | solution.py:38
  39.1 0.0 collective-permute-start.8
  39.1 2.4 %collective-permute-start.10 = (bf16[64,2048]{1,0:T(8,128)(2,1)S(1)}, bf16[64,2048]{1,0:T(8,128)(2,1)S(1)}, u32[]{:S(2)}, u32[]{:S(2)}) collective-permute-start(bf16[64,2048]{1,0:T(8,128)(2,1)S(1)} %attention.3.refs_1_.refs_4_.refs_0_), channel_id=1, source_target_pairs={{0,8},{4,12},{8,0},{12,4},{1,9},{5,13},{9,1},{13,5},{2,10},{6,14},... | collective-permute-start | bytes 786440 | tf_op jit(solution)/shard_map/attended_over_ctx/ppermute | solution.py:38
  41.5 0.0 collective-permute-start.9
  41.5 0.0 collective-permute-done.6.refs_1_
  41.5 12.0 %collective-permute-done.8.refs_3_ = bf16[64,2048]{1,0:T(8,128)(2,1)S(1)} collective-permute-done((bf16[64,2048]{1,0:T(8,128)(2,1)S(1)}, bf16[64,2048]{1,0:T(8,128)(2,1)S(1)}, u32[]{:S(2)}, u32[]{:S(2)}) %collective-permute-start.8) | collective-permute-done | bytes 262176 | tf_op jit(solution)/shard_map/attended_over_ctx/ppermute | solution.py:38
  53.5 0.0 slice-done
  53.5 0.0 slice-done.1
  53.5 2.1 %out_product.2 = (bf16[2,64,1792]{2,1,0:T(8,128)(2,1)S(1)}, f32[2,64,1792]{2,1,0:T(8,128)S(1)}) custom-call(bf16[2048,1792]{1,0:T(8,128)(2,1)S(1)} %bitcast.2, bf16[64,2048]{1,0:T(8,128)(2,1)S(1)} %get-tuple-element.34.refs_0_, bf16[64,2048]{1,0:T(8,128)(2,1)S(1)} %collective-permute-done.6.refs_1_, bf16[64,2048]{1,0:T(8,128)(2,1)S(1)} %attended_over_ctx.1.refs_2_, ...), custom_call_target="tpu_custom_call" | custom-call | flops 1024 | bytes 1024 | tf_op jit(solution)/shard_map/out_product/pallas_call | solution.py:260
  55.6 0.0 collective-permute-done.10.refs_2_
  55.7 2.4 %collective-permute-done.9.refs_1_ = bf16[64,2048]{1,0:T(8,128)(2,1)S(1)} collective-permute-done((bf16[64,2048]{1,0:T(8,128)(2,1)S(1)}, bf16[64,2048]{1,0:T(8,128)(2,1)S(1)}, u32[]{:S(2)}, u32[]{:S(2)}) %collective-permute-start.9) | collective-permute-done | bytes 262176 | tf_op jit(solution)/shard_map/attended_over_ctx/ppermute | solution.py:38
  58.1 0.0 collective-permute-start.11
  58.1 0.3 collective-permute-start.16
  58.4 1.5 %collective-permute-done.11.received_ref = bf16[2,64,1792]{2,1,0:T(8,128)(2,1)S(1)} collective-permute-done((bf16[2,64,1792]{2,1,0:T(8,128)(2,1)S(1)}, bf16[2,64,1792]{2,1,0:T(8,128)(2,1)S(1)}, u32[]{:S(2)}, u32[]{:S(2)}) %collective-permute-start.11) | collective-permute-done | bytes 458784 | tf_op jit(solution)/shard_map/sum_over_cores/ppermute | solution.py:38
  59.9 0.1 sum_over_cores.5
  60.0 1.5 %collective-permute-start.12 = (bf16[64,1792]{1,0:T(8,128)(2,1)S(1)}, bf16[64,1792]{1,0:T(8,128)(2,1)S(1)}, u32[]{:S(2)}, u32[]{:S(2)}) collective-permute-start(bf16[64,1792]{1,0:T(8,128)(2,1)S(1)} %get-tuple-element.42), channel_id=1, source_target_pairs={{0,2},{1,3},{2,0},{3,1},{4,6},{5,7},{6,4},{7,5},{8,10},{9,11},{10,... | collective-permute-start | bytes 688136 | tf_op jit(solution)/shard_map/sum_over_x/ppermute | solution.py:38
  61.5 5.3 %collective-permute-done.16.refs_3_ = bf16[64,2048]{1,0:T(8,128)(2,1)S(1)} collective-permute-done((bf16[64,2048]{1,0:T(8,128)(2,1)S(1)}, bf16[64,2048]{1,0:T(8,128)(2,1)S(1)}, u32[]{:S(2)}, u32[]{:S(2)}) %collective-permute-start.16) | collective-permute-done | bytes 262176 | tf_op jit(solution)/shard_map/attended_over_ctx/ppermute | solution.py:38
  66.8 2.1 %out_product.3 = (bf16[2,64,1792]{2,1,0:T(8,128)(2,1)S(1)}, f32[2,64,1792]{2,1,0:T(8,128)S(1)}) custom-call(bf16[2048,1792]{1,0:T(8,128)(2,1)S(1)} %bitcast.2, bf16[64,2048]{1,0:T(8,128)(2,1)S(1)} %attention.3.refs_1_.refs_4_.refs_0_, bf16[64,2048]{1,0:T(8,128)(2,1)S(1)} %collective-permute-done.9.refs_1_, ...), custom_call_target="tpu_custom_call" | custom-call | flops 1024 | bytes 1024 | tf_op jit(solution)/shard_map/out_product/pallas_call | solution.py:260
  68.9 0.0 collective-permute-done.12.refs_0_.refs_1_
  69.0 0.1 collective-permute-start.17
  69.0 1.8 %collective-permute-done.17.received_ref = bf16[2,64,1792]{2,1,0:T(8,128)(2,1)S(1)} collective-permute-done((bf16[2,64,1792]{2,1,0:T(8,128)(2,1)S(1)}, bf16[2,64,1792]{2,1,0:T(8,128)(2,1)S(1)}, u32[]{:S(2)}, u32[]{:S(2)}) %collective-permute-start.17) | collective-permute-done | bytes 458784 | tf_op jit(solution)/shard_map/sum_over_cores/ppermute | solution.py:38
  70.8 0.1 sum_over_cores.7
  70.9 1.5 %collective-permute-start.18 = (bf16[64,1792]{1,0:T(8,128)(2,1)S(1)}, bf16[64,1792]{1,0:T(8,128)(2,1)S(1)}, u32[]{:S(2)}, u32[]{:S(2)}) collective-permute-start(bf16[64,1792]{1,0:T(8,128)(2,1)S(1)} %get-tuple-element.50), channel_id=1, source_target_pairs={{0,2},{1,3},{2,0},{3,1},{4,6},{5,7},{6,4},{7,5},{8,10},{9,11},{10,... | collective-permute-start | bytes 688136 | tf_op jit(solution)/shard_map/sum_over_x/ppermute | solution.py:38
  72.5 0.4 collective-permute-start.13
  72.9 2.0 %collective-permute-start.14 = (bf16[16,1792]{1,0:T(8,128)(2,1)S(1)}, bf16[16,1792]{1,0:T(8,128)(2,1)S(1)}, u32[]{:S(2)}, u32[]{:S(2)}) collective-permute-start(bf16[16,1792]{1,0:T(8,128)(2,1)S(1)} %get-tuple-element.45), channel_id=1, source_target_pairs={{0,8},{4,12},{8,0},{12,4},{1,9},{5,13},{9,1},{13,5},{2,10},{6,14},... | collective-permute-start | bytes 172040 | tf_op jit(solution)/shard_map/columns_over_ctx/ppermute | solution.py:38
  74.9 2.0 %collective-permute-start.15 = (bf16[16,1792]{1,0:T(8,128)(2,1)S(1)}, bf16[16,1792]{1,0:T(8,128)(2,1)S(1)}, u32[]{:S(2)}, u32[]{:S(2)}) collective-permute-start(bf16[16,1792]{1,0:T(8,128)(2,1)S(1)} %get-tuple-element.46), channel_id=1, source_target_pairs={{0,12},{4,8},{8,4},{12,0},{1,13},{5,9},{9,5},{13,1},{2,14},{6,10},... | collective-permute-start | bytes 172040 | tf_op jit(solution)/shard_map/columns_over_ctx/ppermute | solution.py:38
  76.9 1.7 %collective-permute-done.18.refs_0_ = bf16[64,1792]{1,0:T(8,128)(2,1)S(1)} collective-permute-done((bf16[64,1792]{1,0:T(8,128)(2,1)S(1)}, bf16[64,1792]{1,0:T(8,128)(2,1)S(1)}, u32[]{:S(2)}, u32[]{:S(2)}) %collective-permute-start.18) | collective-permute-done | bytes 229408 | tf_op jit(solution)/shard_map/sum_over_x/ppermute | solution.py:38
  78.7 0.4 collective-permute-start.19
  79.1 2.0 %collective-permute-start.20 = (bf16[16,1792]{1,0:T(8,128)(2,1)S(1)}, bf16[16,1792]{1,0:T(8,128)(2,1)S(1)}, u32[]{:S(2)}, u32[]{:S(2)}) collective-permute-start(bf16[16,1792]{1,0:T(8,128)(2,1)S(1)} %get-tuple-element.53), channel_id=1, source_target_pairs={{0,8},{4,12},{8,0},{12,4},{1,9},{5,13},{9,1},{13,5},{2,10},{6,14},... | collective-permute-start | bytes 172040 | tf_op jit(solution)/shard_map/columns_over_ctx/ppermute | solution.py:38
  81.1 0.0 collective-permute-done.13.refs_1_
  81.1 2.0 %collective-permute-start.21 = (bf16[16,1792]{1,0:T(8,128)(2,1)S(1)}, bf16[16,1792]{1,0:T(8,128)(2,1)S(1)}, u32[]{:S(2)}, u32[]{:S(2)}) collective-permute-start(bf16[16,1792]{1,0:T(8,128)(2,1)S(1)} %get-tuple-element.54), channel_id=1, source_target_pairs={{0,12},{4,8},{8,4},{12,0},{1,13},{5,9},{9,5},{13,1},{2,14},{6,10},... | collective-permute-start | bytes 172040 | tf_op jit(solution)/shard_map/columns_over_ctx/ppermute | solution.py:38
  83.1 0.0 collective-permute-done.14.refs_2_
  83.1 0.0 collective-permute-done.15.refs_3_
  83.1 0.0 collective-permute-done.19.refs_5_
  83.1 1.1 %collective-permute-done.20.refs_6_ = bf16[16,1792]{1,0:T(8,128)(2,1)S(1)} collective-permute-done((bf16[16,1792]{1,0:T(8,128)(2,1)S(1)}, bf16[16,1792]{1,0:T(8,128)(2,1)S(1)}, u32[]{:S(2)}, u32[]{:S(2)}) %collective-permute-start.20) | collective-permute-done | bytes 57376 | tf_op jit(solution)/shard_map/columns_over_ctx/ppermute | solution.py:38
  84.2 2.8 %collective-permute-done.21.refs_7_ = bf16[16,1792]{1,0:T(8,128)(2,1)S(1)} collective-permute-done((bf16[16,1792]{1,0:T(8,128)(2,1)S(1)}, bf16[16,1792]{1,0:T(8,128)(2,1)S(1)}, u32[]{:S(2)}, u32[]{:S(2)}) %collective-permute-start.21) | collective-permute-done | bytes 57376 | tf_op jit(solution)/shard_map/columns_over_ctx/ppermute | solution.py:38
  87.1 0.8 output.1
  (9 shorter events, 0.1 us)
Async XLA Ops:
  1.0 14.8 %collective-permute-start = (bf16[576,128]{1,0:T(8,128)(2,1)S(1)}, bf16[576,128]{1,0:T(8,128)(2,1)S(1)}, u32[]{:S(2)}, u32[]{:S(2)}) collective-permute-start(bf16[576,128]{1,0:T(8,128)(2,1)S(1)} %slice_select_fusion), channel_id=1, source_target_pairs={{0,4},{4,0},{8,12},{12,8},{1,5},{5,1},{9,13},{13,9},{2,6},{6,2},{1... | collective-permute-start | bytes 442376 | tf_op jit(solution)/shard_map/keys_over_ctx/ppermute | solution.py:38
  4.1 14.0 %collective-permute-start.1 = (bf16[576,128]{1,0:T(8,128)(2,1)S(1)}, bf16[576,128]{1,0:T(8,128)(2,1)S(1)}, u32[]{:S(2)}, u32[]{:S(2)}) collective-permute-start(bf16[576,128]{1,0:T(8,128)(2,1)S(1)} %slice_select_fusion), channel_id=1, source_target_pairs={{0,8},{4,12},{8,0},{12,4},{1,9},{5,13},{9,1},{13,5},{2,10},{6,14},... | collective-permute-start | bytes 442376 | tf_op jit(solution)/shard_map/keys_over_ctx/ppermute | solution.py:38
  6.7 11.4 %collective-permute-start.2 = (bf16[576,128]{1,0:T(8,128)(2,1)S(1)}, bf16[576,128]{1,0:T(8,128)(2,1)S(1)}, u32[]{:S(2)}, u32[]{:S(2)}) collective-permute-start(bf16[576,128]{1,0:T(8,128)(2,1)S(1)} %slice_select_fusion), channel_id=1, source_target_pairs={{0,12},{4,8},{8,4},{12,0},{1,13},{5,9},{9,5},{13,1},{2,14},{6,10},... | collective-permute-start | bytes 442376 | tf_op jit(solution)/shard_map/keys_over_ctx/ppermute | solution.py:38
  7.3 1.0 %copy-start = (bf16[256,576]{0,1:T(8,128)(2,1)S(1)}, bf16[256,576]{0,1:T(8,128)(2,1)}, u32[]{:S(2)}) copy-start(bf16[256,576]{0,1:T(8,128)(2,1)} %param.7) | copy-start | bytes 884740
  8.3 1.1 %copy-start.1 = (bf16[128,3072]{1,0:T(8,128)(2,1)S(1)}, bf16[128,3072]{1,0:T(8,128)(2,1)}, u32[]{:S(2)}) copy-start(bf16[128,3072]{1,0:T(8,128)(2,1)} %q_hbm.1) | copy-start | bytes 2359300
  9.4 0.7 copy-start.2
  10.1 43.4 %slice-start = ((s8[7340032]{0:T(1024)(128)(4,1)}), s8[3145728]{0:T(1024)(128)(4,1)S(1)}, s32[]{:S(2)}) async-start(s8[7340032]{0:T(1024)(128)(4,1)} %bitcast.1), calls=%async_computation | async-start | bytes 6291456
  15.8 2.8 %collective-permute-start.3 = (bf16[576,128]{1,0:T(8,128)(2,1)S(1)}, bf16[576,128]{1,0:T(8,128)(2,1)S(1)}, u32[]{:S(2)}, u32[]{:S(2)}) collective-permute-start(bf16[576,128]{1,0:T(8,128)(2,1)S(1)} %keys_over_cores.3.refs_1_), channel_id=1, source_target_pairs={{0,1},{1,0},{2,3},{3,2},{4,5},{5,4},{6,7},{7,6},{8,9},{9,8},{10,11... | collective-permute-start | bytes 442376 | tf_op jit(solution)/shard_map/keys_over_cores/ppermute | solution.py:38
  18.1 1.4 %collective-permute-start.4 = (bf16[576,128]{1,0:T(8,128)(2,1)S(1)}, bf16[576,128]{1,0:T(8,128)(2,1)S(1)}, u32[]{:S(2)}, u32[]{:S(2)}) collective-permute-start(bf16[576,128]{1,0:T(8,128)(2,1)S(1)} %keys_over_cores.4.refs_2_), channel_id=1, source_target_pairs={{0,1},{1,0},{2,3},{3,2},{4,5},{5,4},{6,7},{7,6},{8,9},{9,8},{10,11... | collective-permute-start | bytes 442376 | tf_op jit(solution)/shard_map/keys_over_cores/ppermute | solution.py:38
  18.1 1.6 %collective-permute-start.5 = (bf16[576,128]{1,0:T(8,128)(2,1)S(1)}, bf16[576,128]{1,0:T(8,128)(2,1)S(1)}, u32[]{:S(2)}, u32[]{:S(2)}) collective-permute-start(bf16[576,128]{1,0:T(8,128)(2,1)S(1)} %keys_over_cores.5.refs_3_), channel_id=1, source_target_pairs={{0,1},{1,0},{2,3},{3,2},{4,5},{5,4},{6,7},{7,6},{8,9},{9,8},{10,11... | collective-permute-start | bytes 442376 | tf_op jit(solution)/shard_map/keys_over_cores/ppermute | solution.py:38
  19.7 33.9 %slice-start.1 = ((s8[7340032]{0:T(1024)(128)(4,1)}), s8[4194304]{0:T(1024)(128)(4,1)S(1)}, s32[]{:S(2)}) async-start(s8[7340032]{0:T(1024)(128)(4,1)} %bitcast.1), calls=%async_computation.1 | async-start | bytes 8388608
  23.6 15.5 %collective-permute-start.7 = (bf16[64,2048]{1,0:T(8,128)(2,1)S(1)}, bf16[64,2048]{1,0:T(8,128)(2,1)S(1)}, u32[]{:S(2)}, u32[]{:S(2)}) collective-permute-start(bf16[64,2048]{1,0:T(8,128)(2,1)S(1)} %get-tuple-element.34.refs_0_), channel_id=1, source_target_pairs={{0,8},{4,12},{8,0},{12,4},{1,9},{5,13},{9,1},{13,5},{2,10},{6,14},... | collective-permute-start | bytes 786440 | tf_op jit(solution)/shard_map/attended_over_ctx/ppermute | solution.py:38
  26.7 14.8 %collective-permute-start.6 = (bf16[64,2048]{1,0:T(8,128)(2,1)S(1)}, bf16[64,2048]{1,0:T(8,128)(2,1)S(1)}, u32[]{:S(2)}, u32[]{:S(2)}) collective-permute-start(bf16[64,2048]{1,0:T(8,128)(2,1)S(1)} %get-tuple-element.34.refs_0_), channel_id=1, source_target_pairs={{0,4},{4,0},{8,12},{12,8},{1,5},{5,1},{9,13},{13,9},{2,6},{6,2},{1... | collective-permute-start | bytes 786440 | tf_op jit(solution)/shard_map/attended_over_ctx/ppermute | solution.py:38
  39.1 14.5 %collective-permute-start.8 = (bf16[64,2048]{1,0:T(8,128)(2,1)S(1)}, bf16[64,2048]{1,0:T(8,128)(2,1)S(1)}, u32[]{:S(2)}, u32[]{:S(2)}) collective-permute-start(bf16[64,2048]{1,0:T(8,128)(2,1)S(1)} %attended_over_ctx.1.refs_2_), channel_id=1, source_target_pairs={{0,4},{4,0},{8,12},{12,8},{1,5},{5,1},{9,13},{13,9},{2,6},{6,2},{1... | collective-permute-start | bytes 786440 | tf_op jit(solution)/shard_map/attended_over_ctx/ppermute | solution.py:38
  39.1 16.6 %collective-permute-start.10 = (bf16[64,2048]{1,0:T(8,128)(2,1)S(1)}, bf16[64,2048]{1,0:T(8,128)(2,1)S(1)}, u32[]{:S(2)}, u32[]{:S(2)}) collective-permute-start(bf16[64,2048]{1,0:T(8,128)(2,1)S(1)} %attention.3.refs_1_.refs_4_.refs_0_), channel_id=1, source_target_pairs={{0,8},{4,12},{8,0},{12,4},{1,9},{5,13},{9,1},{13,5},{2,10},{6,14},... | collective-permute-start | bytes 786440 | tf_op jit(solution)/shard_map/attended_over_ctx/ppermute | solution.py:38
  41.5 16.6 %collective-permute-start.9 = (bf16[64,2048]{1,0:T(8,128)(2,1)S(1)}, bf16[64,2048]{1,0:T(8,128)(2,1)S(1)}, u32[]{:S(2)}, u32[]{:S(2)}) collective-permute-start(bf16[64,2048]{1,0:T(8,128)(2,1)S(1)} %attention.3.refs_1_.refs_4_.refs_0_), channel_id=1, source_target_pairs={{0,4},{4,0},{8,12},{12,8},{1,5},{5,1},{9,13},{13,9},{2,6},{6,2},{1... | collective-permute-start | bytes 786440 | tf_op jit(solution)/shard_map/attended_over_ctx/ppermute | solution.py:38
  58.1 1.8 %collective-permute-start.11 = (bf16[2,64,1792]{2,1,0:T(8,128)(2,1)S(1)}, bf16[2,64,1792]{2,1,0:T(8,128)(2,1)S(1)}, u32[]{:S(2)}, u32[]{:S(2)}) collective-permute-start(bf16[2,64,1792]{2,1,0:T(8,128)(2,1)S(1)} %sum_over_cores.4), channel_id=1, source_target_pairs={{0,1},{1,0},{2,3},{3,2},{4,5},{5,4},{6,7},{7,6},{8,9},{9,8},{10,11... | collective-permute-start | bytes 1376264 | tf_op jit(solution)/shard_map/sum_over_cores/ppermute | solution.py:38
  58.1 8.7 %collective-permute-start.16 = (bf16[64,2048]{1,0:T(8,128)(2,1)S(1)}, bf16[64,2048]{1,0:T(8,128)(2,1)S(1)}, u32[]{:S(2)}, u32[]{:S(2)}) collective-permute-start(bf16[64,2048]{1,0:T(8,128)(2,1)S(1)} %collective-permute-done.10.refs_2_), channel_id=1, source_target_pairs={{0,4},{4,0},{8,12},{12,8},{1,5},{5,1},{9,13},{13,9},{2,6},{6,2},{1... | collective-permute-start | bytes 786440 | tf_op jit(solution)/shard_map/attended_over_ctx/ppermute | solution.py:38
  60.0 8.9 %collective-permute-start.12 = (bf16[64,1792]{1,0:T(8,128)(2,1)S(1)}, bf16[64,1792]{1,0:T(8,128)(2,1)S(1)}, u32[]{:S(2)}, u32[]{:S(2)}) collective-permute-start(bf16[64,1792]{1,0:T(8,128)(2,1)S(1)} %get-tuple-element.42), channel_id=1, source_target_pairs={{0,2},{1,3},{2,0},{3,1},{4,6},{5,7},{6,4},{7,5},{8,10},{9,11},{10,... | collective-permute-start | bytes 688136 | tf_op jit(solution)/shard_map/sum_over_x/ppermute | solution.py:38
  69.0 1.9 %collective-permute-start.17 = (bf16[2,64,1792]{2,1,0:T(8,128)(2,1)S(1)}, bf16[2,64,1792]{2,1,0:T(8,128)(2,1)S(1)}, u32[]{:S(2)}, u32[]{:S(2)}) collective-permute-start(bf16[2,64,1792]{2,1,0:T(8,128)(2,1)S(1)} %sum_over_cores.6), channel_id=1, source_target_pairs={{0,1},{1,0},{2,3},{3,2},{4,5},{5,4},{6,7},{7,6},{8,9},{9,8},{10,11... | collective-permute-start | bytes 1376264 | tf_op jit(solution)/shard_map/sum_over_cores/ppermute | solution.py:38
  70.9 7.7 %collective-permute-start.18 = (bf16[64,1792]{1,0:T(8,128)(2,1)S(1)}, bf16[64,1792]{1,0:T(8,128)(2,1)S(1)}, u32[]{:S(2)}, u32[]{:S(2)}) collective-permute-start(bf16[64,1792]{1,0:T(8,128)(2,1)S(1)} %get-tuple-element.50), channel_id=1, source_target_pairs={{0,2},{1,3},{2,0},{3,1},{4,6},{5,7},{6,4},{7,5},{8,10},{9,11},{10,... | collective-permute-start | bytes 688136 | tf_op jit(solution)/shard_map/sum_over_x/ppermute | solution.py:38
  72.5 8.6 %collective-permute-start.13 = (bf16[16,1792]{1,0:T(8,128)(2,1)S(1)}, bf16[16,1792]{1,0:T(8,128)(2,1)S(1)}, u32[]{:S(2)}, u32[]{:S(2)}) collective-permute-start(bf16[16,1792]{1,0:T(8,128)(2,1)S(1)} %get-tuple-element.44), channel_id=1, source_target_pairs={{0,4},{4,0},{8,12},{12,8},{1,5},{5,1},{9,13},{13,9},{2,6},{6,2},{1... | collective-permute-start | bytes 172040 | tf_op jit(solution)/shard_map/columns_over_ctx/ppermute | solution.py:38
  72.9 10.2 %collective-permute-start.14 = (bf16[16,1792]{1,0:T(8,128)(2,1)S(1)}, bf16[16,1792]{1,0:T(8,128)(2,1)S(1)}, u32[]{:S(2)}, u32[]{:S(2)}) collective-permute-start(bf16[16,1792]{1,0:T(8,128)(2,1)S(1)} %get-tuple-element.45), channel_id=1, source_target_pairs={{0,8},{4,12},{8,0},{12,4},{1,9},{5,13},{9,1},{13,5},{2,10},{6,14},... | collective-permute-start | bytes 172040 | tf_op jit(solution)/shard_map/columns_over_ctx/ppermute | solution.py:38
  74.9 8.2 %collective-permute-start.15 = (bf16[16,1792]{1,0:T(8,128)(2,1)S(1)}, bf16[16,1792]{1,0:T(8,128)(2,1)S(1)}, u32[]{:S(2)}, u32[]{:S(2)}) collective-permute-start(bf16[16,1792]{1,0:T(8,128)(2,1)S(1)} %get-tuple-element.46), channel_id=1, source_target_pairs={{0,12},{4,8},{8,4},{12,0},{1,13},{5,9},{9,5},{13,1},{2,14},{6,10},... | collective-permute-start | bytes 172040 | tf_op jit(solution)/shard_map/columns_over_ctx/ppermute | solution.py:38
  78.7 4.5 %collective-permute-start.19 = (bf16[16,1792]{1,0:T(8,128)(2,1)S(1)}, bf16[16,1792]{1,0:T(8,128)(2,1)S(1)}, u32[]{:S(2)}, u32[]{:S(2)}) collective-permute-start(bf16[16,1792]{1,0:T(8,128)(2,1)S(1)} %get-tuple-element.52), channel_id=1, source_target_pairs={{0,4},{4,0},{8,12},{12,8},{1,5},{5,1},{9,13},{13,9},{2,6},{6,2},{1... | collective-permute-start | bytes 172040 | tf_op jit(solution)/shard_map/columns_over_ctx/ppermute | solution.py:38
  79.1 5.2 %collective-permute-start.20 = (bf16[16,1792]{1,0:T(8,128)(2,1)S(1)}, bf16[16,1792]{1,0:T(8,128)(2,1)S(1)}, u32[]{:S(2)}, u32[]{:S(2)}) collective-permute-start(bf16[16,1792]{1,0:T(8,128)(2,1)S(1)} %get-tuple-element.53), channel_id=1, source_target_pairs={{0,8},{4,12},{8,0},{12,4},{1,9},{5,13},{9,1},{13,5},{2,10},{6,14},... | collective-permute-start | bytes 172040 | tf_op jit(solution)/shard_map/columns_over_ctx/ppermute | solution.py:38
  81.1 6.0 %collective-permute-start.21 = (bf16[16,1792]{1,0:T(8,128)(2,1)S(1)}, bf16[16,1792]{1,0:T(8,128)(2,1)S(1)}, u32[]{:S(2)}, u32[]{:S(2)}) collective-permute-start(bf16[16,1792]{1,0:T(8,128)(2,1)S(1)} %get-tuple-element.54), channel_id=1, source_target_pairs={{0,12},{4,8},{8,4},{12,0},{1,13},{5,9},{9,5},{13,1},{2,14},{6,10},... | collective-permute-start | bytes 172040 | tf_op jit(solution)/shard_map/columns_over_ctx/ppermute | solution.py:38

commit v8 on v7

--- a/solution.py
+++ b/solution.py
@@ -293,59 +293,50 @@
     return out[0], out[1:]
 
 
-def x_sum_kernel(count, total_ref, *refs):
-    received, block_refs = refs[:count], refs[count:]
+def x_sum_kernel(total_ref, *refs):
+    received, out_ref = refs[:-1], refs[-1]
     total = total_ref[...]
     for ref in received:
         total = total + ref[...].astype(jnp.float32)
-    rows = block_refs[0].shape[0]
-    for index, block_ref in enumerate(block_refs):
-        block_ref[...] = total[index * rows : (index + 1) * rows].astype(jnp.bfloat16)
+    n_ctx, rows, columns = out_ref.shape
+    ctx = lax.axis_index("ctx")
+    for offset in range(n_ctx):
+        part = total[offset * rows : (offset + 1) * rows]
+        out_ref[ctx ^ offset] = part.astype(jnp.bfloat16)
 
 
 def x_sum(total, received, n_ctx):
     rows, columns = total.shape
-    block = jax.ShapeDtypeStruct((rows // n_ctx, columns), jnp.bfloat16)
     return pl.pallas_call(
-        functools.partial(x_sum_kernel, len(received)),
-        out_shape=[block] * n_ctx,
+        x_sum_kernel,
+        out_shape=jax.ShapeDtypeStruct((n_ctx, rows // n_ctx, columns), jnp.bfloat16),
         in_specs=[IN_VMEM] * (1 + len(received)),
-        out_specs=[IN_VMEM] * n_ctx,
+        out_specs=IN_VMEM,
         compiler_params=params(4),
         cost_estimate=SHORT,
     )(total, *received)
 
 
-def place_kernel(n_ctx, *refs):
-    blocks, out_ref = refs[:-1], refs[-1]
-    ctx = lax.axis_index("ctx")
-    width = blocks[0].shape[1]
-    for offset in range(n_ctx):
-        parts = [block[...].astype(jnp.float32) for block in blocks[offset::n_ctx]]
-        column = pl.multiple_of((ctx ^ offset) * width, 128)
-        out_ref[:, pl.ds(column, width)] = jnp.concatenate(parts, axis=0).astype(jnp.bfloat16)
-
-
-def place_columns(results, n_ctx):
-    width = results[0][0].shape[1]
-    total = sum(result[0].shape[0] for result in results)
-    if width % 128:
-        ctx = lax.axis_index("ctx")
-        out = jnp.zeros((total, n_ctx * width), jnp.bfloat16)
-        for offset in range(n_ctx):
-            block = jnp.concatenate([result[offset] for result in results], axis=0)
-            out = lax.dynamic_update_slice(out, block, (0, (ctx ^ offset) * width))
-        return out
-    blocks = [block for result in results for block in result]
+def place_kernel(*refs):
+    parts, out_ref = refs[:-1], refs[-1]
+    width = parts[0].shape[2]
+    for index in range(parts[0].shape[0]):
+        rows = jnp.concatenate([part[index].astype(jnp.float32) for part in parts], axis=0)
+        out_ref[:, index * width : (index + 1) * width] = rows.astype(jnp.bfloat16)
+
+
+def place_columns(parts):
+    n_ctx, rows, width = parts[0].shape
+    shape = (rows * len(parts), n_ctx * width)
     return pl.pallas_call(
-        functools.partial(place_kernel, n_ctx),
+        place_kernel,
         grid=(1,),
-        out_shape=jax.ShapeDtypeStruct((total, n_ctx * width), jnp.bfloat16),
-        in_specs=[IN_VMEM] * len(blocks),
-        out_specs=pl.BlockSpec((total, n_ctx * width), lambda i: (0, 0)),
+        out_shape=jax.ShapeDtypeStruct(shape, jnp.bfloat16),
+        in_specs=[IN_VMEM] * len(parts),
+        out_specs=pl.BlockSpec(shape, lambda i: (0, 0)),
         compiler_params=params(4),
         cost_estimate=SHORT,
-    )(*blocks)
+    )(*parts)
 
 
 def shards(n_ctx, n_head, queries, kv_rows, w_kv_up, w_out, stretch_order, prefix_len):
@@ -397,10 +388,9 @@
             ]
             total = x_sum(total, crossed, n_ctx)
         with jax.named_scope("columns_over_ctx"):
-            blocks = [total[0]] + [exchange(total[d], "ctx", n_ctx, d) for d in range(1, n_ctx)]
-        results.append(blocks)
+            results.append(lax.all_to_all(total, "ctx", 0, 0))
     with jax.named_scope("output"):
-        return place_columns(results, n_ctx)
+        return place_columns(results)
 
 
 def solution(mesh):

time: 88.1 us -> 94.8 us (1.076)
  blocking collectives: 0 us -> 11.5 us
  starting transfers between devices: 24.2 us -> 18.7 us
    all_to_all x0 -> x1, blocking collectives: none -> 11.5 us  [shards(): results.append(lax.all_to_all(total, 'ctx', 0, 0))]
    ppermute x22 -> x16, starting transfers between devices: 24.2 us -> 15.3 us  [exchange(): return lax.ppermute(array, axis, [(i, i ^ bit) for i in range(size)])]
    all_to_all x0 -> x1, starting transfers between devices: none -> 3.39 us  [shards(): results.append(lax.all_to_all(total, 'ctx', 0, 0))]
    ppermute x22 -> x16, waiting for transfers between devices: 40.5 us -> 39.6 us  [exchange(): return lax.ppermute(array, axis, [(i, i ^ bit) for i in range(size)])]
  transfers between devices with their start and end apart: 22 -> 17, of which waited for: 12 -> 10; matrix products, arithmetic and copies ran while one was open for 0% -> 0% of each run, Pallas kernels for 16% -> 15%
where the time goes in v8:
time: 94.8 us; the launch traced here: 94.5 us
  waiting for transfers between devices  40.5 us (43%)
  Pallas kernels  19.3 us (20%)
  starting transfers between devices  18.7 us (20%)
  blocking collectives  11.5 us (12%)
  local copies, waits for them, and re-layouts  2.75 us (3%)
  other arithmetic  1 us (1%)
    ppermute x16, waiting for transfers between devices, exchange(): return lax.ppermute(array, axis, [(i, i ^ bit) for i in range(size)])  39.6 us
    ppermute x16, starting transfers between devices, exchange(): return lax.ppermute(array, axis, [(i, i ^ bit) for i in range(size)])  15.3 us
    all_to_all x1, blocking collectives, shards(): results.append(lax.all_to_all(total, 'ctx', 0, 0))  11.5 us
    pallas_call x2, Pallas kernels, attention(): pl.pallas_call(functools.partial(attention_kernel, 0 if gathered else len...  7.69 us
    pallas_call x1, Pallas kernels, load(): pl.pallas_call(functools.partial(load_kernel, owners, pieces, cache_rows)...  5.66 us
    pallas_call x2, Pallas kernels, product(): pl.pallas_call(functools.partial(product_kernel, count, n_x, len(after)),...  4.2 us
    all_to_all x1, starting transfers between devices, shards(): results.append(lax.all_to_all(total, 'ctx', 0, 0))  3.39 us
    unnamed x10, local copies, waits for them, and re-layouts  2.75 us
  transfers between devices with their start and end apart: 17, of which 10 were waited for; matrix products, arithmetic and copies ran while one was open for 0% of the time, Pallas kernels for 15%

profile of v8, /device:TPU:0, one launch (start us, length us, event | category | flops | bytes accessed | tf_op | source)
XLA Modules:
  0.0 94.5 jit_solution(2530241573280418736)
XLA Ops:
  0.0 1.0 %slice_select_fusion = bf16[576,128]{1,0:T(8,128)(2,1)S(1)} fusion(bf16[576,256]{1,0:T(8,128)(2,1)} %bitcast.3, pred[]{:T(512)S(6)} %eq.5), kind=kLoop, calls=%fused_computation | loop fusion | flops 73728 | bytes 442369 | tf_op jit(solution)/shard_map/keys_over_ctx/jit(_where)/select_n | solution.py:353
  1.0 3.1 %collective-permute-start = (bf16[576,128]{1,0:T(8,128)(2,1)S(1)}, bf16[576,128]{1,0:T(8,128)(2,1)S(1)}, u32[]{:S(2)}, u32[]{:S(2)}) collective-permute-start(bf16[576,128]{1,0:T(8,128)(2,1)S(1)} %slice_select_fusion), channel_id=1, source_target_pairs={{0,4},{4,0},{8,12},{12,8},{1,5},{5,1},{9,13},{13,9},{2,6},{6,2},{1... | collective-permute-start | bytes 442376 | tf_op jit(solution)/shard_map/keys_over_ctx/ppermute | solution.py:38
  4.1 2.6 %collective-permute-start.1 = (bf16[576,128]{1,0:T(8,128)(2,1)S(1)}, bf16[576,128]{1,0:T(8,128)(2,1)S(1)}, u32[]{:S(2)}, u32[]{:S(2)}) collective-permute-start(bf16[576,128]{1,0:T(8,128)(2,1)S(1)} %slice_select_fusion), channel_id=1, source_target_pairs={{0,8},{4,12},{8,0},{12,4},{1,9},{5,13},{9,1},{13,5},{2,10},{6,14},... | collective-permute-start | bytes 442376 | tf_op jit(solution)/shard_map/keys_over_ctx/ppermute | solution.py:38
  6.7 0.0 collective-permute-start.2
  7.3 0.0 copy-start
  7.3 1.0 %copy-done = bf16[256,576]{0,1:T(8,128)(2,1)S(1)} copy-done((bf16[256,576]{0,1:T(8,128)(2,1)S(1)}, bf16[256,576]{0,1:T(8,128)(2,1)}, u32[]{:S(2)}) %copy-start) | copy-done | bytes 294936
  8.3 0.0 copy-start.1
  8.3 1.1 %copy-done.1 = bf16[128,3072]{1,0:T(8,128)(2,1)S(1)} copy-done((bf16[128,3072]{1,0:T(8,128)(2,1)S(1)}, bf16[128,3072]{1,0:T(8,128)(2,1)}, u32[]{:S(2)}) %copy-start.1) | copy-done | bytes 786456
  9.4 0.0 copy-start.2
  9.4 0.7 copy-done.2
  10.1 0.0 slice-start
  10.1 5.7 %load.1 = (bf16[16,64,576]{2,1,0:T(8,128)(2,1)S(1)}, bf16[16,64,576]{2,1,0:T(8,128)(2,1)S(1)}, f32[64,1024]{1,0:T(8,128)S(1)}, f32[64,1024]{1,0:T(8,128)S(1)}, b...) custom-call(s32[4]{0:T(128)S(1)} %copy-done.2, s32[1]{0:T(128)S(6)} %copy.19.prefix_ref, ...), custom_call_target="tpu_custom_call" | custom-call | flops 1024 | bytes 1024 | tf_op jit(solution)/shard_map/load/pallas_call | solution.py:131
  15.8 0.0 collective-permute-done.refs_0_
  15.8 0.1 collective-permute-start.3
  15.9 2.2 %collective-permute-done.1.refs_0_ = bf16[576,128]{1,0:T(8,128)(2,1)S(1)} collective-permute-done((bf16[576,128]{1,0:T(8,128)(2,1)S(1)}, bf16[576,128]{1,0:T(8,128)(2,1)S(1)}, u32[]{:S(2)}, u32[]{:S(2)}) %collective-permute-start.1) | collective-permute-done | bytes 147488 | tf_op jit(solution)/shard_map/keys_over_ctx/ppermute | solution.py:38
  18.1 0.0 collective-permute-start.4
  18.1 0.0 collective-permute-done.2.refs_0_
  18.1 0.5 collective-permute-start.5
  18.6 0.0 collective-permute-done.3.refs_4_
  18.6 0.9 collective-permute-done.4.refs_5_
  19.5 0.2 collective-permute-done.5.refs_6_
  19.7 0.0 slice-start.1
  19.7 3.9 %attention.2 = (bf16[64,2048]{1,0:T(8,128)(2,1)S(1)}, bf16[576,1024]{1,0:T(8,128)(2,1)S(1)}, bf16[1024,512]{1,0:T(8,128)(2,1)S(1)}) custom-call(bf16[16,64,576]{2,1,0:T(8,128)(2,1)S(1)} %get-tuple-element.22.q_ref, f32[64,1024]{1,0:T(8,128)S(1)} %get-tuple-element.23.bias_ref, bf16[16,512,128]{2,1,0:T(8,128)(2,1)S(1)} %get-tuple-element.24.value_ref, ...), custom_call_target="tpu_custom_call" | custom-call | flops 1024 | bytes 1024 | tf_op jit(solution)/shard_map/attention/pallas_call | solution.py:226
  23.6 3.2 %collective-permute-start.7 = (bf16[64,2048]{1,0:T(8,128)(2,1)S(1)}, bf16[64,2048]{1,0:T(8,128)(2,1)S(1)}, u32[]{:S(2)}, u32[]{:S(2)}) collective-permute-start(bf16[64,2048]{1,0:T(8,128)(2,1)S(1)} %get-tuple-element.26.refs_0_), channel_id=1, source_target_pairs={{0,8},{4,12},{8,0},{12,4},{1,9},{5,13},{9,1},{13,5},{2,10},{6,14},... | collective-permute-start | bytes 786440 | tf_op jit(solution)/shard_map/attended_over_ctx/ppermute | solution.py:38
  26.7 0.0 collective-permute-start.6
  26.7 3.8 %attention.3.refs_1_.refs_4_.refs_0_ = bf16[64,2048]{1,0:T(8,128)(2,1)S(1)} custom-call(bf16[16,64,576]{2,1,0:T(8,128)(2,1)S(1)} %get-tuple-element.27.q_ref, f32[64,1024]{1,0:T(8,128)S(1)} %get-tuple-element.28.bias_ref, bf16[16,512,128]{2,1,0:T(8,128)(2,1)S(1)} %get-tuple-element.24.value_ref, bf16[576,1024]{1,0:T(8,128)(2,1)S(1)} %get-tuple-element.29.refs_0_, ...), custom_call_target="tpu_custom_call" | custom-call | flops 1024 | bytes 1024 | tf_op jit(solution)/shard_map/attention/pallas_call | solution.py:226
  30.5 8.5 %collective-permute-done.7.refs_0_ = bf16[64,2048]{1,0:T(8,128)(2,1)S(1)} collective-permute-done((bf16[64,2048]{1,0:T(8,128)(2,1)S(1)}, bf16[64,2048]{1,0:T(8,128)(2,1)S(1)}, u32[]{:S(2)}, u32[]{:S(2)}) %collective-permute-start.7) | collective-permute-done | bytes 262176 | tf_op jit(solution)/shard_map/attended_over_ctx/ppermute | solution.py:38
  39.1 0.0 collective-permute-start.8
  39.1 2.4 %collective-permute-start.10 = (bf16[64,2048]{1,0:T(8,128)(2,1)S(1)}, bf16[64,2048]{1,0:T(8,128)(2,1)S(1)}, u32[]{:S(2)}, u32[]{:S(2)}) collective-permute-start(bf16[64,2048]{1,0:T(8,128)(2,1)S(1)} %attention.3.refs_1_.refs_4_.refs_0_), channel_id=1, source_target_pairs={{0,8},{4,12},{8,0},{12,4},{1,9},{5,13},{9,1},{13,5},{2,10},{6,14},... | collective-permute-start | bytes 786440 | tf_op jit(solution)/shard_map/attended_over_ctx/ppermute | solution.py:38
  41.5 0.0 collective-permute-start.9
  41.5 0.0 collective-permute-done.6.refs_1_
  41.5 12.0 %collective-permute-done.8.refs_3_ = bf16[64,2048]{1,0:T(8,128)(2,1)S(1)} collective-permute-done((bf16[64,2048]{1,0:T(8,128)(2,1)S(1)}, bf16[64,2048]{1,0:T(8,128)(2,1)S(1)}, u32[]{:S(2)}, u32[]{:S(2)}) %collective-permute-start.8) | collective-permute-done | bytes 262176 | tf_op jit(solution)/shard_map/attended_over_ctx/ppermute | solution.py:38
  53.5 0.0 slice-done
  53.5 0.0 slice-done.1
  53.5 2.1 %out_product.2 = (bf16[2,64,1792]{2,1,0:T(8,128)(2,1)S(1)}, f32[2,64,1792]{2,1,0:T(8,128)S(1)}) custom-call(bf16[2048,1792]{1,0:T(8,128)(2,1)S(1)} %bitcast.2, bf16[64,2048]{1,0:T(8,128)(2,1)S(1)} %get-tuple-element.26.refs_0_, bf16[64,2048]{1,0:T(8,128)(2,1)S(1)} %collective-permute-done.6.refs_1_, bf16[64,2048]{1,0:T(8,128)(2,1)S(1)} %attended_over_ctx.1.refs_2_, ...), custom_call_target="tpu_custom_call" | custom-call | flops 1024 | bytes 1024 | tf_op jit(solution)/shard_map/out_product/pallas_call | solution.py:260
  55.6 0.0 collective-permute-done.10.refs_2_
  55.7 2.4 %collective-permute-done.9.refs_1_ = bf16[64,2048]{1,0:T(8,128)(2,1)S(1)} collective-permute-done((bf16[64,2048]{1,0:T(8,128)(2,1)S(1)}, bf16[64,2048]{1,0:T(8,128)(2,1)S(1)}, u32[]{:S(2)}, u32[]{:S(2)}) %collective-permute-start.9) | collective-permute-done | bytes 262176 | tf_op jit(solution)/shard_map/attended_over_ctx/ppermute | solution.py:38
  58.1 0.0 collective-permute-start.11
  58.1 0.3 collective-permute-start.13
  58.4 1.5 %collective-permute-done.11.received_ref = bf16[2,64,1792]{2,1,0:T(8,128)(2,1)S(1)} collective-permute-done((bf16[2,64,1792]{2,1,0:T(8,128)(2,1)S(1)}, bf16[2,64,1792]{2,1,0:T(8,128)(2,1)S(1)}, u32[]{:S(2)}, u32[]{:S(2)}) %collective-permute-start.11) | collective-permute-done | bytes 458784 | tf_op jit(solution)/shard_map/sum_over_cores/ppermute | solution.py:38
  59.9 0.1 sum_over_cores.5
  60.0 1.5 %collective-permute-start.12 = (bf16[64,1792]{1,0:T(8,128)(2,1)S(1)}, bf16[64,1792]{1,0:T(8,128)(2,1)S(1)}, u32[]{:S(2)}, u32[]{:S(2)}) collective-permute-start(bf16[64,1792]{1,0:T(8,128)(2,1)S(1)} %get-tuple-element.34), channel_id=1, source_target_pairs={{0,2},{1,3},{2,0},{3,1},{4,6},{5,7},{6,4},{7,5},{8,10},{9,11},{10,... | collective-permute-start | bytes 688136 | tf_op jit(solution)/shard_map/sum_over_x/ppermute | solution.py:38
  61.5 5.3 %collective-permute-done.13.refs_3_ = bf16[64,2048]{1,0:T(8,128)(2,1)S(1)} collective-permute-done((bf16[64,2048]{1,0:T(8,128)(2,1)S(1)}, bf16[64,2048]{1,0:T(8,128)(2,1)S(1)}, u32[]{:S(2)}, u32[]{:S(2)}) %collective-permute-start.13) | collective-permute-done | bytes 262176 | tf_op jit(solution)/shard_map/attended_over_ctx/ppermute | solution.py:38
  66.8 2.1 %out_product.3 = (bf16[2,64,1792]{2,1,0:T(8,128)(2,1)S(1)}, f32[2,64,1792]{2,1,0:T(8,128)S(1)}) custom-call(bf16[2048,1792]{1,0:T(8,128)(2,1)S(1)} %bitcast.2, bf16[64,2048]{1,0:T(8,128)(2,1)S(1)} %attention.3.refs_1_.refs_4_.refs_0_, bf16[64,2048]{1,0:T(8,128)(2,1)S(1)} %collective-permute-done.9.refs_1_, ...), custom_call_target="tpu_custom_call" | custom-call | flops 1024 | bytes 1024 | tf_op jit(solution)/shard_map/out_product/pallas_call | solution.py:260
  68.9 0.0 collective-permute-done.12.refs_0_.refs_1_
  69.0 0.1 collective-permute-start.14
  69.0 0.7 sum_over_x.2
  69.8 3.4 %all-to-all-start = ((bf16[4,16,1792]{2,1,0:T(8,128)(2,1)}), bf16[4,16,1792]{2,1,0:T(8,128)(2,1)S(1)}, u32[]{:S(2)}, u32[]{:S(2)}) async-start(bf16[4,16,1792]{2,1,0:T(8,128)(2,1)} %sum_over_x.2), calls=%async_computation | async-start | bytes 458752 | tf_op jit(solution)/shard_map/columns_over_ctx/all_to_all | solution.py:391
  73.2 0.0 collective-permute-done.14.received_ref
  73.2 0.1 sum_over_cores.7
  73.3 1.5 %collective-permute-start.15 = (bf16[64,1792]{1,0:T(8,128)(2,1)S(1)}, bf16[64,1792]{1,0:T(8,128)(2,1)S(1)}, u32[]{:S(2)}, u32[]{:S(2)}) collective-permute-start(bf16[64,1792]{1,0:T(8,128)(2,1)S(1)} %get-tuple-element.38), channel_id=1, source_target_pairs={{0,2},{1,3},{2,0},{3,1},{4,6},{5,7},{6,4},{7,5},{8,10},{9,11},{10,... | collective-permute-start | bytes 688136 | tf_op jit(solution)/shard_map/sum_over_x/ppermute | solution.py:38
  74.8 6.5 %collective-permute-done.15.refs_0_ = bf16[64,1792]{1,0:T(8,128)(2,1)S(1)} collective-permute-done((bf16[64,1792]{1,0:T(8,128)(2,1)S(1)}, bf16[64,1792]{1,0:T(8,128)(2,1)S(1)}, u32[]{:S(2)}, u32[]{:S(2)}) %collective-permute-start.15) | collective-permute-done | bytes 229408 | tf_op jit(solution)/shard_map/sum_over_x/ppermute | solution.py:38
  81.4 0.8 all-to-all-done.refs_0_
  82.2 11.5 %all_to_all.10.refs_1_ = bf16[4,16,1792]{2,1,0:T(8,128)(2,1)S(1)} all-to-all(bf16[4,16,1792]{2,1,0:T(8,128)(2,1)S(1)} %sum_over_x.3), channel_id=1, replica_groups=mesh['groups'=2,'ctx'=4,'head'=4] {'ctx'}, dimensions={0} | all-to-all | bytes 458752 | tf_op jit(solution)/shard_map/columns_over_ctx/all_to_all | solution.py:391
  93.7 0.8 output.1
  (8 shorter events, 0.0 us)
Async XLA Ops:
  1.0 14.8 %collective-permute-start = (bf16[576,128]{1,0:T(8,128)(2,1)S(1)}, bf16[576,128]{1,0:T(8,128)(2,1)S(1)}, u32[]{:S(2)}, u32[]{:S(2)}) collective-permute-start(bf16[576,128]{1,0:T(8,128)(2,1)S(1)} %slice_select_fusion), channel_id=1, source_target_pairs={{0,4},{4,0},{8,12},{12,8},{1,5},{5,1},{9,13},{13,9},{2,6},{6,2},{1... | collective-permute-start | bytes 442376 | tf_op jit(solution)/shard_map/keys_over_ctx/ppermute | solution.py:38
  4.1 14.0 %collective-permute-start.1 = (bf16[576,128]{1,0:T(8,128)(2,1)S(1)}, bf16[576,128]{1,0:T(8,128)(2,1)S(1)}, u32[]{:S(2)}, u32[]{:S(2)}) collective-permute-start(bf16[576,128]{1,0:T(8,128)(2,1)S(1)} %slice_select_fusion), channel_id=1, source_target_pairs={{0,8},{4,12},{8,0},{12,4},{1,9},{5,13},{9,1},{13,5},{2,10},{6,14},... | collective-permute-start | bytes 442376 | tf_op jit(solution)/shard_map/keys_over_ctx/ppermute | solution.py:38
  6.7 11.4 %collective-permute-start.2 = (bf16[576,128]{1,0:T(8,128)(2,1)S(1)}, bf16[576,128]{1,0:T(8,128)(2,1)S(1)}, u32[]{:S(2)}, u32[]{:S(2)}) collective-permute-start(bf16[576,128]{1,0:T(8,128)(2,1)S(1)} %slice_select_fusion), channel_id=1, source_target_pairs={{0,12},{4,8},{8,4},{12,0},{1,13},{5,9},{9,5},{13,1},{2,14},{6,10},... | collective-permute-start | bytes 442376 | tf_op jit(solution)/shard_map/keys_over_ctx/ppermute | solution.py:38
  7.3 1.0 %copy-start = (bf16[256,576]{0,1:T(8,128)(2,1)S(1)}, bf16[256,576]{0,1:T(8,128)(2,1)}, u32[]{:S(2)}) copy-start(bf16[256,576]{0,1:T(8,128)(2,1)} %param.7) | copy-start | bytes 884740
  8.3 1.1 %copy-start.1 = (bf16[128,3072]{1,0:T(8,128)(2,1)S(1)}, bf16[128,3072]{1,0:T(8,128)(2,1)}, u32[]{:S(2)}) copy-start(bf16[128,3072]{1,0:T(8,128)(2,1)} %q_hbm.1) | copy-start | bytes 2359300
  9.4 0.7 copy-start.2
  10.1 43.4 %slice-start = ((s8[7340032]{0:T(1024)(128)(4,1)}), s8[3145728]{0:T(1024)(128)(4,1)S(1)}, s32[]{:S(2)}) async-start(s8[7340032]{0:T(1024)(128)(4,1)} %bitcast.1), calls=%async_computation.2 | async-start | bytes 6291456
  15.8 2.8 %collective-permute-start.3 = (bf16[576,128]{1,0:T(8,128)(2,1)S(1)}, bf16[576,128]{1,0:T(8,128)(2,1)S(1)}, u32[]{:S(2)}, u32[]{:S(2)}) collective-permute-start(bf16[576,128]{1,0:T(8,128)(2,1)S(1)} %keys_over_cores.3.refs_1_), channel_id=1, source_target_pairs={{0,1},{1,0},{2,3},{3,2},{4,5},{5,4},{6,7},{7,6},{8,9},{9,8},{10,11... | collective-permute-start | bytes 442376 | tf_op jit(solution)/shard_map/keys_over_cores/ppermute | solution.py:38
  18.1 1.4 %collective-permute-start.4 = (bf16[576,128]{1,0:T(8,128)(2,1)S(1)}, bf16[576,128]{1,0:T(8,128)(2,1)S(1)}, u32[]{:S(2)}, u32[]{:S(2)}) collective-permute-start(bf16[576,128]{1,0:T(8,128)(2,1)S(1)} %keys_over_cores.4.refs_2_), channel_id=1, source_target_pairs={{0,1},{1,0},{2,3},{3,2},{4,5},{5,4},{6,7},{7,6},{8,9},{9,8},{10,11... | collective-permute-start | bytes 442376 | tf_op jit(solution)/shard_map/keys_over_cores/ppermute | solution.py:38
  18.1 1.6 %collective-permute-start.5 = (bf16[576,128]{1,0:T(8,128)(2,1)S(1)}, bf16[576,128]{1,0:T(8,128)(2,1)S(1)}, u32[]{:S(2)}, u32[]{:S(2)}) collective-permute-start(bf16[576,128]{1,0:T(8,128)(2,1)S(1)} %keys_over_cores.5.refs_3_), channel_id=1, source_target_pairs={{0,1},{1,0},{2,3},{3,2},{4,5},{5,4},{6,7},{7,6},{8,9},{9,8},{10,11... | collective-permute-start | bytes 442376 | tf_op jit(solution)/shard_map/keys_over_cores/ppermute | solution.py:38
  19.7 33.9 %slice-start.1 = ((s8[7340032]{0:T(1024)(128)(4,1)}), s8[4194304]{0:T(1024)(128)(4,1)S(1)}, s32[]{:S(2)}) async-start(s8[7340032]{0:T(1024)(128)(4,1)} %bitcast.1), calls=%async_computation.3 | async-start | bytes 8388608
  23.6 15.5 %collective-permute-start.7 = (bf16[64,2048]{1,0:T(8,128)(2,1)S(1)}, bf16[64,2048]{1,0:T(8,128)(2,1)S(1)}, u32[]{:S(2)}, u32[]{:S(2)}) collective-permute-start(bf16[64,2048]{1,0:T(8,128)(2,1)S(1)} %get-tuple-element.26.refs_0_), channel_id=1, source_target_pairs={{0,8},{4,12},{8,0},{12,4},{1,9},{5,13},{9,1},{13,5},{2,10},{6,14},... | collective-permute-start | bytes 786440 | tf_op jit(solution)/shard_map/attended_over_ctx/ppermute | solution.py:38
  26.7 14.8 %collective-permute-start.6 = (bf16[64,2048]{1,0:T(8,128)(2,1)S(1)}, bf16[64,2048]{1,0:T(8,128)(2,1)S(1)}, u32[]{:S(2)}, u32[]{:S(2)}) collective-permute-start(bf16[64,2048]{1,0:T(8,128)(2,1)S(1)} %get-tuple-element.26.refs_0_), channel_id=1, source_target_pairs={{0,4},{4,0},{8,12},{12,8},{1,5},{5,1},{9,13},{13,9},{2,6},{6,2},{1... | collective-permute-start | bytes 786440 | tf_op jit(solution)/shard_map/attended_over_ctx/ppermute | solution.py:38
  39.1 14.5 %collective-permute-start.8 = (bf16[64,2048]{1,0:T(8,128)(2,1)S(1)}, bf16[64,2048]{1,0:T(8,128)(2,1)S(1)}, u32[]{:S(2)}, u32[]{:S(2)}) collective-permute-start(bf16[64,2048]{1,0:T(8,128)(2,1)S(1)} %attended_over_ctx.1.refs_2_), channel_id=1, source_target_pairs={{0,4},{4,0},{8,12},{12,8},{1,5},{5,1},{9,13},{13,9},{2,6},{6,2},{1... | collective-permute-start | bytes 786440 | tf_op jit(solution)/shard_map/attended_over_ctx/ppermute | solution.py:38
  39.1 16.6 %collective-permute-start.10 = (bf16[64,2048]{1,0:T(8,128)(2,1)S(1)}, bf16[64,2048]{1,0:T(8,128)(2,1)S(1)}, u32[]{:S(2)}, u32[]{:S(2)}) collective-permute-start(bf16[64,2048]{1,0:T(8,128)(2,1)S(1)} %attention.3.refs_1_.refs_4_.refs_0_), channel_id=1, source_target_pairs={{0,8},{4,12},{8,0},{12,4},{1,9},{5,13},{9,1},{13,5},{2,10},{6,14},... | collective-permute-start | bytes 786440 | tf_op jit(solution)/shard_map/attended_over_ctx/ppermute | solution.py:38
  41.5 16.6 %collective-permute-start.9 = (bf16[64,2048]{1,0:T(8,128)(2,1)S(1)}, bf16[64,2048]{1,0:T(8,128)(2,1)S(1)}, u32[]{:S(2)}, u32[]{:S(2)}) collective-permute-start(bf16[64,2048]{1,0:T(8,128)(2,1)S(1)} %attention.3.refs_1_.refs_4_.refs_0_), channel_id=1, source_target_pairs={{0,4},{4,0},{8,12},{12,8},{1,5},{5,1},{9,13},{13,9},{2,6},{6,2},{1... | collective-permute-start | bytes 786440 | tf_op jit(solution)/shard_map/attended_over_ctx/ppermute | solution.py:38
  58.1 1.8 %collective-permute-start.11 = (bf16[2,64,1792]{2,1,0:T(8,128)(2,1)S(1)}, bf16[2,64,1792]{2,1,0:T(8,128)(2,1)S(1)}, u32[]{:S(2)}, u32[]{:S(2)}) collective-permute-start(bf16[2,64,1792]{2,1,0:T(8,128)(2,1)S(1)} %sum_over_cores.4), channel_id=1, source_target_pairs={{0,1},{1,0},{2,3},{3,2},{4,5},{5,4},{6,7},{7,6},{8,9},{9,8},{10,11... | collective-permute-start | bytes 1376264 | tf_op jit(solution)/shard_map/sum_over_cores/ppermute | solution.py:38
  58.1 8.7 %collective-permute-start.13 = (bf16[64,2048]{1,0:T(8,128)(2,1)S(1)}, bf16[64,2048]{1,0:T(8,128)(2,1)S(1)}, u32[]{:S(2)}, u32[]{:S(2)}) collective-permute-start(bf16[64,2048]{1,0:T(8,128)(2,1)S(1)} %collective-permute-done.10.refs_2_), channel_id=1, source_target_pairs={{0,4},{4,0},{8,12},{12,8},{1,5},{5,1},{9,13},{13,9},{2,6},{6,2},{1... | collective-permute-start | bytes 786440 | tf_op jit(solution)/shard_map/attended_over_ctx/ppermute | solution.py:38
  60.0 8.9 %collective-permute-start.12 = (bf16[64,1792]{1,0:T(8,128)(2,1)S(1)}, bf16[64,1792]{1,0:T(8,128)(2,1)S(1)}, u32[]{:S(2)}, u32[]{:S(2)}) collective-permute-start(bf16[64,1792]{1,0:T(8,128)(2,1)S(1)} %get-tuple-element.34), channel_id=1, source_target_pairs={{0,2},{1,3},{2,0},{3,1},{4,6},{5,7},{6,4},{7,5},{8,10},{9,11},{10,... | collective-permute-start | bytes 688136 | tf_op jit(solution)/shard_map/sum_over_x/ppermute | solution.py:38
  69.0 4.2 %collective-permute-start.14 = (bf16[2,64,1792]{2,1,0:T(8,128)(2,1)S(1)}, bf16[2,64,1792]{2,1,0:T(8,128)(2,1)S(1)}, u32[]{:S(2)}, u32[]{:S(2)}) collective-permute-start(bf16[2,64,1792]{2,1,0:T(8,128)(2,1)S(1)} %sum_over_cores.6), channel_id=1, source_target_pairs={{0,1},{1,0},{2,3},{3,2},{4,5},{5,4},{6,7},{7,6},{8,9},{9,8},{10,11... | collective-permute-start | bytes 1376264 | tf_op jit(solution)/shard_map/sum_over_cores/ppermute | solution.py:38
  69.8 12.5 %all-to-all-start = ((bf16[4,16,1792]{2,1,0:T(8,128)(2,1)}), bf16[4,16,1792]{2,1,0:T(8,128)(2,1)S(1)}, u32[]{:S(2)}, u32[]{:S(2)}) async-start(bf16[4,16,1792]{2,1,0:T(8,128)(2,1)} %sum_over_x.2), calls=%async_computation | async-start | bytes 458752 | tf_op jit(solution)/shard_map/columns_over_ctx/all_to_all | solution.py:391
  73.3 8.1 %collective-permute-start.15 = (bf16[64,1792]{1,0:T(8,128)(2,1)S(1)}, bf16[64,1792]{1,0:T(8,128)(2,1)S(1)}, u32[]{:S(2)}, u32[]{:S(2)}) collective-permute-start(bf16[64,1792]{1,0:T(8,128)(2,1)S(1)} %get-tuple-element.38), channel_id=1, source_target_pairs={{0,2},{1,3},{2,0},{3,1},{4,6},{5,7},{6,4},{7,5},{8,10},{9,11},{10,... | collective-permute-start | bytes 688136 | tf_op jit(solution)/shard_map/sum_over_x/ppermute | solution.py:38

commit v9 on v7

--- a/solution.py
+++ b/solution.py
@@ -303,14 +303,14 @@
         block_ref[...] = total[index * rows : (index + 1) * rows].astype(jnp.bfloat16)
 
 
-def x_sum(total, received, n_ctx):
+def x_sum(total, received, count):
     rows, columns = total.shape
-    block = jax.ShapeDtypeStruct((rows // n_ctx, columns), jnp.bfloat16)
+    block = jax.ShapeDtypeStruct((rows // count, columns), jnp.bfloat16)
     return pl.pallas_call(
         functools.partial(x_sum_kernel, len(received)),
-        out_shape=[block] * n_ctx,
+        out_shape=[block] * count,
         in_specs=[IN_VMEM] * (1 + len(received)),
-        out_specs=[IN_VMEM] * n_ctx,
+        out_specs=[IN_VMEM] * count,
         compiler_params=params(4),
         cost_estimate=SHORT,
     )(total, *received)
@@ -378,27 +378,35 @@
             gather_pieces(own, n_ctx, attended[chunk + 1 : chunk + 2])
             for chunk, own in enumerate(attended)
         ]
-    results = []
+    near = [0] + [1 << bit for bit in range(n_ctx.bit_length() - 1)]
+    far = [offset for offset in range(n_ctx) if offset not in near]
+    last = len(pieces) - 1
+    units = [(chunk, list(range(n_ctx))) for chunk in range(last)] + [(last, near), (last, far)]
+    results = [{} for chunk in pieces]
     after = attended[1:]
     crossed = []
-    for chunk in range(len(pieces)):
+    for unit, (chunk, offsets) in enumerate(units):
         with jax.named_scope("out_product"):
-            sent, kept = product(gathered[chunk], w_out, n_x, after)
+            first = after if unit == 0 else []
+            sent, kept = product([gathered[chunk][d] for d in offsets], w_out, n_x, first)
         with jax.named_scope("sum_over_cores"):
-            ahead = list(crossed)
-            if chunk + 1 < len(pieces):
-                ahead += [gathered[chunk + 1][1], gathered[chunk + 1][n_ctx // 2]]
-            sent = tie(sent, ahead)
+            if chunk < last:
+                sent = tie(sent, [gathered[chunk + 1][1], gathered[chunk + 1][n_ctx // 2]])
+            elif offsets is far:
+                sent = tie(sent, [*crossed[0], *after])
             total, sent = core_sum(kept, exchange(sent, "head", n_head, 1))
             after = [total]
         with jax.named_scope("sum_over_x"):
-            crossed = [
-                exchange(array, "head", n_head, 2 * offset) for offset, array in enumerate(sent, 1)
-            ]
-            total = x_sum(total, crossed, n_ctx)
+            if offsets is far:
+                sent = [tie(array, crossed[-1]) for array in sent]
+            crossed.append(
+                [exchange(array, "head", n_head, 2 * d) for d, array in enumerate(sent, 1)]
+            )
+            blocks = x_sum(total, crossed[-1], len(offsets))
         with jax.named_scope("columns_over_ctx"):
-            blocks = [total[0]] + [exchange(total[d], "ctx", n_ctx, d) for d in range(1, n_ctx)]
-        results.append(blocks)
+            for d, block in zip(offsets, blocks):
+                results[chunk][d] = exchange(block, "ctx", n_ctx, d) if d else block
+    results = [[result[d] for d in range(n_ctx)] for result in results]
     with jax.named_scope("output"):
         return place_columns(results, n_ctx)
 

time: 88.1 us -> 87.4 us (level)
  waiting for transfers between devices: 40.5 us -> 37.4 us
  starting transfers between devices: 24.2 us -> 25.7 us
  Pallas kernels: 18.6 us -> 19.5 us
    ppermute x22 -> x24, waiting for transfers between devices: 40.5 us -> 37.4 us  [exchange(): return lax.ppermute(array, axis, [(i, i ^ bit) for i in range(size)])]
    ppermute x22 -> x24, starting transfers between devices: 24.2 us -> 25.7 us  [exchange(): return lax.ppermute(array, axis, [(i, i ^ bit) for i in range(size)])]
    pallas_call x2 -> x3, Pallas kernels: 4.2 us -> 5.1 us  [product(): pl.pallas_call(functools.partial(product_kernel, count, n_x, len(after)),...]
  transfers between devices with their start and end apart: 22 -> 24, of which waited for: 12 -> 12; matrix products, arithmetic and copies ran while one was open for 0% -> 0% of each run, Pallas kernels for 16% -> 17%
where the time goes in v9:
time: 87.4 us; the launch traced here: 87.2 us
  waiting for transfers between devices  37.4 us (43%)
  starting transfers between devices  25.7 us (29%)
  Pallas kernels  19.5 us (22%)
  local copies, waits for them, and re-layouts  2.75 us (3%)
  other arithmetic  1 us (1%)
    ppermute x24, waiting for transfers between devices, exchange(): return lax.ppermute(array, axis, [(i, i ^ bit) for i in range(size)])  37.4 us
    ppermute x24, starting transfers between devices, exchange(): return lax.ppermute(array, axis, [(i, i ^ bit) for i in range(size)])  25.7 us
    pallas_call x2, Pallas kernels, attention(): pl.pallas_call(functools.partial(attention_kernel, 0 if gathered else len...  7.69 us
    pallas_call x1, Pallas kernels, load(): pl.pallas_call(functools.partial(load_kernel, owners, pieces, cache_rows)...  5.66 us
    pallas_call x3, Pallas kernels, product(): pl.pallas_call(functools.partial(product_kernel, count, n_x, len(after)),...  5.1 us
    unnamed x10, local copies, waits for them, and re-layouts  2.75 us
  transfers between devices with their start and end apart: 24, of which 12 were waited for; matrix products, arithmetic and copies ran while one was open for 0% of the time, Pallas kernels for 17%

profile of v9, /device:TPU:0, one launch (start us, length us, event | category | flops | bytes accessed | tf_op | source)
XLA Modules:
  0.0 87.2 jit_solution(4113886680645425555)
XLA Ops:
  0.0 1.0 %slice_select_fusion = bf16[576,128]{1,0:T(8,128)(2,1)S(1)} fusion(bf16[576,256]{1,0:T(8,128)(2,1)} %bitcast.3, pred[]{:T(512)S(6)} %eq.5), kind=kLoop, calls=%fused_computation | loop fusion | flops 73728 | bytes 442369 | tf_op jit(solution)/shard_map/keys_over_ctx/jit(_where)/select_n | solution.py:362
  1.0 3.1 %collective-permute-start = (bf16[576,128]{1,0:T(8,128)(2,1)S(1)}, bf16[576,128]{1,0:T(8,128)(2,1)S(1)}, u32[]{:S(2)}, u32[]{:S(2)}) collective-permute-start(bf16[576,128]{1,0:T(8,128)(2,1)S(1)} %slice_select_fusion), channel_id=1, source_target_pairs={{0,4},{4,0},{8,12},{12,8},{1,5},{5,1},{9,13},{13,9},{2,6},{6,2},{1... | collective-permute-start | bytes 442376 | tf_op jit(solution)/shard_map/keys_over_ctx/ppermute | solution.py:38
  4.1 2.6 %collective-permute-start.1 = (bf16[576,128]{1,0:T(8,128)(2,1)S(1)}, bf16[576,128]{1,0:T(8,128)(2,1)S(1)}, u32[]{:S(2)}, u32[]{:S(2)}) collective-permute-start(bf16[576,128]{1,0:T(8,128)(2,1)S(1)} %slice_select_fusion), channel_id=1, source_target_pairs={{0,8},{4,12},{8,0},{12,4},{1,9},{5,13},{9,1},{13,5},{2,10},{6,14},... | collective-permute-start | bytes 442376 | tf_op jit(solution)/shard_map/keys_over_ctx/ppermute | solution.py:38
  6.7 0.0 collective-permute-start.2
  7.3 0.0 copy-start
  7.3 1.0 %copy-done = bf16[256,576]{0,1:T(8,128)(2,1)S(1)} copy-done((bf16[256,576]{0,1:T(8,128)(2,1)S(1)}, bf16[256,576]{0,1:T(8,128)(2,1)}, u32[]{:S(2)}) %copy-start) | copy-done | bytes 294936
  8.3 1.1 %copy-done.1 = bf16[128,3072]{1,0:T(8,128)(2,1)S(1)} copy-done((bf16[128,3072]{1,0:T(8,128)(2,1)S(1)}, bf16[128,3072]{1,0:T(8,128)(2,1)}, u32[]{:S(2)}) %copy-start.1) | copy-done | bytes 786456
  9.4 0.7 copy-done.2
  10.1 5.7 %load.1 = (bf16[16,64,576]{2,1,0:T(8,128)(2,1)S(1)}, bf16[16,64,576]{2,1,0:T(8,128)(2,1)S(1)}, f32[64,1024]{1,0:T(8,128)S(1)}, f32[64,1024]{1,0:T(8,128)S(1)}, b...) custom-call(s32[4]{0:T(128)S(1)} %copy-done.2, s32[1]{0:T(128)S(6)} %copy.21.prefix_ref, ...), custom_call_target="tpu_custom_call" | custom-call | flops 1024 | bytes 1024 | tf_op jit(solution)/shard_map/load/pallas_call | solution.py:131
  15.8 0.0 collective-permute-done.refs_0_
  15.8 0.1 collective-permute-start.3
  15.9 2.2 %collective-permute-done.1.refs_0_ = bf16[576,128]{1,0:T(8,128)(2,1)S(1)} collective-permute-done((bf16[576,128]{1,0:T(8,128)(2,1)S(1)}, bf16[576,128]{1,0:T(8,128)(2,1)S(1)}, u32[]{:S(2)}, u32[]{:S(2)}) %collective-permute-start.1) | collective-permute-done | bytes 147488 | tf_op jit(solution)/shard_map/keys_over_ctx/ppermute | solution.py:38
  18.1 0.0 collective-permute-start.4
  18.1 0.0 collective-permute-done.2.refs_0_
  18.1 0.5 collective-permute-start.5
  18.6 0.0 collective-permute-done.3.refs_4_
  18.6 0.9 collective-permute-done.4.refs_5_
  19.5 0.2 collective-permute-done.5.refs_6_
  19.7 3.9 %attention.2 = (bf16[64,2048]{1,0:T(8,128)(2,1)S(1)}, bf16[576,1024]{1,0:T(8,128)(2,1)S(1)}, bf16[1024,512]{1,0:T(8,128)(2,1)S(1)}) custom-call(bf16[16,64,576]{2,1,0:T(8,128)(2,1)S(1)} %get-tuple-element.33.q_ref, f32[64,1024]{1,0:T(8,128)S(1)} %get-tuple-element.34.bias_ref, bf16[16,512,128]{2,1,0:T(8,128)(2,1)S(1)} %get-tuple-element.35.value_ref, ...), custom_call_target="tpu_custom_call" | custom-call | flops 1024 | bytes 1024 | tf_op jit(solution)/shard_map/attention/pallas_call | solution.py:226
  23.6 3.2 %collective-permute-start.7 = (bf16[64,2048]{1,0:T(8,128)(2,1)S(1)}, bf16[64,2048]{1,0:T(8,128)(2,1)S(1)}, u32[]{:S(2)}, u32[]{:S(2)}) collective-permute-start(bf16[64,2048]{1,0:T(8,128)(2,1)S(1)} %get-tuple-element.37.refs_0_), channel_id=1, source_target_pairs={{0,8},{4,12},{8,0},{12,4},{1,9},{5,13},{9,1},{13,5},{2,10},{6,14},... | collective-permute-start | bytes 786440 | tf_op jit(solution)/shard_map/attended_over_ctx/ppermute | solution.py:38
  26.7 0.0 collective-permute-start.6
  26.7 3.8 %attention.3.refs_1_.refs_4_.refs_0_ = bf16[64,2048]{1,0:T(8,128)(2,1)S(1)} custom-call(bf16[16,64,576]{2,1,0:T(8,128)(2,1)S(1)} %get-tuple-element.38.q_ref, f32[64,1024]{1,0:T(8,128)S(1)} %get-tuple-element.39.bias_ref, bf16[16,512,128]{2,1,0:T(8,128)(2,1)S(1)} %get-tuple-element.35.value_ref, bf16[576,1024]{1,0:T(8,128)(2,1)S(1)} %get-tuple-element.40.refs_0_, ...), custom_call_target="tpu_custom_call" | custom-call | flops 1024 | bytes 1024 | tf_op jit(solution)/shard_map/attention/pallas_call | solution.py:226
  30.5 8.5 %collective-permute-done.7.refs_0_ = bf16[64,2048]{1,0:T(8,128)(2,1)S(1)} collective-permute-done((bf16[64,2048]{1,0:T(8,128)(2,1)S(1)}, bf16[64,2048]{1,0:T(8,128)(2,1)S(1)}, u32[]{:S(2)}, u32[]{:S(2)}) %collective-permute-start.7) | collective-permute-done | bytes 262176 | tf_op jit(solution)/shard_map/attended_over_ctx/ppermute | solution.py:38
  39.1 0.0 collective-permute-start.8
  39.1 2.4 %collective-permute-start.10 = (bf16[64,2048]{1,0:T(8,128)(2,1)S(1)}, bf16[64,2048]{1,0:T(8,128)(2,1)S(1)}, u32[]{:S(2)}, u32[]{:S(2)}) collective-permute-start(bf16[64,2048]{1,0:T(8,128)(2,1)S(1)} %attention.3.refs_1_.refs_4_.refs_0_), channel_id=1, source_target_pairs={{0,8},{4,12},{8,0},{12,4},{1,9},{5,13},{9,1},{13,5},{2,10},{6,14},... | collective-permute-start | bytes 786440 | tf_op jit(solution)/shard_map/attended_over_ctx/ppermute | solution.py:38
  41.5 0.0 collective-permute-start.9
  41.5 0.0 collective-permute-done.6.refs_1_
  41.5 12.0 %collective-permute-done.8.refs_3_ = bf16[64,2048]{1,0:T(8,128)(2,1)S(1)} collective-permute-done((bf16[64,2048]{1,0:T(8,128)(2,1)S(1)}, bf16[64,2048]{1,0:T(8,128)(2,1)S(1)}, u32[]{:S(2)}, u32[]{:S(2)}) %collective-permute-start.8) | collective-permute-done | bytes 262176 | tf_op jit(solution)/shard_map/attended_over_ctx/ppermute | solution.py:38
  53.5 0.0 slice-done
  53.5 0.0 slice-done.1
  53.5 2.1 %out_product.3 = (bf16[2,64,1792]{2,1,0:T(8,128)(2,1)S(1)}, f32[2,64,1792]{2,1,0:T(8,128)S(1)}) custom-call(bf16[2048,1792]{1,0:T(8,128)(2,1)S(1)} %bitcast.2, bf16[64,2048]{1,0:T(8,128)(2,1)S(1)} %get-tuple-element.37.refs_0_, bf16[64,2048]{1,0:T(8,128)(2,1)S(1)} %collective-permute-done.6.refs_1_, bf16[64,2048]{1,0:T(8,128)(2,1)S(1)} %attended_over_ctx.1.refs_2_, ...), custom_call_target="tpu_custom_call" | custom-call | flops 1024 | bytes 1024 | tf_op jit(solution)/shard_map/out_product/pallas_call | solution.py:260
  55.6 0.0 collective-permute-done.10.refs_2_
  55.7 2.4 %collective-permute-done.9.refs_1_ = bf16[64,2048]{1,0:T(8,128)(2,1)S(1)} collective-permute-done((bf16[64,2048]{1,0:T(8,128)(2,1)S(1)}, bf16[64,2048]{1,0:T(8,128)(2,1)S(1)}, u32[]{:S(2)}, u32[]{:S(2)}) %collective-permute-start.9) | collective-permute-done | bytes 262176 | tf_op jit(solution)/shard_map/attended_over_ctx/ppermute | solution.py:38
  58.1 0.0 collective-permute-start.11
  58.1 1.6 %out_product.4 = (bf16[2,48,1792]{2,1,0:T(8,128)(2,1)S(1)}, f32[2,48,1792]{2,1,0:T(8,128)S(1)}) custom-call(bf16[2048,1792]{1,0:T(8,128)(2,1)S(1)} %bitcast.2, bf16[64,2048]{1,0:T(8,128)(2,1)S(1)} %attention.3.refs_1_.refs_4_.refs_0_, bf16[64,2048]{1,0:T(8,128)(2,1)S(1)} %collective-permute-done.9.refs_1_, bf16[64,2048]{1,0:T(8,128)(2,1)S(1)} %collective-permute-done.10.refs_2_), custom_call_target="tpu_custom_call" | custom-call | flops 1024 | bytes 1024 | tf_op jit(solution)/shard_map/out_product/pallas_call | solution.py:260
  59.7 0.6 collective-permute-start.16
  60.3 0.3 collective-permute-start.20
  60.6 0.0 collective-permute-done.11.received_ref
  60.6 0.1 sum_over_cores.6
  60.7 1.5 %collective-permute-start.12 = (bf16[64,1792]{1,0:T(8,128)(2,1)S(1)}, bf16[64,1792]{1,0:T(8,128)(2,1)S(1)}, u32[]{:S(2)}, u32[]{:S(2)}) collective-permute-start(bf16[64,1792]{1,0:T(8,128)(2,1)S(1)} %get-tuple-element.45), channel_id=1, source_target_pairs={{0,2},{1,3},{2,0},{3,1},{4,6},{5,7},{6,4},{7,5},{8,10},{9,11},{10,... | collective-permute-start | bytes 688136 | tf_op jit(solution)/shard_map/sum_over_x/ppermute | solution.py:38
  62.3 0.0 collective-permute-done.16.received_ref
  62.3 0.1 sum_over_cores.7
  62.3 0.9 %collective-permute-start.17 = (bf16[48,1792]{1,0:T(8,128)(2,1)S(1)}, bf16[48,1792]{1,0:T(8,128)(2,1)S(1)}, u32[]{:S(2)}, u32[]{:S(2)}) collective-permute-start(bf16[48,1792]{1,0:T(8,128)(2,1)S(1)} %get-tuple-element.53), channel_id=1, source_target_pairs={{0,2},{1,3},{2,0},{3,1},{4,6},{5,7},{6,4},{7,5},{8,10},{9,11},{10,... | collective-permute-start | bytes 516104 | tf_op jit(solution)/shard_map/sum_over_x/ppermute | solution.py:38
  63.2 5.4 %collective-permute-done.20.refs_0_ = bf16[64,2048]{1,0:T(8,128)(2,1)S(1)} collective-permute-done((bf16[64,2048]{1,0:T(8,128)(2,1)S(1)}, bf16[64,2048]{1,0:T(8,128)(2,1)S(1)}, u32[]{:S(2)}, u32[]{:S(2)}) %collective-permute-start.20) | collective-permute-done | bytes 262176 | tf_op jit(solution)/shard_map/attended_over_ctx/ppermute | solution.py:38
  68.6 1.4 %out_product.5 = (bf16[2,16,1792]{2,1,0:T(8,128)(2,1)S(1)}, f32[2,16,1792]{2,1,0:T(8,128)S(1)}) custom-call(bf16[2048,1792]{1,0:T(8,128)(2,1)S(1)} %bitcast.2, bf16[64,2048]{1,0:T(8,128)(2,1)S(1)} %collective-permute-done.20.refs_0_), custom_call_target="tpu_custom_call" | custom-call | flops 1024 | bytes 1024 | tf_op jit(solution)/shard_map/out_product/pallas_call | solution.py:260
  70.0 0.0 collective-permute-done.12.refs_0_.refs_1_
  70.0 0.1 collective-permute-start.21
  70.1 1.3 %collective-permute-done.21.received_ref = bf16[2,16,1792]{2,1,0:T(8,128)(2,1)S(1)} collective-permute-done((bf16[2,16,1792]{2,1,0:T(8,128)(2,1)S(1)}, bf16[2,16,1792]{2,1,0:T(8,128)(2,1)S(1)}, u32[]{:S(2)}, u32[]{:S(2)}) %collective-permute-start.21) | collective-permute-done | bytes 114720 | tf_op jit(solution)/shard_map/sum_over_cores/ppermute | solution.py:38
  71.4 0.3 collective-permute-done.17.refs_0_.refs_1_
  71.8 1.5 %collective-permute-start.22 = (bf16[16,1792]{1,0:T(8,128)(2,1)S(1)}, bf16[16,1792]{1,0:T(8,128)(2,1)S(1)}, u32[]{:S(2)}, u32[]{:S(2)}) collective-permute-start(bf16[16,1792]{1,0:T(8,128)(2,1)S(1)} %sum_over_x.6), channel_id=1, source_target_pairs={{0,2},{1,3},{2,0},{3,1},{4,6},{5,7},{6,4},{7,5},{8,10},{9,11},{10,... | collective-permute-start | bytes 172040 | tf_op jit(solution)/shard_map/sum_over_x/ppermute | solution.py:38
  73.3 1.8 %collective-permute-start.18 = (bf16[16,1792]{1,0:T(8,128)(2,1)S(1)}, bf16[16,1792]{1,0:T(8,128)(2,1)S(1)}, u32[]{:S(2)}, u32[]{:S(2)}) collective-permute-start(bf16[16,1792]{1,0:T(8,128)(2,1)S(1)} %get-tuple-element.55), channel_id=1, source_target_pairs={{0,4},{4,0},{8,12},{12,8},{1,5},{5,1},{9,13},{13,9},{2,6},{6,2},{1... | collective-permute-start | bytes 172040 | tf_op jit(solution)/shard_map/columns_over_ctx/ppermute | solution.py:38
  75.1 0.7 collective-permute-start.19
  75.8 1.8 %collective-permute-start.13 = (bf16[16,1792]{1,0:T(8,128)(2,1)S(1)}, bf16[16,1792]{1,0:T(8,128)(2,1)S(1)}, u32[]{:S(2)}, u32[]{:S(2)}) collective-permute-start(bf16[16,1792]{1,0:T(8,128)(2,1)S(1)} %get-tuple-element.47), channel_id=1, source_target_pairs={{0,4},{4,0},{8,12},{12,8},{1,5},{5,1},{9,13},{13,9},{2,6},{6,2},{1... | collective-permute-start | bytes 172040 | tf_op jit(solution)/shard_map/columns_over_ctx/ppermute | solution.py:38
  77.5 0.9 %collective-permute-start.14 = (bf16[16,1792]{1,0:T(8,128)(2,1)S(1)}, bf16[16,1792]{1,0:T(8,128)(2,1)S(1)}, u32[]{:S(2)}, u32[]{:S(2)}) collective-permute-start(bf16[16,1792]{1,0:T(8,128)(2,1)S(1)} %get-tuple-element.48), channel_id=1, source_target_pairs={{0,8},{4,12},{8,0},{12,4},{1,9},{5,13},{9,1},{13,5},{2,10},{6,14},... | collective-permute-start | bytes 172040 | tf_op jit(solution)/shard_map/columns_over_ctx/ppermute | solution.py:38
  78.4 0.0 collective-permute-done.22.refs_0_
  78.4 1.8 %collective-permute-start.15 = (bf16[16,1792]{1,0:T(8,128)(2,1)S(1)}, bf16[16,1792]{1,0:T(8,128)(2,1)S(1)}, u32[]{:S(2)}, u32[]{:S(2)}) collective-permute-start(bf16[16,1792]{1,0:T(8,128)(2,1)S(1)} %get-tuple-element.49), channel_id=1, source_target_pairs={{0,12},{4,8},{8,4},{12,0},{1,13},{5,9},{9,5},{13,1},{2,14},{6,10},... | collective-permute-start | bytes 172040 | tf_op jit(solution)/shard_map/columns_over_ctx/ppermute | solution.py:38
  80.2 0.0 collective-permute-done.18.refs_5_
  80.2 2.1 %collective-permute-start.23 = (bf16[16,1792]{1,0:T(8,128)(2,1)S(1)}, bf16[16,1792]{1,0:T(8,128)(2,1)S(1)}, u32[]{:S(2)}, u32[]{:S(2)}) collective-permute-start(bf16[16,1792]{1,0:T(8,128)(2,1)S(1)} %sum_over_x.7), channel_id=1, source_target_pairs={{0,12},{4,8},{8,4},{12,0},{1,13},{5,9},{9,5},{13,1},{2,14},{6,10},... | collective-permute-start | bytes 172040 | tf_op jit(solution)/shard_map/columns_over_ctx/ppermute | solution.py:38
  82.3 1.4 %collective-permute-done.19.refs_6_ = bf16[16,1792]{1,0:T(8,128)(2,1)S(1)} collective-permute-done((bf16[16,1792]{1,0:T(8,128)(2,1)S(1)}, bf16[16,1792]{1,0:T(8,128)(2,1)S(1)}, u32[]{:S(2)}, u32[]{:S(2)}) %collective-permute-start.19) | collective-permute-done | bytes 57376 | tf_op jit(solution)/shard_map/columns_over_ctx/ppermute | solution.py:38
  83.7 0.0 collective-permute-done.13.refs_1_
  83.8 1.8 %collective-permute-done.14.refs_2_ = bf16[16,1792]{1,0:T(8,128)(2,1)S(1)} collective-permute-done((bf16[16,1792]{1,0:T(8,128)(2,1)S(1)}, bf16[16,1792]{1,0:T(8,128)(2,1)S(1)}, u32[]{:S(2)}, u32[]{:S(2)}) %collective-permute-start.14) | collective-permute-done | bytes 57376 | tf_op jit(solution)/shard_map/columns_over_ctx/ppermute | solution.py:38
  85.6 0.0 collective-permute-done.15.refs_3_
  85.6 0.8 collective-permute-done.23.refs_7_
  86.4 0.8 output.1
  (16 shorter events, 0.1 us)
Async XLA Ops:
  1.0 14.8 %collective-permute-start = (bf16[576,128]{1,0:T(8,128)(2,1)S(1)}, bf16[576,128]{1,0:T(8,128)(2,1)S(1)}, u32[]{:S(2)}, u32[]{:S(2)}) collective-permute-start(bf16[576,128]{1,0:T(8,128)(2,1)S(1)} %slice_select_fusion), channel_id=1, source_target_pairs={{0,4},{4,0},{8,12},{12,8},{1,5},{5,1},{9,13},{13,9},{2,6},{6,2},{1... | collective-permute-start | bytes 442376 | tf_op jit(solution)/shard_map/keys_over_ctx/ppermute | solution.py:38
  4.1 14.0 %collective-permute-start.1 = (bf16[576,128]{1,0:T(8,128)(2,1)S(1)}, bf16[576,128]{1,0:T(8,128)(2,1)S(1)}, u32[]{:S(2)}, u32[]{:S(2)}) collective-permute-start(bf16[576,128]{1,0:T(8,128)(2,1)S(1)} %slice_select_fusion), channel_id=1, source_target_pairs={{0,8},{4,12},{8,0},{12,4},{1,9},{5,13},{9,1},{13,5},{2,10},{6,14},... | collective-permute-start | bytes 442376 | tf_op jit(solution)/shard_map/keys_over_ctx/ppermute | solution.py:38
  6.7 11.4 %collective-permute-start.2 = (bf16[576,128]{1,0:T(8,128)(2,1)S(1)}, bf16[576,128]{1,0:T(8,128)(2,1)S(1)}, u32[]{:S(2)}, u32[]{:S(2)}) collective-permute-start(bf16[576,128]{1,0:T(8,128)(2,1)S(1)} %slice_select_fusion), channel_id=1, source_target_pairs={{0,12},{4,8},{8,4},{12,0},{1,13},{5,9},{9,5},{13,1},{2,14},{6,10},... | collective-permute-start | bytes 442376 | tf_op jit(solution)/shard_map/keys_over_ctx/ppermute | solution.py:38
  7.3 1.0 %copy-start = (bf16[256,576]{0,1:T(8,128)(2,1)S(1)}, bf16[256,576]{0,1:T(8,128)(2,1)}, u32[]{:S(2)}) copy-start(bf16[256,576]{0,1:T(8,128)(2,1)} %param.7) | copy-start | bytes 884740
  8.3 1.1 %copy-start.1 = (bf16[128,3072]{1,0:T(8,128)(2,1)S(1)}, bf16[128,3072]{1,0:T(8,128)(2,1)}, u32[]{:S(2)}) copy-start(bf16[128,3072]{1,0:T(8,128)(2,1)} %q_hbm.1) | copy-start | bytes 2359300
  9.4 0.7 copy-start.2
  10.1 43.4 %slice-start = ((s8[7340032]{0:T(1024)(128)(4,1)}), s8[3145728]{0:T(1024)(128)(4,1)S(1)}, s32[]{:S(2)}) async-start(s8[7340032]{0:T(1024)(128)(4,1)} %bitcast.1), calls=%async_computation | async-start | bytes 6291456
  15.8 2.8 %collective-permute-start.3 = (bf16[576,128]{1,0:T(8,128)(2,1)S(1)}, bf16[576,128]{1,0:T(8,128)(2,1)S(1)}, u32[]{:S(2)}, u32[]{:S(2)}) collective-permute-start(bf16[576,128]{1,0:T(8,128)(2,1)S(1)} %keys_over_cores.3.refs_1_), channel_id=1, source_target_pairs={{0,1},{1,0},{2,3},{3,2},{4,5},{5,4},{6,7},{7,6},{8,9},{9,8},{10,11... | collective-permute-start | bytes 442376 | tf_op jit(solution)/shard_map/keys_over_cores/ppermute | solution.py:38
  18.1 1.4 %collective-permute-start.4 = (bf16[576,128]{1,0:T(8,128)(2,1)S(1)}, bf16[576,128]{1,0:T(8,128)(2,1)S(1)}, u32[]{:S(2)}, u32[]{:S(2)}) collective-permute-start(bf16[576,128]{1,0:T(8,128)(2,1)S(1)} %keys_over_cores.4.refs_2_), channel_id=1, source_target_pairs={{0,1},{1,0},{2,3},{3,2},{4,5},{5,4},{6,7},{7,6},{8,9},{9,8},{10,11... | collective-permute-start | bytes 442376 | tf_op jit(solution)/shard_map/keys_over_cores/ppermute | solution.py:38
  18.1 1.6 %collective-permute-start.5 = (bf16[576,128]{1,0:T(8,128)(2,1)S(1)}, bf16[576,128]{1,0:T(8,128)(2,1)S(1)}, u32[]{:S(2)}, u32[]{:S(2)}) collective-permute-start(bf16[576,128]{1,0:T(8,128)(2,1)S(1)} %keys_over_cores.5.refs_3_), channel_id=1, source_target_pairs={{0,1},{1,0},{2,3},{3,2},{4,5},{5,4},{6,7},{7,6},{8,9},{9,8},{10,11... | collective-permute-start | bytes 442376 | tf_op jit(solution)/shard_map/keys_over_cores/ppermute | solution.py:38
  19.7 33.9 %slice-start.1 = ((s8[7340032]{0:T(1024)(128)(4,1)}), s8[4194304]{0:T(1024)(128)(4,1)S(1)}, s32[]{:S(2)}) async-start(s8[7340032]{0:T(1024)(128)(4,1)} %bitcast.1), calls=%async_computation.1 | async-start | bytes 8388608
  23.6 15.5 %collective-permute-start.7 = (bf16[64,2048]{1,0:T(8,128)(2,1)S(1)}, bf16[64,2048]{1,0:T(8,128)(2,1)S(1)}, u32[]{:S(2)}, u32[]{:S(2)}) collective-permute-start(bf16[64,2048]{1,0:T(8,128)(2,1)S(1)} %get-tuple-element.37.refs_0_), channel_id=1, source_target_pairs={{0,8},{4,12},{8,0},{12,4},{1,9},{5,13},{9,1},{13,5},{2,10},{6,14},... | collective-permute-start | bytes 786440 | tf_op jit(solution)/shard_map/attended_over_ctx/ppermute | solution.py:38
  26.7 14.8 %collective-permute-start.6 = (bf16[64,2048]{1,0:T(8,128)(2,1)S(1)}, bf16[64,2048]{1,0:T(8,128)(2,1)S(1)}, u32[]{:S(2)}, u32[]{:S(2)}) collective-permute-start(bf16[64,2048]{1,0:T(8,128)(2,1)S(1)} %get-tuple-element.37.refs_0_), channel_id=1, source_target_pairs={{0,4},{4,0},{8,12},{12,8},{1,5},{5,1},{9,13},{13,9},{2,6},{6,2},{1... | collective-permute-start | bytes 786440 | tf_op jit(solution)/shard_map/attended_over_ctx/ppermute | solution.py:38
  39.1 14.5 %collective-permute-start.8 = (bf16[64,2048]{1,0:T(8,128)(2,1)S(1)}, bf16[64,2048]{1,0:T(8,128)(2,1)S(1)}, u32[]{:S(2)}, u32[]{:S(2)}) collective-permute-start(bf16[64,2048]{1,0:T(8,128)(2,1)S(1)} %attended_over_ctx.1.refs_2_), channel_id=1, source_target_pairs={{0,4},{4,0},{8,12},{12,8},{1,5},{5,1},{9,13},{13,9},{2,6},{6,2},{1... | collective-permute-start | bytes 786440 | tf_op jit(solution)/shard_map/attended_over_ctx/ppermute | solution.py:38
  39.1 16.6 %collective-permute-start.10 = (bf16[64,2048]{1,0:T(8,128)(2,1)S(1)}, bf16[64,2048]{1,0:T(8,128)(2,1)S(1)}, u32[]{:S(2)}, u32[]{:S(2)}) collective-permute-start(bf16[64,2048]{1,0:T(8,128)(2,1)S(1)} %attention.3.refs_1_.refs_4_.refs_0_), channel_id=1, source_target_pairs={{0,8},{4,12},{8,0},{12,4},{1,9},{5,13},{9,1},{13,5},{2,10},{6,14},... | collective-permute-start | bytes 786440 | tf_op jit(solution)/shard_map/attended_over_ctx/ppermute | solution.py:38
  41.5 16.6 %collective-permute-start.9 = (bf16[64,2048]{1,0:T(8,128)(2,1)S(1)}, bf16[64,2048]{1,0:T(8,128)(2,1)S(1)}, u32[]{:S(2)}, u32[]{:S(2)}) collective-permute-start(bf16[64,2048]{1,0:T(8,128)(2,1)S(1)} %attention.3.refs_1_.refs_4_.refs_0_), channel_id=1, source_target_pairs={{0,4},{4,0},{8,12},{12,8},{1,5},{5,1},{9,13},{13,9},{2,6},{6,2},{1... | collective-permute-start | bytes 786440 | tf_op jit(solution)/shard_map/attended_over_ctx/ppermute | solution.py:38
  58.1 2.5 %collective-permute-start.11 = (bf16[2,64,1792]{2,1,0:T(8,128)(2,1)S(1)}, bf16[2,64,1792]{2,1,0:T(8,128)(2,1)S(1)}, u32[]{:S(2)}, u32[]{:S(2)}) collective-permute-start(bf16[2,64,1792]{2,1,0:T(8,128)(2,1)S(1)} %sum_over_cores.5), channel_id=1, source_target_pairs={{0,1},{1,0},{2,3},{3,2},{4,5},{5,4},{6,7},{7,6},{8,9},{9,8},{10,11... | collective-permute-start | bytes 1376264 | tf_op jit(solution)/shard_map/sum_over_cores/ppermute | solution.py:38
  59.7 2.5 %collective-permute-start.16 = (bf16[2,48,1792]{2,1,0:T(8,128)(2,1)S(1)}, bf16[2,48,1792]{2,1,0:T(8,128)(2,1)S(1)}, u32[]{:S(2)}, u32[]{:S(2)}) collective-permute-start(bf16[2,48,1792]{2,1,0:T(8,128)(2,1)S(1)} %get-tuple-element.51), channel_id=1, source_target_pairs={{0,1},{1,0},{2,3},{3,2},{4,5},{5,4},{6,7},{7,6},{8,9},{9,8},{10,11... | collective-permute-start | bytes 1032200 | tf_op jit(solution)/shard_map/sum_over_cores/ppermute | solution.py:38
  60.3 8.3 %collective-permute-start.20 = (bf16[64,2048]{1,0:T(8,128)(2,1)S(1)}, bf16[64,2048]{1,0:T(8,128)(2,1)S(1)}, u32[]{:S(2)}, u32[]{:S(2)}) collective-permute-start(bf16[64,2048]{1,0:T(8,128)(2,1)S(1)} %collective-permute-done.10.refs_2_), channel_id=1, source_target_pairs={{0,4},{4,0},{8,12},{12,8},{1,5},{5,1},{9,13},{13,9},{2,6},{6,2},{1... | collective-permute-start | bytes 786440 | tf_op jit(solution)/shard_map/attended_over_ctx/ppermute | solution.py:38
  60.7 9.3 %collective-permute-start.12 = (bf16[64,1792]{1,0:T(8,128)(2,1)S(1)}, bf16[64,1792]{1,0:T(8,128)(2,1)S(1)}, u32[]{:S(2)}, u32[]{:S(2)}) collective-permute-start(bf16[64,1792]{1,0:T(8,128)(2,1)S(1)} %get-tuple-element.45), channel_id=1, source_target_pairs={{0,2},{1,3},{2,0},{3,1},{4,6},{5,7},{6,4},{7,5},{8,10},{9,11},{10,... | collective-permute-start | bytes 688136 | tf_op jit(solution)/shard_map/sum_over_x/ppermute | solution.py:38
  62.3 9.4 %collective-permute-start.17 = (bf16[48,1792]{1,0:T(8,128)(2,1)S(1)}, bf16[48,1792]{1,0:T(8,128)(2,1)S(1)}, u32[]{:S(2)}, u32[]{:S(2)}) collective-permute-start(bf16[48,1792]{1,0:T(8,128)(2,1)S(1)} %get-tuple-element.53), channel_id=1, source_target_pairs={{0,2},{1,3},{2,0},{3,1},{4,6},{5,7},{6,4},{7,5},{8,10},{9,11},{10,... | collective-permute-start | bytes 516104 | tf_op jit(solution)/shard_map/sum_over_x/ppermute | solution.py:38
  70.0 1.4 %collective-permute-start.21 = (bf16[2,16,1792]{2,1,0:T(8,128)(2,1)S(1)}, bf16[2,16,1792]{2,1,0:T(8,128)(2,1)S(1)}, u32[]{:S(2)}, u32[]{:S(2)}) collective-permute-start(bf16[2,16,1792]{2,1,0:T(8,128)(2,1)S(1)} %sum_over_cores.8), channel_id=1, source_target_pairs={{0,1},{1,0},{2,3},{3,2},{4,5},{5,4},{6,7},{7,6},{8,9},{9,8},{10,11... | collective-permute-start | bytes 344072 | tf_op jit(solution)/shard_map/sum_over_cores/ppermute | solution.py:38
  71.8 6.6 %collective-permute-start.22 = (bf16[16,1792]{1,0:T(8,128)(2,1)S(1)}, bf16[16,1792]{1,0:T(8,128)(2,1)S(1)}, u32[]{:S(2)}, u32[]{:S(2)}) collective-permute-start(bf16[16,1792]{1,0:T(8,128)(2,1)S(1)} %sum_over_x.6), channel_id=1, source_target_pairs={{0,2},{1,3},{2,0},{3,1},{4,6},{5,7},{6,4},{7,5},{8,10},{9,11},{10,... | collective-permute-start | bytes 172040 | tf_op jit(solution)/shard_map/sum_over_x/ppermute | solution.py:38
  73.3 6.9 %collective-permute-start.18 = (bf16[16,1792]{1,0:T(8,128)(2,1)S(1)}, bf16[16,1792]{1,0:T(8,128)(2,1)S(1)}, u32[]{:S(2)}, u32[]{:S(2)}) collective-permute-start(bf16[16,1792]{1,0:T(8,128)(2,1)S(1)} %get-tuple-element.55), channel_id=1, source_target_pairs={{0,4},{4,0},{8,12},{12,8},{1,5},{5,1},{9,13},{13,9},{2,6},{6,2},{1... | collective-permute-start | bytes 172040 | tf_op jit(solution)/shard_map/columns_over_ctx/ppermute | solution.py:38
  75.1 8.7 %collective-permute-start.19 = (bf16[16,1792]{1,0:T(8,128)(2,1)S(1)}, bf16[16,1792]{1,0:T(8,128)(2,1)S(1)}, u32[]{:S(2)}, u32[]{:S(2)}) collective-permute-start(bf16[16,1792]{1,0:T(8,128)(2,1)S(1)} %get-tuple-element.56), channel_id=1, source_target_pairs={{0,8},{4,12},{8,0},{12,4},{1,9},{5,13},{9,1},{13,5},{2,10},{6,14},... | collective-permute-start | bytes 172040 | tf_op jit(solution)/shard_map/columns_over_ctx/ppermute | solution.py:38
  75.8 8.0 %collective-permute-start.13 = (bf16[16,1792]{1,0:T(8,128)(2,1)S(1)}, bf16[16,1792]{1,0:T(8,128)(2,1)S(1)}, u32[]{:S(2)}, u32[]{:S(2)}) collective-permute-start(bf16[16,1792]{1,0:T(8,128)(2,1)S(1)} %get-tuple-element.47), channel_id=1, source_target_pairs={{0,4},{4,0},{8,12},{12,8},{1,5},{5,1},{9,13},{13,9},{2,6},{6,2},{1... | collective-permute-start | bytes 172040 | tf_op jit(solution)/shard_map/columns_over_ctx/ppermute | solution.py:38
  77.5 8.1 %collective-permute-start.14 = (bf16[16,1792]{1,0:T(8,128)(2,1)S(1)}, bf16[16,1792]{1,0:T(8,128)(2,1)S(1)}, u32[]{:S(2)}, u32[]{:S(2)}) collective-permute-start(bf16[16,1792]{1,0:T(8,128)(2,1)S(1)} %get-tuple-element.48), channel_id=1, source_target_pairs={{0,8},{4,12},{8,0},{12,4},{1,9},{5,13},{9,1},{13,5},{2,10},{6,14},... | collective-permute-start | bytes 172040 | tf_op jit(solution)/shard_map/columns_over_ctx/ppermute | solution.py:38
  78.4 7.2 %collective-permute-start.15 = (bf16[16,1792]{1,0:T(8,128)(2,1)S(1)}, bf16[16,1792]{1,0:T(8,128)(2,1)S(1)}, u32[]{:S(2)}, u32[]{:S(2)}) collective-permute-start(bf16[16,1792]{1,0:T(8,128)(2,1)S(1)} %get-tuple-element.49), channel_id=1, source_target_pairs={{0,12},{4,8},{8,4},{12,0},{1,13},{5,9},{9,5},{13,1},{2,14},{6,10},... | collective-permute-start | bytes 172040 | tf_op jit(solution)/shard_map/columns_over_ctx/ppermute | solution.py:38
  80.2 6.2 %collective-permute-start.23 = (bf16[16,1792]{1,0:T(8,128)(2,1)S(1)}, bf16[16,1792]{1,0:T(8,128)(2,1)S(1)}, u32[]{:S(2)}, u32[]{:S(2)}) collective-permute-start(bf16[16,1792]{1,0:T(8,128)(2,1)S(1)} %sum_over_x.7), channel_id=1, source_target_pairs={{0,12},{4,8},{8,4},{12,0},{1,13},{5,9},{9,5},{13,1},{2,14},{6,10},... | collective-permute-start | bytes 172040 | tf_op jit(solution)/shard_map/columns_over_ctx/ppermute | solution.py:38

commit v10 on v9

--- a/solution.py
+++ b/solution.py
@@ -293,56 +293,57 @@
     return out[0], out[1:]
 
 
-def x_sum_kernel(count, total_ref, *refs):
-    received, block_refs = refs[:count], refs[count:]
-    total = total_ref[...]
-    for ref in received:
-        total = total + ref[...].astype(jnp.float32)
-    rows = block_refs[0].shape[0]
-    for index, block_ref in enumerate(block_refs):
-        block_ref[...] = total[index * rows : (index + 1) * rows].astype(jnp.bfloat16)
-
-
-def x_sum(total, received, count):
-    rows, columns = total.shape
-    block = jax.ShapeDtypeStruct((rows // count, columns), jnp.bfloat16)
+def x_sum_kernel(places, *refs):
+    sources, refs = [], list(refs)
+    for count, rows, indices in places:
+        total = refs.pop(0)[...]
+        for _ in range(count):
+            total = total + refs.pop(0)[...].astype(jnp.float32)
+        sources.append([total[index * rows : (index + 1) * rows] for index in indices])
+    for out_ref, parts in zip(refs, zip(*sources)):
+        out_ref[...] = jnp.concatenate(parts, axis=0).astype(jnp.bfloat16)
+
+
+def x_sum(sources):
+    columns = sources[0][0].shape[1]
+    block = jax.ShapeDtypeStruct((sum(rows for _, _, rows, _ in sources), columns), jnp.bfloat16)
+    arrays = [array for total, received, _, _ in sources for array in [total, *received]]
+    places = [(len(received), rows, indices) for _, received, rows, indices in sources]
+    outputs = len(sources[0][3])
     return pl.pallas_call(
-        functools.partial(x_sum_kernel, len(received)),
-        out_shape=[block] * count,
-        in_specs=[IN_VMEM] * (1 + len(received)),
-        out_specs=[IN_VMEM] * count,
-        compiler_params=params(4),
-        cost_estimate=SHORT,
-    )(total, *received)
-
-
-def place_kernel(n_ctx, *refs):
+        functools.partial(x_sum_kernel, places),
+        out_shape=[block] * outputs,
+        in_specs=[IN_VMEM] * len(arrays),
+        out_specs=[IN_VMEM] * outputs,
+        compiler_params=params(8),
+        cost_estimate=SHORT,
+    )(*arrays)
+
+
+def place_kernel(*refs):
     blocks, out_ref = refs[:-1], refs[-1]
     ctx = lax.axis_index("ctx")
     width = blocks[0].shape[1]
-    for offset in range(n_ctx):
-        parts = [block[...].astype(jnp.float32) for block in blocks[offset::n_ctx]]
+    for offset, block in enumerate(blocks):
         column = pl.multiple_of((ctx ^ offset) * width, 128)
-        out_ref[:, pl.ds(column, width)] = jnp.concatenate(parts, axis=0).astype(jnp.bfloat16)
-
-
-def place_columns(results, n_ctx):
-    width = results[0][0].shape[1]
-    total = sum(result[0].shape[0] for result in results)
+        out_ref[:, pl.ds(column, width)] = block[...]
+
+
+def place_columns(blocks):
+    n_ctx = len(blocks)
+    rows, width = blocks[0].shape
     if width % 128:
         ctx = lax.axis_index("ctx")
-        out = jnp.zeros((total, n_ctx * width), jnp.bfloat16)
-        for offset in range(n_ctx):
-            block = jnp.concatenate([result[offset] for result in results], axis=0)
+        out = jnp.zeros((rows, n_ctx * width), jnp.bfloat16)
+        for offset, block in enumerate(blocks):
             out = lax.dynamic_update_slice(out, block, (0, (ctx ^ offset) * width))
         return out
-    blocks = [block for result in results for block in result]
     return pl.pallas_call(
-        functools.partial(place_kernel, n_ctx),
+        place_kernel,
         grid=(1,),
-        out_shape=jax.ShapeDtypeStruct((total, n_ctx * width), jnp.bfloat16),
-        in_specs=[IN_VMEM] * len(blocks),
-        out_specs=pl.BlockSpec((total, n_ctx * width), lambda i: (0, 0)),
+        out_shape=jax.ShapeDtypeStruct((rows, n_ctx * width), jnp.bfloat16),
+        in_specs=[IN_VMEM] * n_ctx,
+        out_specs=pl.BlockSpec((rows, n_ctx * width), lambda i: (0, 0)),
         compiler_params=params(4),
         cost_estimate=SHORT,
     )(*blocks)
@@ -382,7 +383,7 @@
     far = [offset for offset in range(n_ctx) if offset not in near]
     last = len(pieces) - 1
     units = [(chunk, list(range(n_ctx))) for chunk in range(last)] + [(last, near), (last, far)]
-    results = [{} for chunk in pieces]
+    sums = []
     after = attended[1:]
     crossed = []
     for unit, (chunk, offsets) in enumerate(units):
@@ -402,13 +403,17 @@
             crossed.append(
                 [exchange(array, "head", n_head, 2 * d) for d, array in enumerate(sent, 1)]
             )
-            blocks = x_sum(total, crossed[-1], len(offsets))
+        sums.append((total, crossed[-1], pieces[chunk]))
+    blocks = {}
+    for group, ending in ((near, sums[-2]), (far, sums[-1])):
+        with jax.named_scope("sum_over_x"):
+            sources = [(*part, group) for part in sums[:-2]] + [(*ending, range(len(group)))]
+            blocks.update(zip(group, x_sum(sources)))
         with jax.named_scope("columns_over_ctx"):
-            for d, block in zip(offsets, blocks):
-                results[chunk][d] = exchange(block, "ctx", n_ctx, d) if d else block
-    results = [[result[d] for d in range(n_ctx)] for result in results]
+            for d in reversed(group):
+                blocks[d] = exchange(blocks[d], "ctx", n_ctx, d) if d else blocks[d]
     with jax.named_scope("output"):
-        return place_columns(results, n_ctx)
+        return place_columns([blocks[d] for d in range(n_ctx)])
 
 
 def solution(mesh):

time: 87.4 us -> 86.7 us (level)
  starting transfers between devices: 25.7 us -> 21 us
  waiting for transfers between devices: 37.4 us -> 41.4 us
    ppermute x24 -> x21, starting transfers between devices: 25.7 us -> 21 us  [exchange(): return lax.ppermute(array, axis, [(i, i ^ bit) for i in range(size)])]
    ppermute x24 -> x21, waiting for transfers between devices: 37.4 us -> 41.4 us  [exchange(): return lax.ppermute(array, axis, [(i, i ^ bit) for i in range(size)])]
  transfers between devices with their start and end apart: 24 -> 21, of which waited for: 12 -> 12; matrix products, arithmetic and copies ran while one was open for 0% -> 0% of each run, Pallas kernels for 17% -> 17%
where the time goes in v10:
time: 86.7 us; the launch traced here: 86.5 us
  waiting for transfers between devices  41.4 us (48%)
  starting transfers between devices  21 us (24%)
  Pallas kernels  19.5 us (22%)
  local copies, waits for them, and re-layouts  2.75 us (3%)
  other arithmetic  1 us (1%)
    ppermute x21, waiting for transfers between devices, exchange(): return lax.ppermute(array, axis, [(i, i ^ bit) for i in range(size)])  41.4 us
    ppermute x21, starting transfers between devices, exchange(): return lax.ppermute(array, axis, [(i, i ^ bit) for i in range(size)])  21 us
    pallas_call x2, Pallas kernels, attention(): pl.pallas_call(functools.partial(attention_kernel, 0 if gathered else len...  7.69 us
    pallas_call x1, Pallas kernels, load(): pl.pallas_call(functools.partial(load_kernel, owners, pieces, cache_rows)...  5.66 us
    pallas_call x3, Pallas kernels, product(): pl.pallas_call(functools.partial(product_kernel, count, n_x, len(after)),...  5.1 us
    unnamed x10, local copies, waits for them, and re-layouts  2.75 us
  transfers between devices with their start and end apart: 21, of which 12 were waited for; matrix products, arithmetic and copies ran while one was open for 0% of the time, Pallas kernels for 17%

profile of v10, /device:TPU:0, one launch (start us, length us, event | category | flops | bytes accessed | tf_op | source)
XLA Modules:
  0.0 86.5 jit_solution(2142574748682992580)
XLA Ops:
  0.0 1.0 %slice_select_fusion = bf16[576,128]{1,0:T(8,128)(2,1)S(1)} fusion(bf16[576,256]{1,0:T(8,128)(2,1)} %bitcast.3, pred[]{:T(512)S(6)} %eq.5), kind=kLoop, calls=%fused_computation | loop fusion | flops 73728 | bytes 442369 | tf_op jit(solution)/shard_map/keys_over_ctx/jit(_where)/select_n | solution.py:363
  1.0 3.1 %collective-permute-start = (bf16[576,128]{1,0:T(8,128)(2,1)S(1)}, bf16[576,128]{1,0:T(8,128)(2,1)S(1)}, u32[]{:S(2)}, u32[]{:S(2)}) collective-permute-start(bf16[576,128]{1,0:T(8,128)(2,1)S(1)} %slice_select_fusion), channel_id=1, source_target_pairs={{0,4},{4,0},{8,12},{12,8},{1,5},{5,1},{9,13},{13,9},{2,6},{6,2},{1... | collective-permute-start | bytes 442376 | tf_op jit(solution)/shard_map/keys_over_ctx/ppermute | solution.py:38
  4.1 2.6 %collective-permute-start.1 = (bf16[576,128]{1,0:T(8,128)(2,1)S(1)}, bf16[576,128]{1,0:T(8,128)(2,1)S(1)}, u32[]{:S(2)}, u32[]{:S(2)}) collective-permute-start(bf16[576,128]{1,0:T(8,128)(2,1)S(1)} %slice_select_fusion), channel_id=1, source_target_pairs={{0,8},{4,12},{8,0},{12,4},{1,9},{5,13},{9,1},{13,5},{2,10},{6,14},... | collective-permute-start | bytes 442376 | tf_op jit(solution)/shard_map/keys_over_ctx/ppermute | solution.py:38
  6.7 0.0 collective-permute-start.2
  7.3 0.0 copy-start
  7.3 1.0 %copy-done = bf16[256,576]{0,1:T(8,128)(2,1)S(1)} copy-done((bf16[256,576]{0,1:T(8,128)(2,1)S(1)}, bf16[256,576]{0,1:T(8,128)(2,1)}, u32[]{:S(2)}) %copy-start) | copy-done | bytes 294936
  8.3 0.0 copy-start.1
  8.3 1.1 %copy-done.1 = bf16[128,3072]{1,0:T(8,128)(2,1)S(1)} copy-done((bf16[128,3072]{1,0:T(8,128)(2,1)S(1)}, bf16[128,3072]{1,0:T(8,128)(2,1)}, u32[]{:S(2)}) %copy-start.1) | copy-done | bytes 786456
  9.4 0.0 copy-start.2
  9.4 0.7 copy-done.2
  10.1 0.0 slice-start
  10.1 5.7 %load.1 = (bf16[16,64,576]{2,1,0:T(8,128)(2,1)S(1)}, bf16[16,64,576]{2,1,0:T(8,128)(2,1)S(1)}, f32[64,1024]{1,0:T(8,128)S(1)}, f32[64,1024]{1,0:T(8,128)S(1)}, b...) custom-call(s32[4]{0:T(128)S(1)} %copy-done.2, s32[1]{0:T(128)S(6)} %copy.21.prefix_ref, ...), custom_call_target="tpu_custom_call" | custom-call | flops 1024 | bytes 1024 | tf_op jit(solution)/shard_map/load/pallas_call | solution.py:131
  15.8 0.0 collective-permute-done.refs_0_
  15.8 0.1 collective-permute-start.3
  15.9 2.2 %collective-permute-done.1.refs_0_ = bf16[576,128]{1,0:T(8,128)(2,1)S(1)} collective-permute-done((bf16[576,128]{1,0:T(8,128)(2,1)S(1)}, bf16[576,128]{1,0:T(8,128)(2,1)S(1)}, u32[]{:S(2)}, u32[]{:S(2)}) %collective-permute-start.1) | collective-permute-done | bytes 147488 | tf_op jit(solution)/shard_map/keys_over_ctx/ppermute | solution.py:38
  18.1 0.0 collective-permute-start.4
  18.1 0.0 collective-permute-done.2.refs_0_
  18.1 0.5 collective-permute-start.5
  18.6 0.0 collective-permute-done.3.refs_4_
  18.6 0.9 collective-permute-done.4.refs_5_
  19.5 0.2 collective-permute-done.5.refs_6_
  19.7 0.0 slice-start.1
  19.7 3.9 %attention.2 = (bf16[64,2048]{1,0:T(8,128)(2,1)S(1)}, bf16[576,1024]{1,0:T(8,128)(2,1)S(1)}, bf16[1024,512]{1,0:T(8,128)(2,1)S(1)}) custom-call(bf16[16,64,576]{2,1,0:T(8,128)(2,1)S(1)} %get-tuple-element.29.q_ref, f32[64,1024]{1,0:T(8,128)S(1)} %get-tuple-element.30.bias_ref, bf16[16,512,128]{2,1,0:T(8,128)(2,1)S(1)} %get-tuple-element.31.value_ref, ...), custom_call_target="tpu_custom_call" | custom-call | flops 1024 | bytes 1024 | tf_op jit(solution)/shard_map/attention/pallas_call | solution.py:226
  23.6 3.2 %collective-permute-start.7 = (bf16[64,2048]{1,0:T(8,128)(2,1)S(1)}, bf16[64,2048]{1,0:T(8,128)(2,1)S(1)}, u32[]{:S(2)}, u32[]{:S(2)}) collective-permute-start(bf16[64,2048]{1,0:T(8,128)(2,1)S(1)} %get-tuple-element.33.refs_0_), channel_id=1, source_target_pairs={{0,8},{4,12},{8,0},{12,4},{1,9},{5,13},{9,1},{13,5},{2,10},{6,14},... | collective-permute-start | bytes 786440 | tf_op jit(solution)/shard_map/attended_over_ctx/ppermute | solution.py:38
  26.7 0.0 collective-permute-start.6
  26.7 3.8 %attention.3.refs_1_.refs_4_.refs_0_ = bf16[64,2048]{1,0:T(8,128)(2,1)S(1)} custom-call(bf16[16,64,576]{2,1,0:T(8,128)(2,1)S(1)} %get-tuple-element.34.q_ref, f32[64,1024]{1,0:T(8,128)S(1)} %get-tuple-element.35.bias_ref, bf16[16,512,128]{2,1,0:T(8,128)(2,1)S(1)} %get-tuple-element.31.value_ref, bf16[576,1024]{1,0:T(8,128)(2,1)S(1)} %get-tuple-element.36.refs_0_, ...), custom_call_target="tpu_custom_call" | custom-call | flops 1024 | bytes 1024 | tf_op jit(solution)/shard_map/attention/pallas_call | solution.py:226
  30.5 8.5 %collective-permute-done.7.refs_0_ = bf16[64,2048]{1,0:T(8,128)(2,1)S(1)} collective-permute-done((bf16[64,2048]{1,0:T(8,128)(2,1)S(1)}, bf16[64,2048]{1,0:T(8,128)(2,1)S(1)}, u32[]{:S(2)}, u32[]{:S(2)}) %collective-permute-start.7) | collective-permute-done | bytes 262176 | tf_op jit(solution)/shard_map/attended_over_ctx/ppermute | solution.py:38
  39.1 0.0 collective-permute-start.8
  39.1 2.4 %collective-permute-start.10 = (bf16[64,2048]{1,0:T(8,128)(2,1)S(1)}, bf16[64,2048]{1,0:T(8,128)(2,1)S(1)}, u32[]{:S(2)}, u32[]{:S(2)}) collective-permute-start(bf16[64,2048]{1,0:T(8,128)(2,1)S(1)} %attention.3.refs_1_.refs_4_.refs_0_), channel_id=1, source_target_pairs={{0,8},{4,12},{8,0},{12,4},{1,9},{5,13},{9,1},{13,5},{2,10},{6,14},... | collective-permute-start | bytes 786440 | tf_op jit(solution)/shard_map/attended_over_ctx/ppermute | solution.py:38
  41.5 0.0 collective-permute-start.9
  41.5 0.0 collective-permute-done.6.refs_1_
  41.5 12.0 %collective-permute-done.8.refs_3_ = bf16[64,2048]{1,0:T(8,128)(2,1)S(1)} collective-permute-done((bf16[64,2048]{1,0:T(8,128)(2,1)S(1)}, bf16[64,2048]{1,0:T(8,128)(2,1)S(1)}, u32[]{:S(2)}, u32[]{:S(2)}) %collective-permute-start.8) | collective-permute-done | bytes 262176 | tf_op jit(solution)/shard_map/attended_over_ctx/ppermute | solution.py:38
  53.5 0.0 slice-done
  53.5 0.0 slice-done.1
  53.5 2.1 %out_product.3 = (bf16[2,64,1792]{2,1,0:T(8,128)(2,1)S(1)}, f32[2,64,1792]{2,1,0:T(8,128)S(1)}) custom-call(bf16[2048,1792]{1,0:T(8,128)(2,1)S(1)} %bitcast.2, bf16[64,2048]{1,0:T(8,128)(2,1)S(1)} %get-tuple-element.33.refs_0_, bf16[64,2048]{1,0:T(8,128)(2,1)S(1)} %collective-permute-done.6.refs_1_, bf16[64,2048]{1,0:T(8,128)(2,1)S(1)} %attended_over_ctx.1.refs_2_, ...), custom_call_target="tpu_custom_call" | custom-call | flops 1024 | bytes 1024 | tf_op jit(solution)/shard_map/out_product/pallas_call | solution.py:260
  55.6 0.0 collective-permute-done.10.refs_2_
  55.7 2.4 %collective-permute-done.9.refs_1_ = bf16[64,2048]{1,0:T(8,128)(2,1)S(1)} collective-permute-done((bf16[64,2048]{1,0:T(8,128)(2,1)S(1)}, bf16[64,2048]{1,0:T(8,128)(2,1)S(1)}, u32[]{:S(2)}, u32[]{:S(2)}) %collective-permute-start.9) | collective-permute-done | bytes 262176 | tf_op jit(solution)/shard_map/attended_over_ctx/ppermute | solution.py:38
  58.1 0.0 collective-permute-start.11
  58.1 1.6 %out_product.4 = (bf16[2,48,1792]{2,1,0:T(8,128)(2,1)S(1)}, f32[2,48,1792]{2,1,0:T(8,128)S(1)}) custom-call(bf16[2048,1792]{1,0:T(8,128)(2,1)S(1)} %bitcast.2, bf16[64,2048]{1,0:T(8,128)(2,1)S(1)} %attention.3.refs_1_.refs_4_.refs_0_, bf16[64,2048]{1,0:T(8,128)(2,1)S(1)} %collective-permute-done.9.refs_1_, bf16[64,2048]{1,0:T(8,128)(2,1)S(1)} %collective-permute-done.10.refs_2_), custom_call_target="tpu_custom_call" | custom-call | flops 1024 | bytes 1024 | tf_op jit(solution)/shard_map/out_product/pallas_call | solution.py:260
  59.7 0.6 collective-permute-start.13
  60.3 0.3 collective-permute-start.17
  60.6 0.0 collective-permute-done.11.received_ref
  60.6 0.1 sum_over_cores.6
  60.7 1.5 %collective-permute-start.12 = (bf16[64,1792]{1,0:T(8,128)(2,1)S(1)}, bf16[64,1792]{1,0:T(8,128)(2,1)S(1)}, u32[]{:S(2)}, u32[]{:S(2)}) collective-permute-start(bf16[64,1792]{1,0:T(8,128)(2,1)S(1)} %get-tuple-element.41), channel_id=1, source_target_pairs={{0,2},{1,3},{2,0},{3,1},{4,6},{5,7},{6,4},{7,5},{8,10},{9,11},{10,... | collective-permute-start | bytes 688136 | tf_op jit(solution)/shard_map/sum_over_x/ppermute | solution.py:38
  62.3 0.0 collective-permute-done.13.received_ref
  62.3 0.1 sum_over_cores.7
  62.3 0.9 %collective-permute-start.14 = (bf16[48,1792]{1,0:T(8,128)(2,1)S(1)}, bf16[48,1792]{1,0:T(8,128)(2,1)S(1)}, u32[]{:S(2)}, u32[]{:S(2)}) collective-permute-start(bf16[48,1792]{1,0:T(8,128)(2,1)S(1)} %get-tuple-element.45), channel_id=1, source_target_pairs={{0,2},{1,3},{2,0},{3,1},{4,6},{5,7},{6,4},{7,5},{8,10},{9,11},{10,... | collective-permute-start | bytes 516104 | tf_op jit(solution)/shard_map/sum_over_x/ppermute | solution.py:38
  63.2 5.4 %collective-permute-done.17.refs_0_ = bf16[64,2048]{1,0:T(8,128)(2,1)S(1)} collective-permute-done((bf16[64,2048]{1,0:T(8,128)(2,1)S(1)}, bf16[64,2048]{1,0:T(8,128)(2,1)S(1)}, u32[]{:S(2)}, u32[]{:S(2)}) %collective-permute-start.17) | collective-permute-done | bytes 262176 | tf_op jit(solution)/shard_map/attended_over_ctx/ppermute | solution.py:38
  68.6 1.4 %out_product.5 = (bf16[2,16,1792]{2,1,0:T(8,128)(2,1)S(1)}, f32[2,16,1792]{2,1,0:T(8,128)S(1)}) custom-call(bf16[2048,1792]{1,0:T(8,128)(2,1)S(1)} %bitcast.2, bf16[64,2048]{1,0:T(8,128)(2,1)S(1)} %collective-permute-done.17.refs_0_), custom_call_target="tpu_custom_call" | custom-call | flops 1024 | bytes 1024 | tf_op jit(solution)/shard_map/out_product/pallas_call | solution.py:260
  70.0 0.0 collective-permute-done.12.refs_1_
  70.0 0.1 collective-permute-start.18
  70.1 1.3 %collective-permute-done.18.received_ref = bf16[2,16,1792]{2,1,0:T(8,128)(2,1)S(1)} collective-permute-done((bf16[2,16,1792]{2,1,0:T(8,128)(2,1)S(1)}, bf16[2,16,1792]{2,1,0:T(8,128)(2,1)S(1)}, u32[]{:S(2)}, u32[]{:S(2)}) %collective-permute-start.18) | collective-permute-done | bytes 114720 | tf_op jit(solution)/shard_map/sum_over_cores/ppermute | solution.py:38
  71.4 0.3 collective-permute-done.14.refs_3_.refs_1_
  71.8 1.5 %collective-permute-start.19 = (bf16[16,1792]{1,0:T(8,128)(2,1)S(1)}, bf16[16,1792]{1,0:T(8,128)(2,1)S(1)}, u32[]{:S(2)}, u32[]{:S(2)}) collective-permute-start(bf16[16,1792]{1,0:T(8,128)(2,1)S(1)} %sum_over_x.4), channel_id=1, source_target_pairs={{0,2},{1,3},{2,0},{3,1},{4,6},{5,7},{6,4},{7,5},{8,10},{9,11},{10,... | collective-permute-start | bytes 172040 | tf_op jit(solution)/shard_map/sum_over_x/ppermute | solution.py:38
  73.3 0.1 sum_over_x.3
  73.3 1.8 %collective-permute-start.15 = (bf16[32,1792]{1,0:T(8,128)(2,1)S(1)}, bf16[32,1792]{1,0:T(8,128)(2,1)S(1)}, u32[]{:S(2)}, u32[]{:S(2)}) collective-permute-start(bf16[32,1792]{1,0:T(8,128)(2,1)S(1)} %get-tuple-element.47), channel_id=1, source_target_pairs={{0,4},{4,0},{8,12},{12,8},{1,5},{5,1},{9,13},{13,9},{2,6},{6,2},{1... | collective-permute-start | bytes 344072 | tf_op jit(solution)/shard_map/columns_over_ctx/ppermute | solution.py:38
  75.1 0.7 collective-permute-start.16
  75.7 0.2 collective-permute-done.19.refs_3_
  76.0 1.9 %collective-permute-start.20 = (bf16[32,1792]{1,0:T(8,128)(2,1)S(1)}, bf16[32,1792]{1,0:T(8,128)(2,1)S(1)}, u32[]{:S(2)}, u32[]{:S(2)}) collective-permute-start(bf16[32,1792]{1,0:T(8,128)(2,1)S(1)} %sum_over_x.5), channel_id=1, source_target_pairs={{0,12},{4,8},{8,4},{12,0},{1,13},{5,9},{9,5},{13,1},{2,14},{6,10},... | collective-permute-start | bytes 344072 | tf_op jit(solution)/shard_map/columns_over_ctx/ppermute | solution.py:38
  77.9 1.2 %collective-permute-done.15.refs_1_ = bf16[32,1792]{1,0:T(8,128)(2,1)S(1)} collective-permute-done((bf16[32,1792]{1,0:T(8,128)(2,1)S(1)}, bf16[32,1792]{1,0:T(8,128)(2,1)S(1)}, u32[]{:S(2)}, u32[]{:S(2)}) %collective-permute-start.15) | collective-permute-done | bytes 114720 | tf_op jit(solution)/shard_map/columns_over_ctx/ppermute | solution.py:38
  79.1 6.6 %collective-permute-done.16.refs_2_ = bf16[32,1792]{1,0:T(8,128)(2,1)S(1)} collective-permute-done((bf16[32,1792]{1,0:T(8,128)(2,1)S(1)}, bf16[32,1792]{1,0:T(8,128)(2,1)S(1)}, u32[]{:S(2)}, u32[]{:S(2)}) %collective-permute-start.16) | collective-permute-done | bytes 114720 | tf_op jit(solution)/shard_map/columns_over_ctx/ppermute | solution.py:38
  85.7 0.0 collective-permute-done.20.refs_3_
  85.7 0.8 output.1
  (10 shorter events, 0.1 us)
Async XLA Ops:
  1.0 14.8 %collective-permute-start = (bf16[576,128]{1,0:T(8,128)(2,1)S(1)}, bf16[576,128]{1,0:T(8,128)(2,1)S(1)}, u32[]{:S(2)}, u32[]{:S(2)}) collective-permute-start(bf16[576,128]{1,0:T(8,128)(2,1)S(1)} %slice_select_fusion), channel_id=1, source_target_pairs={{0,4},{4,0},{8,12},{12,8},{1,5},{5,1},{9,13},{13,9},{2,6},{6,2},{1... | collective-permute-start | bytes 442376 | tf_op jit(solution)/shard_map/keys_over_ctx/ppermute | solution.py:38
  4.1 14.0 %collective-permute-start.1 = (bf16[576,128]{1,0:T(8,128)(2,1)S(1)}, bf16[576,128]{1,0:T(8,128)(2,1)S(1)}, u32[]{:S(2)}, u32[]{:S(2)}) collective-permute-start(bf16[576,128]{1,0:T(8,128)(2,1)S(1)} %slice_select_fusion), channel_id=1, source_target_pairs={{0,8},{4,12},{8,0},{12,4},{1,9},{5,13},{9,1},{13,5},{2,10},{6,14},... | collective-permute-start | bytes 442376 | tf_op jit(solution)/shard_map/keys_over_ctx/ppermute | solution.py:38
  6.7 11.4 %collective-permute-start.2 = (bf16[576,128]{1,0:T(8,128)(2,1)S(1)}, bf16[576,128]{1,0:T(8,128)(2,1)S(1)}, u32[]{:S(2)}, u32[]{:S(2)}) collective-permute-start(bf16[576,128]{1,0:T(8,128)(2,1)S(1)} %slice_select_fusion), channel_id=1, source_target_pairs={{0,12},{4,8},{8,4},{12,0},{1,13},{5,9},{9,5},{13,1},{2,14},{6,10},... | collective-permute-start | bytes 442376 | tf_op jit(solution)/shard_map/keys_over_ctx/ppermute | solution.py:38
  7.3 1.0 %copy-start = (bf16[256,576]{0,1:T(8,128)(2,1)S(1)}, bf16[256,576]{0,1:T(8,128)(2,1)}, u32[]{:S(2)}) copy-start(bf16[256,576]{0,1:T(8,128)(2,1)} %param.7) | copy-start | bytes 884740
  8.3 1.1 %copy-start.1 = (bf16[128,3072]{1,0:T(8,128)(2,1)S(1)}, bf16[128,3072]{1,0:T(8,128)(2,1)}, u32[]{:S(2)}) copy-start(bf16[128,3072]{1,0:T(8,128)(2,1)} %q_hbm.1) | copy-start | bytes 2359300
  9.4 0.7 copy-start.2
  10.1 43.4 %slice-start = ((s8[7340032]{0:T(1024)(128)(4,1)}), s8[3145728]{0:T(1024)(128)(4,1)S(1)}, s32[]{:S(2)}) async-start(s8[7340032]{0:T(1024)(128)(4,1)} %bitcast.1), calls=%async_computation | async-start | bytes 6291456
  15.8 2.8 %collective-permute-start.3 = (bf16[576,128]{1,0:T(8,128)(2,1)S(1)}, bf16[576,128]{1,0:T(8,128)(2,1)S(1)}, u32[]{:S(2)}, u32[]{:S(2)}) collective-permute-start(bf16[576,128]{1,0:T(8,128)(2,1)S(1)} %keys_over_cores.3.refs_1_), channel_id=1, source_target_pairs={{0,1},{1,0},{2,3},{3,2},{4,5},{5,4},{6,7},{7,6},{8,9},{9,8},{10,11... | collective-permute-start | bytes 442376 | tf_op jit(solution)/shard_map/keys_over_cores/ppermute | solution.py:38
  18.1 1.4 %collective-permute-start.4 = (bf16[576,128]{1,0:T(8,128)(2,1)S(1)}, bf16[576,128]{1,0:T(8,128)(2,1)S(1)}, u32[]{:S(2)}, u32[]{:S(2)}) collective-permute-start(bf16[576,128]{1,0:T(8,128)(2,1)S(1)} %keys_over_cores.4.refs_2_), channel_id=1, source_target_pairs={{0,1},{1,0},{2,3},{3,2},{4,5},{5,4},{6,7},{7,6},{8,9},{9,8},{10,11... | collective-permute-start | bytes 442376 | tf_op jit(solution)/shard_map/keys_over_cores/ppermute | solution.py:38
  18.1 1.6 %collective-permute-start.5 = (bf16[576,128]{1,0:T(8,128)(2,1)S(1)}, bf16[576,128]{1,0:T(8,128)(2,1)S(1)}, u32[]{:S(2)}, u32[]{:S(2)}) collective-permute-start(bf16[576,128]{1,0:T(8,128)(2,1)S(1)} %keys_over_cores.5.refs_3_), channel_id=1, source_target_pairs={{0,1},{1,0},{2,3},{3,2},{4,5},{5,4},{6,7},{7,6},{8,9},{9,8},{10,11... | collective-permute-start | bytes 442376 | tf_op jit(solution)/shard_map/keys_over_cores/ppermute | solution.py:38
  19.7 33.9 %slice-start.1 = ((s8[7340032]{0:T(1024)(128)(4,1)}), s8[4194304]{0:T(1024)(128)(4,1)S(1)}, s32[]{:S(2)}) async-start(s8[7340032]{0:T(1024)(128)(4,1)} %bitcast.1), calls=%async_computation.1 | async-start | bytes 8388608
  23.6 15.5 %collective-permute-start.7 = (bf16[64,2048]{1,0:T(8,128)(2,1)S(1)}, bf16[64,2048]{1,0:T(8,128)(2,1)S(1)}, u32[]{:S(2)}, u32[]{:S(2)}) collective-permute-start(bf16[64,2048]{1,0:T(8,128)(2,1)S(1)} %get-tuple-element.33.refs_0_), channel_id=1, source_target_pairs={{0,8},{4,12},{8,0},{12,4},{1,9},{5,13},{9,1},{13,5},{2,10},{6,14},... | collective-permute-start | bytes 786440 | tf_op jit(solution)/shard_map/attended_over_ctx/ppermute | solution.py:38
  26.7 14.8 %collective-permute-start.6 = (bf16[64,2048]{1,0:T(8,128)(2,1)S(1)}, bf16[64,2048]{1,0:T(8,128)(2,1)S(1)}, u32[]{:S(2)}, u32[]{:S(2)}) collective-permute-start(bf16[64,2048]{1,0:T(8,128)(2,1)S(1)} %get-tuple-element.33.refs_0_), channel_id=1, source_target_pairs={{0,4},{4,0},{8,12},{12,8},{1,5},{5,1},{9,13},{13,9},{2,6},{6,2},{1... | collective-permute-start | bytes 786440 | tf_op jit(solution)/shard_map/attended_over_ctx/ppermute | solution.py:38
  39.1 14.5 %collective-permute-start.8 = (bf16[64,2048]{1,0:T(8,128)(2,1)S(1)}, bf16[64,2048]{1,0:T(8,128)(2,1)S(1)}, u32[]{:S(2)}, u32[]{:S(2)}) collective-permute-start(bf16[64,2048]{1,0:T(8,128)(2,1)S(1)} %attended_over_ctx.1.refs_2_), channel_id=1, source_target_pairs={{0,4},{4,0},{8,12},{12,8},{1,5},{5,1},{9,13},{13,9},{2,6},{6,2},{1... | collective-permute-start | bytes 786440 | tf_op jit(solution)/shard_map/attended_over_ctx/ppermute | solution.py:38
  39.1 16.6 %collective-permute-start.10 = (bf16[64,2048]{1,0:T(8,128)(2,1)S(1)}, bf16[64,2048]{1,0:T(8,128)(2,1)S(1)}, u32[]{:S(2)}, u32[]{:S(2)}) collective-permute-start(bf16[64,2048]{1,0:T(8,128)(2,1)S(1)} %attention.3.refs_1_.refs_4_.refs_0_), channel_id=1, source_target_pairs={{0,8},{4,12},{8,0},{12,4},{1,9},{5,13},{9,1},{13,5},{2,10},{6,14},... | collective-permute-start | bytes 786440 | tf_op jit(solution)/shard_map/attended_over_ctx/ppermute | solution.py:38
  41.5 16.6 %collective-permute-start.9 = (bf16[64,2048]{1,0:T(8,128)(2,1)S(1)}, bf16[64,2048]{1,0:T(8,128)(2,1)S(1)}, u32[]{:S(2)}, u32[]{:S(2)}) collective-permute-start(bf16[64,2048]{1,0:T(8,128)(2,1)S(1)} %attention.3.refs_1_.refs_4_.refs_0_), channel_id=1, source_target_pairs={{0,4},{4,0},{8,12},{12,8},{1,5},{5,1},{9,13},{13,9},{2,6},{6,2},{1... | collective-permute-start | bytes 786440 | tf_op jit(solution)/shard_map/attended_over_ctx/ppermute | solution.py:38
  58.1 2.5 %collective-permute-start.11 = (bf16[2,64,1792]{2,1,0:T(8,128)(2,1)S(1)}, bf16[2,64,1792]{2,1,0:T(8,128)(2,1)S(1)}, u32[]{:S(2)}, u32[]{:S(2)}) collective-permute-start(bf16[2,64,1792]{2,1,0:T(8,128)(2,1)S(1)} %sum_over_cores.5), channel_id=1, source_target_pairs={{0,1},{1,0},{2,3},{3,2},{4,5},{5,4},{6,7},{7,6},{8,9},{9,8},{10,11... | collective-permute-start | bytes 1376264 | tf_op jit(solution)/shard_map/sum_over_cores/ppermute | solution.py:38
  59.7 2.5 %collective-permute-start.13 = (bf16[2,48,1792]{2,1,0:T(8,128)(2,1)S(1)}, bf16[2,48,1792]{2,1,0:T(8,128)(2,1)S(1)}, u32[]{:S(2)}, u32[]{:S(2)}) collective-permute-start(bf16[2,48,1792]{2,1,0:T(8,128)(2,1)S(1)} %get-tuple-element.43), channel_id=1, source_target_pairs={{0,1},{1,0},{2,3},{3,2},{4,5},{5,4},{6,7},{7,6},{8,9},{9,8},{10,11... | collective-permute-start | bytes 1032200 | tf_op jit(solution)/shard_map/sum_over_cores/ppermute | solution.py:38
  60.3 8.3 %collective-permute-start.17 = (bf16[64,2048]{1,0:T(8,128)(2,1)S(1)}, bf16[64,2048]{1,0:T(8,128)(2,1)S(1)}, u32[]{:S(2)}, u32[]{:S(2)}) collective-permute-start(bf16[64,2048]{1,0:T(8,128)(2,1)S(1)} %collective-permute-done.10.refs_2_), channel_id=1, source_target_pairs={{0,4},{4,0},{8,12},{12,8},{1,5},{5,1},{9,13},{13,9},{2,6},{6,2},{1... | collective-permute-start | bytes 786440 | tf_op jit(solution)/shard_map/attended_over_ctx/ppermute | solution.py:38
  60.7 9.3 %collective-permute-start.12 = (bf16[64,1792]{1,0:T(8,128)(2,1)S(1)}, bf16[64,1792]{1,0:T(8,128)(2,1)S(1)}, u32[]{:S(2)}, u32[]{:S(2)}) collective-permute-start(bf16[64,1792]{1,0:T(8,128)(2,1)S(1)} %get-tuple-element.41), channel_id=1, source_target_pairs={{0,2},{1,3},{2,0},{3,1},{4,6},{5,7},{6,4},{7,5},{8,10},{9,11},{10,... | collective-permute-start | bytes 688136 | tf_op jit(solution)/shard_map/sum_over_x/ppermute | solution.py:38
  62.3 9.4 %collective-permute-start.14 = (bf16[48,1792]{1,0:T(8,128)(2,1)S(1)}, bf16[48,1792]{1,0:T(8,128)(2,1)S(1)}, u32[]{:S(2)}, u32[]{:S(2)}) collective-permute-start(bf16[48,1792]{1,0:T(8,128)(2,1)S(1)} %get-tuple-element.45), channel_id=1, source_target_pairs={{0,2},{1,3},{2,0},{3,1},{4,6},{5,7},{6,4},{7,5},{8,10},{9,11},{10,... | collective-permute-start | bytes 516104 | tf_op jit(solution)/shard_map/sum_over_x/ppermute | solution.py:38
  70.0 1.4 %collective-permute-start.18 = (bf16[2,16,1792]{2,1,0:T(8,128)(2,1)S(1)}, bf16[2,16,1792]{2,1,0:T(8,128)(2,1)S(1)}, u32[]{:S(2)}, u32[]{:S(2)}) collective-permute-start(bf16[2,16,1792]{2,1,0:T(8,128)(2,1)S(1)} %sum_over_cores.8), channel_id=1, source_target_pairs={{0,1},{1,0},{2,3},{3,2},{4,5},{5,4},{6,7},{7,6},{8,9},{9,8},{10,11... | collective-permute-start | bytes 344072 | tf_op jit(solution)/shard_map/sum_over_cores/ppermute | solution.py:38
  71.8 4.2 %collective-permute-start.19 = (bf16[16,1792]{1,0:T(8,128)(2,1)S(1)}, bf16[16,1792]{1,0:T(8,128)(2,1)S(1)}, u32[]{:S(2)}, u32[]{:S(2)}) collective-permute-start(bf16[16,1792]{1,0:T(8,128)(2,1)S(1)} %sum_over_x.4), channel_id=1, source_target_pairs={{0,2},{1,3},{2,0},{3,1},{4,6},{5,7},{6,4},{7,5},{8,10},{9,11},{10,... | collective-permute-start | bytes 172040 | tf_op jit(solution)/shard_map/sum_over_x/ppermute | solution.py:38
  73.3 5.8 %collective-permute-start.15 = (bf16[32,1792]{1,0:T(8,128)(2,1)S(1)}, bf16[32,1792]{1,0:T(8,128)(2,1)S(1)}, u32[]{:S(2)}, u32[]{:S(2)}) collective-permute-start(bf16[32,1792]{1,0:T(8,128)(2,1)S(1)} %get-tuple-element.47), channel_id=1, source_target_pairs={{0,4},{4,0},{8,12},{12,8},{1,5},{5,1},{9,13},{13,9},{2,6},{6,2},{1... | collective-permute-start | bytes 344072 | tf_op jit(solution)/shard_map/columns_over_ctx/ppermute | solution.py:38
  75.1 10.6 %collective-permute-start.16 = (bf16[32,1792]{1,0:T(8,128)(2,1)S(1)}, bf16[32,1792]{1,0:T(8,128)(2,1)S(1)}, u32[]{:S(2)}, u32[]{:S(2)}) collective-permute-start(bf16[32,1792]{1,0:T(8,128)(2,1)S(1)} %get-tuple-element.48), channel_id=1, source_target_pairs={{0,8},{4,12},{8,0},{12,4},{1,9},{5,13},{9,1},{13,5},{2,10},{6,14},... | collective-permute-start | bytes 344072 | tf_op jit(solution)/shard_map/columns_over_ctx/ppermute | solution.py:38
  76.0 9.7 %collective-permute-start.20 = (bf16[32,1792]{1,0:T(8,128)(2,1)S(1)}, bf16[32,1792]{1,0:T(8,128)(2,1)S(1)}, u32[]{:S(2)}, u32[]{:S(2)}) collective-permute-start(bf16[32,1792]{1,0:T(8,128)(2,1)S(1)} %sum_over_x.5), channel_id=1, source_target_pairs={{0,12},{4,8},{8,4},{12,0},{1,13},{5,9},{9,5},{13,1},{2,14},{6,10},... | collective-permute-start | bytes 344072 | tf_op jit(solution)/shard_map/columns_over_ctx/ppermute | solution.py:38

commit v11 on v10

--- a/solution.py
+++ b/solution.py
@@ -17,8 +17,19 @@
 SUB_ROWS = 256
 LOAD_LIMIT = 44
 MASKED = -1e30
+RAISE_LATE = 20
+RAISE_HANDED = 3
+RAISE_X = 4
 LOG2E = 1.4426950408889634
 SCALE = LOG2E / math.sqrt(HEAD)
+
+
+def cost(microseconds):
+    return pl.CostEstimate(
+        flops=int(1e9 * microseconds), bytes_accessed=int(3e6 * microseconds), transcendentals=0
+    )
+
+
 SHORT = pl.CostEstimate(flops=1024, bytes_accessed=1024, transcendentals=0)
 IN_VMEM = pl.BlockSpec(memory_space=pltpu.VMEM)
 IN_SMEM = pl.BlockSpec(memory_space=pltpu.SMEM)
@@ -42,9 +53,7 @@
     pass
 
 
-def tie(array, after):
-    if not after:
-        return array
+def tie(array, after, lead=SHORT):
     return pl.pallas_call(
         tie_kernel,
         out_shape=jax.ShapeDtypeStruct(array.shape, array.dtype),
@@ -52,21 +61,22 @@
         out_specs=ANYWHERE,
         input_output_aliases={0: 0},
         compiler_params=params(1),
-        cost_estimate=SHORT,
+        cost_estimate=lead,
     )(array, *after)
 
 
-def gather_pieces(own, size, after=()):
+def gather_pieces(own, size, after, lead):
     pieces = {0: own}
     bit = size // 2
     while bit:
         pieces[bit] = exchange(own, "ctx", size, bit)
         bit //= 2
+    pieces[1] = tie(pieces[1], [], lead)
     bit = 1
     while bit < size:
         for offset in range(bit + 1, 2 * bit):
             if offset == bit + 1:
-                pieces[bit] = tie(pieces[bit], after)
+                pieces[bit] = tie(pieces[bit], after, lead)
             pieces[offset] = exchange(pieces[bit], "ctx", size, offset ^ bit)
         bit *= 2
     return [pieces[offset] for offset in range(size)]
@@ -268,7 +278,8 @@
     )(w_out, *pieces, *after)
 
 
-def core_sum_kernel(n_x, kept_ref, received_ref, total_ref, *sent_refs):
+def core_sum_kernel(n_x, after, kept_ref, received_ref, *refs):
+    total_ref, *sent_refs = refs[after:]
     x = lax.axis_index("head") // 2
     for offset in range(n_x):
         summed = kept_ref[x ^ offset] + received_ref[x ^ offset].astype(jnp.float32)
@@ -278,43 +289,43 @@
             total_ref[...] = summed
 
 
-def core_sum(kept, received):
+def core_sum(kept, received, after):
     n_x, rows, columns = kept.shape
     own = jax.ShapeDtypeStruct((rows, columns), jnp.float32)
     sent = jax.ShapeDtypeStruct((rows, columns), jnp.bfloat16)
     out = pl.pallas_call(
-        functools.partial(core_sum_kernel, n_x),
+        functools.partial(core_sum_kernel, n_x, len(after)),
         out_shape=[own] + [sent] * (n_x - 1),
-        in_specs=[IN_VMEM, IN_VMEM],
+        in_specs=[IN_VMEM, IN_VMEM] + [ANYWHERE] * len(after),
         out_specs=[IN_VMEM] * n_x,
         compiler_params=params(4),
         cost_estimate=SHORT,
-    )(kept, received)
+    )(kept, received, *after)
     return out[0], out[1:]
 
 
-def x_sum_kernel(places, *refs):
+def x_sum_kernel(counts, rows, places, *refs):
     sources, refs = [], list(refs)
-    for count, rows, indices in places:
+    for count in counts:
         total = refs.pop(0)[...]
         for _ in range(count):
             total = total + refs.pop(0)[...].astype(jnp.float32)
-        sources.append([total[index * rows : (index + 1) * rows] for index in indices])
-    for out_ref, parts in zip(refs, zip(*sources)):
+        sources.append(total)
+    for out_ref, parts in zip(refs, places):
+        parts = [sources[unit][index * rows : (index + 1) * rows] for unit, index in parts]
         out_ref[...] = jnp.concatenate(parts, axis=0).astype(jnp.bfloat16)
 
 
-def x_sum(sources):
-    columns = sources[0][0].shape[1]
-    block = jax.ShapeDtypeStruct((sum(rows for _, _, rows, _ in sources), columns), jnp.bfloat16)
-    arrays = [array for total, received, _, _ in sources for array in [total, *received]]
-    places = [(len(received), rows, indices) for _, received, rows, indices in sources]
-    outputs = len(sources[0][3])
+def x_sum(sums, rows, places):
+    columns = sums[0][0].shape[1]
+    arrays = [array for total, received in sums for array in [total, *received]]
+    counts = [len(received) for _, received in sums]
+    blocks = [jax.ShapeDtypeStruct((rows * len(parts), columns), jnp.bfloat16) for parts in places]
     return pl.pallas_call(
-        functools.partial(x_sum_kernel, places),
-        out_shape=[block] * outputs,
+        functools.partial(x_sum_kernel, counts, rows, places),
+        out_shape=blocks,
         in_specs=[IN_VMEM] * len(arrays),
-        out_specs=[IN_VMEM] * outputs,
+        out_specs=[IN_VMEM] * len(blocks),
         compiler_params=params(8),
         cost_estimate=SHORT,
     )(*arrays)
@@ -375,43 +386,49 @@
         for chunk in range(1, len(pieces)):
             attended += attention(q_ext[chunk], bias[chunk], w_values, keys, True)
     with jax.named_scope("attended_over_ctx"):
-        gathered = [
-            gather_pieces(own, n_ctx, attended[chunk + 1 : chunk + 2])
-            for chunk, own in enumerate(attended)
-        ]
-    near = [0] + [1 << bit for bit in range(n_ctx.bit_length() - 1)]
-    far = [offset for offset in range(n_ctx) if offset not in near]
-    last = len(pieces) - 1
-    units = [(chunk, list(range(n_ctx))) for chunk in range(last)] + [(last, near), (last, far)]
+        early = gather_pieces(attended[0], n_ctx, attended[1:], SHORT)
+        late = gather_pieces(attended[1], n_ctx, [], cost(RAISE_LATE))
+    powers = [1 << bit for bit in range(n_ctx.bit_length() - 1)]
+    handed = [offset for offset in range(1, n_ctx) if offset not in powers]
+    for offset in handed:
+        late[offset] = tie(late[offset], [late[n_ctx // 2]], cost(RAISE_HANDED))
+    gathered = [early, late]
+    units = [
+        [(0, 0), (1, 0)],
+        [(0, offset) for offset in range(1, n_ctx)],
+        [(1, offset) for offset in powers],
+        [(1, offset) for offset in handed],
+    ]
     sums = []
-    after = attended[1:]
-    crossed = []
-    for unit, (chunk, offsets) in enumerate(units):
+    for unit, members in enumerate(units):
         with jax.named_scope("out_product"):
-            first = after if unit == 0 else []
-            sent, kept = product([gathered[chunk][d] for d in offsets], w_out, n_x, first)
+            sources = [gathered[chunk][offset] for chunk, offset in members]
+            after = [*attended[1:], *sums[0][1]] if unit == 1 else []
+            sent, kept = product(sources, w_out, n_x, after)
         with jax.named_scope("sum_over_cores"):
-            if chunk < last:
-                sent = tie(sent, [gathered[chunk + 1][1], gathered[chunk + 1][n_ctx // 2]])
-            elif offsets is far:
-                sent = tie(sent, [*crossed[0], *after])
-            total, sent = core_sum(kept, exchange(sent, "head", n_head, 1))
-            after = [total]
+            if unit == 3:
+                sent = tie(sent, [sums[2][0]])
+            total, sent = core_sum(kept, exchange(sent, "head", n_head, 1), [])
         with jax.named_scope("sum_over_x"):
-            if offsets is far:
-                sent = [tie(array, crossed[-1]) for array in sent]
-            crossed.append(
-                [exchange(array, "head", n_head, 2 * d) for d, array in enumerate(sent, 1)]
-            )
-        sums.append((total, crossed[-1], pieces[chunk]))
+            if unit == 3:
+                before = sums[1][1]
+                sent = [tie(array, before, cost(RAISE_X)) for array in sent]
+            crossed = [exchange(array, "head", n_head, 2 * d) for d, array in enumerate(sent, 1)]
+        sums.append((total, crossed))
     blocks = {}
-    for group, ending in ((near, sums[-2]), (far, sums[-1])):
+    for offsets, last in (([0], 0), (powers, 2), (handed, 3)):
         with jax.named_scope("sum_over_x"):
-            sources = [(*part, group) for part in sums[:-2]] + [(*ending, range(len(group)))]
-            blocks.update(zip(group, x_sum(sources)))
+            sources = [sums[0]] if offsets == [0] else [sums[1], sums[last]]
+            places = []
+            for offset in offsets:
+                parts = [(0, 0), (0, 1)]
+                if offset:
+                    parts = [(0, offset - 1), (1, units[last].index((1, offset)))]
+                places.append(parts)
+            found = x_sum(sources, pieces[0], places)
         with jax.named_scope("columns_over_ctx"):
-            for d in reversed(group):
-                blocks[d] = exchange(blocks[d], "ctx", n_ctx, d) if d else blocks[d]
+            for offset, block in reversed(list(zip(offsets, found))):
+                blocks[offset] = exchange(block, "ctx", n_ctx, offset) if offset else block
     with jax.named_scope("output"):
         return place_columns([blocks[d] for d in range(n_ctx)])
 

time: 86.7 us -> 87.8 us (1.013)
  starting transfers between devices: 21 us -> 23 us
  waiting for transfers between devices: 41.4 us -> 40.2 us
    ppermute x21 -> x23, starting transfers between devices: 21 us -> 23 us  [exchange(): return lax.ppermute(array, axis, [(i, i ^ bit) for i in range(size)])]
    ppermute x21 -> x23, waiting for transfers between devices: 41.4 us -> 40.2 us  [exchange(): return lax.ppermute(array, axis, [(i, i ^ bit) for i in range(size)])]
    pallas_call x3 -> x4, Pallas kernels: 5.1 us -> 5.28 us  [product(): pl.pallas_call(functools.partial(product_kernel, count, n_x, len(after)),...]
  transfers between devices with their start and end apart: 21 -> 23, of which waited for: 12 -> 12; matrix products, arithmetic and copies ran while one was open for 0% -> 0% of each run, Pallas kernels for 17% -> 17%
where the time goes in v11:
time: 87.8 us; the launch traced here: 87.6 us
  waiting for transfers between devices  40.2 us (46%)
  starting transfers between devices  23 us (26%)
  Pallas kernels  19.8 us (23%)
  local copies, waits for them, and re-layouts  2.75 us (3%)
  other arithmetic  1 us (1%)
    ppermute x23, waiting for transfers between devices, exchange(): return lax.ppermute(array, axis, [(i, i ^ bit) for i in range(size)])  40.2 us
    ppermute x23, starting transfers between devices, exchange(): return lax.ppermute(array, axis, [(i, i ^ bit) for i in range(size)])  23 us
    pallas_call x2, Pallas kernels, attention(): pl.pallas_call(functools.partial(attention_kernel, 0 if gathered else len...  7.71 us
    pallas_call x1, Pallas kernels, load(): pl.pallas_call(functools.partial(load_kernel, owners, pieces, cache_rows)...  5.66 us
    pallas_call x4, Pallas kernels, product(): pl.pallas_call(functools.partial(product_kernel, count, n_x, len(after)),...  5.28 us
    unnamed x10, local copies, waits for them, and re-layouts  2.75 us
  transfers between devices with their start and end apart: 23, of which 12 were waited for; matrix products, arithmetic and copies ran while one was open for 0% of the time, Pallas kernels for 17%

profile of v11, /device:TPU:0, one launch (start us, length us, event | category | flops | bytes accessed | tf_op | source)
XLA Modules:
  0.0 87.6 jit_solution(2196726665880220340)
XLA Ops:
  0.0 1.0 %slice_select_fusion = bf16[576,128]{1,0:T(8,128)(2,1)S(1)} fusion(bf16[576,256]{1,0:T(8,128)(2,1)} %bitcast.3, pred[]{:T(512)S(6)} %eq.5), kind=kLoop, calls=%fused_computation | loop fusion | flops 73728 | bytes 442369 | tf_op jit(solution)/shard_map/keys_over_ctx/jit(_where)/select_n | solution.py:374
  1.0 3.1 %collective-permute-start = (bf16[576,128]{1,0:T(8,128)(2,1)S(1)}, bf16[576,128]{1,0:T(8,128)(2,1)S(1)}, u32[]{:S(2)}, u32[]{:S(2)}) collective-permute-start(bf16[576,128]{1,0:T(8,128)(2,1)S(1)} %slice_select_fusion), channel_id=1, source_target_pairs={{0,4},{4,0},{8,12},{12,8},{1,5},{5,1},{9,13},{13,9},{2,6},{6,2},{1... | collective-permute-start | bytes 442376 | tf_op jit(solution)/shard_map/keys_over_ctx/ppermute | solution.py:49
  4.1 2.6 %collective-permute-start.1 = (bf16[576,128]{1,0:T(8,128)(2,1)S(1)}, bf16[576,128]{1,0:T(8,128)(2,1)S(1)}, u32[]{:S(2)}, u32[]{:S(2)}) collective-permute-start(bf16[576,128]{1,0:T(8,128)(2,1)S(1)} %slice_select_fusion), channel_id=1, source_target_pairs={{0,8},{4,12},{8,0},{12,4},{1,9},{5,13},{9,1},{13,5},{2,10},{6,14},... | collective-permute-start | bytes 442376 | tf_op jit(solution)/shard_map/keys_over_ctx/ppermute | solution.py:49
  6.7 0.0 collective-permute-start.2
  7.3 0.0 copy-start
  7.3 1.0 %copy-done = bf16[256,576]{0,1:T(8,128)(2,1)S(1)} copy-done((bf16[256,576]{0,1:T(8,128)(2,1)S(1)}, bf16[256,576]{0,1:T(8,128)(2,1)}, u32[]{:S(2)}) %copy-start) | copy-done | bytes 294936
  8.3 0.0 copy-start.1
  8.3 1.1 %copy-done.1 = bf16[128,3072]{1,0:T(8,128)(2,1)S(1)} copy-done((bf16[128,3072]{1,0:T(8,128)(2,1)S(1)}, bf16[128,3072]{1,0:T(8,128)(2,1)}, u32[]{:S(2)}) %copy-start.1) | copy-done | bytes 786456
  9.4 0.7 copy-done.2
  10.1 5.7 %load.1 = (bf16[16,64,576]{2,1,0:T(8,128)(2,1)S(1)}, bf16[16,64,576]{2,1,0:T(8,128)(2,1)S(1)}, f32[64,1024]{1,0:T(8,128)S(1)}, f32[64,1024]{1,0:T(8,128)S(1)}, b...) custom-call(s32[4]{0:T(128)S(1)} %copy-done.2, s32[1]{0:T(128)S(6)} %copy.27.prefix_ref, ...), custom_call_target="tpu_custom_call" | custom-call | flops 1024 | bytes 1024 | tf_op jit(solution)/shard_map/load/pallas_call | solution.py:141
  15.8 0.0 collective-permute-done.refs_0_
  15.8 0.1 collective-permute-start.3
  15.9 2.2 %collective-permute-done.1.refs_0_ = bf16[576,128]{1,0:T(8,128)(2,1)S(1)} collective-permute-done((bf16[576,128]{1,0:T(8,128)(2,1)S(1)}, bf16[576,128]{1,0:T(8,128)(2,1)S(1)}, u32[]{:S(2)}, u32[]{:S(2)}) %collective-permute-start.1) | collective-permute-done | bytes 147488 | tf_op jit(solution)/shard_map/keys_over_ctx/ppermute | solution.py:49
  18.1 0.0 collective-permute-start.4
  18.1 0.0 collective-permute-done.2.refs_0_
  18.1 0.5 collective-permute-start.5
  18.6 0.0 collective-permute-done.3.refs_4_
  18.6 0.9 collective-permute-done.4.refs_5_
  19.5 0.2 collective-permute-done.5.refs_6_
  19.7 3.9 %attention.2 = (bf16[64,2048]{1,0:T(8,128)(2,1)S(1)}, bf16[576,1024]{1,0:T(8,128)(2,1)S(1)}, bf16[1024,512]{1,0:T(8,128)(2,1)S(1)}) custom-call(bf16[16,64,576]{2,1,0:T(8,128)(2,1)S(1)} %get-tuple-element.32.q_ref, f32[64,1024]{1,0:T(8,128)S(1)} %get-tuple-element.33.bias_ref, bf16[16,512,128]{2,1,0:T(8,128)(2,1)S(1)} %get-tuple-element.34.value_ref, ...), custom_call_target="tpu_custom_call" | custom-call | flops 1024 | bytes 1024 | tf_op jit(solution)/shard_map/attention/pallas_call | solution.py:236
  23.6 3.2 %collective-permute-start.9 = (bf16[64,2048]{1,0:T(8,128)(2,1)S(1)}, bf16[64,2048]{1,0:T(8,128)(2,1)S(1)}, u32[]{:S(2)}, u32[]{:S(2)}) collective-permute-start(bf16[64,2048]{1,0:T(8,128)(2,1)S(1)} %get-tuple-element.36.refs_0_), channel_id=1, source_target_pairs={{0,8},{4,12},{8,0},{12,4},{1,9},{5,13},{9,1},{13,5},{2,10},{6,14},... | collective-permute-start | bytes 786440 | tf_op jit(solution)/shard_map/attended_over_ctx/ppermute | solution.py:49
  26.7 3.8 %attention.3.refs_1_.refs_3_ = bf16[64,2048]{1,0:T(8,128)(2,1)S(1)} custom-call(bf16[16,64,576]{2,1,0:T(8,128)(2,1)S(1)} %get-tuple-element.37.q_ref, f32[64,1024]{1,0:T(8,128)S(1)} %get-tuple-element.38.bias_ref, bf16[16,512,128]{2,1,0:T(8,128)(2,1)S(1)} %get-tuple-element.34.value_ref, bf16[576,1024]{1,0:T(8,128)(2,1)S(1)} %get-tuple-element.39.refs_0_, ...), custom_call_target="tpu_custom_call" | custom-call | flops 1024 | bytes 1024 | tf_op jit(solution)/shard_map/attention/pallas_call | solution.py:236
  30.6 0.1 collective-permute-start.14
  30.6 0.0 slice-done
  30.7 0.0 slice-done.1
  30.7 1.1 %out_product.4 = (bf16[2,32,1792]{2,1,0:T(8,128)(2,1)S(1)}, f32[2,32,1792]{2,1,0:T(8,128)S(1)}) custom-call(bf16[2048,1792]{1,0:T(8,128)(2,1)S(1)} %bitcast.2, bf16[64,2048]{1,0:T(8,128)(2,1)S(1)} %get-tuple-element.36.refs_0_, bf16[64,2048]{1,0:T(8,128)(2,1)S(1)} %attention.3.refs_1_.refs_3_), custom_call_target="tpu_custom_call" | custom-call | flops 1024 | bytes 1024 | tf_op jit(solution)/shard_map/out_product/pallas_call | solution.py:270
  31.8 0.1 collective-permute-start.6
  31.9 1.9 %collective-permute-start.13 = (bf16[64,2048]{1,0:T(8,128)(2,1)S(1)}, bf16[64,2048]{1,0:T(8,128)(2,1)S(1)}, u32[]{:S(2)}, u32[]{:S(2)}) collective-permute-start(bf16[64,2048]{1,0:T(8,128)(2,1)S(1)} %attention.3.refs_1_.refs_3_), channel_id=1, source_target_pairs={{0,4},{4,0},{8,12},{12,8},{1,5},{5,1},{9,13},{13,9},{2,6},{6,2},{1... | collective-permute-start | bytes 786440 | tf_op jit(solution)/shard_map/attended_over_ctx/ppermute | solution.py:49
  33.8 0.1 collective-permute-start.8
  34.0 0.0 collective-permute-done.6.received_ref
  34.0 1.6 %collective-permute-start.7 = (bf16[32,1792]{1,0:T(8,128)(2,1)S(1)}, bf16[32,1792]{1,0:T(8,128)(2,1)S(1)}, u32[]{:S(2)}, u32[]{:S(2)}) collective-permute-start(bf16[32,1792]{1,0:T(8,128)(2,1)S(1)} %get-tuple-element.44), channel_id=1, source_target_pairs={{0,2},{1,3},{2,0},{3,1},{4,6},{5,7},{6,4},{7,5},{8,10},{9,11},{10,... | collective-permute-start | bytes 344072 | tf_op jit(solution)/shard_map/sum_over_x/ppermute | solution.py:49
  35.6 9.6 %collective-permute-done.9.refs_0_ = bf16[64,2048]{1,0:T(8,128)(2,1)S(1)} collective-permute-done((bf16[64,2048]{1,0:T(8,128)(2,1)S(1)}, bf16[64,2048]{1,0:T(8,128)(2,1)S(1)}, u32[]{:S(2)}, u32[]{:S(2)}) %collective-permute-start.9) | collective-permute-done | bytes 262176 | tf_op jit(solution)/shard_map/attended_over_ctx/ppermute | solution.py:49
  45.1 0.0 collective-permute-start.10
  45.2 5.2 %collective-permute-done.14.refs_0_ = bf16[64,2048]{1,0:T(8,128)(2,1)S(1)} collective-permute-done((bf16[64,2048]{1,0:T(8,128)(2,1)S(1)}, bf16[64,2048]{1,0:T(8,128)(2,1)S(1)}, u32[]{:S(2)}, u32[]{:S(2)}) %collective-permute-start.14) | collective-permute-done | bytes 262176 | tf_op jit(solution)/shard_map/attended_over_ctx/ppermute | solution.py:49
  50.3 0.0 collective-permute-start.19
  50.3 6.4 %collective-permute-done.8.refs_0_ = bf16[64,2048]{1,0:T(8,128)(2,1)S(1)} collective-permute-done((bf16[64,2048]{1,0:T(8,128)(2,1)S(1)}, bf16[64,2048]{1,0:T(8,128)(2,1)S(1)}, u32[]{:S(2)}, u32[]{:S(2)}) %collective-permute-start.8) | collective-permute-done | bytes 262176 | tf_op jit(solution)/shard_map/attended_over_ctx/ppermute | solution.py:49
  56.7 0.0 collective-permute-done.7.refs_1_.refs_4_
  56.7 5.6 %collective-permute-done.10.refs_2_ = bf16[64,2048]{1,0:T(8,128)(2,1)S(1)} collective-permute-done((bf16[64,2048]{1,0:T(8,128)(2,1)S(1)}, bf16[64,2048]{1,0:T(8,128)(2,1)S(1)}, u32[]{:S(2)}, u32[]{:S(2)}) %collective-permute-start.10) | collective-permute-done | bytes 262176 | tf_op jit(solution)/shard_map/attended_over_ctx/ppermute | solution.py:49
  62.4 1.6 %out_product.5 = (bf16[2,48,1792]{2,1,0:T(8,128)(2,1)S(1)}, f32[2,48,1792]{2,1,0:T(8,128)S(1)}) custom-call(bf16[2048,1792]{1,0:T(8,128)(2,1)S(1)} %bitcast.2, bf16[64,2048]{1,0:T(8,128)(2,1)S(1)} %attended_over_ctx.4.refs_0_, bf16[64,2048]{1,0:T(8,128)(2,1)S(1)} %attended_over_ctx.5.refs_1_, bf16[64,2048]{1,0:T(8,128)(2,1)S(1)} %collective-permute-done.10.refs_2_, ...), custom_call_target="tpu_custom_call" | custom-call | flops 1024 | bytes 1024 | tf_op jit(solution)/shard_map/out_product/pallas_call | solution.py:270
  64.0 0.1 collective-permute-start.11
  64.1 0.0 collective-permute-done.13.refs_0_
  64.1 1.1 %out_product.6 = (bf16[2,32,1792]{2,1,0:T(8,128)(2,1)S(1)}, f32[2,32,1792]{2,1,0:T(8,128)S(1)}) custom-call(bf16[2048,1792]{1,0:T(8,128)(2,1)S(1)} %bitcast.2, bf16[64,2048]{1,0:T(8,128)(2,1)S(1)} %attended_over_ctx.6.refs_0_, bf16[64,2048]{1,0:T(8,128)(2,1)S(1)} %attended_over_ctx.7.refs_1_), custom_call_target="tpu_custom_call" | custom-call | flops 1024 | bytes 1024 | tf_op jit(solution)/shard_map/out_product/pallas_call | solution.py:270
  65.2 0.5 collective-permute-start.15
  65.8 0.0 collective-permute-done.11.received_ref
  65.8 0.1 sum_over_cores.6
  65.9 1.5 %collective-permute-start.12 = (bf16[48,1792]{1,0:T(8,128)(2,1)S(1)}, bf16[48,1792]{1,0:T(8,128)(2,1)S(1)}, u32[]{:S(2)}, u32[]{:S(2)}) collective-permute-start(bf16[48,1792]{1,0:T(8,128)(2,1)S(1)} %get-tuple-element.48), channel_id=1, source_target_pairs={{0,2},{1,3},{2,0},{3,1},{4,6},{5,7},{6,4},{7,5},{8,10},{9,11},{10,... | collective-permute-start | bytes 516104 | tf_op jit(solution)/shard_map/sum_over_x/ppermute | solution.py:49
  67.4 0.3 collective-permute-done.19.refs_0_
  67.7 0.0 collective-permute-done.15.received_ref
  67.7 0.1 sum_over_cores.7
  67.7 1.4 %out_product.7 = (bf16[2,16,1792]{2,1,0:T(8,128)(2,1)S(1)}, f32[2,16,1792]{2,1,0:T(8,128)S(1)}) custom-call(bf16[2048,1792]{1,0:T(8,128)(2,1)S(1)} %bitcast.2, bf16[64,2048]{1,0:T(8,128)(2,1)S(1)} %shard_map.64.refs_0_), custom_call_target="tpu_custom_call" | custom-call | flops 1024 | bytes 1024 | tf_op jit(solution)/shard_map/out_product/pallas_call | solution.py:270
  69.1 0.1 collective-permute-start.20
  69.2 1.6 %collective-permute-start.16 = (bf16[32,1792]{1,0:T(8,128)(2,1)S(1)}, bf16[32,1792]{1,0:T(8,128)(2,1)S(1)}, u32[]{:S(2)}, u32[]{:S(2)}) collective-permute-start(bf16[32,1792]{1,0:T(8,128)(2,1)S(1)} %get-tuple-element.52), channel_id=1, source_target_pairs={{0,2},{1,3},{2,0},{3,1},{4,6},{5,7},{6,4},{7,5},{8,10},{9,11},{10,... | collective-permute-start | bytes 344072 | tf_op jit(solution)/shard_map/sum_over_x/ppermute | solution.py:49
  70.8 0.0 collective-permute-done.20.received_ref
  70.8 1.5 %collective-permute-done.12.refs_1_ = bf16[48,1792]{1,0:T(8,128)(2,1)S(1)} collective-permute-done((bf16[48,1792]{1,0:T(8,128)(2,1)S(1)}, bf16[48,1792]{1,0:T(8,128)(2,1)S(1)}, u32[]{:S(2)}, u32[]{:S(2)}) %collective-permute-start.12) | collective-permute-done | bytes 172064 | tf_op jit(solution)/shard_map/sum_over_x/ppermute | solution.py:49
  72.3 1.5 %collective-permute-start.21 = (bf16[16,1792]{1,0:T(8,128)(2,1)S(1)}, bf16[16,1792]{1,0:T(8,128)(2,1)S(1)}, u32[]{:S(2)}, u32[]{:S(2)}) collective-permute-start(bf16[16,1792]{1,0:T(8,128)(2,1)S(1)} %sum_over_x.6), channel_id=1, source_target_pairs={{0,2},{1,3},{2,0},{3,1},{4,6},{5,7},{6,4},{7,5},{8,10},{9,11},{10,... | collective-permute-start | bytes 172040 | tf_op jit(solution)/shard_map/sum_over_x/ppermute | solution.py:49
  73.8 1.5 %collective-permute-done.16.refs_3_ = bf16[32,1792]{1,0:T(8,128)(2,1)S(1)} collective-permute-done((bf16[32,1792]{1,0:T(8,128)(2,1)S(1)}, bf16[32,1792]{1,0:T(8,128)(2,1)S(1)}, u32[]{:S(2)}, u32[]{:S(2)}) %collective-permute-start.16) | collective-permute-done | bytes 114720 | tf_op jit(solution)/shard_map/sum_over_x/ppermute | solution.py:49
  75.3 0.1 collective-permute-start.17
  75.3 2.5 %collective-permute-start.18 = (bf16[32,1792]{1,0:T(8,128)(2,1)S(1)}, bf16[32,1792]{1,0:T(8,128)(2,1)S(1)}, u32[]{:S(2)}, u32[]{:S(2)}) collective-permute-start(bf16[32,1792]{1,0:T(8,128)(2,1)S(1)} %get-tuple-element.54), channel_id=1, source_target_pairs={{0,8},{4,12},{8,0},{12,4},{1,9},{5,13},{9,1},{13,5},{2,10},{6,14},... | collective-permute-start | bytes 344072 | tf_op jit(solution)/shard_map/columns_over_ctx/ppermute | solution.py:49
  77.9 0.0 collective-permute-done.21.refs_3_
  77.9 1.9 %collective-permute-start.22 = (bf16[32,1792]{1,0:T(8,128)(2,1)S(1)}, bf16[32,1792]{1,0:T(8,128)(2,1)S(1)}, u32[]{:S(2)}, u32[]{:S(2)}) collective-permute-start(bf16[32,1792]{1,0:T(8,128)(2,1)S(1)} %sum_over_x.7), channel_id=1, source_target_pairs={{0,12},{4,8},{8,4},{12,0},{1,13},{5,9},{9,5},{13,1},{2,14},{6,10},... | collective-permute-start | bytes 344072 | tf_op jit(solution)/shard_map/columns_over_ctx/ppermute | solution.py:49
  79.8 1.2 %collective-permute-done.17.refs_1_ = bf16[32,1792]{1,0:T(8,128)(2,1)S(1)} collective-permute-done((bf16[32,1792]{1,0:T(8,128)(2,1)S(1)}, bf16[32,1792]{1,0:T(8,128)(2,1)S(1)}, u32[]{:S(2)}, u32[]{:S(2)}) %collective-permute-start.17) | collective-permute-done | bytes 114720 | tf_op jit(solution)/shard_map/columns_over_ctx/ppermute | solution.py:49
  81.1 5.7 %collective-permute-done.18.refs_2_ = bf16[32,1792]{1,0:T(8,128)(2,1)S(1)} collective-permute-done((bf16[32,1792]{1,0:T(8,128)(2,1)S(1)}, bf16[32,1792]{1,0:T(8,128)(2,1)S(1)}, u32[]{:S(2)}, u32[]{:S(2)}) %collective-permute-start.18) | collective-permute-done | bytes 114720 | tf_op jit(solution)/shard_map/columns_over_ctx/ppermute | solution.py:49
  86.8 0.0 collective-permute-done.22.refs_3_
  86.8 0.8 output.1
  (19 shorter events, 0.2 us)
Async XLA Ops:
  1.0 14.8 %collective-permute-start = (bf16[576,128]{1,0:T(8,128)(2,1)S(1)}, bf16[576,128]{1,0:T(8,128)(2,1)S(1)}, u32[]{:S(2)}, u32[]{:S(2)}) collective-permute-start(bf16[576,128]{1,0:T(8,128)(2,1)S(1)} %slice_select_fusion), channel_id=1, source_target_pairs={{0,4},{4,0},{8,12},{12,8},{1,5},{5,1},{9,13},{13,9},{2,6},{6,2},{1... | collective-permute-start | bytes 442376 | tf_op jit(solution)/shard_map/keys_over_ctx/ppermute | solution.py:49
  4.1 14.0 %collective-permute-start.1 = (bf16[576,128]{1,0:T(8,128)(2,1)S(1)}, bf16[576,128]{1,0:T(8,128)(2,1)S(1)}, u32[]{:S(2)}, u32[]{:S(2)}) collective-permute-start(bf16[576,128]{1,0:T(8,128)(2,1)S(1)} %slice_select_fusion), channel_id=1, source_target_pairs={{0,8},{4,12},{8,0},{12,4},{1,9},{5,13},{9,1},{13,5},{2,10},{6,14},... | collective-permute-start | bytes 442376 | tf_op jit(solution)/shard_map/keys_over_ctx/ppermute | solution.py:49
  6.7 11.4 %collective-permute-start.2 = (bf16[576,128]{1,0:T(8,128)(2,1)S(1)}, bf16[576,128]{1,0:T(8,128)(2,1)S(1)}, u32[]{:S(2)}, u32[]{:S(2)}) collective-permute-start(bf16[576,128]{1,0:T(8,128)(2,1)S(1)} %slice_select_fusion), channel_id=1, source_target_pairs={{0,12},{4,8},{8,4},{12,0},{1,13},{5,9},{9,5},{13,1},{2,14},{6,10},... | collective-permute-start | bytes 442376 | tf_op jit(solution)/shard_map/keys_over_ctx/ppermute | solution.py:49
  7.3 1.0 %copy-start = (bf16[256,576]{0,1:T(8,128)(2,1)S(1)}, bf16[256,576]{0,1:T(8,128)(2,1)}, u32[]{:S(2)}) copy-start(bf16[256,576]{0,1:T(8,128)(2,1)} %param.7) | copy-start | bytes 884740
  8.3 1.1 %copy-start.1 = (bf16[128,3072]{1,0:T(8,128)(2,1)S(1)}, bf16[128,3072]{1,0:T(8,128)(2,1)}, u32[]{:S(2)}) copy-start(bf16[128,3072]{1,0:T(8,128)(2,1)} %q_hbm.1) | copy-start | bytes 2359300
  9.4 0.7 copy-start.2
  10.1 20.6 %slice-start = ((s8[7340032]{0:T(1024)(128)(4,1)}), s8[3145728]{0:T(1024)(128)(4,1)S(1)}, s32[]{:S(2)}) async-start(s8[7340032]{0:T(1024)(128)(4,1)} %bitcast.1), calls=%async_computation | async-start | bytes 6291456
  15.8 2.8 %collective-permute-start.3 = (bf16[576,128]{1,0:T(8,128)(2,1)S(1)}, bf16[576,128]{1,0:T(8,128)(2,1)S(1)}, u32[]{:S(2)}, u32[]{:S(2)}) collective-permute-start(bf16[576,128]{1,0:T(8,128)(2,1)S(1)} %keys_over_cores.3.refs_1_), channel_id=1, source_target_pairs={{0,1},{1,0},{2,3},{3,2},{4,5},{5,4},{6,7},{7,6},{8,9},{9,8},{10,11... | collective-permute-start | bytes 442376 | tf_op jit(solution)/shard_map/keys_over_cores/ppermute | solution.py:49
  18.1 1.4 %collective-permute-start.4 = (bf16[576,128]{1,0:T(8,128)(2,1)S(1)}, bf16[576,128]{1,0:T(8,128)(2,1)S(1)}, u32[]{:S(2)}, u32[]{:S(2)}) collective-permute-start(bf16[576,128]{1,0:T(8,128)(2,1)S(1)} %keys_over_cores.4.refs_2_), channel_id=1, source_target_pairs={{0,1},{1,0},{2,3},{3,2},{4,5},{5,4},{6,7},{7,6},{8,9},{9,8},{10,11... | collective-permute-start | bytes 442376 | tf_op jit(solution)/shard_map/keys_over_cores/ppermute | solution.py:49
  18.1 1.6 %collective-permute-start.5 = (bf16[576,128]{1,0:T(8,128)(2,1)S(1)}, bf16[576,128]{1,0:T(8,128)(2,1)S(1)}, u32[]{:S(2)}, u32[]{:S(2)}) collective-permute-start(bf16[576,128]{1,0:T(8,128)(2,1)S(1)} %keys_over_cores.5.refs_3_), channel_id=1, source_target_pairs={{0,1},{1,0},{2,3},{3,2},{4,5},{5,4},{6,7},{7,6},{8,9},{9,8},{10,11... | collective-permute-start | bytes 442376 | tf_op jit(solution)/shard_map/keys_over_cores/ppermute | solution.py:49
  19.7 11.0 %slice-start.1 = ((s8[7340032]{0:T(1024)(128)(4,1)}), s8[4194304]{0:T(1024)(128)(4,1)S(1)}, s32[]{:S(2)}) async-start(s8[7340032]{0:T(1024)(128)(4,1)} %bitcast.1), calls=%async_computation.1 | async-start | bytes 8388608
  23.6 21.6 %collective-permute-start.9 = (bf16[64,2048]{1,0:T(8,128)(2,1)S(1)}, bf16[64,2048]{1,0:T(8,128)(2,1)S(1)}, u32[]{:S(2)}, u32[]{:S(2)}) collective-permute-start(bf16[64,2048]{1,0:T(8,128)(2,1)S(1)} %get-tuple-element.36.refs_0_), channel_id=1, source_target_pairs={{0,8},{4,12},{8,0},{12,4},{1,9},{5,13},{9,1},{13,5},{2,10},{6,14},... | collective-permute-start | bytes 786440 | tf_op jit(solution)/shard_map/attended_over_ctx/ppermute | solution.py:49
  30.6 19.7 %collective-permute-start.14 = (bf16[64,2048]{1,0:T(8,128)(2,1)S(1)}, bf16[64,2048]{1,0:T(8,128)(2,1)S(1)}, u32[]{:S(2)}, u32[]{:S(2)}) collective-permute-start(bf16[64,2048]{1,0:T(8,128)(2,1)S(1)} %attention.3.refs_1_.refs_3_), channel_id=1, source_target_pairs={{0,8},{4,12},{8,0},{12,4},{1,9},{5,13},{9,1},{13,5},{2,10},{6,14},... | collective-permute-start | bytes 786440 | tf_op jit(solution)/shard_map/attended_over_ctx/ppermute | solution.py:49
  31.8 2.2 %collective-permute-start.6 = (bf16[2,32,1792]{2,1,0:T(8,128)(2,1)S(1)}, bf16[2,32,1792]{2,1,0:T(8,128)(2,1)S(1)}, u32[]{:S(2)}, u32[]{:S(2)}) collective-permute-start(bf16[2,32,1792]{2,1,0:T(8,128)(2,1)S(1)} %get-tuple-element.42), channel_id=1, source_target_pairs={{0,1},{1,0},{2,3},{3,2},{4,5},{5,4},{6,7},{7,6},{8,9},{9,8},{10,11... | collective-permute-start | bytes 688136 | tf_op jit(solution)/shard_map/sum_over_cores/ppermute | solution.py:49
  31.9 32.2 %collective-permute-start.13 = (bf16[64,2048]{1,0:T(8,128)(2,1)S(1)}, bf16[64,2048]{1,0:T(8,128)(2,1)S(1)}, u32[]{:S(2)}, u32[]{:S(2)}) collective-permute-start(bf16[64,2048]{1,0:T(8,128)(2,1)S(1)} %attention.3.refs_1_.refs_3_), channel_id=1, source_target_pairs={{0,4},{4,0},{8,12},{12,8},{1,5},{5,1},{9,13},{13,9},{2,6},{6,2},{1... | collective-permute-start | bytes 786440 | tf_op jit(solution)/shard_map/attended_over_ctx/ppermute | solution.py:49
  33.8 22.9 %collective-permute-start.8 = (bf16[64,2048]{1,0:T(8,128)(2,1)S(1)}, bf16[64,2048]{1,0:T(8,128)(2,1)S(1)}, u32[]{:S(2)}, u32[]{:S(2)}) collective-permute-start(bf16[64,2048]{1,0:T(8,128)(2,1)S(1)} %get-tuple-element.36.refs_0_), channel_id=1, source_target_pairs={{0,4},{4,0},{8,12},{12,8},{1,5},{5,1},{9,13},{13,9},{2,6},{6,2},{1... | collective-permute-start | bytes 786440 | tf_op jit(solution)/shard_map/attended_over_ctx/ppermute | solution.py:49
  34.0 22.7 %collective-permute-start.7 = (bf16[32,1792]{1,0:T(8,128)(2,1)S(1)}, bf16[32,1792]{1,0:T(8,128)(2,1)S(1)}, u32[]{:S(2)}, u32[]{:S(2)}) collective-permute-start(bf16[32,1792]{1,0:T(8,128)(2,1)S(1)} %get-tuple-element.44), channel_id=1, source_target_pairs={{0,2},{1,3},{2,0},{3,1},{4,6},{5,7},{6,4},{7,5},{8,10},{9,11},{10,... | collective-permute-start | bytes 344072 | tf_op jit(solution)/shard_map/sum_over_x/ppermute | solution.py:49
  45.1 17.2 %collective-permute-start.10 = (bf16[64,2048]{1,0:T(8,128)(2,1)S(1)}, bf16[64,2048]{1,0:T(8,128)(2,1)S(1)}, u32[]{:S(2)}, u32[]{:S(2)}) collective-permute-start(bf16[64,2048]{1,0:T(8,128)(2,1)S(1)} %attended_over_ctx.5.refs_1_), channel_id=1, source_target_pairs={{0,4},{4,0},{8,12},{12,8},{1,5},{5,1},{9,13},{13,9},{2,6},{6,2},{1... | collective-permute-start | bytes 786440 | tf_op jit(solution)/shard_map/attended_over_ctx/ppermute | solution.py:49
  50.3 17.4 %collective-permute-start.19 = (bf16[64,2048]{1,0:T(8,128)(2,1)S(1)}, bf16[64,2048]{1,0:T(8,128)(2,1)S(1)}, u32[]{:S(2)}, u32[]{:S(2)}) collective-permute-start(bf16[64,2048]{1,0:T(8,128)(2,1)S(1)} %attended_over_ctx.7.refs_1_), channel_id=1, source_target_pairs={{0,4},{4,0},{8,12},{12,8},{1,5},{5,1},{9,13},{13,9},{2,6},{6,2},{1... | collective-permute-start | bytes 786440 | tf_op jit(solution)/shard_map/attended_over_ctx/ppermute | solution.py:49
  64.0 1.8 %collective-permute-start.11 = (bf16[2,48,1792]{2,1,0:T(8,128)(2,1)S(1)}, bf16[2,48,1792]{2,1,0:T(8,128)(2,1)S(1)}, u32[]{:S(2)}, u32[]{:S(2)}) collective-permute-start(bf16[2,48,1792]{2,1,0:T(8,128)(2,1)S(1)} %get-tuple-element.46), channel_id=1, source_target_pairs={{0,1},{1,0},{2,3},{3,2},{4,5},{5,4},{6,7},{7,6},{8,9},{9,8},{10,11... | collective-permute-start | bytes 1032200 | tf_op jit(solution)/shard_map/sum_over_cores/ppermute | solution.py:49
  65.2 2.4 %collective-permute-start.15 = (bf16[2,32,1792]{2,1,0:T(8,128)(2,1)S(1)}, bf16[2,32,1792]{2,1,0:T(8,128)(2,1)S(1)}, u32[]{:S(2)}, u32[]{:S(2)}) collective-permute-start(bf16[2,32,1792]{2,1,0:T(8,128)(2,1)S(1)} %get-tuple-element.50), channel_id=1, source_target_pairs={{0,1},{1,0},{2,3},{3,2},{4,5},{5,4},{6,7},{7,6},{8,9},{9,8},{10,11... | collective-permute-start | bytes 688136 | tf_op jit(solution)/shard_map/sum_over_cores/ppermute | solution.py:49
  65.9 6.4 %collective-permute-start.12 = (bf16[48,1792]{1,0:T(8,128)(2,1)S(1)}, bf16[48,1792]{1,0:T(8,128)(2,1)S(1)}, u32[]{:S(2)}, u32[]{:S(2)}) collective-permute-start(bf16[48,1792]{1,0:T(8,128)(2,1)S(1)} %get-tuple-element.48), channel_id=1, source_target_pairs={{0,2},{1,3},{2,0},{3,1},{4,6},{5,7},{6,4},{7,5},{8,10},{9,11},{10,... | collective-permute-start | bytes 516104 | tf_op jit(solution)/shard_map/sum_over_x/ppermute | solution.py:49
  69.1 1.6 %collective-permute-start.20 = (bf16[2,16,1792]{2,1,0:T(8,128)(2,1)S(1)}, bf16[2,16,1792]{2,1,0:T(8,128)(2,1)S(1)}, u32[]{:S(2)}, u32[]{:S(2)}) collective-permute-start(bf16[2,16,1792]{2,1,0:T(8,128)(2,1)S(1)} %sum_over_cores.8), channel_id=1, source_target_pairs={{0,1},{1,0},{2,3},{3,2},{4,5},{5,4},{6,7},{7,6},{8,9},{9,8},{10,11... | collective-permute-start | bytes 344072 | tf_op jit(solution)/shard_map/sum_over_cores/ppermute | solution.py:49
  69.2 6.0 %collective-permute-start.16 = (bf16[32,1792]{1,0:T(8,128)(2,1)S(1)}, bf16[32,1792]{1,0:T(8,128)(2,1)S(1)}, u32[]{:S(2)}, u32[]{:S(2)}) collective-permute-start(bf16[32,1792]{1,0:T(8,128)(2,1)S(1)} %get-tuple-element.52), channel_id=1, source_target_pairs={{0,2},{1,3},{2,0},{3,1},{4,6},{5,7},{6,4},{7,5},{8,10},{9,11},{10,... | collective-permute-start | bytes 344072 | tf_op jit(solution)/shard_map/sum_over_x/ppermute | solution.py:49
  72.3 5.6 %collective-permute-start.21 = (bf16[16,1792]{1,0:T(8,128)(2,1)S(1)}, bf16[16,1792]{1,0:T(8,128)(2,1)S(1)}, u32[]{:S(2)}, u32[]{:S(2)}) collective-permute-start(bf16[16,1792]{1,0:T(8,128)(2,1)S(1)} %sum_over_x.6), channel_id=1, source_target_pairs={{0,2},{1,3},{2,0},{3,1},{4,6},{5,7},{6,4},{7,5},{8,10},{9,11},{10,... | collective-permute-start | bytes 172040 | tf_op jit(solution)/shard_map/sum_over_x/ppermute | solution.py:49
  75.3 5.8 %collective-permute-start.17 = (bf16[32,1792]{1,0:T(8,128)(2,1)S(1)}, bf16[32,1792]{1,0:T(8,128)(2,1)S(1)}, u32[]{:S(2)}, u32[]{:S(2)}) collective-permute-start(bf16[32,1792]{1,0:T(8,128)(2,1)S(1)} %get-tuple-element.53), channel_id=1, source_target_pairs={{0,4},{4,0},{8,12},{12,8},{1,5},{5,1},{9,13},{13,9},{2,6},{6,2},{1... | collective-permute-start | bytes 344072 | tf_op jit(solution)/shard_map/columns_over_ctx/ppermute | solution.py:49
  75.3 11.4 %collective-permute-start.18 = (bf16[32,1792]{1,0:T(8,128)(2,1)S(1)}, bf16[32,1792]{1,0:T(8,128)(2,1)S(1)}, u32[]{:S(2)}, u32[]{:S(2)}) collective-permute-start(bf16[32,1792]{1,0:T(8,128)(2,1)S(1)} %get-tuple-element.54), channel_id=1, source_target_pairs={{0,8},{4,12},{8,0},{12,4},{1,9},{5,13},{9,1},{13,5},{2,10},{6,14},... | collective-permute-start | bytes 344072 | tf_op jit(solution)/shard_map/columns_over_ctx/ppermute | solution.py:49
  77.9 8.9 %collective-permute-start.22 = (bf16[32,1792]{1,0:T(8,128)(2,1)S(1)}, bf16[32,1792]{1,0:T(8,128)(2,1)S(1)}, u32[]{:S(2)}, u32[]{:S(2)}) collective-permute-start(bf16[32,1792]{1,0:T(8,128)(2,1)S(1)} %sum_over_x.7), channel_id=1, source_target_pairs={{0,12},{4,8},{8,4},{12,0},{1,13},{5,9},{9,5},{13,1},{2,14},{6,10},... | collective-permute-start | bytes 344072 | tf_op jit(solution)/shard_map/columns_over_ctx/ppermute | solution.py:49

commit v12 on v11

--- a/solution.py
+++ b/solution.py
@@ -17,9 +17,11 @@
 SUB_ROWS = 256
 LOAD_LIMIT = 44
 MASKED = -1e30
-RAISE_LATE = 20
-RAISE_HANDED = 3
-RAISE_X = 4
+LEAD_EARLY = 6
+LEAD_NEAR = 2
+LEAD_LATE = 3
+LEAD_HANDED = 3
+LEAD_X = 1
 LOG2E = 1.4426950408889634
 SCALE = LOG2E / math.sqrt(HEAD)
 
@@ -65,18 +67,17 @@
     )(array, *after)
 
 
-def gather_pieces(own, size, after, lead):
-    pieces = {0: own}
+def gather_pieces(own, near, size, after, lead, far_lead):
+    pieces = {0: own, 1: tie(exchange(near, "ctx", size, 1), [], lead)}
     bit = size // 2
-    while bit:
+    while bit > 1:
         pieces[bit] = exchange(own, "ctx", size, bit)
         bit //= 2
-    pieces[1] = tie(pieces[1], [], lead)
-    bit = 1
+    bit = 2
     while bit < size:
         for offset in range(bit + 1, 2 * bit):
             if offset == bit + 1:
-                pieces[bit] = tie(pieces[bit], after, lead)
+                pieces[bit] = tie(pieces[bit], after, far_lead)
             pieces[offset] = exchange(pieces[bit], "ctx", size, offset ^ bit)
         bit *= 2
     return [pieces[offset] for offset in range(size)]
@@ -194,7 +195,7 @@
             latent_ref[start : start + width, :] = piece_ref[:LAT, :].T
             start += width
     else:
-        keys_ref, latent_ref, out_ref = refs
+        keys_ref, latent_ref, out_ref, copy_ref = refs
     amount = keys_ref.shape[1]
     group = max(1, min(heads, SUB_ROWS // rows))
     size = group * rows
@@ -223,6 +224,8 @@
                 preferred_element_type=jnp.float32,
             )
             out_ref[:, head * VD : (head + 1) * VD] = result.astype(jnp.bfloat16)
+            if not count:
+                copy_ref[:, head * VD : (head + 1) * VD] = result.astype(jnp.bfloat16)
         scores = later
 
 
@@ -230,7 +233,9 @@
     head_count, rows, depth = q_ext.shape
     amount = bias.shape[1]
     out_shape = [jax.ShapeDtypeStruct((rows, head_count * VD), jnp.bfloat16)]
-    if not gathered:
+    if gathered:
+        out_shape *= 2
+    else:
         out_shape.append(jax.ShapeDtypeStruct((depth, amount), jnp.bfloat16))
         out_shape.append(jax.ShapeDtypeStruct((amount, LAT), jnp.bfloat16))
     return pl.pallas_call(
@@ -382,16 +387,13 @@
         others = [exchange(array, "head", n_head, 1) for array in halves]
     with jax.named_scope("attention"):
         first, *keys = attention(q_ext[0], bias[0], w_values, [own_keys] + halves + others, False)
-        attended = [first]
-        for chunk in range(1, len(pieces)):
-            attended += attention(q_ext[chunk], bias[chunk], w_values, keys, True)
+        second, again = attention(q_ext[1], bias[1], w_values, keys, True)
     with jax.named_scope("attended_over_ctx"):
-        early = gather_pieces(attended[0], n_ctx, attended[1:], SHORT)
-        late = gather_pieces(attended[1], n_ctx, [], cost(RAISE_LATE))
+        early = gather_pieces(first, first, n_ctx, [second], cost(LEAD_EARLY), SHORT)
+        again = tie(again, [early[n_ctx // 2]])
+        late = gather_pieces(second, again, n_ctx, [early[n_ctx - 1]], cost(LEAD_NEAR), cost(LEAD_LATE))
     powers = [1 << bit for bit in range(n_ctx.bit_length() - 1)]
     handed = [offset for offset in range(1, n_ctx) if offset not in powers]
-    for offset in handed:
-        late[offset] = tie(late[offset], [late[n_ctx // 2]], cost(RAISE_HANDED))
     gathered = [early, late]
     units = [
         [(0, 0), (1, 0)],
@@ -402,8 +404,11 @@
     sums = []
     for unit, members in enumerate(units):
         with jax.named_scope("out_product"):
+            if unit == 3:
+                for offset in handed:
+                    late[offset] = tie(late[offset], sums[1][1], cost(LEAD_HANDED))
             sources = [gathered[chunk][offset] for chunk, offset in members]
-            after = [*attended[1:], *sums[0][1]] if unit == 1 else []
+            after = [second, *sums[0][1]] if unit == 1 else []
             sent, kept = product(sources, w_out, n_x, after)
         with jax.named_scope("sum_over_cores"):
             if unit == 3:
@@ -412,7 +417,7 @@
         with jax.named_scope("sum_over_x"):
             if unit == 3:
                 before = sums[1][1]
-                sent = [tie(array, before, cost(RAISE_X)) for array in sent]
+                sent = [tie(array, before, cost(LEAD_X)) for array in sent]
             crossed = [exchange(array, "head", n_head, 2 * d) for d, array in enumerate(sent, 1)]
         sums.append((total, crossed))
     blocks = {}

time: 87.8 us -> 83.9 us (0.956)
  waiting for transfers between devices: 40.2 us -> 35 us
  starting transfers between devices: 23 us -> 24.3 us
    ppermute x23, waiting for transfers between devices: 40.2 us -> 35 us  [exchange(): return lax.ppermute(array, axis, [(i, i ^ bit) for i in range(size)])]
    ppermute x23, starting transfers between devices: 23 us -> 24.3 us  [exchange(): return lax.ppermute(array, axis, [(i, i ^ bit) for i in range(size)])]
  transfers between devices with their start and end apart: 23 -> 23, of which waited for: 12 -> 10; matrix products, arithmetic and copies ran while one was open for 0% -> 0% of each run, Pallas kernels for 17% -> 16%
where the time goes in v12:
time: 83.9 us; the launch traced here: 83.7 us
  waiting for transfers between devices  35 us (42%)
  starting transfers between devices  24.3 us (29%)
  Pallas kernels  19.8 us (24%)
  local copies, waits for them, and re-layouts  2.75 us (3%)
  other arithmetic  1 us (1%)
  between operations  0.89 us (1%)
    ppermute x23, waiting for transfers between devices, exchange(): return lax.ppermute(array, axis, [(i, i ^ bit) for i in range(size)])  35 us
    ppermute x23, starting transfers between devices, exchange(): return lax.ppermute(array, axis, [(i, i ^ bit) for i in range(size)])  24.3 us
    pallas_call x2, Pallas kernels, attention(): pl.pallas_call(functools.partial(attention_kernel, 0 if gathered else len...  7.71 us
    pallas_call x1, Pallas kernels, load(): pl.pallas_call(functools.partial(load_kernel, owners, pieces, cache_rows)...  5.66 us
    pallas_call x4, Pallas kernels, product(): pl.pallas_call(functools.partial(product_kernel, count, n_x, len(after)),...  5.29 us
    unnamed x10, local copies, waits for them, and re-layouts  2.75 us
  transfers between devices with their start and end apart: 23, of which 10 were waited for; matrix products, arithmetic and copies ran while one was open for 0% of the time, Pallas kernels for 16%

profile of v12, /device:TPU:0, one launch (start us, length us, event | category | flops | bytes accessed | tf_op | source)
XLA Modules:
  0.0 83.7 jit_solution(305010803453127465)
XLA Ops:
  0.0 1.0 %slice_select_fusion = bf16[576,128]{1,0:T(8,128)(2,1)S(1)} fusion(bf16[576,256]{1,0:T(8,128)(2,1)} %bitcast.3, pred[]{:T(512)S(6)} %eq.5), kind=kLoop, calls=%fused_computation | loop fusion | flops 73728 | bytes 442369 | tf_op jit(solution)/shard_map/keys_over_ctx/jit(_where)/select_n | solution.py:379
  1.0 3.1 %collective-permute-start = (bf16[576,128]{1,0:T(8,128)(2,1)S(1)}, bf16[576,128]{1,0:T(8,128)(2,1)S(1)}, u32[]{:S(2)}, u32[]{:S(2)}) collective-permute-start(bf16[576,128]{1,0:T(8,128)(2,1)S(1)} %slice_select_fusion), channel_id=1, source_target_pairs={{0,4},{4,0},{8,12},{12,8},{1,5},{5,1},{9,13},{13,9},{2,6},{6,2},{1... | collective-permute-start | bytes 442376 | tf_op jit(solution)/shard_map/keys_over_ctx/ppermute | solution.py:51
  4.1 2.6 %collective-permute-start.1 = (bf16[576,128]{1,0:T(8,128)(2,1)S(1)}, bf16[576,128]{1,0:T(8,128)(2,1)S(1)}, u32[]{:S(2)}, u32[]{:S(2)}) collective-permute-start(bf16[576,128]{1,0:T(8,128)(2,1)S(1)} %slice_select_fusion), channel_id=1, source_target_pairs={{0,8},{4,12},{8,0},{12,4},{1,9},{5,13},{9,1},{13,5},{2,10},{6,14},... | collective-permute-start | bytes 442376 | tf_op jit(solution)/shard_map/keys_over_ctx/ppermute | solution.py:51
  6.7 0.0 collective-permute-start.2
  7.3 0.0 copy-start
  7.3 1.0 %copy-done = bf16[256,576]{0,1:T(8,128)(2,1)S(1)} copy-done((bf16[256,576]{0,1:T(8,128)(2,1)S(1)}, bf16[256,576]{0,1:T(8,128)(2,1)}, u32[]{:S(2)}) %copy-start) | copy-done | bytes 294936
  8.3 0.0 copy-start.1
  8.3 1.1 %copy-done.1 = bf16[128,3072]{1,0:T(8,128)(2,1)S(1)} copy-done((bf16[128,3072]{1,0:T(8,128)(2,1)S(1)}, bf16[128,3072]{1,0:T(8,128)(2,1)}, u32[]{:S(2)}) %copy-start.1) | copy-done | bytes 786456
  9.4 0.7 copy-done.2
  10.1 5.7 %load.1 = (bf16[16,64,576]{2,1,0:T(8,128)(2,1)S(1)}, bf16[16,64,576]{2,1,0:T(8,128)(2,1)S(1)}, f32[64,1024]{1,0:T(8,128)S(1)}, f32[64,1024]{1,0:T(8,128)S(1)}, b...) custom-call(s32[4]{0:T(128)S(1)} %copy-done.2, s32[1]{0:T(128)S(6)} %copy.29.prefix_ref, ...), custom_call_target="tpu_custom_call" | custom-call | flops 1024 | bytes 1024 | tf_op jit(solution)/shard_map/load/pallas_call | solution.py:142
  15.8 0.0 collective-permute-done.refs_0_
  15.8 0.1 collective-permute-start.3
  15.9 2.2 %collective-permute-done.1.refs_0_ = bf16[576,128]{1,0:T(8,128)(2,1)S(1)} collective-permute-done((bf16[576,128]{1,0:T(8,128)(2,1)S(1)}, bf16[576,128]{1,0:T(8,128)(2,1)S(1)}, u32[]{:S(2)}, u32[]{:S(2)}) %collective-permute-start.1) | collective-permute-done | bytes 147488 | tf_op jit(solution)/shard_map/keys_over_ctx/ppermute | solution.py:51
  18.1 0.0 collective-permute-start.4
  18.1 0.0 collective-permute-done.2.refs_0_
  18.1 0.5 collective-permute-start.5
  18.6 0.0 collective-permute-done.3.refs_4_
  18.6 0.9 %collective-permute-done.4.refs_5_ = bf16[576,128]{1,0:T(8,128)(2,1)S(1)} collective-permute-done((bf16[576,128]{1,0:T(8,128)(2,1)S(1)}, bf16[576,128]{1,0:T(8,128)(2,1)S(1)}, u32[]{:S(2)}, u32[]{:S(2)}) %collective-permute-start.4) | collective-permute-done | bytes 147488 | tf_op jit(solution)/shard_map/keys_over_cores/ppermute | solution.py:51
  19.5 0.2 collective-permute-done.5.refs_6_
  19.7 3.9 %attention.2 = (bf16[64,2048]{1,0:T(8,128)(2,1)S(1)}, bf16[576,1024]{1,0:T(8,128)(2,1)S(1)}, bf16[1024,512]{1,0:T(8,128)(2,1)S(1)}) custom-call(bf16[16,64,576]{2,1,0:T(8,128)(2,1)S(1)} %get-tuple-element.34.q_ref, f32[64,1024]{1,0:T(8,128)S(1)} %get-tuple-element.35.bias_ref, bf16[16,512,128]{2,1,0:T(8,128)(2,1)S(1)} %get-tuple-element.36.value_ref, ...), custom_call_target="tpu_custom_call" | custom-call | flops 1024 | bytes 1024 | tf_op jit(solution)/shard_map/attention/pallas_call | solution.py:241
  23.6 3.2 %collective-permute-start.9 = (bf16[64,2048]{1,0:T(8,128)(2,1)S(1)}, bf16[64,2048]{1,0:T(8,128)(2,1)S(1)}, u32[]{:S(2)}, u32[]{:S(2)}) collective-permute-start(bf16[64,2048]{1,0:T(8,128)(2,1)S(1)} %get-tuple-element.38.refs_0_), channel_id=1, source_target_pairs={{0,8},{4,12},{8,0},{12,4},{1,9},{5,13},{9,1},{13,5},{2,10},{6,14},... | collective-permute-start | bytes 786440 | tf_op jit(solution)/shard_map/attended_over_ctx/ppermute | solution.py:51
  26.7 0.0 collective-permute-start.8
  26.7 3.8 %attention.3 = (bf16[64,2048]{1,0:T(8,128)(2,1)S(1)}, bf16[64,2048]{1,0:T(8,128)(2,1)S(1)}) custom-call(bf16[16,64,576]{2,1,0:T(8,128)(2,1)S(1)} %get-tuple-element.39.q_ref, f32[64,1024]{1,0:T(8,128)S(1)} %get-tuple-element.40.bias_ref, bf16[16,512,128]{2,1,0:T(8,128)(2,1)S(1)} %get-tuple-element.36.value_ref, ...), custom_call_target="tpu_custom_call" | custom-call | flops 1024 | bytes 1024 | tf_op jit(solution)/shard_map/attention/pallas_call | solution.py:241
  30.6 0.0 slice-done
  30.6 0.0 slice-done.1
  30.6 1.1 %out_product.5 = (bf16[2,32,1792]{2,1,0:T(8,128)(2,1)S(1)}, f32[2,32,1792]{2,1,0:T(8,128)S(1)}) custom-call(bf16[2048,1792]{1,0:T(8,128)(2,1)S(1)} %bitcast.2, bf16[64,2048]{1,0:T(8,128)(2,1)S(1)} %get-tuple-element.38.refs_0_, bf16[64,2048]{1,0:T(8,128)(2,1)S(1)} %get-tuple-element.43.refs_1_.refs_3_), custom_call_target="tpu_custom_call" | custom-call | flops 1024 | bytes 1024 | tf_op jit(solution)/shard_map/out_product/pallas_call | solution.py:275
  31.7 0.1 collective-permute-start.6
  31.8 2.0 %collective-permute-start.14 = (bf16[64,2048]{1,0:T(8,128)(2,1)S(1)}, bf16[64,2048]{1,0:T(8,128)(2,1)S(1)}, u32[]{:S(2)}, u32[]{:S(2)}) collective-permute-start(bf16[64,2048]{1,0:T(8,128)(2,1)S(1)} %get-tuple-element.43.refs_1_.refs_3_), channel_id=1, source_target_pairs={{0,8},{4,12},{8,0},{12,4},{1,9},{5,13},{9,1},{13,5},{2,10},{6,14},... | collective-permute-start | bytes 786440 | tf_op jit(solution)/shard_map/attended_over_ctx/ppermute | solution.py:51
  33.8 0.0 collective-permute-done.6.received_ref
  33.8 1.6 %collective-permute-start.7 = (bf16[32,1792]{1,0:T(8,128)(2,1)S(1)}, bf16[32,1792]{1,0:T(8,128)(2,1)S(1)}, u32[]{:S(2)}, u32[]{:S(2)}) collective-permute-start(bf16[32,1792]{1,0:T(8,128)(2,1)S(1)} %get-tuple-element.47), channel_id=1, source_target_pairs={{0,2},{1,3},{2,0},{3,1},{4,6},{5,7},{6,4},{7,5},{8,10},{9,11},{10,... | collective-permute-start | bytes 344072 | tf_op jit(solution)/shard_map/sum_over_x/ppermute | solution.py:51
  35.4 4.3 %collective-permute-done.9.refs_0_ = bf16[64,2048]{1,0:T(8,128)(2,1)S(1)} collective-permute-done((bf16[64,2048]{1,0:T(8,128)(2,1)S(1)}, bf16[64,2048]{1,0:T(8,128)(2,1)S(1)}, u32[]{:S(2)}, u32[]{:S(2)}) %collective-permute-start.9) | collective-permute-done | bytes 262176 | tf_op jit(solution)/shard_map/attended_over_ctx/ppermute | solution.py:51
  39.7 0.0 collective-permute-start.10
  39.7 2.0 %collective-permute-start.13 = (bf16[64,2048]{1,0:T(8,128)(2,1)S(1)}, bf16[64,2048]{1,0:T(8,128)(2,1)S(1)}, u32[]{:S(2)}, u32[]{:S(2)}) collective-permute-start(bf16[64,2048]{1,0:T(8,128)(2,1)S(1)} %attended_over_ctx.7), channel_id=1, source_target_pairs={{0,4},{4,0},{8,12},{12,8},{1,5},{5,1},{9,13},{13,9},{2,6},{6,2},{1... | collective-permute-start | bytes 786440 | tf_op jit(solution)/shard_map/attended_over_ctx/ppermute | solution.py:51
  41.7 0.0 collective-permute-done.8.refs_0_
  41.7 0.0 collective-permute-done.7.refs_1_.refs_4_
  41.7 11.7 %collective-permute-done.10.refs_2_.refs_1_ = bf16[64,2048]{1,0:T(8,128)(2,1)S(1)} collective-permute-done((bf16[64,2048]{1,0:T(8,128)(2,1)S(1)}, bf16[64,2048]{1,0:T(8,128)(2,1)S(1)}, u32[]{:S(2)}, u32[]{:S(2)}) %collective-permute-start.10) | collective-permute-done | bytes 262176 | tf_op jit(solution)/shard_map/attended_over_ctx/ppermute | solution.py:51
  53.4 1.6 %out_product.6 = (bf16[2,48,1792]{2,1,0:T(8,128)(2,1)S(1)}, f32[2,48,1792]{2,1,0:T(8,128)S(1)}) custom-call(bf16[2048,1792]{1,0:T(8,128)(2,1)S(1)} %bitcast.2, bf16[64,2048]{1,0:T(8,128)(2,1)S(1)} %attended_over_ctx.5.refs_0_, bf16[64,2048]{1,0:T(8,128)(2,1)S(1)} %attended_over_ctx.6.refs_1_, bf16[64,2048]{1,0:T(8,128)(2,1)S(1)} %collective-permute-done.10.refs_2_.refs_1_, ...), custom_call_target="tpu_custom_call" | custom-call | flops 1024 | bytes 1024 | tf_op jit(solution)/shard_map/out_product/pallas_call | solution.py:275
  55.0 0.1 collective-permute-start.11
  55.1 0.0 collective-permute-done.14.refs_0_
  55.1 0.1 collective-permute-start.19
  55.2 1.5 %collective-permute-done.11.received_ref = bf16[2,48,1792]{2,1,0:T(8,128)(2,1)S(1)} collective-permute-done((bf16[2,48,1792]{2,1,0:T(8,128)(2,1)S(1)}, bf16[2,48,1792]{2,1,0:T(8,128)(2,1)S(1)}, u32[]{:S(2)}, u32[]{:S(2)}) %collective-permute-start.11) | collective-permute-done | bytes 344096 | tf_op jit(solution)/shard_map/sum_over_cores/ppermute | solution.py:51
  56.7 0.1 sum_over_cores.6
  56.8 1.6 %collective-permute-start.12 = (bf16[48,1792]{1,0:T(8,128)(2,1)S(1)}, bf16[48,1792]{1,0:T(8,128)(2,1)S(1)}, u32[]{:S(2)}, u32[]{:S(2)}) collective-permute-start(bf16[48,1792]{1,0:T(8,128)(2,1)S(1)} %get-tuple-element.51), channel_id=1, source_target_pairs={{0,2},{1,3},{2,0},{3,1},{4,6},{5,7},{6,4},{7,5},{8,10},{9,11},{10,... | collective-permute-start | bytes 516104 | tf_op jit(solution)/shard_map/sum_over_x/ppermute | solution.py:51
  58.4 0.0 collective-permute-done.13.refs_0_
  58.4 1.1 %out_product.7 = (bf16[2,32,1792]{2,1,0:T(8,128)(2,1)S(1)}, f32[2,32,1792]{2,1,0:T(8,128)S(1)}) custom-call(bf16[2048,1792]{1,0:T(8,128)(2,1)S(1)} %bitcast.2, bf16[64,2048]{1,0:T(8,128)(2,1)S(1)} %attended_over_ctx.8.refs_0_, bf16[64,2048]{1,0:T(8,128)(2,1)S(1)} %attended_over_ctx.9.refs_1_), custom_call_target="tpu_custom_call" | custom-call | flops 1024 | bytes 1024 | tf_op jit(solution)/shard_map/out_product/pallas_call | solution.py:275
  59.5 0.1 collective-permute-start.15
  59.6 4.2 %collective-permute-done.19.refs_0_ = bf16[64,2048]{1,0:T(8,128)(2,1)S(1)} collective-permute-done((bf16[64,2048]{1,0:T(8,128)(2,1)S(1)}, bf16[64,2048]{1,0:T(8,128)(2,1)S(1)}, u32[]{:S(2)}, u32[]{:S(2)}) %collective-permute-start.19) | collective-permute-done | bytes 262176 | tf_op jit(solution)/shard_map/attended_over_ctx/ppermute | solution.py:51
  63.8 0.0 collective-permute-done.12.refs_1_
  63.8 0.0 collective-permute-done.15.received_ref
  63.8 0.1 sum_over_cores.7
  63.9 1.4 %out_product.9 = (bf16[2,16,1792]{2,1,0:T(8,128)(2,1)S(1)}, f32[2,16,1792]{2,1,0:T(8,128)S(1)}) custom-call(bf16[2048,1792]{1,0:T(8,128)(2,1)S(1)} %bitcast.2, bf16[64,2048]{1,0:T(8,128)(2,1)S(1)} %out_product.8.refs_0_), custom_call_target="tpu_custom_call" | custom-call | flops 1024 | bytes 1024 | tf_op jit(solution)/shard_map/out_product/pallas_call | solution.py:275
  65.3 0.1 collective-permute-start.20
  65.3 1.6 %collective-permute-start.16 = (bf16[32,1792]{1,0:T(8,128)(2,1)S(1)}, bf16[32,1792]{1,0:T(8,128)(2,1)S(1)}, u32[]{:S(2)}, u32[]{:S(2)}) collective-permute-start(bf16[32,1792]{1,0:T(8,128)(2,1)S(1)} %get-tuple-element.56), channel_id=1, source_target_pairs={{0,2},{1,3},{2,0},{3,1},{4,6},{5,7},{6,4},{7,5},{8,10},{9,11},{10,... | collective-permute-start | bytes 344072 | tf_op jit(solution)/shard_map/sum_over_x/ppermute | solution.py:51
  66.9 0.0 collective-permute-done.20.received_ref
  67.0 1.3 %collective-permute-start.21 = (bf16[16,1792]{1,0:T(8,128)(2,1)S(1)}, bf16[16,1792]{1,0:T(8,128)(2,1)S(1)}, u32[]{:S(2)}, u32[]{:S(2)}) collective-permute-start(bf16[16,1792]{1,0:T(8,128)(2,1)S(1)} %sum_over_x.6), channel_id=1, source_target_pairs={{0,2},{1,3},{2,0},{3,1},{4,6},{5,7},{6,4},{7,5},{8,10},{9,11},{10,... | collective-permute-start | bytes 172040 | tf_op jit(solution)/shard_map/sum_over_x/ppermute | solution.py:51
  68.3 3.1 %collective-permute-done.16.refs_3_ = bf16[32,1792]{1,0:T(8,128)(2,1)S(1)} collective-permute-done((bf16[32,1792]{1,0:T(8,128)(2,1)S(1)}, bf16[32,1792]{1,0:T(8,128)(2,1)S(1)}, u32[]{:S(2)}, u32[]{:S(2)}) %collective-permute-start.16) | collective-permute-done | bytes 114720 | tf_op jit(solution)/shard_map/sum_over_x/ppermute | solution.py:51
  71.4 0.3 collective-permute-start.17
  71.7 1.6 %collective-permute-start.18 = (bf16[32,1792]{1,0:T(8,128)(2,1)S(1)}, bf16[32,1792]{1,0:T(8,128)(2,1)S(1)}, u32[]{:S(2)}, u32[]{:S(2)}) collective-permute-start(bf16[32,1792]{1,0:T(8,128)(2,1)S(1)} %get-tuple-element.58), channel_id=1, source_target_pairs={{0,8},{4,12},{8,0},{12,4},{1,9},{5,13},{9,1},{13,5},{2,10},{6,14},... | collective-permute-start | bytes 344072 | tf_op jit(solution)/shard_map/columns_over_ctx/ppermute | solution.py:51
  73.4 0.0 collective-permute-done.21.refs_3_
  73.4 2.6 %collective-permute-start.22 = (bf16[32,1792]{1,0:T(8,128)(2,1)S(1)}, bf16[32,1792]{1,0:T(8,128)(2,1)S(1)}, u32[]{:S(2)}, u32[]{:S(2)}) collective-permute-start(bf16[32,1792]{1,0:T(8,128)(2,1)S(1)} %sum_over_x.7), channel_id=1, source_target_pairs={{0,12},{4,8},{8,4},{12,0},{1,13},{5,9},{9,5},{13,1},{2,14},{6,10},... | collective-permute-start | bytes 344072 | tf_op jit(solution)/shard_map/columns_over_ctx/ppermute | solution.py:51
  76.0 1.0 %collective-permute-done.17.refs_1_ = bf16[32,1792]{1,0:T(8,128)(2,1)S(1)} collective-permute-done((bf16[32,1792]{1,0:T(8,128)(2,1)S(1)}, bf16[32,1792]{1,0:T(8,128)(2,1)S(1)}, u32[]{:S(2)}, u32[]{:S(2)}) %collective-permute-start.17) | collective-permute-done | bytes 114720 | tf_op jit(solution)/shard_map/columns_over_ctx/ppermute | solution.py:51
  77.0 5.9 %collective-permute-done.18.refs_2_ = bf16[32,1792]{1,0:T(8,128)(2,1)S(1)} collective-permute-done((bf16[32,1792]{1,0:T(8,128)(2,1)S(1)}, bf16[32,1792]{1,0:T(8,128)(2,1)S(1)}, u32[]{:S(2)}, u32[]{:S(2)}) %collective-permute-start.18) | collective-permute-done | bytes 114720 | tf_op jit(solution)/shard_map/columns_over_ctx/ppermute | solution.py:51
  82.9 0.0 collective-permute-done.22.refs_3_
  82.9 0.8 output.1
  (20 shorter events, 0.2 us)
Async XLA Ops:
  1.0 14.8 %collective-permute-start = (bf16[576,128]{1,0:T(8,128)(2,1)S(1)}, bf16[576,128]{1,0:T(8,128)(2,1)S(1)}, u32[]{:S(2)}, u32[]{:S(2)}) collective-permute-start(bf16[576,128]{1,0:T(8,128)(2,1)S(1)} %slice_select_fusion), channel_id=1, source_target_pairs={{0,4},{4,0},{8,12},{12,8},{1,5},{5,1},{9,13},{13,9},{2,6},{6,2},{1... | collective-permute-start | bytes 442376 | tf_op jit(solution)/shard_map/keys_over_ctx/ppermute | solution.py:51
  4.1 14.0 %collective-permute-start.1 = (bf16[576,128]{1,0:T(8,128)(2,1)S(1)}, bf16[576,128]{1,0:T(8,128)(2,1)S(1)}, u32[]{:S(2)}, u32[]{:S(2)}) collective-permute-start(bf16[576,128]{1,0:T(8,128)(2,1)S(1)} %slice_select_fusion), channel_id=1, source_target_pairs={{0,8},{4,12},{8,0},{12,4},{1,9},{5,13},{9,1},{13,5},{2,10},{6,14},... | collective-permute-start | bytes 442376 | tf_op jit(solution)/shard_map/keys_over_ctx/ppermute | solution.py:51
  6.7 11.4 %collective-permute-start.2 = (bf16[576,128]{1,0:T(8,128)(2,1)S(1)}, bf16[576,128]{1,0:T(8,128)(2,1)S(1)}, u32[]{:S(2)}, u32[]{:S(2)}) collective-permute-start(bf16[576,128]{1,0:T(8,128)(2,1)S(1)} %slice_select_fusion), channel_id=1, source_target_pairs={{0,12},{4,8},{8,4},{12,0},{1,13},{5,9},{9,5},{13,1},{2,14},{6,10},... | collective-permute-start | bytes 442376 | tf_op jit(solution)/shard_map/keys_over_ctx/ppermute | solution.py:51
  7.3 1.0 %copy-start = (bf16[256,576]{0,1:T(8,128)(2,1)S(1)}, bf16[256,576]{0,1:T(8,128)(2,1)}, u32[]{:S(2)}) copy-start(bf16[256,576]{0,1:T(8,128)(2,1)} %param.7) | copy-start | bytes 884740
  8.3 1.1 %copy-start.1 = (bf16[128,3072]{1,0:T(8,128)(2,1)S(1)}, bf16[128,3072]{1,0:T(8,128)(2,1)}, u32[]{:S(2)}) copy-start(bf16[128,3072]{1,0:T(8,128)(2,1)} %q_hbm.1) | copy-start | bytes 2359300
  9.4 0.7 copy-start.2
  10.1 20.5 %slice-start = ((s8[7340032]{0:T(1024)(128)(4,1)}), s8[3145728]{0:T(1024)(128)(4,1)S(1)}, s32[]{:S(2)}) async-start(s8[7340032]{0:T(1024)(128)(4,1)} %bitcast.1), calls=%async_computation | async-start | bytes 6291456
  15.8 2.8 %collective-permute-start.3 = (bf16[576,128]{1,0:T(8,128)(2,1)S(1)}, bf16[576,128]{1,0:T(8,128)(2,1)S(1)}, u32[]{:S(2)}, u32[]{:S(2)}) collective-permute-start(bf16[576,128]{1,0:T(8,128)(2,1)S(1)} %keys_over_cores.3.refs_1_), channel_id=1, source_target_pairs={{0,1},{1,0},{2,3},{3,2},{4,5},{5,4},{6,7},{7,6},{8,9},{9,8},{10,11... | collective-permute-start | bytes 442376 | tf_op jit(solution)/shard_map/keys_over_cores/ppermute | solution.py:51
  18.1 1.4 %collective-permute-start.4 = (bf16[576,128]{1,0:T(8,128)(2,1)S(1)}, bf16[576,128]{1,0:T(8,128)(2,1)S(1)}, u32[]{:S(2)}, u32[]{:S(2)}) collective-permute-start(bf16[576,128]{1,0:T(8,128)(2,1)S(1)} %keys_over_cores.4.refs_2_), channel_id=1, source_target_pairs={{0,1},{1,0},{2,3},{3,2},{4,5},{5,4},{6,7},{7,6},{8,9},{9,8},{10,11... | collective-permute-start | bytes 442376 | tf_op jit(solution)/shard_map/keys_over_cores/ppermute | solution.py:51
  18.1 1.6 %collective-permute-start.5 = (bf16[576,128]{1,0:T(8,128)(2,1)S(1)}, bf16[576,128]{1,0:T(8,128)(2,1)S(1)}, u32[]{:S(2)}, u32[]{:S(2)}) collective-permute-start(bf16[576,128]{1,0:T(8,128)(2,1)S(1)} %keys_over_cores.5.refs_3_), channel_id=1, source_target_pairs={{0,1},{1,0},{2,3},{3,2},{4,5},{5,4},{6,7},{7,6},{8,9},{9,8},{10,11... | collective-permute-start | bytes 442376 | tf_op jit(solution)/shard_map/keys_over_cores/ppermute | solution.py:51
  19.7 10.9 %slice-start.1 = ((s8[7340032]{0:T(1024)(128)(4,1)}), s8[4194304]{0:T(1024)(128)(4,1)S(1)}, s32[]{:S(2)}) async-start(s8[7340032]{0:T(1024)(128)(4,1)} %bitcast.1), calls=%async_computation.1 | async-start | bytes 8388608
  23.6 16.1 %collective-permute-start.9 = (bf16[64,2048]{1,0:T(8,128)(2,1)S(1)}, bf16[64,2048]{1,0:T(8,128)(2,1)S(1)}, u32[]{:S(2)}, u32[]{:S(2)}) collective-permute-start(bf16[64,2048]{1,0:T(8,128)(2,1)S(1)} %get-tuple-element.38.refs_0_), channel_id=1, source_target_pairs={{0,8},{4,12},{8,0},{12,4},{1,9},{5,13},{9,1},{13,5},{2,10},{6,14},... | collective-permute-start | bytes 786440 | tf_op jit(solution)/shard_map/attended_over_ctx/ppermute | solution.py:51
  26.7 15.0 %collective-permute-start.8 = (bf16[64,2048]{1,0:T(8,128)(2,1)S(1)}, bf16[64,2048]{1,0:T(8,128)(2,1)S(1)}, u32[]{:S(2)}, u32[]{:S(2)}) collective-permute-start(bf16[64,2048]{1,0:T(8,128)(2,1)S(1)} %get-tuple-element.38.refs_0_), channel_id=1, source_target_pairs={{0,4},{4,0},{8,12},{12,8},{1,5},{5,1},{9,13},{13,9},{2,6},{6,2},{1... | collective-permute-start | bytes 786440 | tf_op jit(solution)/shard_map/attended_over_ctx/ppermute | solution.py:51
  31.7 2.0 %collective-permute-start.6 = (bf16[2,32,1792]{2,1,0:T(8,128)(2,1)S(1)}, bf16[2,32,1792]{2,1,0:T(8,128)(2,1)S(1)}, u32[]{:S(2)}, u32[]{:S(2)}) collective-permute-start(bf16[2,32,1792]{2,1,0:T(8,128)(2,1)S(1)} %get-tuple-element.45), channel_id=1, source_target_pairs={{0,1},{1,0},{2,3},{3,2},{4,5},{5,4},{6,7},{7,6},{8,9},{9,8},{10,11... | collective-permute-start | bytes 688136 | tf_op jit(solution)/shard_map/sum_over_cores/ppermute | solution.py:51
  31.8 23.3 %collective-permute-start.14 = (bf16[64,2048]{1,0:T(8,128)(2,1)S(1)}, bf16[64,2048]{1,0:T(8,128)(2,1)S(1)}, u32[]{:S(2)}, u32[]{:S(2)}) collective-permute-start(bf16[64,2048]{1,0:T(8,128)(2,1)S(1)} %get-tuple-element.43.refs_1_.refs_3_), channel_id=1, source_target_pairs={{0,8},{4,12},{8,0},{12,4},{1,9},{5,13},{9,1},{13,5},{2,10},{6,14},... | collective-permute-start | bytes 786440 | tf_op jit(solution)/shard_map/attended_over_ctx/ppermute | solution.py:51
  33.8 7.9 %collective-permute-start.7 = (bf16[32,1792]{1,0:T(8,128)(2,1)S(1)}, bf16[32,1792]{1,0:T(8,128)(2,1)S(1)}, u32[]{:S(2)}, u32[]{:S(2)}) collective-permute-start(bf16[32,1792]{1,0:T(8,128)(2,1)S(1)} %get-tuple-element.47), channel_id=1, source_target_pairs={{0,2},{1,3},{2,0},{3,1},{4,6},{5,7},{6,4},{7,5},{8,10},{9,11},{10,... | collective-permute-start | bytes 344072 | tf_op jit(solution)/shard_map/sum_over_x/ppermute | solution.py:51
  39.7 13.7 %collective-permute-start.10 = (bf16[64,2048]{1,0:T(8,128)(2,1)S(1)}, bf16[64,2048]{1,0:T(8,128)(2,1)S(1)}, u32[]{:S(2)}, u32[]{:S(2)}) collective-permute-start(bf16[64,2048]{1,0:T(8,128)(2,1)S(1)} %attended_over_ctx.6.refs_1_), channel_id=1, source_target_pairs={{0,4},{4,0},{8,12},{12,8},{1,5},{5,1},{9,13},{13,9},{2,6},{6,2},{1... | collective-permute-start | bytes 786440 | tf_op jit(solution)/shard_map/attended_over_ctx/ppermute | solution.py:51
  39.7 18.7 %collective-permute-start.13 = (bf16[64,2048]{1,0:T(8,128)(2,1)S(1)}, bf16[64,2048]{1,0:T(8,128)(2,1)S(1)}, u32[]{:S(2)}, u32[]{:S(2)}) collective-permute-start(bf16[64,2048]{1,0:T(8,128)(2,1)S(1)} %attended_over_ctx.7), channel_id=1, source_target_pairs={{0,4},{4,0},{8,12},{12,8},{1,5},{5,1},{9,13},{13,9},{2,6},{6,2},{1... | collective-permute-start | bytes 786440 | tf_op jit(solution)/shard_map/attended_over_ctx/ppermute | solution.py:51
  55.0 1.7 %collective-permute-start.11 = (bf16[2,48,1792]{2,1,0:T(8,128)(2,1)S(1)}, bf16[2,48,1792]{2,1,0:T(8,128)(2,1)S(1)}, u32[]{:S(2)}, u32[]{:S(2)}) collective-permute-start(bf16[2,48,1792]{2,1,0:T(8,128)(2,1)S(1)} %get-tuple-element.49), channel_id=1, source_target_pairs={{0,1},{1,0},{2,3},{3,2},{4,5},{5,4},{6,7},{7,6},{8,9},{9,8},{10,11... | collective-permute-start | bytes 1032200 | tf_op jit(solution)/shard_map/sum_over_cores/ppermute | solution.py:51
  55.1 8.7 %collective-permute-start.19 = (bf16[64,2048]{1,0:T(8,128)(2,1)S(1)}, bf16[64,2048]{1,0:T(8,128)(2,1)S(1)}, u32[]{:S(2)}, u32[]{:S(2)}) collective-permute-start(bf16[64,2048]{1,0:T(8,128)(2,1)S(1)} %attended_over_ctx.9.refs_1_), channel_id=1, source_target_pairs={{0,4},{4,0},{8,12},{12,8},{1,5},{5,1},{9,13},{13,9},{2,6},{6,2},{1... | collective-permute-start | bytes 786440 | tf_op jit(solution)/shard_map/attended_over_ctx/ppermute | solution.py:51
  56.8 7.0 %collective-permute-start.12 = (bf16[48,1792]{1,0:T(8,128)(2,1)S(1)}, bf16[48,1792]{1,0:T(8,128)(2,1)S(1)}, u32[]{:S(2)}, u32[]{:S(2)}) collective-permute-start(bf16[48,1792]{1,0:T(8,128)(2,1)S(1)} %get-tuple-element.51), channel_id=1, source_target_pairs={{0,2},{1,3},{2,0},{3,1},{4,6},{5,7},{6,4},{7,5},{8,10},{9,11},{10,... | collective-permute-start | bytes 516104 | tf_op jit(solution)/shard_map/sum_over_x/ppermute | solution.py:51
  59.5 4.3 %collective-permute-start.15 = (bf16[2,32,1792]{2,1,0:T(8,128)(2,1)S(1)}, bf16[2,32,1792]{2,1,0:T(8,128)(2,1)S(1)}, u32[]{:S(2)}, u32[]{:S(2)}) collective-permute-start(bf16[2,32,1792]{2,1,0:T(8,128)(2,1)S(1)} %get-tuple-element.54), channel_id=1, source_target_pairs={{0,1},{1,0},{2,3},{3,2},{4,5},{5,4},{6,7},{7,6},{8,9},{9,8},{10,11... | collective-permute-start | bytes 688136 | tf_op jit(solution)/shard_map/sum_over_cores/ppermute | solution.py:51
  65.3 1.6 %collective-permute-start.20 = (bf16[2,16,1792]{2,1,0:T(8,128)(2,1)S(1)}, bf16[2,16,1792]{2,1,0:T(8,128)(2,1)S(1)}, u32[]{:S(2)}, u32[]{:S(2)}) collective-permute-start(bf16[2,16,1792]{2,1,0:T(8,128)(2,1)S(1)} %sum_over_cores.8), channel_id=1, source_target_pairs={{0,1},{1,0},{2,3},{3,2},{4,5},{5,4},{6,7},{7,6},{8,9},{9,8},{10,11... | collective-permute-start | bytes 344072 | tf_op jit(solution)/shard_map/sum_over_cores/ppermute | solution.py:51
  65.3 6.0 %collective-permute-start.16 = (bf16[32,1792]{1,0:T(8,128)(2,1)S(1)}, bf16[32,1792]{1,0:T(8,128)(2,1)S(1)}, u32[]{:S(2)}, u32[]{:S(2)}) collective-permute-start(bf16[32,1792]{1,0:T(8,128)(2,1)S(1)} %get-tuple-element.56), channel_id=1, source_target_pairs={{0,2},{1,3},{2,0},{3,1},{4,6},{5,7},{6,4},{7,5},{8,10},{9,11},{10,... | collective-permute-start | bytes 344072 | tf_op jit(solution)/shard_map/sum_over_x/ppermute | solution.py:51
  67.0 6.4 %collective-permute-start.21 = (bf16[16,1792]{1,0:T(8,128)(2,1)S(1)}, bf16[16,1792]{1,0:T(8,128)(2,1)S(1)}, u32[]{:S(2)}, u32[]{:S(2)}) collective-permute-start(bf16[16,1792]{1,0:T(8,128)(2,1)S(1)} %sum_over_x.6), channel_id=1, source_target_pairs={{0,2},{1,3},{2,0},{3,1},{4,6},{5,7},{6,4},{7,5},{8,10},{9,11},{10,... | collective-permute-start | bytes 172040 | tf_op jit(solution)/shard_map/sum_over_x/ppermute | solution.py:51
  71.4 5.6 %collective-permute-start.17 = (bf16[32,1792]{1,0:T(8,128)(2,1)S(1)}, bf16[32,1792]{1,0:T(8,128)(2,1)S(1)}, u32[]{:S(2)}, u32[]{:S(2)}) collective-permute-start(bf16[32,1792]{1,0:T(8,128)(2,1)S(1)} %get-tuple-element.57), channel_id=1, source_target_pairs={{0,4},{4,0},{8,12},{12,8},{1,5},{5,1},{9,13},{13,9},{2,6},{6,2},{1... | collective-permute-start | bytes 344072 | tf_op jit(solution)/shard_map/columns_over_ctx/ppermute | solution.py:51
  71.7 11.2 %collective-permute-start.18 = (bf16[32,1792]{1,0:T(8,128)(2,1)S(1)}, bf16[32,1792]{1,0:T(8,128)(2,1)S(1)}, u32[]{:S(2)}, u32[]{:S(2)}) collective-permute-start(bf16[32,1792]{1,0:T(8,128)(2,1)S(1)} %get-tuple-element.58), channel_id=1, source_target_pairs={{0,8},{4,12},{8,0},{12,4},{1,9},{5,13},{9,1},{13,5},{2,10},{6,14},... | collective-permute-start | bytes 344072 | tf_op jit(solution)/shard_map/columns_over_ctx/ppermute | solution.py:51
  73.4 9.5 %collective-permute-start.22 = (bf16[32,1792]{1,0:T(8,128)(2,1)S(1)}, bf16[32,1792]{1,0:T(8,128)(2,1)S(1)}, u32[]{:S(2)}, u32[]{:S(2)}) collective-permute-start(bf16[32,1792]{1,0:T(8,128)(2,1)S(1)} %sum_over_x.7), channel_id=1, source_target_pairs={{0,12},{4,8},{8,4},{12,0},{1,13},{5,9},{9,5},{13,1},{2,14},{6,10},... | collective-permute-start | bytes 344072 | tf_op jit(solution)/shard_map/columns_over_ctx/ppermute | solution.py:51

commit v13 on v12

--- a/solution.py
+++ b/solution.py
@@ -21,6 +21,7 @@
 LEAD_NEAR = 2
 LEAD_LATE = 3
 LEAD_HANDED = 3
+LEAD_AHEAD = 3
 LEAD_X = 1
 LOG2E = 1.4426950408889634
 SCALE = LOG2E / math.sqrt(HEAD)
@@ -336,33 +337,37 @@
     )(*arrays)
 
 
-def place_kernel(*refs):
-    blocks, out_ref = refs[:-1], refs[-1]
+def place_kernel(counts, *refs):
+    refs, out_ref = list(refs[:-1]), refs[-1]
     ctx = lax.axis_index("ctx")
-    width = blocks[0].shape[1]
-    for offset, block in enumerate(blocks):
+    width = refs[0].shape[1]
+    for offset, count in enumerate(counts):
+        parts = [refs.pop(0)[...].astype(jnp.float32) for _ in range(count)]
         column = pl.multiple_of((ctx ^ offset) * width, 128)
-        out_ref[:, pl.ds(column, width)] = block[...]
+        out_ref[:, pl.ds(column, width)] = jnp.concatenate(parts, axis=0).astype(jnp.bfloat16)
 
 
 def place_columns(blocks):
     n_ctx = len(blocks)
-    rows, width = blocks[0].shape
+    rows = sum(block.shape[0] for block in blocks[0])
+    width = blocks[0][0].shape[1]
     if width % 128:
         ctx = lax.axis_index("ctx")
         out = jnp.zeros((rows, n_ctx * width), jnp.bfloat16)
-        for offset, block in enumerate(blocks):
+        for offset, parts in enumerate(blocks):
+            block = jnp.concatenate(parts, axis=0)
             out = lax.dynamic_update_slice(out, block, (0, (ctx ^ offset) * width))
         return out
+    arrays = [block for parts in blocks for block in parts]
     return pl.pallas_call(
-        place_kernel,
+        functools.partial(place_kernel, [len(parts) for parts in blocks]),
         grid=(1,),
         out_shape=jax.ShapeDtypeStruct((rows, n_ctx * width), jnp.bfloat16),
-        in_specs=[IN_VMEM] * n_ctx,
+        in_specs=[IN_VMEM] * len(arrays),
         out_specs=pl.BlockSpec((rows, n_ctx * width), lambda i: (0, 0)),
         compiler_params=params(4),
         cost_estimate=SHORT,
-    )(*blocks)
+    )(*arrays)
 
 
 def shards(n_ctx, n_head, queries, kv_rows, w_kv_up, w_out, stretch_order, prefix_len):
@@ -409,6 +414,8 @@
                     late[offset] = tie(late[offset], sums[1][1], cost(LEAD_HANDED))
             sources = [gathered[chunk][offset] for chunk, offset in members]
             after = [second, *sums[0][1]] if unit == 1 else []
+            if unit == 2:
+                after = [sums[1][0]]
             sent, kept = product(sources, w_out, n_x, after)
         with jax.named_scope("sum_over_cores"):
             if unit == 3:
@@ -420,20 +427,24 @@
                 sent = [tie(array, before, cost(LEAD_X)) for array in sent]
             crossed = [exchange(array, "head", n_head, 2 * d) for d, array in enumerate(sent, 1)]
         sums.append((total, crossed))
-    blocks = {}
-    for offsets, last in (([0], 0), (powers, 2), (handed, 3)):
+    def added(units_in, offsets, parts_of):
         with jax.named_scope("sum_over_x"):
-            sources = [sums[0]] if offsets == [0] else [sums[1], sums[last]]
-            places = []
-            for offset in offsets:
-                parts = [(0, 0), (0, 1)]
-                if offset:
-                    parts = [(0, offset - 1), (1, units[last].index((1, offset)))]
-                places.append(parts)
-            found = x_sum(sources, pieces[0], places)
+            places = [parts_of(offset) for offset in offsets]
+            found = x_sum([sums[unit] for unit in units_in], pieces[0], places)
         with jax.named_scope("columns_over_ctx"):
-            for offset, block in reversed(list(zip(offsets, found))):
-                blocks[offset] = exchange(block, "ctx", n_ctx, offset) if offset else block
+            return [
+                exchange(block, "ctx", n_ctx, offset) if offset else block
+                for offset, block in zip(offsets, found)
+            ]
+
+    blocks = {0: added([0], [0], lambda offset: [(0, 0), (0, 1)])}
+    ahead = added([1], handed, lambda offset: [(0, offset - 1)])
+    ahead = [tie(block, [], cost(LEAD_AHEAD)) for block in ahead]
+    both = added([1, 2], powers, lambda offset: [(0, offset - 1), (1, powers.index(offset))])
+    behind = added([3], handed, lambda offset: [(0, handed.index(offset))])
+    blocks.update({offset: [block] for offset, block in zip(powers, both)})
+    for offset, first_rows, last_rows in zip(handed, ahead, behind):
+        blocks[offset] = [first_rows, last_rows]
     with jax.named_scope("output"):
         return place_columns([blocks[d] for d in range(n_ctx)])
 

time: 83.9 us -> 82.5 us (0.983)
  waiting for transfers between devices: 35 us -> 32.1 us
  starting transfers between devices: 24.3 us -> 25.7 us
    ppermute x23 -> x24, waiting for transfers between devices: 35 us -> 32.1 us  [exchange(): return lax.ppermute(array, axis, [(i, i ^ bit) for i in range(size)])]
    ppermute x23 -> x24, starting transfers between devices: 24.3 us -> 25.7 us  [exchange(): return lax.ppermute(array, axis, [(i, i ^ bit) for i in range(size)])]
  transfers between devices with their start and end apart: 23 -> 24, of which waited for: 10 -> 10; matrix products, arithmetic and copies ran while one was open for 0% -> 0% of each run, Pallas kernels for 16% -> 18%
where the time goes in v13:
time: 82.5 us; the launch traced here: 82.2 us
  waiting for transfers between devices  32.1 us (39%)
  starting transfers between devices  25.7 us (31%)
  Pallas kernels  19.8 us (24%)
  local copies, waits for them, and re-layouts  2.75 us (3%)
  other arithmetic  1 us (1%)
  between operations  0.9 us (1%)
    ppermute x24, waiting for transfers between devices, exchange(): return lax.ppermute(array, axis, [(i, i ^ bit) for i in range(size)])  32.1 us
    ppermute x24, starting transfers between devices, exchange(): return lax.ppermute(array, axis, [(i, i ^ bit) for i in range(size)])  25.7 us
    pallas_call x2, Pallas kernels, attention(): pl.pallas_call(functools.partial(attention_kernel, 0 if gathered else len...  7.71 us
    pallas_call x1, Pallas kernels, load(): pl.pallas_call(functools.partial(load_kernel, owners, pieces, cache_rows)...  5.66 us
    pallas_call x4, Pallas kernels, product(): pl.pallas_call(functools.partial(product_kernel, count, n_x, len(after)),...  5.28 us
    unnamed x10, local copies, waits for them, and re-layouts  2.75 us
  transfers between devices with their start and end apart: 24, of which 10 were waited for; matrix products, arithmetic and copies ran while one was open for 0% of the time, Pallas kernels for 18%

profile of v13, /device:TPU:0, one launch (start us, length us, event | category | flops | bytes accessed | tf_op | source)
XLA Modules:
  0.0 82.2 jit_solution(6866437422347461697)
XLA Ops:
  0.0 1.0 %slice_select_fusion = bf16[576,128]{1,0:T(8,128)(2,1)S(1)} fusion(bf16[576,256]{1,0:T(8,128)(2,1)} %bitcast.3, pred[]{:T(512)S(6)} %eq.5), kind=kLoop, calls=%fused_computation | loop fusion | flops 73728 | bytes 442369 | tf_op jit(solution)/shard_map/keys_over_ctx/jit(_where)/select_n | solution.py:384
  1.0 3.1 %collective-permute-start = (bf16[576,128]{1,0:T(8,128)(2,1)S(1)}, bf16[576,128]{1,0:T(8,128)(2,1)S(1)}, u32[]{:S(2)}, u32[]{:S(2)}) collective-permute-start(bf16[576,128]{1,0:T(8,128)(2,1)S(1)} %slice_select_fusion), channel_id=1, source_target_pairs={{0,4},{4,0},{8,12},{12,8},{1,5},{5,1},{9,13},{13,9},{2,6},{6,2},{1... | collective-permute-start | bytes 442376 | tf_op jit(solution)/shard_map/keys_over_ctx/ppermute | solution.py:52
  4.1 2.6 %collective-permute-start.1 = (bf16[576,128]{1,0:T(8,128)(2,1)S(1)}, bf16[576,128]{1,0:T(8,128)(2,1)S(1)}, u32[]{:S(2)}, u32[]{:S(2)}) collective-permute-start(bf16[576,128]{1,0:T(8,128)(2,1)S(1)} %slice_select_fusion), channel_id=1, source_target_pairs={{0,8},{4,12},{8,0},{12,4},{1,9},{5,13},{9,1},{13,5},{2,10},{6,14},... | collective-permute-start | bytes 442376 | tf_op jit(solution)/shard_map/keys_over_ctx/ppermute | solution.py:52
  6.7 0.0 collective-permute-start.2
  7.3 0.0 copy-start
  7.3 1.0 %copy-done = bf16[256,576]{0,1:T(8,128)(2,1)S(1)} copy-done((bf16[256,576]{0,1:T(8,128)(2,1)S(1)}, bf16[256,576]{0,1:T(8,128)(2,1)}, u32[]{:S(2)}) %copy-start) | copy-done | bytes 294936
  8.3 1.1 %copy-done.1 = bf16[128,3072]{1,0:T(8,128)(2,1)S(1)} copy-done((bf16[128,3072]{1,0:T(8,128)(2,1)S(1)}, bf16[128,3072]{1,0:T(8,128)(2,1)}, u32[]{:S(2)}) %copy-start.1) | copy-done | bytes 786456
  9.4 0.7 copy-done.2
  10.1 5.7 %load.1 = (bf16[16,64,576]{2,1,0:T(8,128)(2,1)S(1)}, bf16[16,64,576]{2,1,0:T(8,128)(2,1)S(1)}, f32[64,1024]{1,0:T(8,128)S(1)}, f32[64,1024]{1,0:T(8,128)S(1)}, b...) custom-call(s32[4]{0:T(128)S(1)} %copy-done.2, s32[1]{0:T(128)S(6)} %copy.31.prefix_ref, ...), custom_call_target="tpu_custom_call" | custom-call | flops 1024 | bytes 1024 | tf_op jit(solution)/shard_map/load/pallas_call | solution.py:143
  15.8 0.0 collective-permute-done.refs_0_
  15.8 0.1 collective-permute-start.3
  15.9 2.2 %collective-permute-done.1.refs_0_ = bf16[576,128]{1,0:T(8,128)(2,1)S(1)} collective-permute-done((bf16[576,128]{1,0:T(8,128)(2,1)S(1)}, bf16[576,128]{1,0:T(8,128)(2,1)S(1)}, u32[]{:S(2)}, u32[]{:S(2)}) %collective-permute-start.1) | collective-permute-done | bytes 147488 | tf_op jit(solution)/shard_map/keys_over_ctx/ppermute | solution.py:52
  18.1 0.0 collective-permute-start.4
  18.1 0.0 collective-permute-done.2.refs_0_
  18.1 0.5 collective-permute-start.5
  18.6 0.0 collective-permute-done.3.refs_4_
  18.6 0.9 %collective-permute-done.4.refs_5_ = bf16[576,128]{1,0:T(8,128)(2,1)S(1)} collective-permute-done((bf16[576,128]{1,0:T(8,128)(2,1)S(1)}, bf16[576,128]{1,0:T(8,128)(2,1)S(1)}, u32[]{:S(2)}, u32[]{:S(2)}) %collective-permute-start.4) | collective-permute-done | bytes 147488 | tf_op jit(solution)/shard_map/keys_over_cores/ppermute | solution.py:52
  19.5 0.2 collective-permute-done.5.refs_6_
  19.7 3.9 %attention.2 = (bf16[64,2048]{1,0:T(8,128)(2,1)S(1)}, bf16[576,1024]{1,0:T(8,128)(2,1)S(1)}, bf16[1024,512]{1,0:T(8,128)(2,1)S(1)}) custom-call(bf16[16,64,576]{2,1,0:T(8,128)(2,1)S(1)} %get-tuple-element.34.q_ref, f32[64,1024]{1,0:T(8,128)S(1)} %get-tuple-element.35.bias_ref, bf16[16,512,128]{2,1,0:T(8,128)(2,1)S(1)} %get-tuple-element.36.value_ref, ...), custom_call_target="tpu_custom_call" | custom-call | flops 1024 | bytes 1024 | tf_op jit(solution)/shard_map/attention/pallas_call | solution.py:242
  23.6 3.2 %collective-permute-start.9 = (bf16[64,2048]{1,0:T(8,128)(2,1)S(1)}, bf16[64,2048]{1,0:T(8,128)(2,1)S(1)}, u32[]{:S(2)}, u32[]{:S(2)}) collective-permute-start(bf16[64,2048]{1,0:T(8,128)(2,1)S(1)} %get-tuple-element.38.refs_0_), channel_id=1, source_target_pairs={{0,8},{4,12},{8,0},{12,4},{1,9},{5,13},{9,1},{13,5},{2,10},{6,14},... | collective-permute-start | bytes 786440 | tf_op jit(solution)/shard_map/attended_over_ctx/ppermute | solution.py:52
  26.7 0.0 collective-permute-start.8
  26.7 3.8 %attention.3 = (bf16[64,2048]{1,0:T(8,128)(2,1)S(1)}, bf16[64,2048]{1,0:T(8,128)(2,1)S(1)}) custom-call(bf16[16,64,576]{2,1,0:T(8,128)(2,1)S(1)} %get-tuple-element.39.q_ref, f32[64,1024]{1,0:T(8,128)S(1)} %get-tuple-element.40.bias_ref, bf16[16,512,128]{2,1,0:T(8,128)(2,1)S(1)} %get-tuple-element.36.value_ref, ...), custom_call_target="tpu_custom_call" | custom-call | flops 1024 | bytes 1024 | tf_op jit(solution)/shard_map/attention/pallas_call | solution.py:242
  30.6 0.0 slice-done
  30.6 1.1 %out_product.5 = (bf16[2,32,1792]{2,1,0:T(8,128)(2,1)S(1)}, f32[2,32,1792]{2,1,0:T(8,128)S(1)}) custom-call(bf16[2048,1792]{1,0:T(8,128)(2,1)S(1)} %bitcast.2, bf16[64,2048]{1,0:T(8,128)(2,1)S(1)} %get-tuple-element.38.refs_0_, bf16[64,2048]{1,0:T(8,128)(2,1)S(1)} %get-tuple-element.43.refs_1_.refs_3_), custom_call_target="tpu_custom_call" | custom-call | flops 1024 | bytes 1024 | tf_op jit(solution)/shard_map/out_product/pallas_call | solution.py:276
  31.7 0.1 collective-permute-start.6
  31.8 2.0 %collective-permute-start.14 = (bf16[64,2048]{1,0:T(8,128)(2,1)S(1)}, bf16[64,2048]{1,0:T(8,128)(2,1)S(1)}, u32[]{:S(2)}, u32[]{:S(2)}) collective-permute-start(bf16[64,2048]{1,0:T(8,128)(2,1)S(1)} %get-tuple-element.43.refs_1_.refs_3_), channel_id=1, source_target_pairs={{0,8},{4,12},{8,0},{12,4},{1,9},{5,13},{9,1},{13,5},{2,10},{6,14},... | collective-permute-start | bytes 786440 | tf_op jit(solution)/shard_map/attended_over_ctx/ppermute | solution.py:52
  33.8 0.0 collective-permute-done.6.received_ref
  33.8 1.6 %collective-permute-start.7 = (bf16[32,1792]{1,0:T(8,128)(2,1)S(1)}, bf16[32,1792]{1,0:T(8,128)(2,1)S(1)}, u32[]{:S(2)}, u32[]{:S(2)}) collective-permute-start(bf16[32,1792]{1,0:T(8,128)(2,1)S(1)} %get-tuple-element.47), channel_id=1, source_target_pairs={{0,2},{1,3},{2,0},{3,1},{4,6},{5,7},{6,4},{7,5},{8,10},{9,11},{10,... | collective-permute-start | bytes 344072 | tf_op jit(solution)/shard_map/sum_over_x/ppermute | solution.py:52
  35.4 4.3 %collective-permute-done.9.refs_0_ = bf16[64,2048]{1,0:T(8,128)(2,1)S(1)} collective-permute-done((bf16[64,2048]{1,0:T(8,128)(2,1)S(1)}, bf16[64,2048]{1,0:T(8,128)(2,1)S(1)}, u32[]{:S(2)}, u32[]{:S(2)}) %collective-permute-start.9) | collective-permute-done | bytes 262176 | tf_op jit(solution)/shard_map/attended_over_ctx/ppermute | solution.py:52
  39.7 0.0 collective-permute-start.10
  39.7 2.0 %collective-permute-start.13 = (bf16[64,2048]{1,0:T(8,128)(2,1)S(1)}, bf16[64,2048]{1,0:T(8,128)(2,1)S(1)}, u32[]{:S(2)}, u32[]{:S(2)}) collective-permute-start(bf16[64,2048]{1,0:T(8,128)(2,1)S(1)} %attended_over_ctx.7), channel_id=1, source_target_pairs={{0,4},{4,0},{8,12},{12,8},{1,5},{5,1},{9,13},{13,9},{2,6},{6,2},{1... | collective-permute-start | bytes 786440 | tf_op jit(solution)/shard_map/attended_over_ctx/ppermute | solution.py:52
  41.7 0.0 collective-permute-done.8.refs_0_
  41.7 0.0 collective-permute-done.7.refs_1_.refs_4_
  41.7 11.7 %collective-permute-done.10.refs_2_.refs_1_ = bf16[64,2048]{1,0:T(8,128)(2,1)S(1)} collective-permute-done((bf16[64,2048]{1,0:T(8,128)(2,1)S(1)}, bf16[64,2048]{1,0:T(8,128)(2,1)S(1)}, u32[]{:S(2)}, u32[]{:S(2)}) %collective-permute-start.10) | collective-permute-done | bytes 262176 | tf_op jit(solution)/shard_map/attended_over_ctx/ppermute | solution.py:52
  53.4 1.6 %out_product.6 = (bf16[2,48,1792]{2,1,0:T(8,128)(2,1)S(1)}, f32[2,48,1792]{2,1,0:T(8,128)S(1)}) custom-call(bf16[2048,1792]{1,0:T(8,128)(2,1)S(1)} %bitcast.2, bf16[64,2048]{1,0:T(8,128)(2,1)S(1)} %attended_over_ctx.5.refs_0_, bf16[64,2048]{1,0:T(8,128)(2,1)S(1)} %attended_over_ctx.6.refs_1_, bf16[64,2048]{1,0:T(8,128)(2,1)S(1)} %collective-permute-done.10.refs_2_.refs_1_, ...), custom_call_target="tpu_custom_call" | custom-call | flops 1024 | bytes 1024 | tf_op jit(solution)/shard_map/out_product/pallas_call | solution.py:276
  55.0 0.1 collective-permute-start.11
  55.1 0.0 collective-permute-done.14.refs_0_
  55.1 0.1 collective-permute-start.20
  55.2 1.5 %collective-permute-done.11.received_ref = bf16[2,48,1792]{2,1,0:T(8,128)(2,1)S(1)} collective-permute-done((bf16[2,48,1792]{2,1,0:T(8,128)(2,1)S(1)}, bf16[2,48,1792]{2,1,0:T(8,128)(2,1)S(1)}, u32[]{:S(2)}, u32[]{:S(2)}) %collective-permute-start.11) | collective-permute-done | bytes 344096 | tf_op jit(solution)/shard_map/sum_over_cores/ppermute | solution.py:52
  56.7 0.1 sum_over_cores.6
  56.8 1.6 %collective-permute-start.12 = (bf16[48,1792]{1,0:T(8,128)(2,1)S(1)}, bf16[48,1792]{1,0:T(8,128)(2,1)S(1)}, u32[]{:S(2)}, u32[]{:S(2)}) collective-permute-start(bf16[48,1792]{1,0:T(8,128)(2,1)S(1)} %get-tuple-element.51), channel_id=1, source_target_pairs={{0,2},{1,3},{2,0},{3,1},{4,6},{5,7},{6,4},{7,5},{8,10},{9,11},{10,... | collective-permute-start | bytes 516104 | tf_op jit(solution)/shard_map/sum_over_x/ppermute | solution.py:52
  58.4 0.0 collective-permute-done.13.refs_0_
  58.4 1.1 %out_product.7 = (bf16[2,32,1792]{2,1,0:T(8,128)(2,1)S(1)}, f32[2,32,1792]{2,1,0:T(8,128)S(1)}) custom-call(bf16[2048,1792]{1,0:T(8,128)(2,1)S(1)} %bitcast.2, bf16[64,2048]{1,0:T(8,128)(2,1)S(1)} %attended_over_ctx.8.refs_0_, bf16[64,2048]{1,0:T(8,128)(2,1)S(1)} %attended_over_ctx.9.refs_1_, f32[48,1792]{1,0:T(8,128)S(1)} %get-tuple-element.50.refs_2_.refs_0_), custom_call_target="tpu_custom_call" | custom-call | flops 1024 | bytes 1024 | tf_op jit(solution)/shard_map/out_product/pallas_call | solution.py:276
  59.5 0.1 collective-permute-start.15
  59.6 4.2 %collective-permute-done.20.refs_0_ = bf16[64,2048]{1,0:T(8,128)(2,1)S(1)} collective-permute-done((bf16[64,2048]{1,0:T(8,128)(2,1)S(1)}, bf16[64,2048]{1,0:T(8,128)(2,1)S(1)}, u32[]{:S(2)}, u32[]{:S(2)}) %collective-permute-start.20) | collective-permute-done | bytes 262176 | tf_op jit(solution)/shard_map/attended_over_ctx/ppermute | solution.py:52
  63.8 0.0 collective-permute-done.12.refs_1_
  63.8 1.4 %out_product.9 = (bf16[2,16,1792]{2,1,0:T(8,128)(2,1)S(1)}, f32[2,16,1792]{2,1,0:T(8,128)S(1)}) custom-call(bf16[2048,1792]{1,0:T(8,128)(2,1)S(1)} %bitcast.2, bf16[64,2048]{1,0:T(8,128)(2,1)S(1)} %out_product.8.refs_0_), custom_call_target="tpu_custom_call" | custom-call | flops 1024 | bytes 1024 | tf_op jit(solution)/shard_map/out_product/pallas_call | solution.py:276
  65.2 0.0 collective-permute-done.15.received_ref
  65.2 0.1 sum_over_cores.7
  65.3 0.1 collective-permute-start.21
  65.4 1.6 %collective-permute-start.16 = (bf16[32,1792]{1,0:T(8,128)(2,1)S(1)}, bf16[32,1792]{1,0:T(8,128)(2,1)S(1)}, u32[]{:S(2)}, u32[]{:S(2)}) collective-permute-start(bf16[32,1792]{1,0:T(8,128)(2,1)S(1)} %get-tuple-element.56), channel_id=1, source_target_pairs={{0,2},{1,3},{2,0},{3,1},{4,6},{5,7},{6,4},{7,5},{8,10},{9,11},{10,... | collective-permute-start | bytes 344072 | tf_op jit(solution)/shard_map/sum_over_x/ppermute | solution.py:52
  66.9 0.0 collective-permute-done.21.received_ref
  67.0 1.3 %collective-permute-start.22 = (bf16[16,1792]{1,0:T(8,128)(2,1)S(1)}, bf16[16,1792]{1,0:T(8,128)(2,1)S(1)}, u32[]{:S(2)}, u32[]{:S(2)}) collective-permute-start(bf16[16,1792]{1,0:T(8,128)(2,1)S(1)} %sum_over_x.8), channel_id=1, source_target_pairs={{0,2},{1,3},{2,0},{3,1},{4,6},{5,7},{6,4},{7,5},{8,10},{9,11},{10,... | collective-permute-start | bytes 172040 | tf_op jit(solution)/shard_map/sum_over_x/ppermute | solution.py:52
  68.3 1.4 %collective-permute-start.19 = (bf16[16,1792]{1,0:T(8,128)(2,1)S(1)}, bf16[16,1792]{1,0:T(8,128)(2,1)S(1)}, u32[]{:S(2)}, u32[]{:S(2)}) collective-permute-start(bf16[16,1792]{1,0:T(8,128)(2,1)S(1)} %sum_over_x.7), channel_id=1, source_target_pairs={{0,12},{4,8},{8,4},{12,0},{1,13},{5,9},{9,5},{13,1},{2,14},{6,10},... | collective-permute-start | bytes 172040 | tf_op jit(solution)/shard_map/columns_over_ctx/ppermute | solution.py:52
  69.7 1.7 %collective-permute-done.16.refs_3_ = bf16[32,1792]{1,0:T(8,128)(2,1)S(1)} collective-permute-done((bf16[32,1792]{1,0:T(8,128)(2,1)S(1)}, bf16[32,1792]{1,0:T(8,128)(2,1)S(1)}, u32[]{:S(2)}, u32[]{:S(2)}) %collective-permute-start.16) | collective-permute-done | bytes 114720 | tf_op jit(solution)/shard_map/sum_over_x/ppermute | solution.py:52
  71.4 0.3 collective-permute-start.17
  71.8 1.6 %collective-permute-start.18 = (bf16[32,1792]{1,0:T(8,128)(2,1)S(1)}, bf16[32,1792]{1,0:T(8,128)(2,1)S(1)}, u32[]{:S(2)}, u32[]{:S(2)}) collective-permute-start(bf16[32,1792]{1,0:T(8,128)(2,1)S(1)} %get-tuple-element.58), channel_id=1, source_target_pairs={{0,8},{4,12},{8,0},{12,4},{1,9},{5,13},{9,1},{13,5},{2,10},{6,14},... | collective-permute-start | bytes 344072 | tf_op jit(solution)/shard_map/columns_over_ctx/ppermute | solution.py:52
  73.4 0.0 collective-permute-done.22.refs_1_
  73.4 2.6 %collective-permute-start.23 = (bf16[16,1792]{1,0:T(8,128)(2,1)S(1)}, bf16[16,1792]{1,0:T(8,128)(2,1)S(1)}, u32[]{:S(2)}, u32[]{:S(2)}) collective-permute-start(bf16[16,1792]{1,0:T(8,128)(2,1)S(1)} %sum_over_x.9), channel_id=1, source_target_pairs={{0,12},{4,8},{8,4},{12,0},{1,13},{5,9},{9,5},{13,1},{2,14},{6,10},... | collective-permute-start | bytes 172040 | tf_op jit(solution)/shard_map/columns_over_ctx/ppermute | solution.py:52
  76.0 0.0 collective-permute-done.19.refs_0_
  76.0 4.1 %collective-permute-done.23.refs_4_ = bf16[16,1792]{1,0:T(8,128)(2,1)S(1)} collective-permute-done((bf16[16,1792]{1,0:T(8,128)(2,1)S(1)}, bf16[16,1792]{1,0:T(8,128)(2,1)S(1)}, u32[]{:S(2)}, u32[]{:S(2)}) %collective-permute-start.23) | collective-permute-done | bytes 57376 | tf_op jit(solution)/shard_map/columns_over_ctx/ppermute | solution.py:52
  80.1 0.0 collective-permute-done.17.refs_1_
  80.1 1.3 %collective-permute-done.18.refs_2_ = bf16[32,1792]{1,0:T(8,128)(2,1)S(1)} collective-permute-done((bf16[32,1792]{1,0:T(8,128)(2,1)S(1)}, bf16[32,1792]{1,0:T(8,128)(2,1)S(1)}, u32[]{:S(2)}, u32[]{:S(2)}) %collective-permute-start.18) | collective-permute-done | bytes 114720 | tf_op jit(solution)/shard_map/columns_over_ctx/ppermute | solution.py:52
  81.4 0.8 output.1
  (24 shorter events, 0.2 us)
Async XLA Ops:
  1.0 14.8 %collective-permute-start = (bf16[576,128]{1,0:T(8,128)(2,1)S(1)}, bf16[576,128]{1,0:T(8,128)(2,1)S(1)}, u32[]{:S(2)}, u32[]{:S(2)}) collective-permute-start(bf16[576,128]{1,0:T(8,128)(2,1)S(1)} %slice_select_fusion), channel_id=1, source_target_pairs={{0,4},{4,0},{8,12},{12,8},{1,5},{5,1},{9,13},{13,9},{2,6},{6,2},{1... | collective-permute-start | bytes 442376 | tf_op jit(solution)/shard_map/keys_over_ctx/ppermute | solution.py:52
  4.1 14.0 %collective-permute-start.1 = (bf16[576,128]{1,0:T(8,128)(2,1)S(1)}, bf16[576,128]{1,0:T(8,128)(2,1)S(1)}, u32[]{:S(2)}, u32[]{:S(2)}) collective-permute-start(bf16[576,128]{1,0:T(8,128)(2,1)S(1)} %slice_select_fusion), channel_id=1, source_target_pairs={{0,8},{4,12},{8,0},{12,4},{1,9},{5,13},{9,1},{13,5},{2,10},{6,14},... | collective-permute-start | bytes 442376 | tf_op jit(solution)/shard_map/keys_over_ctx/ppermute | solution.py:52
  6.7 11.4 %collective-permute-start.2 = (bf16[576,128]{1,0:T(8,128)(2,1)S(1)}, bf16[576,128]{1,0:T(8,128)(2,1)S(1)}, u32[]{:S(2)}, u32[]{:S(2)}) collective-permute-start(bf16[576,128]{1,0:T(8,128)(2,1)S(1)} %slice_select_fusion), channel_id=1, source_target_pairs={{0,12},{4,8},{8,4},{12,0},{1,13},{5,9},{9,5},{13,1},{2,14},{6,10},... | collective-permute-start | bytes 442376 | tf_op jit(solution)/shard_map/keys_over_ctx/ppermute | solution.py:52
  7.3 1.0 %copy-start = (bf16[256,576]{0,1:T(8,128)(2,1)S(1)}, bf16[256,576]{0,1:T(8,128)(2,1)}, u32[]{:S(2)}) copy-start(bf16[256,576]{0,1:T(8,128)(2,1)} %param.7) | copy-start | bytes 884740
  8.3 1.1 %copy-start.1 = (bf16[128,3072]{1,0:T(8,128)(2,1)S(1)}, bf16[128,3072]{1,0:T(8,128)(2,1)}, u32[]{:S(2)}) copy-start(bf16[128,3072]{1,0:T(8,128)(2,1)} %q_hbm.1) | copy-start | bytes 2359300
  9.4 0.7 copy-start.2
  10.1 20.5 %slice-start = ((s8[7340032]{0:T(1024)(128)(4,1)}), s8[3145728]{0:T(1024)(128)(4,1)S(1)}, s32[]{:S(2)}) async-start(s8[7340032]{0:T(1024)(128)(4,1)} %bitcast.1), calls=%async_computation | async-start | bytes 6291456
  15.8 2.8 %collective-permute-start.3 = (bf16[576,128]{1,0:T(8,128)(2,1)S(1)}, bf16[576,128]{1,0:T(8,128)(2,1)S(1)}, u32[]{:S(2)}, u32[]{:S(2)}) collective-permute-start(bf16[576,128]{1,0:T(8,128)(2,1)S(1)} %keys_over_cores.3.refs_1_), channel_id=1, source_target_pairs={{0,1},{1,0},{2,3},{3,2},{4,5},{5,4},{6,7},{7,6},{8,9},{9,8},{10,11... | collective-permute-start | bytes 442376 | tf_op jit(solution)/shard_map/keys_over_cores/ppermute | solution.py:52
  18.1 1.4 %collective-permute-start.4 = (bf16[576,128]{1,0:T(8,128)(2,1)S(1)}, bf16[576,128]{1,0:T(8,128)(2,1)S(1)}, u32[]{:S(2)}, u32[]{:S(2)}) collective-permute-start(bf16[576,128]{1,0:T(8,128)(2,1)S(1)} %keys_over_cores.4.refs_2_), channel_id=1, source_target_pairs={{0,1},{1,0},{2,3},{3,2},{4,5},{5,4},{6,7},{7,6},{8,9},{9,8},{10,11... | collective-permute-start | bytes 442376 | tf_op jit(solution)/shard_map/keys_over_cores/ppermute | solution.py:52
  18.1 1.6 %collective-permute-start.5 = (bf16[576,128]{1,0:T(8,128)(2,1)S(1)}, bf16[576,128]{1,0:T(8,128)(2,1)S(1)}, u32[]{:S(2)}, u32[]{:S(2)}) collective-permute-start(bf16[576,128]{1,0:T(8,128)(2,1)S(1)} %keys_over_cores.5.refs_3_), channel_id=1, source_target_pairs={{0,1},{1,0},{2,3},{3,2},{4,5},{5,4},{6,7},{7,6},{8,9},{9,8},{10,11... | collective-permute-start | bytes 442376 | tf_op jit(solution)/shard_map/keys_over_cores/ppermute | solution.py:52
  19.7 10.9 %slice-start.1 = ((s8[7340032]{0:T(1024)(128)(4,1)}), s8[4194304]{0:T(1024)(128)(4,1)S(1)}, s32[]{:S(2)}) async-start(s8[7340032]{0:T(1024)(128)(4,1)} %bitcast.1), calls=%async_computation.1 | async-start | bytes 8388608
  23.6 16.1 %collective-permute-start.9 = (bf16[64,2048]{1,0:T(8,128)(2,1)S(1)}, bf16[64,2048]{1,0:T(8,128)(2,1)S(1)}, u32[]{:S(2)}, u32[]{:S(2)}) collective-permute-start(bf16[64,2048]{1,0:T(8,128)(2,1)S(1)} %get-tuple-element.38.refs_0_), channel_id=1, source_target_pairs={{0,8},{4,12},{8,0},{12,4},{1,9},{5,13},{9,1},{13,5},{2,10},{6,14},... | collective-permute-start | bytes 786440 | tf_op jit(solution)/shard_map/attended_over_ctx/ppermute | solution.py:52
  26.7 15.0 %collective-permute-start.8 = (bf16[64,2048]{1,0:T(8,128)(2,1)S(1)}, bf16[64,2048]{1,0:T(8,128)(2,1)S(1)}, u32[]{:S(2)}, u32[]{:S(2)}) collective-permute-start(bf16[64,2048]{1,0:T(8,128)(2,1)S(1)} %get-tuple-element.38.refs_0_), channel_id=1, source_target_pairs={{0,4},{4,0},{8,12},{12,8},{1,5},{5,1},{9,13},{13,9},{2,6},{6,2},{1... | collective-permute-start | bytes 786440 | tf_op jit(solution)/shard_map/attended_over_ctx/ppermute | solution.py:52
  31.7 2.0 %collective-permute-start.6 = (bf16[2,32,1792]{2,1,0:T(8,128)(2,1)S(1)}, bf16[2,32,1792]{2,1,0:T(8,128)(2,1)S(1)}, u32[]{:S(2)}, u32[]{:S(2)}) collective-permute-start(bf16[2,32,1792]{2,1,0:T(8,128)(2,1)S(1)} %get-tuple-element.45), channel_id=1, source_target_pairs={{0,1},{1,0},{2,3},{3,2},{4,5},{5,4},{6,7},{7,6},{8,9},{9,8},{10,11... | collective-permute-start | bytes 688136 | tf_op jit(solution)/shard_map/sum_over_cores/ppermute | solution.py:52
  31.8 23.3 %collective-permute-start.14 = (bf16[64,2048]{1,0:T(8,128)(2,1)S(1)}, bf16[64,2048]{1,0:T(8,128)(2,1)S(1)}, u32[]{:S(2)}, u32[]{:S(2)}) collective-permute-start(bf16[64,2048]{1,0:T(8,128)(2,1)S(1)} %get-tuple-element.43.refs_1_.refs_3_), channel_id=1, source_target_pairs={{0,8},{4,12},{8,0},{12,4},{1,9},{5,13},{9,1},{13,5},{2,10},{6,14},... | collective-permute-start | bytes 786440 | tf_op jit(solution)/shard_map/attended_over_ctx/ppermute | solution.py:52
  33.8 7.9 %collective-permute-start.7 = (bf16[32,1792]{1,0:T(8,128)(2,1)S(1)}, bf16[32,1792]{1,0:T(8,128)(2,1)S(1)}, u32[]{:S(2)}, u32[]{:S(2)}) collective-permute-start(bf16[32,1792]{1,0:T(8,128)(2,1)S(1)} %get-tuple-element.47), channel_id=1, source_target_pairs={{0,2},{1,3},{2,0},{3,1},{4,6},{5,7},{6,4},{7,5},{8,10},{9,11},{10,... | collective-permute-start | bytes 344072 | tf_op jit(solution)/shard_map/sum_over_x/ppermute | solution.py:52
  39.7 13.7 %collective-permute-start.10 = (bf16[64,2048]{1,0:T(8,128)(2,1)S(1)}, bf16[64,2048]{1,0:T(8,128)(2,1)S(1)}, u32[]{:S(2)}, u32[]{:S(2)}) collective-permute-start(bf16[64,2048]{1,0:T(8,128)(2,1)S(1)} %attended_over_ctx.6.refs_1_), channel_id=1, source_target_pairs={{0,4},{4,0},{8,12},{12,8},{1,5},{5,1},{9,13},{13,9},{2,6},{6,2},{1... | collective-permute-start | bytes 786440 | tf_op jit(solution)/shard_map/attended_over_ctx/ppermute | solution.py:52
  39.7 18.7 %collective-permute-start.13 = (bf16[64,2048]{1,0:T(8,128)(2,1)S(1)}, bf16[64,2048]{1,0:T(8,128)(2,1)S(1)}, u32[]{:S(2)}, u32[]{:S(2)}) collective-permute-start(bf16[64,2048]{1,0:T(8,128)(2,1)S(1)} %attended_over_ctx.7), channel_id=1, source_target_pairs={{0,4},{4,0},{8,12},{12,8},{1,5},{5,1},{9,13},{13,9},{2,6},{6,2},{1... | collective-permute-start | bytes 786440 | tf_op jit(solution)/shard_map/attended_over_ctx/ppermute | solution.py:52
  55.0 1.7 %collective-permute-start.11 = (bf16[2,48,1792]{2,1,0:T(8,128)(2,1)S(1)}, bf16[2,48,1792]{2,1,0:T(8,128)(2,1)S(1)}, u32[]{:S(2)}, u32[]{:S(2)}) collective-permute-start(bf16[2,48,1792]{2,1,0:T(8,128)(2,1)S(1)} %get-tuple-element.49), channel_id=1, source_target_pairs={{0,1},{1,0},{2,3},{3,2},{4,5},{5,4},{6,7},{7,6},{8,9},{9,8},{10,11... | collective-permute-start | bytes 1032200 | tf_op jit(solution)/shard_map/sum_over_cores/ppermute | solution.py:52
  55.1 8.7 %collective-permute-start.20 = (bf16[64,2048]{1,0:T(8,128)(2,1)S(1)}, bf16[64,2048]{1,0:T(8,128)(2,1)S(1)}, u32[]{:S(2)}, u32[]{:S(2)}) collective-permute-start(bf16[64,2048]{1,0:T(8,128)(2,1)S(1)} %attended_over_ctx.9.refs_1_), channel_id=1, source_target_pairs={{0,4},{4,0},{8,12},{12,8},{1,5},{5,1},{9,13},{13,9},{2,6},{6,2},{1... | collective-permute-start | bytes 786440 | tf_op jit(solution)/shard_map/attended_over_ctx/ppermute | solution.py:52
  56.8 7.0 %collective-permute-start.12 = (bf16[48,1792]{1,0:T(8,128)(2,1)S(1)}, bf16[48,1792]{1,0:T(8,128)(2,1)S(1)}, u32[]{:S(2)}, u32[]{:S(2)}) collective-permute-start(bf16[48,1792]{1,0:T(8,128)(2,1)S(1)} %get-tuple-element.51), channel_id=1, source_target_pairs={{0,2},{1,3},{2,0},{3,1},{4,6},{5,7},{6,4},{7,5},{8,10},{9,11},{10,... | collective-permute-start | bytes 516104 | tf_op jit(solution)/shard_map/sum_over_x/ppermute | solution.py:52
  59.5 5.7 %collective-permute-start.15 = (bf16[2,32,1792]{2,1,0:T(8,128)(2,1)S(1)}, bf16[2,32,1792]{2,1,0:T(8,128)(2,1)S(1)}, u32[]{:S(2)}, u32[]{:S(2)}) collective-permute-start(bf16[2,32,1792]{2,1,0:T(8,128)(2,1)S(1)} %get-tuple-element.54), channel_id=1, source_target_pairs={{0,1},{1,0},{2,3},{3,2},{4,5},{5,4},{6,7},{7,6},{8,9},{9,8},{10,11... | collective-permute-start | bytes 688136 | tf_op jit(solution)/shard_map/sum_over_cores/ppermute | solution.py:52
  65.3 1.6 %collective-permute-start.21 = (bf16[2,16,1792]{2,1,0:T(8,128)(2,1)S(1)}, bf16[2,16,1792]{2,1,0:T(8,128)(2,1)S(1)}, u32[]{:S(2)}, u32[]{:S(2)}) collective-permute-start(bf16[2,16,1792]{2,1,0:T(8,128)(2,1)S(1)} %sum_over_cores.8), channel_id=1, source_target_pairs={{0,1},{1,0},{2,3},{3,2},{4,5},{5,4},{6,7},{7,6},{8,9},{9,8},{10,11... | collective-permute-start | bytes 344072 | tf_op jit(solution)/shard_map/sum_over_cores/ppermute | solution.py:52
  65.4 6.0 %collective-permute-start.16 = (bf16[32,1792]{1,0:T(8,128)(2,1)S(1)}, bf16[32,1792]{1,0:T(8,128)(2,1)S(1)}, u32[]{:S(2)}, u32[]{:S(2)}) collective-permute-start(bf16[32,1792]{1,0:T(8,128)(2,1)S(1)} %get-tuple-element.56), channel_id=1, source_target_pairs={{0,2},{1,3},{2,0},{3,1},{4,6},{5,7},{6,4},{7,5},{8,10},{9,11},{10,... | collective-permute-start | bytes 344072 | tf_op jit(solution)/shard_map/sum_over_x/ppermute | solution.py:52
  67.0 6.4 %collective-permute-start.22 = (bf16[16,1792]{1,0:T(8,128)(2,1)S(1)}, bf16[16,1792]{1,0:T(8,128)(2,1)S(1)}, u32[]{:S(2)}, u32[]{:S(2)}) collective-permute-start(bf16[16,1792]{1,0:T(8,128)(2,1)S(1)} %sum_over_x.8), channel_id=1, source_target_pairs={{0,2},{1,3},{2,0},{3,1},{4,6},{5,7},{6,4},{7,5},{8,10},{9,11},{10,... | collective-permute-start | bytes 172040 | tf_op jit(solution)/shard_map/sum_over_x/ppermute | solution.py:52
  68.3 7.7 %collective-permute-start.19 = (bf16[16,1792]{1,0:T(8,128)(2,1)S(1)}, bf16[16,1792]{1,0:T(8,128)(2,1)S(1)}, u32[]{:S(2)}, u32[]{:S(2)}) collective-permute-start(bf16[16,1792]{1,0:T(8,128)(2,1)S(1)} %sum_over_x.7), channel_id=1, source_target_pairs={{0,12},{4,8},{8,4},{12,0},{1,13},{5,9},{9,5},{13,1},{2,14},{6,10},... | collective-permute-start | bytes 172040 | tf_op jit(solution)/shard_map/columns_over_ctx/ppermute | solution.py:52
  71.4 8.7 %collective-permute-start.17 = (bf16[32,1792]{1,0:T(8,128)(2,1)S(1)}, bf16[32,1792]{1,0:T(8,128)(2,1)S(1)}, u32[]{:S(2)}, u32[]{:S(2)}) collective-permute-start(bf16[32,1792]{1,0:T(8,128)(2,1)S(1)} %get-tuple-element.57), channel_id=1, source_target_pairs={{0,4},{4,0},{8,12},{12,8},{1,5},{5,1},{9,13},{13,9},{2,6},{6,2},{1... | collective-permute-start | bytes 344072 | tf_op jit(solution)/shard_map/columns_over_ctx/ppermute | solution.py:52
  71.8 9.7 %collective-permute-start.18 = (bf16[32,1792]{1,0:T(8,128)(2,1)S(1)}, bf16[32,1792]{1,0:T(8,128)(2,1)S(1)}, u32[]{:S(2)}, u32[]{:S(2)}) collective-permute-start(bf16[32,1792]{1,0:T(8,128)(2,1)S(1)} %get-tuple-element.58), channel_id=1, source_target_pairs={{0,8},{4,12},{8,0},{12,4},{1,9},{5,13},{9,1},{13,5},{2,10},{6,14},... | collective-permute-start | bytes 344072 | tf_op jit(solution)/shard_map/columns_over_ctx/ppermute | solution.py:52
  73.4 6.7 %collective-permute-start.23 = (bf16[16,1792]{1,0:T(8,128)(2,1)S(1)}, bf16[16,1792]{1,0:T(8,128)(2,1)S(1)}, u32[]{:S(2)}, u32[]{:S(2)}) collective-permute-start(bf16[16,1792]{1,0:T(8,128)(2,1)S(1)} %sum_over_x.9), channel_id=1, source_target_pairs={{0,12},{4,8},{8,4},{12,0},{1,13},{5,9},{9,5},{13,1},{2,14},{6,10},... | collective-permute-start | bytes 172040 | tf_op jit(solution)/shard_map/columns_over_ctx/ppermute | solution.py:52

commit v14 on v13

--- a/solution.py
+++ b/solution.py
@@ -14,9 +14,10 @@
 VD = 128
 HEAD = NOPE + ROPE
 PROJ = NOPE + VD
-SUB_ROWS = 256
+SUB_ROWS = 512
 LOAD_LIMIT = 44
 MASKED = -1e30
+LEAD_KEYS = 0.1
 LEAD_EARLY = 6
 LEAD_NEAR = 2
 LEAD_LATE = 3
@@ -42,6 +43,10 @@
 
 def chunk_rows(owned):
     return (owned // 2, owned // 2)
+
+
+def key_order(n_ctx):
+    return [*range(2, n_ctx), 1]
 
 
 def params(mebibytes):
@@ -167,8 +172,8 @@
     own = lax.axis_index("ctx")
     core = lax.axis_index("head") % 2
     blocks = [(0, 0), (0, 1)]
-    blocks += [(offset, core) for offset in range(1, n_ctx)]
-    blocks += [(offset, 1 - core) for offset in range(1, n_ctx)]
+    blocks += [(offset, core) for offset in key_order(n_ctx)]
+    blocks += [(offset, 1 - core) for offset in key_order(n_ctx)]
     row = lax.broadcasted_iota(jnp.int32, (rows, half), 0)
     column = lax.broadcasted_iota(jnp.int32, (rows, half), 1)
     within_own = row // piece * (query_rows // owners) + start + row % piece
@@ -382,13 +387,14 @@
     with jax.named_scope("keys_over_ctx"):
         kv_t = kv_rows.T
         own_half = jnp.where(core == 0, kv_t[:, :half], kv_t[:, half:])
-        halves = [exchange(own_half, "ctx", n_ctx, offset) for offset in range(1, n_ctx)]
+        halves = [exchange(own_half, "ctx", n_ctx, offset) for offset in key_order(n_ctx)]
     with jax.named_scope("load"):
         q_ext, bias, w_values, own_keys = load(
             queries, w_kv_up, kv_t, stretch_order, prefix_len, n_head, pieces, cache_rows
         )
     with jax.named_scope("keys_over_cores"):
-        halves = [tie(array, [own_keys]) for array in halves]
+        leads = [cost(LEAD_KEYS)] * (n_ctx - 2) + [SHORT]
+        halves = [tie(array, [own_keys], lead) for array, lead in zip(halves, leads)]
         others = [exchange(array, "head", n_head, 1) for array in halves]
     with jax.named_scope("attention"):
         first, *keys = attention(q_ext[0], bias[0], w_values, [own_keys] + halves + others, False)

time: 82.5 us -> 83.5 us (1.012)
  waiting for transfers between devices: 32.1 us -> 34.2 us
    ppermute x24, waiting for transfers between devices: 32.1 us -> 34.2 us  [exchange(): return lax.ppermute(array, axis, [(i, i ^ bit) for i in range(size)])]
  transfers between devices with their start and end apart: 24 -> 24, of which waited for: 10 -> 12; matrix products, arithmetic and copies ran while one was open for 0% -> 0% of each run, Pallas kernels for 18% -> 18%
where the time goes in v14:
time: 83.5 us; the launch traced here: 83.2 us
  waiting for transfers between devices  34.2 us (41%)
  starting transfers between devices  25.1 us (30%)
  Pallas kernels  19.4 us (23%)
  local copies, waits for them, and re-layouts  2.75 us (3%)
  other arithmetic  1 us (1%)
  between operations  0.88 us (1%)
    ppermute x24, waiting for transfers between devices, exchange(): return lax.ppermute(array, axis, [(i, i ^ bit) for i in range(size)])  34.2 us
    ppermute x24, starting transfers between devices, exchange(): return lax.ppermute(array, axis, [(i, i ^ bit) for i in range(size)])  25.1 us
    pallas_call x2, Pallas kernels, attention(): pl.pallas_call(functools.partial(attention_kernel, 0 if gathered else len...  7.33 us
    pallas_call x1, Pallas kernels, load(): pl.pallas_call(functools.partial(load_kernel, owners, pieces, cache_rows)...  5.66 us
    pallas_call x4, Pallas kernels, product(): pl.pallas_call(functools.partial(product_kernel, count, n_x, len(after)),...  5.27 us
    unnamed x10, local copies, waits for them, and re-layouts  2.75 us
  transfers between devices with their start and end apart: 24, of which 12 were waited for; matrix products, arithmetic and copies ran while one was open for 0% of the time, Pallas kernels for 18%

profile of v14, /device:TPU:0, one launch (start us, length us, event | category | flops | bytes accessed | tf_op | source)
XLA Modules:
  0.0 83.2 jit_solution(14735548411893539827)
XLA Ops:
  0.0 1.0 %slice_select_fusion = bf16[576,128]{1,0:T(8,128)(2,1)S(1)} fusion(bf16[576,256]{1,0:T(8,128)(2,1)} %bitcast.3, pred[]{:T(512)S(6)} %eq.5), kind=kLoop, calls=%fused_computation | loop fusion | flops 73728 | bytes 442369 | tf_op jit(solution)/shard_map/keys_over_ctx/jit(_where)/select_n | solution.py:389
  1.0 4.1 %collective-permute-start = (bf16[576,128]{1,0:T(8,128)(2,1)S(1)}, bf16[576,128]{1,0:T(8,128)(2,1)S(1)}, u32[]{:S(2)}, u32[]{:S(2)}) collective-permute-start(bf16[576,128]{1,0:T(8,128)(2,1)S(1)} %slice_select_fusion), channel_id=1, source_target_pairs={{0,8},{4,12},{8,0},{12,4},{1,9},{5,13},{9,1},{13,5},{2,10},{6,14},... | collective-permute-start | bytes 442376 | tf_op jit(solution)/shard_map/keys_over_ctx/ppermute | solution.py:57
  5.1 1.3 %collective-permute-start.1 = (bf16[576,128]{1,0:T(8,128)(2,1)S(1)}, bf16[576,128]{1,0:T(8,128)(2,1)S(1)}, u32[]{:S(2)}, u32[]{:S(2)}) collective-permute-start(bf16[576,128]{1,0:T(8,128)(2,1)S(1)} %slice_select_fusion), channel_id=1, source_target_pairs={{0,12},{4,8},{8,4},{12,0},{1,13},{5,9},{9,5},{13,1},{2,14},{6,10},... | collective-permute-start | bytes 442376 | tf_op jit(solution)/shard_map/keys_over_ctx/ppermute | solution.py:57
  6.5 0.2 collective-permute-start.2
  7.3 0.0 copy-start
  7.3 1.0 %copy-done = bf16[256,576]{0,1:T(8,128)(2,1)S(1)} copy-done((bf16[256,576]{0,1:T(8,128)(2,1)S(1)}, bf16[256,576]{0,1:T(8,128)(2,1)}, u32[]{:S(2)}) %copy-start) | copy-done | bytes 294936
  8.3 1.1 %copy-done.1 = bf16[128,3072]{1,0:T(8,128)(2,1)S(1)} copy-done((bf16[128,3072]{1,0:T(8,128)(2,1)S(1)}, bf16[128,3072]{1,0:T(8,128)(2,1)}, u32[]{:S(2)}) %copy-start.1) | copy-done | bytes 786456
  9.4 0.7 copy-done.2
  10.1 5.7 %load.1 = (bf16[16,64,576]{2,1,0:T(8,128)(2,1)S(1)}, bf16[16,64,576]{2,1,0:T(8,128)(2,1)S(1)}, f32[64,1024]{1,0:T(8,128)S(1)}, f32[64,1024]{1,0:T(8,128)S(1)}, b...) custom-call(s32[4]{0:T(128)S(1)} %copy-done.2, s32[1]{0:T(128)S(6)} %copy.31.prefix_ref, ...), custom_call_target="tpu_custom_call" | custom-call | flops 1024 | bytes 1024 | tf_op jit(solution)/shard_map/load/pallas_call | solution.py:148
  15.8 0.4 collective-permute-done.refs_0_
  16.1 0.0 collective-permute-start.3
  16.2 0.0 collective-permute-done.1.refs_0_
  16.2 0.5 collective-permute-start.4
  16.7 0.0 collective-permute-done.2.refs_0_
  16.7 0.1 collective-permute-start.5
  16.7 0.8 collective-permute-done.3.refs_4_
  17.5 0.2 collective-permute-done.4.refs_5_
  17.7 0.3 collective-permute-done.5.refs_6_
  18.0 3.7 %attention.2 = (bf16[64,2048]{1,0:T(8,128)(2,1)S(1)}, bf16[576,1024]{1,0:T(8,128)(2,1)S(1)}, bf16[1024,512]{1,0:T(8,128)(2,1)S(1)}) custom-call(bf16[16,64,576]{2,1,0:T(8,128)(2,1)S(1)} %get-tuple-element.34.q_ref, f32[64,1024]{1,0:T(8,128)S(1)} %get-tuple-element.35.bias_ref, bf16[16,512,128]{2,1,0:T(8,128)(2,1)S(1)} %get-tuple-element.36.value_ref, ...), custom_call_target="tpu_custom_call" | custom-call | flops 1024 | bytes 1024 | tf_op jit(solution)/shard_map/attention/pallas_call | solution.py:247
  21.7 4.7 %collective-permute-start.9 = (bf16[64,2048]{1,0:T(8,128)(2,1)S(1)}, bf16[64,2048]{1,0:T(8,128)(2,1)S(1)}, u32[]{:S(2)}, u32[]{:S(2)}) collective-permute-start(bf16[64,2048]{1,0:T(8,128)(2,1)S(1)} %get-tuple-element.38.refs_0_), channel_id=1, source_target_pairs={{0,8},{4,12},{8,0},{12,4},{1,9},{5,13},{9,1},{13,5},{2,10},{6,14},... | collective-permute-start | bytes 786440 | tf_op jit(solution)/shard_map/attended_over_ctx/ppermute | solution.py:57
  26.5 0.0 collective-permute-start.8
  26.5 3.7 %attention.3 = (bf16[64,2048]{1,0:T(8,128)(2,1)S(1)}, bf16[64,2048]{1,0:T(8,128)(2,1)S(1)}) custom-call(bf16[16,64,576]{2,1,0:T(8,128)(2,1)S(1)} %get-tuple-element.39.q_ref, f32[64,1024]{1,0:T(8,128)S(1)} %get-tuple-element.40.bias_ref, bf16[16,512,128]{2,1,0:T(8,128)(2,1)S(1)} %get-tuple-element.36.value_ref, ...), custom_call_target="tpu_custom_call" | custom-call | flops 1024 | bytes 1024 | tf_op jit(solution)/shard_map/attention/pallas_call | solution.py:247
  30.1 0.0 slice-done
  30.1 1.1 %out_product.5 = (bf16[2,32,1792]{2,1,0:T(8,128)(2,1)S(1)}, f32[2,32,1792]{2,1,0:T(8,128)S(1)}) custom-call(bf16[2048,1792]{1,0:T(8,128)(2,1)S(1)} %bitcast.2, bf16[64,2048]{1,0:T(8,128)(2,1)S(1)} %get-tuple-element.38.refs_0_, bf16[64,2048]{1,0:T(8,128)(2,1)S(1)} %get-tuple-element.43.refs_1_.refs_3_), custom_call_target="tpu_custom_call" | custom-call | flops 1024 | bytes 1024 | tf_op jit(solution)/shard_map/out_product/pallas_call | solution.py:281
  31.3 0.1 collective-permute-start.6
  31.4 1.1 %collective-permute-start.14 = (bf16[64,2048]{1,0:T(8,128)(2,1)S(1)}, bf16[64,2048]{1,0:T(8,128)(2,1)S(1)}, u32[]{:S(2)}, u32[]{:S(2)}) collective-permute-start(bf16[64,2048]{1,0:T(8,128)(2,1)S(1)} %get-tuple-element.43.refs_1_.refs_3_), channel_id=1, source_target_pairs={{0,8},{4,12},{8,0},{12,4},{1,9},{5,13},{9,1},{13,5},{2,10},{6,14},... | collective-permute-start | bytes 786440 | tf_op jit(solution)/shard_map/attended_over_ctx/ppermute | solution.py:57
  32.4 0.4 collective-permute-done.6.received_ref
  32.9 1.6 %collective-permute-start.7 = (bf16[32,1792]{1,0:T(8,128)(2,1)S(1)}, bf16[32,1792]{1,0:T(8,128)(2,1)S(1)}, u32[]{:S(2)}, u32[]{:S(2)}) collective-permute-start(bf16[32,1792]{1,0:T(8,128)(2,1)S(1)} %get-tuple-element.47), channel_id=1, source_target_pairs={{0,2},{1,3},{2,0},{3,1},{4,6},{5,7},{6,4},{7,5},{8,10},{9,11},{10,... | collective-permute-start | bytes 344072 | tf_op jit(solution)/shard_map/sum_over_x/ppermute | solution.py:57
  34.4 5.3 %collective-permute-done.9.refs_0_ = bf16[64,2048]{1,0:T(8,128)(2,1)S(1)} collective-permute-done((bf16[64,2048]{1,0:T(8,128)(2,1)S(1)}, bf16[64,2048]{1,0:T(8,128)(2,1)S(1)}, u32[]{:S(2)}, u32[]{:S(2)}) %collective-permute-start.9) | collective-permute-done | bytes 262176 | tf_op jit(solution)/shard_map/attended_over_ctx/ppermute | solution.py:57
  39.8 0.0 collective-permute-start.10
  39.8 2.0 %collective-permute-start.13 = (bf16[64,2048]{1,0:T(8,128)(2,1)S(1)}, bf16[64,2048]{1,0:T(8,128)(2,1)S(1)}, u32[]{:S(2)}, u32[]{:S(2)}) collective-permute-start(bf16[64,2048]{1,0:T(8,128)(2,1)S(1)} %attended_over_ctx.7), channel_id=1, source_target_pairs={{0,4},{4,0},{8,12},{12,8},{1,5},{5,1},{9,13},{13,9},{2,6},{6,2},{1... | collective-permute-start | bytes 786440 | tf_op jit(solution)/shard_map/attended_over_ctx/ppermute | solution.py:57
  41.8 0.0 collective-permute-done.8.refs_0_
  41.8 0.0 collective-permute-done.7.refs_1_.refs_4_
  41.8 12.6 %collective-permute-done.10.refs_2_.refs_1_ = bf16[64,2048]{1,0:T(8,128)(2,1)S(1)} collective-permute-done((bf16[64,2048]{1,0:T(8,128)(2,1)S(1)}, bf16[64,2048]{1,0:T(8,128)(2,1)S(1)}, u32[]{:S(2)}, u32[]{:S(2)}) %collective-permute-start.10) | collective-permute-done | bytes 262176 | tf_op jit(solution)/shard_map/attended_over_ctx/ppermute | solution.py:57
  54.4 1.6 %out_product.6 = (bf16[2,48,1792]{2,1,0:T(8,128)(2,1)S(1)}, f32[2,48,1792]{2,1,0:T(8,128)S(1)}) custom-call(bf16[2048,1792]{1,0:T(8,128)(2,1)S(1)} %bitcast.2, bf16[64,2048]{1,0:T(8,128)(2,1)S(1)} %attended_over_ctx.5.refs_0_, bf16[64,2048]{1,0:T(8,128)(2,1)S(1)} %attended_over_ctx.6.refs_1_, bf16[64,2048]{1,0:T(8,128)(2,1)S(1)} %collective-permute-done.10.refs_2_.refs_1_, ...), custom_call_target="tpu_custom_call" | custom-call | flops 1024 | bytes 1024 | tf_op jit(solution)/shard_map/out_product/pallas_call | solution.py:281
  56.0 0.1 collective-permute-start.11
  56.1 0.0 collective-permute-done.14.refs_0_
  56.1 0.1 collective-permute-start.20
  56.2 1.5 %collective-permute-done.11.received_ref = bf16[2,48,1792]{2,1,0:T(8,128)(2,1)S(1)} collective-permute-done((bf16[2,48,1792]{2,1,0:T(8,128)(2,1)S(1)}, bf16[2,48,1792]{2,1,0:T(8,128)(2,1)S(1)}, u32[]{:S(2)}, u32[]{:S(2)}) %collective-permute-start.11) | collective-permute-done | bytes 344096 | tf_op jit(solution)/shard_map/sum_over_cores/ppermute | solution.py:57
  57.7 0.1 sum_over_cores.6
  57.8 1.6 %collective-permute-start.12 = (bf16[48,1792]{1,0:T(8,128)(2,1)S(1)}, bf16[48,1792]{1,0:T(8,128)(2,1)S(1)}, u32[]{:S(2)}, u32[]{:S(2)}) collective-permute-start(bf16[48,1792]{1,0:T(8,128)(2,1)S(1)} %get-tuple-element.51), channel_id=1, source_target_pairs={{0,2},{1,3},{2,0},{3,1},{4,6},{5,7},{6,4},{7,5},{8,10},{9,11},{10,... | collective-permute-start | bytes 516104 | tf_op jit(solution)/shard_map/sum_over_x/ppermute | solution.py:57
  59.4 0.0 collective-permute-done.13.refs_0_
  59.4 1.1 %out_product.7 = (bf16[2,32,1792]{2,1,0:T(8,128)(2,1)S(1)}, f32[2,32,1792]{2,1,0:T(8,128)S(1)}) custom-call(bf16[2048,1792]{1,0:T(8,128)(2,1)S(1)} %bitcast.2, bf16[64,2048]{1,0:T(8,128)(2,1)S(1)} %attended_over_ctx.8.refs_0_, bf16[64,2048]{1,0:T(8,128)(2,1)S(1)} %attended_over_ctx.9.refs_1_, f32[48,1792]{1,0:T(8,128)S(1)} %get-tuple-element.50.refs_2_.refs_0_), custom_call_target="tpu_custom_call" | custom-call | flops 1024 | bytes 1024 | tf_op jit(solution)/shard_map/out_product/pallas_call | solution.py:281
  60.5 0.1 collective-permute-start.15
  60.6 4.2 %collective-permute-done.20.refs_0_ = bf16[64,2048]{1,0:T(8,128)(2,1)S(1)} collective-permute-done((bf16[64,2048]{1,0:T(8,128)(2,1)S(1)}, bf16[64,2048]{1,0:T(8,128)(2,1)S(1)}, u32[]{:S(2)}, u32[]{:S(2)}) %collective-permute-start.20) | collective-permute-done | bytes 262176 | tf_op jit(solution)/shard_map/attended_over_ctx/ppermute | solution.py:57
  64.8 0.0 collective-permute-done.12.refs_1_
  64.8 1.4 %out_product.9 = (bf16[2,16,1792]{2,1,0:T(8,128)(2,1)S(1)}, f32[2,16,1792]{2,1,0:T(8,128)S(1)}) custom-call(bf16[2048,1792]{1,0:T(8,128)(2,1)S(1)} %bitcast.2, bf16[64,2048]{1,0:T(8,128)(2,1)S(1)} %out_product.8.refs_0_), custom_call_target="tpu_custom_call" | custom-call | flops 1024 | bytes 1024 | tf_op jit(solution)/shard_map/out_product/pallas_call | solution.py:281
  66.2 0.0 collective-permute-done.15.received_ref
  66.2 0.1 sum_over_cores.7
  66.3 0.1 collective-permute-start.21
  66.4 1.6 %collective-permute-start.16 = (bf16[32,1792]{1,0:T(8,128)(2,1)S(1)}, bf16[32,1792]{1,0:T(8,128)(2,1)S(1)}, u32[]{:S(2)}, u32[]{:S(2)}) collective-permute-start(bf16[32,1792]{1,0:T(8,128)(2,1)S(1)} %get-tuple-element.56), channel_id=1, source_target_pairs={{0,2},{1,3},{2,0},{3,1},{4,6},{5,7},{6,4},{7,5},{8,10},{9,11},{10,... | collective-permute-start | bytes 344072 | tf_op jit(solution)/shard_map/sum_over_x/ppermute | solution.py:57
  67.9 0.0 collective-permute-done.21.received_ref
  68.0 1.3 %collective-permute-start.22 = (bf16[16,1792]{1,0:T(8,128)(2,1)S(1)}, bf16[16,1792]{1,0:T(8,128)(2,1)S(1)}, u32[]{:S(2)}, u32[]{:S(2)}) collective-permute-start(bf16[16,1792]{1,0:T(8,128)(2,1)S(1)} %sum_over_x.8), channel_id=1, source_target_pairs={{0,2},{1,3},{2,0},{3,1},{4,6},{5,7},{6,4},{7,5},{8,10},{9,11},{10,... | collective-permute-start | bytes 172040 | tf_op jit(solution)/shard_map/sum_over_x/ppermute | solution.py:57
  69.3 0.1 collective-permute-start.19
  69.4 3.0 %collective-permute-done.16.refs_3_ = bf16[32,1792]{1,0:T(8,128)(2,1)S(1)} collective-permute-done((bf16[32,1792]{1,0:T(8,128)(2,1)S(1)}, bf16[32,1792]{1,0:T(8,128)(2,1)S(1)}, u32[]{:S(2)}, u32[]{:S(2)}) %collective-permute-start.16) | collective-permute-done | bytes 114720 | tf_op jit(solution)/shard_map/sum_over_x/ppermute | solution.py:57
  72.4 0.3 collective-permute-start.17
  72.8 1.2 %collective-permute-start.18 = (bf16[32,1792]{1,0:T(8,128)(2,1)S(1)}, bf16[32,1792]{1,0:T(8,128)(2,1)S(1)}, u32[]{:S(2)}, u32[]{:S(2)}) collective-permute-start(bf16[32,1792]{1,0:T(8,128)(2,1)S(1)} %get-tuple-element.58), channel_id=1, source_target_pairs={{0,8},{4,12},{8,0},{12,4},{1,9},{5,13},{9,1},{13,5},{2,10},{6,14},... | collective-permute-start | bytes 344072 | tf_op jit(solution)/shard_map/columns_over_ctx/ppermute | solution.py:57
  73.9 0.0 collective-permute-done.22.refs_1_
  73.9 3.0 %collective-permute-start.23 = (bf16[16,1792]{1,0:T(8,128)(2,1)S(1)}, bf16[16,1792]{1,0:T(8,128)(2,1)S(1)}, u32[]{:S(2)}, u32[]{:S(2)}) collective-permute-start(bf16[16,1792]{1,0:T(8,128)(2,1)S(1)} %sum_over_x.9), channel_id=1, source_target_pairs={{0,12},{4,8},{8,4},{12,0},{1,13},{5,9},{9,5},{13,1},{2,14},{6,10},... | collective-permute-start | bytes 172040 | tf_op jit(solution)/shard_map/columns_over_ctx/ppermute | solution.py:57
  77.0 0.0 collective-permute-done.19.refs_0_
  77.0 4.1 %collective-permute-done.23.refs_4_ = bf16[16,1792]{1,0:T(8,128)(2,1)S(1)} collective-permute-done((bf16[16,1792]{1,0:T(8,128)(2,1)S(1)}, bf16[16,1792]{1,0:T(8,128)(2,1)S(1)}, u32[]{:S(2)}, u32[]{:S(2)}) %collective-permute-start.23) | collective-permute-done | bytes 57376 | tf_op jit(solution)/shard_map/columns_over_ctx/ppermute | solution.py:57
  81.1 0.0 collective-permute-done.17.refs_1_
  81.1 1.3 %collective-permute-done.18.refs_2_ = bf16[32,1792]{1,0:T(8,128)(2,1)S(1)} collective-permute-done((bf16[32,1792]{1,0:T(8,128)(2,1)S(1)}, bf16[32,1792]{1,0:T(8,128)(2,1)S(1)}, u32[]{:S(2)}, u32[]{:S(2)}) %collective-permute-start.18) | collective-permute-done | bytes 114720 | tf_op jit(solution)/shard_map/columns_over_ctx/ppermute | solution.py:57
  82.4 0.8 output.1
  (24 shorter events, 0.2 us)
Async XLA Ops:
  1.0 15.1 %collective-permute-start = (bf16[576,128]{1,0:T(8,128)(2,1)S(1)}, bf16[576,128]{1,0:T(8,128)(2,1)S(1)}, u32[]{:S(2)}, u32[]{:S(2)}) collective-permute-start(bf16[576,128]{1,0:T(8,128)(2,1)S(1)} %slice_select_fusion), channel_id=1, source_target_pairs={{0,8},{4,12},{8,0},{12,4},{1,9},{5,13},{9,1},{13,5},{2,10},{6,14},... | collective-permute-start | bytes 442376 | tf_op jit(solution)/shard_map/keys_over_ctx/ppermute | solution.py:57
  5.1 11.0 %collective-permute-start.1 = (bf16[576,128]{1,0:T(8,128)(2,1)S(1)}, bf16[576,128]{1,0:T(8,128)(2,1)S(1)}, u32[]{:S(2)}, u32[]{:S(2)}) collective-permute-start(bf16[576,128]{1,0:T(8,128)(2,1)S(1)} %slice_select_fusion), channel_id=1, source_target_pairs={{0,12},{4,8},{8,4},{12,0},{1,13},{5,9},{9,5},{13,1},{2,14},{6,10},... | collective-permute-start | bytes 442376 | tf_op jit(solution)/shard_map/keys_over_ctx/ppermute | solution.py:57
  6.5 10.2 %collective-permute-start.2 = (bf16[576,128]{1,0:T(8,128)(2,1)S(1)}, bf16[576,128]{1,0:T(8,128)(2,1)S(1)}, u32[]{:S(2)}, u32[]{:S(2)}) collective-permute-start(bf16[576,128]{1,0:T(8,128)(2,1)S(1)} %slice_select_fusion), channel_id=1, source_target_pairs={{0,4},{4,0},{8,12},{12,8},{1,5},{5,1},{9,13},{13,9},{2,6},{6,2},{1... | collective-permute-start | bytes 442376 | tf_op jit(solution)/shard_map/keys_over_ctx/ppermute | solution.py:57
  7.3 1.0 %copy-start = (bf16[256,576]{0,1:T(8,128)(2,1)S(1)}, bf16[256,576]{0,1:T(8,128)(2,1)}, u32[]{:S(2)}) copy-start(bf16[256,576]{0,1:T(8,128)(2,1)} %param.7) | copy-start | bytes 884740
  8.3 1.1 %copy-start.1 = (bf16[128,3072]{1,0:T(8,128)(2,1)S(1)}, bf16[128,3072]{1,0:T(8,128)(2,1)}, u32[]{:S(2)}) copy-start(bf16[128,3072]{1,0:T(8,128)(2,1)} %q_hbm.1) | copy-start | bytes 2359300
  9.4 0.7 copy-start.2
  10.1 20.0 %slice-start = ((s8[7340032]{0:T(1024)(128)(4,1)}), s8[3145728]{0:T(1024)(128)(4,1)S(1)}, s32[]{:S(2)}) async-start(s8[7340032]{0:T(1024)(128)(4,1)} %bitcast.1), calls=%async_computation | async-start | bytes 6291456
  16.1 1.4 %collective-permute-start.3 = (bf16[576,128]{1,0:T(8,128)(2,1)S(1)}, bf16[576,128]{1,0:T(8,128)(2,1)S(1)}, u32[]{:S(2)}, u32[]{:S(2)}) collective-permute-start(bf16[576,128]{1,0:T(8,128)(2,1)S(1)} %keys_over_cores.3.refs_1_), channel_id=1, source_target_pairs={{0,1},{1,0},{2,3},{3,2},{4,5},{5,4},{6,7},{7,6},{8,9},{9,8},{10,11... | collective-permute-start | bytes 442376 | tf_op jit(solution)/shard_map/keys_over_cores/ppermute | solution.py:57
  16.2 1.6 %collective-permute-start.4 = (bf16[576,128]{1,0:T(8,128)(2,1)S(1)}, bf16[576,128]{1,0:T(8,128)(2,1)S(1)}, u32[]{:S(2)}, u32[]{:S(2)}) collective-permute-start(bf16[576,128]{1,0:T(8,128)(2,1)S(1)} %keys_over_cores.4.refs_2_), channel_id=1, source_target_pairs={{0,1},{1,0},{2,3},{3,2},{4,5},{5,4},{6,7},{7,6},{8,9},{9,8},{10,11... | collective-permute-start | bytes 442376 | tf_op jit(solution)/shard_map/keys_over_cores/ppermute | solution.py:57
  16.7 1.4 %collective-permute-start.5 = (bf16[576,128]{1,0:T(8,128)(2,1)S(1)}, bf16[576,128]{1,0:T(8,128)(2,1)S(1)}, u32[]{:S(2)}, u32[]{:S(2)}) collective-permute-start(bf16[576,128]{1,0:T(8,128)(2,1)S(1)} %keys_over_cores.5.refs_3_), channel_id=1, source_target_pairs={{0,1},{1,0},{2,3},{3,2},{4,5},{5,4},{6,7},{7,6},{8,9},{9,8},{10,11... | collective-permute-start | bytes 442376 | tf_op jit(solution)/shard_map/keys_over_cores/ppermute | solution.py:57
  18.0 12.1 %slice-start.1 = ((s8[7340032]{0:T(1024)(128)(4,1)}), s8[4194304]{0:T(1024)(128)(4,1)S(1)}, s32[]{:S(2)}) async-start(s8[7340032]{0:T(1024)(128)(4,1)} %bitcast.1), calls=%async_computation.1 | async-start | bytes 8388608
  21.7 18.0 %collective-permute-start.9 = (bf16[64,2048]{1,0:T(8,128)(2,1)S(1)}, bf16[64,2048]{1,0:T(8,128)(2,1)S(1)}, u32[]{:S(2)}, u32[]{:S(2)}) collective-permute-start(bf16[64,2048]{1,0:T(8,128)(2,1)S(1)} %get-tuple-element.38.refs_0_), channel_id=1, source_target_pairs={{0,8},{4,12},{8,0},{12,4},{1,9},{5,13},{9,1},{13,5},{2,10},{6,14},... | collective-permute-start | bytes 786440 | tf_op jit(solution)/shard_map/attended_over_ctx/ppermute | solution.py:57
  26.5 15.3 %collective-permute-start.8 = (bf16[64,2048]{1,0:T(8,128)(2,1)S(1)}, bf16[64,2048]{1,0:T(8,128)(2,1)S(1)}, u32[]{:S(2)}, u32[]{:S(2)}) collective-permute-start(bf16[64,2048]{1,0:T(8,128)(2,1)S(1)} %get-tuple-element.38.refs_0_), channel_id=1, source_target_pairs={{0,4},{4,0},{8,12},{12,8},{1,5},{5,1},{9,13},{13,9},{2,6},{6,2},{1... | collective-permute-start | bytes 786440 | tf_op jit(solution)/shard_map/attended_over_ctx/ppermute | solution.py:57
  31.3 1.6 %collective-permute-start.6 = (bf16[2,32,1792]{2,1,0:T(8,128)(2,1)S(1)}, bf16[2,32,1792]{2,1,0:T(8,128)(2,1)S(1)}, u32[]{:S(2)}, u32[]{:S(2)}) collective-permute-start(bf16[2,32,1792]{2,1,0:T(8,128)(2,1)S(1)} %get-tuple-element.45), channel_id=1, source_target_pairs={{0,1},{1,0},{2,3},{3,2},{4,5},{5,4},{6,7},{7,6},{8,9},{9,8},{10,11... | collective-permute-start | bytes 688136 | tf_op jit(solution)/shard_map/sum_over_cores/ppermute | solution.py:57
  31.4 24.7 %collective-permute-start.14 = (bf16[64,2048]{1,0:T(8,128)(2,1)S(1)}, bf16[64,2048]{1,0:T(8,128)(2,1)S(1)}, u32[]{:S(2)}, u32[]{:S(2)}) collective-permute-start(bf16[64,2048]{1,0:T(8,128)(2,1)S(1)} %get-tuple-element.43.refs_1_.refs_3_), channel_id=1, source_target_pairs={{0,8},{4,12},{8,0},{12,4},{1,9},{5,13},{9,1},{13,5},{2,10},{6,14},... | collective-permute-start | bytes 786440 | tf_op jit(solution)/shard_map/attended_over_ctx/ppermute | solution.py:57
  32.9 8.9 %collective-permute-start.7 = (bf16[32,1792]{1,0:T(8,128)(2,1)S(1)}, bf16[32,1792]{1,0:T(8,128)(2,1)S(1)}, u32[]{:S(2)}, u32[]{:S(2)}) collective-permute-start(bf16[32,1792]{1,0:T(8,128)(2,1)S(1)} %get-tuple-element.47), channel_id=1, source_target_pairs={{0,2},{1,3},{2,0},{3,1},{4,6},{5,7},{6,4},{7,5},{8,10},{9,11},{10,... | collective-permute-start | bytes 344072 | tf_op jit(solution)/shard_map/sum_over_x/ppermute | solution.py:57
  39.8 14.6 %collective-permute-start.10 = (bf16[64,2048]{1,0:T(8,128)(2,1)S(1)}, bf16[64,2048]{1,0:T(8,128)(2,1)S(1)}, u32[]{:S(2)}, u32[]{:S(2)}) collective-permute-start(bf16[64,2048]{1,0:T(8,128)(2,1)S(1)} %attended_over_ctx.6.refs_1_), channel_id=1, source_target_pairs={{0,4},{4,0},{8,12},{12,8},{1,5},{5,1},{9,13},{13,9},{2,6},{6,2},{1... | collective-permute-start | bytes 786440 | tf_op jit(solution)/shard_map/attended_over_ctx/ppermute | solution.py:57
  39.8 19.6 %collective-permute-start.13 = (bf16[64,2048]{1,0:T(8,128)(2,1)S(1)}, bf16[64,2048]{1,0:T(8,128)(2,1)S(1)}, u32[]{:S(2)}, u32[]{:S(2)}) collective-permute-start(bf16[64,2048]{1,0:T(8,128)(2,1)S(1)} %attended_over_ctx.7), channel_id=1, source_target_pairs={{0,4},{4,0},{8,12},{12,8},{1,5},{5,1},{9,13},{13,9},{2,6},{6,2},{1... | collective-permute-start | bytes 786440 | tf_op jit(solution)/shard_map/attended_over_ctx/ppermute | solution.py:57
  56.0 1.7 %collective-permute-start.11 = (bf16[2,48,1792]{2,1,0:T(8,128)(2,1)S(1)}, bf16[2,48,1792]{2,1,0:T(8,128)(2,1)S(1)}, u32[]{:S(2)}, u32[]{:S(2)}) collective-permute-start(bf16[2,48,1792]{2,1,0:T(8,128)(2,1)S(1)} %get-tuple-element.49), channel_id=1, source_target_pairs={{0,1},{1,0},{2,3},{3,2},{4,5},{5,4},{6,7},{7,6},{8,9},{9,8},{10,11... | collective-permute-start | bytes 1032200 | tf_op jit(solution)/shard_map/sum_over_cores/ppermute | solution.py:57
  56.1 8.7 %collective-permute-start.20 = (bf16[64,2048]{1,0:T(8,128)(2,1)S(1)}, bf16[64,2048]{1,0:T(8,128)(2,1)S(1)}, u32[]{:S(2)}, u32[]{:S(2)}) collective-permute-start(bf16[64,2048]{1,0:T(8,128)(2,1)S(1)} %attended_over_ctx.9.refs_1_), channel_id=1, source_target_pairs={{0,4},{4,0},{8,12},{12,8},{1,5},{5,1},{9,13},{13,9},{2,6},{6,2},{1... | collective-permute-start | bytes 786440 | tf_op jit(solution)/shard_map/attended_over_ctx/ppermute | solution.py:57
  57.8 7.0 %collective-permute-start.12 = (bf16[48,1792]{1,0:T(8,128)(2,1)S(1)}, bf16[48,1792]{1,0:T(8,128)(2,1)S(1)}, u32[]{:S(2)}, u32[]{:S(2)}) collective-permute-start(bf16[48,1792]{1,0:T(8,128)(2,1)S(1)} %get-tuple-element.51), channel_id=1, source_target_pairs={{0,2},{1,3},{2,0},{3,1},{4,6},{5,7},{6,4},{7,5},{8,10},{9,11},{10,... | collective-permute-start | bytes 516104 | tf_op jit(solution)/shard_map/sum_over_x/ppermute | solution.py:57
  60.5 5.7 %collective-permute-start.15 = (bf16[2,32,1792]{2,1,0:T(8,128)(2,1)S(1)}, bf16[2,32,1792]{2,1,0:T(8,128)(2,1)S(1)}, u32[]{:S(2)}, u32[]{:S(2)}) collective-permute-start(bf16[2,32,1792]{2,1,0:T(8,128)(2,1)S(1)} %get-tuple-element.54), channel_id=1, source_target_pairs={{0,1},{1,0},{2,3},{3,2},{4,5},{5,4},{6,7},{7,6},{8,9},{9,8},{10,11... | collective-permute-start | bytes 688136 | tf_op jit(solution)/shard_map/sum_over_cores/ppermute | solution.py:57
  66.3 1.7 %collective-permute-start.21 = (bf16[2,16,1792]{2,1,0:T(8,128)(2,1)S(1)}, bf16[2,16,1792]{2,1,0:T(8,128)(2,1)S(1)}, u32[]{:S(2)}, u32[]{:S(2)}) collective-permute-start(bf16[2,16,1792]{2,1,0:T(8,128)(2,1)S(1)} %sum_over_cores.8), channel_id=1, source_target_pairs={{0,1},{1,0},{2,3},{3,2},{4,5},{5,4},{6,7},{7,6},{8,9},{9,8},{10,11... | collective-permute-start | bytes 344072 | tf_op jit(solution)/shard_map/sum_over_cores/ppermute | solution.py:57
  66.4 6.0 %collective-permute-start.16 = (bf16[32,1792]{1,0:T(8,128)(2,1)S(1)}, bf16[32,1792]{1,0:T(8,128)(2,1)S(1)}, u32[]{:S(2)}, u32[]{:S(2)}) collective-permute-start(bf16[32,1792]{1,0:T(8,128)(2,1)S(1)} %get-tuple-element.56), channel_id=1, source_target_pairs={{0,2},{1,3},{2,0},{3,1},{4,6},{5,7},{6,4},{7,5},{8,10},{9,11},{10,... | collective-permute-start | bytes 344072 | tf_op jit(solution)/shard_map/sum_over_x/ppermute | solution.py:57
  68.0 5.9 %collective-permute-start.22 = (bf16[16,1792]{1,0:T(8,128)(2,1)S(1)}, bf16[16,1792]{1,0:T(8,128)(2,1)S(1)}, u32[]{:S(2)}, u32[]{:S(2)}) collective-permute-start(bf16[16,1792]{1,0:T(8,128)(2,1)S(1)} %sum_over_x.8), channel_id=1, source_target_pairs={{0,2},{1,3},{2,0},{3,1},{4,6},{5,7},{6,4},{7,5},{8,10},{9,11},{10,... | collective-permute-start | bytes 172040 | tf_op jit(solution)/shard_map/sum_over_x/ppermute | solution.py:57
  69.3 7.7 %collective-permute-start.19 = (bf16[16,1792]{1,0:T(8,128)(2,1)S(1)}, bf16[16,1792]{1,0:T(8,128)(2,1)S(1)}, u32[]{:S(2)}, u32[]{:S(2)}) collective-permute-start(bf16[16,1792]{1,0:T(8,128)(2,1)S(1)} %sum_over_x.7), channel_id=1, source_target_pairs={{0,12},{4,8},{8,4},{12,0},{1,13},{5,9},{9,5},{13,1},{2,14},{6,10},... | collective-permute-start | bytes 172040 | tf_op jit(solution)/shard_map/columns_over_ctx/ppermute | solution.py:57
  72.4 8.7 %collective-permute-start.17 = (bf16[32,1792]{1,0:T(8,128)(2,1)S(1)}, bf16[32,1792]{1,0:T(8,128)(2,1)S(1)}, u32[]{:S(2)}, u32[]{:S(2)}) collective-permute-start(bf16[32,1792]{1,0:T(8,128)(2,1)S(1)} %get-tuple-element.57), channel_id=1, source_target_pairs={{0,4},{4,0},{8,12},{12,8},{1,5},{5,1},{9,13},{13,9},{2,6},{6,2},{1... | collective-permute-start | bytes 344072 | tf_op jit(solution)/shard_map/columns_over_ctx/ppermute | solution.py:57
  72.8 9.7 %collective-permute-start.18 = (bf16[32,1792]{1,0:T(8,128)(2,1)S(1)}, bf16[32,1792]{1,0:T(8,128)(2,1)S(1)}, u32[]{:S(2)}, u32[]{:S(2)}) collective-permute-start(bf16[32,1792]{1,0:T(8,128)(2,1)S(1)} %get-tuple-element.58), channel_id=1, source_target_pairs={{0,8},{4,12},{8,0},{12,4},{1,9},{5,13},{9,1},{13,5},{2,10},{6,14},... | collective-permute-start | bytes 344072 | tf_op jit(solution)/shard_map/columns_over_ctx/ppermute | solution.py:57
  73.9 7.2 %collective-permute-start.23 = (bf16[16,1792]{1,0:T(8,128)(2,1)S(1)}, bf16[16,1792]{1,0:T(8,128)(2,1)S(1)}, u32[]{:S(2)}, u32[]{:S(2)}) collective-permute-start(bf16[16,1792]{1,0:T(8,128)(2,1)S(1)} %sum_over_x.9), channel_id=1, source_target_pairs={{0,12},{4,8},{8,4},{12,0},{1,13},{5,9},{9,5},{13,1},{2,14},{6,10},... | collective-permute-start | bytes 172040 | tf_op jit(solution)/shard_map/columns_over_ctx/ppermute | solution.py:57

commit v15 on v13

--- a/solution.py
+++ b/solution.py
@@ -14,7 +14,8 @@
 VD = 128
 HEAD = NOPE + ROPE
 PROJ = NOPE + VD
-SUB_ROWS = 256
+SUB_ROWS = 512
+ABSORB_LIMIT = 56
 LOAD_LIMIT = 44
 MASKED = -1e30
 LEAD_EARLY = 6
@@ -84,29 +85,19 @@
     return [pieces[offset] for offset in range(size)]
 
 
-def load_kernel(owners, pieces, cache_rows, order_ref, prefix_ref, q_hbm, up_hbm, own_hbm, *refs):
+def absorb_kernel(owners, pieces, first, q_hbm, up_hbm, *refs):
     count = len(pieces)
-    q_exts, biases, refs = refs[:count], refs[count : 2 * count], refs[2 * count :]
-    value_ref, own_ref, q_ref, key_ref, sems, key_sems, value_sems = refs
+    q_exts, (q_ref, key_ref, q_sem, key_sems) = refs[:count], refs[count:]
     rows = q_ref.shape[0]
     head_count = key_ref.shape[0]
-    q_copy = pltpu.make_async_copy(q_hbm, q_ref, sems.at[0])
-    own_copy = pltpu.make_async_copy(own_hbm, own_ref, sems.at[1])
+    window = pl.ds(first * HEAD, head_count * HEAD)
+    q_copy = pltpu.make_async_copy(q_hbm.at[:, window], q_ref, q_sem)
     q_copy.start()
-    key_copies, value_copies = [], []
+    key_copies = []
     for head in range(head_count):
-        source = up_hbm.at[:, pl.ds(head * PROJ, NOPE)]
+        source = up_hbm.at[:, pl.ds((first + head) * PROJ, NOPE)]
         key_copies.append(pltpu.make_async_copy(source, key_ref.at[head], key_sems.at[head]))
-        source = up_hbm.at[:, pl.ds(head * PROJ + NOPE, VD)]
-        value_copies.append(pltpu.make_async_copy(source, value_ref.at[head], value_sems.at[head]))
-    for copy in key_copies + [own_copy] + value_copies:
-        copy.start()
-    start = 0
-    for piece, bias_ref in zip(pieces, biases):
-        visible_bias(
-            order_ref, prefix_ref, bias_ref, rows, owners, start, own_hbm.shape[1], cache_rows
-        )
-        start += piece
+        key_copies[-1].start()
     q_copy.wait()
     for head in range(head_count):
         nope = q_ref[:, head * HEAD : head * HEAD + NOPE]
@@ -124,34 +115,74 @@
             part = rope[:, start : start + piece].reshape(owners * piece, ROPE)
             q_ext[head, :, LAT:] = part.astype(jnp.bfloat16)
             start += piece
-    for copy in [own_copy] + value_copies:
+
+
+def load_kernel(owners, pieces, cache_rows, first, order_ref, prefix_ref, q_hbm, up_hbm, own_hbm, *refs):
+    count = len(pieces)
+    q_exts, biases, refs = refs[:count], refs[count : 2 * count], refs[2 * count :]
+    value_ref, own_ref, q_ref, key_ref, q_sem, key_sems, own_sem, value_sems = refs
+    copies = [pltpu.make_async_copy(own_hbm, own_ref, own_sem)]
+    for head in range(value_ref.shape[0]):
+        source = up_hbm.at[:, pl.ds(head * PROJ + NOPE, VD)]
+        copies.append(pltpu.make_async_copy(source, value_ref.at[head], value_sems.at[head]))
+    for copy in copies:
+        copy.start()
+    start = 0
+    for piece, bias_ref in zip(pieces, biases):
+        visible_bias(
+            order_ref, prefix_ref, bias_ref, q_ref.shape[0], owners, start, own_hbm.shape[1], cache_rows
+        )
+        start += piece
+    absorb_kernel(owners, pieces, first, q_hbm, up_hbm, *q_exts, q_ref, key_ref, q_sem, key_sems)
+    for copy in copies:
         copy.wait()
 
 
-def load(queries, w_kv_up, own_keys, stretch_order, prefix_len, owners, pieces, cache_rows):
-    head_count = w_kv_up.shape[1] // PROJ
-    amount = stretch_order.shape[0] * own_keys.shape[1]
-    out_shape = [
+def absorb_shapes(queries, head_count, owners, pieces):
+    results = [
         jax.ShapeDtypeStruct((head_count, owners * piece, LAT + ROPE), jnp.bfloat16)
         for piece in pieces
     ]
-    out_shape += [jax.ShapeDtypeStruct((owners * piece, amount), jnp.float32) for piece in pieces]
-    out_shape += [
+    scratch = [
+        pltpu.VMEM((queries.shape[0], head_count * HEAD), jnp.bfloat16),
+        pltpu.VMEM((head_count, LAT, NOPE), jnp.bfloat16),
+        pltpu.SemaphoreType.DMA,
+        pltpu.SemaphoreType.DMA((head_count,)),
+    ]
+    return results, scratch
+
+
+def absorb(queries, w_kv_up, owners, pieces):
+    half = w_kv_up.shape[1] // PROJ // 2
+    results, scratch = absorb_shapes(queries, half, owners, pieces)
+    return pl.pallas_call(
+        functools.partial(absorb_kernel, owners, pieces, 0),
+        out_shape=results,
+        in_specs=[IN_HBM] * 2,
+        out_specs=[IN_VMEM] * len(results),
+        scratch_shapes=scratch,
+        compiler_params=params(ABSORB_LIMIT),
+        cost_estimate=SHORT,
+    )(queries, w_kv_up)
+
+
+def load(queries, w_kv_up, own_keys, stretch_order, prefix_len, owners, pieces, cache_rows):
+    head_count = w_kv_up.shape[1] // PROJ
+    half = head_count // 2
+    amount = stretch_order.shape[0] * own_keys.shape[1]
+    results, scratch = absorb_shapes(queries, half, owners, pieces)
+    results += [jax.ShapeDtypeStruct((owners * piece, amount), jnp.float32) for piece in pieces]
+    results += [
         jax.ShapeDtypeStruct((head_count, LAT, VD), jnp.bfloat16),
         jax.ShapeDtypeStruct(own_keys.shape, jnp.bfloat16),
     ]
+    scratch += [pltpu.SemaphoreType.DMA, pltpu.SemaphoreType.DMA((head_count,))]
     out = pl.pallas_call(
-        functools.partial(load_kernel, owners, pieces, cache_rows),
-        out_shape=out_shape,
+        functools.partial(load_kernel, owners, pieces, cache_rows, half),
+        out_shape=results,
         in_specs=[IN_SMEM, IN_SMEM] + [IN_HBM] * 3,
-        out_specs=[IN_VMEM] * len(out_shape),
-        scratch_shapes=[
-            pltpu.VMEM(queries.shape, jnp.bfloat16),
-            pltpu.VMEM((head_count, LAT, NOPE), jnp.bfloat16),
-            pltpu.SemaphoreType.DMA((2,)),
-            pltpu.SemaphoreType.DMA((head_count,)),
-            pltpu.SemaphoreType.DMA((head_count,)),
-        ],
+        out_specs=[IN_VMEM] * len(results),
+        scratch_shapes=scratch,
         compiler_params=params(LOAD_LIMIT),
         cost_estimate=SHORT,
     )(stretch_order, prefix_len, queries, w_kv_up, own_keys)
@@ -185,8 +216,9 @@
         bias_ref[:, index * half : (index + 1) * half] = bias
 
 
-def attention_kernel(count, q_ref, bias_ref, value_ref, *refs):
-    heads, rows, depth = q_ref.shape
+def attention_kernel(count, low_ref, high_ref, bias_ref, value_ref, *refs):
+    part, rows, depth = low_ref.shape
+    heads = 2 * part
     if count:
         piece_refs, (out_ref, keys_ref, latent_ref) = refs[:count], refs[count:]
         start = 0
@@ -198,11 +230,12 @@
     else:
         keys_ref, latent_ref, out_ref, copy_ref = refs
     amount = keys_ref.shape[1]
-    group = max(1, min(heads, SUB_ROWS // rows))
+    group = max(1, min(part, SUB_ROWS // rows))
     size = group * rows
 
     def score(first):
-        queries = q_ref[first : first + group].reshape(size, depth)
+        q_ref = low_ref if first < part else high_ref
+        queries = q_ref[first % part : first % part + group].reshape(size, depth)
         return jnp.dot(queries, keys_ref[...], preferred_element_type=jnp.float32)
 
     scores = score(0)
@@ -231,7 +264,8 @@
 
 
 def attention(q_ext, bias, w_values, keys, gathered):
-    head_count, rows, depth = q_ext.shape
+    part, rows, depth = q_ext[0].shape
+    head_count = 2 * part
     amount = bias.shape[1]
     out_shape = [jax.ShapeDtypeStruct((rows, head_count * VD), jnp.bfloat16)]
     if gathered:
@@ -242,11 +276,11 @@
     return pl.pallas_call(
         functools.partial(attention_kernel, 0 if gathered else len(keys)),
         out_shape=out_shape,
-        in_specs=[IN_VMEM] * (3 + len(keys)),
+        in_specs=[IN_VMEM] * (4 + len(keys)),
         out_specs=[IN_VMEM] * len(out_shape),
         compiler_params=params(16 if amount <= 1024 else 40),
         cost_estimate=SHORT,
-    )(q_ext, bias, w_values, *keys)
+    )(*q_ext, bias, w_values, *keys)
 
 
 def product_kernel(count, n_x, after, weight_ref, *refs):
@@ -382,13 +416,29 @@
     with jax.named_scope("keys_over_ctx"):
         kv_t = kv_rows.T
         own_half = jnp.where(core == 0, kv_t[:, :half], kv_t[:, half:])
-        halves = [exchange(own_half, "ctx", n_ctx, offset) for offset in range(1, n_ctx)]
+        halves = {}
+        for bit in reversed(range(n_ctx.bit_length() - 1)):
+            halves[1 << bit] = exchange(own_half, "ctx", n_ctx, 1 << bit)
     with jax.named_scope("load"):
-        q_ext, bias, w_values, own_keys = load(
+        low = absorb(queries, w_kv_up, n_head, pieces)
+    with jax.named_scope("keys_over_ctx"):
+        direct = list(halves)
+        for offset in direct:
+            halves[offset] = tie(halves[offset], low[:1])
+        for offset in range(3, n_ctx):
+            near = 1 << (offset.bit_length() - 1)
+            if offset != near:
+                halves[offset] = exchange(halves[near], "ctx", n_ctx, offset ^ near)
+    with jax.named_scope("load"):
+        high, bias, w_values, own_keys = load(
             queries, w_kv_up, kv_t, stretch_order, prefix_len, n_head, pieces, cache_rows
         )
+        q_ext = list(zip(low, high))
     with jax.named_scope("keys_over_cores"):
-        halves = [tie(array, [own_keys]) for array in halves]
+        for offset in range(3, n_ctx):
+            if offset not in direct:
+                halves[offset] = tie(halves[offset], [own_keys])
+        halves = [halves[offset] for offset in range(1, n_ctx)]
         others = [exchange(array, "head", n_head, 1) for array in halves]
     with jax.named_scope("attention"):
         first, *keys = attention(q_ext[0], bias[0], w_values, [own_keys] + halves + others, False)

time: 82.5 us -> 84.1 us (1.019)
  starting transfers between devices: 25.7 us -> 27.4 us
  local copies, waits for them, and re-layouts: 2.75 us -> 1.12 us
  Pallas kernels: 19.8 us -> 21.4 us
    pallas_call x1 -> x2, Pallas kernels: 5.66 us -> 7.87 us  [the longest x1 4.33 us: absorb(): pl.pallas_call(functools.partial(absorb_kernel, owners, pieces, 0), out_s...]
    ppermute x24, starting transfers between devices: 25.7 us -> 27.4 us  [exchange(): return lax.ppermute(array, axis, [(i, i ^ bit) for i in range(size)])]
    unnamed x10 -> x18, local copies, waits for them, and re-layouts: 2.75 us -> 1.12 us
  transfers between devices with their start and end apart: 24 -> 24, of which waited for: 10 -> 11; matrix products, arithmetic and copies ran while one was open for 0% -> 0% of each run, Pallas kernels for 18% -> 20%
where the time goes in v15:
time: 84.1 us; the launch traced here: 83.9 us
  waiting for transfers between devices  31.9 us (38%)
  starting transfers between devices  27.4 us (33%)
  Pallas kernels  21.4 us (25%)
  other arithmetic  1.15 us (1%)
  local copies, waits for them, and re-layouts  1.12 us (1%)
  between operations  0.96 us (1%)
    ppermute x24, waiting for transfers between devices, exchange(): return lax.ppermute(array, axis, [(i, i ^ bit) for i in range(size)])  31.9 us
    ppermute x24, starting transfers between devices, exchange(): return lax.ppermute(array, axis, [(i, i ^ bit) for i in range(size)])  27.4 us
    pallas_call x2, Pallas kernels, attention(): pl.pallas_call(functools.partial(attention_kernel, 0 if gathered else len...  7.12 us
    pallas_call x4, Pallas kernels, product(): pl.pallas_call(functools.partial(product_kernel, count, n_x, len(after)),...  5.28 us
    pallas_call x1, Pallas kernels, absorb(): pl.pallas_call(functools.partial(absorb_kernel, owners, pieces, 0), out_s...  4.33 us
    pallas_call x1, Pallas kernels, load(): pl.pallas_call(functools.partial(load_kernel, owners, pieces, cache_rows,...  3.53 us
  transfers between devices with their start and end apart: 24, of which 11 were waited for; matrix products, arithmetic and copies ran while one was open for 0% of the time, Pallas kernels for 20%

profile of v15, /device:TPU:0, one launch (start us, length us, event | category | flops | bytes accessed | tf_op | source)
XLA Modules:
  0.0 83.9 jit_solution(15636309533456616441)
XLA Ops:
  0.0 1.1 %slice_select_fusion = bf16[576,128]{1,0:T(8,128)(2,1)S(1)} fusion(bf16[576,256]{1,0:T(8,128)(2,1)} %bitcast.3, pred[]{:T(512)S(6)} %eq.5), kind=kLoop, calls=%fused_computation | loop fusion | flops 73728 | bytes 442369 | tf_op jit(solution)/shard_map/keys_over_ctx/jit(_where)/select_n | solution.py:418
  1.2 4.1 %collective-permute-start.1 = (bf16[576,128]{1,0:T(8,128)(2,1)S(1)}, bf16[576,128]{1,0:T(8,128)(2,1)S(1)}, u32[]{:S(2)}, u32[]{:S(2)}) collective-permute-start(bf16[576,128]{1,0:T(8,128)(2,1)S(1)} %slice_select_fusion), channel_id=1, source_target_pairs={{0,8},{4,12},{8,0},{12,4},{1,9},{5,13},{9,1},{13,5},{2,10},{6,14},... | collective-permute-start | bytes 442376 | tf_op jit(solution)/shard_map/keys_over_ctx/ppermute | solution.py:53
  5.3 1.6 %collective-permute-start = (bf16[576,128]{1,0:T(8,128)(2,1)S(1)}, bf16[576,128]{1,0:T(8,128)(2,1)S(1)}, u32[]{:S(2)}, u32[]{:S(2)}) collective-permute-start(bf16[576,128]{1,0:T(8,128)(2,1)S(1)} %slice_select_fusion), channel_id=1, source_target_pairs={{0,4},{4,0},{8,12},{12,8},{1,5},{5,1},{9,13},{13,9},{2,6},{6,2},{1... | collective-permute-start | bytes 442376 | tf_op jit(solution)/shard_map/keys_over_ctx/ppermute | solution.py:53
  6.9 4.3 %load.2 = (bf16[8,64,576]{2,1,0:T(8,128)(2,1)}, bf16[8,64,576]{2,1,0:T(8,128)(2,1)}) custom-call(bf16[128,3072]{1,0:T(8,128)(2,1)} %q_hbm.3, bf16[512,4096]{1,0:T(8,128)(2,1)} %up_hbm.3), custom_call_target="tpu_custom_call" | custom-call | flops 1024 | bytes 1024 | tf_op jit(solution)/shard_map/load/pallas_call | solution.py:158
  11.2 1.2 %collective-permute-done.1.refs_0_ = bf16[576,128]{1,0:T(8,128)(2,1)S(1)} collective-permute-done((bf16[576,128]{1,0:T(8,128)(2,1)S(1)}, bf16[576,128]{1,0:T(8,128)(2,1)S(1)}, u32[]{:S(2)}, u32[]{:S(2)}) %collective-permute-start.1) | collective-permute-done | bytes 147488 | tf_op jit(solution)/shard_map/keys_over_ctx/ppermute | solution.py:53
  12.4 1.1 %copy-done.1 = bf16[8,64,576]{2,1,0:T(8,128)(2,1)S(1)} copy-done((bf16[8,64,576]{2,1,0:T(8,128)(2,1)S(1)}, bf16[8,64,576]{2,1,0:T(8,128)(2,1)}, u32[]{:S(2)}) %copy-start.1) | copy-done | bytes 589848
  13.5 0.6 collective-permute-start.2
  14.8 0.0 slice-start
  14.8 3.5 %load.3 = (bf16[8,64,576]{2,1,0:T(8,128)(2,1)S(1)}, bf16[8,64,576]{2,1,0:T(8,128)(2,1)S(1)}, f32[64,1024]{1,0:T(8,128)S(1)}, f32[64,1024]{1,0:T(8,128)S(1)}, bf1...) custom-call(s32[4]{0:T(128)S(1)} %copy-done.6, s32[1]{0:T(128)S(6)} %copy.31.prefix_ref, ...), custom_call_target="tpu_custom_call" | custom-call | flops 1024 | bytes 1024 | tf_op jit(solution)/shard_map/load/pallas_call | solution.py:180
  18.4 0.1 collective-permute-start.4
  18.4 0.0 collective-permute-done.refs_0_
  18.5 0.5 collective-permute-start.3
  19.0 0.0 collective-permute-done.2.refs_0_
  19.0 0.1 collective-permute-start.5
  19.1 1.0 %collective-permute-done.3.refs_4_ = bf16[576,128]{1,0:T(8,128)(2,1)S(1)} collective-permute-done((bf16[576,128]{1,0:T(8,128)(2,1)S(1)}, bf16[576,128]{1,0:T(8,128)(2,1)S(1)}, u32[]{:S(2)}, u32[]{:S(2)}) %collective-permute-start.3) | collective-permute-done | bytes 147488 | tf_op jit(solution)/shard_map/keys_over_cores/ppermute | solution.py:53
  20.0 0.0 collective-permute-done.4.refs_5_
  20.0 0.3 collective-permute-done.5.refs_6_
  20.3 3.5 %attention.2 = (bf16[64,2048]{1,0:T(8,128)(2,1)S(1)}, bf16[576,1024]{1,0:T(8,128)(2,1)S(1)}, bf16[1024,512]{1,0:T(8,128)(2,1)S(1)}) custom-call(bf16[8,64,576]{2,1,0:T(8,128)(2,1)S(1)} %copy-done.2, bf16[8,64,576]{2,1,0:T(8,128)(2,1)S(1)} %get-tuple-element.37.high_ref, f32[64,1024]{1,0:T(8,128)S(1)} %get-tuple-element.38.bias_ref, ...), custom_call_target="tpu_custom_call" | custom-call | flops 1024 | bytes 1024 | tf_op jit(solution)/shard_map/attention/pallas_call | solution.py:276
  23.9 3.4 %collective-permute-start.9 = (bf16[64,2048]{1,0:T(8,128)(2,1)S(1)}, bf16[64,2048]{1,0:T(8,128)(2,1)S(1)}, u32[]{:S(2)}, u32[]{:S(2)}) collective-permute-start(bf16[64,2048]{1,0:T(8,128)(2,1)S(1)} %get-tuple-element.41.refs_0_), channel_id=1, source_target_pairs={{0,8},{4,12},{8,0},{12,4},{1,9},{5,13},{9,1},{13,5},{2,10},{6,14},... | collective-permute-start | bytes 786440 | tf_op jit(solution)/shard_map/attended_over_ctx/ppermute | solution.py:53
  27.3 0.9 %collective-permute-start.8 = (bf16[64,2048]{1,0:T(8,128)(2,1)S(1)}, bf16[64,2048]{1,0:T(8,128)(2,1)S(1)}, u32[]{:S(2)}, u32[]{:S(2)}) collective-permute-start(bf16[64,2048]{1,0:T(8,128)(2,1)S(1)} %get-tuple-element.41.refs_0_), channel_id=1, source_target_pairs={{0,4},{4,0},{8,12},{12,8},{1,5},{5,1},{9,13},{13,9},{2,6},{6,2},{1... | collective-permute-start | bytes 786440 | tf_op jit(solution)/shard_map/attended_over_ctx/ppermute | solution.py:53
  28.3 3.6 %attention.3 = (bf16[64,2048]{1,0:T(8,128)(2,1)S(1)}, bf16[64,2048]{1,0:T(8,128)(2,1)S(1)}) custom-call(bf16[8,64,576]{2,1,0:T(8,128)(2,1)S(1)} %copy-done.5, bf16[8,64,576]{2,1,0:T(8,128)(2,1)S(1)} %get-tuple-element.43.high_ref, f32[64,1024]{1,0:T(8,128)S(1)} %get-tuple-element.44.bias_ref, bf16[16,512,128]{2,1,0:T(8,128)(2,1)S(1)} %get-tuple-element.39.value_ref, ...), custom_call_target="tpu_custom_call" | custom-call | flops 1024 | bytes 1024 | tf_op jit(solution)/shard_map/attention/pallas_call | solution.py:276
  31.8 0.0 slice-done
  31.9 0.0 slice-done.1
  31.9 1.1 %out_product.5 = (bf16[2,32,1792]{2,1,0:T(8,128)(2,1)S(1)}, f32[2,32,1792]{2,1,0:T(8,128)S(1)}) custom-call(bf16[2048,1792]{1,0:T(8,128)(2,1)S(1)} %bitcast.2, bf16[64,2048]{1,0:T(8,128)(2,1)S(1)} %get-tuple-element.41.refs_0_, bf16[64,2048]{1,0:T(8,128)(2,1)S(1)} %get-tuple-element.47.refs_1_.refs_3_), custom_call_target="tpu_custom_call" | custom-call | flops 1024 | bytes 1024 | tf_op jit(solution)/shard_map/out_product/pallas_call | solution.py:310
  33.0 0.1 collective-permute-start.6
  33.1 0.1 collective-permute-start.14
  33.2 1.3 %collective-permute-done.6.received_ref = bf16[2,32,1792]{2,1,0:T(8,128)(2,1)S(1)} collective-permute-done((bf16[2,32,1792]{2,1,0:T(8,128)(2,1)S(1)}, bf16[2,32,1792]{2,1,0:T(8,128)(2,1)S(1)}, u32[]{:S(2)}, u32[]{:S(2)}) %collective-permute-start.6) | collective-permute-done | bytes 229408 | tf_op jit(solution)/shard_map/sum_over_cores/ppermute | solution.py:53
  34.6 1.6 %collective-permute-start.7 = (bf16[32,1792]{1,0:T(8,128)(2,1)S(1)}, bf16[32,1792]{1,0:T(8,128)(2,1)S(1)}, u32[]{:S(2)}, u32[]{:S(2)}) collective-permute-start(bf16[32,1792]{1,0:T(8,128)(2,1)S(1)} %get-tuple-element.51), channel_id=1, source_target_pairs={{0,2},{1,3},{2,0},{3,1},{4,6},{5,7},{6,4},{7,5},{8,10},{9,11},{10,... | collective-permute-start | bytes 344072 | tf_op jit(solution)/shard_map/sum_over_x/ppermute | solution.py:53
  36.2 4.3 %collective-permute-done.9.refs_0_ = bf16[64,2048]{1,0:T(8,128)(2,1)S(1)} collective-permute-done((bf16[64,2048]{1,0:T(8,128)(2,1)S(1)}, bf16[64,2048]{1,0:T(8,128)(2,1)S(1)}, u32[]{:S(2)}, u32[]{:S(2)}) %collective-permute-start.9) | collective-permute-done | bytes 262176 | tf_op jit(solution)/shard_map/attended_over_ctx/ppermute | solution.py:53
  40.5 0.1 collective-permute-start.10
  40.7 1.9 %collective-permute-start.13 = (bf16[64,2048]{1,0:T(8,128)(2,1)S(1)}, bf16[64,2048]{1,0:T(8,128)(2,1)S(1)}, u32[]{:S(2)}, u32[]{:S(2)}) collective-permute-start(bf16[64,2048]{1,0:T(8,128)(2,1)S(1)} %attended_over_ctx.7), channel_id=1, source_target_pairs={{0,4},{4,0},{8,12},{12,8},{1,5},{5,1},{9,13},{13,9},{2,6},{6,2},{1... | collective-permute-start | bytes 786440 | tf_op jit(solution)/shard_map/attended_over_ctx/ppermute | solution.py:53
  42.5 0.0 collective-permute-done.8.refs_0_
  42.5 0.0 collective-permute-done.7.refs_1_.refs_4_
  42.5 12.4 %collective-permute-done.10.refs_2_.refs_1_ = bf16[64,2048]{1,0:T(8,128)(2,1)S(1)} collective-permute-done((bf16[64,2048]{1,0:T(8,128)(2,1)S(1)}, bf16[64,2048]{1,0:T(8,128)(2,1)S(1)}, u32[]{:S(2)}, u32[]{:S(2)}) %collective-permute-start.10) | collective-permute-done | bytes 262176 | tf_op jit(solution)/shard_map/attended_over_ctx/ppermute | solution.py:53
  55.0 1.6 %out_product.6 = (bf16[2,48,1792]{2,1,0:T(8,128)(2,1)S(1)}, f32[2,48,1792]{2,1,0:T(8,128)S(1)}) custom-call(bf16[2048,1792]{1,0:T(8,128)(2,1)S(1)} %bitcast.2, bf16[64,2048]{1,0:T(8,128)(2,1)S(1)} %attended_over_ctx.5.refs_0_, bf16[64,2048]{1,0:T(8,128)(2,1)S(1)} %attended_over_ctx.6.refs_1_, bf16[64,2048]{1,0:T(8,128)(2,1)S(1)} %collective-permute-done.10.refs_2_.refs_1_, ...), custom_call_target="tpu_custom_call" | custom-call | flops 1024 | bytes 1024 | tf_op jit(solution)/shard_map/out_product/pallas_call | solution.py:310
  56.6 0.1 collective-permute-start.11
  56.7 0.0 collective-permute-done.14.refs_0_
  56.7 0.1 collective-permute-start.20
  56.8 1.5 %collective-permute-done.11.received_ref = bf16[2,48,1792]{2,1,0:T(8,128)(2,1)S(1)} collective-permute-done((bf16[2,48,1792]{2,1,0:T(8,128)(2,1)S(1)}, bf16[2,48,1792]{2,1,0:T(8,128)(2,1)S(1)}, u32[]{:S(2)}, u32[]{:S(2)}) %collective-permute-start.11) | collective-permute-done | bytes 344096 | tf_op jit(solution)/shard_map/sum_over_cores/ppermute | solution.py:53
  58.3 0.1 sum_over_cores.6
  58.4 1.6 %collective-permute-start.12 = (bf16[48,1792]{1,0:T(8,128)(2,1)S(1)}, bf16[48,1792]{1,0:T(8,128)(2,1)S(1)}, u32[]{:S(2)}, u32[]{:S(2)}) collective-permute-start(bf16[48,1792]{1,0:T(8,128)(2,1)S(1)} %get-tuple-element.55), channel_id=1, source_target_pairs={{0,2},{1,3},{2,0},{3,1},{4,6},{5,7},{6,4},{7,5},{8,10},{9,11},{10,... | collective-permute-start | bytes 516104 | tf_op jit(solution)/shard_map/sum_over_x/ppermute | solution.py:53
  60.0 0.0 collective-permute-done.13.refs_0_
  60.0 1.1 %out_product.7 = (bf16[2,32,1792]{2,1,0:T(8,128)(2,1)S(1)}, f32[2,32,1792]{2,1,0:T(8,128)S(1)}) custom-call(bf16[2048,1792]{1,0:T(8,128)(2,1)S(1)} %bitcast.2, bf16[64,2048]{1,0:T(8,128)(2,1)S(1)} %attended_over_ctx.8.refs_0_, bf16[64,2048]{1,0:T(8,128)(2,1)S(1)} %attended_over_ctx.9.refs_1_, f32[48,1792]{1,0:T(8,128)S(1)} %get-tuple-element.54.refs_2_.refs_0_), custom_call_target="tpu_custom_call" | custom-call | flops 1024 | bytes 1024 | tf_op jit(solution)/shard_map/out_product/pallas_call | solution.py:310
  61.2 0.1 collective-permute-start.15
  61.2 4.2 %collective-permute-done.20.refs_0_ = bf16[64,2048]{1,0:T(8,128)(2,1)S(1)} collective-permute-done((bf16[64,2048]{1,0:T(8,128)(2,1)S(1)}, bf16[64,2048]{1,0:T(8,128)(2,1)S(1)}, u32[]{:S(2)}, u32[]{:S(2)}) %collective-permute-start.20) | collective-permute-done | bytes 262176 | tf_op jit(solution)/shard_map/attended_over_ctx/ppermute | solution.py:53
  65.4 0.0 collective-permute-done.12.refs_1_
  65.4 1.4 %out_product.9 = (bf16[2,16,1792]{2,1,0:T(8,128)(2,1)S(1)}, f32[2,16,1792]{2,1,0:T(8,128)S(1)}) custom-call(bf16[2048,1792]{1,0:T(8,128)(2,1)S(1)} %bitcast.2, bf16[64,2048]{1,0:T(8,128)(2,1)S(1)} %out_product.8.refs_0_), custom_call_target="tpu_custom_call" | custom-call | flops 1024 | bytes 1024 | tf_op jit(solution)/shard_map/out_product/pallas_call | solution.py:310
  66.8 0.0 collective-permute-done.15.received_ref
  66.8 0.1 sum_over_cores.7
  66.9 0.1 collective-permute-start.21
  67.0 1.6 %collective-permute-start.16 = (bf16[32,1792]{1,0:T(8,128)(2,1)S(1)}, bf16[32,1792]{1,0:T(8,128)(2,1)S(1)}, u32[]{:S(2)}, u32[]{:S(2)}) collective-permute-start(bf16[32,1792]{1,0:T(8,128)(2,1)S(1)} %get-tuple-element.60), channel_id=1, source_target_pairs={{0,2},{1,3},{2,0},{3,1},{4,6},{5,7},{6,4},{7,5},{8,10},{9,11},{10,... | collective-permute-start | bytes 344072 | tf_op jit(solution)/shard_map/sum_over_x/ppermute | solution.py:53
  68.6 0.0 collective-permute-done.21.received_ref
  68.6 1.3 %collective-permute-start.22 = (bf16[16,1792]{1,0:T(8,128)(2,1)S(1)}, bf16[16,1792]{1,0:T(8,128)(2,1)S(1)}, u32[]{:S(2)}, u32[]{:S(2)}) collective-permute-start(bf16[16,1792]{1,0:T(8,128)(2,1)S(1)} %sum_over_x.8), channel_id=1, source_target_pairs={{0,2},{1,3},{2,0},{3,1},{4,6},{5,7},{6,4},{7,5},{8,10},{9,11},{10,... | collective-permute-start | bytes 172040 | tf_op jit(solution)/shard_map/sum_over_x/ppermute | solution.py:53
  69.9 3.0 %collective-permute-start.19 = (bf16[16,1792]{1,0:T(8,128)(2,1)S(1)}, bf16[16,1792]{1,0:T(8,128)(2,1)S(1)}, u32[]{:S(2)}, u32[]{:S(2)}) collective-permute-start(bf16[16,1792]{1,0:T(8,128)(2,1)S(1)} %sum_over_x.7), channel_id=1, source_target_pairs={{0,12},{4,8},{8,4},{12,0},{1,13},{5,9},{9,5},{13,1},{2,14},{6,10},... | collective-permute-start | bytes 172040 | tf_op jit(solution)/shard_map/columns_over_ctx/ppermute | solution.py:53
  72.9 0.1 collective-permute-done.16.refs_3_
  73.0 0.3 collective-permute-start.17
  73.4 3.2 %collective-permute-start.18 = (bf16[32,1792]{1,0:T(8,128)(2,1)S(1)}, bf16[32,1792]{1,0:T(8,128)(2,1)S(1)}, u32[]{:S(2)}, u32[]{:S(2)}) collective-permute-start(bf16[32,1792]{1,0:T(8,128)(2,1)S(1)} %get-tuple-element.62), channel_id=1, source_target_pairs={{0,8},{4,12},{8,0},{12,4},{1,9},{5,13},{9,1},{13,5},{2,10},{6,14},... | collective-permute-start | bytes 344072 | tf_op jit(solution)/shard_map/columns_over_ctx/ppermute | solution.py:53
  76.6 0.0 collective-permute-done.22.refs_1_
  76.6 1.0 %collective-permute-start.23 = (bf16[16,1792]{1,0:T(8,128)(2,1)S(1)}, bf16[16,1792]{1,0:T(8,128)(2,1)S(1)}, u32[]{:S(2)}, u32[]{:S(2)}) collective-permute-start(bf16[16,1792]{1,0:T(8,128)(2,1)S(1)} %sum_over_x.9), channel_id=1, source_target_pairs={{0,12},{4,8},{8,4},{12,0},{1,13},{5,9},{9,5},{13,1},{2,14},{6,10},... | collective-permute-start | bytes 172040 | tf_op jit(solution)/shard_map/columns_over_ctx/ppermute | solution.py:53
  77.6 0.0 collective-permute-done.19.refs_0_
  77.6 5.1 %collective-permute-done.23.refs_4_ = bf16[16,1792]{1,0:T(8,128)(2,1)S(1)} collective-permute-done((bf16[16,1792]{1,0:T(8,128)(2,1)S(1)}, bf16[16,1792]{1,0:T(8,128)(2,1)S(1)}, u32[]{:S(2)}, u32[]{:S(2)}) %collective-permute-start.23) | collective-permute-done | bytes 57376 | tf_op jit(solution)/shard_map/columns_over_ctx/ppermute | solution.py:53
  82.7 0.0 collective-permute-done.17.refs_1_
  82.7 0.5 collective-permute-done.18.refs_2_
  83.1 0.8 output.1
  (33 shorter events, 0.2 us)
Async XLA Ops:
  0.0 14.8 %copy-start.4 = (bf16[256,576]{0,1:T(8,128)(2,1)S(1)}, bf16[256,576]{0,1:T(8,128)(2,1)}, u32[]{:S(2)}) copy-start(bf16[256,576]{0,1:T(8,128)(2,1)} %param.7) | copy-start | bytes 884740
  0.0 14.8 %copy-start.3 = (bf16[128,3072]{1,0:T(8,128)(2,1)S(1)}, bf16[128,3072]{1,0:T(8,128)(2,1)}, u32[]{:S(2)}) copy-start(bf16[128,3072]{1,0:T(8,128)(2,1)} %q_hbm.3) | copy-start | bytes 2359300
  0.0 14.8 %copy-start.6 = (s32[4]{0:T(128)S(1)}, s32[4]{0:T(128)}, u32[]{:S(2)}) copy-start(s32[4]{0:T(128)} %order_ref.1) | copy-start | bytes 52
  0.0 14.8 %copy-start = (bf16[512,4096]{1,0:T(8,128)(2,1)S(1)}, bf16[512,4096]{1,0:T(8,128)(2,1)}, u32[]{:S(2)}) copy-start(bf16[512,4096]{1,0:T(8,128)(2,1)} %up_hbm.3) | copy-start | bytes 12582916
  1.2 11.2 %collective-permute-start.1 = (bf16[576,128]{1,0:T(8,128)(2,1)S(1)}, bf16[576,128]{1,0:T(8,128)(2,1)S(1)}, u32[]{:S(2)}, u32[]{:S(2)}) collective-permute-start(bf16[576,128]{1,0:T(8,128)(2,1)S(1)} %slice_select_fusion), channel_id=1, source_target_pairs={{0,8},{4,12},{8,0},{12,4},{1,9},{5,13},{9,1},{13,5},{2,10},{6,14},... | collective-permute-start | bytes 442376 | tf_op jit(solution)/shard_map/keys_over_ctx/ppermute | solution.py:53
  5.3 13.2 %collective-permute-start = (bf16[576,128]{1,0:T(8,128)(2,1)S(1)}, bf16[576,128]{1,0:T(8,128)(2,1)S(1)}, u32[]{:S(2)}, u32[]{:S(2)}) collective-permute-start(bf16[576,128]{1,0:T(8,128)(2,1)S(1)} %slice_select_fusion), channel_id=1, source_target_pairs={{0,4},{4,0},{8,12},{12,8},{1,5},{5,1},{9,13},{13,9},{2,6},{6,2},{1... | collective-permute-start | bytes 442376 | tf_op jit(solution)/shard_map/keys_over_ctx/ppermute | solution.py:53
  12.4 1.1 %copy-start.1 = (bf16[8,64,576]{2,1,0:T(8,128)(2,1)S(1)}, bf16[8,64,576]{2,1,0:T(8,128)(2,1)}, u32[]{:S(2)}) copy-start(bf16[8,64,576]{2,1,0:T(8,128)(2,1)} %get-tuple-element.36.refs_1_.low_ref) | copy-start | bytes 1769476
  13.5 5.0 %copy-start.2 = (bf16[8,64,576]{2,1,0:T(8,128)(2,1)S(1)}, bf16[8,64,576]{2,1,0:T(8,128)(2,1)}, u32[]{:S(2)}) copy-start(bf16[8,64,576]{2,1,0:T(8,128)(2,1)} %get-tuple-element.36.refs_1_.low_ref) | copy-start | bytes 1769476
  13.5 5.5 %collective-permute-start.2 = (bf16[576,128]{1,0:T(8,128)(2,1)S(1)}, bf16[576,128]{1,0:T(8,128)(2,1)S(1)}, u32[]{:S(2)}, u32[]{:S(2)}) collective-permute-start(bf16[576,128]{1,0:T(8,128)(2,1)S(1)} %keys_over_ctx.3.refs_2_), channel_id=1, source_target_pairs={{0,4},{4,0},{8,12},{12,8},{1,5},{5,1},{9,13},{13,9},{2,6},{6,2},{1... | collective-permute-start | bytes 442376 | tf_op jit(solution)/shard_map/keys_over_ctx/ppermute | solution.py:53
  14.8 17.0 %slice-start = ((s8[7340032]{0:T(1024)(128)(4,1)}), s8[3145728]{0:T(1024)(128)(4,1)S(1)}, s32[]{:S(2)}) async-start(s8[7340032]{0:T(1024)(128)(4,1)} %bitcast.1), calls=%async_computation | async-start | bytes 6291456
  18.4 9.9 %copy-start.5 = (bf16[8,64,576]{2,1,0:T(8,128)(2,1)S(1)}, bf16[8,64,576]{2,1,0:T(8,128)(2,1)}, u32[]{:S(2)}) copy-start(bf16[8,64,576]{2,1,0:T(8,128)(2,1)} %get-tuple-element.42.low_ref) | copy-start | bytes 1769476
  18.4 1.7 %collective-permute-start.4 = (bf16[576,128]{1,0:T(8,128)(2,1)S(1)}, bf16[576,128]{1,0:T(8,128)(2,1)S(1)}, u32[]{:S(2)}, u32[]{:S(2)}) collective-permute-start(bf16[576,128]{1,0:T(8,128)(2,1)S(1)} %keys_over_ctx.3.refs_2_), channel_id=1, source_target_pairs={{0,1},{1,0},{2,3},{3,2},{4,5},{5,4},{6,7},{7,6},{8,9},{9,8},{10,11... | collective-permute-start | bytes 442376 | tf_op jit(solution)/shard_map/keys_over_cores/ppermute | solution.py:53
  18.5 1.5 %collective-permute-start.3 = (bf16[576,128]{1,0:T(8,128)(2,1)S(1)}, bf16[576,128]{1,0:T(8,128)(2,1)S(1)}, u32[]{:S(2)}, u32[]{:S(2)}) collective-permute-start(bf16[576,128]{1,0:T(8,128)(2,1)S(1)} %keys_over_ctx.2.refs_1_), channel_id=1, source_target_pairs={{0,1},{1,0},{2,3},{3,2},{4,5},{5,4},{6,7},{7,6},{8,9},{9,8},{10,11... | collective-permute-start | bytes 442376 | tf_op jit(solution)/shard_map/keys_over_cores/ppermute | solution.py:53
  19.0 1.4 %collective-permute-start.5 = (bf16[576,128]{1,0:T(8,128)(2,1)S(1)}, bf16[576,128]{1,0:T(8,128)(2,1)S(1)}, u32[]{:S(2)}, u32[]{:S(2)}) collective-permute-start(bf16[576,128]{1,0:T(8,128)(2,1)S(1)} %keys_over_cores.1.refs_3_), channel_id=1, source_target_pairs={{0,1},{1,0},{2,3},{3,2},{4,5},{5,4},{6,7},{7,6},{8,9},{9,8},{10,11... | collective-permute-start | bytes 442376 | tf_op jit(solution)/shard_map/keys_over_cores/ppermute | solution.py:53
  20.3 11.5 %slice-start.1 = ((s8[7340032]{0:T(1024)(128)(4,1)}), s8[4194304]{0:T(1024)(128)(4,1)S(1)}, s32[]{:S(2)}) async-start(s8[7340032]{0:T(1024)(128)(4,1)} %bitcast.1), calls=%async_computation.1 | async-start | bytes 8388608
  23.9 16.6 %collective-permute-start.9 = (bf16[64,2048]{1,0:T(8,128)(2,1)S(1)}, bf16[64,2048]{1,0:T(8,128)(2,1)S(1)}, u32[]{:S(2)}, u32[]{:S(2)}) collective-permute-start(bf16[64,2048]{1,0:T(8,128)(2,1)S(1)} %get-tuple-element.41.refs_0_), channel_id=1, source_target_pairs={{0,8},{4,12},{8,0},{12,4},{1,9},{5,13},{9,1},{13,5},{2,10},{6,14},... | collective-permute-start | bytes 786440 | tf_op jit(solution)/shard_map/attended_over_ctx/ppermute | solution.py:53
  27.3 15.2 %collective-permute-start.8 = (bf16[64,2048]{1,0:T(8,128)(2,1)S(1)}, bf16[64,2048]{1,0:T(8,128)(2,1)S(1)}, u32[]{:S(2)}, u32[]{:S(2)}) collective-permute-start(bf16[64,2048]{1,0:T(8,128)(2,1)S(1)} %get-tuple-element.41.refs_0_), channel_id=1, source_target_pairs={{0,4},{4,0},{8,12},{12,8},{1,5},{5,1},{9,13},{13,9},{2,6},{6,2},{1... | collective-permute-start | bytes 786440 | tf_op jit(solution)/shard_map/attended_over_ctx/ppermute | solution.py:53
  33.0 1.6 %collective-permute-start.6 = (bf16[2,32,1792]{2,1,0:T(8,128)(2,1)S(1)}, bf16[2,32,1792]{2,1,0:T(8,128)(2,1)S(1)}, u32[]{:S(2)}, u32[]{:S(2)}) collective-permute-start(bf16[2,32,1792]{2,1,0:T(8,128)(2,1)S(1)} %get-tuple-element.49), channel_id=1, source_target_pairs={{0,1},{1,0},{2,3},{3,2},{4,5},{5,4},{6,7},{7,6},{8,9},{9,8},{10,11... | collective-permute-start | bytes 688136 | tf_op jit(solution)/shard_map/sum_over_cores/ppermute | solution.py:53
  33.1 23.6 %collective-permute-start.14 = (bf16[64,2048]{1,0:T(8,128)(2,1)S(1)}, bf16[64,2048]{1,0:T(8,128)(2,1)S(1)}, u32[]{:S(2)}, u32[]{:S(2)}) collective-permute-start(bf16[64,2048]{1,0:T(8,128)(2,1)S(1)} %get-tuple-element.47.refs_1_.refs_3_), channel_id=1, source_target_pairs={{0,8},{4,12},{8,0},{12,4},{1,9},{5,13},{9,1},{13,5},{2,10},{6,14},... | collective-permute-start | bytes 786440 | tf_op jit(solution)/shard_map/attended_over_ctx/ppermute | solution.py:53
  34.6 7.9 %collective-permute-start.7 = (bf16[32,1792]{1,0:T(8,128)(2,1)S(1)}, bf16[32,1792]{1,0:T(8,128)(2,1)S(1)}, u32[]{:S(2)}, u32[]{:S(2)}) collective-permute-start(bf16[32,1792]{1,0:T(8,128)(2,1)S(1)} %get-tuple-element.51), channel_id=1, source_target_pairs={{0,2},{1,3},{2,0},{3,1},{4,6},{5,7},{6,4},{7,5},{8,10},{9,11},{10,... | collective-permute-start | bytes 344072 | tf_op jit(solution)/shard_map/sum_over_x/ppermute | solution.py:53
  40.5 14.5 %collective-permute-start.10 = (bf16[64,2048]{1,0:T(8,128)(2,1)S(1)}, bf16[64,2048]{1,0:T(8,128)(2,1)S(1)}, u32[]{:S(2)}, u32[]{:S(2)}) collective-permute-start(bf16[64,2048]{1,0:T(8,128)(2,1)S(1)} %attended_over_ctx.6.refs_1_), channel_id=1, source_target_pairs={{0,4},{4,0},{8,12},{12,8},{1,5},{5,1},{9,13},{13,9},{2,6},{6,2},{1... | collective-permute-start | bytes 786440 | tf_op jit(solution)/shard_map/attended_over_ctx/ppermute | solution.py:53
  40.7 19.3 %collective-permute-start.13 = (bf16[64,2048]{1,0:T(8,128)(2,1)S(1)}, bf16[64,2048]{1,0:T(8,128)(2,1)S(1)}, u32[]{:S(2)}, u32[]{:S(2)}) collective-permute-start(bf16[64,2048]{1,0:T(8,128)(2,1)S(1)} %attended_over_ctx.7), channel_id=1, source_target_pairs={{0,4},{4,0},{8,12},{12,8},{1,5},{5,1},{9,13},{13,9},{2,6},{6,2},{1... | collective-permute-start | bytes 786440 | tf_op jit(solution)/shard_map/attended_over_ctx/ppermute | solution.py:53
  56.6 1.7 %collective-permute-start.11 = (bf16[2,48,1792]{2,1,0:T(8,128)(2,1)S(1)}, bf16[2,48,1792]{2,1,0:T(8,128)(2,1)S(1)}, u32[]{:S(2)}, u32[]{:S(2)}) collective-permute-start(bf16[2,48,1792]{2,1,0:T(8,128)(2,1)S(1)} %get-tuple-element.53), channel_id=1, source_target_pairs={{0,1},{1,0},{2,3},{3,2},{4,5},{5,4},{6,7},{7,6},{8,9},{9,8},{10,11... | collective-permute-start | bytes 1032200 | tf_op jit(solution)/shard_map/sum_over_cores/ppermute | solution.py:53
  56.7 8.7 %collective-permute-start.20 = (bf16[64,2048]{1,0:T(8,128)(2,1)S(1)}, bf16[64,2048]{1,0:T(8,128)(2,1)S(1)}, u32[]{:S(2)}, u32[]{:S(2)}) collective-permute-start(bf16[64,2048]{1,0:T(8,128)(2,1)S(1)} %attended_over_ctx.9.refs_1_), channel_id=1, source_target_pairs={{0,4},{4,0},{8,12},{12,8},{1,5},{5,1},{9,13},{13,9},{2,6},{6,2},{1... | collective-permute-start | bytes 786440 | tf_op jit(solution)/shard_map/attended_over_ctx/ppermute | solution.py:53
  58.4 7.0 %collective-permute-start.12 = (bf16[48,1792]{1,0:T(8,128)(2,1)S(1)}, bf16[48,1792]{1,0:T(8,128)(2,1)S(1)}, u32[]{:S(2)}, u32[]{:S(2)}) collective-permute-start(bf16[48,1792]{1,0:T(8,128)(2,1)S(1)} %get-tuple-element.55), channel_id=1, source_target_pairs={{0,2},{1,3},{2,0},{3,1},{4,6},{5,7},{6,4},{7,5},{8,10},{9,11},{10,... | collective-permute-start | bytes 516104 | tf_op jit(solution)/shard_map/sum_over_x/ppermute | solution.py:53
  61.2 5.7 %collective-permute-start.15 = (bf16[2,32,1792]{2,1,0:T(8,128)(2,1)S(1)}, bf16[2,32,1792]{2,1,0:T(8,128)(2,1)S(1)}, u32[]{:S(2)}, u32[]{:S(2)}) collective-permute-start(bf16[2,32,1792]{2,1,0:T(8,128)(2,1)S(1)} %get-tuple-element.58), channel_id=1, source_target_pairs={{0,1},{1,0},{2,3},{3,2},{4,5},{5,4},{6,7},{7,6},{8,9},{9,8},{10,11... | collective-permute-start | bytes 688136 | tf_op jit(solution)/shard_map/sum_over_cores/ppermute | solution.py:53
  66.9 1.7 %collective-permute-start.21 = (bf16[2,16,1792]{2,1,0:T(8,128)(2,1)S(1)}, bf16[2,16,1792]{2,1,0:T(8,128)(2,1)S(1)}, u32[]{:S(2)}, u32[]{:S(2)}) collective-permute-start(bf16[2,16,1792]{2,1,0:T(8,128)(2,1)S(1)} %sum_over_cores.8), channel_id=1, source_target_pairs={{0,1},{1,0},{2,3},{3,2},{4,5},{5,4},{6,7},{7,6},{8,9},{9,8},{10,11... | collective-permute-start | bytes 344072 | tf_op jit(solution)/shard_map/sum_over_cores/ppermute | solution.py:53
  67.0 6.0 %collective-permute-start.16 = (bf16[32,1792]{1,0:T(8,128)(2,1)S(1)}, bf16[32,1792]{1,0:T(8,128)(2,1)S(1)}, u32[]{:S(2)}, u32[]{:S(2)}) collective-permute-start(bf16[32,1792]{1,0:T(8,128)(2,1)S(1)} %get-tuple-element.60), channel_id=1, source_target_pairs={{0,2},{1,3},{2,0},{3,1},{4,6},{5,7},{6,4},{7,5},{8,10},{9,11},{10,... | collective-permute-start | bytes 344072 | tf_op jit(solution)/shard_map/sum_over_x/ppermute | solution.py:53
  68.6 8.0 %collective-permute-start.22 = (bf16[16,1792]{1,0:T(8,128)(2,1)S(1)}, bf16[16,1792]{1,0:T(8,128)(2,1)S(1)}, u32[]{:S(2)}, u32[]{:S(2)}) collective-permute-start(bf16[16,1792]{1,0:T(8,128)(2,1)S(1)} %sum_over_x.8), channel_id=1, source_target_pairs={{0,2},{1,3},{2,0},{3,1},{4,6},{5,7},{6,4},{7,5},{8,10},{9,11},{10,... | collective-permute-start | bytes 172040 | tf_op jit(solution)/shard_map/sum_over_x/ppermute | solution.py:53
  69.9 7.6 %collective-permute-start.19 = (bf16[16,1792]{1,0:T(8,128)(2,1)S(1)}, bf16[16,1792]{1,0:T(8,128)(2,1)S(1)}, u32[]{:S(2)}, u32[]{:S(2)}) collective-permute-start(bf16[16,1792]{1,0:T(8,128)(2,1)S(1)} %sum_over_x.7), channel_id=1, source_target_pairs={{0,12},{4,8},{8,4},{12,0},{1,13},{5,9},{9,5},{13,1},{2,14},{6,10},... | collective-permute-start | bytes 172040 | tf_op jit(solution)/shard_map/columns_over_ctx/ppermute | solution.py:53
  73.0 9.6 %collective-permute-start.17 = (bf16[32,1792]{1,0:T(8,128)(2,1)S(1)}, bf16[32,1792]{1,0:T(8,128)(2,1)S(1)}, u32[]{:S(2)}, u32[]{:S(2)}) collective-permute-start(bf16[32,1792]{1,0:T(8,128)(2,1)S(1)} %get-tuple-element.61), channel_id=1, source_target_pairs={{0,4},{4,0},{8,12},{12,8},{1,5},{5,1},{9,13},{13,9},{2,6},{6,2},{1... | collective-permute-start | bytes 344072 | tf_op jit(solution)/shard_map/columns_over_ctx/ppermute | solution.py:53
  73.4 9.8 %collective-permute-start.18 = (bf16[32,1792]{1,0:T(8,128)(2,1)S(1)}, bf16[32,1792]{1,0:T(8,128)(2,1)S(1)}, u32[]{:S(2)}, u32[]{:S(2)}) collective-permute-start(bf16[32,1792]{1,0:T(8,128)(2,1)S(1)} %get-tuple-element.62), channel_id=1, source_target_pairs={{0,8},{4,12},{8,0},{12,4},{1,9},{5,13},{9,1},{13,5},{2,10},{6,14},... | collective-permute-start | bytes 344072 | tf_op jit(solution)/shard_map/columns_over_ctx/ppermute | solution.py:53
  76.6 6.0 %collective-permute-start.23 = (bf16[16,1792]{1,0:T(8,128)(2,1)S(1)}, bf16[16,1792]{1,0:T(8,128)(2,1)S(1)}, u32[]{:S(2)}, u32[]{:S(2)}) collective-permute-start(bf16[16,1792]{1,0:T(8,128)(2,1)S(1)} %sum_over_x.9), channel_id=1, source_target_pairs={{0,12},{4,8},{8,4},{12,0},{1,13},{5,9},{9,5},{13,1},{2,14},{6,10},... | collective-permute-start | bytes 172040 | tf_op jit(solution)/shard_map/columns_over_ctx/ppermute | solution.py:53

commit v16 on v13

--- a/solution.py
+++ b/solution.py
@@ -14,14 +14,14 @@
 VD = 128
 HEAD = NOPE + ROPE
 PROJ = NOPE + VD
-SUB_ROWS = 256
+SUB_ROWS = 512
 LOAD_LIMIT = 44
 MASKED = -1e30
 LEAD_EARLY = 6
 LEAD_NEAR = 2
 LEAD_LATE = 3
 LEAD_HANDED = 3
-LEAD_AHEAD = 3
+LEAD_AHEAD = 1
 LEAD_X = 1
 LOG2E = 1.4426950408889634
 SCALE = LOG2E / math.sqrt(HEAD)
@@ -438,13 +438,21 @@
             ]
 
     blocks = {0: added([0], [0], lambda offset: [(0, 0), (0, 1)])}
-    ahead = added([1], handed, lambda offset: [(0, offset - 1)])
+    crossing = [offset for offset in range(1, n_ctx) if offset >= n_ctx // 2]
+    ahead = added([1], crossing, lambda offset: [(0, offset - 1)])
     ahead = [tie(block, [], cost(LEAD_AHEAD)) for block in ahead]
-    both = added([1, 2], powers, lambda offset: [(0, offset - 1), (1, powers.index(offset))])
-    behind = added([3], handed, lambda offset: [(0, handed.index(offset))])
-    blocks.update({offset: [block] for offset, block in zip(powers, both)})
-    for offset, first_rows, last_rows in zip(handed, ahead, behind):
-        blocks[offset] = [first_rows, last_rows]
+    blocks.update({offset: [block] for offset, block in zip(crossing, ahead)})
+
+    def rest(unit, offsets):
+        def parts_of(offset):
+            last_rows = (1, offsets.index(offset))
+            return [last_rows] if offset in crossing else [(0, offset - 1), last_rows]
+
+        for offset, block in zip(offsets, added([1, unit], offsets, parts_of)):
+            blocks[offset] = [*blocks.get(offset, []), block]
+
+    rest(2, powers)
+    rest(3, handed)
     with jax.named_scope("output"):
         return place_columns([blocks[d] for d in range(n_ctx)])
 

time: 82.5 us -> 81.5 us (0.988)
  starting transfers between devices: 25.7 us -> 23.3 us
  waiting for transfers between devices: 32.1 us -> 33.9 us
    ppermute x24 -> x25, starting transfers between devices: 25.7 us -> 23.3 us  [exchange(): return lax.ppermute(array, axis, [(i, i ^ bit) for i in range(size)])]
    ppermute x24 -> x25, waiting for transfers between devices: 32.1 us -> 33.9 us  [exchange(): return lax.ppermute(array, axis, [(i, i ^ bit) for i in range(size)])]
  transfers between devices with their start and end apart: 24 -> 25, of which waited for: 10 -> 10; matrix products, arithmetic and copies ran while one was open for 0% -> 0% of each run, Pallas kernels for 18% -> 18%
where the time goes in v16:
time: 81.5 us; the launch traced here: 81.3 us
  waiting for transfers between devices  33.9 us (42%)
  starting transfers between devices  23.3 us (29%)
  Pallas kernels  19.4 us (24%)
  local copies, waits for them, and re-layouts  2.75 us (3%)
  other arithmetic  1 us (1%)
  between operations  0.91 us (1%)
    ppermute x25, waiting for transfers between devices, exchange(): return lax.ppermute(array, axis, [(i, i ^ bit) for i in range(size)])  33.9 us
    ppermute x25, starting transfers between devices, exchange(): return lax.ppermute(array, axis, [(i, i ^ bit) for i in range(size)])  23.3 us
    pallas_call x2, Pallas kernels, attention(): pl.pallas_call(functools.partial(attention_kernel, 0 if gathered else len...  7.33 us
    pallas_call x1, Pallas kernels, load(): pl.pallas_call(functools.partial(load_kernel, owners, pieces, cache_rows)...  5.66 us
    pallas_call x4, Pallas kernels, product(): pl.pallas_call(functools.partial(product_kernel, count, n_x, len(after)),...  5.28 us
    unnamed x10, local copies, waits for them, and re-layouts  2.75 us
  transfers between devices with their start and end apart: 25, of which 10 were waited for; matrix products, arithmetic and copies ran while one was open for 0% of the time, Pallas kernels for 18%

profile of v16, /device:TPU:0, one launch (start us, length us, event | category | flops | bytes accessed | tf_op | source)
XLA Modules:
  0.0 81.3 jit_solution(1685161251789260681)
XLA Ops:
  0.0 1.0 %slice_select_fusion = bf16[576,128]{1,0:T(8,128)(2,1)S(1)} fusion(bf16[576,256]{1,0:T(8,128)(2,1)} %bitcast.3, pred[]{:T(512)S(6)} %eq.5), kind=kLoop, calls=%fused_computation | loop fusion | flops 73728 | bytes 442369 | tf_op jit(solution)/shard_map/keys_over_ctx/jit(_where)/select_n | solution.py:384
  1.0 3.1 %collective-permute-start = (bf16[576,128]{1,0:T(8,128)(2,1)S(1)}, bf16[576,128]{1,0:T(8,128)(2,1)S(1)}, u32[]{:S(2)}, u32[]{:S(2)}) collective-permute-start(bf16[576,128]{1,0:T(8,128)(2,1)S(1)} %slice_select_fusion), channel_id=1, source_target_pairs={{0,4},{4,0},{8,12},{12,8},{1,5},{5,1},{9,13},{13,9},{2,6},{6,2},{1... | collective-permute-start | bytes 442376 | tf_op jit(solution)/shard_map/keys_over_ctx/ppermute | solution.py:52
  4.1 2.6 %collective-permute-start.1 = (bf16[576,128]{1,0:T(8,128)(2,1)S(1)}, bf16[576,128]{1,0:T(8,128)(2,1)S(1)}, u32[]{:S(2)}, u32[]{:S(2)}) collective-permute-start(bf16[576,128]{1,0:T(8,128)(2,1)S(1)} %slice_select_fusion), channel_id=1, source_target_pairs={{0,8},{4,12},{8,0},{12,4},{1,9},{5,13},{9,1},{13,5},{2,10},{6,14},... | collective-permute-start | bytes 442376 | tf_op jit(solution)/shard_map/keys_over_ctx/ppermute | solution.py:52
  6.7 0.0 collective-permute-start.2
  7.3 0.0 copy-start
  7.3 1.0 %copy-done = bf16[256,576]{0,1:T(8,128)(2,1)S(1)} copy-done((bf16[256,576]{0,1:T(8,128)(2,1)S(1)}, bf16[256,576]{0,1:T(8,128)(2,1)}, u32[]{:S(2)}) %copy-start) | copy-done | bytes 294936
  8.3 1.1 %copy-done.1 = bf16[128,3072]{1,0:T(8,128)(2,1)S(1)} copy-done((bf16[128,3072]{1,0:T(8,128)(2,1)S(1)}, bf16[128,3072]{1,0:T(8,128)(2,1)}, u32[]{:S(2)}) %copy-start.1) | copy-done | bytes 786456
  9.4 0.7 copy-done.2
  10.1 5.7 %load.1 = (bf16[16,64,576]{2,1,0:T(8,128)(2,1)S(1)}, bf16[16,64,576]{2,1,0:T(8,128)(2,1)S(1)}, f32[64,1024]{1,0:T(8,128)S(1)}, f32[64,1024]{1,0:T(8,128)S(1)}, b...) custom-call(s32[4]{0:T(128)S(1)} %copy-done.2, s32[1]{0:T(128)S(6)} %copy.33.prefix_ref, ...), custom_call_target="tpu_custom_call" | custom-call | flops 1024 | bytes 1024 | tf_op jit(solution)/shard_map/load/pallas_call | solution.py:143
  15.8 0.0 collective-permute-done.refs_0_
  15.8 0.1 collective-permute-start.3
  15.9 2.2 %collective-permute-done.1.refs_0_ = bf16[576,128]{1,0:T(8,128)(2,1)S(1)} collective-permute-done((bf16[576,128]{1,0:T(8,128)(2,1)S(1)}, bf16[576,128]{1,0:T(8,128)(2,1)S(1)}, u32[]{:S(2)}, u32[]{:S(2)}) %collective-permute-start.1) | collective-permute-done | bytes 147488 | tf_op jit(solution)/shard_map/keys_over_ctx/ppermute | solution.py:52
  18.1 0.0 collective-permute-start.4
  18.1 0.0 collective-permute-done.2.refs_0_
  18.1 0.5 collective-permute-start.5
  18.6 0.0 collective-permute-done.3.refs_4_
  18.6 0.9 %collective-permute-done.4.refs_5_ = bf16[576,128]{1,0:T(8,128)(2,1)S(1)} collective-permute-done((bf16[576,128]{1,0:T(8,128)(2,1)S(1)}, bf16[576,128]{1,0:T(8,128)(2,1)S(1)}, u32[]{:S(2)}, u32[]{:S(2)}) %collective-permute-start.4) | collective-permute-done | bytes 147488 | tf_op jit(solution)/shard_map/keys_over_cores/ppermute | solution.py:52
  19.5 0.2 collective-permute-done.5.refs_6_
  19.7 3.7 %attention.2 = (bf16[64,2048]{1,0:T(8,128)(2,1)S(1)}, bf16[576,1024]{1,0:T(8,128)(2,1)S(1)}, bf16[1024,512]{1,0:T(8,128)(2,1)S(1)}) custom-call(bf16[16,64,576]{2,1,0:T(8,128)(2,1)S(1)} %get-tuple-element.36.q_ref, f32[64,1024]{1,0:T(8,128)S(1)} %get-tuple-element.37.bias_ref, bf16[16,512,128]{2,1,0:T(8,128)(2,1)S(1)} %get-tuple-element.38.value_ref, ...), custom_call_target="tpu_custom_call" | custom-call | flops 1024 | bytes 1024 | tf_op jit(solution)/shard_map/attention/pallas_call | solution.py:242
  23.4 3.2 %collective-permute-start.9 = (bf16[64,2048]{1,0:T(8,128)(2,1)S(1)}, bf16[64,2048]{1,0:T(8,128)(2,1)S(1)}, u32[]{:S(2)}, u32[]{:S(2)}) collective-permute-start(bf16[64,2048]{1,0:T(8,128)(2,1)S(1)} %get-tuple-element.40.refs_0_), channel_id=1, source_target_pairs={{0,8},{4,12},{8,0},{12,4},{1,9},{5,13},{9,1},{13,5},{2,10},{6,14},... | collective-permute-start | bytes 786440 | tf_op jit(solution)/shard_map/attended_over_ctx/ppermute | solution.py:52
  26.5 0.0 collective-permute-start.8
  26.5 3.7 %attention.3 = (bf16[64,2048]{1,0:T(8,128)(2,1)S(1)}, bf16[64,2048]{1,0:T(8,128)(2,1)S(1)}) custom-call(bf16[16,64,576]{2,1,0:T(8,128)(2,1)S(1)} %get-tuple-element.41.q_ref, f32[64,1024]{1,0:T(8,128)S(1)} %get-tuple-element.42.bias_ref, bf16[16,512,128]{2,1,0:T(8,128)(2,1)S(1)} %get-tuple-element.38.value_ref, ...), custom_call_target="tpu_custom_call" | custom-call | flops 1024 | bytes 1024 | tf_op jit(solution)/shard_map/attention/pallas_call | solution.py:242
  30.2 1.1 %out_product.5 = (bf16[2,32,1792]{2,1,0:T(8,128)(2,1)S(1)}, f32[2,32,1792]{2,1,0:T(8,128)S(1)}) custom-call(bf16[2048,1792]{1,0:T(8,128)(2,1)S(1)} %bitcast.2, bf16[64,2048]{1,0:T(8,128)(2,1)S(1)} %get-tuple-element.40.refs_0_, bf16[64,2048]{1,0:T(8,128)(2,1)S(1)} %get-tuple-element.45.refs_1_.refs_3_), custom_call_target="tpu_custom_call" | custom-call | flops 1024 | bytes 1024 | tf_op jit(solution)/shard_map/out_product/pallas_call | solution.py:276
  31.4 0.1 collective-permute-start.6
  31.4 2.0 %collective-permute-start.14 = (bf16[64,2048]{1,0:T(8,128)(2,1)S(1)}, bf16[64,2048]{1,0:T(8,128)(2,1)S(1)}, u32[]{:S(2)}, u32[]{:S(2)}) collective-permute-start(bf16[64,2048]{1,0:T(8,128)(2,1)S(1)} %get-tuple-element.45.refs_1_.refs_3_), channel_id=1, source_target_pairs={{0,8},{4,12},{8,0},{12,4},{1,9},{5,13},{9,1},{13,5},{2,10},{6,14},... | collective-permute-start | bytes 786440 | tf_op jit(solution)/shard_map/attended_over_ctx/ppermute | solution.py:52
  33.4 0.0 collective-permute-done.6.received_ref
  33.5 1.6 %collective-permute-start.7 = (bf16[32,1792]{1,0:T(8,128)(2,1)S(1)}, bf16[32,1792]{1,0:T(8,128)(2,1)S(1)}, u32[]{:S(2)}, u32[]{:S(2)}) collective-permute-start(bf16[32,1792]{1,0:T(8,128)(2,1)S(1)} %get-tuple-element.49), channel_id=1, source_target_pairs={{0,2},{1,3},{2,0},{3,1},{4,6},{5,7},{6,4},{7,5},{8,10},{9,11},{10,... | collective-permute-start | bytes 344072 | tf_op jit(solution)/shard_map/sum_over_x/ppermute | solution.py:52
  35.0 4.5 %collective-permute-done.9.refs_0_ = bf16[64,2048]{1,0:T(8,128)(2,1)S(1)} collective-permute-done((bf16[64,2048]{1,0:T(8,128)(2,1)S(1)}, bf16[64,2048]{1,0:T(8,128)(2,1)S(1)}, u32[]{:S(2)}, u32[]{:S(2)}) %collective-permute-start.9) | collective-permute-done | bytes 262176 | tf_op jit(solution)/shard_map/attended_over_ctx/ppermute | solution.py:52
  39.5 0.0 collective-permute-start.10
  39.5 2.0 %collective-permute-start.13 = (bf16[64,2048]{1,0:T(8,128)(2,1)S(1)}, bf16[64,2048]{1,0:T(8,128)(2,1)S(1)}, u32[]{:S(2)}, u32[]{:S(2)}) collective-permute-start(bf16[64,2048]{1,0:T(8,128)(2,1)S(1)} %attended_over_ctx.7), channel_id=1, source_target_pairs={{0,4},{4,0},{8,12},{12,8},{1,5},{5,1},{9,13},{13,9},{2,6},{6,2},{1... | collective-permute-start | bytes 786440 | tf_op jit(solution)/shard_map/attended_over_ctx/ppermute | solution.py:52
  41.5 0.0 collective-permute-done.8.refs_0_
  41.5 0.0 collective-permute-done.7.refs_1_.refs_4_
  41.5 11.7 %collective-permute-done.10.refs_2_.refs_1_ = bf16[64,2048]{1,0:T(8,128)(2,1)S(1)} collective-permute-done((bf16[64,2048]{1,0:T(8,128)(2,1)S(1)}, bf16[64,2048]{1,0:T(8,128)(2,1)S(1)}, u32[]{:S(2)}, u32[]{:S(2)}) %collective-permute-start.10) | collective-permute-done | bytes 262176 | tf_op jit(solution)/shard_map/attended_over_ctx/ppermute | solution.py:52
  53.2 1.6 %out_product.6 = (bf16[2,48,1792]{2,1,0:T(8,128)(2,1)S(1)}, f32[2,48,1792]{2,1,0:T(8,128)S(1)}) custom-call(bf16[2048,1792]{1,0:T(8,128)(2,1)S(1)} %bitcast.2, bf16[64,2048]{1,0:T(8,128)(2,1)S(1)} %attended_over_ctx.5.refs_0_, bf16[64,2048]{1,0:T(8,128)(2,1)S(1)} %attended_over_ctx.6.refs_1_, bf16[64,2048]{1,0:T(8,128)(2,1)S(1)} %collective-permute-done.10.refs_2_.refs_1_, ...), custom_call_target="tpu_custom_call" | custom-call | flops 1024 | bytes 1024 | tf_op jit(solution)/shard_map/out_product/pallas_call | solution.py:276
  54.8 0.1 collective-permute-start.11
  54.9 0.0 collective-permute-done.14.refs_0_
  54.9 0.1 collective-permute-start.21
  55.0 1.5 %collective-permute-done.11.received_ref = bf16[2,48,1792]{2,1,0:T(8,128)(2,1)S(1)} collective-permute-done((bf16[2,48,1792]{2,1,0:T(8,128)(2,1)S(1)}, bf16[2,48,1792]{2,1,0:T(8,128)(2,1)S(1)}, u32[]{:S(2)}, u32[]{:S(2)}) %collective-permute-start.11) | collective-permute-done | bytes 344096 | tf_op jit(solution)/shard_map/sum_over_cores/ppermute | solution.py:52
  56.5 0.1 sum_over_cores.6
  56.6 1.6 %collective-permute-start.12 = (bf16[48,1792]{1,0:T(8,128)(2,1)S(1)}, bf16[48,1792]{1,0:T(8,128)(2,1)S(1)}, u32[]{:S(2)}, u32[]{:S(2)}) collective-permute-start(bf16[48,1792]{1,0:T(8,128)(2,1)S(1)} %get-tuple-element.53), channel_id=1, source_target_pairs={{0,2},{1,3},{2,0},{3,1},{4,6},{5,7},{6,4},{7,5},{8,10},{9,11},{10,... | collective-permute-start | bytes 516104 | tf_op jit(solution)/shard_map/sum_over_x/ppermute | solution.py:52
  58.2 0.0 collective-permute-done.13.refs_0_
  58.2 1.1 %out_product.7 = (bf16[2,32,1792]{2,1,0:T(8,128)(2,1)S(1)}, f32[2,32,1792]{2,1,0:T(8,128)S(1)}) custom-call(bf16[2048,1792]{1,0:T(8,128)(2,1)S(1)} %bitcast.2, bf16[64,2048]{1,0:T(8,128)(2,1)S(1)} %attended_over_ctx.8.refs_0_, bf16[64,2048]{1,0:T(8,128)(2,1)S(1)} %attended_over_ctx.9.refs_1_, f32[48,1792]{1,0:T(8,128)S(1)} %get-tuple-element.52.refs_2_.refs_0_), custom_call_target="tpu_custom_call" | custom-call | flops 1024 | bytes 1024 | tf_op jit(solution)/shard_map/out_product/pallas_call | solution.py:276
  59.3 0.1 collective-permute-start.15
  59.4 4.2 %collective-permute-done.21.refs_0_ = bf16[64,2048]{1,0:T(8,128)(2,1)S(1)} collective-permute-done((bf16[64,2048]{1,0:T(8,128)(2,1)S(1)}, bf16[64,2048]{1,0:T(8,128)(2,1)S(1)}, u32[]{:S(2)}, u32[]{:S(2)}) %collective-permute-start.21) | collective-permute-done | bytes 262176 | tf_op jit(solution)/shard_map/attended_over_ctx/ppermute | solution.py:52
  63.6 0.0 collective-permute-done.12.refs_1_
  63.6 1.4 %out_product.9 = (bf16[2,16,1792]{2,1,0:T(8,128)(2,1)S(1)}, f32[2,16,1792]{2,1,0:T(8,128)S(1)}) custom-call(bf16[2048,1792]{1,0:T(8,128)(2,1)S(1)} %bitcast.2, bf16[64,2048]{1,0:T(8,128)(2,1)S(1)} %out_product.8.refs_0_), custom_call_target="tpu_custom_call" | custom-call | flops 1024 | bytes 1024 | tf_op jit(solution)/shard_map/out_product/pallas_call | solution.py:276
  65.0 0.0 collective-permute-done.15.received_ref
  65.0 0.1 sum_over_cores.7
  65.1 0.1 collective-permute-start.22
  65.2 1.6 %collective-permute-start.16 = (bf16[32,1792]{1,0:T(8,128)(2,1)S(1)}, bf16[32,1792]{1,0:T(8,128)(2,1)S(1)}, u32[]{:S(2)}, u32[]{:S(2)}) collective-permute-start(bf16[32,1792]{1,0:T(8,128)(2,1)S(1)} %get-tuple-element.58), channel_id=1, source_target_pairs={{0,2},{1,3},{2,0},{3,1},{4,6},{5,7},{6,4},{7,5},{8,10},{9,11},{10,... | collective-permute-start | bytes 344072 | tf_op jit(solution)/shard_map/sum_over_x/ppermute | solution.py:52
  66.8 0.2 collective-permute-start.18
  67.0 2.5 %collective-permute-start.20 = (bf16[16,1792]{1,0:T(8,128)(2,1)S(1)}, bf16[16,1792]{1,0:T(8,128)(2,1)S(1)}, u32[]{:S(2)}, u32[]{:S(2)}) collective-permute-start(bf16[16,1792]{1,0:T(8,128)(2,1)S(1)} %get-tuple-element.62), channel_id=1, source_target_pairs={{0,12},{4,8},{8,4},{12,0},{1,13},{5,9},{9,5},{13,1},{2,14},{6,10},... | collective-permute-start | bytes 172040 | tf_op jit(solution)/shard_map/columns_over_ctx/ppermute | solution.py:52
  69.5 0.0 collective-permute-done.22.received_ref
  69.5 0.6 collective-permute-start.23
  70.1 0.6 collective-permute-done.16.refs_3_
  70.8 0.3 collective-permute-start.17
  71.1 3.0 %collective-permute-done.18.refs_0_ = bf16[16,1792]{1,0:T(8,128)(2,1)S(1)} collective-permute-done((bf16[16,1792]{1,0:T(8,128)(2,1)S(1)}, bf16[16,1792]{1,0:T(8,128)(2,1)S(1)}, u32[]{:S(2)}, u32[]{:S(2)}) %collective-permute-start.18) | collective-permute-done | bytes 57376 | tf_op jit(solution)/shard_map/columns_over_ctx/ppermute | solution.py:52
  74.1 0.0 collective-permute-done.23.refs_3_
  74.1 1.2 %collective-permute-start.24 = (bf16[16,1792]{1,0:T(8,128)(2,1)S(1)}, bf16[16,1792]{1,0:T(8,128)(2,1)S(1)}, u32[]{:S(2)}, u32[]{:S(2)}) collective-permute-start(bf16[16,1792]{1,0:T(8,128)(2,1)S(1)} %sum_over_x.9), channel_id=1, source_target_pairs={{0,12},{4,8},{8,4},{12,0},{1,13},{5,9},{9,5},{13,1},{2,14},{6,10},... | collective-permute-start | bytes 172040 | tf_op jit(solution)/shard_map/columns_over_ctx/ppermute | solution.py:52
  75.3 0.0 collective-permute-done.20.refs_0_
  75.3 5.1 %collective-permute-done.19.refs_3_ = bf16[16,1792]{1,0:T(8,128)(2,1)S(1)} collective-permute-done((bf16[16,1792]{1,0:T(8,128)(2,1)S(1)}, bf16[16,1792]{1,0:T(8,128)(2,1)S(1)}, u32[]{:S(2)}, u32[]{:S(2)}) %collective-permute-start.19) | collective-permute-done | bytes 57376 | tf_op jit(solution)/shard_map/columns_over_ctx/ppermute | solution.py:52
  80.4 0.0 collective-permute-done.24.refs_5_
  80.4 0.0 collective-permute-done.17.refs_1_
  80.4 0.8 %output.1 = bf16[32,7168]{1,0:T(8,128)(2,1)} custom-call(bf16[32,1792]{1,0:T(8,128)(2,1)S(1)} %sum_over_x.5.refs_0_, bf16[32,1792]{1,0:T(8,128)(2,1)S(1)} %collective-permute-done.17.refs_1_, bf16[16,1792]{1,0:T(8,128)(2,1)S(1)} %shard_map.64.refs_2_, bf16[16,1792]{1,0:T(8,128)(2,1)S(1)} %collective-permute-done.19.refs_3_, ...), custom_call_target="tpu_custom_call" | custom-call | flops 1024 | bytes 1024 | tf_op jit(solution)/shard_map/output/pallas_call | solution.py:362
  (27 shorter events, 0.2 us)
Async XLA Ops:
  1.0 14.8 %collective-permute-start = (bf16[576,128]{1,0:T(8,128)(2,1)S(1)}, bf16[576,128]{1,0:T(8,128)(2,1)S(1)}, u32[]{:S(2)}, u32[]{:S(2)}) collective-permute-start(bf16[576,128]{1,0:T(8,128)(2,1)S(1)} %slice_select_fusion), channel_id=1, source_target_pairs={{0,4},{4,0},{8,12},{12,8},{1,5},{5,1},{9,13},{13,9},{2,6},{6,2},{1... | collective-permute-start | bytes 442376 | tf_op jit(solution)/shard_map/keys_over_ctx/ppermute | solution.py:52
  4.1 14.0 %collective-permute-start.1 = (bf16[576,128]{1,0:T(8,128)(2,1)S(1)}, bf16[576,128]{1,0:T(8,128)(2,1)S(1)}, u32[]{:S(2)}, u32[]{:S(2)}) collective-permute-start(bf16[576,128]{1,0:T(8,128)(2,1)S(1)} %slice_select_fusion), channel_id=1, source_target_pairs={{0,8},{4,12},{8,0},{12,4},{1,9},{5,13},{9,1},{13,5},{2,10},{6,14},... | collective-permute-start | bytes 442376 | tf_op jit(solution)/shard_map/keys_over_ctx/ppermute | solution.py:52
  6.7 11.4 %collective-permute-start.2 = (bf16[576,128]{1,0:T(8,128)(2,1)S(1)}, bf16[576,128]{1,0:T(8,128)(2,1)S(1)}, u32[]{:S(2)}, u32[]{:S(2)}) collective-permute-start(bf16[576,128]{1,0:T(8,128)(2,1)S(1)} %slice_select_fusion), channel_id=1, source_target_pairs={{0,12},{4,8},{8,4},{12,0},{1,13},{5,9},{9,5},{13,1},{2,14},{6,10},... | collective-permute-start | bytes 442376 | tf_op jit(solution)/shard_map/keys_over_ctx/ppermute | solution.py:52
  7.3 1.0 %copy-start = (bf16[256,576]{0,1:T(8,128)(2,1)S(1)}, bf16[256,576]{0,1:T(8,128)(2,1)}, u32[]{:S(2)}) copy-start(bf16[256,576]{0,1:T(8,128)(2,1)} %param.7) | copy-start | bytes 884740
  8.3 1.1 %copy-start.1 = (bf16[128,3072]{1,0:T(8,128)(2,1)S(1)}, bf16[128,3072]{1,0:T(8,128)(2,1)}, u32[]{:S(2)}) copy-start(bf16[128,3072]{1,0:T(8,128)(2,1)} %q_hbm.1) | copy-start | bytes 2359300
  9.4 0.7 copy-start.2
  10.1 20.1 %slice-start = ((s8[7340032]{0:T(1024)(128)(4,1)}), s8[3145728]{0:T(1024)(128)(4,1)S(1)}, s32[]{:S(2)}) async-start(s8[7340032]{0:T(1024)(128)(4,1)} %bitcast.1), calls=%async_computation | async-start | bytes 6291456
  15.8 2.8 %collective-permute-start.3 = (bf16[576,128]{1,0:T(8,128)(2,1)S(1)}, bf16[576,128]{1,0:T(8,128)(2,1)S(1)}, u32[]{:S(2)}, u32[]{:S(2)}) collective-permute-start(bf16[576,128]{1,0:T(8,128)(2,1)S(1)} %keys_over_cores.3.refs_1_), channel_id=1, source_target_pairs={{0,1},{1,0},{2,3},{3,2},{4,5},{5,4},{6,7},{7,6},{8,9},{9,8},{10,11... | collective-permute-start | bytes 442376 | tf_op jit(solution)/shard_map/keys_over_cores/ppermute | solution.py:52
  18.1 1.4 %collective-permute-start.4 = (bf16[576,128]{1,0:T(8,128)(2,1)S(1)}, bf16[576,128]{1,0:T(8,128)(2,1)S(1)}, u32[]{:S(2)}, u32[]{:S(2)}) collective-permute-start(bf16[576,128]{1,0:T(8,128)(2,1)S(1)} %keys_over_cores.4.refs_2_), channel_id=1, source_target_pairs={{0,1},{1,0},{2,3},{3,2},{4,5},{5,4},{6,7},{7,6},{8,9},{9,8},{10,11... | collective-permute-start | bytes 442376 | tf_op jit(solution)/shard_map/keys_over_cores/ppermute | solution.py:52
  18.1 1.6 %collective-permute-start.5 = (bf16[576,128]{1,0:T(8,128)(2,1)S(1)}, bf16[576,128]{1,0:T(8,128)(2,1)S(1)}, u32[]{:S(2)}, u32[]{:S(2)}) collective-permute-start(bf16[576,128]{1,0:T(8,128)(2,1)S(1)} %keys_over_cores.5.refs_3_), channel_id=1, source_target_pairs={{0,1},{1,0},{2,3},{3,2},{4,5},{5,4},{6,7},{7,6},{8,9},{9,8},{10,11... | collective-permute-start | bytes 442376 | tf_op jit(solution)/shard_map/keys_over_cores/ppermute | solution.py:52
  19.7 10.5 %slice-start.1 = ((s8[7340032]{0:T(1024)(128)(4,1)}), s8[4194304]{0:T(1024)(128)(4,1)S(1)}, s32[]{:S(2)}) async-start(s8[7340032]{0:T(1024)(128)(4,1)} %bitcast.1), calls=%async_computation.1 | async-start | bytes 8388608
  23.4 16.1 %collective-permute-start.9 = (bf16[64,2048]{1,0:T(8,128)(2,1)S(1)}, bf16[64,2048]{1,0:T(8,128)(2,1)S(1)}, u32[]{:S(2)}, u32[]{:S(2)}) collective-permute-start(bf16[64,2048]{1,0:T(8,128)(2,1)S(1)} %get-tuple-element.40.refs_0_), channel_id=1, source_target_pairs={{0,8},{4,12},{8,0},{12,4},{1,9},{5,13},{9,1},{13,5},{2,10},{6,14},... | collective-permute-start | bytes 786440 | tf_op jit(solution)/shard_map/attended_over_ctx/ppermute | solution.py:52
  26.5 15.0 %collective-permute-start.8 = (bf16[64,2048]{1,0:T(8,128)(2,1)S(1)}, bf16[64,2048]{1,0:T(8,128)(2,1)S(1)}, u32[]{:S(2)}, u32[]{:S(2)}) collective-permute-start(bf16[64,2048]{1,0:T(8,128)(2,1)S(1)} %get-tuple-element.40.refs_0_), channel_id=1, source_target_pairs={{0,4},{4,0},{8,12},{12,8},{1,5},{5,1},{9,13},{13,9},{2,6},{6,2},{1... | collective-permute-start | bytes 786440 | tf_op jit(solution)/shard_map/attended_over_ctx/ppermute | solution.py:52
  31.4 2.1 %collective-permute-start.6 = (bf16[2,32,1792]{2,1,0:T(8,128)(2,1)S(1)}, bf16[2,32,1792]{2,1,0:T(8,128)(2,1)S(1)}, u32[]{:S(2)}, u32[]{:S(2)}) collective-permute-start(bf16[2,32,1792]{2,1,0:T(8,128)(2,1)S(1)} %get-tuple-element.47), channel_id=1, source_target_pairs={{0,1},{1,0},{2,3},{3,2},{4,5},{5,4},{6,7},{7,6},{8,9},{9,8},{10,11... | collective-permute-start | bytes 688136 | tf_op jit(solution)/shard_map/sum_over_cores/ppermute | solution.py:52
  31.4 23.4 %collective-permute-start.14 = (bf16[64,2048]{1,0:T(8,128)(2,1)S(1)}, bf16[64,2048]{1,0:T(8,128)(2,1)S(1)}, u32[]{:S(2)}, u32[]{:S(2)}) collective-permute-start(bf16[64,2048]{1,0:T(8,128)(2,1)S(1)} %get-tuple-element.45.refs_1_.refs_3_), channel_id=1, source_target_pairs={{0,8},{4,12},{8,0},{12,4},{1,9},{5,13},{9,1},{13,5},{2,10},{6,14},... | collective-permute-start | bytes 786440 | tf_op jit(solution)/shard_map/attended_over_ctx/ppermute | solution.py:52
  33.5 8.0 %collective-permute-start.7 = (bf16[32,1792]{1,0:T(8,128)(2,1)S(1)}, bf16[32,1792]{1,0:T(8,128)(2,1)S(1)}, u32[]{:S(2)}, u32[]{:S(2)}) collective-permute-start(bf16[32,1792]{1,0:T(8,128)(2,1)S(1)} %get-tuple-element.49), channel_id=1, source_target_pairs={{0,2},{1,3},{2,0},{3,1},{4,6},{5,7},{6,4},{7,5},{8,10},{9,11},{10,... | collective-permute-start | bytes 344072 | tf_op jit(solution)/shard_map/sum_over_x/ppermute | solution.py:52
  39.5 13.7 %collective-permute-start.10 = (bf16[64,2048]{1,0:T(8,128)(2,1)S(1)}, bf16[64,2048]{1,0:T(8,128)(2,1)S(1)}, u32[]{:S(2)}, u32[]{:S(2)}) collective-permute-start(bf16[64,2048]{1,0:T(8,128)(2,1)S(1)} %attended_over_ctx.6.refs_1_), channel_id=1, source_target_pairs={{0,4},{4,0},{8,12},{12,8},{1,5},{5,1},{9,13},{13,9},{2,6},{6,2},{1... | collective-permute-start | bytes 786440 | tf_op jit(solution)/shard_map/attended_over_ctx/ppermute | solution.py:52
  39.5 18.7 %collective-permute-start.13 = (bf16[64,2048]{1,0:T(8,128)(2,1)S(1)}, bf16[64,2048]{1,0:T(8,128)(2,1)S(1)}, u32[]{:S(2)}, u32[]{:S(2)}) collective-permute-start(bf16[64,2048]{1,0:T(8,128)(2,1)S(1)} %attended_over_ctx.7), channel_id=1, source_target_pairs={{0,4},{4,0},{8,12},{12,8},{1,5},{5,1},{9,13},{13,9},{2,6},{6,2},{1... | collective-permute-start | bytes 786440 | tf_op jit(solution)/shard_map/attended_over_ctx/ppermute | solution.py:52
  54.8 1.7 %collective-permute-start.11 = (bf16[2,48,1792]{2,1,0:T(8,128)(2,1)S(1)}, bf16[2,48,1792]{2,1,0:T(8,128)(2,1)S(1)}, u32[]{:S(2)}, u32[]{:S(2)}) collective-permute-start(bf16[2,48,1792]{2,1,0:T(8,128)(2,1)S(1)} %get-tuple-element.51), channel_id=1, source_target_pairs={{0,1},{1,0},{2,3},{3,2},{4,5},{5,4},{6,7},{7,6},{8,9},{9,8},{10,11... | collective-permute-start | bytes 1032200 | tf_op jit(solution)/shard_map/sum_over_cores/ppermute | solution.py:52
  54.9 8.7 %collective-permute-start.21 = (bf16[64,2048]{1,0:T(8,128)(2,1)S(1)}, bf16[64,2048]{1,0:T(8,128)(2,1)S(1)}, u32[]{:S(2)}, u32[]{:S(2)}) collective-permute-start(bf16[64,2048]{1,0:T(8,128)(2,1)S(1)} %attended_over_ctx.9.refs_1_), channel_id=1, source_target_pairs={{0,4},{4,0},{8,12},{12,8},{1,5},{5,1},{9,13},{13,9},{2,6},{6,2},{1... | collective-permute-start | bytes 786440 | tf_op jit(solution)/shard_map/attended_over_ctx/ppermute | solution.py:52
  56.6 7.0 %collective-permute-start.12 = (bf16[48,1792]{1,0:T(8,128)(2,1)S(1)}, bf16[48,1792]{1,0:T(8,128)(2,1)S(1)}, u32[]{:S(2)}, u32[]{:S(2)}) collective-permute-start(bf16[48,1792]{1,0:T(8,128)(2,1)S(1)} %get-tuple-element.53), channel_id=1, source_target_pairs={{0,2},{1,3},{2,0},{3,1},{4,6},{5,7},{6,4},{7,5},{8,10},{9,11},{10,... | collective-permute-start | bytes 516104 | tf_op jit(solution)/shard_map/sum_over_x/ppermute | solution.py:52
  59.3 5.7 %collective-permute-start.15 = (bf16[2,32,1792]{2,1,0:T(8,128)(2,1)S(1)}, bf16[2,32,1792]{2,1,0:T(8,128)(2,1)S(1)}, u32[]{:S(2)}, u32[]{:S(2)}) collective-permute-start(bf16[2,32,1792]{2,1,0:T(8,128)(2,1)S(1)} %get-tuple-element.56), channel_id=1, source_target_pairs={{0,1},{1,0},{2,3},{3,2},{4,5},{5,4},{6,7},{7,6},{8,9},{9,8},{10,11... | collective-permute-start | bytes 688136 | tf_op jit(solution)/shard_map/sum_over_cores/ppermute | solution.py:52
  65.1 4.4 %collective-permute-start.22 = (bf16[2,16,1792]{2,1,0:T(8,128)(2,1)S(1)}, bf16[2,16,1792]{2,1,0:T(8,128)(2,1)S(1)}, u32[]{:S(2)}, u32[]{:S(2)}) collective-permute-start(bf16[2,16,1792]{2,1,0:T(8,128)(2,1)S(1)} %sum_over_cores.8), channel_id=1, source_target_pairs={{0,1},{1,0},{2,3},{3,2},{4,5},{5,4},{6,7},{7,6},{8,9},{9,8},{10,11... | collective-permute-start | bytes 344072 | tf_op jit(solution)/shard_map/sum_over_cores/ppermute | solution.py:52
  65.2 5.6 %collective-permute-start.16 = (bf16[32,1792]{1,0:T(8,128)(2,1)S(1)}, bf16[32,1792]{1,0:T(8,128)(2,1)S(1)}, u32[]{:S(2)}, u32[]{:S(2)}) collective-permute-start(bf16[32,1792]{1,0:T(8,128)(2,1)S(1)} %get-tuple-element.58), channel_id=1, source_target_pairs={{0,2},{1,3},{2,0},{3,1},{4,6},{5,7},{6,4},{7,5},{8,10},{9,11},{10,... | collective-permute-start | bytes 344072 | tf_op jit(solution)/shard_map/sum_over_x/ppermute | solution.py:52
  66.8 7.3 %collective-permute-start.18 = (bf16[16,1792]{1,0:T(8,128)(2,1)S(1)}, bf16[16,1792]{1,0:T(8,128)(2,1)S(1)}, u32[]{:S(2)}, u32[]{:S(2)}) collective-permute-start(bf16[16,1792]{1,0:T(8,128)(2,1)S(1)} %get-tuple-element.60), channel_id=1, source_target_pairs={{0,8},{4,12},{8,0},{12,4},{1,9},{5,13},{9,1},{13,5},{2,10},{6,14},... | collective-permute-start | bytes 172040 | tf_op jit(solution)/shard_map/columns_over_ctx/ppermute | solution.py:52
  67.0 8.3 %collective-permute-start.20 = (bf16[16,1792]{1,0:T(8,128)(2,1)S(1)}, bf16[16,1792]{1,0:T(8,128)(2,1)S(1)}, u32[]{:S(2)}, u32[]{:S(2)}) collective-permute-start(bf16[16,1792]{1,0:T(8,128)(2,1)S(1)} %get-tuple-element.62), channel_id=1, source_target_pairs={{0,12},{4,8},{8,4},{12,0},{1,13},{5,9},{9,5},{13,1},{2,14},{6,10},... | collective-permute-start | bytes 172040 | tf_op jit(solution)/shard_map/columns_over_ctx/ppermute | solution.py:52
  69.5 4.6 %collective-permute-start.23 = (bf16[16,1792]{1,0:T(8,128)(2,1)S(1)}, bf16[16,1792]{1,0:T(8,128)(2,1)S(1)}, u32[]{:S(2)}, u32[]{:S(2)}) collective-permute-start(bf16[16,1792]{1,0:T(8,128)(2,1)S(1)} %sum_over_x.8), channel_id=1, source_target_pairs={{0,2},{1,3},{2,0},{3,1},{4,6},{5,7},{6,4},{7,5},{8,10},{9,11},{10,... | collective-permute-start | bytes 172040 | tf_op jit(solution)/shard_map/sum_over_x/ppermute | solution.py:52
  70.8 9.7 %collective-permute-start.17 = (bf16[32,1792]{1,0:T(8,128)(2,1)S(1)}, bf16[32,1792]{1,0:T(8,128)(2,1)S(1)}, u32[]{:S(2)}, u32[]{:S(2)}) collective-permute-start(bf16[32,1792]{1,0:T(8,128)(2,1)S(1)} %get-tuple-element.59), channel_id=1, source_target_pairs={{0,4},{4,0},{8,12},{12,8},{1,5},{5,1},{9,13},{13,9},{2,6},{6,2},{1... | collective-permute-start | bytes 344072 | tf_op jit(solution)/shard_map/columns_over_ctx/ppermute | solution.py:52
  74.1 6.3 %collective-permute-start.19 = (bf16[16,1792]{1,0:T(8,128)(2,1)S(1)}, bf16[16,1792]{1,0:T(8,128)(2,1)S(1)}, u32[]{:S(2)}, u32[]{:S(2)}) collective-permute-start(bf16[16,1792]{1,0:T(8,128)(2,1)S(1)} %get-tuple-element.61), channel_id=1, source_target_pairs={{0,8},{4,12},{8,0},{12,4},{1,9},{5,13},{9,1},{13,5},{2,10},{6,14},... | collective-permute-start | bytes 172040 | tf_op jit(solution)/shard_map/columns_over_ctx/ppermute | solution.py:52
  74.1 6.3 %collective-permute-start.24 = (bf16[16,1792]{1,0:T(8,128)(2,1)S(1)}, bf16[16,1792]{1,0:T(8,128)(2,1)S(1)}, u32[]{:S(2)}, u32[]{:S(2)}) collective-permute-start(bf16[16,1792]{1,0:T(8,128)(2,1)S(1)} %sum_over_x.9), channel_id=1, source_target_pairs={{0,12},{4,8},{8,4},{12,0},{1,13},{5,9},{9,5},{13,1},{2,14},{6,10},... | collective-permute-start | bytes 172040 | tf_op jit(solution)/shard_map/columns_over_ctx/ppermute | solution.py:52

commit v17 on v16

--- a/solution.py
+++ b/solution.py
@@ -21,7 +21,7 @@
 LEAD_NEAR = 2
 LEAD_LATE = 3
 LEAD_HANDED = 3
-LEAD_AHEAD = 1
+LEAD_AHEAD = 2
 LEAD_X = 1
 LOG2E = 1.4426950408889634
 SCALE = LOG2E / math.sqrt(HEAD)
@@ -440,7 +440,7 @@
     blocks = {0: added([0], [0], lambda offset: [(0, 0), (0, 1)])}
     crossing = [offset for offset in range(1, n_ctx) if offset >= n_ctx // 2]
     ahead = added([1], crossing, lambda offset: [(0, offset - 1)])
-    ahead = [tie(block, [], cost(LEAD_AHEAD)) for block in ahead]
+    ahead[0] = tie(ahead[0], ahead[1:], cost(LEAD_AHEAD))
     blocks.update({offset: [block] for offset, block in zip(crossing, ahead)})
 
     def rest(unit, offsets):

time: 81.5 us -> 81.5 us (level)
  starting transfers between devices: 23.3 us -> 27 us
  waiting for transfers between devices: 33.9 us -> 30.2 us
    ppermute x25, starting transfers between devices: 23.3 us -> 27 us  [exchange(): return lax.ppermute(array, axis, [(i, i ^ bit) for i in range(size)])]
    ppermute x25, waiting for transfers between devices: 33.9 us -> 30.2 us  [exchange(): return lax.ppermute(array, axis, [(i, i ^ bit) for i in range(size)])]
where the time goes in v17:
time: 81.5 us; the launch traced here: 81.3 us
  waiting for transfers between devices  30.2 us (37%)
  starting transfers between devices  27 us (33%)
  Pallas kernels  19.4 us (24%)
  local copies, waits for them, and re-layouts  2.75 us (3%)
  other arithmetic  1 us (1%)
  between operations  0.9 us (1%)
    ppermute x25, waiting for transfers between devices, exchange(): return lax.ppermute(array, axis, [(i, i ^ bit) for i in range(size)])  30.2 us
    ppermute x25, starting transfers between devices, exchange(): return lax.ppermute(array, axis, [(i, i ^ bit) for i in range(size)])  27 us
    pallas_call x2, Pallas kernels, attention(): pl.pallas_call(functools.partial(attention_kernel, 0 if gathered else len...  7.33 us
    pallas_call x1, Pallas kernels, load(): pl.pallas_call(functools.partial(load_kernel, owners, pieces, cache_rows)...  5.66 us
    pallas_call x4, Pallas kernels, product(): pl.pallas_call(functools.partial(product_kernel, count, n_x, len(after)),...  5.28 us
    unnamed x10, local copies, waits for them, and re-layouts  2.75 us
  transfers between devices with their start and end apart: 25, of which 10 were waited for; matrix products, arithmetic and copies ran while one was open for 0% of the time, Pallas kernels for 18%

profile of v17, /device:TPU:0, one launch (start us, length us, event | category | flops | bytes accessed | tf_op | source)
XLA Modules:
  0.0 81.3 jit_solution(1438798762085566278)
XLA Ops:
  0.0 1.0 %slice_select_fusion = bf16[576,128]{1,0:T(8,128)(2,1)S(1)} fusion(bf16[576,256]{1,0:T(8,128)(2,1)} %bitcast.3, pred[]{:T(512)S(6)} %eq.5), kind=kLoop, calls=%fused_computation | loop fusion | flops 73728 | bytes 442369 | tf_op jit(solution)/shard_map/keys_over_ctx/jit(_where)/select_n | solution.py:384
  1.0 3.1 %collective-permute-start = (bf16[576,128]{1,0:T(8,128)(2,1)S(1)}, bf16[576,128]{1,0:T(8,128)(2,1)S(1)}, u32[]{:S(2)}, u32[]{:S(2)}) collective-permute-start(bf16[576,128]{1,0:T(8,128)(2,1)S(1)} %slice_select_fusion), channel_id=1, source_target_pairs={{0,4},{4,0},{8,12},{12,8},{1,5},{5,1},{9,13},{13,9},{2,6},{6,2},{1... | collective-permute-start | bytes 442376 | tf_op jit(solution)/shard_map/keys_over_ctx/ppermute | solution.py:52
  4.1 2.6 %collective-permute-start.1 = (bf16[576,128]{1,0:T(8,128)(2,1)S(1)}, bf16[576,128]{1,0:T(8,128)(2,1)S(1)}, u32[]{:S(2)}, u32[]{:S(2)}) collective-permute-start(bf16[576,128]{1,0:T(8,128)(2,1)S(1)} %slice_select_fusion), channel_id=1, source_target_pairs={{0,8},{4,12},{8,0},{12,4},{1,9},{5,13},{9,1},{13,5},{2,10},{6,14},... | collective-permute-start | bytes 442376 | tf_op jit(solution)/shard_map/keys_over_ctx/ppermute | solution.py:52
  6.7 0.0 collective-permute-start.2
  7.3 0.0 copy-start
  7.3 1.0 %copy-done = bf16[256,576]{0,1:T(8,128)(2,1)S(1)} copy-done((bf16[256,576]{0,1:T(8,128)(2,1)S(1)}, bf16[256,576]{0,1:T(8,128)(2,1)}, u32[]{:S(2)}) %copy-start) | copy-done | bytes 294936
  8.3 1.1 %copy-done.1 = bf16[128,3072]{1,0:T(8,128)(2,1)S(1)} copy-done((bf16[128,3072]{1,0:T(8,128)(2,1)S(1)}, bf16[128,3072]{1,0:T(8,128)(2,1)}, u32[]{:S(2)}) %copy-start.1) | copy-done | bytes 786456
  9.4 0.7 copy-done.2
  10.1 5.7 %load.1 = (bf16[16,64,576]{2,1,0:T(8,128)(2,1)S(1)}, bf16[16,64,576]{2,1,0:T(8,128)(2,1)S(1)}, f32[64,1024]{1,0:T(8,128)S(1)}, f32[64,1024]{1,0:T(8,128)S(1)}, b...) custom-call(s32[4]{0:T(128)S(1)} %copy-done.2, s32[1]{0:T(128)S(6)} %copy.31.prefix_ref, ...), custom_call_target="tpu_custom_call" | custom-call | flops 1024 | bytes 1024 | tf_op jit(solution)/shard_map/load/pallas_call | solution.py:143
  15.8 0.0 collective-permute-done.refs_0_
  15.8 0.1 collective-permute-start.3
  15.9 2.2 %collective-permute-done.1.refs_0_ = bf16[576,128]{1,0:T(8,128)(2,1)S(1)} collective-permute-done((bf16[576,128]{1,0:T(8,128)(2,1)S(1)}, bf16[576,128]{1,0:T(8,128)(2,1)S(1)}, u32[]{:S(2)}, u32[]{:S(2)}) %collective-permute-start.1) | collective-permute-done | bytes 147488 | tf_op jit(solution)/shard_map/keys_over_ctx/ppermute | solution.py:52
  18.1 0.0 collective-permute-start.4
  18.1 0.0 collective-permute-done.2.refs_0_
  18.1 0.5 collective-permute-start.5
  18.6 0.0 collective-permute-done.3.refs_4_
  18.6 0.9 %collective-permute-done.4.refs_5_ = bf16[576,128]{1,0:T(8,128)(2,1)S(1)} collective-permute-done((bf16[576,128]{1,0:T(8,128)(2,1)S(1)}, bf16[576,128]{1,0:T(8,128)(2,1)S(1)}, u32[]{:S(2)}, u32[]{:S(2)}) %collective-permute-start.4) | collective-permute-done | bytes 147488 | tf_op jit(solution)/shard_map/keys_over_cores/ppermute | solution.py:52
  19.5 0.2 collective-permute-done.5.refs_6_
  19.7 3.7 %attention.2 = (bf16[64,2048]{1,0:T(8,128)(2,1)S(1)}, bf16[576,1024]{1,0:T(8,128)(2,1)S(1)}, bf16[1024,512]{1,0:T(8,128)(2,1)S(1)}) custom-call(bf16[16,64,576]{2,1,0:T(8,128)(2,1)S(1)} %get-tuple-element.36.q_ref, f32[64,1024]{1,0:T(8,128)S(1)} %get-tuple-element.37.bias_ref, bf16[16,512,128]{2,1,0:T(8,128)(2,1)S(1)} %get-tuple-element.38.value_ref, ...), custom_call_target="tpu_custom_call" | custom-call | flops 1024 | bytes 1024 | tf_op jit(solution)/shard_map/attention/pallas_call | solution.py:242
  23.4 3.2 %collective-permute-start.9 = (bf16[64,2048]{1,0:T(8,128)(2,1)S(1)}, bf16[64,2048]{1,0:T(8,128)(2,1)S(1)}, u32[]{:S(2)}, u32[]{:S(2)}) collective-permute-start(bf16[64,2048]{1,0:T(8,128)(2,1)S(1)} %get-tuple-element.40.refs_0_), channel_id=1, source_target_pairs={{0,8},{4,12},{8,0},{12,4},{1,9},{5,13},{9,1},{13,5},{2,10},{6,14},... | collective-permute-start | bytes 786440 | tf_op jit(solution)/shard_map/attended_over_ctx/ppermute | solution.py:52
  26.5 0.0 collective-permute-start.8
  26.5 3.7 %attention.3 = (bf16[64,2048]{1,0:T(8,128)(2,1)S(1)}, bf16[64,2048]{1,0:T(8,128)(2,1)S(1)}) custom-call(bf16[16,64,576]{2,1,0:T(8,128)(2,1)S(1)} %get-tuple-element.41.q_ref, f32[64,1024]{1,0:T(8,128)S(1)} %get-tuple-element.42.bias_ref, bf16[16,512,128]{2,1,0:T(8,128)(2,1)S(1)} %get-tuple-element.38.value_ref, ...), custom_call_target="tpu_custom_call" | custom-call | flops 1024 | bytes 1024 | tf_op jit(solution)/shard_map/attention/pallas_call | solution.py:242
  30.2 1.1 %out_product.5 = (bf16[2,32,1792]{2,1,0:T(8,128)(2,1)S(1)}, f32[2,32,1792]{2,1,0:T(8,128)S(1)}) custom-call(bf16[2048,1792]{1,0:T(8,128)(2,1)S(1)} %bitcast.2, bf16[64,2048]{1,0:T(8,128)(2,1)S(1)} %get-tuple-element.40.refs_0_, bf16[64,2048]{1,0:T(8,128)(2,1)S(1)} %get-tuple-element.45.refs_1_.refs_3_), custom_call_target="tpu_custom_call" | custom-call | flops 1024 | bytes 1024 | tf_op jit(solution)/shard_map/out_product/pallas_call | solution.py:276
  31.4 0.1 collective-permute-start.6
  31.4 2.0 %collective-permute-start.14 = (bf16[64,2048]{1,0:T(8,128)(2,1)S(1)}, bf16[64,2048]{1,0:T(8,128)(2,1)S(1)}, u32[]{:S(2)}, u32[]{:S(2)}) collective-permute-start(bf16[64,2048]{1,0:T(8,128)(2,1)S(1)} %get-tuple-element.45.refs_1_.refs_3_), channel_id=1, source_target_pairs={{0,8},{4,12},{8,0},{12,4},{1,9},{5,13},{9,1},{13,5},{2,10},{6,14},... | collective-permute-start | bytes 786440 | tf_op jit(solution)/shard_map/attended_over_ctx/ppermute | solution.py:52
  33.4 0.0 collective-permute-done.6.received_ref
  33.5 1.6 %collective-permute-start.7 = (bf16[32,1792]{1,0:T(8,128)(2,1)S(1)}, bf16[32,1792]{1,0:T(8,128)(2,1)S(1)}, u32[]{:S(2)}, u32[]{:S(2)}) collective-permute-start(bf16[32,1792]{1,0:T(8,128)(2,1)S(1)} %get-tuple-element.49), channel_id=1, source_target_pairs={{0,2},{1,3},{2,0},{3,1},{4,6},{5,7},{6,4},{7,5},{8,10},{9,11},{10,... | collective-permute-start | bytes 344072 | tf_op jit(solution)/shard_map/sum_over_x/ppermute | solution.py:52
  35.0 4.5 %collective-permute-done.9.refs_0_ = bf16[64,2048]{1,0:T(8,128)(2,1)S(1)} collective-permute-done((bf16[64,2048]{1,0:T(8,128)(2,1)S(1)}, bf16[64,2048]{1,0:T(8,128)(2,1)S(1)}, u32[]{:S(2)}, u32[]{:S(2)}) %collective-permute-start.9) | collective-permute-done | bytes 262176 | tf_op jit(solution)/shard_map/attended_over_ctx/ppermute | solution.py:52
  39.5 0.0 collective-permute-start.10
  39.5 2.0 %collective-permute-start.13 = (bf16[64,2048]{1,0:T(8,128)(2,1)S(1)}, bf16[64,2048]{1,0:T(8,128)(2,1)S(1)}, u32[]{:S(2)}, u32[]{:S(2)}) collective-permute-start(bf16[64,2048]{1,0:T(8,128)(2,1)S(1)} %attended_over_ctx.7), channel_id=1, source_target_pairs={{0,4},{4,0},{8,12},{12,8},{1,5},{5,1},{9,13},{13,9},{2,6},{6,2},{1... | collective-permute-start | bytes 786440 | tf_op jit(solution)/shard_map/attended_over_ctx/ppermute | solution.py:52
  41.5 0.0 collective-permute-done.8.refs_0_
  41.5 0.0 collective-permute-done.7.refs_1_.refs_4_
  41.5 11.7 %collective-permute-done.10.refs_2_.refs_1_ = bf16[64,2048]{1,0:T(8,128)(2,1)S(1)} collective-permute-done((bf16[64,2048]{1,0:T(8,128)(2,1)S(1)}, bf16[64,2048]{1,0:T(8,128)(2,1)S(1)}, u32[]{:S(2)}, u32[]{:S(2)}) %collective-permute-start.10) | collective-permute-done | bytes 262176 | tf_op jit(solution)/shard_map/attended_over_ctx/ppermute | solution.py:52
  53.2 1.6 %out_product.6 = (bf16[2,48,1792]{2,1,0:T(8,128)(2,1)S(1)}, f32[2,48,1792]{2,1,0:T(8,128)S(1)}) custom-call(bf16[2048,1792]{1,0:T(8,128)(2,1)S(1)} %bitcast.2, bf16[64,2048]{1,0:T(8,128)(2,1)S(1)} %attended_over_ctx.5.refs_0_, bf16[64,2048]{1,0:T(8,128)(2,1)S(1)} %attended_over_ctx.6.refs_1_, bf16[64,2048]{1,0:T(8,128)(2,1)S(1)} %collective-permute-done.10.refs_2_.refs_1_, ...), custom_call_target="tpu_custom_call" | custom-call | flops 1024 | bytes 1024 | tf_op jit(solution)/shard_map/out_product/pallas_call | solution.py:276
  54.8 0.1 collective-permute-start.11
  54.9 0.0 collective-permute-done.14.refs_0_
  54.9 0.1 collective-permute-start.21
  55.0 1.5 %collective-permute-done.11.received_ref = bf16[2,48,1792]{2,1,0:T(8,128)(2,1)S(1)} collective-permute-done((bf16[2,48,1792]{2,1,0:T(8,128)(2,1)S(1)}, bf16[2,48,1792]{2,1,0:T(8,128)(2,1)S(1)}, u32[]{:S(2)}, u32[]{:S(2)}) %collective-permute-start.11) | collective-permute-done | bytes 344096 | tf_op jit(solution)/shard_map/sum_over_cores/ppermute | solution.py:52
  56.5 0.1 sum_over_cores.6
  56.6 1.6 %collective-permute-start.12 = (bf16[48,1792]{1,0:T(8,128)(2,1)S(1)}, bf16[48,1792]{1,0:T(8,128)(2,1)S(1)}, u32[]{:S(2)}, u32[]{:S(2)}) collective-permute-start(bf16[48,1792]{1,0:T(8,128)(2,1)S(1)} %get-tuple-element.53), channel_id=1, source_target_pairs={{0,2},{1,3},{2,0},{3,1},{4,6},{5,7},{6,4},{7,5},{8,10},{9,11},{10,... | collective-permute-start | bytes 516104 | tf_op jit(solution)/shard_map/sum_over_x/ppermute | solution.py:52
  58.2 0.0 collective-permute-done.13.refs_0_
  58.2 1.1 %out_product.7 = (bf16[2,32,1792]{2,1,0:T(8,128)(2,1)S(1)}, f32[2,32,1792]{2,1,0:T(8,128)S(1)}) custom-call(bf16[2048,1792]{1,0:T(8,128)(2,1)S(1)} %bitcast.2, bf16[64,2048]{1,0:T(8,128)(2,1)S(1)} %attended_over_ctx.8.refs_0_, bf16[64,2048]{1,0:T(8,128)(2,1)S(1)} %attended_over_ctx.9.refs_1_, f32[48,1792]{1,0:T(8,128)S(1)} %get-tuple-element.52.refs_2_.refs_0_), custom_call_target="tpu_custom_call" | custom-call | flops 1024 | bytes 1024 | tf_op jit(solution)/shard_map/out_product/pallas_call | solution.py:276
  59.3 0.1 collective-permute-start.15
  59.4 4.2 %collective-permute-done.21.refs_0_ = bf16[64,2048]{1,0:T(8,128)(2,1)S(1)} collective-permute-done((bf16[64,2048]{1,0:T(8,128)(2,1)S(1)}, bf16[64,2048]{1,0:T(8,128)(2,1)S(1)}, u32[]{:S(2)}, u32[]{:S(2)}) %collective-permute-start.21) | collective-permute-done | bytes 262176 | tf_op jit(solution)/shard_map/attended_over_ctx/ppermute | solution.py:52
  63.6 0.0 collective-permute-done.12.refs_1_
  63.6 1.4 %out_product.9 = (bf16[2,16,1792]{2,1,0:T(8,128)(2,1)S(1)}, f32[2,16,1792]{2,1,0:T(8,128)S(1)}) custom-call(bf16[2048,1792]{1,0:T(8,128)(2,1)S(1)} %bitcast.2, bf16[64,2048]{1,0:T(8,128)(2,1)S(1)} %out_product.8.refs_0_), custom_call_target="tpu_custom_call" | custom-call | flops 1024 | bytes 1024 | tf_op jit(solution)/shard_map/out_product/pallas_call | solution.py:276
  65.0 0.0 collective-permute-done.15.received_ref
  65.0 0.1 sum_over_cores.7
  65.1 0.1 collective-permute-start.22
  65.2 1.6 %collective-permute-start.16 = (bf16[32,1792]{1,0:T(8,128)(2,1)S(1)}, bf16[32,1792]{1,0:T(8,128)(2,1)S(1)}, u32[]{:S(2)}, u32[]{:S(2)}) collective-permute-start(bf16[32,1792]{1,0:T(8,128)(2,1)S(1)} %get-tuple-element.58), channel_id=1, source_target_pairs={{0,2},{1,3},{2,0},{3,1},{4,6},{5,7},{6,4},{7,5},{8,10},{9,11},{10,... | collective-permute-start | bytes 344072 | tf_op jit(solution)/shard_map/sum_over_x/ppermute | solution.py:52
  66.7 0.0 collective-permute-done.22.received_ref
  66.8 1.3 %collective-permute-start.23 = (bf16[16,1792]{1,0:T(8,128)(2,1)S(1)}, bf16[16,1792]{1,0:T(8,128)(2,1)S(1)}, u32[]{:S(2)}, u32[]{:S(2)}) collective-permute-start(bf16[16,1792]{1,0:T(8,128)(2,1)S(1)} %sum_over_x.8), channel_id=1, source_target_pairs={{0,2},{1,3},{2,0},{3,1},{4,6},{5,7},{6,4},{7,5},{8,10},{9,11},{10,... | collective-permute-start | bytes 172040 | tf_op jit(solution)/shard_map/sum_over_x/ppermute | solution.py:52
  68.1 0.2 collective-permute-start.18
  68.3 2.5 %collective-permute-start.19 = (bf16[16,1792]{1,0:T(8,128)(2,1)S(1)}, bf16[16,1792]{1,0:T(8,128)(2,1)S(1)}, u32[]{:S(2)}, u32[]{:S(2)}) collective-permute-start(bf16[16,1792]{1,0:T(8,128)(2,1)S(1)} %get-tuple-element.61), channel_id=1, source_target_pairs={{0,12},{4,8},{8,4},{12,0},{1,13},{5,9},{9,5},{13,1},{2,14},{6,10},... | collective-permute-start | bytes 172040 | tf_op jit(solution)/shard_map/columns_over_ctx/ppermute | solution.py:52
  70.8 0.3 collective-permute-done.16.refs_3_
  71.2 0.5 collective-permute-start.20
  71.7 1.5 %collective-permute-start.17 = (bf16[32,1792]{1,0:T(8,128)(2,1)S(1)}, bf16[32,1792]{1,0:T(8,128)(2,1)S(1)}, u32[]{:S(2)}, u32[]{:S(2)}) collective-permute-start(bf16[32,1792]{1,0:T(8,128)(2,1)S(1)} %get-tuple-element.59), channel_id=1, source_target_pairs={{0,4},{4,0},{8,12},{12,8},{1,5},{5,1},{9,13},{13,9},{2,6},{6,2},{1... | collective-permute-start | bytes 344072 | tf_op jit(solution)/shard_map/columns_over_ctx/ppermute | solution.py:52
  73.2 0.0 collective-permute-done.23.refs_3_
  73.2 2.5 %collective-permute-start.24 = (bf16[16,1792]{1,0:T(8,128)(2,1)S(1)}, bf16[16,1792]{1,0:T(8,128)(2,1)S(1)}, u32[]{:S(2)}, u32[]{:S(2)}) collective-permute-start(bf16[16,1792]{1,0:T(8,128)(2,1)S(1)} %sum_over_x.9), channel_id=1, source_target_pairs={{0,12},{4,8},{8,4},{12,0},{1,13},{5,9},{9,5},{13,1},{2,14},{6,10},... | collective-permute-start | bytes 172040 | tf_op jit(solution)/shard_map/columns_over_ctx/ppermute | solution.py:52
  75.7 0.9 %collective-permute-done.18.refs_0_ = bf16[16,1792]{1,0:T(8,128)(2,1)S(1)} collective-permute-done((bf16[16,1792]{1,0:T(8,128)(2,1)S(1)}, bf16[16,1792]{1,0:T(8,128)(2,1)S(1)}, u32[]{:S(2)}, u32[]{:S(2)}) %collective-permute-start.18) | collective-permute-done | bytes 57376 | tf_op jit(solution)/shard_map/columns_over_ctx/ppermute | solution.py:52
  76.6 0.0 collective-permute-done.19.refs_1_.refs_4_
  76.6 3.8 %collective-permute-done.20.refs_3_ = bf16[16,1792]{1,0:T(8,128)(2,1)S(1)} collective-permute-done((bf16[16,1792]{1,0:T(8,128)(2,1)S(1)}, bf16[16,1792]{1,0:T(8,128)(2,1)S(1)}, u32[]{:S(2)}, u32[]{:S(2)}) %collective-permute-start.20) | collective-permute-done | bytes 57376 | tf_op jit(solution)/shard_map/columns_over_ctx/ppermute | solution.py:52
  80.4 0.0 collective-permute-done.24.refs_5_
  80.4 0.8 %output.1 = bf16[32,7168]{1,0:T(8,128)(2,1)} custom-call(bf16[32,1792]{1,0:T(8,128)(2,1)S(1)} %sum_over_x.5.refs_0_, bf16[32,1792]{1,0:T(8,128)(2,1)S(1)} %collective-permute-done.17.refs_1_, bf16[16,1792]{1,0:T(8,128)(2,1)S(1)} %shard_map.64.refs_2_, bf16[16,1792]{1,0:T(8,128)(2,1)S(1)} %collective-permute-done.20.refs_3_, ...), custom_call_target="tpu_custom_call" | custom-call | flops 1024 | bytes 1024 | tf_op jit(solution)/shard_map/output/pallas_call | solution.py:362
  (26 shorter events, 0.2 us)
Async XLA Ops:
  1.0 14.8 %collective-permute-start = (bf16[576,128]{1,0:T(8,128)(2,1)S(1)}, bf16[576,128]{1,0:T(8,128)(2,1)S(1)}, u32[]{:S(2)}, u32[]{:S(2)}) collective-permute-start(bf16[576,128]{1,0:T(8,128)(2,1)S(1)} %slice_select_fusion), channel_id=1, source_target_pairs={{0,4},{4,0},{8,12},{12,8},{1,5},{5,1},{9,13},{13,9},{2,6},{6,2},{1... | collective-permute-start | bytes 442376 | tf_op jit(solution)/shard_map/keys_over_ctx/ppermute | solution.py:52
  4.1 14.0 %collective-permute-start.1 = (bf16[576,128]{1,0:T(8,128)(2,1)S(1)}, bf16[576,128]{1,0:T(8,128)(2,1)S(1)}, u32[]{:S(2)}, u32[]{:S(2)}) collective-permute-start(bf16[576,128]{1,0:T(8,128)(2,1)S(1)} %slice_select_fusion), channel_id=1, source_target_pairs={{0,8},{4,12},{8,0},{12,4},{1,9},{5,13},{9,1},{13,5},{2,10},{6,14},... | collective-permute-start | bytes 442376 | tf_op jit(solution)/shard_map/keys_over_ctx/ppermute | solution.py:52
  6.7 11.4 %collective-permute-start.2 = (bf16[576,128]{1,0:T(8,128)(2,1)S(1)}, bf16[576,128]{1,0:T(8,128)(2,1)S(1)}, u32[]{:S(2)}, u32[]{:S(2)}) collective-permute-start(bf16[576,128]{1,0:T(8,128)(2,1)S(1)} %slice_select_fusion), channel_id=1, source_target_pairs={{0,12},{4,8},{8,4},{12,0},{1,13},{5,9},{9,5},{13,1},{2,14},{6,10},... | collective-permute-start | bytes 442376 | tf_op jit(solution)/shard_map/keys_over_ctx/ppermute | solution.py:52
  7.3 1.0 %copy-start = (bf16[256,576]{0,1:T(8,128)(2,1)S(1)}, bf16[256,576]{0,1:T(8,128)(2,1)}, u32[]{:S(2)}) copy-start(bf16[256,576]{0,1:T(8,128)(2,1)} %param.7) | copy-start | bytes 884740
  8.3 1.1 %copy-start.1 = (bf16[128,3072]{1,0:T(8,128)(2,1)S(1)}, bf16[128,3072]{1,0:T(8,128)(2,1)}, u32[]{:S(2)}) copy-start(bf16[128,3072]{1,0:T(8,128)(2,1)} %q_hbm.1) | copy-start | bytes 2359300
  9.4 0.7 copy-start.2
  10.1 20.1 %slice-start = ((s8[7340032]{0:T(1024)(128)(4,1)}), s8[3145728]{0:T(1024)(128)(4,1)S(1)}, s32[]{:S(2)}) async-start(s8[7340032]{0:T(1024)(128)(4,1)} %bitcast.1), calls=%async_computation | async-start | bytes 6291456
  15.8 2.8 %collective-permute-start.3 = (bf16[576,128]{1,0:T(8,128)(2,1)S(1)}, bf16[576,128]{1,0:T(8,128)(2,1)S(1)}, u32[]{:S(2)}, u32[]{:S(2)}) collective-permute-start(bf16[576,128]{1,0:T(8,128)(2,1)S(1)} %keys_over_cores.3.refs_1_), channel_id=1, source_target_pairs={{0,1},{1,0},{2,3},{3,2},{4,5},{5,4},{6,7},{7,6},{8,9},{9,8},{10,11... | collective-permute-start | bytes 442376 | tf_op jit(solution)/shard_map/keys_over_cores/ppermute | solution.py:52
  18.1 1.4 %collective-permute-start.4 = (bf16[576,128]{1,0:T(8,128)(2,1)S(1)}, bf16[576,128]{1,0:T(8,128)(2,1)S(1)}, u32[]{:S(2)}, u32[]{:S(2)}) collective-permute-start(bf16[576,128]{1,0:T(8,128)(2,1)S(1)} %keys_over_cores.4.refs_2_), channel_id=1, source_target_pairs={{0,1},{1,0},{2,3},{3,2},{4,5},{5,4},{6,7},{7,6},{8,9},{9,8},{10,11... | collective-permute-start | bytes 442376 | tf_op jit(solution)/shard_map/keys_over_cores/ppermute | solution.py:52
  18.1 1.6 %collective-permute-start.5 = (bf16[576,128]{1,0:T(8,128)(2,1)S(1)}, bf16[576,128]{1,0:T(8,128)(2,1)S(1)}, u32[]{:S(2)}, u32[]{:S(2)}) collective-permute-start(bf16[576,128]{1,0:T(8,128)(2,1)S(1)} %keys_over_cores.5.refs_3_), channel_id=1, source_target_pairs={{0,1},{1,0},{2,3},{3,2},{4,5},{5,4},{6,7},{7,6},{8,9},{9,8},{10,11... | collective-permute-start | bytes 442376 | tf_op jit(solution)/shard_map/keys_over_cores/ppermute | solution.py:52
  19.7 10.5 %slice-start.1 = ((s8[7340032]{0:T(1024)(128)(4,1)}), s8[4194304]{0:T(1024)(128)(4,1)S(1)}, s32[]{:S(2)}) async-start(s8[7340032]{0:T(1024)(128)(4,1)} %bitcast.1), calls=%async_computation.1 | async-start | bytes 8388608
  23.4 16.1 %collective-permute-start.9 = (bf16[64,2048]{1,0:T(8,128)(2,1)S(1)}, bf16[64,2048]{1,0:T(8,128)(2,1)S(1)}, u32[]{:S(2)}, u32[]{:S(2)}) collective-permute-start(bf16[64,2048]{1,0:T(8,128)(2,1)S(1)} %get-tuple-element.40.refs_0_), channel_id=1, source_target_pairs={{0,8},{4,12},{8,0},{12,4},{1,9},{5,13},{9,1},{13,5},{2,10},{6,14},... | collective-permute-start | bytes 786440 | tf_op jit(solution)/shard_map/attended_over_ctx/ppermute | solution.py:52
  26.5 15.0 %collective-permute-start.8 = (bf16[64,2048]{1,0:T(8,128)(2,1)S(1)}, bf16[64,2048]{1,0:T(8,128)(2,1)S(1)}, u32[]{:S(2)}, u32[]{:S(2)}) collective-permute-start(bf16[64,2048]{1,0:T(8,128)(2,1)S(1)} %get-tuple-element.40.refs_0_), channel_id=1, source_target_pairs={{0,4},{4,0},{8,12},{12,8},{1,5},{5,1},{9,13},{13,9},{2,6},{6,2},{1... | collective-permute-start | bytes 786440 | tf_op jit(solution)/shard_map/attended_over_ctx/ppermute | solution.py:52
  31.4 2.1 %collective-permute-start.6 = (bf16[2,32,1792]{2,1,0:T(8,128)(2,1)S(1)}, bf16[2,32,1792]{2,1,0:T(8,128)(2,1)S(1)}, u32[]{:S(2)}, u32[]{:S(2)}) collective-permute-start(bf16[2,32,1792]{2,1,0:T(8,128)(2,1)S(1)} %get-tuple-element.47), channel_id=1, source_target_pairs={{0,1},{1,0},{2,3},{3,2},{4,5},{5,4},{6,7},{7,6},{8,9},{9,8},{10,11... | collective-permute-start | bytes 688136 | tf_op jit(solution)/shard_map/sum_over_cores/ppermute | solution.py:52
  31.4 23.4 %collective-permute-start.14 = (bf16[64,2048]{1,0:T(8,128)(2,1)S(1)}, bf16[64,2048]{1,0:T(8,128)(2,1)S(1)}, u32[]{:S(2)}, u32[]{:S(2)}) collective-permute-start(bf16[64,2048]{1,0:T(8,128)(2,1)S(1)} %get-tuple-element.45.refs_1_.refs_3_), channel_id=1, source_target_pairs={{0,8},{4,12},{8,0},{12,4},{1,9},{5,13},{9,1},{13,5},{2,10},{6,14},... | collective-permute-start | bytes 786440 | tf_op jit(solution)/shard_map/attended_over_ctx/ppermute | solution.py:52
  33.5 8.0 %collective-permute-start.7 = (bf16[32,1792]{1,0:T(8,128)(2,1)S(1)}, bf16[32,1792]{1,0:T(8,128)(2,1)S(1)}, u32[]{:S(2)}, u32[]{:S(2)}) collective-permute-start(bf16[32,1792]{1,0:T(8,128)(2,1)S(1)} %get-tuple-element.49), channel_id=1, source_target_pairs={{0,2},{1,3},{2,0},{3,1},{4,6},{5,7},{6,4},{7,5},{8,10},{9,11},{10,... | collective-permute-start | bytes 344072 | tf_op jit(solution)/shard_map/sum_over_x/ppermute | solution.py:52
  39.5 13.7 %collective-permute-start.10 = (bf16[64,2048]{1,0:T(8,128)(2,1)S(1)}, bf16[64,2048]{1,0:T(8,128)(2,1)S(1)}, u32[]{:S(2)}, u32[]{:S(2)}) collective-permute-start(bf16[64,2048]{1,0:T(8,128)(2,1)S(1)} %attended_over_ctx.6.refs_1_), channel_id=1, source_target_pairs={{0,4},{4,0},{8,12},{12,8},{1,5},{5,1},{9,13},{13,9},{2,6},{6,2},{1... | collective-permute-start | bytes 786440 | tf_op jit(solution)/shard_map/attended_over_ctx/ppermute | solution.py:52
  39.5 18.7 %collective-permute-start.13 = (bf16[64,2048]{1,0:T(8,128)(2,1)S(1)}, bf16[64,2048]{1,0:T(8,128)(2,1)S(1)}, u32[]{:S(2)}, u32[]{:S(2)}) collective-permute-start(bf16[64,2048]{1,0:T(8,128)(2,1)S(1)} %attended_over_ctx.7), channel_id=1, source_target_pairs={{0,4},{4,0},{8,12},{12,8},{1,5},{5,1},{9,13},{13,9},{2,6},{6,2},{1... | collective-permute-start | bytes 786440 | tf_op jit(solution)/shard_map/attended_over_ctx/ppermute | solution.py:52
  54.8 1.7 %collective-permute-start.11 = (bf16[2,48,1792]{2,1,0:T(8,128)(2,1)S(1)}, bf16[2,48,1792]{2,1,0:T(8,128)(2,1)S(1)}, u32[]{:S(2)}, u32[]{:S(2)}) collective-permute-start(bf16[2,48,1792]{2,1,0:T(8,128)(2,1)S(1)} %get-tuple-element.51), channel_id=1, source_target_pairs={{0,1},{1,0},{2,3},{3,2},{4,5},{5,4},{6,7},{7,6},{8,9},{9,8},{10,11... | collective-permute-start | bytes 1032200 | tf_op jit(solution)/shard_map/sum_over_cores/ppermute | solution.py:52
  54.9 8.7 %collective-permute-start.21 = (bf16[64,2048]{1,0:T(8,128)(2,1)S(1)}, bf16[64,2048]{1,0:T(8,128)(2,1)S(1)}, u32[]{:S(2)}, u32[]{:S(2)}) collective-permute-start(bf16[64,2048]{1,0:T(8,128)(2,1)S(1)} %attended_over_ctx.9.refs_1_), channel_id=1, source_target_pairs={{0,4},{4,0},{8,12},{12,8},{1,5},{5,1},{9,13},{13,9},{2,6},{6,2},{1... | collective-permute-start | bytes 786440 | tf_op jit(solution)/shard_map/attended_over_ctx/ppermute | solution.py:52
  56.6 7.0 %collective-permute-start.12 = (bf16[48,1792]{1,0:T(8,128)(2,1)S(1)}, bf16[48,1792]{1,0:T(8,128)(2,1)S(1)}, u32[]{:S(2)}, u32[]{:S(2)}) collective-permute-start(bf16[48,1792]{1,0:T(8,128)(2,1)S(1)} %get-tuple-element.53), channel_id=1, source_target_pairs={{0,2},{1,3},{2,0},{3,1},{4,6},{5,7},{6,4},{7,5},{8,10},{9,11},{10,... | collective-permute-start | bytes 516104 | tf_op jit(solution)/shard_map/sum_over_x/ppermute | solution.py:52
  59.3 5.7 %collective-permute-start.15 = (bf16[2,32,1792]{2,1,0:T(8,128)(2,1)S(1)}, bf16[2,32,1792]{2,1,0:T(8,128)(2,1)S(1)}, u32[]{:S(2)}, u32[]{:S(2)}) collective-permute-start(bf16[2,32,1792]{2,1,0:T(8,128)(2,1)S(1)} %get-tuple-element.56), channel_id=1, source_target_pairs={{0,1},{1,0},{2,3},{3,2},{4,5},{5,4},{6,7},{7,6},{8,9},{9,8},{10,11... | collective-permute-start | bytes 688136 | tf_op jit(solution)/shard_map/sum_over_cores/ppermute | solution.py:52
  65.1 1.7 %collective-permute-start.22 = (bf16[2,16,1792]{2,1,0:T(8,128)(2,1)S(1)}, bf16[2,16,1792]{2,1,0:T(8,128)(2,1)S(1)}, u32[]{:S(2)}, u32[]{:S(2)}) collective-permute-start(bf16[2,16,1792]{2,1,0:T(8,128)(2,1)S(1)} %sum_over_cores.8), channel_id=1, source_target_pairs={{0,1},{1,0},{2,3},{3,2},{4,5},{5,4},{6,7},{7,6},{8,9},{9,8},{10,11... | collective-permute-start | bytes 344072 | tf_op jit(solution)/shard_map/sum_over_cores/ppermute | solution.py:52
  65.2 6.0 %collective-permute-start.16 = (bf16[32,1792]{1,0:T(8,128)(2,1)S(1)}, bf16[32,1792]{1,0:T(8,128)(2,1)S(1)}, u32[]{:S(2)}, u32[]{:S(2)}) collective-permute-start(bf16[32,1792]{1,0:T(8,128)(2,1)S(1)} %get-tuple-element.58), channel_id=1, source_target_pairs={{0,2},{1,3},{2,0},{3,1},{4,6},{5,7},{6,4},{7,5},{8,10},{9,11},{10,... | collective-permute-start | bytes 344072 | tf_op jit(solution)/shard_map/sum_over_x/ppermute | solution.py:52
  66.8 6.4 %collective-permute-start.23 = (bf16[16,1792]{1,0:T(8,128)(2,1)S(1)}, bf16[16,1792]{1,0:T(8,128)(2,1)S(1)}, u32[]{:S(2)}, u32[]{:S(2)}) collective-permute-start(bf16[16,1792]{1,0:T(8,128)(2,1)S(1)} %sum_over_x.8), channel_id=1, source_target_pairs={{0,2},{1,3},{2,0},{3,1},{4,6},{5,7},{6,4},{7,5},{8,10},{9,11},{10,... | collective-permute-start | bytes 172040 | tf_op jit(solution)/shard_map/sum_over_x/ppermute | solution.py:52
  68.1 8.5 %collective-permute-start.18 = (bf16[16,1792]{1,0:T(8,128)(2,1)S(1)}, bf16[16,1792]{1,0:T(8,128)(2,1)S(1)}, u32[]{:S(2)}, u32[]{:S(2)}) collective-permute-start(bf16[16,1792]{1,0:T(8,128)(2,1)S(1)} %get-tuple-element.60), channel_id=1, source_target_pairs={{0,8},{4,12},{8,0},{12,4},{1,9},{5,13},{9,1},{13,5},{2,10},{6,14},... | collective-permute-start | bytes 172040 | tf_op jit(solution)/shard_map/columns_over_ctx/ppermute | solution.py:52
  68.3 8.3 %collective-permute-start.19 = (bf16[16,1792]{1,0:T(8,128)(2,1)S(1)}, bf16[16,1792]{1,0:T(8,128)(2,1)S(1)}, u32[]{:S(2)}, u32[]{:S(2)}) collective-permute-start(bf16[16,1792]{1,0:T(8,128)(2,1)S(1)} %get-tuple-element.61), channel_id=1, source_target_pairs={{0,12},{4,8},{8,4},{12,0},{1,13},{5,9},{9,5},{13,1},{2,14},{6,10},... | collective-permute-start | bytes 172040 | tf_op jit(solution)/shard_map/columns_over_ctx/ppermute | solution.py:52
  71.2 9.2 %collective-permute-start.20 = (bf16[16,1792]{1,0:T(8,128)(2,1)S(1)}, bf16[16,1792]{1,0:T(8,128)(2,1)S(1)}, u32[]{:S(2)}, u32[]{:S(2)}) collective-permute-start(bf16[16,1792]{1,0:T(8,128)(2,1)S(1)} %get-tuple-element.62), channel_id=1, source_target_pairs={{0,8},{4,12},{8,0},{12,4},{1,9},{5,13},{9,1},{13,5},{2,10},{6,14},... | collective-permute-start | bytes 172040 | tf_op jit(solution)/shard_map/columns_over_ctx/ppermute | solution.py:52
  71.7 8.8 %collective-permute-start.17 = (bf16[32,1792]{1,0:T(8,128)(2,1)S(1)}, bf16[32,1792]{1,0:T(8,128)(2,1)S(1)}, u32[]{:S(2)}, u32[]{:S(2)}) collective-permute-start(bf16[32,1792]{1,0:T(8,128)(2,1)S(1)} %get-tuple-element.59), channel_id=1, source_target_pairs={{0,4},{4,0},{8,12},{12,8},{1,5},{5,1},{9,13},{13,9},{2,6},{6,2},{1... | collective-permute-start | bytes 344072 | tf_op jit(solution)/shard_map/columns_over_ctx/ppermute | solution.py:52
  73.2 7.2 %collective-permute-start.24 = (bf16[16,1792]{1,0:T(8,128)(2,1)S(1)}, bf16[16,1792]{1,0:T(8,128)(2,1)S(1)}, u32[]{:S(2)}, u32[]{:S(2)}) collective-permute-start(bf16[16,1792]{1,0:T(8,128)(2,1)S(1)} %sum_over_x.9), channel_id=1, source_target_pairs={{0,12},{4,8},{8,4},{12,0},{1,13},{5,9},{9,5},{13,1},{2,14},{6,10},... | collective-permute-start | bytes 172040 | tf_op jit(solution)/shard_map/columns_over_ctx/ppermute | solution.py:52

commit v18 on v16

--- a/solution.py
+++ b/solution.py
@@ -257,16 +257,13 @@
     for index, piece_ref in enumerate(piece_refs):
         rows_ref[index * rows : (index + 1) * rows, :] = piece_ref[...]
     is_first = lax.axis_index("head") % 2 == 0
-    width = 256 if columns % 256 == 0 else columns
-    for start in range(0, columns, width):
-        span = slice(start, start + width)
-        result = jnp.dot(rows_ref[...], weight_ref[:, span], preferred_element_type=jnp.float32)
-        result = result.reshape(count, n_x, 2, rows // (2 * n_x), width)
-        for x in range(n_x):
-            first = result[:, x, 0].reshape(rows * count // (2 * n_x), width)
-            second = result[:, x, 1].reshape(rows * count // (2 * n_x), width)
-            sent_ref[x, :, span] = jnp.where(is_first, second, first).astype(jnp.bfloat16)
-            kept_ref[x, :, span] = jnp.where(is_first, first, second)
+    result = jnp.dot(rows_ref[...], weight_ref[...], preferred_element_type=jnp.float32)
+    result = result.reshape(count, n_x, 2, rows // (2 * n_x), columns)
+    for x in range(n_x):
+        first = result[:, x, 0].reshape(rows * count // (2 * n_x), columns)
+        second = result[:, x, 1].reshape(rows * count // (2 * n_x), columns)
+        sent_ref[x] = jnp.where(is_first, second, first).astype(jnp.bfloat16)
+        kept_ref[x] = jnp.where(is_first, first, second)
 
 
 def product(pieces, w_out, n_x, after):

time: 81.5 us -> 81.5 us (level)
  no operation moved by 1% of the time
where the time goes in v18:
time: 81.5 us; the launch traced here: 81.3 us
  waiting for transfers between devices  33.9 us (42%)
  starting transfers between devices  23.3 us (29%)
  Pallas kernels  19.4 us (24%)
  local copies, waits for them, and re-layouts  2.75 us (3%)
  other arithmetic  1 us (1%)
  between operations  0.91 us (1%)
    ppermute x25, waiting for transfers between devices, exchange(): return lax.ppermute(array, axis, [(i, i ^ bit) for i in range(size)])  33.9 us
    ppermute x25, starting transfers between devices, exchange(): return lax.ppermute(array, axis, [(i, i ^ bit) for i in range(size)])  23.3 us
    pallas_call x2, Pallas kernels, attention(): pl.pallas_call(functools.partial(attention_kernel, 0 if gathered else len...  7.33 us
    pallas_call x1, Pallas kernels, load(): pl.pallas_call(functools.partial(load_kernel, owners, pieces, cache_rows)...  5.66 us
    pallas_call x4, Pallas kernels, product(): pl.pallas_call(functools.partial(product_kernel, count, n_x, len(after)),...  5.28 us
    unnamed x10, local copies, waits for them, and re-layouts  2.75 us
  transfers between devices with their start and end apart: 25, of which 10 were waited for; matrix products, arithmetic and copies ran while one was open for 0% of the time, Pallas kernels for 18%

profile of v18, /device:TPU:0, one launch (start us, length us, event | category | flops | bytes accessed | tf_op | source)
XLA Modules:
  0.0 81.3 jit_solution(1685161251789260681)
XLA Ops:
  0.0 1.0 %slice_select_fusion = bf16[576,128]{1,0:T(8,128)(2,1)S(1)} fusion(bf16[576,256]{1,0:T(8,128)(2,1)} %bitcast.3, pred[]{:T(512)S(6)} %eq.5), kind=kLoop, calls=%fused_computation | loop fusion | flops 73728 | bytes 442369 | tf_op jit(solution)/shard_map/keys_over_ctx/jit(_where)/select_n | solution.py:381
  1.0 3.1 %collective-permute-start = (bf16[576,128]{1,0:T(8,128)(2,1)S(1)}, bf16[576,128]{1,0:T(8,128)(2,1)S(1)}, u32[]{:S(2)}, u32[]{:S(2)}) collective-permute-start(bf16[576,128]{1,0:T(8,128)(2,1)S(1)} %slice_select_fusion), channel_id=1, source_target_pairs={{0,4},{4,0},{8,12},{12,8},{1,5},{5,1},{9,13},{13,9},{2,6},{6,2},{1... | collective-permute-start | bytes 442376 | tf_op jit(solution)/shard_map/keys_over_ctx/ppermute | solution.py:52
  4.1 2.6 %collective-permute-start.1 = (bf16[576,128]{1,0:T(8,128)(2,1)S(1)}, bf16[576,128]{1,0:T(8,128)(2,1)S(1)}, u32[]{:S(2)}, u32[]{:S(2)}) collective-permute-start(bf16[576,128]{1,0:T(8,128)(2,1)S(1)} %slice_select_fusion), channel_id=1, source_target_pairs={{0,8},{4,12},{8,0},{12,4},{1,9},{5,13},{9,1},{13,5},{2,10},{6,14},... | collective-permute-start | bytes 442376 | tf_op jit(solution)/shard_map/keys_over_ctx/ppermute | solution.py:52
  6.7 0.0 collective-permute-start.2
  7.3 0.0 copy-start
  7.3 1.0 %copy-done = bf16[256,576]{0,1:T(8,128)(2,1)S(1)} copy-done((bf16[256,576]{0,1:T(8,128)(2,1)S(1)}, bf16[256,576]{0,1:T(8,128)(2,1)}, u32[]{:S(2)}) %copy-start) | copy-done | bytes 294936
  8.3 1.1 %copy-done.1 = bf16[128,3072]{1,0:T(8,128)(2,1)S(1)} copy-done((bf16[128,3072]{1,0:T(8,128)(2,1)S(1)}, bf16[128,3072]{1,0:T(8,128)(2,1)}, u32[]{:S(2)}) %copy-start.1) | copy-done | bytes 786456
  9.4 0.7 copy-done.2
  10.1 5.7 %load.1 = (bf16[16,64,576]{2,1,0:T(8,128)(2,1)S(1)}, bf16[16,64,576]{2,1,0:T(8,128)(2,1)S(1)}, f32[64,1024]{1,0:T(8,128)S(1)}, f32[64,1024]{1,0:T(8,128)S(1)}, b...) custom-call(s32[4]{0:T(128)S(1)} %copy-done.2, s32[1]{0:T(128)S(6)} %copy.33.prefix_ref, ...), custom_call_target="tpu_custom_call" | custom-call | flops 1024 | bytes 1024 | tf_op jit(solution)/shard_map/load/pallas_call | solution.py:143
  15.8 0.0 collective-permute-done.refs_0_
  15.8 0.1 collective-permute-start.3
  15.9 2.2 %collective-permute-done.1.refs_0_ = bf16[576,128]{1,0:T(8,128)(2,1)S(1)} collective-permute-done((bf16[576,128]{1,0:T(8,128)(2,1)S(1)}, bf16[576,128]{1,0:T(8,128)(2,1)S(1)}, u32[]{:S(2)}, u32[]{:S(2)}) %collective-permute-start.1) | collective-permute-done | bytes 147488 | tf_op jit(solution)/shard_map/keys_over_ctx/ppermute | solution.py:52
  18.1 0.0 collective-permute-start.4
  18.1 0.0 collective-permute-done.2.refs_0_
  18.1 0.5 collective-permute-start.5
  18.6 0.0 collective-permute-done.3.refs_4_
  18.6 0.9 %collective-permute-done.4.refs_5_ = bf16[576,128]{1,0:T(8,128)(2,1)S(1)} collective-permute-done((bf16[576,128]{1,0:T(8,128)(2,1)S(1)}, bf16[576,128]{1,0:T(8,128)(2,1)S(1)}, u32[]{:S(2)}, u32[]{:S(2)}) %collective-permute-start.4) | collective-permute-done | bytes 147488 | tf_op jit(solution)/shard_map/keys_over_cores/ppermute | solution.py:52
  19.5 0.2 collective-permute-done.5.refs_6_
  19.7 3.7 %attention.2 = (bf16[64,2048]{1,0:T(8,128)(2,1)S(1)}, bf16[576,1024]{1,0:T(8,128)(2,1)S(1)}, bf16[1024,512]{1,0:T(8,128)(2,1)S(1)}) custom-call(bf16[16,64,576]{2,1,0:T(8,128)(2,1)S(1)} %get-tuple-element.36.q_ref, f32[64,1024]{1,0:T(8,128)S(1)} %get-tuple-element.37.bias_ref, bf16[16,512,128]{2,1,0:T(8,128)(2,1)S(1)} %get-tuple-element.38.value_ref, ...), custom_call_target="tpu_custom_call" | custom-call | flops 1024 | bytes 1024 | tf_op jit(solution)/shard_map/attention/pallas_call | solution.py:242
  23.4 3.2 %collective-permute-start.9 = (bf16[64,2048]{1,0:T(8,128)(2,1)S(1)}, bf16[64,2048]{1,0:T(8,128)(2,1)S(1)}, u32[]{:S(2)}, u32[]{:S(2)}) collective-permute-start(bf16[64,2048]{1,0:T(8,128)(2,1)S(1)} %get-tuple-element.40.refs_0_), channel_id=1, source_target_pairs={{0,8},{4,12},{8,0},{12,4},{1,9},{5,13},{9,1},{13,5},{2,10},{6,14},... | collective-permute-start | bytes 786440 | tf_op jit(solution)/shard_map/attended_over_ctx/ppermute | solution.py:52
  26.5 0.0 collective-permute-start.8
  26.5 3.7 %attention.3 = (bf16[64,2048]{1,0:T(8,128)(2,1)S(1)}, bf16[64,2048]{1,0:T(8,128)(2,1)S(1)}) custom-call(bf16[16,64,576]{2,1,0:T(8,128)(2,1)S(1)} %get-tuple-element.41.q_ref, f32[64,1024]{1,0:T(8,128)S(1)} %get-tuple-element.42.bias_ref, bf16[16,512,128]{2,1,0:T(8,128)(2,1)S(1)} %get-tuple-element.38.value_ref, ...), custom_call_target="tpu_custom_call" | custom-call | flops 1024 | bytes 1024 | tf_op jit(solution)/shard_map/attention/pallas_call | solution.py:242
  30.2 1.1 %out_product.5 = (bf16[2,32,1792]{2,1,0:T(8,128)(2,1)S(1)}, f32[2,32,1792]{2,1,0:T(8,128)S(1)}) custom-call(bf16[2048,1792]{1,0:T(8,128)(2,1)S(1)} %bitcast.2, bf16[64,2048]{1,0:T(8,128)(2,1)S(1)} %get-tuple-element.40.refs_0_, bf16[64,2048]{1,0:T(8,128)(2,1)S(1)} %get-tuple-element.45.refs_1_.refs_3_), custom_call_target="tpu_custom_call" | custom-call | flops 1024 | bytes 1024 | tf_op jit(solution)/shard_map/out_product/pallas_call | solution.py:273
  31.4 0.1 collective-permute-start.6
  31.4 2.0 %collective-permute-start.14 = (bf16[64,2048]{1,0:T(8,128)(2,1)S(1)}, bf16[64,2048]{1,0:T(8,128)(2,1)S(1)}, u32[]{:S(2)}, u32[]{:S(2)}) collective-permute-start(bf16[64,2048]{1,0:T(8,128)(2,1)S(1)} %get-tuple-element.45.refs_1_.refs_3_), channel_id=1, source_target_pairs={{0,8},{4,12},{8,0},{12,4},{1,9},{5,13},{9,1},{13,5},{2,10},{6,14},... | collective-permute-start | bytes 786440 | tf_op jit(solution)/shard_map/attended_over_ctx/ppermute | solution.py:52
  33.4 0.0 collective-permute-done.6.received_ref
  33.5 1.6 %collective-permute-start.7 = (bf16[32,1792]{1,0:T(8,128)(2,1)S(1)}, bf16[32,1792]{1,0:T(8,128)(2,1)S(1)}, u32[]{:S(2)}, u32[]{:S(2)}) collective-permute-start(bf16[32,1792]{1,0:T(8,128)(2,1)S(1)} %get-tuple-element.49), channel_id=1, source_target_pairs={{0,2},{1,3},{2,0},{3,1},{4,6},{5,7},{6,4},{7,5},{8,10},{9,11},{10,... | collective-permute-start | bytes 344072 | tf_op jit(solution)/shard_map/sum_over_x/ppermute | solution.py:52
  35.0 4.5 %collective-permute-done.9.refs_0_ = bf16[64,2048]{1,0:T(8,128)(2,1)S(1)} collective-permute-done((bf16[64,2048]{1,0:T(8,128)(2,1)S(1)}, bf16[64,2048]{1,0:T(8,128)(2,1)S(1)}, u32[]{:S(2)}, u32[]{:S(2)}) %collective-permute-start.9) | collective-permute-done | bytes 262176 | tf_op jit(solution)/shard_map/attended_over_ctx/ppermute | solution.py:52
  39.5 0.0 collective-permute-start.10
  39.5 2.0 %collective-permute-start.13 = (bf16[64,2048]{1,0:T(8,128)(2,1)S(1)}, bf16[64,2048]{1,0:T(8,128)(2,1)S(1)}, u32[]{:S(2)}, u32[]{:S(2)}) collective-permute-start(bf16[64,2048]{1,0:T(8,128)(2,1)S(1)} %attended_over_ctx.7), channel_id=1, source_target_pairs={{0,4},{4,0},{8,12},{12,8},{1,5},{5,1},{9,13},{13,9},{2,6},{6,2},{1... | collective-permute-start | bytes 786440 | tf_op jit(solution)/shard_map/attended_over_ctx/ppermute | solution.py:52
  41.5 0.0 collective-permute-done.8.refs_0_
  41.5 0.0 collective-permute-done.7.refs_1_.refs_4_
  41.5 11.7 %collective-permute-done.10.refs_2_.refs_1_ = bf16[64,2048]{1,0:T(8,128)(2,1)S(1)} collective-permute-done((bf16[64,2048]{1,0:T(8,128)(2,1)S(1)}, bf16[64,2048]{1,0:T(8,128)(2,1)S(1)}, u32[]{:S(2)}, u32[]{:S(2)}) %collective-permute-start.10) | collective-permute-done | bytes 262176 | tf_op jit(solution)/shard_map/attended_over_ctx/ppermute | solution.py:52
  53.2 1.6 %out_product.6 = (bf16[2,48,1792]{2,1,0:T(8,128)(2,1)S(1)}, f32[2,48,1792]{2,1,0:T(8,128)S(1)}) custom-call(bf16[2048,1792]{1,0:T(8,128)(2,1)S(1)} %bitcast.2, bf16[64,2048]{1,0:T(8,128)(2,1)S(1)} %attended_over_ctx.5.refs_0_, bf16[64,2048]{1,0:T(8,128)(2,1)S(1)} %attended_over_ctx.6.refs_1_, bf16[64,2048]{1,0:T(8,128)(2,1)S(1)} %collective-permute-done.10.refs_2_.refs_1_, ...), custom_call_target="tpu_custom_call" | custom-call | flops 1024 | bytes 1024 | tf_op jit(solution)/shard_map/out_product/pallas_call | solution.py:273
  54.8 0.1 collective-permute-start.11
  54.9 0.0 collective-permute-done.14.refs_0_
  54.9 0.1 collective-permute-start.21
  55.0 1.5 %collective-permute-done.11.received_ref = bf16[2,48,1792]{2,1,0:T(8,128)(2,1)S(1)} collective-permute-done((bf16[2,48,1792]{2,1,0:T(8,128)(2,1)S(1)}, bf16[2,48,1792]{2,1,0:T(8,128)(2,1)S(1)}, u32[]{:S(2)}, u32[]{:S(2)}) %collective-permute-start.11) | collective-permute-done | bytes 344096 | tf_op jit(solution)/shard_map/sum_over_cores/ppermute | solution.py:52
  56.5 0.1 sum_over_cores.6
  56.6 1.6 %collective-permute-start.12 = (bf16[48,1792]{1,0:T(8,128)(2,1)S(1)}, bf16[48,1792]{1,0:T(8,128)(2,1)S(1)}, u32[]{:S(2)}, u32[]{:S(2)}) collective-permute-start(bf16[48,1792]{1,0:T(8,128)(2,1)S(1)} %get-tuple-element.53), channel_id=1, source_target_pairs={{0,2},{1,3},{2,0},{3,1},{4,6},{5,7},{6,4},{7,5},{8,10},{9,11},{10,... | collective-permute-start | bytes 516104 | tf_op jit(solution)/shard_map/sum_over_x/ppermute | solution.py:52
  58.2 0.0 collective-permute-done.13.refs_0_
  58.2 1.1 %out_product.7 = (bf16[2,32,1792]{2,1,0:T(8,128)(2,1)S(1)}, f32[2,32,1792]{2,1,0:T(8,128)S(1)}) custom-call(bf16[2048,1792]{1,0:T(8,128)(2,1)S(1)} %bitcast.2, bf16[64,2048]{1,0:T(8,128)(2,1)S(1)} %attended_over_ctx.8.refs_0_, bf16[64,2048]{1,0:T(8,128)(2,1)S(1)} %attended_over_ctx.9.refs_1_, f32[48,1792]{1,0:T(8,128)S(1)} %get-tuple-element.52.refs_2_.refs_0_), custom_call_target="tpu_custom_call" | custom-call | flops 1024 | bytes 1024 | tf_op jit(solution)/shard_map/out_product/pallas_call | solution.py:273
  59.3 0.1 collective-permute-start.15
  59.4 4.2 %collective-permute-done.21.refs_0_ = bf16[64,2048]{1,0:T(8,128)(2,1)S(1)} collective-permute-done((bf16[64,2048]{1,0:T(8,128)(2,1)S(1)}, bf16[64,2048]{1,0:T(8,128)(2,1)S(1)}, u32[]{:S(2)}, u32[]{:S(2)}) %collective-permute-start.21) | collective-permute-done | bytes 262176 | tf_op jit(solution)/shard_map/attended_over_ctx/ppermute | solution.py:52
  63.6 0.0 collective-permute-done.12.refs_1_
  63.6 1.4 %out_product.9 = (bf16[2,16,1792]{2,1,0:T(8,128)(2,1)S(1)}, f32[2,16,1792]{2,1,0:T(8,128)S(1)}) custom-call(bf16[2048,1792]{1,0:T(8,128)(2,1)S(1)} %bitcast.2, bf16[64,2048]{1,0:T(8,128)(2,1)S(1)} %out_product.8.refs_0_), custom_call_target="tpu_custom_call" | custom-call | flops 1024 | bytes 1024 | tf_op jit(solution)/shard_map/out_product/pallas_call | solution.py:273
  65.0 0.0 collective-permute-done.15.received_ref
  65.0 0.1 sum_over_cores.7
  65.1 0.1 collective-permute-start.22
  65.2 1.6 %collective-permute-start.16 = (bf16[32,1792]{1,0:T(8,128)(2,1)S(1)}, bf16[32,1792]{1,0:T(8,128)(2,1)S(1)}, u32[]{:S(2)}, u32[]{:S(2)}) collective-permute-start(bf16[32,1792]{1,0:T(8,128)(2,1)S(1)} %get-tuple-element.58), channel_id=1, source_target_pairs={{0,2},{1,3},{2,0},{3,1},{4,6},{5,7},{6,4},{7,5},{8,10},{9,11},{10,... | collective-permute-start | bytes 344072 | tf_op jit(solution)/shard_map/sum_over_x/ppermute | solution.py:52
  66.8 0.2 collective-permute-start.18
  67.0 2.5 %collective-permute-start.20 = (bf16[16,1792]{1,0:T(8,128)(2,1)S(1)}, bf16[16,1792]{1,0:T(8,128)(2,1)S(1)}, u32[]{:S(2)}, u32[]{:S(2)}) collective-permute-start(bf16[16,1792]{1,0:T(8,128)(2,1)S(1)} %get-tuple-element.62), channel_id=1, source_target_pairs={{0,12},{4,8},{8,4},{12,0},{1,13},{5,9},{9,5},{13,1},{2,14},{6,10},... | collective-permute-start | bytes 172040 | tf_op jit(solution)/shard_map/columns_over_ctx/ppermute | solution.py:52
  69.5 0.0 collective-permute-done.22.received_ref
  69.5 0.6 collective-permute-start.23
  70.1 0.6 collective-permute-done.16.refs_3_
  70.8 0.3 collective-permute-start.17
  71.1 3.0 %collective-permute-done.18.refs_0_ = bf16[16,1792]{1,0:T(8,128)(2,1)S(1)} collective-permute-done((bf16[16,1792]{1,0:T(8,128)(2,1)S(1)}, bf16[16,1792]{1,0:T(8,128)(2,1)S(1)}, u32[]{:S(2)}, u32[]{:S(2)}) %collective-permute-start.18) | collective-permute-done | bytes 57376 | tf_op jit(solution)/shard_map/columns_over_ctx/ppermute | solution.py:52
  74.1 0.0 collective-permute-done.23.refs_3_
  74.1 1.2 %collective-permute-start.24 = (bf16[16,1792]{1,0:T(8,128)(2,1)S(1)}, bf16[16,1792]{1,0:T(8,128)(2,1)S(1)}, u32[]{:S(2)}, u32[]{:S(2)}) collective-permute-start(bf16[16,1792]{1,0:T(8,128)(2,1)S(1)} %sum_over_x.9), channel_id=1, source_target_pairs={{0,12},{4,8},{8,4},{12,0},{1,13},{5,9},{9,5},{13,1},{2,14},{6,10},... | collective-permute-start | bytes 172040 | tf_op jit(solution)/shard_map/columns_over_ctx/ppermute | solution.py:52
  75.3 0.0 collective-permute-done.20.refs_0_
  75.3 5.1 %collective-permute-done.19.refs_3_ = bf16[16,1792]{1,0:T(8,128)(2,1)S(1)} collective-permute-done((bf16[16,1792]{1,0:T(8,128)(2,1)S(1)}, bf16[16,1792]{1,0:T(8,128)(2,1)S(1)}, u32[]{:S(2)}, u32[]{:S(2)}) %collective-permute-start.19) | collective-permute-done | bytes 57376 | tf_op jit(solution)/shard_map/columns_over_ctx/ppermute | solution.py:52
  80.4 0.0 collective-permute-done.24.refs_5_
  80.4 0.0 collective-permute-done.17.refs_1_
  80.4 0.8 %output.1 = bf16[32,7168]{1,0:T(8,128)(2,1)} custom-call(bf16[32,1792]{1,0:T(8,128)(2,1)S(1)} %sum_over_x.5.refs_0_, bf16[32,1792]{1,0:T(8,128)(2,1)S(1)} %collective-permute-done.17.refs_1_, bf16[16,1792]{1,0:T(8,128)(2,1)S(1)} %shard_map.64.refs_2_, bf16[16,1792]{1,0:T(8,128)(2,1)S(1)} %collective-permute-done.19.refs_3_, ...), custom_call_target="tpu_custom_call" | custom-call | flops 1024 | bytes 1024 | tf_op jit(solution)/shard_map/output/pallas_call | solution.py:359
  (27 shorter events, 0.2 us)
Async XLA Ops:
  1.0 14.8 %collective-permute-start = (bf16[576,128]{1,0:T(8,128)(2,1)S(1)}, bf16[576,128]{1,0:T(8,128)(2,1)S(1)}, u32[]{:S(2)}, u32[]{:S(2)}) collective-permute-start(bf16[576,128]{1,0:T(8,128)(2,1)S(1)} %slice_select_fusion), channel_id=1, source_target_pairs={{0,4},{4,0},{8,12},{12,8},{1,5},{5,1},{9,13},{13,9},{2,6},{6,2},{1... | collective-permute-start | bytes 442376 | tf_op jit(solution)/shard_map/keys_over_ctx/ppermute | solution.py:52
  4.1 14.0 %collective-permute-start.1 = (bf16[576,128]{1,0:T(8,128)(2,1)S(1)}, bf16[576,128]{1,0:T(8,128)(2,1)S(1)}, u32[]{:S(2)}, u32[]{:S(2)}) collective-permute-start(bf16[576,128]{1,0:T(8,128)(2,1)S(1)} %slice_select_fusion), channel_id=1, source_target_pairs={{0,8},{4,12},{8,0},{12,4},{1,9},{5,13},{9,1},{13,5},{2,10},{6,14},... | collective-permute-start | bytes 442376 | tf_op jit(solution)/shard_map/keys_over_ctx/ppermute | solution.py:52
  6.7 11.4 %collective-permute-start.2 = (bf16[576,128]{1,0:T(8,128)(2,1)S(1)}, bf16[576,128]{1,0:T(8,128)(2,1)S(1)}, u32[]{:S(2)}, u32[]{:S(2)}) collective-permute-start(bf16[576,128]{1,0:T(8,128)(2,1)S(1)} %slice_select_fusion), channel_id=1, source_target_pairs={{0,12},{4,8},{8,4},{12,0},{1,13},{5,9},{9,5},{13,1},{2,14},{6,10},... | collective-permute-start | bytes 442376 | tf_op jit(solution)/shard_map/keys_over_ctx/ppermute | solution.py:52
  7.3 1.0 %copy-start = (bf16[256,576]{0,1:T(8,128)(2,1)S(1)}, bf16[256,576]{0,1:T(8,128)(2,1)}, u32[]{:S(2)}) copy-start(bf16[256,576]{0,1:T(8,128)(2,1)} %param.7) | copy-start | bytes 884740
  8.3 1.1 %copy-start.1 = (bf16[128,3072]{1,0:T(8,128)(2,1)S(1)}, bf16[128,3072]{1,0:T(8,128)(2,1)}, u32[]{:S(2)}) copy-start(bf16[128,3072]{1,0:T(8,128)(2,1)} %q_hbm.1) | copy-start | bytes 2359300
  9.4 0.7 copy-start.2
  10.1 20.1 %slice-start = ((s8[7340032]{0:T(1024)(128)(4,1)}), s8[3145728]{0:T(1024)(128)(4,1)S(1)}, s32[]{:S(2)}) async-start(s8[7340032]{0:T(1024)(128)(4,1)} %bitcast.1), calls=%async_computation | async-start | bytes 6291456
  15.8 2.8 %collective-permute-start.3 = (bf16[576,128]{1,0:T(8,128)(2,1)S(1)}, bf16[576,128]{1,0:T(8,128)(2,1)S(1)}, u32[]{:S(2)}, u32[]{:S(2)}) collective-permute-start(bf16[576,128]{1,0:T(8,128)(2,1)S(1)} %keys_over_cores.3.refs_1_), channel_id=1, source_target_pairs={{0,1},{1,0},{2,3},{3,2},{4,5},{5,4},{6,7},{7,6},{8,9},{9,8},{10,11... | collective-permute-start | bytes 442376 | tf_op jit(solution)/shard_map/keys_over_cores/ppermute | solution.py:52
  18.1 1.4 %collective-permute-start.4 = (bf16[576,128]{1,0:T(8,128)(2,1)S(1)}, bf16[576,128]{1,0:T(8,128)(2,1)S(1)}, u32[]{:S(2)}, u32[]{:S(2)}) collective-permute-start(bf16[576,128]{1,0:T(8,128)(2,1)S(1)} %keys_over_cores.4.refs_2_), channel_id=1, source_target_pairs={{0,1},{1,0},{2,3},{3,2},{4,5},{5,4},{6,7},{7,6},{8,9},{9,8},{10,11... | collective-permute-start | bytes 442376 | tf_op jit(solution)/shard_map/keys_over_cores/ppermute | solution.py:52
  18.1 1.6 %collective-permute-start.5 = (bf16[576,128]{1,0:T(8,128)(2,1)S(1)}, bf16[576,128]{1,0:T(8,128)(2,1)S(1)}, u32[]{:S(2)}, u32[]{:S(2)}) collective-permute-start(bf16[576,128]{1,0:T(8,128)(2,1)S(1)} %keys_over_cores.5.refs_3_), channel_id=1, source_target_pairs={{0,1},{1,0},{2,3},{3,2},{4,5},{5,4},{6,7},{7,6},{8,9},{9,8},{10,11... | collective-permute-start | bytes 442376 | tf_op jit(solution)/shard_map/keys_over_cores/ppermute | solution.py:52
  19.7 10.5 %slice-start.1 = ((s8[7340032]{0:T(1024)(128)(4,1)}), s8[4194304]{0:T(1024)(128)(4,1)S(1)}, s32[]{:S(2)}) async-start(s8[7340032]{0:T(1024)(128)(4,1)} %bitcast.1), calls=%async_computation.1 | async-start | bytes 8388608
  23.4 16.1 %collective-permute-start.9 = (bf16[64,2048]{1,0:T(8,128)(2,1)S(1)}, bf16[64,2048]{1,0:T(8,128)(2,1)S(1)}, u32[]{:S(2)}, u32[]{:S(2)}) collective-permute-start(bf16[64,2048]{1,0:T(8,128)(2,1)S(1)} %get-tuple-element.40.refs_0_), channel_id=1, source_target_pairs={{0,8},{4,12},{8,0},{12,4},{1,9},{5,13},{9,1},{13,5},{2,10},{6,14},... | collective-permute-start | bytes 786440 | tf_op jit(solution)/shard_map/attended_over_ctx/ppermute | solution.py:52
  26.5 15.0 %collective-permute-start.8 = (bf16[64,2048]{1,0:T(8,128)(2,1)S(1)}, bf16[64,2048]{1,0:T(8,128)(2,1)S(1)}, u32[]{:S(2)}, u32[]{:S(2)}) collective-permute-start(bf16[64,2048]{1,0:T(8,128)(2,1)S(1)} %get-tuple-element.40.refs_0_), channel_id=1, source_target_pairs={{0,4},{4,0},{8,12},{12,8},{1,5},{5,1},{9,13},{13,9},{2,6},{6,2},{1... | collective-permute-start | bytes 786440 | tf_op jit(solution)/shard_map/attended_over_ctx/ppermute | solution.py:52
  31.4 2.1 %collective-permute-start.6 = (bf16[2,32,1792]{2,1,0:T(8,128)(2,1)S(1)}, bf16[2,32,1792]{2,1,0:T(8,128)(2,1)S(1)}, u32[]{:S(2)}, u32[]{:S(2)}) collective-permute-start(bf16[2,32,1792]{2,1,0:T(8,128)(2,1)S(1)} %get-tuple-element.47), channel_id=1, source_target_pairs={{0,1},{1,0},{2,3},{3,2},{4,5},{5,4},{6,7},{7,6},{8,9},{9,8},{10,11... | collective-permute-start | bytes 688136 | tf_op jit(solution)/shard_map/sum_over_cores/ppermute | solution.py:52
  31.4 23.4 %collective-permute-start.14 = (bf16[64,2048]{1,0:T(8,128)(2,1)S(1)}, bf16[64,2048]{1,0:T(8,128)(2,1)S(1)}, u32[]{:S(2)}, u32[]{:S(2)}) collective-permute-start(bf16[64,2048]{1,0:T(8,128)(2,1)S(1)} %get-tuple-element.45.refs_1_.refs_3_), channel_id=1, source_target_pairs={{0,8},{4,12},{8,0},{12,4},{1,9},{5,13},{9,1},{13,5},{2,10},{6,14},... | collective-permute-start | bytes 786440 | tf_op jit(solution)/shard_map/attended_over_ctx/ppermute | solution.py:52
  33.5 8.0 %collective-permute-start.7 = (bf16[32,1792]{1,0:T(8,128)(2,1)S(1)}, bf16[32,1792]{1,0:T(8,128)(2,1)S(1)}, u32[]{:S(2)}, u32[]{:S(2)}) collective-permute-start(bf16[32,1792]{1,0:T(8,128)(2,1)S(1)} %get-tuple-element.49), channel_id=1, source_target_pairs={{0,2},{1,3},{2,0},{3,1},{4,6},{5,7},{6,4},{7,5},{8,10},{9,11},{10,... | collective-permute-start | bytes 344072 | tf_op jit(solution)/shard_map/sum_over_x/ppermute | solution.py:52
  39.5 13.7 %collective-permute-start.10 = (bf16[64,2048]{1,0:T(8,128)(2,1)S(1)}, bf16[64,2048]{1,0:T(8,128)(2,1)S(1)}, u32[]{:S(2)}, u32[]{:S(2)}) collective-permute-start(bf16[64,2048]{1,0:T(8,128)(2,1)S(1)} %attended_over_ctx.6.refs_1_), channel_id=1, source_target_pairs={{0,4},{4,0},{8,12},{12,8},{1,5},{5,1},{9,13},{13,9},{2,6},{6,2},{1... | collective-permute-start | bytes 786440 | tf_op jit(solution)/shard_map/attended_over_ctx/ppermute | solution.py:52
  39.5 18.7 %collective-permute-start.13 = (bf16[64,2048]{1,0:T(8,128)(2,1)S(1)}, bf16[64,2048]{1,0:T(8,128)(2,1)S(1)}, u32[]{:S(2)}, u32[]{:S(2)}) collective-permute-start(bf16[64,2048]{1,0:T(8,128)(2,1)S(1)} %attended_over_ctx.7), channel_id=1, source_target_pairs={{0,4},{4,0},{8,12},{12,8},{1,5},{5,1},{9,13},{13,9},{2,6},{6,2},{1... | collective-permute-start | bytes 786440 | tf_op jit(solution)/shard_map/attended_over_ctx/ppermute | solution.py:52
  54.8 1.7 %collective-permute-start.11 = (bf16[2,48,1792]{2,1,0:T(8,128)(2,1)S(1)}, bf16[2,48,1792]{2,1,0:T(8,128)(2,1)S(1)}, u32[]{:S(2)}, u32[]{:S(2)}) collective-permute-start(bf16[2,48,1792]{2,1,0:T(8,128)(2,1)S(1)} %get-tuple-element.51), channel_id=1, source_target_pairs={{0,1},{1,0},{2,3},{3,2},{4,5},{5,4},{6,7},{7,6},{8,9},{9,8},{10,11... | collective-permute-start | bytes 1032200 | tf_op jit(solution)/shard_map/sum_over_cores/ppermute | solution.py:52
  54.9 8.7 %collective-permute-start.21 = (bf16[64,2048]{1,0:T(8,128)(2,1)S(1)}, bf16[64,2048]{1,0:T(8,128)(2,1)S(1)}, u32[]{:S(2)}, u32[]{:S(2)}) collective-permute-start(bf16[64,2048]{1,0:T(8,128)(2,1)S(1)} %attended_over_ctx.9.refs_1_), channel_id=1, source_target_pairs={{0,4},{4,0},{8,12},{12,8},{1,5},{5,1},{9,13},{13,9},{2,6},{6,2},{1... | collective-permute-start | bytes 786440 | tf_op jit(solution)/shard_map/attended_over_ctx/ppermute | solution.py:52
  56.6 7.0 %collective-permute-start.12 = (bf16[48,1792]{1,0:T(8,128)(2,1)S(1)}, bf16[48,1792]{1,0:T(8,128)(2,1)S(1)}, u32[]{:S(2)}, u32[]{:S(2)}) collective-permute-start(bf16[48,1792]{1,0:T(8,128)(2,1)S(1)} %get-tuple-element.53), channel_id=1, source_target_pairs={{0,2},{1,3},{2,0},{3,1},{4,6},{5,7},{6,4},{7,5},{8,10},{9,11},{10,... | collective-permute-start | bytes 516104 | tf_op jit(solution)/shard_map/sum_over_x/ppermute | solution.py:52
  59.3 5.7 %collective-permute-start.15 = (bf16[2,32,1792]{2,1,0:T(8,128)(2,1)S(1)}, bf16[2,32,1792]{2,1,0:T(8,128)(2,1)S(1)}, u32[]{:S(2)}, u32[]{:S(2)}) collective-permute-start(bf16[2,32,1792]{2,1,0:T(8,128)(2,1)S(1)} %get-tuple-element.56), channel_id=1, source_target_pairs={{0,1},{1,0},{2,3},{3,2},{4,5},{5,4},{6,7},{7,6},{8,9},{9,8},{10,11... | collective-permute-start | bytes 688136 | tf_op jit(solution)/shard_map/sum_over_cores/ppermute | solution.py:52
  65.1 4.4 %collective-permute-start.22 = (bf16[2,16,1792]{2,1,0:T(8,128)(2,1)S(1)}, bf16[2,16,1792]{2,1,0:T(8,128)(2,1)S(1)}, u32[]{:S(2)}, u32[]{:S(2)}) collective-permute-start(bf16[2,16,1792]{2,1,0:T(8,128)(2,1)S(1)} %sum_over_cores.8), channel_id=1, source_target_pairs={{0,1},{1,0},{2,3},{3,2},{4,5},{5,4},{6,7},{7,6},{8,9},{9,8},{10,11... | collective-permute-start | bytes 344072 | tf_op jit(solution)/shard_map/sum_over_cores/ppermute | solution.py:52
  65.2 5.6 %collective-permute-start.16 = (bf16[32,1792]{1,0:T(8,128)(2,1)S(1)}, bf16[32,1792]{1,0:T(8,128)(2,1)S(1)}, u32[]{:S(2)}, u32[]{:S(2)}) collective-permute-start(bf16[32,1792]{1,0:T(8,128)(2,1)S(1)} %get-tuple-element.58), channel_id=1, source_target_pairs={{0,2},{1,3},{2,0},{3,1},{4,6},{5,7},{6,4},{7,5},{8,10},{9,11},{10,... | collective-permute-start | bytes 344072 | tf_op jit(solution)/shard_map/sum_over_x/ppermute | solution.py:52
  66.8 7.3 %collective-permute-start.18 = (bf16[16,1792]{1,0:T(8,128)(2,1)S(1)}, bf16[16,1792]{1,0:T(8,128)(2,1)S(1)}, u32[]{:S(2)}, u32[]{:S(2)}) collective-permute-start(bf16[16,1792]{1,0:T(8,128)(2,1)S(1)} %get-tuple-element.60), channel_id=1, source_target_pairs={{0,8},{4,12},{8,0},{12,4},{1,9},{5,13},{9,1},{13,5},{2,10},{6,14},... | collective-permute-start | bytes 172040 | tf_op jit(solution)/shard_map/columns_over_ctx/ppermute | solution.py:52
  67.0 8.3 %collective-permute-start.20 = (bf16[16,1792]{1,0:T(8,128)(2,1)S(1)}, bf16[16,1792]{1,0:T(8,128)(2,1)S(1)}, u32[]{:S(2)}, u32[]{:S(2)}) collective-permute-start(bf16[16,1792]{1,0:T(8,128)(2,1)S(1)} %get-tuple-element.62), channel_id=1, source_target_pairs={{0,12},{4,8},{8,4},{12,0},{1,13},{5,9},{9,5},{13,1},{2,14},{6,10},... | collective-permute-start | bytes 172040 | tf_op jit(solution)/shard_map/columns_over_ctx/ppermute | solution.py:52
  69.5 4.6 %collective-permute-start.23 = (bf16[16,1792]{1,0:T(8,128)(2,1)S(1)}, bf16[16,1792]{1,0:T(8,128)(2,1)S(1)}, u32[]{:S(2)}, u32[]{:S(2)}) collective-permute-start(bf16[16,1792]{1,0:T(8,128)(2,1)S(1)} %sum_over_x.8), channel_id=1, source_target_pairs={{0,2},{1,3},{2,0},{3,1},{4,6},{5,7},{6,4},{7,5},{8,10},{9,11},{10,... | collective-permute-start | bytes 172040 | tf_op jit(solution)/shard_map/sum_over_x/ppermute | solution.py:52
  70.8 9.7 %collective-permute-start.17 = (bf16[32,1792]{1,0:T(8,128)(2,1)S(1)}, bf16[32,1792]{1,0:T(8,128)(2,1)S(1)}, u32[]{:S(2)}, u32[]{:S(2)}) collective-permute-start(bf16[32,1792]{1,0:T(8,128)(2,1)S(1)} %get-tuple-element.59), channel_id=1, source_target_pairs={{0,4},{4,0},{8,12},{12,8},{1,5},{5,1},{9,13},{13,9},{2,6},{6,2},{1... | collective-permute-start | bytes 344072 | tf_op jit(solution)/shard_map/columns_over_ctx/ppermute | solution.py:52
  74.1 6.3 %collective-permute-start.19 = (bf16[16,1792]{1,0:T(8,128)(2,1)S(1)}, bf16[16,1792]{1,0:T(8,128)(2,1)S(1)}, u32[]{:S(2)}, u32[]{:S(2)}) collective-permute-start(bf16[16,1792]{1,0:T(8,128)(2,1)S(1)} %get-tuple-element.61), channel_id=1, source_target_pairs={{0,8},{4,12},{8,0},{12,4},{1,9},{5,13},{9,1},{13,5},{2,10},{6,14},... | collective-permute-start | bytes 172040 | tf_op jit(solution)/shard_map/columns_over_ctx/ppermute | solution.py:52
  74.1 6.3 %collective-permute-start.24 = (bf16[16,1792]{1,0:T(8,128)(2,1)S(1)}, bf16[16,1792]{1,0:T(8,128)(2,1)S(1)}, u32[]{:S(2)}, u32[]{:S(2)}) collective-permute-start(bf16[16,1792]{1,0:T(8,128)(2,1)S(1)} %sum_over_x.9), channel_id=1, source_target_pairs={{0,12},{4,8},{8,4},{12,0},{1,13},{5,9},{9,5},{13,1},{2,14},{6,10},... | collective-permute-start | bytes 172040 | tf_op jit(solution)/shard_map/columns_over_ctx/ppermute | solution.py:52
